TPU v7x, 32 devices: a whole 2x2x4 slice. The times are simulated.
32 devices in a mesh: blk: 8 (over y, x, core), rep: 4 (over z).
Axes of the slice: x: 2, y: 2, z: 4, core: 2. Of those that a mesh axis runs over, the one named last changes fastest.
Arguments:
- cotangent: bfloat16 [256, 256, 128], P('blk', 'rep'), may hold values from -6 to 6
- relu_mask: int32 [256, 256, 128], P('blk', 'rep'), may hold values 0 or 1
- aggregated: bfloat16 [256, 256, 128], P('blk', 'rep'), may hold values from -6 to 6
- weight: bfloat16 [256, 256], P('rep'), may hold values from -0.375 to 0.375
- tiles: bfloat16 [256, 16, 128, 128], P('blk'), may hold values from -0.125 to 0.125
- col_block: int32 [256, 16], P('blk'), may hold values from 0 to 255, as said below
- live_count: int32 [256], P('blk'), may hold values from 1 to 16, as said below
Outputs:
- input_grad: bfloat16 [256, 256, 128], P('blk', 'rep')
- weight_grad: float32 [256, 256], P('rep')
Inputs may be any that keep to these rules, and one draw needn't show every extreme that they name: The slab of a row block b is b // 32; the slab of col_block[b, s] lies at most 2 slabs from it around the closed cycle of the 8 slabs, and both distance 2 directions occur. `live_count`: row blocks of one slab share a density level, so live counts differ from slab to slab; some row block has all 16 slots live.
All inputs are finite; a program needn't handle non-finite values. No bound on the sum of `relu_mask` on one device may be relied on, other than what follows from the above.
Results may differ from a plain program's by a relative error of at most 0.0049.
Values may be sent and summed in bfloat16 or wider, within the bound.
No kernel may reach another device: no remote copies, remote signals or barrier semaphores. Data moves between devices by JAX's collectives and lax.ppermute only.
A program may use at most 128 MiB of HBM per device.

v0:
```python
import math

import jax
import jax.numpy as jnp
from jax import lax
from jax.sharding import PartitionSpec as P

REACH = 2


def from_behind(value, axis, steps):
    count = lax.axis_size(axis)
    pairs = [(source, (source + steps) % count) for source in range(count)]
    return lax.ppermute(value, axis, pairs)


def on_device(cotangent, relu_mask, aggregated, weight, tiles, col_block, live_count):
    blocks_here = cotangent.shape[0]
    cols_here = cotangent.shape[1]
    tile_size = cotangent.shape[2]
    grad_z = cotangent * relu_mask.astype(jnp.bfloat16)
    gathered_part = lax.all_gather(grad_z, "rep", axis=1, tiled=True)
    grad_h = jnp.einsum("io,bon->bin", weight, gathered_part, preferred_element_type=jnp.float32)
    col_part = jnp.einsum(
        "bin,bon->io", aggregated, gathered_part, preferred_element_type=jnp.float32
    )
    grad_w = col_part
    grad_h, grad_w = (grad_h, grad_w)
    nodes_all = lax.axis_size("blk") * blocks_here * tile_size
    weight_grad = lax.psum(grad_w, "blk") * (1.0 / math.sqrt(nodes_all))
    grad_hb = grad_h.astype(jnp.bfloat16)
    slot_count = tiles.shape[1]
    slot_ids = jnp.arange(slot_count, dtype=jnp.int32)
    live = (slot_ids[None, :] < live_count[:, None]).astype(jnp.float32).reshape(-1)
    contrib = jnp.einsum("bkij,bfi->bkfj", tiles, grad_hb, preferred_element_type=jnp.float32)
    flat_terms = contrib.reshape(blocks_here * slot_count, cols_here * tile_size)
    targets = col_block.reshape(-1)
    slabs = lax.axis_size("blk")
    own_slab = lax.axis_index("blk")
    target_slab = targets // blocks_here
    window_slot = (target_slab - own_slab + REACH + slabs) % slabs
    position = window_slot * blocks_here + targets % blocks_here
    window_rows = (2 * REACH + 1) * blocks_here
    row_ids = jnp.arange(window_rows, dtype=jnp.int32)
    selector = (position[None, :] == row_ids[:, None]).astype(jnp.float32) * live[None, :]
    window = jnp.dot(
        selector, flat_terms, preferred_element_type=jnp.float32, precision=lax.Precision.HIGHEST
    )
    window = window.reshape(2 * REACH + 1, blocks_here, cols_here, tile_size)
    input_grad = window[REACH]
    for offset in range(-REACH, REACH + 1):
        if offset != 0:
            input_grad = input_grad + from_behind(window[offset + REACH], "blk", offset)
    return (input_grad.astype(jnp.bfloat16), weight_grad)


def solution(mesh):
    placed = (
        P("blk", "rep", None),
        P("blk", "rep", None),
        P("blk", "rep", None),
        P("rep", None),
        P("blk", None, None, None),
        P("blk", None),
        P("blk"),
    )
    return jax.shard_map(
        on_device,
        mesh=mesh,
        in_specs=placed,
        out_specs=(P("blk", "rep", None), P("rep", None)),
        check_vma=False,
    )
```

profile of v0, /device:TPU:0, one launch (start us, length us, event | category | flops | bytes accessed | tf_op | source)
XLA Modules:
  0.0 177.9 jit_solution(5061053292171917626)
XLA Ops:
  7.2 0.0 copy-start
  7.2 0.0 all-gather.2.cloned.1.call-start
  7.2 2.3 %convert_multiply_fusion = bf16[32,64,128]{2,1,0:T(8,128)(2,1)} fusion(bf16[32,64,128]{2,1,0:T(8,128)(2,1)} %param.7, s32[32,64,128]{2,1,0:T(8,128)} %param.8), kind=kLoop, calls=%fused_computation.17 | loop fusion | flops 524288 | bytes 2097152 | tf_op jit(solution)/shard_map/mul | solution.py:21
  9.5 0.0 all-gather.2.cloned.1.call-update
  9.5 0.0 all-reduce.2.cloned.1.call-start
  9.6 0.8 copy.9
  10.4 0.1 reshape.102
  10.5 0.7 fusion.15
  11.2 0.1 reshape.104
  11.3 47.5 %all-gather.2.cloned.1.call-done = bf16[32,256,128]{2,1,0:T(8,128)(2,1)} async-done(((bf16[32,64,128]{2,1,0:T(8,128)(2,1)}), bf16[32,256,128]{2,1,0:T(8,128)(2,1)}) %all-gather.2.cloned.1.call-update) | async-done | bytes 2097168 | tf_op jit(solution)/shard_map/all_gather | solution.py:22
  58.8 11.3 %fusion.8 = f32[32,64,16,128]{3,1,2,0:T(8,128)} fusion(bf16[32,16,128,128]{3,2,1,0:T(8,128)(2,1)} %param.11, bf16[32,256,128]{2,1,0:T(8,128)(2,1)} %all-gather.2.cloned.1.call-done, bf16[64,256]{1,0:T(8,128)(2,1)} %param.10), kind=kOutput, calls=%fused_computation.16 | convolution fusion | flops 1208221696 | bytes 35684352 | tf_op jit(solution)/shard_map/bkij,bfi->bkfj/dot_general | solution.py:35
  70.2 20.3 %fusion = f32[160,8192]{1,0:T(8,128)S(1)} fusion(f32[64,8,64,128]{3,2,1,0:T(8,128)} %bitcast.48, f32[512]{0:T(512)S(1)} %reshape.104, s32[512]{0:T(512)S(1)} %fusion.20), kind=kOutput, calls=%fused_computation | convolution fusion | flops 8053227520 | bytes 22024192 | tf_op jit(solution)/shard_map/dot_general | solution.py:46
  90.5 0.4 slice_bitcast_fusion.4
  90.9 0.0 copy-start.1
  91.0 1.2 copy.16
  92.1 1.2 copy.15
  93.3 1.2 copy.14
  94.5 1.2 copy.13
  95.7 2.4 %collective-permute-start = (f32[32,64,128]{2,1,0:T(8,128)}, f32[32,64,128]{2,1,0:T(8,128)}, u32[]{:S(2)}, u32[]{:S(2)}) collective-permute-start(f32[32,64,128]{2,1,0:T(8,128)} %bitcast.14), channel_id=1, source_target_pairs={{0,24},{4,28},{8,0},{12,4},{16,8},{20,12},{24,16},{28,20},{1,25},{... | collective-permute-start | bytes 3145736 | tf_op jit(solution)/shard_map/ppermute | solution.py:14
  98.1 0.0 collective-permute-start.1
  98.1 0.5 collective-permute-start.2
  98.6 0.7 collective-permute-start.3
  99.3 1.4 convolution_bitcast_fusion
  100.6 0.0 all-reduce.2.cloned.1.call-update
  100.7 0.2 copy.12
  100.9 52.4 %all-reduce.2.cloned.1.call-done = f32[64,256]{1,0:T(8,128)} async-done(((f32[64,256]{1,0:T(8,128)}), f32[64,256]{1,0:T(8,128)}) %all-reduce.2.cloned.1.call-update) | async-done | bytes 65552 | tf_op jit(solution)/shard_map/psum | solution.py:30
  153.3 1.5 broadcast_multiply_fusion
  154.8 0.0 collective-permute-done
  154.8 0.0 collective-permute-done.1
  154.8 0.0 collective-permute-done.2
  154.8 12.8 %collective-permute-done.3 = f32[32,64,128]{2,1,0:T(8,128)} collective-permute-done((f32[32,64,128]{2,1,0:T(8,128)}, f32[32,64,128]{2,1,0:T(8,128)}, u32[]{:S(2)}, u32[]{:S(2)}) %collective-permute-start.3) | collective-permute-done | bytes 1048608 | tf_op jit(solution)/shard_map/ppermute | solution.py:14
  167.6 3.5 %fusion.7 = bf16[32,64,128]{2,1,0:T(8,128)(2,1)} fusion(f32[32,64,128]{2,1,0:T(8,128)} %collective-permute-done.3, f32[32,64,128]{2,1,0:T(8,128)} %collective-permute-done.2, f32[32,64,128]{2,1,0:T(8,128)} %collective-permute-done.1, f32[32,64,128]{2,1,0:T(8,128)} %collective-permute-done, f32[4,8,64,128]{3,2,1,0:T(8,128)S(1)} %copy.12), kind=kLoop, calls=%fused_computation.10 | loop fusion | flops 1310720 | bytes 5767168 | tf_op jit(solution)/shard_map/convert_element_type | solution.py:54
  (3 shorter events, 0.0 us)
Async XLA Ops:
  7.2 92.1 %copy-start = (bf16[32,64,128]{2,1,0:T(8,128)(2,1)S(1)}, bf16[32,64,128]{2,1,0:T(8,128)(2,1)}, u32[]{:S(2)}) copy-start(bf16[32,64,128]{2,1,0:T(8,128)(2,1)} %param.9) | copy-start | bytes 1572868
  7.2 51.7 %all-gather.2.cloned.1.call-start = ((), (), s32[]{:S(2)}) async-start(), calls=%async_computation | async-start | bytes 2621440 | tf_op jit(solution)/shard_map/all_gather | solution.py:22
  9.5 143.8 %all-reduce.2.cloned.1.call-start = ((), (), s32[]{:S(2)}) async-start(), calls=%async_computation.1 | async-start | bytes 131072 | tf_op jit(solution)/shard_map/psum | solution.py:30
  90.9 8.3 %copy-start.1 = (bf16[32,256,128]{2,1,0:T(8,128)(2,1)S(1)}, bf16[32,256,128]{2,1,0:T(8,128)(2,1)}, u32[]{:S(2)}) copy-start(bf16[32,256,128]{2,1,0:T(8,128)(2,1)} %all-gather.2.cloned.1.call-done) | copy-start | bytes 6291460
  95.7 59.1 %collective-permute-start = (f32[32,64,128]{2,1,0:T(8,128)}, f32[32,64,128]{2,1,0:T(8,128)}, u32[]{:S(2)}, u32[]{:S(2)}) collective-permute-start(f32[32,64,128]{2,1,0:T(8,128)} %bitcast.14), channel_id=1, source_target_pairs={{0,24},{4,28},{8,0},{12,4},{16,8},{20,12},{24,16},{28,20},{1,25},{... | collective-permute-start | bytes 3145736 | tf_op jit(solution)/shard_map/ppermute | solution.py:14
  98.1 56.7 %collective-permute-start.1 = (f32[32,64,128]{2,1,0:T(8,128)}, f32[32,64,128]{2,1,0:T(8,128)}, u32[]{:S(2)}, u32[]{:S(2)}) collective-permute-start(f32[32,64,128]{2,1,0:T(8,128)} %bitcast.16), channel_id=1, source_target_pairs={{0,28},{4,0},{8,4},{12,8},{16,12},{20,16},{24,20},{28,24},{1,29},{... | collective-permute-start | bytes 3145736 | tf_op jit(solution)/shard_map/ppermute | solution.py:14
  98.1 56.7 %collective-permute-start.2 = (f32[32,64,128]{2,1,0:T(8,128)}, f32[32,64,128]{2,1,0:T(8,128)}, u32[]{:S(2)}, u32[]{:S(2)}) collective-permute-start(f32[32,64,128]{2,1,0:T(8,128)} %bitcast.18), channel_id=1, source_target_pairs={{0,4},{4,8},{8,12},{12,16},{16,20},{20,24},{24,28},{28,0},{1,5},{5... | collective-permute-start | bytes 3145736 | tf_op jit(solution)/shard_map/ppermute | solution.py:14
  98.6 69.0 %collective-permute-start.3 = (f32[32,64,128]{2,1,0:T(8,128)}, f32[32,64,128]{2,1,0:T(8,128)}, u32[]{:S(2)}, u32[]{:S(2)}) collective-permute-start(f32[32,64,128]{2,1,0:T(8,128)} %bitcast.20), channel_id=1, source_target_pairs={{0,8},{4,12},{8,16},{12,20},{16,24},{20,28},{24,0},{28,4},{1,9},{5... | collective-permute-start | bytes 3145736 | tf_op jit(solution)/shard_map/ppermute | solution.py:14
Sparse Core Ops, SparseCore 0:
  10.2 48.6 all-gather.1
  100.8 52.4 all-reduce.1
where the time goes:
time: 178 us
  waiting for transfers between devices  113 us (63%)
  matrix products  33.1 us (19%)
  between operations  14.1 us (8%)
  other arithmetic  7.98 us (4%)
  local copies, waits for them, and re-layouts  6.31 us (4%)
  starting transfers between devices  3.62 us (2%)
    psum x1, waiting for transfers between devices, on_device(): weight_grad = lax.psum(grad_w, 'blk') * (1.0 / math.sqrt(nodes_all))  52.4 us
    all_gather x1, waiting for transfers between devices, on_device(): gathered_part = lax.all_gather(grad_z, 'rep', axis=1, tiled=True)  47.5 us
    dot_general x1, matrix products, on_device(): jnp.dot(selector, flat_terms, preferred_element_type=jnp.float32, precisi...  20.3 us
    ppermute x4, waiting for transfers between devices, from_behind(): return lax.ppermute(value, axis, pairs)  12.8 us
    dot_general x1, matrix products, on_device(): jnp.einsum('bkij,bfi->bkfj', tiles, grad_hb, preferred_element_type=jnp.f...  11.3 us
    unnamed x11, local copies, waits for them, and re-layouts  6.15 us
  transfers between devices with their start and end apart: 6, of which 3 were waited for; matrix products, arithmetic and copies ran while one was open for 3% of the time, Pallas kernels for 0%

commit v1 on v0

v1 whole, which is shorter than its diff:
```python
import functools
import math

import jax
import jax.numpy as jnp
from jax import lax
from jax.experimental import pallas as pl
from jax.experimental.pallas import tpu as pltpu
from jax.sharding import PartitionSpec as P

REACH = 2
CHUNKS = 2
BF16 = jnp.bfloat16
F32 = jnp.float32


def vmem():
    return pl.BlockSpec(memory_space=pltpu.VMEM)


def smem():
    return pl.BlockSpec(memory_space=pltpu.SMEM)


def hbm():
    return pl.BlockSpec(memory_space=pl.ANY)


def tiles_kernel(slabs, chunk, where, cols, z_ref, tiles_ref, *rest):
    outs, (held, total, sems) = rest[:-3], rest[-3:]
    blocks, slots = tiles_ref.shape[:2]
    window = (2 * REACH + 1) * blocks
    for b in range(blocks):
        pltpu.make_async_copy(tiles_ref.at[b], held.at[b], sems.at[b]).start()

    def clear(i, carry):
        total[i] = jnp.zeros(total.shape[1:], F32)
        return carry

    lax.fori_loop(0, window, clear, 0)
    own = where[0]
    sign = 2 * lax.rem(own, 2) - 1

    def row_block(b, carry):
        pltpu.make_async_copy(tiles_ref.at[b], held.at[b], sems.at[b]).wait()
        z = z_ref[b]
        live = cols[b, slots]
        for s in range(slots):
            col = cols[b, s]
            slab = lax.div(col, blocks)
            offset = lax.rem(slab - own + REACH + slabs, slabs) - REACH
            place = (offset * sign + REACH) * blocks + lax.rem(col, blocks)
            place = jnp.where(s < live, place, window)
            total[place] += jnp.dot(z, held[b, s], preferred_element_type=F32)
        return carry

    lax.fori_loop(0, blocks, row_block, 0)

    parts = 2 * REACH + 1
    chunks = blocks // chunk
    for part in range(parts):
        for k in range(chunks):

            def store(i, carry, out=outs[part * chunks + k], base=part * blocks + k * chunk):
                out[i] = total[base + i].astype(BF16)
                return carry

            lax.fori_loop(0, chunk, store, 0)


def contributions(where, cols, z, tiles, slabs, chunk):
    blocks, features, nodes = z.shape
    slots = tiles.shape[1]
    chunks = blocks // chunk
    parts = 2 * REACH + 1
    window = parts * blocks
    outs = pl.pallas_call(
        functools.partial(tiles_kernel, slabs, chunk),
        out_shape=[jax.ShapeDtypeStruct((chunk, features, nodes), BF16)] * (parts * chunks),
        in_specs=[smem(), smem(), vmem(), hbm()],
        out_specs=[vmem()] * (parts * chunks),
        scratch_shapes=[
            pltpu.VMEM(tiles.shape, BF16),
            pltpu.VMEM((window + 1, features, nodes), F32),
            pltpu.SemaphoreType.DMA((blocks,)),
        ],
        compiler_params=pltpu.CompilerParams(vmem_limit_bytes=40 << 20),
        cost_estimate=pl.CostEstimate(
            flops=2 * blocks * slots * features * nodes * nodes,
            bytes_accessed=tiles.size * 2 + 6 * z.size * 2,
            transcendentals=0,
        ),
    )(where, cols, z, tiles)
    return [outs[part * chunks : (part + 1) * chunks] for part in range(parts)]


def lay_features(where, shares, whole, reps):
    width = shares[0].shape[1]
    for s, share in enumerate(shares):
        first = lax.rem(where[1] - s + reps, reps) * width
        whole[:, pl.ds(pl.multiple_of(first, width), width), :] = share[...]


def weight_kernel(reps, where, *rest):
    aggs, shares = rest[:reps], rest[reps : 2 * reps]
    outs, whole = rest[2 * reps : 3 * reps], rest[3 * reps]
    lay_features(where, shares, whole, reps)
    blocks = whole.shape[0]
    for s in range(reps):
        total = jnp.zeros(outs[s].shape, F32)
        for b in range(blocks):
            total += lax.dot_general(
                aggs[s][b], whole[b], (((1,), (1,)), ((), ())), preferred_element_type=F32
            )
        outs[s][...] = total.astype(outs[s].dtype)


def weight_partial(where, aggs, shares):
    reps = len(shares)
    blocks, features, nodes = shares[0].shape
    width = reps * features
    return pl.pallas_call(
        functools.partial(weight_kernel, reps),
        out_shape=[jax.ShapeDtypeStruct((features, width), F32)] * reps,
        in_specs=[smem()] + [vmem()] * (2 * reps),
        out_specs=[vmem()] * reps,
        scratch_shapes=[pltpu.VMEM((blocks, width, nodes), BF16)],
        cost_estimate=pl.CostEstimate(
            flops=2 * blocks * nodes * width * width,
            bytes_accessed=4 * blocks * nodes * width + 4 * width * width,
            transcendentals=0,
        ),
    )(where, *aggs, *shares)


def mix_kernel(reps, where, *rest):
    weights, shares = rest[:reps], rest[reps : 2 * reps]
    outs, whole = rest[2 * reps : 3 * reps], rest[3 * reps]
    lay_features(where, shares, whole, reps)
    for b in range(whole.shape[0]):
        for s in range(reps):
            mixed = jnp.dot(weights[s][...], whole[b], preferred_element_type=F32)
            outs[s][b] = mixed.astype(BF16)


def mix(where, weights, shares):
    reps = len(shares)
    blocks, features, nodes = shares[0].shape
    width = reps * features
    return pl.pallas_call(
        functools.partial(mix_kernel, reps),
        out_shape=[jax.ShapeDtypeStruct((blocks, features, nodes), BF16)] * reps,
        in_specs=[smem()] + [vmem()] * (2 * reps),
        out_specs=[vmem()] * reps,
        scratch_shapes=[pltpu.VMEM((blocks, width, nodes), BF16)],
        cost_estimate=pl.CostEstimate(
            flops=2 * blocks * nodes * width * width,
            bytes_accessed=4 * blocks * nodes * width,
            transcendentals=0,
        ),
    )(where, *weights, *shares)


def lay_kernel(reps, chunks, where, *rest):
    shares, out, sems = rest[: reps * chunks], rest[-2], rest[-1]
    copies = []
    for k in range(chunks):
        for s in range(reps):
            share = shares[k * reps + s]
            blocks = share.shape[0]
            first = (k * reps + lax.rem(where[1] - s + reps, reps)) * blocks
            copy = pltpu.make_async_copy(share, out.at[pl.ds(first, blocks)], sems.at[k * reps + s])
            copy.start()
            copies.append(copy)
    for copy in copies:
        copy.wait()


def lay_blocks(where, shares, shape):
    chunks, reps = len(shares), len(shares[0])
    return pl.pallas_call(
        functools.partial(lay_kernel, reps, chunks),
        out_shape=jax.ShapeDtypeStruct(shape, BF16),
        in_specs=[smem()] + [hbm()] * (reps * chunks),
        out_specs=hbm(),
        scratch_shapes=[pltpu.SemaphoreType.DMA((reps * chunks,))],
    )(where, *[share for chunk in shares for share in chunk])


def shift(value, axis, steps):
    count = lax.axis_size(axis)
    if steps % count == 0:
        return value
    return lax.ppermute(value, axis, [(i, (i + steps) % count) for i in range(count)])


def node_share(value, steps):
    reps = lax.axis_size("rep")
    blocks = value.shape[0] // reps
    first = lax.rem(lax.axis_index("rep") + steps, reps) * blocks
    return lax.dynamic_slice_in_dim(value, first, blocks, 0)


def to_node_shares(value):
    return [shift(node_share(value, s), "rep", s) for s in range(lax.axis_size("rep"))]


def on_device(cotangent, relu_mask, aggregated, weight, tiles, col_block, live_count):
    blocks = cotangent.shape[0]
    nodes = cotangent.shape[2]
    slabs, reps = lax.axis_size("blk"), lax.axis_size("rep")
    chunk = blocks // CHUNKS
    where = jnp.stack([lax.axis_index("blk"), lax.axis_index("rep")]).astype(jnp.int32)
    cols = jnp.concatenate([col_block, live_count[:, None]], axis=1)

    grad_z = cotangent * relu_mask.astype(BF16)
    aggs = to_node_shares(aggregated)
    shares = to_node_shares(grad_z)
    weights = [shift(weight, "rep", -s) for s in range(reps)]

    near, beside, own, first, second = contributions(where, cols, grad_z, tiles, slabs, chunk)

    grad_w = weight_partial(where, aggs, shares)
    grad_w = sum(shift(part.astype(BF16), "rep", -s).astype(F32) for s, part in enumerate(grad_w))
    step = 1
    while step < slabs:
        pairs = [(i, i ^ step) for i in range(slabs)]
        grad_w = grad_w + lax.ppermute(grad_w, "blk", pairs)
        step *= 2
    weight_grad = grad_w * (1.0 / math.sqrt(slabs * blocks * nodes))

    pair = [(i, i ^ 1) for i in range(slabs)]
    across = [(i, (i - 3) % slabs) for i in range(slabs) if i % 4 == 0]
    across += [(i, (i + 3) % slabs) for i in range(slabs) if i % 4 == 3]
    to_one = [(i, (i + 1) % slabs) for i in range(slabs) if i % 4 == 1]
    to_one += [(i, (i - 1) % slabs) for i in range(slabs) if i % 4 == 2]
    to_two = [(i, (i + 2) % slabs) for i in range(slabs) if i % 4 == 1]
    to_two += [(i, (i - 2) % slabs) for i in range(slabs) if i % 4 == 2]

    def add(*terms):
        return sum(term.astype(F32) for term in terms).astype(BF16)

    mixed = []
    for k in range(CHUNKS):
        one = add(first[k], lax.ppermute(near[k], "blk", pair))
        two = second[k]
        held = lax.ppermute(beside[k], "blk", pair)
        one_over = lax.ppermute(one, "blk", across)
        two_over = lax.ppermute(two, "blk", across)
        one_in = lax.ppermute(add(one, two_over), "blk", to_one)
        two_in = lax.ppermute(add(two, one_over), "blk", to_two)
        sums = add(own[k], held, one_in, two_in)
        outs = mix(where, weights, to_node_shares(sums))
        mixed.append([shift(part, "rep", s) for s, part in enumerate(outs)])
    return lay_blocks(where, mixed, cotangent.shape), weight_grad


def solution(mesh):
    placed = (
        P("blk", "rep", None),
        P("blk", "rep", None),
        P("blk", "rep", None),
        P("rep", None),
        P("blk", None, None, None),
        P("blk", None),
        P("blk"),
    )
    return jax.shard_map(
        on_device,
        mesh=mesh,
        in_specs=placed,
        out_specs=(P("blk", "rep", None), P("rep", None)),
        check_vma=False,
    )
```

time: 178 us -> 128 us (0.72)
  waiting for transfers between devices: 113 us -> 15.3 us
  starting transfers between devices: 3.62 us -> 58.8 us
  Pallas kernels: 0 us -> 36.9 us
  matrix products: 33.1 us -> 0 us
  between operations: 14.1 us -> 1.06 us
    ppermute x4 -> x39, starting transfers between devices: 3.54 us -> 58.8 us  [the longest x24 39 us: shift(): lax.ppermute(value, axis, [(i, (i + steps) % count) for i in range(count)])]
    psum x1 -> x0, waiting for transfers between devices: 52.4 us -> none  [on_device(): weight_grad = lax.psum(grad_w, 'blk') * (1.0 / math.sqrt(nodes_all))]
    all_gather x1 -> x0, waiting for transfers between devices: 47.5 us -> none  [on_device(): gathered_part = lax.all_gather(grad_z, 'rep', axis=1, tiled=True)]
    pallas_call x0 -> x5, Pallas kernels: none -> 36.9 us  [the longest x1 17.7 us: lay_blocks(): pl.pallas_call(functools.partial(lay_kernel, reps, chunks), out_shape=jax...]
    dot_general x3 -> x0, matrix products: 33.1 us -> none  [the longest x1 20.3 us: on_device(): jnp.dot(selector, flat_terms, preferred_element_type=jnp.float32, precisi...]
    unnamed x11 -> x43, local copies, waits for them, and re-layouts: 6.15 us -> 3.28 us
    dynamic_slice x0 -> x4, local copies, waits for them, and re-layouts: none -> 2.87 us  [node_share(): return lax.dynamic_slice_in_dim(value, first, blocks, 0)]
    ppermute x4 -> x39, waiting for transfers between devices: 12.8 us -> 15.3 us  [the longest x24 12.8 us: shift(): lax.ppermute(value, axis, [(i, (i + steps) % count) for i in range(count)])]
  transfers between devices with their start and end apart: 6 -> 39, of which waited for: 3 -> 8; matrix products, arithmetic and copies ran while one was open for 3% -> 8% of each run, Pallas kernels for 0% -> 15%
where the time goes in v1:
time: 128 us; the launch traced here: 127 us
  starting transfers between devices  58.8 us (46%)
  Pallas kernels  36.9 us (29%)
  waiting for transfers between devices  15.3 us (12%)
  other arithmetic  8.32 us (6%)
  local copies, waits for them, and re-layouts  6.88 us (5%)
    ppermute x24, starting transfers between devices, shift(): lax.ppermute(value, axis, [(i, (i + steps) % count) for i in range(count)])  39 us
    pallas_call x1, Pallas kernels, lay_blocks(): pl.pallas_call(functools.partial(lay_kernel, reps, chunks), out_shape=jax...  17.7 us
    ppermute x24, waiting for transfers between devices, shift(): lax.ppermute(value, axis, [(i, (i + steps) % count) for i in range(count)])  12.8 us
    pallas_call x1, Pallas kernels, contributions(): pl.pallas_call(functools.partial(tiles_kernel, slabs, chunk), out_shape=[...  12.4 us
    ppermute x2, starting transfers between devices, on_device(): held = lax.ppermute(beside[k], 'blk', pair)  5.07 us
    pallas_call x2, Pallas kernels, mix(): pl.pallas_call(functools.partial(mix_kernel, reps), out_shape=[jax.ShapeD...  4.05 us
    ppermute x2, starting transfers between devices, on_device(): two_over = lax.ppermute(two, 'blk', across)  3.97 us
    ppermute x2, starting transfers between devices, on_device(): one_over = lax.ppermute(one, 'blk', across)  3.4 us
  transfers between devices with their start and end apart: 39, of which 8 were waited for; matrix products, arithmetic and copies ran while one was open for 8% of the time, Pallas kernels for 15%

profile of v1, /device:TPU:0, one launch (start us, length us, event | category | flops | bytes accessed | tf_op | source)
XLA Modules:
  0.0 127.2 jit_solution(16491560839619684901)
XLA Ops:
  0.7 1.5 %convert_multiply_fusion.z_ref = bf16[32,64,128]{2,1,0:T(8,128)(2,1)S(1)} fusion(bf16[32,64,128]{2,1,0:T(8,128)(2,1)} %param.7, s32[32,64,128]{2,1,0:T(8,128)} %param.8), kind=kLoop, calls=%fused_computation.8 | loop fusion | flops 524288 | bytes 2097152 | tf_op jit(solution)/shard_map/mul | solution.py:216
  3.0 3.0 %collective-permute-start.30 = (bf16[8,64,128]{2,1,0:T(8,128)(2,1)}, bf16[8,64,128]{2,1,0:T(8,128)(2,1)}, u32[]{:S(2)}, u32[]{:S(2)}) collective-permute-start(bf16[8,64,128]{2,1,0:T(8,128)(2,1)} %get-tuple-element.52), channel_id=1, source_target_pairs={{0,1},{1,2},{2,3},{3,0},{4,5},{5,6},{6,7},{7,4},{8,9},{9,10},{10,1... | collective-permute-start | bytes 393224 | tf_op jit(solution)/shard_map/ppermute | solution.py:194
  6.0 2.6 %collective-permute-start.31 = (bf16[8,64,128]{2,1,0:T(8,128)(2,1)}, bf16[8,64,128]{2,1,0:T(8,128)(2,1)}, u32[]{:S(2)}, u32[]{:S(2)}) collective-permute-start(bf16[8,64,128]{2,1,0:T(8,128)(2,1)} %get-tuple-element.51), channel_id=1, source_target_pairs={{0,2},{1,3},{2,0},{3,1},{4,6},{5,7},{6,4},{7,5},{8,10},{9,11},{10,... | collective-permute-start | bytes 393224 | tf_op jit(solution)/shard_map/ppermute | solution.py:194
  8.6 1.3 %collective-permute-start.32 = (bf16[8,64,128]{2,1,0:T(8,128)(2,1)}, bf16[8,64,128]{2,1,0:T(8,128)(2,1)}, u32[]{:S(2)}, u32[]{:S(2)}) collective-permute-start(bf16[8,64,128]{2,1,0:T(8,128)(2,1)} %get-tuple-element.50), channel_id=1, source_target_pairs={{0,3},{1,0},{2,1},{3,2},{4,7},{5,4},{6,5},{7,6},{8,11},{9,8},{10,9... | collective-permute-start | bytes 393224 | tf_op jit(solution)/shard_map/ppermute | solution.py:194
  11.6 12.4 %shard_map.86 = (bf16[16,64,128]{2,1,0:T(8,128)(2,1)S(1)}, bf16[16,64,128]{2,1,0:T(8,128)(2,1)S(1)}, bf16[16,64,128]{2,1,0:T(8,128)(2,1)S(1)}, bf16[16,64,128]{2...) custom-call(s32[2]{0:T(128)S(1)} %pad_add_fusion.1.where, ...), custom_call_target="tpu_custom_call" | custom-call | flops 1073741824 | bytes 19922944 | tf_op jit(solution)/shard_map/pallas_call | solution.py:77
  24.0 2.0 %collective-permute-start.17 = (bf16[16,64,128]{2,1,0:T(8,128)(2,1)S(1)}, bf16[16,64,128]{2,1,0:T(8,128)(2,1)S(1)}, u32[]{:S(2)}, u32[]{:S(2)}) collective-permute-start(bf16[16,64,128]{2,1,0:T(8,128)(2,1)S(1)} %get-tuple-element.37), channel_id=1, source_target_pairs={{0,20},{16,4},{12,24},{28,8},{1,21},{17,5},{13,25},{29,9},{2,22},{... | collective-permute-start | bytes 786440 | tf_op jit(solution)/shard_map/ppermute | solution.py:249
  27.8 2.9 %collective-permute-start.29 = (bf16[8,64,128]{2,1,0:T(8,128)(2,1)S(1)}, bf16[8,64,128]{2,1,0:T(8,128)(2,1)S(1)}, u32[]{:S(2)}, u32[]{:S(2)}) collective-permute-start(bf16[8,64,128]{2,1,0:T(8,128)(2,1)S(1)} %get-tuple-element.54), channel_id=1, source_target_pairs={{0,3},{1,0},{2,1},{3,2},{4,7},{5,4},{6,5},{7,6},{8,11},{9,8},{10,9... | collective-permute-start | bytes 393224 | tf_op jit(solution)/shard_map/ppermute | solution.py:194
  30.7 4.3 %collective-permute-done.27.rest_1_ = bf16[8,64,128]{2,1,0:T(8,128)(2,1)S(1)} collective-permute-done((bf16[8,64,128]{2,1,0:T(8,128)(2,1)S(1)}, bf16[8,64,128]{2,1,0:T(8,128)(2,1)S(1)}, u32[]{:S(2)}, u32[]{:S(2)}) %collective-permute-start.27) | collective-permute-done | bytes 131104 | tf_op jit(solution)/shard_map/ppermute | solution.py:194
  35.0 5.2 %collective-permute-done.28.rest_2_ = bf16[8,64,128]{2,1,0:T(8,128)(2,1)S(1)} collective-permute-done((bf16[8,64,128]{2,1,0:T(8,128)(2,1)S(1)}, bf16[8,64,128]{2,1,0:T(8,128)(2,1)S(1)}, u32[]{:S(2)}, u32[]{:S(2)}) %collective-permute-start.28) | collective-permute-done | bytes 131104 | tf_op jit(solution)/shard_map/ppermute | solution.py:194
  40.2 2.0 %collective-permute-start.5 = (bf16[16,64,128]{2,1,0:T(8,128)(2,1)S(1)}, bf16[16,64,128]{2,1,0:T(8,128)(2,1)}, u32[]{:S(2)}, u32[]{:S(2)}) collective-permute-start(bf16[16,64,128]{2,1,0:T(8,128)(2,1)S(1)} %get-tuple-element.28), channel_id=1, source_target_pairs={{0,20},{16,4},{12,24},{28,8},{1,21},{17,5},{13,25},{29,9},{2,22},{... | collective-permute-start | bytes 786440 | tf_op jit(solution)/shard_map/ppermute | solution.py:249
  42.8 2.8 %shard_map.90 = (f32[64,256]{1,0:T(8,128)}, f32[64,256]{1,0:T(8,128)}, f32[64,256]{1,0:T(8,128)}, f32[64,256]{1,0:T(8,128)}) custom-call(s32[2]{0:T(128)} %copy-done, bf16[8,64,128]{2,1,0:T(8,128)(2,1)} %get-tuple-element.56.rest_0_, bf16[8,64,128]{2,1,0:T(8,128)(2,1)} %copy-done.6, bf16[8,64,128]{2,1,0:T(8,128)(2,1)} %copy-done.7, ...), custom_call_target="tpu_custom_call" | custom-call | flops 134217728 | bytes 1310720 | tf_op jit(solution)/shard_map/pallas_call | solution.py:122
  48.1 3.1 %collective-permute-start.33 = (bf16[64,256]{1,0:T(8,128)(2,1)S(1)}, bf16[64,256]{1,0:T(8,128)(2,1)S(1)}, u32[]{:S(2)}, u32[]{:S(2)}) collective-permute-start(bf16[64,256]{1,0:T(8,128)(2,1)S(1)} %convert_element_type.142), channel_id=1, source_target_pairs={{0,3},{1,0},{2,1},{3,2},{4,7},{5,4},{6,5},{7,6},{8,11},{9,8},{10,9... | collective-permute-start | bytes 98312 | tf_op jit(solution)/shard_map/ppermute | solution.py:194
  52.1 2.1 %collective-permute-start.19 = (bf16[16,64,128]{2,1,0:T(8,128)(2,1)S(1)}, bf16[16,64,128]{2,1,0:T(8,128)(2,1)S(1)}, u32[]{:S(2)}, u32[]{:S(2)}) collective-permute-start(bf16[16,64,128]{2,1,0:T(8,128)(2,1)S(1)} %get-tuple-element.47), channel_id=1, source_target_pairs={{0,20},{16,4},{12,24},{28,8},{1,21},{17,5},{13,25},{29,9},{2,22},{... | collective-permute-start | bytes 786440 | tf_op jit(solution)/shard_map/ppermute | solution.py:248
  54.2 1.2 add_convert_fusion.6
  55.4 1.3 %collective-permute-start.7 = (bf16[16,64,128]{2,1,0:T(8,128)(2,1)S(1)}, bf16[16,64,128]{2,1,0:T(8,128)(2,1)S(1)}, u32[]{:S(2)}, u32[]{:S(2)}) collective-permute-start(bf16[16,64,128]{2,1,0:T(8,128)(2,1)S(1)} %get-tuple-element.49), channel_id=1, source_target_pairs={{0,20},{16,4},{12,24},{28,8},{1,21},{17,5},{13,25},{29,9},{2,22},{... | collective-permute-start | bytes 786440 | tf_op jit(solution)/shard_map/ppermute | solution.py:248
  58.9 1.3 %collective-permute-start.20 = (bf16[16,64,128]{2,1,0:T(8,128)(2,1)S(1)}, bf16[16,64,128]{2,1,0:T(8,128)(2,1)S(1)}, u32[]{:S(2)}, u32[]{:S(2)}) collective-permute-start(bf16[16,64,128]{2,1,0:T(8,128)(2,1)S(1)} %add_convert_fusion.1), channel_id=1, source_target_pairs={{4,12},{20,28},{8,0},{24,16},{5,13},{21,29},{9,1},{25,17},{6,14},{... | collective-permute-start | bytes 786440 | tf_op jit(solution)/shard_map/ppermute | solution.py:251
  60.3 2.8 %collective-permute-start = (bf16[64,256]{1,0:T(8,128)(2,1)S(1)}, bf16[64,256]{1,0:T(8,128)(2,1)S(1)}, u32[]{:S(2)}, u32[]{:S(2)}) collective-permute-start(bf16[64,256]{1,0:T(8,128)(2,1)S(1)} %copy-done.2), channel_id=1, source_target_pairs={{0,3},{1,0},{2,1},{3,2},{4,7},{5,4},{6,5},{7,6},{8,11},{9,8},{10,9... | collective-permute-start | bytes 98312 | tf_op jit(solution)/shard_map/ppermute | solution.py:194
  64.9 5.1 %collective-permute-start.3 = (bf16[16,64,128]{2,1,0:T(8,128)(2,1)S(1)}, bf16[16,64,128]{2,1,0:T(8,128)(2,1)S(1)}, u32[]{:S(2)}, u32[]{:S(2)}) collective-permute-start(bf16[16,64,128]{2,1,0:T(8,128)(2,1)S(1)} %get-tuple-element.25), channel_id=1, source_target_pairs={{0,4},{4,0},{8,12},{12,8},{16,20},{20,16},{24,28},{28,24},{1,5},{5... | collective-permute-start | bytes 786440 | tf_op jit(solution)/shard_map/ppermute | solution.py:247
  70.7 1.3 %collective-permute-start.8 = (bf16[16,64,128]{2,1,0:T(8,128)(2,1)S(1)}, bf16[16,64,128]{2,1,0:T(8,128)(2,1)S(1)}, u32[]{:S(2)}, u32[]{:S(2)}) collective-permute-start(bf16[16,64,128]{2,1,0:T(8,128)(2,1)S(1)} %add_convert_fusion.5), channel_id=1, source_target_pairs={{4,12},{20,28},{8,0},{24,16},{5,13},{21,29},{9,1},{25,17},{6,14},{... | collective-permute-start | bytes 786440 | tf_op jit(solution)/shard_map/ppermute | solution.py:251
  72.8 2.8 %collective-permute-start.2 = (bf16[64,256]{1,0:T(8,128)(2,1)S(1)}, bf16[64,256]{1,0:T(8,128)(2,1)S(1)}, u32[]{:S(2)}, u32[]{:S(2)}) collective-permute-start(bf16[64,256]{1,0:T(8,128)(2,1)S(1)} %copy-done.2), channel_id=1, source_target_pairs={{0,1},{1,2},{2,3},{3,0},{4,5},{5,6},{6,7},{7,4},{8,9},{9,10},{10,1... | collective-permute-start | bytes 98312 | tf_op jit(solution)/shard_map/ppermute | solution.py:194
  75.7 2.7 %collective-permute-start.37 = (f32[64,256]{1,0:T(8,128)S(1)}, f32[64,256]{1,0:T(8,128)S(1)}, u32[]{:S(2)}, u32[]{:S(2)}) collective-permute-start(f32[64,256]{1,0:T(8,128)S(1)} %add.130), channel_id=1, source_target_pairs={{0,8},{4,12},{8,0},{12,4},{16,24},{20,28},{24,16},{28,20},{1,9},{5... | collective-permute-start | bytes 196616 | tf_op jit(solution)/shard_map/ppermute | solution.py:228
  78.3 2.4 %collective-permute-done.8 = bf16[16,64,128]{2,1,0:T(8,128)(2,1)S(1)} collective-permute-done((bf16[16,64,128]{2,1,0:T(8,128)(2,1)S(1)}, bf16[16,64,128]{2,1,0:T(8,128)(2,1)S(1)}, u32[]{:S(2)}, u32[]{:S(2)}) %collective-permute-start.8) | collective-permute-done | bytes 262176 | tf_op jit(solution)/shard_map/ppermute | solution.py:251
  80.8 1.8 %collective-permute-start.21 = (bf16[4,64,128]{2,1,0:T(8,128)(2,1)S(1)}, bf16[4,64,128]{2,1,0:T(8,128)(2,1)S(1)}, u32[]{:S(2)}, u32[]{:S(2)}) collective-permute-start(bf16[4,64,128]{2,1,0:T(8,128)(2,1)S(1)} %get-tuple-element.60), channel_id=1, source_target_pairs={{0,1},{1,2},{2,3},{3,0},{4,5},{5,6},{6,7},{7,4},{8,9},{9,10},{10,1... | collective-permute-start | bytes 196616 | tf_op jit(solution)/shard_map/ppermute | solution.py:194
  83.5 2.5 %collective-permute-start.23 = (bf16[4,64,128]{2,1,0:T(8,128)(2,1)S(1)}, bf16[4,64,128]{2,1,0:T(8,128)(2,1)S(1)}, u32[]{:S(2)}, u32[]{:S(2)}) collective-permute-start(bf16[4,64,128]{2,1,0:T(8,128)(2,1)S(1)} %get-tuple-element.58), channel_id=1, source_target_pairs={{0,3},{1,0},{2,1},{3,2},{4,7},{5,4},{6,5},{7,6},{8,11},{9,8},{10,9... | collective-permute-start | bytes 196616 | tf_op jit(solution)/shard_map/ppermute | solution.py:194
  91.1 2.0 %shard_map.88 = (bf16[4,64,128]{2,1,0:T(8,128)(2,1)}, bf16[4,64,128]{2,1,0:T(8,128)(2,1)}, bf16[4,64,128]{2,1,0:T(8,128)(2,1)}, bf16[4,64,128]{2,1,0:T(8,128)(2,1)}) custom-call(s32[2]{0:T(128)} %copy-done, bf16[64,256]{1,0:T(8,128)(2,1)} %rest_0_.3, bf16[64,256]{1,0:T(8,128)(2,1)} %copy-done.3, bf16[64,256]{1,0:T(8,128)(2,1)} %copy-done.4, ...), custom_call_target="tpu_custom_call" | custom-call | flops 67108864 | bytes 524288 | tf_op jit(solution)/shard_map/pallas_call | solution.py:150
  93.1 2.6 %collective-permute-start.24 = (bf16[4,64,128]{2,1,0:T(8,128)(2,1)}, bf16[4,64,128]{2,1,0:T(8,128)(2,1)S(1)}, u32[]{:S(2)}, u32[]{:S(2)}) collective-permute-start(bf16[4,64,128]{2,1,0:T(8,128)(2,1)} %get-tuple-element.39), channel_id=1, source_target_pairs={{0,1},{1,2},{2,3},{3,0},{4,5},{5,6},{6,7},{7,4},{8,9},{9,10},{10,1... | collective-permute-start | bytes 196616 | tf_op jit(solution)/shard_map/ppermute | solution.py:194
  95.7 2.8 %collective-permute-start.25 = (bf16[4,64,128]{2,1,0:T(8,128)(2,1)}, bf16[4,64,128]{2,1,0:T(8,128)(2,1)S(1)}, u32[]{:S(2)}, u32[]{:S(2)}) collective-permute-start(bf16[4,64,128]{2,1,0:T(8,128)(2,1)} %get-tuple-element.40), channel_id=1, source_target_pairs={{0,2},{1,3},{2,0},{3,1},{4,6},{5,7},{6,4},{7,5},{8,10},{9,11},{10,... | collective-permute-start | bytes 196616 | tf_op jit(solution)/shard_map/ppermute | solution.py:194
  99.1 2.0 %shard_map.87 = (bf16[4,64,128]{2,1,0:T(8,128)(2,1)}, bf16[4,64,128]{2,1,0:T(8,128)(2,1)}, bf16[4,64,128]{2,1,0:T(8,128)(2,1)}, bf16[4,64,128]{2,1,0:T(8,128)(2,1)}) custom-call(s32[2]{0:T(128)} %copy-done, bf16[64,256]{1,0:T(8,128)(2,1)} %rest_0_.3, bf16[64,256]{1,0:T(8,128)(2,1)} %copy-done.3, bf16[64,256]{1,0:T(8,128)(2,1)} %copy-done.4, ...), custom_call_target="tpu_custom_call" | custom-call | flops 67108864 | bytes 524288 | tf_op jit(solution)/shard_map/pallas_call | solution.py:150
  101.2 2.0 %collective-permute-start.12 = (bf16[4,64,128]{2,1,0:T(8,128)(2,1)}, bf16[4,64,128]{2,1,0:T(8,128)(2,1)S(1)}, u32[]{:S(2)}, u32[]{:S(2)}) collective-permute-start(bf16[4,64,128]{2,1,0:T(8,128)(2,1)} %get-tuple-element.30), channel_id=1, source_target_pairs={{0,1},{1,2},{2,3},{3,0},{4,5},{5,6},{6,7},{7,4},{8,9},{9,10},{10,1... | collective-permute-start | bytes 196616 | tf_op jit(solution)/shard_map/ppermute | solution.py:194
  103.3 2.3 %collective-permute-start.14 = (bf16[4,64,128]{2,1,0:T(8,128)(2,1)}, bf16[4,64,128]{2,1,0:T(8,128)(2,1)S(1)}, u32[]{:S(2)}, u32[]{:S(2)}) collective-permute-start(bf16[4,64,128]{2,1,0:T(8,128)(2,1)} %get-tuple-element.32), channel_id=1, source_target_pairs={{0,3},{1,0},{2,1},{3,2},{4,7},{5,4},{6,5},{7,6},{8,11},{9,8},{10,9... | collective-permute-start | bytes 196616 | tf_op jit(solution)/shard_map/ppermute | solution.py:194
  107.4 1.4 %collective-permute-done.13.rest_2_ = bf16[4,64,128]{2,1,0:T(8,128)(2,1)S(1)} collective-permute-done((bf16[4,64,128]{2,1,0:T(8,128)(2,1)}, bf16[4,64,128]{2,1,0:T(8,128)(2,1)S(1)}, u32[]{:S(2)}, u32[]{:S(2)}) %collective-permute-start.13) | collective-permute-done | bytes 65568 | tf_op jit(solution)/shard_map/ppermute | solution.py:194
  109.5 17.7 %shard_map.89 = bf16[32,64,128]{2,1,0:T(8,128)(2,1)} custom-call(s32[2]{0:T(128)} %copy-done, bf16[4,64,128]{2,1,0:T(8,128)(2,1)} %get-tuple-element.29.rest_0_, bf16[4,64,128]{2,1,0:T(8,128)(2,1)} %copy-done.18, bf16[4,64,128]{2,1,0:T(8,128)(2,1)} %copy-done.19, bf16[4,64,128]{2,1,0:T(8,128)(2,1)} %copy-done.20, ...), custom_call_target="tpu_custom_call" | custom-call | tf_op jit(solution)/shard_map/pallas_call | solution.py:181
  (115 shorter events, 23.0 us)
Async XLA Ops:
  3.0 23.8 %collective-permute-start.30 = (bf16[8,64,128]{2,1,0:T(8,128)(2,1)}, bf16[8,64,128]{2,1,0:T(8,128)(2,1)}, u32[]{:S(2)}, u32[]{:S(2)}) collective-permute-start(bf16[8,64,128]{2,1,0:T(8,128)(2,1)} %get-tuple-element.52), channel_id=1, source_target_pairs={{0,1},{1,2},{2,3},{3,0},{4,5},{5,6},{6,7},{7,4},{8,9},{9,10},{10,1... | collective-permute-start | bytes 393224 | tf_op jit(solution)/shard_map/ppermute | solution.py:194
  6.0 21.4 %collective-permute-start.31 = (bf16[8,64,128]{2,1,0:T(8,128)(2,1)}, bf16[8,64,128]{2,1,0:T(8,128)(2,1)}, u32[]{:S(2)}, u32[]{:S(2)}) collective-permute-start(bf16[8,64,128]{2,1,0:T(8,128)(2,1)} %get-tuple-element.51), channel_id=1, source_target_pairs={{0,2},{1,3},{2,0},{3,1},{4,6},{5,7},{6,4},{7,5},{8,10},{9,11},{10,... | collective-permute-start | bytes 393224 | tf_op jit(solution)/shard_map/ppermute | solution.py:194
  8.6 19.2 %collective-permute-start.32 = (bf16[8,64,128]{2,1,0:T(8,128)(2,1)}, bf16[8,64,128]{2,1,0:T(8,128)(2,1)}, u32[]{:S(2)}, u32[]{:S(2)}) collective-permute-start(bf16[8,64,128]{2,1,0:T(8,128)(2,1)} %get-tuple-element.50), channel_id=1, source_target_pairs={{0,3},{1,0},{2,1},{3,2},{4,7},{5,4},{6,5},{7,6},{8,11},{9,8},{10,9... | collective-permute-start | bytes 393224 | tf_op jit(solution)/shard_map/ppermute | solution.py:194
  24.0 24.1 %collective-permute-start.17 = (bf16[16,64,128]{2,1,0:T(8,128)(2,1)S(1)}, bf16[16,64,128]{2,1,0:T(8,128)(2,1)S(1)}, u32[]{:S(2)}, u32[]{:S(2)}) collective-permute-start(bf16[16,64,128]{2,1,0:T(8,128)(2,1)S(1)} %get-tuple-element.37), channel_id=1, source_target_pairs={{0,20},{16,4},{12,24},{28,8},{1,21},{17,5},{13,25},{29,9},{2,22},{... | collective-permute-start | bytes 786440 | tf_op jit(solution)/shard_map/ppermute | solution.py:249
  26.0 25.3 %collective-permute-start.16 = (bf16[16,64,128]{2,1,0:T(8,128)(2,1)S(1)}, bf16[16,64,128]{2,1,0:T(8,128)(2,1)S(1)}, u32[]{:S(2)}, u32[]{:S(2)}) collective-permute-start(bf16[16,64,128]{2,1,0:T(8,128)(2,1)S(1)} %get-tuple-element.36), channel_id=1, source_target_pairs={{0,4},{4,0},{8,12},{12,8},{16,20},{20,16},{24,28},{28,24},{1,5},{5... | collective-permute-start | bytes 786440 | tf_op jit(solution)/shard_map/ppermute | solution.py:245
  26.8 8.2 %collective-permute-start.27 = (bf16[8,64,128]{2,1,0:T(8,128)(2,1)S(1)}, bf16[8,64,128]{2,1,0:T(8,128)(2,1)S(1)}, u32[]{:S(2)}, u32[]{:S(2)}) collective-permute-start(bf16[8,64,128]{2,1,0:T(8,128)(2,1)S(1)} %get-tuple-element.55), channel_id=1, source_target_pairs={{0,1},{1,2},{2,3},{3,0},{4,5},{5,6},{6,7},{7,4},{8,9},{9,10},{10,1... | collective-permute-start | bytes 393224 | tf_op jit(solution)/shard_map/ppermute | solution.py:194
  27.5 12.7 %collective-permute-start.28 = (bf16[8,64,128]{2,1,0:T(8,128)(2,1)S(1)}, bf16[8,64,128]{2,1,0:T(8,128)(2,1)S(1)}, u32[]{:S(2)}, u32[]{:S(2)}) collective-permute-start(bf16[8,64,128]{2,1,0:T(8,128)(2,1)S(1)} %get-tuple-element.57), channel_id=1, source_target_pairs={{0,2},{1,3},{2,0},{3,1},{4,6},{5,7},{6,4},{7,5},{8,10},{9,11},{10,... | collective-permute-start | bytes 393224 | tf_op jit(solution)/shard_map/ppermute | solution.py:194
  27.8 14.4 %collective-permute-start.29 = (bf16[8,64,128]{2,1,0:T(8,128)(2,1)S(1)}, bf16[8,64,128]{2,1,0:T(8,128)(2,1)S(1)}, u32[]{:S(2)}, u32[]{:S(2)}) collective-permute-start(bf16[8,64,128]{2,1,0:T(8,128)(2,1)S(1)} %get-tuple-element.54), channel_id=1, source_target_pairs={{0,3},{1,0},{2,1},{3,2},{4,7},{5,4},{6,5},{7,6},{8,11},{9,8},{10,9... | collective-permute-start | bytes 393224 | tf_op jit(solution)/shard_map/ppermute | solution.py:194
  35.0 29.9 %collective-permute-start.15 = (bf16[16,64,128]{2,1,0:T(8,128)(2,1)S(1)}, bf16[16,64,128]{2,1,0:T(8,128)(2,1)S(1)}, u32[]{:S(2)}, u32[]{:S(2)}) collective-permute-start(bf16[16,64,128]{2,1,0:T(8,128)(2,1)S(1)} %get-tuple-element.34), channel_id=1, source_target_pairs={{0,4},{4,0},{8,12},{12,8},{16,20},{20,16},{24,28},{28,24},{1,5},{5... | collective-permute-start | bytes 786440 | tf_op jit(solution)/shard_map/ppermute | solution.py:247
  40.2 11.3 %collective-permute-start.5 = (bf16[16,64,128]{2,1,0:T(8,128)(2,1)S(1)}, bf16[16,64,128]{2,1,0:T(8,128)(2,1)}, u32[]{:S(2)}, u32[]{:S(2)}) collective-permute-start(bf16[16,64,128]{2,1,0:T(8,128)(2,1)S(1)} %get-tuple-element.28), channel_id=1, source_target_pairs={{0,20},{16,4},{12,24},{28,8},{1,21},{17,5},{13,25},{29,9},{2,22},{... | collective-permute-start | bytes 786440 | tf_op jit(solution)/shard_map/ppermute | solution.py:249
  42.2 10.0 %collective-permute-start.4 = (bf16[16,64,128]{2,1,0:T(8,128)(2,1)S(1)}, bf16[16,64,128]{2,1,0:T(8,128)(2,1)}, u32[]{:S(2)}, u32[]{:S(2)}) collective-permute-start(bf16[16,64,128]{2,1,0:T(8,128)(2,1)S(1)} %get-tuple-element.27), channel_id=1, source_target_pairs={{0,4},{4,0},{8,12},{12,8},{16,20},{20,16},{24,28},{28,24},{1,5},{5... | collective-permute-start | bytes 786440 | tf_op jit(solution)/shard_map/ppermute | solution.py:245
  48.1 7.3 %collective-permute-start.33 = (bf16[64,256]{1,0:T(8,128)(2,1)S(1)}, bf16[64,256]{1,0:T(8,128)(2,1)S(1)}, u32[]{:S(2)}, u32[]{:S(2)}) collective-permute-start(bf16[64,256]{1,0:T(8,128)(2,1)S(1)} %convert_element_type.142), channel_id=1, source_target_pairs={{0,3},{1,0},{2,1},{3,2},{4,7},{5,4},{6,5},{7,6},{8,11},{9,8},{10,9... | collective-permute-start | bytes 98312 | tf_op jit(solution)/shard_map/ppermute | solution.py:194
  52.1 6.7 %collective-permute-start.19 = (bf16[16,64,128]{2,1,0:T(8,128)(2,1)S(1)}, bf16[16,64,128]{2,1,0:T(8,128)(2,1)S(1)}, u32[]{:S(2)}, u32[]{:S(2)}) collective-permute-start(bf16[16,64,128]{2,1,0:T(8,128)(2,1)S(1)} %get-tuple-element.47), channel_id=1, source_target_pairs={{0,20},{16,4},{12,24},{28,8},{1,21},{17,5},{13,25},{29,9},{2,22},{... | collective-permute-start | bytes 786440 | tf_op jit(solution)/shard_map/ppermute | solution.py:248
  55.4 8.5 %collective-permute-start.7 = (bf16[16,64,128]{2,1,0:T(8,128)(2,1)S(1)}, bf16[16,64,128]{2,1,0:T(8,128)(2,1)S(1)}, u32[]{:S(2)}, u32[]{:S(2)}) collective-permute-start(bf16[16,64,128]{2,1,0:T(8,128)(2,1)S(1)} %get-tuple-element.49), channel_id=1, source_target_pairs={{0,20},{16,4},{12,24},{28,8},{1,21},{17,5},{13,25},{29,9},{2,22},{... | collective-permute-start | bytes 786440 | tf_op jit(solution)/shard_map/ppermute | solution.py:248
  58.1 11.9 %collective-permute-start.18 = (bf16[16,64,128]{2,1,0:T(8,128)(2,1)S(1)}, bf16[16,64,128]{2,1,0:T(8,128)(2,1)S(1)}, u32[]{:S(2)}, u32[]{:S(2)}) collective-permute-start(bf16[16,64,128]{2,1,0:T(8,128)(2,1)S(1)} %get-tuple-element.46), channel_id=1, source_target_pairs={{4,8},{20,24},{8,4},{24,20},{5,9},{21,25},{9,5},{25,21},{6,10},{22... | collective-permute-start | bytes 786440 | tf_op jit(solution)/shard_map/ppermute | solution.py:250
  58.9 11.8 %collective-permute-start.20 = (bf16[16,64,128]{2,1,0:T(8,128)(2,1)S(1)}, bf16[16,64,128]{2,1,0:T(8,128)(2,1)S(1)}, u32[]{:S(2)}, u32[]{:S(2)}) collective-permute-start(bf16[16,64,128]{2,1,0:T(8,128)(2,1)S(1)} %add_convert_fusion.1), channel_id=1, source_target_pairs={{4,12},{20,28},{8,0},{24,16},{5,13},{21,29},{9,1},{25,17},{6,14},{... | collective-permute-start | bytes 786440 | tf_op jit(solution)/shard_map/ppermute | solution.py:251
  60.3 22.4 %collective-permute-start = (bf16[64,256]{1,0:T(8,128)(2,1)S(1)}, bf16[64,256]{1,0:T(8,128)(2,1)S(1)}, u32[]{:S(2)}, u32[]{:S(2)}) collective-permute-start(bf16[64,256]{1,0:T(8,128)(2,1)S(1)} %copy-done.2), channel_id=1, source_target_pairs={{0,3},{1,0},{2,1},{3,2},{4,7},{5,4},{6,5},{7,6},{8,11},{9,8},{10,9... | collective-permute-start | bytes 98312 | tf_op jit(solution)/shard_map/ppermute | solution.py:194
  63.9 19.6 %collective-permute-start.1 = (bf16[64,256]{1,0:T(8,128)(2,1)S(1)}, bf16[64,256]{1,0:T(8,128)(2,1)S(1)}, u32[]{:S(2)}, u32[]{:S(2)}) collective-permute-start(bf16[64,256]{1,0:T(8,128)(2,1)S(1)} %copy-done.2), channel_id=1, source_target_pairs={{0,2},{1,3},{2,0},{3,1},{4,6},{5,7},{6,4},{7,5},{8,10},{9,11},{10,... | collective-permute-start | bytes 98312 | tf_op jit(solution)/shard_map/ppermute | solution.py:194
  64.9 7.9 %collective-permute-start.3 = (bf16[16,64,128]{2,1,0:T(8,128)(2,1)S(1)}, bf16[16,64,128]{2,1,0:T(8,128)(2,1)S(1)}, u32[]{:S(2)}, u32[]{:S(2)}) collective-permute-start(bf16[16,64,128]{2,1,0:T(8,128)(2,1)S(1)} %get-tuple-element.25), channel_id=1, source_target_pairs={{0,4},{4,0},{8,12},{12,8},{16,20},{20,16},{24,28},{28,24},{1,5},{5... | collective-permute-start | bytes 786440 | tf_op jit(solution)/shard_map/ppermute | solution.py:247
  70.7 10.0 %collective-permute-start.8 = (bf16[16,64,128]{2,1,0:T(8,128)(2,1)S(1)}, bf16[16,64,128]{2,1,0:T(8,128)(2,1)S(1)}, u32[]{:S(2)}, u32[]{:S(2)}) collective-permute-start(bf16[16,64,128]{2,1,0:T(8,128)(2,1)S(1)} %add_convert_fusion.5), channel_id=1, source_target_pairs={{4,12},{20,28},{8,0},{24,16},{5,13},{21,29},{9,1},{25,17},{6,14},{... | collective-permute-start | bytes 786440 | tf_op jit(solution)/shard_map/ppermute | solution.py:251
  72.8 13.8 %collective-permute-start.2 = (bf16[64,256]{1,0:T(8,128)(2,1)S(1)}, bf16[64,256]{1,0:T(8,128)(2,1)S(1)}, u32[]{:S(2)}, u32[]{:S(2)}) collective-permute-start(bf16[64,256]{1,0:T(8,128)(2,1)S(1)} %copy-done.2), channel_id=1, source_target_pairs={{0,1},{1,2},{2,3},{3,0},{4,5},{5,6},{6,7},{7,4},{8,9},{9,10},{10,1... | collective-permute-start | bytes 98312 | tf_op jit(solution)/shard_map/ppermute | solution.py:194
  75.7 11.8 %collective-permute-start.37 = (f32[64,256]{1,0:T(8,128)S(1)}, f32[64,256]{1,0:T(8,128)S(1)}, u32[]{:S(2)}, u32[]{:S(2)}) collective-permute-start(f32[64,256]{1,0:T(8,128)S(1)} %add.130), channel_id=1, source_target_pairs={{0,8},{4,12},{8,0},{12,4},{16,24},{20,28},{24,16},{28,20},{1,9},{5... | collective-permute-start | bytes 196616 | tf_op jit(solution)/shard_map/ppermute | solution.py:228
  80.8 7.8 %collective-permute-start.21 = (bf16[4,64,128]{2,1,0:T(8,128)(2,1)S(1)}, bf16[4,64,128]{2,1,0:T(8,128)(2,1)S(1)}, u32[]{:S(2)}, u32[]{:S(2)}) collective-permute-start(bf16[4,64,128]{2,1,0:T(8,128)(2,1)S(1)} %get-tuple-element.60), channel_id=1, source_target_pairs={{0,1},{1,2},{2,3},{3,0},{4,5},{5,6},{6,7},{7,4},{8,9},{9,10},{10,1... | collective-permute-start | bytes 196616 | tf_op jit(solution)/shard_map/ppermute | solution.py:194
  82.7 7.0 %collective-permute-start.22 = (bf16[4,64,128]{2,1,0:T(8,128)(2,1)S(1)}, bf16[4,64,128]{2,1,0:T(8,128)(2,1)S(1)}, u32[]{:S(2)}, u32[]{:S(2)}) collective-permute-start(bf16[4,64,128]{2,1,0:T(8,128)(2,1)S(1)} %get-tuple-element.59), channel_id=1, source_target_pairs={{0,2},{1,3},{2,0},{3,1},{4,6},{5,7},{6,4},{7,5},{8,10},{9,11},{10,... | collective-permute-start | bytes 196616 | tf_op jit(solution)/shard_map/ppermute | solution.py:194
  83.5 6.9 %collective-permute-start.23 = (bf16[4,64,128]{2,1,0:T(8,128)(2,1)S(1)}, bf16[4,64,128]{2,1,0:T(8,128)(2,1)S(1)}, u32[]{:S(2)}, u32[]{:S(2)}) collective-permute-start(bf16[4,64,128]{2,1,0:T(8,128)(2,1)S(1)} %get-tuple-element.58), channel_id=1, source_target_pairs={{0,3},{1,0},{2,1},{3,2},{4,7},{5,4},{6,5},{7,6},{8,11},{9,8},{10,9... | collective-permute-start | bytes 196616 | tf_op jit(solution)/shard_map/ppermute | solution.py:194
  86.7 9.0 %collective-permute-start.10 = (bf16[4,64,128]{2,1,0:T(8,128)(2,1)S(1)}, bf16[4,64,128]{2,1,0:T(8,128)(2,1)S(1)}, u32[]{:S(2)}, u32[]{:S(2)}) collective-permute-start(bf16[4,64,128]{2,1,0:T(8,128)(2,1)S(1)} %get-tuple-element.63), channel_id=1, source_target_pairs={{0,2},{1,3},{2,0},{3,1},{4,6},{5,7},{6,4},{7,5},{8,10},{9,11},{10,... | collective-permute-start | bytes 196616 | tf_op jit(solution)/shard_map/ppermute | solution.py:194
  87.5 11.0 %collective-permute-start.11 = (bf16[4,64,128]{2,1,0:T(8,128)(2,1)S(1)}, bf16[4,64,128]{2,1,0:T(8,128)(2,1)S(1)}, u32[]{:S(2)}, u32[]{:S(2)}) collective-permute-start(bf16[4,64,128]{2,1,0:T(8,128)(2,1)S(1)} %get-tuple-element.62), channel_id=1, source_target_pairs={{0,3},{1,0},{2,1},{3,2},{4,7},{5,4},{6,5},{7,6},{8,11},{9,8},{10,9... | collective-permute-start | bytes 196616 | tf_op jit(solution)/shard_map/ppermute | solution.py:194
  88.6 9.9 %collective-permute-start.9 = (bf16[4,64,128]{2,1,0:T(8,128)(2,1)S(1)}, bf16[4,64,128]{2,1,0:T(8,128)(2,1)S(1)}, u32[]{:S(2)}, u32[]{:S(2)}) collective-permute-start(bf16[4,64,128]{2,1,0:T(8,128)(2,1)S(1)} %get-tuple-element.64), channel_id=1, source_target_pairs={{0,1},{1,2},{2,3},{3,0},{4,5},{5,6},{6,7},{7,4},{8,9},{9,10},{10,1... | collective-permute-start | bytes 196616 | tf_op jit(solution)/shard_map/ppermute | solution.py:194
  89.7 13.5 %collective-permute-start.38 = (f32[64,256]{1,0:T(8,128)S(1)}, f32[64,256]{1,0:T(8,128)S(1)}, u32[]{:S(2)}, u32[]{:S(2)}) collective-permute-start(f32[64,256]{1,0:T(8,128)S(1)} %add.131), channel_id=1, source_target_pairs={{0,16},{4,20},{8,24},{12,28},{16,0},{20,4},{24,8},{28,12},{1,17},{... | collective-permute-start | bytes 196616 | tf_op jit(solution)/shard_map/ppermute | solution.py:228
  93.1 10.2 %collective-permute-start.24 = (bf16[4,64,128]{2,1,0:T(8,128)(2,1)}, bf16[4,64,128]{2,1,0:T(8,128)(2,1)S(1)}, u32[]{:S(2)}, u32[]{:S(2)}) collective-permute-start(bf16[4,64,128]{2,1,0:T(8,128)(2,1)} %get-tuple-element.39), channel_id=1, source_target_pairs={{0,1},{1,2},{2,3},{3,0},{4,5},{5,6},{6,7},{7,4},{8,9},{9,10},{10,1... | collective-permute-start | bytes 196616 | tf_op jit(solution)/shard_map/ppermute | solution.py:194
  95.7 10.6 %collective-permute-start.25 = (bf16[4,64,128]{2,1,0:T(8,128)(2,1)}, bf16[4,64,128]{2,1,0:T(8,128)(2,1)S(1)}, u32[]{:S(2)}, u32[]{:S(2)}) collective-permute-start(bf16[4,64,128]{2,1,0:T(8,128)(2,1)} %get-tuple-element.40), channel_id=1, source_target_pairs={{0,2},{1,3},{2,0},{3,1},{4,6},{5,7},{6,4},{7,5},{8,10},{9,11},{10,... | collective-permute-start | bytes 196616 | tf_op jit(solution)/shard_map/ppermute | solution.py:194
  98.5 7.8 %collective-permute-start.26 = (bf16[4,64,128]{2,1,0:T(8,128)(2,1)}, bf16[4,64,128]{2,1,0:T(8,128)(2,1)S(1)}, u32[]{:S(2)}, u32[]{:S(2)}) collective-permute-start(bf16[4,64,128]{2,1,0:T(8,128)(2,1)} %get-tuple-element.41), channel_id=1, source_target_pairs={{0,3},{1,0},{2,1},{3,2},{4,7},{5,4},{6,5},{7,6},{8,11},{9,8},{10,9... | collective-permute-start | bytes 196616 | tf_op jit(solution)/shard_map/ppermute | solution.py:194
  (28 other events, 191.2 us)

commit v2 on v1

v2 whole, which is shorter than its diff:
```python
import functools
import math

import jax
import jax.numpy as jnp
from jax import lax
from jax.experimental import pallas as pl
from jax.experimental.pallas import tpu as pltpu
from jax.sharding import PartitionSpec as P

REACH = 2
CHUNKS = 2
BF16 = jnp.bfloat16
F32 = jnp.float32


def vmem():
    return pl.BlockSpec(memory_space=pltpu.VMEM)


def smem():
    return pl.BlockSpec(memory_space=pltpu.SMEM)


def hbm():
    return pl.BlockSpec(memory_space=pl.ANY)


def tiles_kernel(slabs, chunk, where, cols, z_ref, tiles_ref, *rest):
    outs, (held, total, sems) = rest[:-3], rest[-3:]
    blocks, slots = tiles_ref.shape[:2]
    window = (2 * REACH + 1) * blocks
    for b in range(blocks):
        pltpu.make_async_copy(tiles_ref.at[b], held.at[b], sems.at[b]).start()

    def clear(i, carry):
        total[i] = jnp.zeros(total.shape[1:], F32)
        return carry

    lax.fori_loop(0, window, clear, 0)
    own = where[0]
    sign = 2 * lax.rem(own, 2) - 1

    def row_block(b, carry):
        pltpu.make_async_copy(tiles_ref.at[b], held.at[b], sems.at[b]).wait()
        z = z_ref[b]
        live = cols[b, slots]
        for s in range(slots):
            col = cols[b, s]
            slab = lax.div(col, blocks)
            offset = lax.rem(slab - own + REACH + slabs, slabs) - REACH
            place = (offset * sign + REACH) * blocks + lax.rem(col, blocks)
            place = jnp.where(s < live, place, window)
            total[place] += jnp.dot(z, held[b, s], preferred_element_type=F32)
        return carry

    lax.fori_loop(0, blocks, row_block, 0)

    parts = 2 * REACH + 1
    chunks = blocks // chunk
    for part in range(parts):
        for k in range(chunks):

            def store(i, carry, out=outs[part * chunks + k], base=part * blocks + k * chunk):
                out[i] = total[base + i].astype(BF16)
                return carry

            lax.fori_loop(0, chunk, store, 0)


def contributions(where, cols, z, tiles, slabs, chunk):
    blocks, features, nodes = z.shape
    slots = tiles.shape[1]
    chunks = blocks // chunk
    parts = 2 * REACH + 1
    window = parts * blocks
    outs = pl.pallas_call(
        functools.partial(tiles_kernel, slabs, chunk),
        out_shape=[jax.ShapeDtypeStruct((chunk, features, nodes), BF16)] * (parts * chunks),
        in_specs=[smem(), smem(), vmem(), hbm()],
        out_specs=[vmem()] * (parts * chunks),
        scratch_shapes=[
            pltpu.VMEM(tiles.shape, BF16),
            pltpu.VMEM((window + 1, features, nodes), F32),
            pltpu.SemaphoreType.DMA((blocks,)),
        ],
        compiler_params=pltpu.CompilerParams(vmem_limit_bytes=40 << 20),
        cost_estimate=pl.CostEstimate(
            flops=2 * blocks * slots * features * nodes * nodes,
            bytes_accessed=tiles.size * 2 + 6 * z.size * 2,
            transcendentals=0,
        ),
    )(where, cols, z, tiles)
    return [outs[part * chunks : (part + 1) * chunks] for part in range(parts)]


def weight_kernel(reps, parts, packed, out, whole_z, whole_a):
    blocks, features = packed.shape[1] // parts, packed.shape[2]
    for q in range(reps):
        rows = pl.ds(q * features, features)
        whole_z[:, rows, :] = packed[q, :blocks]
        whole_a[:, rows, :] = packed[q, blocks : 2 * blocks]
    total = jnp.zeros((reps * features, reps * features), F32)
    for b in range(blocks):
        total += lax.dot_general(
            whole_a[b], whole_z[b], (((1,), (1,)), ((), ())), preferred_element_type=F32
        )
    out[...] = total.astype(BF16)


def weight_partial(packed, parts):
    reps, packs, features, nodes = packed.shape
    blocks = packs // parts
    width = reps * features
    return pl.pallas_call(
        functools.partial(weight_kernel, reps, parts),
        out_shape=jax.ShapeDtypeStruct((width, width), BF16),
        in_specs=[vmem()],
        out_specs=vmem(),
        scratch_shapes=[pltpu.VMEM((blocks, width, nodes), BF16)] * 2,
        cost_estimate=pl.CostEstimate(
            flops=2 * blocks * nodes * width * width,
            bytes_accessed=4 * blocks * nodes * width + 2 * width * width,
            transcendentals=0,
        ),
    )(packed)


def mix_kernel(reps, weights, shares, out, whole):
    blocks, features = shares.shape[1:3]
    for q in range(reps):
        whole[:, pl.ds(q * features, features), :] = shares[q]
    for b in range(blocks):
        mixed = jnp.dot(weights[...], whole[b], preferred_element_type=F32)
        for q in range(reps):
            out[q, b] = mixed[q * features : (q + 1) * features].astype(BF16)


def mix(weights, shares):
    reps, blocks, features, nodes = shares.shape
    width = reps * features
    return pl.pallas_call(
        functools.partial(mix_kernel, reps),
        out_shape=jax.ShapeDtypeStruct(shares.shape, BF16),
        in_specs=[vmem(), vmem()],
        out_specs=vmem(),
        scratch_shapes=[pltpu.VMEM((blocks, width, nodes), BF16)],
        cost_estimate=pl.CostEstimate(
            flops=2 * blocks * nodes * width * width,
            bytes_accessed=4 * blocks * nodes * width,
            transcendentals=0,
        ),
    )(weights, shares)


def exchange(value, axis):
    return lax.all_to_all(value, axis, 0, 0, tiled=True)


def on_device(cotangent, relu_mask, aggregated, weight, tiles, col_block, live_count):
    blocks, features, nodes = cotangent.shape
    slabs, reps = lax.axis_size("blk"), lax.axis_size("rep")
    width = weight.shape[1]
    chunk = blocks // CHUNKS
    share = blocks // reps
    where = lax.axis_index("blk").astype(jnp.int32)[None]
    cols = jnp.concatenate([col_block, live_count[:, None]], axis=1)

    grad_z = cotangent * relu_mask.astype(BF16)
    by_share = (reps, share, features, nodes)
    packed = jnp.concatenate([grad_z.reshape(by_share), aggregated.reshape(by_share)], axis=1)
    packed = exchange(packed, "rep")
    weights = exchange(jnp.broadcast_to(weight[None], (reps, features, width)), "rep")
    weights = weights.reshape(reps * features, width)

    near, beside, own, first, second = contributions(where, cols, grad_z, tiles, slabs, chunk)

    pair = [(i, i ^ 1) for i in range(slabs)]
    to_one = [(i, (i + (1 if i % 2 else -1)) % slabs) for i in range(slabs)]
    to_two = [(i, (i + (2 if i % 2 else -2)) % slabs) for i in range(slabs)]

    def add(*terms):
        return sum(term.astype(F32) for term in terms).astype(BF16)

    grad_w = weight_partial(packed, 2).reshape(reps, features, width)
    mixed = []
    for k in range(CHUNKS):
        one = add(first[k], lax.ppermute(near[k], "blk", pair))
        held = lax.ppermute(beside[k], "blk", pair)
        two_in = lax.ppermute(second[k], "blk", to_two)
        one_in = lax.ppermute(one, "blk", to_one)
        sums = add(own[k], held, one_in, two_in)
        shares = exchange(sums.reshape(reps, chunk // reps, features, nodes), "rep")
        mixed.append(exchange(mix(weights, shares), "rep").reshape(chunk, features, nodes))

    grad_w = exchange(grad_w, "rep").astype(F32).sum(0)
    step = 1
    while step < slabs:
        grad_w = grad_w + lax.ppermute(grad_w, "blk", [(i, i ^ step) for i in range(slabs)])
        step *= 2
    weight_grad = grad_w * (1.0 / math.sqrt(slabs * blocks * nodes))
    return jnp.concatenate(mixed, axis=0), weight_grad


def solution(mesh):
    placed = (
        P("blk", "rep", None),
        P("blk", "rep", None),
        P("blk", "rep", None),
        P("rep", None),
        P("blk", None, None, None),
        P("blk", None),
        P("blk"),
    )
    return jax.shard_map(
        on_device,
        mesh=mesh,
        in_specs=placed,
        out_specs=(P("blk", "rep", None), P("rep", None)),
        check_vma=False,
    )
```

time: 128 us -> 126 us (0.984)
  waiting for transfers between devices: 15.3 us -> 50.6 us
  Pallas kernels: 36.9 us -> 18.7 us
  starting transfers between devices: 58.8 us -> 43.6 us
  local copies, waits for them, and re-layouts: 6.88 us -> 2.24 us
    all_to_all x0 -> x7, waiting for transfers between devices: none -> 41 us  [exchange(): return lax.all_to_all(value, axis, 0, 0, tiled=True)]
    ppermute x35 -> x7, starting transfers between devices: 53.6 us -> 15.9 us  [the longest x3 8.89 us: on_device(): lax.ppermute(grad_w, 'blk', [(i, i ^ step) for i in range(slabs)])]
    all_to_all x0 -> x7, starting transfers between devices: none -> 26.8 us  [exchange(): return lax.all_to_all(value, axis, 0, 0, tiled=True)]
    pallas_call x4 -> x3, Pallas kernels: 24.6 us -> 6.37 us  [the longest x2 4.04 us: mix(): pl.pallas_call(functools.partial(mix_kernel, reps), out_shape=jax.ShapeDt...]
    ppermute x35 -> x7, waiting for transfers between devices: 15.3 us -> 9.57 us  [the longest x3 5.06 us: on_device(): lax.ppermute(grad_w, 'blk', [(i, i ^ step) for i in range(slabs)])]
    ppermute x2, starting transfers between devices: 5.07 us -> 0.33 us  [on_device(): held = lax.ppermute(beside[k], 'blk', pair)]
    convert_element_type x6 -> x4, other arithmetic: 1.82 us -> 5.37 us  [add(): return sum((term.astype(F32) for term in terms)).astype(BF16)]
    dynamic_slice x4 -> x0, local copies, waits for them, and re-layouts: 2.87 us -> none  [node_share(): return lax.dynamic_slice_in_dim(value, first, blocks, 0)]
  transfers between devices with their start and end apart: 39 -> 18, of which waited for: 8 -> 10; matrix products, arithmetic and copies ran while one was open for 8% -> 6% of each run, Pallas kernels for 15% -> 5%
where the time goes in v2:
time: 126 us; the launch traced here: 125 us
  waiting for transfers between devices  50.6 us (40%)
  starting transfers between devices  43.6 us (35%)
  Pallas kernels  18.7 us (15%)
  other arithmetic  9.51 us (8%)
  local copies, waits for them, and re-layouts  2.24 us (2%)
    all_to_all x7, waiting for transfers between devices, exchange(): return lax.all_to_all(value, axis, 0, 0, tiled=True)  41 us
    all_to_all x7, starting transfers between devices, exchange(): return lax.all_to_all(value, axis, 0, 0, tiled=True)  26.8 us
    pallas_call x1, Pallas kernels, contributions(): pl.pallas_call(functools.partial(tiles_kernel, slabs, chunk), out_shape=[...  12.4 us
    ppermute x3, starting transfers between devices, on_device(): lax.ppermute(grad_w, 'blk', [(i, i ^ step) for i in range(slabs)])  8.89 us
    ppermute x2, starting transfers between devices, on_device(): two_in = lax.ppermute(second[k], 'blk', to_two)  5.61 us
    convert_element_type x4, other arithmetic, add(): return sum((term.astype(F32) for term in terms)).astype(BF16)  5.37 us
    ppermute x3, waiting for transfers between devices, on_device(): lax.ppermute(grad_w, 'blk', [(i, i ^ step) for i in range(slabs)])  5.06 us
    ppermute x2, waiting for transfers between devices, on_device(): one_in = lax.ppermute(one, 'blk', to_one)  4.51 us
  transfers between devices with their start and end apart: 18, of which 10 were waited for; matrix products, arithmetic and copies ran while one was open for 6% of the time, Pallas kernels for 5%

profile of v2, /device:TPU:0, one launch (start us, length us, event | category | flops | bytes accessed | tf_op | source)
XLA Modules:
  0.0 125.5 jit_solution(13312454891306105685)
XLA Ops:
  0.7 0.8 copy.9
  2.3 1.5 %convert_multiply_fusion.z_ref = bf16[32,64,128]{2,1,0:T(8,128)(2,1)S(1)} fusion(bf16[32,64,128]{2,1,0:T(8,128)(2,1)} %param.7, s32[32,64,128]{2,1,0:T(8,128)} %param.8), kind=kLoop, calls=%fused_computation.6 | loop fusion | flops 524288 | bytes 2097152 | tf_op jit(solution)/shard_map/mul | solution.py:169
  3.8 12.4 %shard_map.86 = (bf16[16,64,128]{2,1,0:T(8,128)(2,1)S(1)}, bf16[16,64,128]{2,1,0:T(8,128)(2,1)S(1)}, bf16[16,64,128]{2,1,0:T(8,128)(2,1)S(1)}, bf16[16,64,128]{2...) custom-call(s32[1]{0:T(128)} %bitcast.1.where, ...), custom_call_target="tpu_custom_call" | custom-call | flops 1073741824 | bytes 19922944 | tf_op jit(solution)/shard_map/pallas_call | solution.py:77
  17.0 3.5 %collective-permute-start.3 = (bf16[16,64,128]{2,1,0:T(8,128)(2,1)S(1)}, bf16[16,64,128]{2,1,0:T(8,128)(2,1)}, u32[]{:S(2)}, u32[]{:S(2)}) collective-permute-start(bf16[16,64,128]{2,1,0:T(8,128)(2,1)S(1)} %get-tuple-element.16), channel_id=1, source_target_pairs={{0,24},{4,12},{8,0},{12,20},{16,8},{20,28},{24,16},{28,4},{1,25},{... | collective-permute-start | bytes 786440 | tf_op jit(solution)/shard_map/ppermute | solution.py:190
  22.7 4.9 %all-to-all-start = ((bf16[4,64,256]{2,1,0:T(8,128)(2,1)}), bf16[4,64,256]{2,1,0:T(8,128)(2,1)S(1)}, u32[]{:S(2)}, u32[]{:S(2)}) async-start(bf16[4,64,256]{2,1,0:T(8,128)(2,1)} %broadcast_in_dim.12), calls=%async_computation | async-start | bytes 262144 | tf_op jit(solution)/shard_map/all_to_all | solution.py:157
  27.6 2.1 %collective-permute-start.7 = (bf16[16,64,128]{2,1,0:T(8,128)(2,1)S(1)}, bf16[16,64,128]{2,1,0:T(8,128)(2,1)S(1)}, u32[]{:S(2)}, u32[]{:S(2)}) collective-permute-start(bf16[16,64,128]{2,1,0:T(8,128)(2,1)S(1)} %get-tuple-element.21), channel_id=1, source_target_pairs={{0,24},{4,12},{8,0},{12,20},{16,8},{20,28},{24,16},{28,4},{1,25},{... | collective-permute-start | bytes 786440 | tf_op jit(solution)/shard_map/ppermute | solution.py:190
  29.7 1.7 %add_convert_fusion.1 = bf16[16,64,128]{2,1,0:T(8,128)(2,1)} fusion(bf16[16,64,128]{2,1,0:T(8,128)(2,1)} %collective-permute-done.5, bf16[16,64,128]{2,1,0:T(8,128)(2,1)S(1)} %get-tuple-element.19), kind=kLoop, calls=%fused_computation.3 | loop fusion | flops 524288 | bytes 786432 | tf_op jit(solution)/shard_map/convert_element_type | solution.py:183
  32.1 1.0 collective-permute-done.2
  33.1 2.0 %add_convert_fusion.2 = bf16[16,64,128]{2,1,0:T(8,128)(2,1)} fusion(bf16[16,64,128]{2,1,0:T(8,128)(2,1)} %collective-permute-done.3, bf16[16,64,128]{2,1,0:T(8,128)(2,1)} %collective-permute-done.2, bf16[16,64,128]{2,1,0:T(8,128)(2,1)} %collective-permute-done, bf16[16,64,128]{2,1,0:T(8,128)(2,1)S(1)} %get-tuple-element.12), kind=kLoop, calls=%fused_computation.4 | loop fusion | flops 1048576 | bytes 1310720 | tf_op jit(solution)/shard_map/convert_element_type | solution.py:183
  35.1 4.9 %all-to-all-start.1 = ((bf16[4,4,64,128]{3,2,1,0:T(8,128)(2,1)}), bf16[4,4,64,128]{3,2,1,0:T(8,128)(2,1)S(1)}, u32[]{:S(2)}, u32[]{:S(2)}) async-start(bf16[4,4,64,128]{3,2,1,0:T(8,128)(2,1)} %bitcast.3), calls=%async_computation.1 | async-start | bytes 524288 | tf_op jit(solution)/shard_map/all_to_all | solution.py:157
  39.9 3.5 %collective-permute-done.6 = bf16[16,64,128]{2,1,0:T(8,128)(2,1)S(1)} collective-permute-done((bf16[16,64,128]{2,1,0:T(8,128)(2,1)}, bf16[16,64,128]{2,1,0:T(8,128)(2,1)S(1)}, u32[]{:S(2)}, u32[]{:S(2)}) %collective-permute-start.6) | collective-permute-done | bytes 262176 | tf_op jit(solution)/shard_map/ppermute | solution.py:191
  43.5 0.9 add_convert_fusion
  44.3 4.6 %all-to-all-done.1.shares = bf16[4,4,64,128]{3,2,1,0:T(8,128)(2,1)S(1)} async-done(((bf16[4,4,64,128]{3,2,1,0:T(8,128)(2,1)}), bf16[4,4,64,128]{3,2,1,0:T(8,128)(2,1)S(1)}, u32[]{:S(2)}, u32[]{:S(2)}) %all-to-all-start.1) | async-done | bytes 262176 | tf_op jit(solution)/shard_map/all_to_all | solution.py:157
  48.9 3.4 %all-to-all-start.3 = ((bf16[4,4,64,128]{3,2,1,0:T(8,128)(2,1)}), bf16[4,4,64,128]{3,2,1,0:T(8,128)(2,1)S(1)}, u32[]{:S(2)}, u32[]{:S(2)}) async-start(bf16[4,4,64,128]{3,2,1,0:T(8,128)(2,1)} %bitcast.5), calls=%async_computation.3 | async-start | bytes 524288 | tf_op jit(solution)/shard_map/all_to_all | solution.py:157
  52.3 1.1 pad_maximum_fusion
  53.4 5.9 %all-to-all-done.3.shares = bf16[4,4,64,128]{3,2,1,0:T(8,128)(2,1)S(1)} async-done(((bf16[4,4,64,128]{3,2,1,0:T(8,128)(2,1)}), bf16[4,4,64,128]{3,2,1,0:T(8,128)(2,1)S(1)}, u32[]{:S(2)}, u32[]{:S(2)}) %all-to-all-start.3) | async-done | bytes 262176 | tf_op jit(solution)/shard_map/all_to_all | solution.py:157
  59.3 3.5 %all-to-all-start.5 = ((bf16[4,16,64,128]{3,2,1,0:T(8,128)(2,1)}), bf16[4,16,64,128]{3,2,1,0:T(8,128)(2,1)S(1)}, u32[]{:S(2)}, u32[]{:S(2)}) async-start(bf16[4,16,64,128]{3,2,1,0:T(8,128)(2,1)} %pad_maximum_fusion), calls=%async_computation.5 | async-start | bytes 2097152 | tf_op jit(solution)/shard_map/all_to_all | solution.py:157
  62.8 2.0 %shard_map.87 = bf16[4,4,64,128]{3,2,1,0:T(8,128)(2,1)} custom-call(bf16[256,256]{1,0:T(8,128)(2,1)} %bitcast.11, bf16[4,4,64,128]{3,2,1,0:T(8,128)(2,1)} %copy-done.2), custom_call_target="tpu_custom_call" | custom-call | flops 67108864 | bytes 524288 | tf_op jit(solution)/shard_map/pallas_call | solution.py:142
  64.9 20.9 %all-to-all-done.5.packed = bf16[4,16,64,128]{3,2,1,0:T(8,128)(2,1)S(1)} async-done(((bf16[4,16,64,128]{3,2,1,0:T(8,128)(2,1)}), bf16[4,16,64,128]{3,2,1,0:T(8,128)(2,1)S(1)}, u32[]{:S(2)}, u32[]{:S(2)}) %all-to-all-start.5) | async-done | bytes 1048608 | tf_op jit(solution)/shard_map/all_to_all | solution.py:157
  85.8 3.4 %all-to-all-start.2 = ((bf16[4,4,64,128]{3,2,1,0:T(8,128)(2,1)}), bf16[4,4,64,128]{3,2,1,0:T(8,128)(2,1)S(1)}, u32[]{:S(2)}, u32[]{:S(2)}) async-start(bf16[4,4,64,128]{3,2,1,0:T(8,128)(2,1)} %shard_map.87), calls=%async_computation.2 | async-start | bytes 524288 | tf_op jit(solution)/shard_map/all_to_all | solution.py:157
  89.2 2.3 %shard_map.89 = bf16[256,256]{1,0:T(8,128)(2,1)} custom-call(bf16[4,16,64,128]{3,2,1,0:T(8,128)(2,1)} %copy-done), custom_call_target="tpu_custom_call" | custom-call | flops 134217728 | bytes 1179648 | tf_op jit(solution)/shard_map/pallas_call | solution.py:115
  91.5 5.8 %all-to-all-done.2 = bf16[4,4,64,128]{3,2,1,0:T(8,128)(2,1)S(1)} async-done(((bf16[4,4,64,128]{3,2,1,0:T(8,128)(2,1)}), bf16[4,4,64,128]{3,2,1,0:T(8,128)(2,1)S(1)}, u32[]{:S(2)}, u32[]{:S(2)}) %all-to-all-start.2) | async-done | bytes 262176 | tf_op jit(solution)/shard_map/all_to_all | solution.py:157
  97.3 3.3 %all-to-all-start.6 = ((bf16[4,64,256]{2,1,0:T(8,128)(2,1)}), bf16[4,64,256]{2,1,0:T(8,128)(2,1)S(1)}, u32[]{:S(2)}, u32[]{:S(2)}) async-start(bf16[4,64,256]{2,1,0:T(8,128)(2,1)} %bitcast.15), calls=%async_computation.6 | async-start | bytes 262144 | tf_op jit(solution)/shard_map/all_to_all | solution.py:157
  100.7 2.0 %shard_map.88 = bf16[4,4,64,128]{3,2,1,0:T(8,128)(2,1)} custom-call(bf16[256,256]{1,0:T(8,128)(2,1)} %bitcast.12, bf16[4,4,64,128]{3,2,1,0:T(8,128)(2,1)} %copy-done.3), custom_call_target="tpu_custom_call" | custom-call | flops 67108864 | bytes 524288 | tf_op jit(solution)/shard_map/pallas_call | solution.py:142
  102.7 3.9 %all-to-all-done.6 = bf16[4,64,256]{2,1,0:T(8,128)(2,1)S(1)} async-done(((bf16[4,64,256]{2,1,0:T(8,128)(2,1)}), bf16[4,64,256]{2,1,0:T(8,128)(2,1)S(1)}, u32[]{:S(2)}, u32[]{:S(2)}) %all-to-all-start.6) | async-done | bytes 131104 | tf_op jit(solution)/shard_map/all_to_all | solution.py:157
  106.6 3.4 %all-to-all-start.4 = ((bf16[4,4,64,128]{3,2,1,0:T(8,128)(2,1)}), bf16[4,4,64,128]{3,2,1,0:T(8,128)(2,1)S(1)}, u32[]{:S(2)}, u32[]{:S(2)}) async-start(bf16[4,4,64,128]{3,2,1,0:T(8,128)(2,1)} %shard_map.88), calls=%async_computation.4 | async-start | bytes 524288 | tf_op jit(solution)/shard_map/all_to_all | solution.py:157
  110.1 1.2 collective-permute-done.8
  111.3 6.5 %collective-permute-start.9 = (f32[64,256]{1,0:T(8,128)S(1)}, f32[64,256]{1,0:T(8,128)S(1)}, u32[]{:S(2)}, u32[]{:S(2)}) collective-permute-start(f32[64,256]{1,0:T(8,128)S(1)} %add.41), channel_id=1, source_target_pairs={{0,8},{4,12},{8,0},{12,4},{16,24},{20,28},{24,16},{28,20},{1,9},{5... | collective-permute-start | bytes 196616 | tf_op jit(solution)/shard_map/ppermute | solution.py:199
  117.9 2.4 %collective-permute-done.9 = f32[64,256]{1,0:T(8,128)S(1)} collective-permute-done((f32[64,256]{1,0:T(8,128)S(1)}, f32[64,256]{1,0:T(8,128)S(1)}, u32[]{:S(2)}, u32[]{:S(2)}) %collective-permute-start.9) | collective-permute-done | bytes 65568 | tf_op jit(solution)/shard_map/ppermute | solution.py:199
  120.3 2.3 %collective-permute-start.10 = (f32[64,256]{1,0:T(8,128)S(1)}, f32[64,256]{1,0:T(8,128)S(1)}, u32[]{:S(2)}, u32[]{:S(2)}) collective-permute-start(f32[64,256]{1,0:T(8,128)S(1)} %add.42), channel_id=1, source_target_pairs={{0,16},{4,20},{8,24},{12,28},{16,0},{20,4},{24,8},{28,12},{1,17},{... | collective-permute-start | bytes 196616 | tf_op jit(solution)/shard_map/ppermute | solution.py:199
  122.6 0.8 pad_maximum_fusion.1
  123.4 1.4 %collective-permute-done.10 = f32[64,256]{1,0:T(8,128)S(1)} collective-permute-done((f32[64,256]{1,0:T(8,128)S(1)}, f32[64,256]{1,0:T(8,128)S(1)}, u32[]{:S(2)}, u32[]{:S(2)}) %collective-permute-start.10) | collective-permute-done | bytes 65568 | tf_op jit(solution)/shard_map/ppermute | solution.py:199
  (35 shorter events, 5.3 us)
Async XLA Ops:
  0.6 21.4 %copy-start.5 = (bf16[64,256]{1,0:T(8,128)(2,1)S(1)}, bf16[64,256]{1,0:T(8,128)(2,1)}, u32[]{:S(2)}) copy-start(bf16[64,256]{1,0:T(8,128)(2,1)} %param.10) | copy-start | bytes 98308
  0.6 51.7 %copy-start.4 = (bf16[32,64,128]{2,1,0:T(8,128)(2,1)S(1)}, bf16[32,64,128]{2,1,0:T(8,128)(2,1)}, u32[]{:S(2)}) copy-start(bf16[32,64,128]{2,1,0:T(8,128)(2,1)} %param.9) | copy-start | bytes 1572868
  16.1 4.5 %collective-permute-start.1 = (bf16[16,64,128]{2,1,0:T(8,128)(2,1)S(1)}, bf16[16,64,128]{2,1,0:T(8,128)(2,1)S(1)}, u32[]{:S(2)}, u32[]{:S(2)}) collective-permute-start(bf16[16,64,128]{2,1,0:T(8,128)(2,1)S(1)} %get-tuple-element.15), channel_id=1, source_target_pairs={{0,4},{4,0},{8,12},{12,8},{16,20},{20,16},{24,28},{28,24},{1,5},{5... | collective-permute-start | bytes 786440 | tf_op jit(solution)/shard_map/ppermute | solution.py:188
  16.5 11.0 %collective-permute-start.5 = (bf16[16,64,128]{2,1,0:T(8,128)(2,1)S(1)}, bf16[16,64,128]{2,1,0:T(8,128)(2,1)}, u32[]{:S(2)}, u32[]{:S(2)}) collective-permute-start(bf16[16,64,128]{2,1,0:T(8,128)(2,1)S(1)} %get-tuple-element.20), channel_id=1, source_target_pairs={{0,4},{4,0},{8,12},{12,8},{16,20},{20,16},{24,28},{28,24},{1,5},{5... | collective-permute-start | bytes 786440 | tf_op jit(solution)/shard_map/ppermute | solution.py:188
  16.7 14.7 %collective-permute-start = (bf16[16,64,128]{2,1,0:T(8,128)(2,1)S(1)}, bf16[16,64,128]{2,1,0:T(8,128)(2,1)}, u32[]{:S(2)}, u32[]{:S(2)}) collective-permute-start(bf16[16,64,128]{2,1,0:T(8,128)(2,1)S(1)} %get-tuple-element.13), channel_id=1, source_target_pairs={{0,4},{4,0},{8,12},{12,8},{16,20},{20,16},{24,28},{28,24},{1,5},{5... | collective-permute-start | bytes 786440 | tf_op jit(solution)/shard_map/ppermute | solution.py:189
  17.0 15.0 %collective-permute-start.3 = (bf16[16,64,128]{2,1,0:T(8,128)(2,1)S(1)}, bf16[16,64,128]{2,1,0:T(8,128)(2,1)}, u32[]{:S(2)}, u32[]{:S(2)}) collective-permute-start(bf16[16,64,128]{2,1,0:T(8,128)(2,1)S(1)} %get-tuple-element.16), channel_id=1, source_target_pairs={{0,24},{4,12},{8,0},{12,20},{16,8},{20,28},{24,16},{28,4},{1,25},{... | collective-permute-start | bytes 786440 | tf_op jit(solution)/shard_map/ppermute | solution.py:190
  21.4 11.7 %collective-permute-start.2 = (bf16[16,64,128]{2,1,0:T(8,128)(2,1)}, bf16[16,64,128]{2,1,0:T(8,128)(2,1)}, u32[]{:S(2)}, u32[]{:S(2)}) collective-permute-start(bf16[16,64,128]{2,1,0:T(8,128)(2,1)} %add_convert_fusion.3), channel_id=1, source_target_pairs={{0,28},{4,8},{8,4},{12,16},{16,12},{20,24},{24,20},{28,0},{1,29},{... | collective-permute-start | bytes 786440 | tf_op jit(solution)/shard_map/ppermute | solution.py:191
  22.7 12.4 %all-to-all-start = ((bf16[4,64,256]{2,1,0:T(8,128)(2,1)}), bf16[4,64,256]{2,1,0:T(8,128)(2,1)S(1)}, u32[]{:S(2)}, u32[]{:S(2)}) async-start(bf16[4,64,256]{2,1,0:T(8,128)(2,1)} %broadcast_in_dim.12), calls=%async_computation | async-start | bytes 262144 | tf_op jit(solution)/shard_map/all_to_all | solution.py:157
  27.6 12.4 %collective-permute-start.4 = (bf16[16,64,128]{2,1,0:T(8,128)(2,1)S(1)}, bf16[16,64,128]{2,1,0:T(8,128)(2,1)S(1)}, u32[]{:S(2)}, u32[]{:S(2)}) collective-permute-start(bf16[16,64,128]{2,1,0:T(8,128)(2,1)S(1)} %get-tuple-element.18), channel_id=1, source_target_pairs={{0,4},{4,0},{8,12},{12,8},{16,20},{20,16},{24,28},{28,24},{1,5},{5... | collective-permute-start | bytes 786440 | tf_op jit(solution)/shard_map/ppermute | solution.py:189
  27.6 12.4 %collective-permute-start.7 = (bf16[16,64,128]{2,1,0:T(8,128)(2,1)S(1)}, bf16[16,64,128]{2,1,0:T(8,128)(2,1)S(1)}, u32[]{:S(2)}, u32[]{:S(2)}) collective-permute-start(bf16[16,64,128]{2,1,0:T(8,128)(2,1)S(1)} %get-tuple-element.21), channel_id=1, source_target_pairs={{0,24},{4,12},{8,0},{12,20},{16,8},{20,28},{24,16},{28,4},{1,25},{... | collective-permute-start | bytes 786440 | tf_op jit(solution)/shard_map/ppermute | solution.py:190
  31.4 12.1 %collective-permute-start.6 = (bf16[16,64,128]{2,1,0:T(8,128)(2,1)}, bf16[16,64,128]{2,1,0:T(8,128)(2,1)S(1)}, u32[]{:S(2)}, u32[]{:S(2)}) collective-permute-start(bf16[16,64,128]{2,1,0:T(8,128)(2,1)} %add_convert_fusion.1), channel_id=1, source_target_pairs={{0,28},{4,8},{8,4},{12,16},{16,12},{20,24},{24,20},{28,0},{1,29},{... | collective-permute-start | bytes 786440 | tf_op jit(solution)/shard_map/ppermute | solution.py:191
  35.1 27.8 %copy-start.1 = (bf16[4,64,256]{2,1,0:T(8,128)(2,1)}, bf16[4,64,256]{2,1,0:T(8,128)(2,1)S(1)}, u32[]{:S(2)}) copy-start(bf16[4,64,256]{2,1,0:T(8,128)(2,1)S(1)} %all-to-all-done) | copy-start | bytes 393220
  35.1 13.8 %all-to-all-start.1 = ((bf16[4,4,64,128]{3,2,1,0:T(8,128)(2,1)}), bf16[4,4,64,128]{3,2,1,0:T(8,128)(2,1)S(1)}, u32[]{:S(2)}, u32[]{:S(2)}) async-start(bf16[4,4,64,128]{3,2,1,0:T(8,128)(2,1)} %bitcast.3), calls=%async_computation.1 | async-start | bytes 524288 | tf_op jit(solution)/shard_map/all_to_all | solution.py:157
  48.9 13.9 %copy-start.2 = (bf16[4,4,64,128]{3,2,1,0:T(8,128)(2,1)}, bf16[4,4,64,128]{3,2,1,0:T(8,128)(2,1)S(1)}, u32[]{:S(2)}) copy-start(bf16[4,4,64,128]{3,2,1,0:T(8,128)(2,1)S(1)} %all-to-all-done.1.shares) | copy-start | bytes 786436
  48.9 10.4 %all-to-all-start.3 = ((bf16[4,4,64,128]{3,2,1,0:T(8,128)(2,1)}), bf16[4,4,64,128]{3,2,1,0:T(8,128)(2,1)S(1)}, u32[]{:S(2)}, u32[]{:S(2)}) async-start(bf16[4,4,64,128]{3,2,1,0:T(8,128)(2,1)} %bitcast.5), calls=%async_computation.3 | async-start | bytes 524288 | tf_op jit(solution)/shard_map/all_to_all | solution.py:157
  59.3 41.4 %copy-start.3 = (bf16[4,4,64,128]{3,2,1,0:T(8,128)(2,1)}, bf16[4,4,64,128]{3,2,1,0:T(8,128)(2,1)S(1)}, u32[]{:S(2)}) copy-start(bf16[4,4,64,128]{3,2,1,0:T(8,128)(2,1)S(1)} %all-to-all-done.3.shares) | copy-start | bytes 786436
  59.3 26.5 %all-to-all-start.5 = ((bf16[4,16,64,128]{3,2,1,0:T(8,128)(2,1)}), bf16[4,16,64,128]{3,2,1,0:T(8,128)(2,1)S(1)}, u32[]{:S(2)}, u32[]{:S(2)}) async-start(bf16[4,16,64,128]{3,2,1,0:T(8,128)(2,1)} %pad_maximum_fusion), calls=%async_computation.5 | async-start | bytes 2097152 | tf_op jit(solution)/shard_map/all_to_all | solution.py:157
  85.8 3.4 %copy-start = (bf16[4,16,64,128]{3,2,1,0:T(8,128)(2,1)}, bf16[4,16,64,128]{3,2,1,0:T(8,128)(2,1)S(1)}, u32[]{:S(2)}) copy-start(bf16[4,16,64,128]{3,2,1,0:T(8,128)(2,1)S(1)} %all-to-all-done.5.packed) | copy-start | bytes 3145732
  85.8 11.6 %all-to-all-start.2 = ((bf16[4,4,64,128]{3,2,1,0:T(8,128)(2,1)}), bf16[4,4,64,128]{3,2,1,0:T(8,128)(2,1)S(1)}, u32[]{:S(2)}, u32[]{:S(2)}) async-start(bf16[4,4,64,128]{3,2,1,0:T(8,128)(2,1)} %shard_map.87), calls=%async_computation.2 | async-start | bytes 524288 | tf_op jit(solution)/shard_map/all_to_all | solution.py:157
  97.3 9.2 %all-to-all-start.6 = ((bf16[4,64,256]{2,1,0:T(8,128)(2,1)}), bf16[4,64,256]{2,1,0:T(8,128)(2,1)S(1)}, u32[]{:S(2)}, u32[]{:S(2)}) async-start(bf16[4,64,256]{2,1,0:T(8,128)(2,1)} %bitcast.15), calls=%async_computation.6 | async-start | bytes 262144 | tf_op jit(solution)/shard_map/all_to_all | solution.py:157
  106.6 16.0 %all-to-all-start.4 = ((bf16[4,4,64,128]{3,2,1,0:T(8,128)(2,1)}), bf16[4,4,64,128]{3,2,1,0:T(8,128)(2,1)S(1)}, u32[]{:S(2)}, u32[]{:S(2)}) async-start(bf16[4,4,64,128]{3,2,1,0:T(8,128)(2,1)} %shard_map.88), calls=%async_computation.4 | async-start | bytes 524288 | tf_op jit(solution)/shard_map/all_to_all | solution.py:157
  110.0 1.3 %collective-permute-start.8 = (f32[64,256]{1,0:T(8,128)S(1)}, f32[64,256]{1,0:T(8,128)S(1)}, u32[]{:S(2)}, u32[]{:S(2)}) collective-permute-start(f32[64,256]{1,0:T(8,128)S(1)} %convert_reduce_fusion), channel_id=1, source_target_pairs={{0,4},{4,0},{8,12},{12,8},{16,20},{20,16},{24,28},{28,24},{1,5},{5... | collective-permute-start | bytes 196616 | tf_op jit(solution)/shard_map/ppermute | solution.py:199
  111.3 8.9 %collective-permute-start.9 = (f32[64,256]{1,0:T(8,128)S(1)}, f32[64,256]{1,0:T(8,128)S(1)}, u32[]{:S(2)}, u32[]{:S(2)}) collective-permute-start(f32[64,256]{1,0:T(8,128)S(1)} %add.41), channel_id=1, source_target_pairs={{0,8},{4,12},{8,0},{12,4},{16,24},{20,28},{24,16},{28,20},{1,9},{5... | collective-permute-start | bytes 196616 | tf_op jit(solution)/shard_map/ppermute | solution.py:199
  120.3 4.5 %collective-permute-start.10 = (f32[64,256]{1,0:T(8,128)S(1)}, f32[64,256]{1,0:T(8,128)S(1)}, u32[]{:S(2)}, u32[]{:S(2)}) collective-permute-start(f32[64,256]{1,0:T(8,128)S(1)} %add.42), channel_id=1, source_target_pairs={{0,16},{4,20},{8,24},{12,28},{16,0},{20,4},{24,8},{28,12},{1,17},{... | collective-permute-start | bytes 196616 | tf_op jit(solution)/shard_map/ppermute | solution.py:199

commit v3 on v2

v3 whole, which is shorter than its diff:
```python
import functools
import math

import jax
import jax.numpy as jnp
from jax import lax
from jax.experimental import pallas as pl
from jax.experimental.pallas import tpu as pltpu
from jax.sharding import PartitionSpec as P

REACH = 2
CHUNKS = 2
BF16 = jnp.bfloat16
F32 = jnp.float32


def vmem():
    return pl.BlockSpec(memory_space=pltpu.VMEM)


def smem():
    return pl.BlockSpec(memory_space=pltpu.SMEM)


def hbm():
    return pl.BlockSpec(memory_space=pl.ANY)


def tiles_kernel(slabs, where, cols, z_ref, tiles_ref, aside, own_out, *rest):
    leave, (held, total, sems) = rest[:-3], rest[-3:]
    blocks, slots = tiles_ref.shape[:2]
    nodes = z_ref.shape[2]
    window = (2 * REACH + 1) * blocks
    for b in range(blocks):
        pltpu.make_async_copy(tiles_ref.at[b], held.at[b], sems.at[b]).start()

    def clear(i, carry):
        total[i] = jnp.zeros(total.shape[1:], F32)
        return carry

    lax.fori_loop(0, window, clear, 0)
    own = where[0]
    sign = 2 * lax.rem(own, 2) - 1

    def row_block(b, carry):
        pltpu.make_async_copy(tiles_ref.at[b], held.at[b], sems.at[b]).wait()
        z = z_ref[b]
        live = cols[b, slots]
        for s in range(0, slots, 2):
            both = jnp.concatenate([held[b, s], held[b, s + 1]], axis=1)
            terms = jnp.dot(z, both, preferred_element_type=F32)
            for half in range(2):
                col = cols[b, s + half]
                slab = lax.div(col, blocks)
                offset = lax.rem(slab - own + REACH + slabs, slabs) - REACH
                place = (offset * sign + REACH) * blocks + lax.rem(col, blocks)
                place = jnp.where(s + half < live, place, window)
                total[place] += terms[:, half * nodes : (half + 1) * nodes]
        return carry

    lax.fori_loop(0, blocks, row_block, 0)

    def store(out, base):
        def one(i, carry):
            out[i] = total[base + i].astype(BF16)
            return carry

        lax.fori_loop(0, out.shape[0], one, 0)

    store(aside, 0)
    store(own_out, REACH * blocks)
    chunk = leave[0].shape[0]
    for i, out in enumerate(leave):
        store(out, (REACH + 1) * blocks + i * chunk)


def contributions(where, cols, z, tiles, slabs):
    blocks, features, nodes = z.shape
    chunk = blocks // CHUNKS
    window = (2 * REACH + 1) * blocks
    counts = [REACH * blocks, blocks] + [chunk] * (REACH * CHUNKS)
    aside, own, *leave = pl.pallas_call(
        functools.partial(tiles_kernel, slabs),
        out_shape=[jax.ShapeDtypeStruct((count, features, nodes), BF16) for count in counts],
        in_specs=[smem(), smem(), vmem(), hbm()],
        out_specs=[vmem()] * len(counts),
        scratch_shapes=[
            pltpu.VMEM(tiles.shape, BF16),
            pltpu.VMEM((window + 1, features, nodes), F32),
            pltpu.SemaphoreType.DMA((blocks,)),
        ],
        compiler_params=pltpu.CompilerParams(vmem_limit_bytes=40 << 20),
        cost_estimate=pl.CostEstimate(flops=0, bytes_accessed=0, transcendentals=0),
    )(where, cols, z, tiles)
    return aside, own, leave[:CHUNKS], leave[CHUNKS:]


def weight_kernel(packed, out, whole_z, whole_a):
    blocks, features = whole_z.shape[0], packed.shape[2]
    for q in range(packed.shape[0]):
        rows = pl.ds(q * features, features)
        whole_z[:, rows, :] = packed[q, :blocks]
        whole_a[:, rows, :] = packed[q, blocks : 2 * blocks]
    total = jnp.zeros((whole_a.shape[1], whole_z.shape[1]), F32)
    for b in range(blocks):
        total += lax.dot_general(
            whole_a[b], whole_z[b], (((1,), (1,)), ((), ())), preferred_element_type=F32
        )
    nodes = out.shape[3]
    for q in range(out.shape[0]):
        for h in range(out.shape[1]):
            part = total[q * features : (q + 1) * features, h * nodes : (h + 1) * nodes]
            out[q, h] = part.astype(BF16)


def weight_partial(packed, blocks):
    reps, _, features, nodes = packed.shape
    width = reps * features
    return pl.pallas_call(
        weight_kernel,
        out_shape=jax.ShapeDtypeStruct((reps, width // nodes, features, nodes), BF16),
        in_specs=[vmem()],
        out_specs=vmem(),
        scratch_shapes=[pltpu.VMEM((blocks, width, nodes), BF16)] * 2,
        cost_estimate=pl.CostEstimate(
            flops=2 * blocks * nodes * width * width,
            bytes_accessed=4 * blocks * nodes * width + 2 * width * width,
            transcendentals=0,
        ),
    )(packed)


def lay_weight(packed, first, whole):
    features, nodes = packed.shape[2:]
    for q in range(packed.shape[0]):
        for h in range(whole.shape[1] // nodes):
            whole[pl.ds(q * features, features), pl.ds(h * nodes, nodes)] = packed[q, first + h]


def mix_kernel(first, packed, shares, out, weights, whole):
    lay_weight(packed, first, weights)
    reps, blocks, features = shares.shape[:3]
    for q in range(reps):
        whole[:, pl.ds(q * features, features), :] = shares[q]
    for b in range(blocks):
        mixed = jnp.dot(weights[...], whole[b], preferred_element_type=F32)
        for q in range(reps):
            out[q, b] = mixed[q * features : (q + 1) * features].astype(BF16)


def mix(packed, first, shares):
    reps, blocks, features, nodes = shares.shape
    width = reps * features
    return pl.pallas_call(
        functools.partial(mix_kernel, first),
        out_shape=jax.ShapeDtypeStruct(shares.shape, BF16),
        in_specs=[vmem(), vmem()],
        out_specs=vmem(),
        scratch_shapes=[pltpu.VMEM((width, width), BF16), pltpu.VMEM((blocks, width, nodes), BF16)],
        cost_estimate=pl.CostEstimate(
            flops=2 * blocks * nodes * width * width,
            bytes_accessed=4 * blocks * nodes * width,
            transcendentals=0,
        ),
    )(packed, shares)


def mix_apart_kernel(first, reps, where, packed, *rest):
    shares, outs, (weights, whole) = rest[:reps], rest[reps : 2 * reps], rest[2 * reps :]
    lay_weight(packed, first, weights)
    features = shares[0].shape[1]
    blocks = whole.shape[0]
    for s in range(reps):
        rows = pl.multiple_of(lax.rem(where[1] - s + reps, reps) * features, features)
        whole[:, pl.ds(rows, features), :] = shares[s][:blocks]
    for s in range(reps):
        rows = pl.multiple_of(lax.rem(where[1] + s, reps) * features, features)
        part = weights[pl.ds(rows, features), :]
        for b in range(blocks):
            outs[s][b] = jnp.dot(part, whole[b], preferred_element_type=F32).astype(BF16)


def mix_apart(where, packed, first, shares, blocks):
    reps = len(shares)
    _, features, nodes = shares[0].shape
    width = reps * features
    return pl.pallas_call(
        functools.partial(mix_apart_kernel, first, reps),
        out_shape=[jax.ShapeDtypeStruct((blocks, features, nodes), BF16)] * reps,
        in_specs=[smem()] + [vmem()] * (1 + reps),
        out_specs=[vmem()] * reps,
        scratch_shapes=[pltpu.VMEM((width, width), BF16), pltpu.VMEM((blocks, width, nodes), BF16)],
        cost_estimate=pl.CostEstimate(
            flops=2 * blocks * nodes * width * width,
            bytes_accessed=4 * blocks * nodes * width,
            transcendentals=0,
        ),
    )(where, packed, *shares)


def lay_kernel(where, done, *rest):
    shares, out = rest[:-1], rest[-1]
    reps, blocks = len(shares), shares[0].shape[0]
    start = done.shape[0]
    out[:start] = done[...]
    for s in range(reps):
        first = start + lax.rem(where[1] - s + reps, reps) * blocks
        out[pl.ds(first, blocks)] = shares[s][...]


def lay_blocks(where, done, shares, shape):
    return pl.pallas_call(
        lay_kernel,
        out_shape=jax.ShapeDtypeStruct(shape, BF16),
        in_specs=[smem()] + [vmem()] * (1 + len(shares)),
        out_specs=vmem(),
    )(where, done, *shares)


def exchange(value):
    return lax.all_to_all(value, "rep", 0, 0, tiled=True)


def shift(value, steps):
    reps = lax.axis_size("rep")
    if steps % reps == 0:
        return value
    return lax.ppermute(value, "rep", [(i, (i + steps) % reps) for i in range(reps)])


def on_device(cotangent, relu_mask, aggregated, weight, tiles, col_block, live_count):
    blocks, features, nodes = cotangent.shape
    slabs, reps = lax.axis_size("blk"), lax.axis_size("rep")
    width = weight.shape[1]
    pieces = width // nodes
    chunk = blocks // CHUNKS
    share = blocks // reps
    rep = lax.axis_index("rep")
    where = jnp.stack([lax.axis_index("blk"), rep]).astype(jnp.int32)
    cols = jnp.concatenate([col_block, live_count[:, None]], axis=1)

    grad_z = cotangent * relu_mask.astype(BF16)
    by_share = (reps, share, features, nodes)
    weight_pieces = weight.reshape(features, pieces, nodes).transpose(1, 0, 2)
    weight_pieces = jnp.broadcast_to(weight_pieces[None], (reps, pieces, features, nodes))
    packed = jnp.concatenate(
        [grad_z.reshape(by_share), aggregated.reshape(by_share), weight_pieces], axis=1
    )
    packed, grad_z = lax.optimization_barrier((packed, grad_z))
    packed = exchange(packed)

    aside, own, first, second = contributions(where, cols, grad_z, tiles, slabs)

    to_one = [(i, (i + (1 if i % 2 else -1)) % slabs) for i in range(slabs)]
    to_two = [(i, (i + (2 if i % 2 else -2)) % slabs) for i in range(slabs)]

    def add(*terms):
        return sum(term.astype(F32) for term in terms).astype(BF16)

    aside = lax.ppermute(aside, "blk", [(i, i ^ 1) for i in range(slabs)])
    sums = []
    for k in range(CHUNKS):
        span = slice(k * chunk, (k + 1) * chunk)
        two_in = lax.ppermute(second[k], "blk", to_two)
        one_in = lax.ppermute(add(first[k], aside[span]), "blk", to_one)
        sums.append(add(own[span], aside[blocks:][span], one_in, two_in))

    sums[0], packed = lax.optimization_barrier((sums[0], packed))
    part = chunk // reps
    mixed = mix(packed, 2 * share, exchange(sums[0].reshape(reps, part, features, nodes)))
    mixed = exchange(mixed).reshape(chunk, features, nodes)

    grad_w = weight_partial(packed, share)
    both = jnp.concatenate([sums[1].reshape(reps, part, features, nodes), grad_w], axis=1)

    def for_target(s):
        return lax.dynamic_index_in_dim(both, lax.rem(rep + s, reps), 0, keepdims=False)

    shares = [shift(for_target(s), s) for s in range(reps)]
    outs = mix_apart(where, packed, 2 * share, shares, part)
    outs = [shift(out, s) for s, out in enumerate(outs)]

    grad_w = sum(part_in[part:].astype(F32) for part_in in shares)
    step = 1
    while step < slabs:
        grad_w = grad_w + lax.ppermute(grad_w, "blk", [(i, i ^ step) for i in range(slabs)])
        step *= 2
    grad_w = grad_w.transpose(1, 0, 2).reshape(features, width)
    weight_grad = grad_w * (1.0 / math.sqrt(slabs * blocks * nodes))
    return lay_blocks(where, mixed, outs, cotangent.shape), weight_grad


def solution(mesh):
    placed = (
        P("blk", "rep", None),
        P("blk", "rep", None),
        P("blk", "rep", None),
        P("rep", None),
        P("blk", None, None, None),
        P("blk", None),
        P("blk"),
    )
    return jax.shard_map(
        on_device,
        mesh=mesh,
        in_specs=placed,
        out_specs=(P("blk", "rep", None), P("rep", None)),
        check_vma=False,
    )
```

time: 126 us -> 103 us (0.82)
  waiting for transfers between devices: 50.6 us -> 37.5 us
  starting transfers between devices: 43.6 us -> 32.7 us
  Pallas kernels: 18.7 us -> 22 us
  other arithmetic: 9.51 us -> 7.59 us
    all_to_all x7 -> x3, waiting for transfers between devices: 41 us -> 1.85 us  [exchange(): return lax.all_to_all(value, 'rep', 0, 0, tiled=True)]
    ppermute x6 -> x9, waiting for transfers between devices: 4.52 us -> 24.9 us  [the longest x6 14.3 us: shift(): lax.ppermute(value, 'rep', [(i, (i + steps) % reps) for i in range(reps)])]
    all_to_all x7 -> x3, starting transfers between devices: 26.8 us -> 13.9 us  [exchange(): return lax.all_to_all(value, 'rep', 0, 0, tiled=True)]
    ppermute x6 -> x9, starting transfers between devices: 2.28 us -> 13.8 us  [the longest x6 10.8 us: shift(): lax.ppermute(value, 'rep', [(i, (i + steps) % reps) for i in range(reps)])]
    ppermute x2, waiting for transfers between devices: 0.01 us -> 7.77 us  [on_device(): two_in = lax.ppermute(second[k], 'blk', to_two)]
    ppermute x3, starting transfers between devices: 8.89 us -> 2.01 us  [on_device(): lax.ppermute(grad_w, 'blk', [(i, i ^ step) for i in range(slabs)])]
    pallas_call x4 -> x5, Pallas kernels: 18.7 us -> 22 us  [the longest x1 13.1 us: contributions(): pl.pallas_call(functools.partial(tiles_kernel, slabs), out_shape=[jax.Sha...]
    ppermute x2, starting transfers between devices: 5.61 us -> 2.99 us  [on_device(): two_in = lax.ppermute(second[k], 'blk', to_two)]
  transfers between devices with their start and end apart: 18 -> 17, of which waited for: 10 -> 10; matrix products, arithmetic and copies ran while one was open for 6% -> 5% of each run, Pallas kernels for 5% -> 5%
where the time goes in v3:
time: 103 us
  waiting for transfers between devices  37.5 us (36%)
  starting transfers between devices  32.7 us (32%)
  Pallas kernels  22 us (21%)
  other arithmetic  7.59 us (7%)
  local copies, waits for them, and re-layouts  2.38 us (2%)
    ppermute x6, waiting for transfers between devices, shift(): lax.ppermute(value, 'rep', [(i, (i + steps) % reps) for i in range(reps)])  14.3 us
    all_to_all x3, starting transfers between devices, exchange(): return lax.all_to_all(value, 'rep', 0, 0, tiled=True)  13.9 us
    pallas_call x1, Pallas kernels, contributions(): pl.pallas_call(functools.partial(tiles_kernel, slabs), out_shape=[jax.Sha...  13.1 us
    ppermute x6, starting transfers between devices, shift(): lax.ppermute(value, 'rep', [(i, (i + steps) % reps) for i in range(reps)])  10.8 us
    ppermute x2, waiting for transfers between devices, on_device(): one_in = lax.ppermute(add(first[k], aside[span]), 'blk', to_one)  10.7 us
    ppermute x2, waiting for transfers between devices, on_device(): two_in = lax.ppermute(second[k], 'blk', to_two)  7.77 us
    convert_element_type x2, other arithmetic, add(): return sum((term.astype(F32) for term in terms)).astype(BF16)  3.29 us
    ppermute x2, starting transfers between devices, on_device(): two_in = lax.ppermute(second[k], 'blk', to_two)  2.99 us
  transfers between devices with their start and end apart: 17, of which 10 were waited for; matrix products, arithmetic and copies ran while one was open for 5% of the time, Pallas kernels for 5%

profile of v3, /device:TPU:0, one launch (start us, length us, event | category | flops | bytes accessed | tf_op | source)
XLA Modules:
  0.0 103.0 jit_solution(4952474925107073959)
XLA Ops:
  0.7 0.7 copy-done
  1.4 1.5 %convert_multiply_fusion.z_ref = bf16[32,64,128]{2,1,0:T(8,128)(2,1)S(1)} fusion(bf16[32,64,128]{2,1,0:T(8,128)(2,1)} %param.7, s32[32,64,128]{2,1,0:T(8,128)} %param.8), kind=kLoop, calls=%fused_computation.9 | loop fusion | flops 524288 | bytes 2097152 | tf_op jit(solution)/shard_map/mul | solution.py:242
  2.9 1.2 %pad_maximum_fusion = bf16[4,18,64,128]{3,2,1,0:T(8,128)(2,1)} fusion(bf16[4,2,64,128]{3,2,1,0:T(8,128)(2,1)S(1)} %broadcast_in_dim.10, bf16[4,8,64,128]{3,2,1,0:T(8,128)(2,1)S(1)} %bitcast.37, bf16[4,8,64,128]{3,2,1,0:T(8,128)(2,1)S(1)} %bitcast.33), kind=kLoop, calls=%fused_computation | loop fusion | flops 1179648 | bytes 2359296 | tf_op jit(solution)/shard_map/concatenate | solution.py:246
  4.4 13.1 %shard_map.86 = (bf16[64,64,128]{2,1,0:T(8,128)(2,1)S(1)}, bf16[32,64,128]{2,1,0:T(8,128)(2,1)S(1)}, bf16[16,64,128]{2,1,0:T(8,128)(2,1)S(1)}, bf16[16,64,128]{2...) custom-call(s32[2]{0:T(128)S(1)} %pad_add_fusion.1.where, ...), custom_call_target="tpu_custom_call" | custom-call | tf_op jit(solution)/shard_map/pallas_call | solution.py:82
  17.8 6.2 %all-to-all-start = ((bf16[4,18,64,128]{3,2,1,0:T(8,128)(2,1)}), bf16[4,18,64,128]{3,2,1,0:T(8,128)(2,1)}, u32[]{:S(2)}, u32[]{:S(2)}) async-start(bf16[4,18,64,128]{3,2,1,0:T(8,128)(2,1)} %pad_maximum_fusion), calls=%async_computation | async-start | bytes 2359296 | tf_op jit(solution)/shard_map/all_to_all | solution.py:221
  24.0 2.3 %collective-permute-start.2 = (bf16[16,64,128]{2,1,0:T(8,128)(2,1)S(1)}, bf16[16,64,128]{2,1,0:T(8,128)(2,1)S(1)}, u32[]{:S(2)}, u32[]{:S(2)}) collective-permute-start(bf16[16,64,128]{2,1,0:T(8,128)(2,1)S(1)} %get-tuple-element.20), channel_id=1, source_target_pairs={{0,24},{4,12},{8,0},{12,20},{16,8},{20,28},{24,16},{28,4},{1,25},{... | collective-permute-start | bytes 786440 | tf_op jit(solution)/shard_map/ppermute | solution.py:264
  27.0 1.2 %add_convert_fusion.1 = (bf16[16,64,128]{2,1,0:T(8,128)(2,1)S(1)}, bf16[16,64,128]{2,1,0:T(8,128)(2,1)S(1)}) fusion(bf16[16,64,128]{2,1,0:T(8,128)(2,1)S(1)} %get-tuple-element.24, bf16[64,64,128]{2,1,0:T(8,128)(2,1)} %collective-permute-done, bf16[16,64,128]{2,1,0:T(8,128)(2,1)S(1)} %get-tuple-element.19), kind=kLoop, calls=%fused_computation.6 | loop fusion | flops 1048576 | bytes 1572864 | tf_op jit(solution)/shard_map/convert_element_type | solution.py:258
  28.7 2.2 %collective-permute-start.3 = (bf16[16,64,128]{2,1,0:T(8,128)(2,1)S(1)}, bf16[16,64,128]{2,1,0:T(8,128)(2,1)S(1)}, u32[]{:S(2)}, u32[]{:S(2)}) collective-permute-start(bf16[16,64,128]{2,1,0:T(8,128)(2,1)S(1)} %get-tuple-element.32), channel_id=1, source_target_pairs={{0,28},{4,8},{8,4},{12,16},{16,12},{20,24},{24,20},{28,0},{1,29},{... | collective-permute-start | bytes 786440 | tf_op jit(solution)/shard_map/ppermute | solution.py:265
  30.9 2.2 %collective-permute-done.2 = bf16[16,64,128]{2,1,0:T(8,128)(2,1)S(1)} collective-permute-done((bf16[16,64,128]{2,1,0:T(8,128)(2,1)S(1)}, bf16[16,64,128]{2,1,0:T(8,128)(2,1)S(1)}, u32[]{:S(2)}, u32[]{:S(2)}) %collective-permute-start.2) | collective-permute-done | bytes 262176 | tf_op jit(solution)/shard_map/ppermute | solution.py:264
  33.1 5.6 %collective-permute-done.4 = bf16[16,64,128]{2,1,0:T(8,128)(2,1)S(1)} collective-permute-done((bf16[16,64,128]{2,1,0:T(8,128)(2,1)S(1)}, bf16[16,64,128]{2,1,0:T(8,128)(2,1)S(1)}, u32[]{:S(2)}, u32[]{:S(2)}) %collective-permute-start.4) | collective-permute-done | bytes 262176 | tf_op jit(solution)/shard_map/ppermute | solution.py:264
  38.7 5.6 %collective-permute-done.1 = bf16[16,64,128]{2,1,0:T(8,128)(2,1)S(1)} collective-permute-done((bf16[16,64,128]{2,1,0:T(8,128)(2,1)S(1)}, bf16[16,64,128]{2,1,0:T(8,128)(2,1)S(1)}, u32[]{:S(2)}, u32[]{:S(2)}) %collective-permute-start.1) | collective-permute-done | bytes 262176 | tf_op jit(solution)/shard_map/ppermute | solution.py:265
  44.3 5.0 %collective-permute-done.3 = bf16[16,64,128]{2,1,0:T(8,128)(2,1)S(1)} collective-permute-done((bf16[16,64,128]{2,1,0:T(8,128)(2,1)S(1)}, bf16[16,64,128]{2,1,0:T(8,128)(2,1)S(1)}, u32[]{:S(2)}, u32[]{:S(2)}) %collective-permute-start.3) | collective-permute-done | bytes 262176 | tf_op jit(solution)/shard_map/ppermute | solution.py:265
  49.3 2.1 %add_convert_fusion = (bf16[16,64,128]{2,1,0:T(8,128)(2,1)S(1)}, bf16[16,64,128]{2,1,0:T(8,128)(2,1)}) fusion(bf16[16,64,128]{2,1,0:T(8,128)(2,1)S(1)} %collective-permute-done.4, bf16[16,64,128]{2,1,0:T(8,128)(2,1)S(1)} %collective-permute-done.3, bf16[64,64,128]{2,1,0:T(8,128)(2,1)} %collective-permute-done, bf16[32,64,128]{2,1,0:T(8,128)(2,1)S(1)} %get-tuple-element.17, ...), kind=kLoop, calls=%fused_computation.5 | loop fusion | flops 2097152 | bytes 2621440 | tf_op jit(solution)/shard_map/convert_element_type | solution.py:258
  51.4 1.8 %all-to-all-done.packed = bf16[4,18,64,128]{3,2,1,0:T(8,128)(2,1)} async-done(((bf16[4,18,64,128]{3,2,1,0:T(8,128)(2,1)}), bf16[4,18,64,128]{3,2,1,0:T(8,128)(2,1)}, u32[]{:S(2)}, u32[]{:S(2)}) %all-to-all-start) | async-done | bytes 1179680 | tf_op jit(solution)/shard_map/all_to_all | solution.py:221
  53.3 2.4 %shard_map.88 = bf16[4,2,64,128]{3,2,1,0:T(8,128)(2,1)} custom-call(bf16[4,18,64,128]{3,2,1,0:T(8,128)(2,1)} %all-to-all-done.packed), custom_call_target="tpu_custom_call" | custom-call | flops 134217728 | bytes 1179648 | tf_op jit(solution)/shard_map/pallas_call | solution.py:119
  55.6 3.4 %all-to-all-start.1 = ((bf16[4,4,64,128]{3,2,1,0:T(8,128)(2,1)}), bf16[4,4,64,128]{3,2,1,0:T(8,128)(2,1)S(1)}, u32[]{:S(2)}, u32[]{:S(2)}) async-start(bf16[4,4,64,128]{3,2,1,0:T(8,128)(2,1)} %bitcast.6), calls=%async_computation.1 | async-start | bytes 524288 | tf_op jit(solution)/shard_map/all_to_all | solution.py:221
  59.0 0.9 fusion.1
  59.9 2.0 %collective-permute-start.5 = (bf16[6,64,128]{2,1,0:T(8,128)(2,1)S(1)}, bf16[6,64,128]{2,1,0:T(8,128)(2,1)S(1)}, u32[]{:S(2)}, u32[]{:S(2)}) collective-permute-start(bf16[6,64,128]{2,1,0:T(8,128)(2,1)S(1)} %get-tuple-element.36), channel_id=1, source_target_pairs={{0,1},{1,2},{2,3},{3,0},{4,5},{5,6},{6,7},{7,4},{8,9},{9,10},{10,1... | collective-permute-start | bytes 294920 | tf_op jit(solution)/shard_map/ppermute | solution.py:228
  61.9 2.4 %collective-permute-start.6 = (bf16[6,64,128]{2,1,0:T(8,128)(2,1)S(1)}, bf16[6,64,128]{2,1,0:T(8,128)(2,1)S(1)}, u32[]{:S(2)}, u32[]{:S(2)}) collective-permute-start(bf16[6,64,128]{2,1,0:T(8,128)(2,1)S(1)} %get-tuple-element.37), channel_id=1, source_target_pairs={{0,2},{1,3},{2,0},{3,1},{4,6},{5,7},{6,4},{7,5},{8,10},{9,11},{10,... | collective-permute-start | bytes 294920 | tf_op jit(solution)/shard_map/ppermute | solution.py:228
  64.3 1.5 %collective-permute-start.7 = (bf16[6,64,128]{2,1,0:T(8,128)(2,1)S(1)}, bf16[6,64,128]{2,1,0:T(8,128)(2,1)S(1)}, u32[]{:S(2)}, u32[]{:S(2)}) collective-permute-start(bf16[6,64,128]{2,1,0:T(8,128)(2,1)S(1)} %get-tuple-element.34), channel_id=1, source_target_pairs={{0,3},{1,0},{2,1},{3,2},{4,7},{5,4},{6,5},{7,6},{8,11},{9,8},{10,9... | collective-permute-start | bytes 294920 | tf_op jit(solution)/shard_map/ppermute | solution.py:228
  65.8 5.2 %collective-permute-done.5.rest_1_ = bf16[6,64,128]{2,1,0:T(8,128)(2,1)S(1)} collective-permute-done((bf16[6,64,128]{2,1,0:T(8,128)(2,1)S(1)}, bf16[6,64,128]{2,1,0:T(8,128)(2,1)S(1)}, u32[]{:S(2)}, u32[]{:S(2)}) %collective-permute-start.5) | collective-permute-done | bytes 98336 | tf_op jit(solution)/shard_map/ppermute | solution.py:228
  70.9 4.6 %collective-permute-done.6.rest_2_ = bf16[6,64,128]{2,1,0:T(8,128)(2,1)S(1)} collective-permute-done((bf16[6,64,128]{2,1,0:T(8,128)(2,1)S(1)}, bf16[6,64,128]{2,1,0:T(8,128)(2,1)S(1)}, u32[]{:S(2)}, u32[]{:S(2)}) %collective-permute-start.6) | collective-permute-done | bytes 98336 | tf_op jit(solution)/shard_map/ppermute | solution.py:228
  75.7 0.7 copy-done.3
  76.4 2.3 %shard_map.87 = bf16[4,4,64,128]{3,2,1,0:T(8,128)(2,1)} custom-call(bf16[4,18,64,128]{3,2,1,0:T(8,128)(2,1)} %all-to-all-done.packed, bf16[4,4,64,128]{3,2,1,0:T(8,128)(2,1)} %copy-done.3), custom_call_target="tpu_custom_call" | custom-call | flops 67108864 | bytes 524288 | tf_op jit(solution)/shard_map/pallas_call | solution.py:154
  78.7 4.4 %all-to-all-start.2 = ((bf16[4,4,64,128]{3,2,1,0:T(8,128)(2,1)}), bf16[4,4,64,128]{3,2,1,0:T(8,128)(2,1)S(1)}, u32[]{:S(2)}, u32[]{:S(2)}) async-start(bf16[4,4,64,128]{3,2,1,0:T(8,128)(2,1)} %shard_map.87), calls=%async_computation.2 | async-start | bytes 524288 | tf_op jit(solution)/shard_map/all_to_all | solution.py:221
  83.1 1.4 %collective-permute-start.12 = (f32[2,64,128]{2,1,0:T(8,128)S(1)}, f32[2,64,128]{2,1,0:T(8,128)S(1)}, u32[]{:S(2)}, u32[]{:S(2)}) collective-permute-start(f32[2,64,128]{2,1,0:T(8,128)S(1)} %add.82), channel_id=1, source_target_pairs={{0,8},{4,12},{8,0},{12,4},{16,24},{20,28},{24,16},{28,20},{1,9},{5... | collective-permute-start | bytes 196616 | tf_op jit(solution)/shard_map/ppermute | solution.py:286
  84.5 2.9 %collective-permute-done.12 = f32[2,64,128]{2,1,0:T(8,128)S(1)} collective-permute-done((f32[2,64,128]{2,1,0:T(8,128)S(1)}, f32[2,64,128]{2,1,0:T(8,128)S(1)}, u32[]{:S(2)}, u32[]{:S(2)}) %collective-permute-start.12) | collective-permute-done | bytes 65568 | tf_op jit(solution)/shard_map/ppermute | solution.py:286
  88.0 2.3 %shard_map.89 = (bf16[4,64,128]{2,1,0:T(8,128)(2,1)}, bf16[4,64,128]{2,1,0:T(8,128)(2,1)}, bf16[4,64,128]{2,1,0:T(8,128)(2,1)}, bf16[4,64,128]{2,1,0:T(8,128)(2,1)}) custom-call(s32[2]{0:T(128)} %copy-done.1, bf16[4,18,64,128]{3,2,1,0:T(8,128)(2,1)} %all-to-all-done.packed, bf16[6,64,128]{2,1,0:T(8,128)(2,1)} %bitcast.36, bf16[6,64,128]{2,1,0:T(8,128)(2,1)} %copy-done.6, ...), custom_call_target="tpu_custom_call" | custom-call | flops 67108864 | bytes 524288 | tf_op jit(solution)/shard_map/pallas_call | solution.py:187
  90.3 3.8 %collective-permute-start.10 = (bf16[4,64,128]{2,1,0:T(8,128)(2,1)}, bf16[4,64,128]{2,1,0:T(8,128)(2,1)S(1)}, u32[]{:S(2)}, u32[]{:S(2)}) collective-permute-start(bf16[4,64,128]{2,1,0:T(8,128)(2,1)} %get-tuple-element.29), channel_id=1, source_target_pairs={{0,3},{1,0},{2,1},{3,2},{4,7},{5,4},{6,5},{7,6},{8,11},{9,8},{10,9... | collective-permute-start | bytes 196616 | tf_op jit(solution)/shard_map/ppermute | solution.py:228
  94.2 1.1 %collective-permute-start.9 = (bf16[4,64,128]{2,1,0:T(8,128)(2,1)}, bf16[4,64,128]{2,1,0:T(8,128)(2,1)S(1)}, u32[]{:S(2)}, u32[]{:S(2)}) collective-permute-start(bf16[4,64,128]{2,1,0:T(8,128)(2,1)} %get-tuple-element.28), channel_id=1, source_target_pairs={{0,2},{1,3},{2,0},{3,1},{4,6},{5,7},{6,4},{7,5},{8,10},{9,11},{10,... | collective-permute-start | bytes 196616 | tf_op jit(solution)/shard_map/ppermute | solution.py:228
  96.4 4.0 %collective-permute-done.8.rest_1_ = bf16[4,64,128]{2,1,0:T(8,128)(2,1)S(1)} collective-permute-done((bf16[4,64,128]{2,1,0:T(8,128)(2,1)}, bf16[4,64,128]{2,1,0:T(8,128)(2,1)S(1)}, u32[]{:S(2)}, u32[]{:S(2)}) %collective-permute-start.8) | collective-permute-done | bytes 65568 | tf_op jit(solution)/shard_map/ppermute | solution.py:228
  101.2 1.9 %shard_map.90 = bf16[32,64,128]{2,1,0:T(8,128)(2,1)} custom-call(s32[2]{0:T(128)} %copy-done.1, bf16[16,64,128]{2,1,0:T(8,128)(2,1)} %bitcast.35, bf16[4,64,128]{2,1,0:T(8,128)(2,1)} %get-tuple-element.26.rest_0_, bf16[4,64,128]{2,1,0:T(8,128)(2,1)} %copy-done.10, bf16[4,64,128]{2,1,0:T(8,128)(2,1)} %copy-done.11, bf16[4,64,128]{2,1,0:T(8,128)(2,1)} %copy-done.9), custom_call_target="tpu_custom_call" | custom-call | tf_op jit(solution)/shard_map/pallas_call | solution.py:212
  (50 shorter events, 4.3 us)
Async XLA Ops:
  0.6 0.8 copy-start
  0.6 2.2 %copy-start.5 = (bf16[32,64,128]{2,1,0:T(8,128)(2,1)S(1)}, bf16[32,64,128]{2,1,0:T(8,128)(2,1)}, u32[]{:S(2)}) copy-start(bf16[32,64,128]{2,1,0:T(8,128)(2,1)} %param.9) | copy-start | bytes 1572868
  2.9 1.2 %copy-start.12 = (s32[32,16]{0,1:T(8,128)S(1)}, s32[32,16]{0,1:T(8,128)}, u32[]{:S(2)}) copy-start(s32[32,16]{0,1:T(8,128)} %param.12) | copy-start | bytes 6148
  2.9 1.2 %copy-start.13 = (s32[32]{0:T(128)S(1)}, s32[32]{0:T(128)}, u32[]{:S(2)}) copy-start(s32[32]{0:T(128)} %param.13) | copy-start | bytes 388
  4.3 13.2 %copy-start.1 = (s32[2]{0:T(128)}, s32[2]{0:T(128)S(1)}, u32[]{:S(2)}) copy-start(s32[2]{0:T(128)S(1)} %pad_add_fusion.1.where) | copy-start | bytes 28
  17.6 9.4 %collective-permute-start = (bf16[64,64,128]{2,1,0:T(8,128)(2,1)S(1)}, bf16[64,64,128]{2,1,0:T(8,128)(2,1)}, u32[]{:S(2)}, u32[]{:S(2)}) collective-permute-start(bf16[64,64,128]{2,1,0:T(8,128)(2,1)S(1)} %get-tuple-element.18), channel_id=1, source_target_pairs={{0,4},{4,0},{8,12},{12,8},{16,20},{20,16},{24,28},{28,24},{1,5},{5... | collective-permute-start | bytes 3145736 | tf_op jit(solution)/shard_map/ppermute | solution.py:260
  17.8 35.5 %all-to-all-start = ((bf16[4,18,64,128]{3,2,1,0:T(8,128)(2,1)}), bf16[4,18,64,128]{3,2,1,0:T(8,128)(2,1)}, u32[]{:S(2)}, u32[]{:S(2)}) async-start(bf16[4,18,64,128]{3,2,1,0:T(8,128)(2,1)} %pad_maximum_fusion), calls=%async_computation | async-start | bytes 2359296 | tf_op jit(solution)/shard_map/all_to_all | solution.py:221
  24.0 9.1 %collective-permute-start.2 = (bf16[16,64,128]{2,1,0:T(8,128)(2,1)S(1)}, bf16[16,64,128]{2,1,0:T(8,128)(2,1)S(1)}, u32[]{:S(2)}, u32[]{:S(2)}) collective-permute-start(bf16[16,64,128]{2,1,0:T(8,128)(2,1)S(1)} %get-tuple-element.20), channel_id=1, source_target_pairs={{0,24},{4,12},{8,0},{12,20},{16,8},{20,28},{24,16},{28,4},{1,25},{... | collective-permute-start | bytes 786440 | tf_op jit(solution)/shard_map/ppermute | solution.py:264
  26.3 12.4 %collective-permute-start.4 = (bf16[16,64,128]{2,1,0:T(8,128)(2,1)S(1)}, bf16[16,64,128]{2,1,0:T(8,128)(2,1)S(1)}, u32[]{:S(2)}, u32[]{:S(2)}) collective-permute-start(bf16[16,64,128]{2,1,0:T(8,128)(2,1)S(1)} %get-tuple-element.25), channel_id=1, source_target_pairs={{0,24},{4,12},{8,0},{12,20},{16,8},{20,28},{24,16},{28,4},{1,25},{... | collective-permute-start | bytes 786440 | tf_op jit(solution)/shard_map/ppermute | solution.py:264
  28.2 16.1 %collective-permute-start.1 = (bf16[16,64,128]{2,1,0:T(8,128)(2,1)S(1)}, bf16[16,64,128]{2,1,0:T(8,128)(2,1)S(1)}, u32[]{:S(2)}, u32[]{:S(2)}) collective-permute-start(bf16[16,64,128]{2,1,0:T(8,128)(2,1)S(1)} %get-tuple-element.33), channel_id=1, source_target_pairs={{0,28},{4,8},{8,4},{12,16},{16,12},{20,24},{24,20},{28,0},{1,29},{... | collective-permute-start | bytes 786440 | tf_op jit(solution)/shard_map/ppermute | solution.py:265
  28.7 20.6 %collective-permute-start.3 = (bf16[16,64,128]{2,1,0:T(8,128)(2,1)S(1)}, bf16[16,64,128]{2,1,0:T(8,128)(2,1)S(1)}, u32[]{:S(2)}, u32[]{:S(2)}) collective-permute-start(bf16[16,64,128]{2,1,0:T(8,128)(2,1)S(1)} %get-tuple-element.32), channel_id=1, source_target_pairs={{0,28},{4,8},{8,4},{12,16},{16,12},{20,24},{24,20},{28,0},{1,29},{... | collective-permute-start | bytes 786440 | tf_op jit(solution)/shard_map/ppermute | solution.py:265
  55.6 20.0 %all-to-all-start.1 = ((bf16[4,4,64,128]{3,2,1,0:T(8,128)(2,1)}), bf16[4,4,64,128]{3,2,1,0:T(8,128)(2,1)S(1)}, u32[]{:S(2)}, u32[]{:S(2)}) async-start(bf16[4,4,64,128]{3,2,1,0:T(8,128)(2,1)} %bitcast.6), calls=%async_computation.1 | async-start | bytes 524288 | tf_op jit(solution)/shard_map/all_to_all | solution.py:221
  59.9 18.8 %copy-start.4 = (bf16[1,6,64,128]{3,2,1,0:T(8,128)(2,1)}, bf16[1,6,64,128]{3,2,1,0:T(8,128)(2,1)S(1)}, u32[]{:S(2)}) copy-start(bf16[1,6,64,128]{3,2,1,0:T(8,128)(2,1)S(1)} %get-tuple-element.35) | copy-start | bytes 294916
  59.9 11.0 %collective-permute-start.5 = (bf16[6,64,128]{2,1,0:T(8,128)(2,1)S(1)}, bf16[6,64,128]{2,1,0:T(8,128)(2,1)S(1)}, u32[]{:S(2)}, u32[]{:S(2)}) collective-permute-start(bf16[6,64,128]{2,1,0:T(8,128)(2,1)S(1)} %get-tuple-element.36), channel_id=1, source_target_pairs={{0,1},{1,2},{2,3},{3,0},{4,5},{5,6},{6,7},{7,4},{8,9},{9,10},{10,1... | collective-permute-start | bytes 294920 | tf_op jit(solution)/shard_map/ppermute | solution.py:228
  61.9 13.6 %collective-permute-start.6 = (bf16[6,64,128]{2,1,0:T(8,128)(2,1)S(1)}, bf16[6,64,128]{2,1,0:T(8,128)(2,1)S(1)}, u32[]{:S(2)}, u32[]{:S(2)}) collective-permute-start(bf16[6,64,128]{2,1,0:T(8,128)(2,1)S(1)} %get-tuple-element.37), channel_id=1, source_target_pairs={{0,2},{1,3},{2,0},{3,1},{4,6},{5,7},{6,4},{7,5},{8,10},{9,11},{10,... | collective-permute-start | bytes 294920 | tf_op jit(solution)/shard_map/ppermute | solution.py:228
  64.3 11.2 %collective-permute-start.7 = (bf16[6,64,128]{2,1,0:T(8,128)(2,1)S(1)}, bf16[6,64,128]{2,1,0:T(8,128)(2,1)S(1)}, u32[]{:S(2)}, u32[]{:S(2)}) collective-permute-start(bf16[6,64,128]{2,1,0:T(8,128)(2,1)S(1)} %get-tuple-element.34), channel_id=1, source_target_pairs={{0,3},{1,0},{2,1},{3,2},{4,7},{5,4},{6,5},{7,6},{8,11},{9,8},{10,9... | collective-permute-start | bytes 294920 | tf_op jit(solution)/shard_map/ppermute | solution.py:228
  70.9 7.8 %copy-start.6 = (bf16[6,64,128]{2,1,0:T(8,128)(2,1)}, bf16[6,64,128]{2,1,0:T(8,128)(2,1)S(1)}, u32[]{:S(2)}) copy-start(bf16[6,64,128]{2,1,0:T(8,128)(2,1)S(1)} %collective-permute-done.5.rest_1_) | copy-start | bytes 294916
  75.6 12.4 %copy-start.7 = (bf16[6,64,128]{2,1,0:T(8,128)(2,1)}, bf16[6,64,128]{2,1,0:T(8,128)(2,1)S(1)}, u32[]{:S(2)}) copy-start(bf16[6,64,128]{2,1,0:T(8,128)(2,1)S(1)} %collective-permute-done.6.rest_2_) | copy-start | bytes 294916
  75.6 12.4 %copy-start.8 = (bf16[6,64,128]{2,1,0:T(8,128)(2,1)}, bf16[6,64,128]{2,1,0:T(8,128)(2,1)S(1)}, u32[]{:S(2)}) copy-start(bf16[6,64,128]{2,1,0:T(8,128)(2,1)S(1)} %collective-permute-done.7.rest_3_) | copy-start | bytes 294916
  75.6 7.5 %collective-permute-start.11 = (f32[2,64,128]{2,1,0:T(8,128)S(1)}, f32[2,64,128]{2,1,0:T(8,128)S(1)}, u32[]{:S(2)}, u32[]{:S(2)}) collective-permute-start(f32[2,64,128]{2,1,0:T(8,128)S(1)} %fusion.8), channel_id=1, source_target_pairs={{0,4},{4,0},{8,12},{12,8},{16,20},{20,16},{24,28},{28,24},{1,5},{5... | collective-permute-start | bytes 196616 | tf_op jit(solution)/shard_map/ppermute | solution.py:286
  75.7 0.7 copy-start.3
  78.7 21.7 %all-to-all-start.2 = ((bf16[4,4,64,128]{3,2,1,0:T(8,128)(2,1)}), bf16[4,4,64,128]{3,2,1,0:T(8,128)(2,1)S(1)}, u32[]{:S(2)}, u32[]{:S(2)}) async-start(bf16[4,4,64,128]{3,2,1,0:T(8,128)(2,1)} %shard_map.87), calls=%async_computation.2 | async-start | bytes 524288 | tf_op jit(solution)/shard_map/all_to_all | solution.py:221
  83.1 4.3 %collective-permute-start.12 = (f32[2,64,128]{2,1,0:T(8,128)S(1)}, f32[2,64,128]{2,1,0:T(8,128)S(1)}, u32[]{:S(2)}, u32[]{:S(2)}) collective-permute-start(f32[2,64,128]{2,1,0:T(8,128)S(1)} %add.82), channel_id=1, source_target_pairs={{0,8},{4,12},{8,0},{12,4},{16,24},{20,28},{24,16},{28,20},{1,9},{5... | collective-permute-start | bytes 196616 | tf_op jit(solution)/shard_map/ppermute | solution.py:286
  87.4 7.8 %collective-permute-start.13 = (f32[2,64,128]{2,1,0:T(8,128)S(1)}, f32[2,64,128]{2,1,0:T(8,128)S(1)}, u32[]{:S(2)}, u32[]{:S(2)}) collective-permute-start(f32[2,64,128]{2,1,0:T(8,128)S(1)} %add.83), channel_id=1, source_target_pairs={{0,16},{4,20},{8,24},{12,28},{16,0},{20,4},{24,8},{28,12},{1,17},{... | collective-permute-start | bytes 196616 | tf_op jit(solution)/shard_map/ppermute | solution.py:286
  90.3 6.0 %collective-permute-start.10 = (bf16[4,64,128]{2,1,0:T(8,128)(2,1)}, bf16[4,64,128]{2,1,0:T(8,128)(2,1)S(1)}, u32[]{:S(2)}, u32[]{:S(2)}) collective-permute-start(bf16[4,64,128]{2,1,0:T(8,128)(2,1)} %get-tuple-element.29), channel_id=1, source_target_pairs={{0,3},{1,0},{2,1},{3,2},{4,7},{5,4},{6,5},{7,6},{8,11},{9,8},{10,9... | collective-permute-start | bytes 196616 | tf_op jit(solution)/shard_map/ppermute | solution.py:228
  94.1 6.3 %collective-permute-start.8 = (bf16[4,64,128]{2,1,0:T(8,128)(2,1)}, bf16[4,64,128]{2,1,0:T(8,128)(2,1)S(1)}, u32[]{:S(2)}, u32[]{:S(2)}) collective-permute-start(bf16[4,64,128]{2,1,0:T(8,128)(2,1)} %get-tuple-element.27), channel_id=1, source_target_pairs={{0,1},{1,2},{2,3},{3,0},{4,5},{5,6},{6,7},{7,4},{8,9},{9,10},{10,1... | collective-permute-start | bytes 196616 | tf_op jit(solution)/shard_map/ppermute | solution.py:228
  94.2 6.3 %collective-permute-start.9 = (bf16[4,64,128]{2,1,0:T(8,128)(2,1)}, bf16[4,64,128]{2,1,0:T(8,128)(2,1)S(1)}, u32[]{:S(2)}, u32[]{:S(2)}) collective-permute-start(bf16[4,64,128]{2,1,0:T(8,128)(2,1)} %get-tuple-element.28), channel_id=1, source_target_pairs={{0,2},{1,3},{2,0},{3,1},{4,6},{5,7},{6,4},{7,5},{8,10},{9,11},{10,... | collective-permute-start | bytes 196616 | tf_op jit(solution)/shard_map/ppermute | solution.py:228
  96.4 4.1 %copy-start.9 = (bf16[4,64,128]{2,1,0:T(8,128)(2,1)}, bf16[4,64,128]{2,1,0:T(8,128)(2,1)S(1)}, u32[]{:S(2)}) copy-start(bf16[4,64,128]{2,1,0:T(8,128)(2,1)S(1)} %collective-permute-done.10.rest_3_) | copy-start | bytes 196612
  100.4 0.6 copy-start.10
  100.4 0.6 copy-start.11
  100.4 0.7 copy-start.2

commit v4 on v3

--- a/solution.py
+++ b/solution.py
@@ -10,6 +10,7 @@
 
 REACH = 2
 CHUNKS = 2
+STEP = 4
 BF16 = jnp.bfloat16
 F32 = jnp.float32
 
@@ -42,7 +43,7 @@
     own = where[0]
     sign = 2 * lax.rem(own, 2) - 1
 
-    def row_block(b, carry):
+    def row_block(b):
         pltpu.make_async_copy(tiles_ref.at[b], held.at[b], sems.at[b]).wait()
         z = z_ref[b]
         live = cols[b, slots]
@@ -56,9 +57,13 @@
                 place = (offset * sign + REACH) * blocks + lax.rem(col, blocks)
                 place = jnp.where(s + half < live, place, window)
                 total[place] += terms[:, half * nodes : (half + 1) * nodes]
+
+    def step(i, carry):
+        for b in range(STEP):
+            row_block(i * STEP + b)
         return carry
 
-    lax.fori_loop(0, blocks, row_block, 0)
+    lax.fori_loop(0, blocks // STEP, step, 0)
 
     def store(out, base):
         def one(i, carry):
@@ -258,14 +263,20 @@
         return sum(term.astype(F32) for term in terms).astype(BF16)
 
     aside = lax.ppermute(aside, "blk", [(i, i ^ 1) for i in range(slabs)])
-    sums = []
+    near, beside = aside[:blocks], aside[blocks:]
+    one = [add(first[k], near[k * chunk : (k + 1) * chunk]) for k in range(CHUNKS)]
+    one_in, two_in, sums = [], [], []
+    for k in range(CHUNKS):
+        if k == CHUNKS - 1:
+            one[k], second[k], packed = lax.optimization_barrier((one[k], second[k], packed))
+        two_in.append(lax.ppermute(second[k], "blk", to_two))
+        one_in.append(lax.ppermute(one[k], "blk", to_one))
     for k in range(CHUNKS):
         span = slice(k * chunk, (k + 1) * chunk)
-        two_in = lax.ppermute(second[k], "blk", to_two)
-        one_in = lax.ppermute(add(first[k], aside[span]), "blk", to_one)
-        sums.append(add(own[span], aside[blocks:][span], one_in, two_in))
-
-    sums[0], packed = lax.optimization_barrier((sums[0], packed))
+        if k:
+            one_in[k], sums[k - 1] = lax.optimization_barrier((one_in[k], sums[k - 1]))
+        sums.append(add(own[span], beside[span], one_in[k], two_in[k]))
+
     part = chunk // reps
     mixed = mix(packed, 2 * share, exchange(sums[0].reshape(reps, part, features, nodes)))
     mixed = exchange(mixed).reshape(chunk, features, nodes)

time: 103 us -> 111 us (1.078)
  waiting for transfers between devices: 37.5 us -> 43.1 us
  starting transfers between devices: 32.7 us -> 34.2 us
    all_to_all x3, waiting for transfers between devices: 1.85 us -> 13.1 us  [exchange(): return lax.all_to_all(value, 'rep', 0, 0, tiled=True)]
    ppermute x4, waiting for transfers between devices: 18.4 us -> 15.2 us  [the longest x2 8.92 us: on_device(): one_in.append(lax.ppermute(one[k], 'blk', to_one))]
    ppermute x3, starting transfers between devices: 2.01 us -> 4.72 us  [on_device(): lax.ppermute(grad_w, 'blk', [(i, i ^ step) for i in range(slabs)])]
    ppermute x6, waiting for transfers between devices: 14.3 us -> 12.3 us  [shift(): lax.ppermute(value, 'rep', [(i, (i + steps) % reps) for i in range(reps)])]
    convert_element_type x2 -> x3, other arithmetic: 3.29 us -> 4.13 us  [add(): return sum((term.astype(F32) for term in terms)).astype(BF16)]
    unnamed x29 -> x31, local copies, waits for them, and re-layouts: 2.27 us -> 2.28 us
  transfers between devices with their start and end apart: 17 -> 17, of which waited for: 10 -> 10; matrix products, arithmetic and copies ran while one was open for 5% -> 4% of each run, Pallas kernels for 5% -> 6%
where the time goes in v4:
time: 111 us; the launch traced here: 110 us
  waiting for transfers between devices  43.1 us (39%)
  starting transfers between devices  34.2 us (31%)
  Pallas kernels  21.9 us (20%)
  other arithmetic  7.63 us (7%)
  local copies, waits for them, and re-layouts  2.39 us (2%)
    all_to_all x3, starting transfers between devices, exchange(): return lax.all_to_all(value, 'rep', 0, 0, tiled=True)  13.4 us
    all_to_all x3, waiting for transfers between devices, exchange(): return lax.all_to_all(value, 'rep', 0, 0, tiled=True)  13.1 us
    pallas_call x1, Pallas kernels, contributions(): pl.pallas_call(functools.partial(tiles_kernel, slabs), out_shape=[jax.Sha...  13 us
    ppermute x6, waiting for transfers between devices, shift(): lax.ppermute(value, 'rep', [(i, (i + steps) % reps) for i in range(reps)])  12.3 us
    ppermute x6, starting transfers between devices, shift(): lax.ppermute(value, 'rep', [(i, (i + steps) % reps) for i in range(reps)])  10.1 us
    ppermute x2, waiting for transfers between devices, on_device(): one_in.append(lax.ppermute(one[k], 'blk', to_one))  8.92 us
    ppermute x2, waiting for transfers between devices, on_device(): two_in.append(lax.ppermute(second[k], 'blk', to_two))  6.32 us
    ppermute x3, starting transfers between devices, on_device(): lax.ppermute(grad_w, 'blk', [(i, i ^ step) for i in range(slabs)])  4.72 us
  transfers between devices with their start and end apart: 17, of which 10 were waited for; matrix products, arithmetic and copies ran while one was open for 4% of the time, Pallas kernels for 6%

profile of v4, /device:TPU:0, one launch (start us, length us, event | category | flops | bytes accessed | tf_op | source)
XLA Modules:
  0.0 110.1 jit_solution(2604926038456196982)
XLA Ops:
  0.7 0.7 copy-done
  1.4 1.5 %convert_multiply_fusion.z_ref = bf16[32,64,128]{2,1,0:T(8,128)(2,1)S(1)} fusion(bf16[32,64,128]{2,1,0:T(8,128)(2,1)} %param.7, s32[32,64,128]{2,1,0:T(8,128)} %param.8), kind=kLoop, calls=%fused_computation.9 | loop fusion | flops 524288 | bytes 2097152 | tf_op jit(solution)/shard_map/mul | solution.py:247
  2.9 1.2 %pad_maximum_fusion = bf16[4,18,64,128]{3,2,1,0:T(8,128)(2,1)} fusion(bf16[4,2,64,128]{3,2,1,0:T(8,128)(2,1)S(1)} %broadcast_in_dim.10, bf16[4,8,64,128]{3,2,1,0:T(8,128)(2,1)S(1)} %bitcast.37, bf16[4,8,64,128]{3,2,1,0:T(8,128)(2,1)S(1)} %bitcast.33), kind=kLoop, calls=%fused_computation | loop fusion | flops 1179648 | bytes 2359296 | tf_op jit(solution)/shard_map/concatenate | solution.py:251
  4.4 13.0 %shard_map.86 = (bf16[64,64,128]{2,1,0:T(8,128)(2,1)S(1)}, bf16[32,64,128]{2,1,0:T(8,128)(2,1)S(1)}, bf16[16,64,128]{2,1,0:T(8,128)(2,1)S(1)}, bf16[16,64,128]{2...) custom-call(s32[2]{0:T(128)S(1)} %pad_add_fusion.1.where, ...), custom_call_target="tpu_custom_call" | custom-call | tf_op jit(solution)/shard_map/pallas_call | solution.py:87
  18.0 5.8 %all-to-all-start = ((bf16[4,18,64,128]{3,2,1,0:T(8,128)(2,1)}), bf16[4,18,64,128]{3,2,1,0:T(8,128)(2,1)}, u32[]{:S(2)}, u32[]{:S(2)}) async-start(bf16[4,18,64,128]{3,2,1,0:T(8,128)(2,1)} %pad_maximum_fusion), calls=%async_computation | async-start | bytes 2359296 | tf_op jit(solution)/shard_map/all_to_all | solution.py:226
  23.8 2.7 %collective-permute-start.3 = (bf16[16,64,128]{2,1,0:T(8,128)(2,1)S(1)}, bf16[16,64,128]{2,1,0:T(8,128)(2,1)S(1)}, u32[]{:S(2)}, u32[]{:S(2)}) collective-permute-start(bf16[16,64,128]{2,1,0:T(8,128)(2,1)S(1)} %get-tuple-element.28), channel_id=1, source_target_pairs={{0,24},{4,12},{8,0},{12,20},{16,8},{20,28},{24,16},{28,4},{1,25},{... | collective-permute-start | bytes 786440 | tf_op jit(solution)/shard_map/ppermute | solution.py:272
  26.5 1.0 add_convert_fusion.2
  27.6 5.7 %collective-permute-done.3 = bf16[16,64,128]{2,1,0:T(8,128)(2,1)S(1)} collective-permute-done((bf16[16,64,128]{2,1,0:T(8,128)(2,1)S(1)}, bf16[16,64,128]{2,1,0:T(8,128)(2,1)S(1)}, u32[]{:S(2)}, u32[]{:S(2)}) %collective-permute-start.3) | collective-permute-done | bytes 262176 | tf_op jit(solution)/shard_map/ppermute | solution.py:272
  33.3 4.8 %collective-permute-done.2 = bf16[16,64,128]{2,1,0:T(8,128)(2,1)S(1)} collective-permute-done((bf16[16,64,128]{2,1,0:T(8,128)(2,1)S(1)}, bf16[16,64,128]{2,1,0:T(8,128)(2,1)S(1)}, u32[]{:S(2)}, u32[]{:S(2)}) %collective-permute-start.2) | collective-permute-done | bytes 262176 | tf_op jit(solution)/shard_map/ppermute | solution.py:273
  38.0 2.0 %add_convert_fusion.1 = (bf16[16,64,128]{2,1,0:T(8,128)(2,1)}, bf16[16,64,128]{2,1,0:T(8,128)(2,1)S(1)}) fusion(bf16[16,64,128]{2,1,0:T(8,128)(2,1)S(1)} %collective-permute-done.3, bf16[16,64,128]{2,1,0:T(8,128)(2,1)S(1)} %collective-permute-done.2, bf16[64,64,128]{2,1,0:T(8,128)(2,1)} %collective-permute-done, ...), kind=kLoop, calls=%fused_computation.6 | loop fusion | flops 1572864 | bytes 2097152 | tf_op jit(solution)/shard_map/convert_element_type | solution.py:263
  40.0 13.1 %all-to-all-done.packed = bf16[4,18,64,128]{3,2,1,0:T(8,128)(2,1)} async-done(((bf16[4,18,64,128]{3,2,1,0:T(8,128)(2,1)}), bf16[4,18,64,128]{3,2,1,0:T(8,128)(2,1)}, u32[]{:S(2)}, u32[]{:S(2)}) %all-to-all-start) | async-done | bytes 1179680 | tf_op jit(solution)/shard_map/all_to_all | solution.py:226
  53.1 1.6 %collective-permute-start.1 = (bf16[16,64,128]{2,1,0:T(8,128)(2,1)S(1)}, bf16[16,64,128]{2,1,0:T(8,128)(2,1)S(1)}, u32[]{:S(2)}, u32[]{:S(2)}) collective-permute-start(bf16[16,64,128]{2,1,0:T(8,128)(2,1)S(1)} %get-tuple-element.25), channel_id=1, source_target_pairs={{0,28},{4,8},{8,4},{12,16},{16,12},{20,24},{24,20},{28,0},{1,29},{... | collective-permute-start | bytes 786440 | tf_op jit(solution)/shard_map/ppermute | solution.py:273
  54.8 1.0 collective-permute-start.4
  55.8 2.4 %shard_map.88 = bf16[4,2,64,128]{3,2,1,0:T(8,128)(2,1)} custom-call(bf16[4,18,64,128]{3,2,1,0:T(8,128)(2,1)} %all-to-all-done.packed), custom_call_target="tpu_custom_call" | custom-call | flops 134217728 | bytes 1179648 | tf_op jit(solution)/shard_map/pallas_call | solution.py:124
  58.2 4.1 %collective-permute-done.1 = bf16[16,64,128]{2,1,0:T(8,128)(2,1)S(1)} collective-permute-done((bf16[16,64,128]{2,1,0:T(8,128)(2,1)S(1)}, bf16[16,64,128]{2,1,0:T(8,128)(2,1)S(1)}, u32[]{:S(2)}, u32[]{:S(2)}) %collective-permute-start.1) | collective-permute-done | bytes 262176 | tf_op jit(solution)/shard_map/ppermute | solution.py:273
  62.3 3.4 %all-to-all-start.1 = ((bf16[4,4,64,128]{3,2,1,0:T(8,128)(2,1)}), bf16[4,4,64,128]{3,2,1,0:T(8,128)(2,1)S(1)}, u32[]{:S(2)}, u32[]{:S(2)}) async-start(bf16[4,4,64,128]{3,2,1,0:T(8,128)(2,1)} %bitcast.6), calls=%async_computation.1 | async-start | bytes 524288 | tf_op jit(solution)/shard_map/all_to_all | solution.py:226
  66.4 1.1 %add_convert_fusion = bf16[16,64,128]{2,1,0:T(8,128)(2,1)S(1)} fusion(bf16[16,64,128]{2,1,0:T(8,128)(2,1)S(1)} %collective-permute-done.4, bf16[16,64,128]{2,1,0:T(8,128)(2,1)S(1)} %collective-permute-done.1, bf16[64,64,128]{2,1,0:T(8,128)(2,1)} %collective-permute-done, bf16[32,64,128]{2,1,0:T(8,128)(2,1)S(1)} %get-tuple-element.26), kind=kLoop, calls=%fused_computation.5 | loop fusion | flops 1048576 | bytes 1310720 | tf_op jit(solution)/shard_map/convert_element_type | solution.py:263
  67.6 1.4 %collective-permute-start.5 = (bf16[6,64,128]{2,1,0:T(8,128)(2,1)S(1)}, bf16[6,64,128]{2,1,0:T(8,128)(2,1)S(1)}, u32[]{:S(2)}, u32[]{:S(2)}) collective-permute-start(bf16[6,64,128]{2,1,0:T(8,128)(2,1)S(1)} %get-tuple-element.40), channel_id=1, source_target_pairs={{0,1},{1,2},{2,3},{3,0},{4,5},{5,6},{6,7},{7,4},{8,9},{9,10},{10,1... | collective-permute-start | bytes 294920 | tf_op jit(solution)/shard_map/ppermute | solution.py:233
  69.0 2.4 %collective-permute-start.6 = (bf16[6,64,128]{2,1,0:T(8,128)(2,1)S(1)}, bf16[6,64,128]{2,1,0:T(8,128)(2,1)S(1)}, u32[]{:S(2)}, u32[]{:S(2)}) collective-permute-start(bf16[6,64,128]{2,1,0:T(8,128)(2,1)S(1)} %get-tuple-element.41), channel_id=1, source_target_pairs={{0,2},{1,3},{2,0},{3,1},{4,6},{5,7},{6,4},{7,5},{8,10},{9,11},{10,... | collective-permute-start | bytes 294920 | tf_op jit(solution)/shard_map/ppermute | solution.py:233
  71.3 1.5 %collective-permute-start.7 = (bf16[6,64,128]{2,1,0:T(8,128)(2,1)S(1)}, bf16[6,64,128]{2,1,0:T(8,128)(2,1)S(1)}, u32[]{:S(2)}, u32[]{:S(2)}) collective-permute-start(bf16[6,64,128]{2,1,0:T(8,128)(2,1)S(1)} %get-tuple-element.38), channel_id=1, source_target_pairs={{0,3},{1,0},{2,1},{3,2},{4,7},{5,4},{6,5},{7,6},{8,11},{9,8},{10,9... | collective-permute-start | bytes 294920 | tf_op jit(solution)/shard_map/ppermute | solution.py:233
  72.8 2.8 %collective-permute-done.5.rest_1_ = bf16[6,64,128]{2,1,0:T(8,128)(2,1)S(1)} collective-permute-done((bf16[6,64,128]{2,1,0:T(8,128)(2,1)S(1)}, bf16[6,64,128]{2,1,0:T(8,128)(2,1)S(1)}, u32[]{:S(2)}, u32[]{:S(2)}) %collective-permute-start.5) | collective-permute-done | bytes 98336 | tf_op jit(solution)/shard_map/ppermute | solution.py:233
  75.6 5.0 %collective-permute-done.6.rest_2_ = bf16[6,64,128]{2,1,0:T(8,128)(2,1)S(1)} collective-permute-done((bf16[6,64,128]{2,1,0:T(8,128)(2,1)S(1)}, bf16[6,64,128]{2,1,0:T(8,128)(2,1)S(1)}, u32[]{:S(2)}, u32[]{:S(2)}) %collective-permute-start.6) | collective-permute-done | bytes 98336 | tf_op jit(solution)/shard_map/ppermute | solution.py:233
  81.4 2.3 %shard_map.87 = bf16[4,4,64,128]{3,2,1,0:T(8,128)(2,1)} custom-call(bf16[4,18,64,128]{3,2,1,0:T(8,128)(2,1)} %all-to-all-done.packed, bf16[4,4,64,128]{3,2,1,0:T(8,128)(2,1)} %copy-done.3), custom_call_target="tpu_custom_call" | custom-call | flops 67108864 | bytes 524288 | tf_op jit(solution)/shard_map/pallas_call | solution.py:159
  83.8 4.1 %all-to-all-start.2 = ((bf16[4,4,64,128]{3,2,1,0:T(8,128)(2,1)}), bf16[4,4,64,128]{3,2,1,0:T(8,128)(2,1)S(1)}, u32[]{:S(2)}, u32[]{:S(2)}) async-start(bf16[4,4,64,128]{3,2,1,0:T(8,128)(2,1)} %shard_map.87), calls=%async_computation.2 | async-start | bytes 524288 | tf_op jit(solution)/shard_map/all_to_all | solution.py:226
  87.9 1.9 %collective-permute-start.12 = (f32[2,64,128]{2,1,0:T(8,128)S(1)}, f32[2,64,128]{2,1,0:T(8,128)S(1)}, u32[]{:S(2)}, u32[]{:S(2)}) collective-permute-start(f32[2,64,128]{2,1,0:T(8,128)S(1)} %add.82), channel_id=1, source_target_pairs={{0,8},{4,12},{8,0},{12,4},{16,24},{20,28},{24,16},{28,20},{1,9},{5... | collective-permute-start | bytes 196616 | tf_op jit(solution)/shard_map/ppermute | solution.py:297
  89.8 2.5 %collective-permute-done.12 = f32[2,64,128]{2,1,0:T(8,128)S(1)} collective-permute-done((f32[2,64,128]{2,1,0:T(8,128)S(1)}, f32[2,64,128]{2,1,0:T(8,128)S(1)}, u32[]{:S(2)}, u32[]{:S(2)}) %collective-permute-start.12) | collective-permute-done | bytes 65568 | tf_op jit(solution)/shard_map/ppermute | solution.py:297
  92.3 2.8 %collective-permute-start.13 = (f32[2,64,128]{2,1,0:T(8,128)S(1)}, f32[2,64,128]{2,1,0:T(8,128)S(1)}, u32[]{:S(2)}, u32[]{:S(2)}) collective-permute-start(f32[2,64,128]{2,1,0:T(8,128)S(1)} %add.83), channel_id=1, source_target_pairs={{0,16},{4,20},{8,24},{12,28},{16,0},{20,4},{24,8},{28,12},{1,17},{... | collective-permute-start | bytes 196616 | tf_op jit(solution)/shard_map/ppermute | solution.py:297
  95.1 2.3 %shard_map.89 = (bf16[4,64,128]{2,1,0:T(8,128)(2,1)}, bf16[4,64,128]{2,1,0:T(8,128)(2,1)}, bf16[4,64,128]{2,1,0:T(8,128)(2,1)}, bf16[4,64,128]{2,1,0:T(8,128)(2,1)}) custom-call(s32[2]{0:T(128)} %copy-done.1, bf16[4,18,64,128]{3,2,1,0:T(8,128)(2,1)} %all-to-all-done.packed, bf16[6,64,128]{2,1,0:T(8,128)(2,1)} %bitcast.36, bf16[6,64,128]{2,1,0:T(8,128)(2,1)} %copy-done.7, ...), custom_call_target="tpu_custom_call" | custom-call | flops 67108864 | bytes 524288 | tf_op jit(solution)/shard_map/pallas_call | solution.py:192
  97.4 3.8 %collective-permute-start.10 = (bf16[4,64,128]{2,1,0:T(8,128)(2,1)}, bf16[4,64,128]{2,1,0:T(8,128)(2,1)S(1)}, u32[]{:S(2)}, u32[]{:S(2)}) collective-permute-start(bf16[4,64,128]{2,1,0:T(8,128)(2,1)} %get-tuple-element.35), channel_id=1, source_target_pairs={{0,3},{1,0},{2,1},{3,2},{4,7},{5,4},{6,5},{7,6},{8,11},{9,8},{10,9... | collective-permute-start | bytes 196616 | tf_op jit(solution)/shard_map/ppermute | solution.py:233
  101.2 1.1 %collective-permute-start.9 = (bf16[4,64,128]{2,1,0:T(8,128)(2,1)}, bf16[4,64,128]{2,1,0:T(8,128)(2,1)S(1)}, u32[]{:S(2)}, u32[]{:S(2)}) collective-permute-start(bf16[4,64,128]{2,1,0:T(8,128)(2,1)} %get-tuple-element.34), channel_id=1, source_target_pairs={{0,2},{1,3},{2,0},{3,1},{4,6},{5,7},{6,4},{7,5},{8,10},{9,11},{10,... | collective-permute-start | bytes 196616 | tf_op jit(solution)/shard_map/ppermute | solution.py:233
  103.4 4.0 %collective-permute-done.8.rest_1_ = bf16[4,64,128]{2,1,0:T(8,128)(2,1)S(1)} collective-permute-done((bf16[4,64,128]{2,1,0:T(8,128)(2,1)}, bf16[4,64,128]{2,1,0:T(8,128)(2,1)S(1)}, u32[]{:S(2)}, u32[]{:S(2)}) %collective-permute-start.8) | collective-permute-done | bytes 65568 | tf_op jit(solution)/shard_map/ppermute | solution.py:233
  108.3 1.9 %shard_map.90 = bf16[32,64,128]{2,1,0:T(8,128)(2,1)} custom-call(s32[2]{0:T(128)} %copy-done.1, bf16[16,64,128]{2,1,0:T(8,128)(2,1)} %bitcast.35, bf16[4,64,128]{2,1,0:T(8,128)(2,1)} %get-tuple-element.32.rest_0_, bf16[4,64,128]{2,1,0:T(8,128)(2,1)} %copy-done.11, bf16[4,64,128]{2,1,0:T(8,128)(2,1)} %copy-done.12, bf16[4,64,128]{2,1,0:T(8,128)(2,1)} %copy-done.10), custom_call_target="tpu_custom_call" | custom-call | tf_op jit(solution)/shard_map/pallas_call | solution.py:217
  (53 shorter events, 4.4 us)
Async XLA Ops:
  0.6 0.8 copy-start
  0.6 2.2 %copy-start.6 = (bf16[32,64,128]{2,1,0:T(8,128)(2,1)S(1)}, bf16[32,64,128]{2,1,0:T(8,128)(2,1)}, u32[]{:S(2)}) copy-start(bf16[32,64,128]{2,1,0:T(8,128)(2,1)} %param.9) | copy-start | bytes 1572868
  2.9 1.2 %copy-start.13 = (s32[32,16]{0,1:T(8,128)S(1)}, s32[32,16]{0,1:T(8,128)}, u32[]{:S(2)}) copy-start(s32[32,16]{0,1:T(8,128)} %param.12) | copy-start | bytes 6148
  2.9 1.2 %copy-start.14 = (s32[32]{0:T(128)S(1)}, s32[32]{0:T(128)}, u32[]{:S(2)}) copy-start(s32[32]{0:T(128)} %param.13) | copy-start | bytes 388
  4.3 13.1 %copy-start.1 = (s32[2]{0:T(128)}, s32[2]{0:T(128)S(1)}, u32[]{:S(2)}) copy-start(s32[2]{0:T(128)S(1)} %pad_add_fusion.1.where) | copy-start | bytes 28
  17.4 9.1 %collective-permute-start = (bf16[64,64,128]{2,1,0:T(8,128)(2,1)S(1)}, bf16[64,64,128]{2,1,0:T(8,128)(2,1)}, u32[]{:S(2)}, u32[]{:S(2)}) collective-permute-start(bf16[64,64,128]{2,1,0:T(8,128)(2,1)S(1)} %get-tuple-element.21), channel_id=1, source_target_pairs={{0,4},{4,0},{8,12},{12,8},{16,20},{20,16},{24,28},{28,24},{1,5},{5... | collective-permute-start | bytes 3145736 | tf_op jit(solution)/shard_map/ppermute | solution.py:265
  18.0 35.1 %all-to-all-start = ((bf16[4,18,64,128]{3,2,1,0:T(8,128)(2,1)}), bf16[4,18,64,128]{3,2,1,0:T(8,128)(2,1)}, u32[]{:S(2)}, u32[]{:S(2)}) async-start(bf16[4,18,64,128]{3,2,1,0:T(8,128)(2,1)} %pad_maximum_fusion), calls=%async_computation | async-start | bytes 2359296 | tf_op jit(solution)/shard_map/all_to_all | solution.py:226
  23.8 9.4 %collective-permute-start.3 = (bf16[16,64,128]{2,1,0:T(8,128)(2,1)S(1)}, bf16[16,64,128]{2,1,0:T(8,128)(2,1)S(1)}, u32[]{:S(2)}, u32[]{:S(2)}) collective-permute-start(bf16[16,64,128]{2,1,0:T(8,128)(2,1)S(1)} %get-tuple-element.28), channel_id=1, source_target_pairs={{0,24},{4,12},{8,0},{12,20},{16,8},{20,28},{24,16},{28,4},{1,25},{... | collective-permute-start | bytes 786440 | tf_op jit(solution)/shard_map/ppermute | solution.py:272
  27.5 10.5 %collective-permute-start.2 = (bf16[16,64,128]{2,1,0:T(8,128)(2,1)S(1)}, bf16[16,64,128]{2,1,0:T(8,128)(2,1)S(1)}, u32[]{:S(2)}, u32[]{:S(2)}) collective-permute-start(bf16[16,64,128]{2,1,0:T(8,128)(2,1)S(1)} %add_convert_fusion.2), channel_id=1, source_target_pairs={{0,28},{4,8},{8,4},{12,16},{16,12},{20,24},{24,20},{28,0},{1,29},{... | collective-permute-start | bytes 786440 | tf_op jit(solution)/shard_map/ppermute | solution.py:273
  53.1 9.2 %collective-permute-start.1 = (bf16[16,64,128]{2,1,0:T(8,128)(2,1)S(1)}, bf16[16,64,128]{2,1,0:T(8,128)(2,1)S(1)}, u32[]{:S(2)}, u32[]{:S(2)}) collective-permute-start(bf16[16,64,128]{2,1,0:T(8,128)(2,1)S(1)} %get-tuple-element.25), channel_id=1, source_target_pairs={{0,28},{4,8},{8,4},{12,16},{16,12},{20,24},{24,20},{28,0},{1,29},{... | collective-permute-start | bytes 786440 | tf_op jit(solution)/shard_map/ppermute | solution.py:273
  54.8 11.6 %collective-permute-start.4 = (bf16[16,64,128]{2,1,0:T(8,128)(2,1)S(1)}, bf16[16,64,128]{2,1,0:T(8,128)(2,1)S(1)}, u32[]{:S(2)}, u32[]{:S(2)}) collective-permute-start(bf16[16,64,128]{2,1,0:T(8,128)(2,1)S(1)} %get-tuple-element.31), channel_id=1, source_target_pairs={{0,24},{4,12},{8,0},{12,20},{16,8},{20,28},{24,16},{28,4},{1,25},{... | collective-permute-start | bytes 786440 | tf_op jit(solution)/shard_map/ppermute | solution.py:272
  58.2 9.4 %copy-start.5 = (bf16[4,2,64,128]{3,2,1,0:T(8,128)(2,1)S(1)}, bf16[4,2,64,128]{3,2,1,0:T(8,128)(2,1)}, u32[]{:S(2)}) copy-start(bf16[4,2,64,128]{3,2,1,0:T(8,128)(2,1)} %shard_map.88) | copy-start | bytes 393220
  62.3 18.4 %all-to-all-start.1 = ((bf16[4,4,64,128]{3,2,1,0:T(8,128)(2,1)}), bf16[4,4,64,128]{3,2,1,0:T(8,128)(2,1)S(1)}, u32[]{:S(2)}, u32[]{:S(2)}) async-start(bf16[4,4,64,128]{3,2,1,0:T(8,128)(2,1)} %bitcast.6), calls=%async_computation.1 | async-start | bytes 524288 | tf_op jit(solution)/shard_map/all_to_all | solution.py:226
  67.6 16.2 %copy-start.4 = (bf16[1,6,64,128]{3,2,1,0:T(8,128)(2,1)}, bf16[1,6,64,128]{3,2,1,0:T(8,128)(2,1)S(1)}, u32[]{:S(2)}) copy-start(bf16[1,6,64,128]{3,2,1,0:T(8,128)(2,1)S(1)} %get-tuple-element.39) | copy-start | bytes 294916
  67.6 8.0 %collective-permute-start.5 = (bf16[6,64,128]{2,1,0:T(8,128)(2,1)S(1)}, bf16[6,64,128]{2,1,0:T(8,128)(2,1)S(1)}, u32[]{:S(2)}, u32[]{:S(2)}) collective-permute-start(bf16[6,64,128]{2,1,0:T(8,128)(2,1)S(1)} %get-tuple-element.40), channel_id=1, source_target_pairs={{0,1},{1,2},{2,3},{3,0},{4,5},{5,6},{6,7},{7,4},{8,9},{9,10},{10,1... | collective-permute-start | bytes 294920 | tf_op jit(solution)/shard_map/ppermute | solution.py:233
  69.0 11.6 %collective-permute-start.6 = (bf16[6,64,128]{2,1,0:T(8,128)(2,1)S(1)}, bf16[6,64,128]{2,1,0:T(8,128)(2,1)S(1)}, u32[]{:S(2)}, u32[]{:S(2)}) collective-permute-start(bf16[6,64,128]{2,1,0:T(8,128)(2,1)S(1)} %get-tuple-element.41), channel_id=1, source_target_pairs={{0,2},{1,3},{2,0},{3,1},{4,6},{5,7},{6,4},{7,5},{8,10},{9,11},{10,... | collective-permute-start | bytes 294920 | tf_op jit(solution)/shard_map/ppermute | solution.py:233
  71.3 9.3 %collective-permute-start.7 = (bf16[6,64,128]{2,1,0:T(8,128)(2,1)S(1)}, bf16[6,64,128]{2,1,0:T(8,128)(2,1)S(1)}, u32[]{:S(2)}, u32[]{:S(2)}) collective-permute-start(bf16[6,64,128]{2,1,0:T(8,128)(2,1)S(1)} %get-tuple-element.38), channel_id=1, source_target_pairs={{0,3},{1,0},{2,1},{3,2},{4,7},{5,4},{6,5},{7,6},{8,11},{9,8},{10,9... | collective-permute-start | bytes 294920 | tf_op jit(solution)/shard_map/ppermute | solution.py:233
  75.6 8.2 %copy-start.7 = (bf16[6,64,128]{2,1,0:T(8,128)(2,1)}, bf16[6,64,128]{2,1,0:T(8,128)(2,1)S(1)}, u32[]{:S(2)}) copy-start(bf16[6,64,128]{2,1,0:T(8,128)(2,1)S(1)} %collective-permute-done.5.rest_1_) | copy-start | bytes 294916
  80.6 14.5 %copy-start.8 = (bf16[6,64,128]{2,1,0:T(8,128)(2,1)}, bf16[6,64,128]{2,1,0:T(8,128)(2,1)S(1)}, u32[]{:S(2)}) copy-start(bf16[6,64,128]{2,1,0:T(8,128)(2,1)S(1)} %collective-permute-done.6.rest_2_) | copy-start | bytes 294916
  80.6 14.5 %copy-start.9 = (bf16[6,64,128]{2,1,0:T(8,128)(2,1)}, bf16[6,64,128]{2,1,0:T(8,128)(2,1)S(1)}, u32[]{:S(2)}) copy-start(bf16[6,64,128]{2,1,0:T(8,128)(2,1)S(1)} %collective-permute-done.7.rest_3_) | copy-start | bytes 294916
  80.6 7.3 %collective-permute-start.11 = (f32[2,64,128]{2,1,0:T(8,128)S(1)}, f32[2,64,128]{2,1,0:T(8,128)S(1)}, u32[]{:S(2)}, u32[]{:S(2)}) collective-permute-start(f32[2,64,128]{2,1,0:T(8,128)S(1)} %fusion.8), channel_id=1, source_target_pairs={{0,4},{4,0},{8,12},{12,8},{16,20},{20,16},{24,28},{28,24},{1,5},{5... | collective-permute-start | bytes 196616 | tf_op jit(solution)/shard_map/ppermute | solution.py:297
  80.7 0.7 copy-start.3
  83.8 23.8 %all-to-all-start.2 = ((bf16[4,4,64,128]{3,2,1,0:T(8,128)(2,1)}), bf16[4,4,64,128]{3,2,1,0:T(8,128)(2,1)S(1)}, u32[]{:S(2)}, u32[]{:S(2)}) async-start(bf16[4,4,64,128]{3,2,1,0:T(8,128)(2,1)} %shard_map.87), calls=%async_computation.2 | async-start | bytes 524288 | tf_op jit(solution)/shard_map/all_to_all | solution.py:226
  87.9 4.3 %collective-permute-start.12 = (f32[2,64,128]{2,1,0:T(8,128)S(1)}, f32[2,64,128]{2,1,0:T(8,128)S(1)}, u32[]{:S(2)}, u32[]{:S(2)}) collective-permute-start(f32[2,64,128]{2,1,0:T(8,128)S(1)} %add.82), channel_id=1, source_target_pairs={{0,8},{4,12},{8,0},{12,4},{16,24},{20,28},{24,16},{28,20},{1,9},{5... | collective-permute-start | bytes 196616 | tf_op jit(solution)/shard_map/ppermute | solution.py:297
  92.3 10.1 %collective-permute-start.13 = (f32[2,64,128]{2,1,0:T(8,128)S(1)}, f32[2,64,128]{2,1,0:T(8,128)S(1)}, u32[]{:S(2)}, u32[]{:S(2)}) collective-permute-start(f32[2,64,128]{2,1,0:T(8,128)S(1)} %add.83), channel_id=1, source_target_pairs={{0,16},{4,20},{8,24},{12,28},{16,0},{20,4},{24,8},{28,12},{1,17},{... | collective-permute-start | bytes 196616 | tf_op jit(solution)/shard_map/ppermute | solution.py:297
  97.4 6.0 %collective-permute-start.10 = (bf16[4,64,128]{2,1,0:T(8,128)(2,1)}, bf16[4,64,128]{2,1,0:T(8,128)(2,1)S(1)}, u32[]{:S(2)}, u32[]{:S(2)}) collective-permute-start(bf16[4,64,128]{2,1,0:T(8,128)(2,1)} %get-tuple-element.35), channel_id=1, source_target_pairs={{0,3},{1,0},{2,1},{3,2},{4,7},{5,4},{6,5},{7,6},{8,11},{9,8},{10,9... | collective-permute-start | bytes 196616 | tf_op jit(solution)/shard_map/ppermute | solution.py:233
  101.2 6.3 %collective-permute-start.8 = (bf16[4,64,128]{2,1,0:T(8,128)(2,1)}, bf16[4,64,128]{2,1,0:T(8,128)(2,1)S(1)}, u32[]{:S(2)}, u32[]{:S(2)}) collective-permute-start(bf16[4,64,128]{2,1,0:T(8,128)(2,1)} %get-tuple-element.33), channel_id=1, source_target_pairs={{0,1},{1,2},{2,3},{3,0},{4,5},{5,6},{6,7},{7,4},{8,9},{9,10},{10,1... | collective-permute-start | bytes 196616 | tf_op jit(solution)/shard_map/ppermute | solution.py:233
  101.2 6.3 %collective-permute-start.9 = (bf16[4,64,128]{2,1,0:T(8,128)(2,1)}, bf16[4,64,128]{2,1,0:T(8,128)(2,1)S(1)}, u32[]{:S(2)}, u32[]{:S(2)}) collective-permute-start(bf16[4,64,128]{2,1,0:T(8,128)(2,1)} %get-tuple-element.34), channel_id=1, source_target_pairs={{0,2},{1,3},{2,0},{3,1},{4,6},{5,7},{6,4},{7,5},{8,10},{9,11},{10,... | collective-permute-start | bytes 196616 | tf_op jit(solution)/shard_map/ppermute | solution.py:233
  103.4 4.1 %copy-start.10 = (bf16[4,64,128]{2,1,0:T(8,128)(2,1)}, bf16[4,64,128]{2,1,0:T(8,128)(2,1)S(1)}, u32[]{:S(2)}) copy-start(bf16[4,64,128]{2,1,0:T(8,128)(2,1)S(1)} %collective-permute-done.10.rest_3_) | copy-start | bytes 196612
  107.5 0.6 copy-start.11
  107.5 0.6 copy-start.12
  107.5 0.7 copy-start.2

commit v5 on v2

v5 whole, which is shorter than its diff:
```python
import functools
import math

import jax
import jax.numpy as jnp
from jax import lax
from jax.experimental import pallas as pl
from jax.experimental.pallas import tpu as pltpu
from jax.sharding import PartitionSpec as P

REACH = 2
STEP = 16
BF16 = jnp.bfloat16
F32 = jnp.float32


def vmem():
    return pl.BlockSpec(memory_space=pltpu.VMEM)


def smem():
    return pl.BlockSpec(memory_space=pltpu.SMEM)


def hbm():
    return pl.BlockSpec(memory_space=pl.ANY)


NEAR, LEAVE, STAY = 0, 1, 2
GROUPS = 3


def list_kernel(slabs, where, cols, lists):
    blocks, slots = cols.shape[0], cols.shape[1] - 1
    count = blocks * slots
    own = where[0]
    sign = 2 * lax.rem(own, 2) - 1

    def row_block(b, lengths):
        def slot(s, lengths):
            col = cols[b, s]
            offset = lax.rem(lax.div(col, blocks) - own + REACH + slabs, slabs) - REACH
            order = offset * sign + REACH
            group = jnp.where(order == 0, NEAR, jnp.where(order <= REACH, STAY, LEAVE))
            first = jnp.where(order <= REACH, 1, REACH + 1)
            half = jnp.where(order == 0, 0, order - first)
            place = half * blocks + lax.rem(col, blocks)
            length = jnp.where(group == 0, lengths[0], jnp.where(group == 1, lengths[1], lengths[2]))
            lists[group * count + length] = (b * slots + s) * (2 * blocks) + place
            return tuple(
                length + (group == g).astype(jnp.int32) for g, length in enumerate(lengths)
            )

        return lax.fori_loop(0, cols[b, slots], slot, lengths)

    zero = jnp.int32(0)
    lengths = lax.fori_loop(0, blocks, row_block, (zero,) * GROUPS)
    for g in range(GROUPS):
        lists[GROUPS * count + g] = lengths[g]


def list_tiles(where, cols, slabs):
    count = cols.shape[0] * (cols.shape[1] - 1)
    return pl.pallas_call(
        functools.partial(list_kernel, slabs),
        out_shape=jax.ShapeDtypeStruct((GROUPS * count + 8,), jnp.int32),
        in_specs=[smem(), smem()],
        out_specs=smem(),
    )(where, cols)


def tiles_kernel(group, slots, lists, z_ref, held, *rest):
    outs, totals = rest[:-2], rest[-2:]
    blocks = z_ref.shape[0]
    count = held.shape[0]
    window = len(outs) * blocks

    def clear(i, carry):
        for total in totals:
            total[i] = jnp.zeros(total.shape[1:], F32)
        return carry

    lax.fori_loop(0, window, clear, 0)
    length = lists[GROUPS * count + group]

    def step(i, carry):
        for u in range(STEP):
            k = i * STEP + u
            entry = lists[group * count + jnp.minimum(k, count - 1)]
            entry = jnp.where(k < length, entry, window)
            tile = lax.div(entry, 2 * blocks)
            place = jnp.where(k < length, lax.rem(entry, 2 * blocks), window)
            tile = jnp.where(k < length, tile, 0)
            total = totals[u % 2]
            total[place] += jnp.dot(
                z_ref[lax.div(tile, slots)], held[tile], preferred_element_type=F32
            )
        return carry

    lax.fori_loop(0, lax.div(length + STEP - 1, STEP), step, 0)

    for part, out in enumerate(outs):

        def store(i, carry, out=out, base=part * blocks):
            out[i] = (totals[0][base + i] + totals[1][base + i]).astype(BF16)
            return carry

        lax.fori_loop(0, blocks, store, 0)


def tile_sums(group, lists, z, held, slots):
    blocks, features, nodes = z.shape
    parts = 1 if group == NEAR else 2
    return pl.pallas_call(
        functools.partial(tiles_kernel, group, slots),
        out_shape=[jax.ShapeDtypeStruct(z.shape, BF16)] * parts,
        in_specs=[smem(), vmem(), vmem()],
        out_specs=[vmem()] * parts,
        scratch_shapes=[pltpu.VMEM((parts * blocks + 1, features, nodes), F32)] * 2,
        compiler_params=pltpu.CompilerParams(vmem_limit_bytes=28 << 20),
        cost_estimate=pl.CostEstimate(
            flops=parts * blocks * slots * features * nodes * nodes // 4,
            bytes_accessed=parts * z.size * 4,
            transcendentals=0,
        ),
    )(lists, z, pltpu.with_memory_space_constraint(held, pltpu.VMEM))


def weight_kernel(packed, aggs, out, whole_z, whole_a):
    blocks, features = whole_z.shape[0], packed.shape[2]
    for q in range(packed.shape[0]):
        rows = pl.ds(q * features, features)
        whole_z[:, rows, :] = packed[q, :blocks]
        whole_a[:, rows, :] = aggs[q]
    total = jnp.zeros((whole_a.shape[1], whole_z.shape[1]), F32)
    for b in range(blocks):
        total += lax.dot_general(
            whole_a[b], whole_z[b], (((1,), (1,)), ((), ())), preferred_element_type=F32
        )
    nodes = out.shape[3]
    for q in range(out.shape[0]):
        for h in range(out.shape[1]):
            part = total[q * features : (q + 1) * features, h * nodes : (h + 1) * nodes]
            out[q, h] = part.astype(BF16)


def weight_partial(packed, aggs):
    reps, blocks, features, nodes = aggs.shape
    width = reps * features
    return pl.pallas_call(
        weight_kernel,
        out_shape=jax.ShapeDtypeStruct((reps, width // nodes, features, nodes), BF16),
        in_specs=[vmem(), vmem()],
        out_specs=vmem(),
        scratch_shapes=[pltpu.VMEM((blocks, width, nodes), BF16)] * 2,
        cost_estimate=pl.CostEstimate(
            flops=2 * blocks * nodes * width * width,
            bytes_accessed=4 * blocks * nodes * width + 2 * width * width,
            transcendentals=0,
        ),
    )(packed, aggs)


def mix_kernel(packed, out, weights, whole):
    reps, blocks, features, nodes = out.shape
    for q in range(reps):
        rows = pl.ds(q * features, features)
        for h in range(weights.shape[1] // nodes):
            weights[rows, pl.ds(h * nodes, nodes)] = packed[q, blocks + h]
        whole[:, rows, :] = packed[q, :blocks]
    for b in range(blocks):
        mixed = jnp.dot(weights[...], whole[b], preferred_element_type=F32)
        for q in range(reps):
            out[q, b] = mixed[q * features : (q + 1) * features].astype(BF16)


def mix(packed, blocks):
    reps, _, features, nodes = packed.shape
    width = reps * features
    return pl.pallas_call(
        mix_kernel,
        out_shape=jax.ShapeDtypeStruct((reps, blocks, features, nodes), BF16),
        in_specs=[vmem()],
        out_specs=vmem(),
        scratch_shapes=[pltpu.VMEM((width, width), BF16), pltpu.VMEM((blocks, width, nodes), BF16)],
        cost_estimate=pl.CostEstimate(
            flops=2 * blocks * nodes * width * width,
            bytes_accessed=4 * blocks * nodes * width,
            transcendentals=0,
        ),
    )(packed)


def exchange(value):
    return lax.all_to_all(value, "rep", 0, 0, tiled=True)


def on_device(cotangent, relu_mask, aggregated, weight, tiles, col_block, live_count):
    blocks, features, nodes = cotangent.shape
    slots = tiles.shape[1]
    slabs, reps = lax.axis_size("blk"), lax.axis_size("rep")
    width = weight.shape[1]
    pieces = width // nodes
    share = blocks // reps
    where = lax.axis_index("blk").astype(jnp.int32)[None]
    cols = jnp.concatenate([col_block, live_count[:, None]], axis=1)

    grad_z = cotangent * relu_mask.astype(BF16)
    by_share = (reps, share, features, nodes)
    weight_pieces = weight.reshape(features, pieces, nodes).transpose(1, 0, 2)
    weight_pieces = jnp.broadcast_to(weight_pieces[None], (reps, pieces, features, nodes))
    packed = jnp.concatenate([grad_z.reshape(by_share), weight_pieces], axis=1)
    packed, cols = lax.optimization_barrier((packed, cols))
    packed = exchange(packed)
    lists = list_tiles(where, cols, slabs)
    held = tiles.reshape(blocks * slots, nodes, nodes)
    grad_h = exchange(mix(packed, share)).reshape(blocks, features, nodes)

    pair = [(i, i ^ 1) for i in range(slabs)]
    to_one = [(i, (i + (1 if i % 2 else -1)) % slabs) for i in range(slabs)]
    to_two = [(i, (i + (2 if i % 2 else -2)) % slabs) for i in range(slabs)]

    def add(*terms):
        return sum(term.astype(F32) for term in terms).astype(BF16)

    (near,) = tile_sums(NEAR, lists, grad_h, held, slots)
    near_in = lax.ppermute(near, "blk", pair)
    one, two = tile_sums(LEAVE, lists, grad_h, held, slots)
    one = add(one, near_in)
    two_in = lax.ppermute(two, "blk", to_two)
    one_in = lax.ppermute(one, "blk", to_one)
    beside, own = tile_sums(STAY, lists, grad_h, held, slots)
    beside_in = lax.ppermute(beside, "blk", pair)
    input_grad = add(own, beside_in, one_in, two_in)

    aggs, near = lax.optimization_barrier((aggregated, near))
    grad_w = weight_partial(packed, exchange(aggs.reshape(by_share)))
    grad_w = exchange(grad_w).astype(F32).sum(0)
    step = 1
    while step < slabs:
        grad_w = grad_w + lax.ppermute(grad_w, "blk", [(i, i ^ step) for i in range(slabs)])
        step *= 2
    grad_w = grad_w.transpose(1, 0, 2).reshape(features, width)
    return input_grad, grad_w * (1.0 / math.sqrt(slabs * blocks * nodes))


def solution(mesh):
    placed = (
        P("blk", "rep", None),
        P("blk", "rep", None),
        P("blk", "rep", None),
        P("rep", None),
        P("blk", None, None, None),
        P("blk", None),
        P("blk"),
    )
    return jax.shard_map(
        on_device,
        mesh=mesh,
        in_specs=placed,
        out_specs=(P("blk", "rep", None), P("rep", None)),
        check_vma=False,
    )
```

time: 126 us -> 107 us (0.85)
  waiting for transfers between devices: 50.6 us -> 9.99 us
  blocking collectives: 0 us -> 34.9 us
  starting transfers between devices: 43.6 us -> 10.1 us
  local copies, waits for them, and re-layouts: 2.24 us -> 14.6 us
  Pallas kernels: 18.7 us -> 29 us
  other arithmetic: 9.51 us -> 7.09 us
    all_to_all x7 -> x2, waiting for transfers between devices: 41 us -> 0.96 us  [exchange(): return lax.all_to_all(value, 'rep', 0, 0, tiled=True)]
    all_to_all x0 -> x2, blocking collectives: none -> 34.9 us  [exchange(): return lax.all_to_all(value, 'rep', 0, 0, tiled=True)]
    all_to_all x7 -> x2, starting transfers between devices: 26.8 us -> 7.59 us  [exchange(): return lax.all_to_all(value, 'rep', 0, 0, tiled=True)]
    unnamed x13, local copies, waits for them, and re-layouts: 0.85 us -> 13.8 us
    pallas_call x4 -> x6, Pallas kernels: 18.7 us -> 29 us  [the longest x1 12.6 us: list_tiles(): pl.pallas_call(functools.partial(list_kernel, slabs), out_shape=jax.Shape...]
    ppermute x3, starting transfers between devices: 8.89 us -> 0.45 us  [on_device(): lax.ppermute(grad_w, 'blk', [(i, i ^ step) for i in range(slabs)])]
    ppermute x6 -> x3, starting transfers between devices: 6.52 us -> 0.2 us  [the longest x1 0.07 us: on_device(): near_in = lax.ppermute(near, 'blk', pair)]
    ppermute x2 -> x1, waiting for transfers between devices: 4.51 us -> 0.01 us  [on_device(): one_in = lax.ppermute(one, 'blk', to_one)]
  transfers between devices with their start and end apart: 18 -> 9, of which waited for: 10 -> 4; matrix products, arithmetic and copies ran while one was open for 6% -> 4% of each run, Pallas kernels for 5% -> 23%
where the time goes in v5:
time: 107 us
  blocking collectives  34.9 us (33%)
  Pallas kernels  29 us (27%)
  local copies, waits for them, and re-layouts  14.6 us (14%)
  starting transfers between devices  10.1 us (9%)
  waiting for transfers between devices  9.99 us (9%)
  other arithmetic  7.09 us (7%)
    all_to_all x2, blocking collectives, exchange(): return lax.all_to_all(value, 'rep', 0, 0, tiled=True)  34.9 us
    unnamed x13, local copies, waits for them, and re-layouts  13.8 us
    pallas_call x1, Pallas kernels, list_tiles(): pl.pallas_call(functools.partial(list_kernel, slabs), out_shape=jax.Shape...  12.6 us
    pallas_call x3, Pallas kernels, tile_sums(): pl.pallas_call(functools.partial(tiles_kernel, group, slots), out_shape=[...  11.7 us
    ppermute x3, waiting for transfers between devices, on_device(): lax.ppermute(grad_w, 'blk', [(i, i ^ step) for i in range(slabs)])  9.03 us
    all_to_all x2, starting transfers between devices, exchange(): return lax.all_to_all(value, 'rep', 0, 0, tiled=True)  7.59 us
    convert_element_type x2, other arithmetic, add(): return sum((term.astype(F32) for term in terms)).astype(BF16)  4.21 us
    pallas_call x1, Pallas kernels, weight_partial(): pl.pallas_call(weight_kernel, out_shape=jax.ShapeDtypeStruct((reps, width...  2.35 us
  transfers between devices with their start and end apart: 9, of which 4 were waited for; matrix products, arithmetic and copies ran while one was open for 4% of the time, Pallas kernels for 23%

profile of v5, /device:TPU:0, one launch (start us, length us, event | category | flops | bytes accessed | tf_op | source)
XLA Modules:
  0.0 106.5 jit_solution(8643112650999182013)
XLA Ops:
  0.6 0.8 copy.16
  1.4 0.7 copy.17
  2.2 0.7 pad_add_fusion.cols
  2.8 1.5 %convert_multiply_fusion = bf16[32,64,128]{2,1,0:T(8,128)(2,1)S(1)} fusion(bf16[32,64,128]{2,1,0:T(8,128)(2,1)} %param.7, s32[32,64,128]{2,1,0:T(8,128)} %param.8), kind=kLoop, calls=%fused_computation.3 | loop fusion | flops 524288 | bytes 2097152 | tf_op jit(solution)/shard_map/mul | solution.py:208
  4.3 0.1 pad_maximum_fusion
  4.4 23.5 %all_to_all.20.packed = bf16[4,10,64,128]{3,2,1,0:T(8,128)(2,1)} all-to-all(bf16[4,10,64,128]{3,2,1,0:T(8,128)(2,1)S(1)} %pad_maximum_fusion), channel_id=1, replica_groups=mesh['blk'=8,'rep'=4] {'rep'}, dimensions={0} | all-to-all | bytes 1310720 | tf_op jit(solution)/shard_map/all_to_all | solution.py:195
  27.9 2.3 %shard_map.87 = bf16[4,8,64,128]{3,2,1,0:T(8,128)(2,1)} custom-call(bf16[4,10,64,128]{3,2,1,0:T(8,128)(2,1)} %all_to_all.20.packed), custom_call_target="tpu_custom_call" | custom-call | flops 134217728 | bytes 1048576 | tf_op jit(solution)/shard_map/pallas_call | solution.py:180
  30.2 3.5 %all-to-all-start.1 = ((bf16[4,8,64,128]{3,2,1,0:T(8,128)(2,1)}), bf16[4,8,64,128]{3,2,1,0:T(8,128)(2,1)S(1)}, u32[]{:S(2)}, u32[]{:S(2)}) async-start(bf16[4,8,64,128]{3,2,1,0:T(8,128)(2,1)} %shard_map.87), calls=%async_computation.1 | async-start | bytes 1048576 | tf_op jit(solution)/shard_map/all_to_all | solution.py:195
  33.7 12.6 %shard_map.86.lists = s32[1544]{0:T(1024)} custom-call(s32[1]{0:T(128)} %bitcast.where, s32[32,17]{1,0:T(8,128)} %pad_add_fusion.cols), custom_call_target="tpu_custom_call" | custom-call | tf_op jit(solution)/shard_map/pallas_call | solution.py:64
  46.4 1.0 all-to-all-done.1
  47.3 5.8 %copy-done.1 = bf16[32,16,128,128]{3,2,1,0:T(8,128)(2,1)S(1)} copy-done((bf16[32,16,128,128]{3,2,1,0:T(8,128)(2,1)S(1)}, bf16[32,16,128,128]{3,2,1,0:T(8,128)(2,1)}, u32[]{:S(2)}) %copy-start.1) | copy-done | bytes 16777240
  53.1 0.7 copy-done.3
  53.8 2.5 %shard_map.90 = bf16[32,64,128]{2,1,0:T(8,128)(2,1)S(1)} custom-call(s32[1544]{0:T(1024)S(1)} %copy-done.3, bf16[32,64,128]{2,1,0:T(8,128)(2,1)S(1)} %bitcast.22, bf16[512,128,128]{2,1,0:T(8,128)(2,1)S(1)} %bitcast.19), custom_call_target="tpu_custom_call" | custom-call | flops 134217728 | bytes 1048576 | tf_op jit(solution)/shard_map/pallas_call | solution.py:114
  56.3 0.1 collective-permute-start.1
  56.4 4.1 %all-to-all-start.2 = ((bf16[4,8,64,128]{3,2,1,0:T(8,128)(2,1)}), bf16[4,8,64,128]{3,2,1,0:T(8,128)(2,1)S(1)}, u32[]{:S(2)}, u32[]{:S(2)}) async-start(bf16[4,8,64,128]{3,2,1,0:T(8,128)(2,1)} %bitcast.6), calls=%async_computation.2 | async-start | bytes 1048576 | tf_op jit(solution)/shard_map/all_to_all | solution.py:195
  60.5 5.8 %copy-done.2 = bf16[32,16,128,128]{3,2,1,0:T(8,128)(2,1)S(1)} copy-done((bf16[32,16,128,128]{3,2,1,0:T(8,128)(2,1)S(1)}, bf16[32,16,128,128]{3,2,1,0:T(8,128)(2,1)}, u32[]{:S(2)}) %copy-start.2) | copy-done | bytes 16777240
  66.3 4.6 %shard_map.88 = (bf16[32,64,128]{2,1,0:T(8,128)(2,1)S(1)}, bf16[32,64,128]{2,1,0:T(8,128)(2,1)S(1)}) custom-call(s32[1544]{0:T(1024)S(1)} %copy-done.4, bf16[32,64,128]{2,1,0:T(8,128)(2,1)S(1)} %bitcast.23, bf16[512,128,128]{2,1,0:T(8,128)(2,1)S(1)} %bitcast.20), custom_call_target="tpu_custom_call" | custom-call | flops 268435456 | bytes 2097152 | tf_op jit(solution)/shard_map/pallas_call | solution.py:114
  70.9 0.1 collective-permute-start
  71.0 4.6 %shard_map.89 = (bf16[32,64,128]{2,1,0:T(8,128)(2,1)S(1)}, bf16[32,64,128]{2,1,0:T(8,128)(2,1)S(1)}) custom-call(s32[1544]{0:T(1024)S(1)} %copy-done.4, bf16[32,64,128]{2,1,0:T(8,128)(2,1)S(1)} %bitcast.24, bf16[512,128,128]{2,1,0:T(8,128)(2,1)S(1)} %bitcast.21), custom_call_target="tpu_custom_call" | custom-call | flops 268435456 | bytes 2097152 | tf_op jit(solution)/shard_map/pallas_call | solution.py:114
  75.7 2.0 %add_convert_fusion.1 = bf16[32,64,128]{2,1,0:T(8,128)(2,1)} fusion(bf16[32,64,128]{2,1,0:T(8,128)(2,1)} %collective-permute-done.1, bf16[32,64,128]{2,1,0:T(8,128)(2,1)S(1)} %get-tuple-element.13), kind=kLoop, calls=%fused_computation.1 | loop fusion | flops 1048576 | bytes 1572864 | tf_op jit(solution)/shard_map/convert_element_type | solution.py:224
  77.7 1.9 %collective-permute-start.2 = (bf16[32,64,128]{2,1,0:T(8,128)(2,1)}, bf16[32,64,128]{2,1,0:T(8,128)(2,1)S(1)}, u32[]{:S(2)}, u32[]{:S(2)}) collective-permute-start(bf16[32,64,128]{2,1,0:T(8,128)(2,1)} %add_convert_fusion.1), channel_id=1, source_target_pairs={{0,28},{4,8},{8,4},{12,16},{16,12},{20,24},{24,20},{28,0},{1,29},{... | collective-permute-start | bytes 1572872 | tf_op jit(solution)/shard_map/ppermute | solution.py:231
  79.6 0.8 copy-done.5
  80.4 2.4 %shard_map.91 = bf16[4,2,64,128]{3,2,1,0:T(8,128)(2,1)} custom-call(bf16[4,10,64,128]{3,2,1,0:T(8,128)(2,1)} %all_to_all.20.packed, bf16[4,8,64,128]{3,2,1,0:T(8,128)(2,1)} %copy-done.5), custom_call_target="tpu_custom_call" | custom-call | flops 134217728 | bytes 1179648 | tf_op jit(solution)/shard_map/pallas_call | solution.py:150
  82.7 11.4 %all_to_all.21 = bf16[4,2,64,128]{3,2,1,0:T(8,128)(2,1)S(1)} all-to-all(bf16[4,2,64,128]{3,2,1,0:T(8,128)(2,1)} %shard_map.91), channel_id=1, replica_groups=mesh['blk'=8,'rep'=4] {'rep'}, dimensions={0} | all-to-all | bytes 262144 | tf_op jit(solution)/shard_map/all_to_all | solution.py:195
  94.2 0.1 collective-permute-start.4
  94.2 1.2 %collective-permute-done.4 = f32[2,64,128]{2,1,0:T(8,128)S(1)} collective-permute-done((f32[2,64,128]{2,1,0:T(8,128)S(1)}, f32[2,64,128]{2,1,0:T(8,128)S(1)}, u32[]{:S(2)}, u32[]{:S(2)}) %collective-permute-start.4) | collective-permute-done | bytes 65568 | tf_op jit(solution)/shard_map/ppermute | solution.py:241
  95.5 0.1 collective-permute-start.5
  95.6 6.0 %collective-permute-done.5 = f32[2,64,128]{2,1,0:T(8,128)S(1)} collective-permute-done((f32[2,64,128]{2,1,0:T(8,128)S(1)}, f32[2,64,128]{2,1,0:T(8,128)S(1)}, u32[]{:S(2)}, u32[]{:S(2)}) %collective-permute-start.5) | collective-permute-done | bytes 65568 | tf_op jit(solution)/shard_map/ppermute | solution.py:241
  101.5 0.3 collective-permute-start.6
  101.9 2.2 %add_convert_fusion = bf16[32,64,128]{2,1,0:T(8,128)(2,1)} fusion(bf16[32,64,128]{2,1,0:T(8,128)(2,1)S(1)} %collective-permute-done.3, bf16[32,64,128]{2,1,0:T(8,128)(2,1)S(1)} %collective-permute-done.2, bf16[32,64,128]{2,1,0:T(8,128)(2,1)} %collective-permute-done, bf16[32,64,128]{2,1,0:T(8,128)(2,1)S(1)} %get-tuple-element.11), kind=kLoop, calls=%fused_computation | loop fusion | flops 2097152 | bytes 2621440 | tf_op jit(solution)/shard_map/convert_element_type | solution.py:224
  104.0 1.8 %collective-permute-done.6 = f32[2,64,128]{2,1,0:T(8,128)S(1)} collective-permute-done((f32[2,64,128]{2,1,0:T(8,128)S(1)}, f32[2,64,128]{2,1,0:T(8,128)S(1)}, u32[]{:S(2)}, u32[]{:S(2)}) %collective-permute-start.6) | collective-permute-done | bytes 65568 | tf_op jit(solution)/shard_map/ppermute | solution.py:241
  105.9 0.6 copy_bitcast_fusion
  (19 shorter events, 0.1 us)
Async XLA Ops:
  0.6 1.5 %copy-start = (bf16[64,256]{1,0:T(8,128)(2,1)S(1)}, bf16[64,256]{1,0:T(8,128)(2,1)}, u32[]{:S(2)}) copy-start(bf16[64,256]{1,0:T(8,128)(2,1)} %param.10) | copy-start | bytes 98308
  30.2 17.1 %all-to-all-start.1 = ((bf16[4,8,64,128]{3,2,1,0:T(8,128)(2,1)}), bf16[4,8,64,128]{3,2,1,0:T(8,128)(2,1)S(1)}, u32[]{:S(2)}, u32[]{:S(2)}) async-start(bf16[4,8,64,128]{3,2,1,0:T(8,128)(2,1)} %shard_map.87), calls=%async_computation.1 | async-start | bytes 1048576 | tf_op jit(solution)/shard_map/all_to_all | solution.py:195
  47.3 5.8 %copy-start.1 = (bf16[32,16,128,128]{3,2,1,0:T(8,128)(2,1)S(1)}, bf16[32,16,128,128]{3,2,1,0:T(8,128)(2,1)}, u32[]{:S(2)}) copy-start(bf16[32,16,128,128]{3,2,1,0:T(8,128)(2,1)} %param.11) | copy-start | bytes 50331652
  53.1 0.7 copy-start.3
  53.8 6.7 %copy-start.4 = (s32[1544]{0:T(1024)S(1)}, s32[1544]{0:T(1024)}, u32[]{:S(2)}) copy-start(s32[1544]{0:T(1024)} %shard_map.86.lists) | copy-start | bytes 18532
  56.3 19.4 %collective-permute-start.1 = (bf16[32,64,128]{2,1,0:T(8,128)(2,1)S(1)}, bf16[32,64,128]{2,1,0:T(8,128)(2,1)}, u32[]{:S(2)}, u32[]{:S(2)}) collective-permute-start(bf16[32,64,128]{2,1,0:T(8,128)(2,1)S(1)} %shard_map.90), channel_id=1, source_target_pairs={{0,4},{4,0},{8,12},{12,8},{16,20},{20,16},{24,28},{28,24},{1,5},{5... | collective-permute-start | bytes 1572872 | tf_op jit(solution)/shard_map/ppermute | solution.py:227
  56.4 23.2 %all-to-all-start.2 = ((bf16[4,8,64,128]{3,2,1,0:T(8,128)(2,1)}), bf16[4,8,64,128]{3,2,1,0:T(8,128)(2,1)S(1)}, u32[]{:S(2)}, u32[]{:S(2)}) async-start(bf16[4,8,64,128]{3,2,1,0:T(8,128)(2,1)} %bitcast.6), calls=%async_computation.2 | async-start | bytes 1048576 | tf_op jit(solution)/shard_map/all_to_all | solution.py:195
  60.5 5.8 %copy-start.2 = (bf16[32,16,128,128]{3,2,1,0:T(8,128)(2,1)S(1)}, bf16[32,16,128,128]{3,2,1,0:T(8,128)(2,1)}, u32[]{:S(2)}) copy-start(bf16[32,16,128,128]{3,2,1,0:T(8,128)(2,1)} %param.11) | copy-start | bytes 50331652
  70.9 31.0 %collective-permute-start = (bf16[32,64,128]{2,1,0:T(8,128)(2,1)S(1)}, bf16[32,64,128]{2,1,0:T(8,128)(2,1)}, u32[]{:S(2)}, u32[]{:S(2)}) collective-permute-start(bf16[32,64,128]{2,1,0:T(8,128)(2,1)S(1)} %get-tuple-element.12), channel_id=1, source_target_pairs={{0,4},{4,0},{8,12},{12,8},{16,20},{20,16},{24,28},{28,24},{1,5},{5... | collective-permute-start | bytes 1572872 | tf_op jit(solution)/shard_map/ppermute | solution.py:233
  75.6 26.2 %collective-permute-start.3 = (bf16[32,64,128]{2,1,0:T(8,128)(2,1)S(1)}, bf16[32,64,128]{2,1,0:T(8,128)(2,1)S(1)}, u32[]{:S(2)}, u32[]{:S(2)}) collective-permute-start(bf16[32,64,128]{2,1,0:T(8,128)(2,1)S(1)} %get-tuple-element.14), channel_id=1, source_target_pairs={{0,24},{4,12},{8,0},{12,20},{16,8},{20,28},{24,16},{28,4},{1,25},{... | collective-permute-start | bytes 1572872 | tf_op jit(solution)/shard_map/ppermute | solution.py:230
  77.7 24.1 %collective-permute-start.2 = (bf16[32,64,128]{2,1,0:T(8,128)(2,1)}, bf16[32,64,128]{2,1,0:T(8,128)(2,1)S(1)}, u32[]{:S(2)}, u32[]{:S(2)}) collective-permute-start(bf16[32,64,128]{2,1,0:T(8,128)(2,1)} %add_convert_fusion.1), channel_id=1, source_target_pairs={{0,28},{4,8},{8,4},{12,16},{16,12},{20,24},{24,20},{28,0},{1,29},{... | collective-permute-start | bytes 1572872 | tf_op jit(solution)/shard_map/ppermute | solution.py:231
  79.6 0.8 copy-start.5
  94.2 1.3 %collective-permute-start.4 = (f32[2,64,128]{2,1,0:T(8,128)S(1)}, f32[2,64,128]{2,1,0:T(8,128)S(1)}, u32[]{:S(2)}, u32[]{:S(2)}) collective-permute-start(f32[2,64,128]{2,1,0:T(8,128)S(1)} %convert_reduce_fusion), channel_id=1, source_target_pairs={{0,4},{4,0},{8,12},{12,8},{16,20},{20,16},{24,28},{28,24},{1,5},{5... | collective-permute-start | bytes 196616 | tf_op jit(solution)/shard_map/ppermute | solution.py:241
  95.5 6.0 %collective-permute-start.5 = (f32[2,64,128]{2,1,0:T(8,128)S(1)}, f32[2,64,128]{2,1,0:T(8,128)S(1)}, u32[]{:S(2)}, u32[]{:S(2)}) collective-permute-start(f32[2,64,128]{2,1,0:T(8,128)S(1)} %add.25), channel_id=1, source_target_pairs={{0,8},{4,12},{8,0},{12,4},{16,24},{20,28},{24,16},{28,20},{1,9},{5... | collective-permute-start | bytes 196616 | tf_op jit(solution)/shard_map/ppermute | solution.py:241
  101.5 4.3 %collective-permute-start.6 = (f32[2,64,128]{2,1,0:T(8,128)S(1)}, f32[2,64,128]{2,1,0:T(8,128)S(1)}, u32[]{:S(2)}, u32[]{:S(2)}) collective-permute-start(f32[2,64,128]{2,1,0:T(8,128)S(1)} %add.26), channel_id=1, source_target_pairs={{0,16},{4,20},{8,24},{12,28},{16,0},{20,4},{24,8},{28,12},{1,17},{... | collective-permute-start | bytes 196616 | tf_op jit(solution)/shard_map/ppermute | solution.py:241

commit v6 on v5

v6 whole, which is shorter than its diff:
```python
import functools
import math

import jax
import jax.numpy as jnp
from jax import lax
from jax.experimental import pallas as pl
from jax.experimental.pallas import tpu as pltpu
from jax.sharding import PartitionSpec as P

REACH = 2
STEP = 16
RING = 4
BF16 = jnp.bfloat16
F32 = jnp.float32


def vmem():
    return pl.BlockSpec(memory_space=pltpu.VMEM)


def smem():
    return pl.BlockSpec(memory_space=pltpu.SMEM)


def hbm():
    return pl.BlockSpec(memory_space=pl.ANY)


NEAR, LEAVE, STAY, DEAD = 0, 1, 2, 3


def tile_codes(col_block, live_count, own, slabs):
    blocks, slots = col_block.shape
    sign = 2 * (own % 2) - 1
    offset = (col_block // blocks - own + REACH + slabs) % slabs - REACH
    order = offset * sign + REACH
    group = jnp.where(order == 0, NEAR, jnp.where(order <= REACH, STAY, LEAVE))
    half = jnp.where(order == 0, 0, (order - 1) % 2)
    slot = lax.broadcasted_iota(jnp.int32, (blocks, slots), 1)
    tile = lax.broadcasted_iota(jnp.int32, (blocks, slots), 0) * slots + slot
    group = jnp.where(slot < live_count[:, None], group, DEAD)
    return (group << 16) + tile * (2 * blocks) + half * blocks + col_block % blocks


def list_kernel(codes, lists):
    blocks, slots = codes.shape
    count = blocks * slots

    def row_block(b, lengths):
        for s in range(slots):
            code = codes[b, s]
            group = code >> 16
            length = jnp.where(group == 0, lengths[0], jnp.where(group == 1, lengths[1], lengths[2]))
            length = jnp.where(group == DEAD, 0, length)
            lists[group * count + length] = code & 0xFFFF
            lengths = tuple(
                length + jnp.where(group == g, 1, 0) for g, length in enumerate(lengths)
            )
        return lengths

    lengths = lax.fori_loop(0, blocks, row_block, (jnp.int32(0),) * DEAD)
    for g in range(DEAD):
        lists[(DEAD + 1) * count + g] = lengths[g]


def list_tiles(codes):
    return pl.pallas_call(
        list_kernel,
        out_shape=jax.ShapeDtypeStruct(((DEAD + 1) * codes.size + 8,), jnp.int32),
        in_specs=[smem()],
        out_specs=smem(),
    )(codes)


def tiles_kernel(group, slots, reps, where, lists, *rest):
    shares, tiles, rest = rest[:reps], rest[reps], rest[reps + 1 :]
    outs, (z, ring, first, second, sems) = rest[:-5], rest[-5:]
    totals = (first, second)
    count, blocks = tiles.shape[0], z.shape[0]
    window = len(outs) * blocks
    length = lists[(DEAD + 1) * count + group]
    steps = lax.div(length + STEP - 1, STEP)

    def entry(k):
        return lists[group * count + jnp.minimum(k, count - 1)]

    def fetch(i):
        slot = lax.rem(i, RING)
        for u in range(STEP):
            k = i * STEP + u
            tile = jnp.where(k < length, lax.div(entry(k), 2 * blocks), 0)
            pltpu.make_async_copy(tiles.at[tile], ring.at[slot, u], sems.at[slot]).start()

    for i in range(RING - 1):
        pl.when(i < steps)(functools.partial(fetch, jnp.int32(i)))

    share = blocks // reps
    for s in range(reps):
        source = lax.rem(where[1] - s + reps, reps)
        z[pl.ds(source * share, share)] = shares[s][...]

    def clear(i, carry):
        for total in totals:
            total[i] = jnp.zeros(total.shape[1:], F32)
        return carry

    lax.fori_loop(0, window, clear, 0)

    def step(i, carry):
        slot = lax.rem(i, RING)
        pltpu.make_async_copy(tiles.at[pl.ds(0, STEP)], ring.at[slot], sems.at[slot]).wait()
        pl.when(i + RING - 1 < steps)(functools.partial(fetch, i + RING - 1))
        for u in range(STEP):
            k = i * STEP + u
            code = entry(k)
            row = jnp.where(k < length, lax.div(code, 2 * blocks * slots), 0)
            place = jnp.where(k < length, lax.rem(code, 2 * blocks), window)
            total = totals[u % 2]
            total[place] += jnp.dot(z[row], ring[slot, u], preferred_element_type=F32)
        return carry

    lax.fori_loop(0, steps, step, 0)

    for part, out in enumerate(outs):

        def store(i, carry, out=out, base=part * blocks):
            out[i] = (first[base + i] + second[base + i]).astype(BF16)
            return carry

        lax.fori_loop(0, blocks, store, 0)


def tile_sums(group, where, lists, shares, tiles, slots):
    reps = len(shares)
    share, features, nodes = shares[0].shape
    blocks = share * reps
    parts = 1 if group == NEAR else 2
    shape = (blocks, features, nodes)
    total = pltpu.VMEM((parts * blocks + 1, features, nodes), F32)
    return pl.pallas_call(
        functools.partial(tiles_kernel, group, slots, reps),
        out_shape=[jax.ShapeDtypeStruct(shape, BF16)] * parts,
        in_specs=[smem(), smem()] + [vmem()] * reps + [hbm()],
        out_specs=[vmem()] * parts,
        scratch_shapes=[
            pltpu.VMEM(shape, BF16),
            pltpu.VMEM((RING, STEP, nodes, nodes), BF16),
            total,
            total,
            pltpu.SemaphoreType.DMA((RING,)),
        ],
        compiler_params=pltpu.CompilerParams(vmem_limit_bytes=40 << 20),
        cost_estimate=pl.CostEstimate(
            flops=parts * blocks * slots * features * nodes * nodes // 4,
            bytes_accessed=parts * tiles.size // 4,
            transcendentals=0,
        ),
    )(where, lists, *shares, tiles)


def lay_features(where, shares, whole):
    reps, blocks = len(shares), whole.shape[0]
    features = shares[0].shape[1]
    for s in range(reps):
        first = pl.multiple_of(lax.rem(where[1] - s + reps, reps) * features, features)
        whole[:, pl.ds(first, features), :] = shares[s][:blocks]


def mix_kernel(reps, where, *rest):
    shares, outs, (weights, whole) = rest[:reps], rest[reps : 2 * reps], rest[2 * reps :]
    blocks, features, nodes = outs[0].shape
    lay_features(where, shares, whole)
    for s in range(reps):
        for h in range(weights.shape[1] // nodes):
            rows, columns = pl.ds(s * features, features), pl.ds(h * nodes, nodes)
            weights[rows, columns] = shares[(reps - s) % reps][blocks + h]
    for b in range(blocks):
        mixed = jnp.dot(weights[...], whole[b], preferred_element_type=F32)
        for s in range(reps):
            outs[s][b] = mixed[s * features : (s + 1) * features].astype(BF16)


def mix(where, shares, blocks):
    reps = len(shares)
    _, features, nodes = shares[0].shape
    width = reps * features
    return pl.pallas_call(
        functools.partial(mix_kernel, reps),
        out_shape=[jax.ShapeDtypeStruct((blocks, features, nodes), BF16)] * reps,
        in_specs=[smem()] + [vmem()] * reps,
        out_specs=[vmem()] * reps,
        scratch_shapes=[pltpu.VMEM((width, width), BF16), pltpu.VMEM((blocks, width, nodes), BF16)],
        cost_estimate=pl.CostEstimate(
            flops=2 * blocks * nodes * width * width,
            bytes_accessed=4 * blocks * nodes * width,
            transcendentals=0,
        ),
    )(where, *shares)


def weight_kernel(reps, where, *rest):
    shares, aggs, outs = rest[:reps], rest[reps : 2 * reps], rest[2 * reps : 3 * reps]
    whole, whole_a = rest[3 * reps :]
    lay_features(where, shares, whole)
    blocks, features, nodes = aggs[0].shape
    for s in range(reps):
        whole_a[:, pl.ds(s * features, features), :] = aggs[s][...]
    total = jnp.zeros((whole_a.shape[1], whole.shape[1]), F32)
    for b in range(blocks):
        total += lax.dot_general(
            whole_a[b], whole[b], (((1,), (1,)), ((), ())), preferred_element_type=F32
        )
    for s in range(reps):
        for h in range(outs[s].shape[0]):
            part = total[s * features : (s + 1) * features, h * nodes : (h + 1) * nodes]
            outs[s][h] = part.astype(BF16)


def weight_partial(where, shares, aggs):
    reps = len(aggs)
    blocks, features, nodes = aggs[0].shape
    width = reps * features
    return pl.pallas_call(
        functools.partial(weight_kernel, reps),
        out_shape=[jax.ShapeDtypeStruct((width // nodes, features, nodes), BF16)] * reps,
        in_specs=[smem()] + [vmem()] * (2 * reps),
        out_specs=[vmem()] * reps,
        scratch_shapes=[pltpu.VMEM((blocks, width, nodes), BF16)] * 2,
        cost_estimate=pl.CostEstimate(
            flops=2 * blocks * nodes * width * width,
            bytes_accessed=4 * blocks * nodes * width + 2 * width * width,
            transcendentals=0,
        ),
    )(where, *shares, *aggs)


def add_kernel(*refs):
    terms, out = refs[:-1], refs[-1]

    def one(i, carry):
        total = terms[0][i].astype(F32)
        for term in terms[1:]:
            total += term[i].astype(F32)
        out[i] = total.astype(BF16)
        return carry

    lax.fori_loop(0, out.shape[0], one, 0)


def add(*terms):
    return pl.pallas_call(
        add_kernel,
        out_shape=jax.ShapeDtypeStruct(terms[0].shape, BF16),
        in_specs=[vmem()] * len(terms),
        out_specs=vmem(),
        cost_estimate=pl.CostEstimate(
            flops=len(terms) * terms[0].size,
            bytes_accessed=2 * (len(terms) + 1) * terms[0].size,
            transcendentals=0,
        ),
    )(*terms)


def shift(value, steps):
    reps = lax.axis_size("rep")
    if steps % reps == 0:
        return value
    return lax.ppermute(value, "rep", [(i, (i + steps) % reps) for i in range(reps)])


def node_share(value, steps):
    reps = lax.axis_size("rep")
    blocks = value.shape[0] // reps
    first = lax.rem(lax.axis_index("rep") + steps, reps) * blocks
    return lax.dynamic_slice_in_dim(value, first, blocks, 0)


def on_device(cotangent, relu_mask, aggregated, weight, tiles, col_block, live_count):
    blocks, features, nodes = cotangent.shape
    slots = tiles.shape[1]
    slabs, reps = lax.axis_size("blk"), lax.axis_size("rep")
    width = weight.shape[1]
    share = blocks // reps
    where = jnp.stack([lax.axis_index("blk"), lax.axis_index("rep")]).astype(jnp.int32)

    grad_z = cotangent * relu_mask.astype(BF16)
    weight_pieces = weight.reshape(features, width // nodes, nodes).transpose(1, 0, 2)
    shares = [
        shift(jnp.concatenate([node_share(grad_z, s), weight_pieces], axis=0), s)
        for s in range(reps)
    ]
    lists = list_tiles(tile_codes(col_block, live_count, lax.axis_index("blk"), slabs))
    grad_h = [shift(part, s) for s, part in enumerate(mix(where, shares, share))]

    pair = [(i, i ^ 1) for i in range(slabs)]
    to_one = [(i, (i + (1 if i % 2 else -1)) % slabs) for i in range(slabs)]
    to_two = [(i, (i + (2 if i % 2 else -2)) % slabs) for i in range(slabs)]

    held = tiles.reshape(blocks * slots, nodes, nodes)
    (near,) = tile_sums(NEAR, where, lists, grad_h, held, slots)
    near_in = lax.ppermute(near, "blk", pair)
    one, two = tile_sums(LEAVE, where, lists, grad_h, held, slots)
    two_in = lax.ppermute(two, "blk", to_two)
    one = add(one, near_in)
    one_in = lax.ppermute(one, "blk", to_one)
    stay_lists, _ = lax.optimization_barrier((lists, one))
    beside, own = tile_sums(STAY, where, stay_lists, grad_h, held, slots)
    beside_in = lax.ppermute(beside, "blk", pair)
    input_grad = add(own, beside_in, one_in, two_in)

    aggregated, _ = lax.optimization_barrier((aggregated, near))
    aggs = [shift(node_share(aggregated, s), s) for s in range(reps)]
    aggs, _ = lax.optimization_barrier((aggs, beside))
    grad_w = weight_partial(where, shares, aggs)
    grad_w = sum(shift(part, -s).astype(F32) for s, part in enumerate(grad_w))
    step = 1
    while step < slabs:
        grad_w = grad_w + lax.ppermute(grad_w, "blk", [(i, i ^ step) for i in range(slabs)])
        step *= 2
    grad_w = grad_w.transpose(1, 0, 2).reshape(features, width)
    return input_grad, grad_w * (1.0 / math.sqrt(slabs * blocks * nodes))


def solution(mesh):
    placed = (
        P("blk", "rep", None),
        P("blk", "rep", None),
        P("blk", "rep", None),
        P("rep", None),
        P("blk", None, None, None),
        P("blk", None),
        P("blk"),
    )
    return jax.shard_map(
        on_device,
        mesh=mesh,
        in_specs=placed,
        out_specs=(P("blk", "rep", None), P("rep", None)),
        check_vma=False,
    )
```

time: 107 us -> 107 us (level)
  blocking collectives: 34.9 us -> 0 us
  waiting for transfers between devices: 9.99 us -> 41.2 us
  starting transfers between devices: 10.1 us -> 18.5 us
  local copies, waits for them, and re-layouts: 14.6 us -> 9.42 us
  Pallas kernels: 29 us -> 30.6 us
  other arithmetic: 7.09 us -> 5.57 us
    all_to_all x2 -> x0, blocking collectives: 34.9 us -> none  [exchange(): return lax.all_to_all(value, 'rep', 0, 0, tiled=True)]
    ppermute x0 -> x12, waiting for transfers between devices: none -> 18.8 us  [shift(): lax.ppermute(value, 'rep', [(i, (i + steps) % reps) for i in range(reps)])]
    ppermute x0 -> x12, starting transfers between devices: none -> 18.1 us  [shift(): lax.ppermute(value, 'rep', [(i, (i + steps) % reps) for i in range(reps)])]
    ppermute x3, waiting for transfers between devices: 9.03 us -> 22.4 us  [on_device(): lax.ppermute(grad_w, 'blk', [(i, i ^ step) for i in range(slabs)])]
    all_to_all x2 -> x0, starting transfers between devices: 7.59 us -> none  [exchange(): return lax.all_to_all(value, 'rep', 0, 0, tiled=True)]
    unnamed x13 -> x43, local copies, waits for them, and re-layouts: 13.8 us -> 8.66 us
    convert_element_type x2 -> x0, other arithmetic: 4.21 us -> none  [add(): return sum((term.astype(F32) for term in terms)).astype(BF16)]
    add x0 -> x2, other arithmetic: none -> 2.12 us  [the longest x1 1.34 us: tile_codes(): (group << 16) + tile * (2 * blocks) + half * blocks + col_block % blocks]
  transfers between devices with their start and end apart: 9 -> 19, of which waited for: 4 -> 10; matrix products, arithmetic and copies ran while one was open for 4% -> 5% of each run, Pallas kernels for 23% -> 18%
where the time goes in v6:
time: 107 us; the launch traced here: 106 us
  waiting for transfers between devices  41.2 us (39%)
  Pallas kernels  30.6 us (29%)
  starting transfers between devices  18.5 us (17%)
  local copies, waits for them, and re-layouts  9.42 us (9%)
  other arithmetic  5.57 us (5%)
    ppermute x3, waiting for transfers between devices, on_device(): lax.ppermute(grad_w, 'blk', [(i, i ^ step) for i in range(slabs)])  22.4 us
    ppermute x12, waiting for transfers between devices, shift(): lax.ppermute(value, 'rep', [(i, (i + steps) % reps) for i in range(reps)])  18.8 us
    ppermute x12, starting transfers between devices, shift(): lax.ppermute(value, 'rep', [(i, (i + steps) % reps) for i in range(reps)])  18.1 us
    pallas_call x3, Pallas kernels, tile_sums(): pl.pallas_call(functools.partial(tiles_kernel, group, slots, reps), out_s...  15.6 us
    unnamed x43, local copies, waits for them, and re-layouts  8.66 us
    pallas_call x1, Pallas kernels, list_tiles(): pl.pallas_call(list_kernel, out_shape=jax.ShapeDtypeStruct(((DEAD + 1) *...  5.18 us
    pallas_call x2, Pallas kernels, add(): pl.pallas_call(add_kernel, out_shape=jax.ShapeDtypeStruct(terms[0].shape,...  5.03 us
    pallas_call x1, Pallas kernels, weight_partial(): pl.pallas_call(functools.partial(weight_kernel, reps), out_shape=[jax.Sha...  2.48 us
  transfers between devices with their start and end apart: 19, of which 10 were waited for; matrix products, arithmetic and copies ran while one was open for 5% of the time, Pallas kernels for 18%

profile of v6, /device:TPU:0, one launch (start us, length us, event | category | flops | bytes accessed | tf_op | source)
XLA Modules:
  0.0 106.2 jit_solution(14347727912473197126)
XLA Ops:
  1.4 1.5 %convert_multiply_fusion = bf16[32,64,128]{2,1,0:T(8,128)(2,1)S(1)} fusion(bf16[32,64,128]{2,1,0:T(8,128)(2,1)} %param.7, s32[32,64,128]{2,1,0:T(8,128)} %param.8), kind=kLoop, calls=%fused_computation | loop fusion | flops 524288 | bytes 2097152 | tf_op jit(solution)/shard_map/mul | solution.py:287
  3.6 5.0 %collective-permute-start.2 = (bf16[10,64,128]{2,1,0:T(8,128)(2,1)S(1)}, bf16[10,64,128]{2,1,0:T(8,128)(2,1)S(1)}, u32[]{:S(2)}, u32[]{:S(2)}) collective-permute-start(bf16[10,64,128]{2,1,0:T(8,128)(2,1)S(1)} %get-tuple-element.46), channel_id=1, source_target_pairs={{0,3},{1,0},{2,1},{3,2},{4,7},{5,4},{6,5},{7,6},{8,11},{9,8},{10,9... | collective-permute-start | bytes 491528 | tf_op jit(solution)/shard_map/ppermute | solution.py:269
  8.7 1.0 collective-permute-start.1
  9.7 0.8 copy.13
  11.1 2.2 %collective-permute-done.2.rest_3_ = bf16[10,64,128]{2,1,0:T(8,128)(2,1)S(1)} collective-permute-done((bf16[10,64,128]{2,1,0:T(8,128)(2,1)S(1)}, bf16[10,64,128]{2,1,0:T(8,128)(2,1)S(1)}, u32[]{:S(2)}, u32[]{:S(2)}) %collective-permute-start.2) | collective-permute-done | bytes 163872 | tf_op jit(solution)/shard_map/ppermute | solution.py:269
  13.3 4.4 %collective-permute-done.rest_1_ = bf16[10,64,128]{2,1,0:T(8,128)(2,1)S(1)} collective-permute-done((bf16[10,64,128]{2,1,0:T(8,128)(2,1)S(1)}, bf16[10,64,128]{2,1,0:T(8,128)(2,1)S(1)}, u32[]{:S(2)}, u32[]{:S(2)}) %collective-permute-start) | collective-permute-done | bytes 163872 | tf_op jit(solution)/shard_map/ppermute | solution.py:269
  17.7 4.9 %collective-permute-done.1.rest_2_ = bf16[10,64,128]{2,1,0:T(8,128)(2,1)S(1)} collective-permute-done((bf16[10,64,128]{2,1,0:T(8,128)(2,1)S(1)}, bf16[10,64,128]{2,1,0:T(8,128)(2,1)S(1)}, u32[]{:S(2)}, u32[]{:S(2)}) %collective-permute-start.1) | collective-permute-done | bytes 163872 | tf_op jit(solution)/shard_map/ppermute | solution.py:269
  23.3 2.4 %shard_map.87 = (bf16[8,64,128]{2,1,0:T(8,128)(2,1)}, bf16[8,64,128]{2,1,0:T(8,128)(2,1)}, bf16[8,64,128]{2,1,0:T(8,128)(2,1)}, bf16[8,64,128]{2,1,0:T(8,128)(2,1)}) custom-call(s32[2]{0:T(128)} %pad_add_fusion.where, bf16[10,64,128]{2,1,0:T(8,128)(2,1)} %get-tuple-element.49.rest_0_, bf16[10,64,128]{2,1,0:T(8,128)(2,1)} %copy-done.10, ...), custom_call_target="tpu_custom_call" | custom-call | flops 134217728 | bytes 1048576 | tf_op jit(solution)/shard_map/pallas_call | solution.py:188
  25.6 3.2 %collective-permute-start.4 = (bf16[8,64,128]{2,1,0:T(8,128)(2,1)}, bf16[8,64,128]{2,1,0:T(8,128)(2,1)S(1)}, u32[]{:S(2)}, u32[]{:S(2)}) collective-permute-start(bf16[8,64,128]{2,1,0:T(8,128)(2,1)} %get-tuple-element.22), channel_id=1, source_target_pairs={{0,2},{1,3},{2,0},{3,1},{4,6},{5,7},{6,4},{7,5},{8,10},{9,11},{10,... | collective-permute-start | bytes 393224 | tf_op jit(solution)/shard_map/ppermute | solution.py:269
  29.5 1.3 %fusion.9.codes = s32[32,16]{1,0:T(8,128)} fusion(s32[32,16]{1,0:T(8,128)S(1)} %copy.13, s32[32]{0:T(128)S(1)} %iota_multiply_fusion, s32[]{:T(128)S(6)} %sub.26, s32[]{:T(128)} %axis_index.15, s32[32]{0:T(128)} %param.13), kind=kLoop, calls=%fused_computation.29 | loop fusion | flops 31232 | bytes 4360 | tf_op jit(solution)/shard_map/add | solution.py:43
  30.8 5.2 %shard_map.86.lists = s32[2056]{0:T(1024)} custom-call(s32[32,16]{1,0:T(8,128)} %fusion.9.codes), custom_call_target="tpu_custom_call" | custom-call | tf_op jit(solution)/shard_map/pallas_call | solution.py:68
  36.0 2.0 %collective-permute-done.4.rest_2_ = bf16[8,64,128]{2,1,0:T(8,128)(2,1)S(1)} collective-permute-done((bf16[8,64,128]{2,1,0:T(8,128)(2,1)}, bf16[8,64,128]{2,1,0:T(8,128)(2,1)S(1)}, u32[]{:S(2)}, u32[]{:S(2)}) %collective-permute-start.4) | collective-permute-done | bytes 131104 | tf_op jit(solution)/shard_map/ppermute | solution.py:269
  38.0 0.9 copy-done.1
  40.2 3.6 %shard_map.89 = bf16[32,64,128]{2,1,0:T(8,128)(2,1)S(1)} custom-call(s32[2]{0:T(128)S(1)} %copy-done.7, s32[2056]{0:T(1024)S(1)} %copy-done.5, bf16[8,64,128]{2,1,0:T(8,128)(2,1)S(1)} %copy-done.1, bf16[8,64,128]{2,1,0:T(8,128)(2,1)S(1)} %collective-permute-done.3.rest_1_, bf16[8,64,128]{2,1,0:T(8,128)(2,1)S(1)} %collective-permute-done.4.rest_2_, ...), custom_call_target="tpu_custom_call" | custom-call | flops 134217728 | bytes 2097152 | tf_op jit(solution)/shard_map/pallas_call | solution.py:141
  44.6 2.3 %collective-permute-start.12 = (bf16[8,64,128]{2,1,0:T(8,128)(2,1)S(1)}, bf16[8,64,128]{2,1,0:T(8,128)(2,1)S(1)}, u32[]{:S(2)}, u32[]{:S(2)}) collective-permute-start(bf16[8,64,128]{2,1,0:T(8,128)(2,1)S(1)} %get-tuple-element.38), channel_id=1, source_target_pairs={{0,3},{1,0},{2,1},{3,2},{4,7},{5,4},{6,5},{7,6},{8,11},{9,8},{10,9... | collective-permute-start | bytes 393224 | tf_op jit(solution)/shard_map/ppermute | solution.py:269
  47.0 1.4 %collective-permute-start.11 = (bf16[8,64,128]{2,1,0:T(8,128)(2,1)S(1)}, bf16[8,64,128]{2,1,0:T(8,128)(2,1)S(1)}, u32[]{:S(2)}, u32[]{:S(2)}) collective-permute-start(bf16[8,64,128]{2,1,0:T(8,128)(2,1)S(1)} %get-tuple-element.39), channel_id=1, source_target_pairs={{0,2},{1,3},{2,0},{3,1},{4,6},{5,7},{6,4},{7,5},{8,10},{9,11},{10,... | collective-permute-start | bytes 393224 | tf_op jit(solution)/shard_map/ppermute | solution.py:269
  48.4 5.9 %shard_map.88 = (bf16[32,64,128]{2,1,0:T(8,128)(2,1)S(1)}, bf16[32,64,128]{2,1,0:T(8,128)(2,1)S(1)}) custom-call(s32[2]{0:T(128)S(1)} %copy-done.7, s32[2056]{0:T(1024)S(1)} %copy-done.5, bf16[8,64,128]{2,1,0:T(8,128)(2,1)S(1)} %copy-done.1, bf16[8,64,128]{2,1,0:T(8,128)(2,1)S(1)} %collective-permute-done.3.rest_1_, ...), custom_call_target="tpu_custom_call" | custom-call | flops 268435456 | bytes 4194304 | tf_op jit(solution)/shard_map/pallas_call | solution.py:141
  54.4 0.8 copy-done.4
  55.2 0.8 copy-done.16
  56.0 2.3 %shard_map.90 = bf16[32,64,128]{2,1,0:T(8,128)(2,1)} custom-call(bf16[32,64,128]{2,1,0:T(8,128)(2,1)} %copy-done.4, bf16[32,64,128]{2,1,0:T(8,128)(2,1)} %copy-done.16), custom_call_target="tpu_custom_call" | custom-call | flops 524288 | bytes 1572864 | tf_op jit(solution)/shard_map/pallas_call | solution.py:252
  58.3 6.0 %shard_map.91 = (bf16[32,64,128]{2,1,0:T(8,128)(2,1)S(1)}, bf16[32,64,128]{2,1,0:T(8,128)(2,1)S(1)}) custom-call(s32[2]{0:T(128)S(1)} %copy-done.8, s32[2056]{0:T(1024)S(1)} %copy-done.6, bf16[8,64,128]{2,1,0:T(8,128)(2,1)S(1)} %copy-done.2, bf16[8,64,128]{2,1,0:T(8,128)(2,1)S(1)} %collective-permute-done.3.rest_1_, ...), custom_call_target="tpu_custom_call" | custom-call | flops 268435456 | bytes 4194304 | tf_op jit(solution)/shard_map/pallas_call | solution.py:141
  64.4 0.8 copy-done.3
  65.9 2.5 %shard_map.93 = (bf16[2,64,128]{2,1,0:T(8,128)(2,1)}, bf16[2,64,128]{2,1,0:T(8,128)(2,1)}, bf16[2,64,128]{2,1,0:T(8,128)(2,1)}, bf16[2,64,128]{2,1,0:T(8,128)(2,1)}) custom-call(s32[2]{0:T(128)} %pad_add_fusion.where, bf16[10,64,128]{2,1,0:T(8,128)(2,1)} %get-tuple-element.49.rest_0_, bf16[10,64,128]{2,1,0:T(8,128)(2,1)} %copy-done.10, ...), custom_call_target="tpu_custom_call" | custom-call | flops 134217728 | bytes 1179648 | tf_op jit(solution)/shard_map/pallas_call | solution.py:224
  68.4 3.8 %collective-permute-start.13 = (bf16[2,64,128]{2,1,0:T(8,128)(2,1)}, bf16[2,64,128]{2,1,0:T(8,128)(2,1)S(1)}, u32[]{:S(2)}, u32[]{:S(2)}) collective-permute-start(bf16[2,64,128]{2,1,0:T(8,128)(2,1)} %get-tuple-element.35), channel_id=1, source_target_pairs={{0,3},{1,0},{2,1},{3,2},{4,7},{5,4},{6,5},{7,6},{8,11},{9,8},{10,9... | collective-permute-start | bytes 98312 | tf_op jit(solution)/shard_map/ppermute | solution.py:269
  72.8 1.3 %collective-permute-done.13 = bf16[2,64,128]{2,1,0:T(8,128)(2,1)S(1)} collective-permute-done((bf16[2,64,128]{2,1,0:T(8,128)(2,1)}, bf16[2,64,128]{2,1,0:T(8,128)(2,1)S(1)}, u32[]{:S(2)}, u32[]{:S(2)}) %collective-permute-start.13) | collective-permute-done | bytes 32800 | tf_op jit(solution)/shard_map/ppermute | solution.py:269
  74.1 3.1 %collective-permute-done.14 = bf16[2,64,128]{2,1,0:T(8,128)(2,1)S(1)} collective-permute-done((bf16[2,64,128]{2,1,0:T(8,128)(2,1)}, bf16[2,64,128]{2,1,0:T(8,128)(2,1)S(1)}, u32[]{:S(2)}, u32[]{:S(2)}) %collective-permute-start.14) | collective-permute-done | bytes 32800 | tf_op jit(solution)/shard_map/ppermute | solution.py:269
  77.2 0.9 collective-permute-done.15
  78.1 0.8 convert_add_fusion
  79.0 1.2 %collective-permute-done.16 = f32[2,64,128]{2,1,0:T(8,128)S(1)} collective-permute-done((f32[2,64,128]{2,1,0:T(8,128)S(1)}, f32[2,64,128]{2,1,0:T(8,128)S(1)}, u32[]{:S(2)}, u32[]{:S(2)}) %collective-permute-start.16) | collective-permute-done | bytes 65568 | tf_op jit(solution)/shard_map/ppermute | solution.py:319
  80.3 17.0 %collective-permute-done.17 = f32[2,64,128]{2,1,0:T(8,128)S(1)} collective-permute-done((f32[2,64,128]{2,1,0:T(8,128)S(1)}, f32[2,64,128]{2,1,0:T(8,128)S(1)}, u32[]{:S(2)}, u32[]{:S(2)}) %collective-permute-start.17) | collective-permute-done | bytes 65568 | tf_op jit(solution)/shard_map/ppermute | solution.py:319
  97.5 4.2 %collective-permute-done.18 = f32[2,64,128]{2,1,0:T(8,128)S(1)} collective-permute-done((f32[2,64,128]{2,1,0:T(8,128)S(1)}, f32[2,64,128]{2,1,0:T(8,128)S(1)}, u32[]{:S(2)}, u32[]{:S(2)}) %collective-permute-start.18) | collective-permute-done | bytes 65568 | tf_op jit(solution)/shard_map/ppermute | solution.py:319
  103.5 2.7 %shard_map.92 = bf16[32,64,128]{2,1,0:T(8,128)(2,1)} custom-call(bf16[32,64,128]{2,1,0:T(8,128)(2,1)} %copy-done.3, bf16[32,64,128]{2,1,0:T(8,128)(2,1)} %copy-done.14, bf16[32,64,128]{2,1,0:T(8,128)(2,1)} %copy-done.15, bf16[32,64,128]{2,1,0:T(8,128)(2,1)} %copy-done.13), custom_call_target="tpu_custom_call" | custom-call | flops 1048576 | bytes 2621440 | tf_op jit(solution)/shard_map/pallas_call | solution.py:252
  (69 shorter events, 9.0 us)
Async XLA Ops:
  0.6 43.3 %copy-start.17 = (bf16[32,64,128]{2,1,0:T(8,128)(2,1)S(1)}, bf16[32,64,128]{2,1,0:T(8,128)(2,1)}, u32[]{:S(2)}) copy-start(bf16[32,64,128]{2,1,0:T(8,128)(2,1)} %param.9) | copy-start | bytes 1572868
  3.6 9.7 %collective-permute-start.2 = (bf16[10,64,128]{2,1,0:T(8,128)(2,1)S(1)}, bf16[10,64,128]{2,1,0:T(8,128)(2,1)S(1)}, u32[]{:S(2)}, u32[]{:S(2)}) collective-permute-start(bf16[10,64,128]{2,1,0:T(8,128)(2,1)S(1)} %get-tuple-element.46), channel_id=1, source_target_pairs={{0,3},{1,0},{2,1},{3,2},{4,7},{5,4},{6,5},{7,6},{8,11},{9,8},{10,9... | collective-permute-start | bytes 491528 | tf_op jit(solution)/shard_map/ppermute | solution.py:269
  8.7 9.0 %collective-permute-start = (bf16[10,64,128]{2,1,0:T(8,128)(2,1)S(1)}, bf16[10,64,128]{2,1,0:T(8,128)(2,1)S(1)}, u32[]{:S(2)}, u32[]{:S(2)}) collective-permute-start(bf16[10,64,128]{2,1,0:T(8,128)(2,1)S(1)} %get-tuple-element.47), channel_id=1, source_target_pairs={{0,1},{1,2},{2,3},{3,0},{4,5},{5,6},{6,7},{7,4},{8,9},{9,10},{10,1... | collective-permute-start | bytes 491528 | tf_op jit(solution)/shard_map/ppermute | solution.py:269
  8.7 13.9 %collective-permute-start.1 = (bf16[10,64,128]{2,1,0:T(8,128)(2,1)S(1)}, bf16[10,64,128]{2,1,0:T(8,128)(2,1)S(1)}, u32[]{:S(2)}, u32[]{:S(2)}) collective-permute-start(bf16[10,64,128]{2,1,0:T(8,128)(2,1)S(1)} %get-tuple-element.48), channel_id=1, source_target_pairs={{0,2},{1,3},{2,0},{3,1},{4,6},{5,7},{6,4},{7,5},{8,10},{9,11},{10,... | collective-permute-start | bytes 491528 | tf_op jit(solution)/shard_map/ppermute | solution.py:269
  13.3 9.3 %copy-start.9 = (bf16[10,64,128]{2,1,0:T(8,128)(2,1)}, bf16[10,64,128]{2,1,0:T(8,128)(2,1)S(1)}, u32[]{:S(2)}) copy-start(bf16[10,64,128]{2,1,0:T(8,128)(2,1)S(1)} %collective-permute-done.2.rest_3_) | copy-start | bytes 491524
  17.7 4.9 %copy-start.10 = (bf16[10,64,128]{2,1,0:T(8,128)(2,1)}, bf16[10,64,128]{2,1,0:T(8,128)(2,1)S(1)}, u32[]{:S(2)}) copy-start(bf16[10,64,128]{2,1,0:T(8,128)(2,1)S(1)} %collective-permute-done.rest_1_) | copy-start | bytes 491524
  25.6 10.4 %collective-permute-start.3 = (bf16[8,64,128]{2,1,0:T(8,128)(2,1)}, bf16[8,64,128]{2,1,0:T(8,128)(2,1)S(1)}, u32[]{:S(2)}, u32[]{:S(2)}) collective-permute-start(bf16[8,64,128]{2,1,0:T(8,128)(2,1)} %get-tuple-element.21), channel_id=1, source_target_pairs={{0,1},{1,2},{2,3},{3,0},{4,5},{5,6},{6,7},{7,4},{8,9},{9,10},{10,1... | collective-permute-start | bytes 393224 | tf_op jit(solution)/shard_map/ppermute | solution.py:269
  25.6 12.4 %collective-permute-start.4 = (bf16[8,64,128]{2,1,0:T(8,128)(2,1)}, bf16[8,64,128]{2,1,0:T(8,128)(2,1)S(1)}, u32[]{:S(2)}, u32[]{:S(2)}) collective-permute-start(bf16[8,64,128]{2,1,0:T(8,128)(2,1)} %get-tuple-element.22), channel_id=1, source_target_pairs={{0,2},{1,3},{2,0},{3,1},{4,6},{5,7},{6,4},{7,5},{8,10},{9,11},{10,... | collective-permute-start | bytes 393224 | tf_op jit(solution)/shard_map/ppermute | solution.py:269
  28.8 9.1 %collective-permute-start.5 = (bf16[8,64,128]{2,1,0:T(8,128)(2,1)}, bf16[8,64,128]{2,1,0:T(8,128)(2,1)S(1)}, u32[]{:S(2)}, u32[]{:S(2)}) collective-permute-start(bf16[8,64,128]{2,1,0:T(8,128)(2,1)} %get-tuple-element.23), channel_id=1, source_target_pairs={{0,3},{1,0},{2,1},{3,2},{4,7},{5,4},{6,5},{7,6},{8,11},{9,8},{10,9... | collective-permute-start | bytes 393224 | tf_op jit(solution)/shard_map/ppermute | solution.py:269
  38.0 0.9 copy-start.1
  40.2 18.0 %copy-start.2 = (bf16[8,64,128]{2,1,0:T(8,128)(2,1)S(1)}, bf16[8,64,128]{2,1,0:T(8,128)(2,1)}, u32[]{:S(2)}) copy-start(bf16[8,64,128]{2,1,0:T(8,128)(2,1)} %get-tuple-element.20.rest_0_) | copy-start | bytes 393220
  40.2 18.0 %copy-start.6 = (s32[2056]{0:T(1024)S(1)}, s32[2056]{0:T(1024)}, u32[]{:S(2)}) copy-start(s32[2056]{0:T(1024)} %shard_map.86.lists) | copy-start | bytes 24676
  40.2 18.0 %copy-start.8 = (s32[2]{0:T(128)S(1)}, s32[2]{0:T(128)}, u32[]{:S(2)}) copy-start(s32[2]{0:T(128)} %pad_add_fusion.where) | copy-start | bytes 28
  43.9 11.3 %collective-permute-start.6 = (bf16[32,64,128]{2,1,0:T(8,128)(2,1)S(1)}, bf16[32,64,128]{2,1,0:T(8,128)(2,1)S(1)}, u32[]{:S(2)}, u32[]{:S(2)}) collective-permute-start(bf16[32,64,128]{2,1,0:T(8,128)(2,1)S(1)} %shard_map.89), channel_id=1, source_target_pairs={{0,4},{4,0},{8,12},{12,8},{16,20},{20,16},{24,28},{28,24},{1,5},{5... | collective-permute-start | bytes 1572872 | tf_op jit(solution)/shard_map/ppermute | solution.py:302
  44.6 20.5 %collective-permute-start.12 = (bf16[8,64,128]{2,1,0:T(8,128)(2,1)S(1)}, bf16[8,64,128]{2,1,0:T(8,128)(2,1)S(1)}, u32[]{:S(2)}, u32[]{:S(2)}) collective-permute-start(bf16[8,64,128]{2,1,0:T(8,128)(2,1)S(1)} %get-tuple-element.38), channel_id=1, source_target_pairs={{0,3},{1,0},{2,1},{3,2},{4,7},{5,4},{6,5},{7,6},{8,11},{9,8},{10,9... | collective-permute-start | bytes 393224 | tf_op jit(solution)/shard_map/ppermute | solution.py:269
  47.0 18.2 %collective-permute-start.11 = (bf16[8,64,128]{2,1,0:T(8,128)(2,1)S(1)}, bf16[8,64,128]{2,1,0:T(8,128)(2,1)S(1)}, u32[]{:S(2)}, u32[]{:S(2)}) collective-permute-start(bf16[8,64,128]{2,1,0:T(8,128)(2,1)S(1)} %get-tuple-element.39), channel_id=1, source_target_pairs={{0,2},{1,3},{2,0},{3,1},{4,6},{5,7},{6,4},{7,5},{8,10},{9,11},{10,... | collective-permute-start | bytes 393224 | tf_op jit(solution)/shard_map/ppermute | solution.py:269
  48.4 16.7 %collective-permute-start.10 = (bf16[8,64,128]{2,1,0:T(8,128)(2,1)S(1)}, bf16[8,64,128]{2,1,0:T(8,128)(2,1)S(1)}, u32[]{:S(2)}, u32[]{:S(2)}) collective-permute-start(bf16[8,64,128]{2,1,0:T(8,128)(2,1)S(1)} %get-tuple-element.40), channel_id=1, source_target_pairs={{0,1},{1,2},{2,3},{3,0},{4,5},{5,6},{6,7},{7,4},{8,9},{9,10},{10,1... | collective-permute-start | bytes 393224 | tf_op jit(solution)/shard_map/ppermute | solution.py:269
  55.2 0.8 copy-start.16
  58.3 15.8 %copy-start.12 = (bf16[32,64,128]{2,1,0:T(8,128)(2,1)S(1)}, bf16[32,64,128]{2,1,0:T(8,128)(2,1)}, u32[]{:S(2)}) copy-start(bf16[32,64,128]{2,1,0:T(8,128)(2,1)} %shard_map.90) | copy-start | bytes 1572868
  64.3 0.8 copy-start.3
  68.4 5.7 %collective-permute-start.13 = (bf16[2,64,128]{2,1,0:T(8,128)(2,1)}, bf16[2,64,128]{2,1,0:T(8,128)(2,1)S(1)}, u32[]{:S(2)}, u32[]{:S(2)}) collective-permute-start(bf16[2,64,128]{2,1,0:T(8,128)(2,1)} %get-tuple-element.35), channel_id=1, source_target_pairs={{0,3},{1,0},{2,1},{3,2},{4,7},{5,4},{6,5},{7,6},{8,11},{9,8},{10,9... | collective-permute-start | bytes 98312 | tf_op jit(solution)/shard_map/ppermute | solution.py:269
  72.2 5.0 %collective-permute-start.14 = (bf16[2,64,128]{2,1,0:T(8,128)(2,1)}, bf16[2,64,128]{2,1,0:T(8,128)(2,1)S(1)}, u32[]{:S(2)}, u32[]{:S(2)}) collective-permute-start(bf16[2,64,128]{2,1,0:T(8,128)(2,1)} %get-tuple-element.36), channel_id=1, source_target_pairs={{0,2},{1,3},{2,0},{3,1},{4,6},{5,7},{6,4},{7,5},{8,10},{9,11},{10,... | collective-permute-start | bytes 98312 | tf_op jit(solution)/shard_map/ppermute | solution.py:269
  72.2 5.9 %collective-permute-start.15 = (bf16[2,64,128]{2,1,0:T(8,128)(2,1)}, bf16[2,64,128]{2,1,0:T(8,128)(2,1)S(1)}, u32[]{:S(2)}, u32[]{:S(2)}) collective-permute-start(bf16[2,64,128]{2,1,0:T(8,128)(2,1)} %get-tuple-element.37), channel_id=1, source_target_pairs={{0,1},{1,2},{2,3},{3,0},{4,5},{5,6},{6,7},{7,4},{8,9},{9,10},{10,1... | collective-permute-start | bytes 98312 | tf_op jit(solution)/shard_map/ppermute | solution.py:269
  72.8 29.5 %collective-permute-start.9 = (bf16[32,64,128]{2,1,0:T(8,128)(2,1)S(1)}, bf16[32,64,128]{2,1,0:T(8,128)(2,1)S(1)}, u32[]{:S(2)}, u32[]{:S(2)}) collective-permute-start(bf16[32,64,128]{2,1,0:T(8,128)(2,1)S(1)} %get-tuple-element.28), channel_id=1, source_target_pairs={{0,24},{4,12},{8,0},{12,20},{16,8},{20,28},{24,16},{28,4},{1,25},{... | collective-permute-start | bytes 1572872 | tf_op jit(solution)/shard_map/ppermute | solution.py:304
  72.8 29.5 %collective-permute-start.7 = (bf16[32,64,128]{2,1,0:T(8,128)(2,1)S(1)}, bf16[32,64,128]{2,1,0:T(8,128)(2,1)S(1)}, u32[]{:S(2)}, u32[]{:S(2)}) collective-permute-start(bf16[32,64,128]{2,1,0:T(8,128)(2,1)S(1)} %get-tuple-element.27), channel_id=1, source_target_pairs={{0,4},{4,0},{8,12},{12,8},{16,20},{20,16},{24,28},{28,24},{1,5},{5... | collective-permute-start | bytes 1572872 | tf_op jit(solution)/shard_map/ppermute | solution.py:309
  74.1 28.2 %collective-permute-start.8 = (bf16[32,64,128]{2,1,0:T(8,128)(2,1)S(1)}, bf16[32,64,128]{2,1,0:T(8,128)(2,1)S(1)}, u32[]{:S(2)}, u32[]{:S(2)}) collective-permute-start(bf16[32,64,128]{2,1,0:T(8,128)(2,1)S(1)} %copy-done.12), channel_id=1, source_target_pairs={{0,28},{4,8},{8,4},{12,16},{16,12},{20,24},{24,20},{28,0},{1,29},{... | collective-permute-start | bytes 1572872 | tf_op jit(solution)/shard_map/ppermute | solution.py:306
  78.9 1.3 %collective-permute-start.16 = (f32[2,64,128]{2,1,0:T(8,128)S(1)}, f32[2,64,128]{2,1,0:T(8,128)S(1)}, u32[]{:S(2)}, u32[]{:S(2)}) collective-permute-start(f32[2,64,128]{2,1,0:T(8,128)S(1)} %convert_add_fusion), channel_id=1, source_target_pairs={{0,4},{4,0},{8,12},{12,8},{16,20},{20,16},{24,28},{28,24},{1,5},{5... | collective-permute-start | bytes 196616 | tf_op jit(solution)/shard_map/ppermute | solution.py:319
  80.2 17.1 %collective-permute-start.17 = (f32[2,64,128]{2,1,0:T(8,128)S(1)}, f32[2,64,128]{2,1,0:T(8,128)S(1)}, u32[]{:S(2)}, u32[]{:S(2)}) collective-permute-start(f32[2,64,128]{2,1,0:T(8,128)S(1)} %add.115), channel_id=1, source_target_pairs={{0,8},{4,12},{8,0},{12,4},{16,24},{20,28},{24,16},{28,20},{1,9},{5... | collective-permute-start | bytes 196616 | tf_op jit(solution)/shard_map/ppermute | solution.py:319
  97.3 4.3 %collective-permute-start.18 = (f32[2,64,128]{2,1,0:T(8,128)S(1)}, f32[2,64,128]{2,1,0:T(8,128)S(1)}, u32[]{:S(2)}, u32[]{:S(2)}) collective-permute-start(f32[2,64,128]{2,1,0:T(8,128)S(1)} %add.116), channel_id=1, source_target_pairs={{0,16},{4,20},{8,24},{12,28},{16,0},{20,4},{24,8},{28,12},{1,17},{... | collective-permute-start | bytes 196616 | tf_op jit(solution)/shard_map/ppermute | solution.py:319
  102.3 0.8 copy-start.13
  102.3 1.0 copy-start.14
  102.3 1.1 %copy-start.15 = (bf16[32,64,128]{2,1,0:T(8,128)(2,1)}, bf16[32,64,128]{2,1,0:T(8,128)(2,1)S(1)}, u32[]{:S(2)}) copy-start(bf16[32,64,128]{2,1,0:T(8,128)(2,1)S(1)} %collective-permute-done.8.refs_2_) | copy-start | bytes 1572868
  (8 other events, 5.6 us)

commit v7 on v6

v7 whole, which is shorter than its diff:
```python
import functools
import math

import jax
import jax.numpy as jnp
from jax import lax
from jax.experimental import pallas as pl
from jax.experimental.pallas import tpu as pltpu
from jax.sharding import PartitionSpec as P

REACH = 2
GROUP = 4
STEP = 4
RING = 10
BF16 = jnp.bfloat16
F32 = jnp.float32
MIB = 1 << 20


def vmem():
    return pl.BlockSpec(memory_space=pltpu.VMEM)


def smem():
    return pl.BlockSpec(memory_space=pltpu.SMEM)


def hbm():
    return pl.BlockSpec(memory_space=pl.ANY)


def in_hbm(value):
    return pltpu.with_memory_space_constraint(value, pltpu.HBM)


def wrap(value, size):
    if size & (size - 1):
        return lax.rem(value + size, size)
    return value & (size - 1)


def tiles_kernel(slabs, where, cols, live, cot, mask, tiles, *rest):
    outs, (cot_in, mask_in, z, ring, first, second, rows, left, sems, z_sems) = rest[:5], rest[5:]
    totals = (first, second)
    blocks, slots = cols.shape
    per_row = slots // GROUP
    window = (2 * REACH + 1) * blocks
    copies = [
        pltpu.make_async_copy(cot, cot_in, z_sems.at[0]),
        pltpu.make_async_copy(mask, mask_in, z_sems.at[1]),
    ]
    for copy in copies:
        copy.start()

    def list_row(b, count):
        for g in range(per_row):
            rows[count + g] = b * per_row + g
            left[count + g] = live[b] - g * GROUP
        return count + lax.shift_right_logical(live[b] + GROUP - 1, GROUP.bit_length() - 1)

    count = lax.fori_loop(0, blocks, list_row, jnp.int32(0))
    for u in range(STEP):
        rows[count + u] = 0
        left[count + u] = 0
    steps = lax.div(count + STEP - 1, STEP)

    def fetch(i):
        slot = lax.rem(i, RING)
        for u in range(STEP):
            start = rows[i * STEP + u] * GROUP
            pltpu.make_async_copy(
                tiles.at[pl.ds(start, GROUP)], ring.at[slot, pl.ds(u * GROUP, GROUP)], sems.at[slot]
            ).start()

    for i in range(RING - 1):
        pl.when(i < steps)(functools.partial(fetch, jnp.int32(i)))

    def clear(i, carry):
        for total in totals:
            total[i] = jnp.zeros(total.shape[1:], F32)
        return carry

    lax.fori_loop(0, window, clear, 0)
    for copy in copies:
        copy.wait()

    def mask_row(b, carry):
        z[b] = cot_in[b] * mask_in[b].astype(BF16)
        return carry

    lax.fori_loop(0, blocks, mask_row, 0)
    shift = REACH * blocks - where[0] * blocks

    def step(i, carry):
        slot = lax.rem(i, RING)
        pltpu.make_async_copy(
            tiles.at[pl.ds(0, STEP * GROUP)], ring.at[slot], sems.at[slot]
        ).wait()
        pl.when(i + RING - 1 < steps)(functools.partial(fetch, i + RING - 1))
        for u in range(STEP):
            row, remain = rows[i * STEP + u], left[i * STEP + u]
            b, g = lax.div(row, per_row), lax.rem(row, per_row)
            z_row = z[b]
            for j in range(GROUP):
                place = wrap(cols[b, g * GROUP + j] + shift, slabs * blocks)
                place = jnp.where(j < remain, place, window)
                totals[j % 2][place] += jnp.dot(
                    z_row, ring[slot, u * GROUP + j], preferred_element_type=F32
                )
        return carry

    lax.fori_loop(0, steps, step, 0)
    sign = 2 * lax.rem(where[0], 2) - 1
    for order, out in enumerate(outs):
        base = ((order - REACH) * sign + REACH) * blocks

        def store(i, carry, out=out, base=base):
            out[i] = (first[base + i] + second[base + i]).astype(BF16)
            return carry

        lax.fori_loop(0, blocks, store, 0)


def contributions(where, cols, live, cot, mask, tiles, slabs):
    blocks, slots, nodes = tiles.shape[:3]
    features = cot.shape[1]
    window = (2 * REACH + 1) * blocks
    lists = blocks * (slots // GROUP) + slots // GROUP + STEP
    total = pltpu.VMEM((window + 1, features, nodes), F32)
    return pl.pallas_call(
        functools.partial(tiles_kernel, slabs),
        out_shape=[jax.ShapeDtypeStruct(cot.shape, BF16)] * 5,
        in_specs=[smem(), smem(), smem(), hbm(), hbm(), hbm()],
        out_specs=[vmem()] * 5,
        scratch_shapes=[
            pltpu.VMEM(cot.shape, BF16),
            pltpu.VMEM(mask.shape, jnp.int32),
            pltpu.VMEM(cot.shape, BF16),
            pltpu.VMEM((RING, STEP * GROUP, nodes, nodes), BF16),
            total,
            total,
            pltpu.SMEM((lists,), jnp.int32),
            pltpu.SMEM((lists,), jnp.int32),
            pltpu.SemaphoreType.DMA((RING,)),
            pltpu.SemaphoreType.DMA((2,)),
        ],
        compiler_params=pltpu.CompilerParams(vmem_limit_bytes=26 * MIB),
        cost_estimate=pl.CostEstimate(
            flops=2 * blocks * slots * features * nodes * nodes,
            bytes_accessed=tiles.size * 2,
            transcendentals=0,
        ),
    )(
        where,
        cols,
        live,
        in_hbm(cot),
        in_hbm(mask),
        in_hbm(tiles.reshape(blocks * slots, nodes, nodes)),
    )


def lay_features(where, shares, whole):
    reps, blocks = len(shares), whole.shape[0]
    features = shares[0].shape[1]
    for s in range(reps):
        first = pl.multiple_of(wrap(where[1] - s, reps) * features, features)
        whole[:, pl.ds(first, features), :] = shares[s][:blocks]


def mix_kernel(reps, first, where, *rest):
    shares, packed, outs = rest[:reps], rest[reps : 2 * reps], rest[2 * reps : 3 * reps]
    weights, whole = rest[3 * reps :]
    blocks, features, nodes = outs[0].shape
    lay_features(where, shares, whole)
    for s in range(reps):
        for h in range(weights.shape[1] // nodes):
            rows, columns = pl.ds(s * features, features), pl.ds(h * nodes, nodes)
            weights[rows, columns] = packed[(reps - s) % reps][first + h]
    for b in range(blocks):
        mixed = jnp.dot(weights[...], whole[b], preferred_element_type=F32)
        for s in range(reps):
            outs[s][b] = mixed[s * features : (s + 1) * features].astype(BF16)


def mix(where, shares, packed, first):
    reps = len(shares)
    blocks, features, nodes = shares[0].shape
    width = reps * features
    return pl.pallas_call(
        functools.partial(mix_kernel, reps, first),
        out_shape=[jax.ShapeDtypeStruct((blocks, features, nodes), BF16)] * reps,
        in_specs=[smem()] + [vmem()] * (2 * reps),
        out_specs=[vmem()] * reps,
        scratch_shapes=[pltpu.VMEM((width, width), BF16), pltpu.VMEM((blocks, width, nodes), BF16)],
        compiler_params=pltpu.CompilerParams(vmem_limit_bytes=4 * MIB),
        cost_estimate=pl.CostEstimate(
            flops=2 * blocks * nodes * width * width,
            bytes_accessed=4 * blocks * nodes * width,
            transcendentals=0,
        ),
    )(where, *shares, *packed)


def weight_kernel(reps, blocks, where, *rest):
    packed, outs, (whole_z, whole_a) = rest[:reps], rest[reps : 2 * reps], rest[2 * reps :]
    features, nodes = outs[0].shape[1:]
    lay_features(where, packed, whole_z)
    for s in range(reps):
        whole_a[:, pl.ds(s * features, features), :] = packed[s][blocks : 2 * blocks]
    total = jnp.zeros((whole_a.shape[1], whole_z.shape[1]), F32)
    for b in range(blocks):
        total += lax.dot_general(
            whole_a[b], whole_z[b], (((1,), (1,)), ((), ())), preferred_element_type=F32
        )
    for s in range(reps):
        for h in range(outs[s].shape[0]):
            part = total[s * features : (s + 1) * features, h * nodes : (h + 1) * nodes]
            outs[s][h] = part.astype(BF16)


def weight_partial(where, packed, blocks):
    reps = len(packed)
    _, features, nodes = packed[0].shape
    width = reps * features
    return pl.pallas_call(
        functools.partial(weight_kernel, reps, blocks),
        out_shape=[jax.ShapeDtypeStruct((width // nodes, features, nodes), BF16)] * reps,
        in_specs=[smem()] + [vmem()] * reps,
        out_specs=[vmem()] * reps,
        scratch_shapes=[pltpu.VMEM((blocks, width, nodes), BF16)] * 2,
        compiler_params=pltpu.CompilerParams(vmem_limit_bytes=4 * MIB),
        cost_estimate=pl.CostEstimate(
            flops=2 * blocks * nodes * width * width,
            bytes_accessed=4 * blocks * nodes * width + 2 * width * width,
            transcendentals=0,
        ),
    )(where, *packed)


def add_kernel(one, other, out):
    def row(i, carry):
        out[i] = (one[i].astype(F32) + other[i].astype(F32)).astype(BF16)
        return carry

    lax.fori_loop(0, out.shape[0], row, 0)


def add(one, other):
    return pl.pallas_call(
        add_kernel,
        out_shape=jax.ShapeDtypeStruct(one.shape, BF16),
        in_specs=[vmem()] * 2,
        out_specs=vmem(),
        compiler_params=pltpu.CompilerParams(vmem_limit_bytes=2 * MIB),
        cost_estimate=pl.CostEstimate(
            flops=one.size, bytes_accessed=6 * one.size, transcendentals=0
        ),
    )(one, other)


def total_kernel(reps, where, *rest):
    terms, outs = rest[:-reps], rest[-reps:]
    share = outs[0].shape[0]
    for s, out in enumerate(outs):
        first = wrap(where[1] + s, reps) * share
        for i in range(share):
            total = terms[0][first + i].astype(F32)
            for term in terms[1:]:
                total += term[first + i].astype(F32)
            out[i] = total.astype(BF16)


def total_shares(where, terms, reps):
    blocks, features, nodes = terms[0].shape
    return pl.pallas_call(
        functools.partial(total_kernel, reps),
        out_shape=[jax.ShapeDtypeStruct((blocks // reps, features, nodes), BF16)] * reps,
        in_specs=[smem()] + [vmem()] * len(terms),
        out_specs=[vmem()] * reps,
        compiler_params=pltpu.CompilerParams(vmem_limit_bytes=2 * MIB),
        cost_estimate=pl.CostEstimate(
            flops=4 * terms[0].size, bytes_accessed=10 * terms[0].size, transcendentals=0
        ),
    )(where, *terms)


def lay_kernel(reps, where, *rest):
    shares, out, sems = rest[:reps], rest[reps], rest[reps + 1]
    blocks = shares[0].shape[0]
    copies = []
    for s in range(reps):
        first = wrap(where[1] - s, reps) * blocks
        copies.append(pltpu.make_async_copy(shares[s], out.at[pl.ds(first, blocks)], sems.at[s]))
        copies[s].start()
    for copy in copies:
        copy.wait()


def lay_blocks(where, shares, shape):
    reps = len(shares)
    return pl.pallas_call(
        functools.partial(lay_kernel, reps),
        out_shape=jax.ShapeDtypeStruct(shape, BF16),
        in_specs=[smem()] + [vmem()] * reps,
        out_specs=hbm(),
        scratch_shapes=[pltpu.SemaphoreType.DMA((reps,))],
        compiler_params=pltpu.CompilerParams(vmem_limit_bytes=2 * MIB),
        cost_estimate=pl.CostEstimate(flops=0, bytes_accessed=32 * MIB, transcendentals=0),
    )(where, *shares)


def shift(value, steps):
    reps = lax.axis_size("rep")
    if steps % reps == 0:
        return value
    return lax.ppermute(value, "rep", [(i, (i + steps) % reps) for i in range(reps)])


def node_share(value, steps):
    reps = lax.axis_size("rep")
    blocks = value.shape[0] // reps
    first = lax.rem(lax.axis_index("rep") + steps, reps) * blocks
    return lax.dynamic_slice_in_dim(value, first, blocks, 0)


def on_device(cotangent, relu_mask, aggregated, weight, tiles, col_block, live_count):
    blocks, features, nodes = cotangent.shape
    slabs, reps = lax.axis_size("blk"), lax.axis_size("rep")
    width = weight.shape[1]
    share = blocks // reps
    where = jnp.stack([lax.axis_index("blk"), lax.axis_index("rep")]).astype(jnp.int32)

    pair = [(i, i ^ 1) for i in range(slabs)]
    to_one = [(i, (i + (1 if i % 2 else -1)) % slabs) for i in range(slabs)]
    to_two = [(i, (i + (2 if i % 2 else -2)) % slabs) for i in range(slabs)]
    near, beside, own, one, two = contributions(
        where, col_block, live_count, cotangent, relu_mask, tiles, slabs
    )
    near_in = lax.ppermute(near, "blk", pair)
    two_in = lax.ppermute(two, "blk", to_two)
    one = add(one, near_in)
    one_in = lax.ppermute(one, "blk", to_one)
    beside_in = lax.ppermute(beside, "blk", pair)

    cotangent, relu_mask, aggregated, weight, _ = lax.optimization_barrier(
        (cotangent, relu_mask, aggregated, weight, one)
    )
    grad_z = cotangent * relu_mask.astype(BF16)
    weight_pieces = weight.reshape(features, width // nodes, nodes).transpose(1, 0, 2)
    packed = [
        shift(
            jnp.concatenate([node_share(grad_z, s), node_share(aggregated, s), weight_pieces]), s
        )
        for s in range(reps)
    ]

    shares = total_shares(where, [own, beside_in, one_in, two_in], reps)
    shares = [shift(value, s) for s, value in enumerate(shares)]
    held, _ = lax.optimization_barrier((packed, shares))
    outs = [shift(value, s) for s, value in enumerate(mix(where, shares, packed, 2 * share))]
    input_grad = lay_blocks(where, outs, cotangent.shape)

    grad_w = weight_partial(where, held, share)
    grad_w = sum(shift(part, -s).astype(F32) for s, part in enumerate(grad_w))
    grad_w = grad_w + lax.ppermute(grad_w, "blk", pair)
    grad_w = grad_w + sum(
        lax.ppermute(grad_w, "blk", [(i, i ^ step) for i in range(slabs)])
        for step in range(2, slabs, 2)
    )
    grad_w = grad_w.transpose(1, 0, 2).reshape(features, width)
    return input_grad, grad_w * (1.0 / math.sqrt(slabs * blocks * nodes))


def solution(mesh):
    placed = (
        P("blk", "rep", None),
        P("blk", "rep", None),
        P("blk", "rep", None),
        P("rep", None),
        P("blk", None, None, None),
        P("blk", None),
        P("blk"),
    )
    return jax.shard_map(
        on_device,
        mesh=mesh,
        in_specs=placed,
        out_specs=(P("blk", "rep", None), P("rep", None)),
        check_vma=False,
    )
```

time: 107 us -> 84.2 us (0.79)
  Pallas kernels: 30.6 us -> 15.5 us
  starting transfers between devices: 18.5 us -> 31.8 us
  waiting for transfers between devices: 41.2 us -> 30.8 us
  local copies, waits for them, and re-layouts: 9.42 us -> 2.68 us
  other arithmetic: 5.57 us -> 2.36 us
    ppermute x3, waiting for transfers between devices: 22.4 us -> 0.01 us  [on_device(): lax.ppermute(grad_w, 'blk', [(i, i ^ step) for i in range(slabs)])]
    pallas_call x8 -> x6, Pallas kernels: 30.6 us -> 15.5 us  [the longest x1 11.1 us: contributions(): pl.pallas_call(functools.partial(tiles_kernel, slabs), out_shape=[jax.Sha...]
    ppermute x1, waiting for transfers between devices: 0.01 us -> 10.2 us  [on_device(): one_in = lax.ppermute(one, 'blk', to_one)]
    unnamed x43 -> x5, local copies, waits for them, and re-layouts: 8.66 us -> 1.44 us
    ppermute x1, starting transfers between devices: 0.01 us -> 5.07 us  [on_device(): two_in = lax.ppermute(two, 'blk', to_two)]
    ppermute x3, starting transfers between devices: 0.29 us -> 3.85 us  [on_device(): lax.ppermute(grad_w, 'blk', [(i, i ^ step) for i in range(slabs)])]
    ppermute x12, starting transfers between devices: 18.1 us -> 20.8 us  [shift(): lax.ppermute(value, 'rep', [(i, (i + steps) % reps) for i in range(reps)])]
    ppermute x1, waiting for transfers between devices: 0.01 us -> 2.22 us  [on_device(): two_in = lax.ppermute(two, 'blk', to_two)]
  transfers between devices with their start and end apart: 19 -> 20, of which waited for: 10 -> 7; matrix products, arithmetic and copies ran while one was open for 5% -> 3% of each run, Pallas kernels for 18% -> 4%
where the time goes in v7:
time: 84.2 us; the launch traced here: 83.9 us
  starting transfers between devices  31.8 us (38%)
  waiting for transfers between devices  30.8 us (37%)
  Pallas kernels  15.5 us (18%)
  local copies, waits for them, and re-layouts  2.68 us (3%)
  other arithmetic  2.36 us (3%)
    ppermute x12, starting transfers between devices, shift(): lax.ppermute(value, 'rep', [(i, (i + steps) % reps) for i in range(reps)])  20.8 us
    ppermute x12, waiting for transfers between devices, shift(): lax.ppermute(value, 'rep', [(i, (i + steps) % reps) for i in range(reps)])  17.1 us
    pallas_call x1, Pallas kernels, contributions(): pl.pallas_call(functools.partial(tiles_kernel, slabs), out_shape=[jax.Sha...  11.1 us
    ppermute x1, waiting for transfers between devices, on_device(): one_in = lax.ppermute(one, 'blk', to_one)  10.2 us
    ppermute x1, starting transfers between devices, on_device(): two_in = lax.ppermute(two, 'blk', to_two)  5.07 us
    ppermute x3, starting transfers between devices, on_device(): lax.ppermute(grad_w, 'blk', [(i, i ^ step) for i in range(slabs)])  3.85 us
    ppermute x1, waiting for transfers between devices, on_device(): two_in = lax.ppermute(two, 'blk', to_two)  2.22 us
  transfers between devices with their start and end apart: 20, of which 7 were waited for; matrix products, arithmetic and copies ran while one was open for 3% of the time, Pallas kernels for 4%

profile of v7, /device:TPU:0, one launch (start us, length us, event | category | flops | bytes accessed | tf_op | source)
XLA Modules:
  0.0 83.9 jit_solution(7218681012442492952)
XLA Ops:
  0.7 0.8 copy.10.cols
  1.5 0.7 copy-done.1
  2.2 11.1 %shard_map.86 = (bf16[32,64,128]{2,1,0:T(8,128)(2,1)}, bf16[32,64,128]{2,1,0:T(8,128)(2,1)}, bf16[32,64,128]{2,1,0:T(8,128)(2,1)S(1)}, bf16[32,64,128]{2,1,0:T(8,128)(2,1)S(1)}, bf16[32,64,128]{2,1,0:T(8,128)(2,1)S(1)}) custom-call(s32[2]{0:T(128)S(1)} %pad_add_fusion.where, s32[32,16]{1,0:T(8,128)S(1)} %copy.10.cols, s32[32]{0:T(128)S(1)} %copy-done.1, ...), custom_call_target="tpu_custom_call" | custom-call | flops 1073741824 | bytes 16777216 | tf_op jit(solution)/shard_map/pallas_call | solution.py:130
  13.8 5.1 %collective-permute-start.3 = (bf16[32,64,128]{2,1,0:T(8,128)(2,1)S(1)}, bf16[32,64,128]{2,1,0:T(8,128)(2,1)S(1)}, u32[]{:S(2)}, u32[]{:S(2)}) collective-permute-start(bf16[32,64,128]{2,1,0:T(8,128)(2,1)S(1)} %get-tuple-element.31), channel_id=1, source_target_pairs={{0,24},{4,12},{8,0},{12,20},{16,8},{20,28},{24,16},{28,4},{1,25},{... | collective-permute-start | bytes 1572872 | tf_op jit(solution)/shard_map/ppermute | solution.py:341
  19.2 1.4 %collective-permute-start.2 = (bf16[32,64,128]{2,1,0:T(8,128)(2,1)S(1)}, bf16[32,64,128]{2,1,0:T(8,128)(2,1)S(1)}, u32[]{:S(2)}, u32[]{:S(2)}) collective-permute-start(bf16[32,64,128]{2,1,0:T(8,128)(2,1)S(1)} %shard_map.87), channel_id=1, source_target_pairs={{0,28},{4,8},{8,4},{12,16},{16,12},{20,24},{24,20},{28,0},{1,29},{... | collective-permute-start | bytes 1572872 | tf_op jit(solution)/shard_map/ppermute | solution.py:343
  20.6 1.5 %convert_multiply_fusion = bf16[32,64,128]{2,1,0:T(8,128)(2,1)S(1)} fusion(bf16[32,64,128]{2,1,0:T(8,128)(2,1)} %cot.1, s32[32,64,128]{2,1,0:T(8,128)} %mask.1), kind=kLoop, calls=%fused_computation.4 | loop fusion | flops 524288 | bytes 2097152 | tf_op jit(solution)/shard_map/mul | solution.py:349
  22.1 1.2 %constant_dynamic-slice_fusion = (bf16[8,64,128]{2,1,0:T(8,128)(2,1)S(1)}, bf16[8,64,128]{2,1,0:T(8,128)(2,1)S(1)}, bf16[8,64,128]{2,1,0:T(8,128)(2,1)S(1)}, bf1...) fusion(bf16[32,64,128]{2,1,0:T(8,128)(2,1)} %param.9, ...), kind=kLoop, calls=%fused_computation.9 | loop fusion | bytes 2097168 | tf_op jit(solution)/shard_map/dynamic_slice | solution.py:324
  23.5 1.6 %collective-permute-start.7 = (bf16[18,64,128]{2,1,0:T(8,128)(2,1)S(1)}, bf16[18,64,128]{2,1,0:T(8,128)(2,1)S(1)}, u32[]{:S(2)}, u32[]{:S(2)}) collective-permute-start(bf16[18,64,128]{2,1,0:T(8,128)(2,1)S(1)} %get-tuple-element.61), channel_id=1, source_target_pairs={{0,1},{1,2},{2,3},{3,0},{4,5},{5,6},{6,7},{7,4},{8,9},{9,10},{10,1... | collective-permute-start | bytes 884744 | tf_op jit(solution)/shard_map/ppermute | solution.py:317
  25.1 2.6 %collective-permute-start.8 = (bf16[18,64,128]{2,1,0:T(8,128)(2,1)S(1)}, bf16[18,64,128]{2,1,0:T(8,128)(2,1)S(1)}, u32[]{:S(2)}, u32[]{:S(2)}) collective-permute-start(bf16[18,64,128]{2,1,0:T(8,128)(2,1)S(1)} %get-tuple-element.62), channel_id=1, source_target_pairs={{0,2},{1,3},{2,0},{3,1},{4,6},{5,7},{6,4},{7,5},{8,10},{9,11},{10,... | collective-permute-start | bytes 884744 | tf_op jit(solution)/shard_map/ppermute | solution.py:317
  27.7 1.3 %collective-permute-start.9 = (bf16[18,64,128]{2,1,0:T(8,128)(2,1)S(1)}, bf16[18,64,128]{2,1,0:T(8,128)(2,1)S(1)}, u32[]{:S(2)}, u32[]{:S(2)}) collective-permute-start(bf16[18,64,128]{2,1,0:T(8,128)(2,1)S(1)} %get-tuple-element.60), channel_id=1, source_target_pairs={{0,3},{1,0},{2,1},{3,2},{4,7},{5,4},{6,5},{7,6},{8,11},{9,8},{10,9... | collective-permute-start | bytes 884744 | tf_op jit(solution)/shard_map/ppermute | solution.py:317
  29.0 2.2 %collective-permute-done.3.rest_3_ = bf16[32,64,128]{2,1,0:T(8,128)(2,1)S(1)} collective-permute-done((bf16[32,64,128]{2,1,0:T(8,128)(2,1)S(1)}, bf16[32,64,128]{2,1,0:T(8,128)(2,1)S(1)}, u32[]{:S(2)}, u32[]{:S(2)}) %collective-permute-start.3) | collective-permute-done | bytes 524320 | tf_op jit(solution)/shard_map/ppermute | solution.py:341
  31.2 10.2 %collective-permute-done.2.rest_2_ = bf16[32,64,128]{2,1,0:T(8,128)(2,1)S(1)} collective-permute-done((bf16[32,64,128]{2,1,0:T(8,128)(2,1)S(1)}, bf16[32,64,128]{2,1,0:T(8,128)(2,1)S(1)}, u32[]{:S(2)}, u32[]{:S(2)}) %collective-permute-start.2) | collective-permute-done | bytes 524320 | tf_op jit(solution)/shard_map/ppermute | solution.py:343
  41.5 0.8 shard_map.88
  42.3 1.6 %collective-permute-start.4 = (bf16[8,64,128]{2,1,0:T(8,128)(2,1)S(1)}, bf16[8,64,128]{2,1,0:T(8,128)(2,1)S(1)}, u32[]{:S(2)}, u32[]{:S(2)}) collective-permute-start(bf16[8,64,128]{2,1,0:T(8,128)(2,1)S(1)} %get-tuple-element.33), channel_id=1, source_target_pairs={{0,1},{1,2},{2,3},{3,0},{4,5},{5,6},{6,7},{7,4},{8,9},{9,10},{10,1... | collective-permute-start | bytes 393224 | tf_op jit(solution)/shard_map/ppermute | solution.py:317
  43.9 2.6 %collective-permute-start.5 = (bf16[8,64,128]{2,1,0:T(8,128)(2,1)S(1)}, bf16[8,64,128]{2,1,0:T(8,128)(2,1)S(1)}, u32[]{:S(2)}, u32[]{:S(2)}) collective-permute-start(bf16[8,64,128]{2,1,0:T(8,128)(2,1)S(1)} %get-tuple-element.34), channel_id=1, source_target_pairs={{0,2},{1,3},{2,0},{3,1},{4,6},{5,7},{6,4},{7,5},{8,10},{9,11},{10,... | collective-permute-start | bytes 393224 | tf_op jit(solution)/shard_map/ppermute | solution.py:317
  46.5 1.3 %collective-permute-start.6 = (bf16[8,64,128]{2,1,0:T(8,128)(2,1)S(1)}, bf16[8,64,128]{2,1,0:T(8,128)(2,1)S(1)}, u32[]{:S(2)}, u32[]{:S(2)}) collective-permute-start(bf16[8,64,128]{2,1,0:T(8,128)(2,1)S(1)} %get-tuple-element.35), channel_id=1, source_target_pairs={{0,3},{1,0},{2,1},{3,2},{4,7},{5,4},{6,5},{7,6},{8,11},{9,8},{10,9... | collective-permute-start | bytes 393224 | tf_op jit(solution)/shard_map/ppermute | solution.py:317
  47.9 2.8 %collective-permute-done.4.rest_1_ = bf16[8,64,128]{2,1,0:T(8,128)(2,1)S(1)} collective-permute-done((bf16[8,64,128]{2,1,0:T(8,128)(2,1)S(1)}, bf16[8,64,128]{2,1,0:T(8,128)(2,1)S(1)}, u32[]{:S(2)}, u32[]{:S(2)}) %collective-permute-start.4) | collective-permute-done | bytes 131104 | tf_op jit(solution)/shard_map/ppermute | solution.py:317
  50.7 10.9 %collective-permute-done.5.rest_2_ = bf16[8,64,128]{2,1,0:T(8,128)(2,1)S(1)} collective-permute-done((bf16[8,64,128]{2,1,0:T(8,128)(2,1)S(1)}, bf16[8,64,128]{2,1,0:T(8,128)(2,1)S(1)}, u32[]{:S(2)}, u32[]{:S(2)}) %collective-permute-start.5) | collective-permute-done | bytes 131104 | tf_op jit(solution)/shard_map/ppermute | solution.py:317
  61.6 1.0 %shard_map.91 = (bf16[2,64,128]{2,1,0:T(8,128)(2,1)S(1)}, bf16[2,64,128]{2,1,0:T(8,128)(2,1)S(1)}, bf16[2,64,128]{2,1,0:T(8,128)(2,1)S(1)}, bf16[2,64,128]{2,1,0:T(8,128)(2,1)S(1)}) custom-call(s32[2]{0:T(128)S(1)} %pad_add_fusion.where, bf16[18,64,128]{2,1,0:T(8,128)(2,1)S(1)} %get-tuple-element.44.rest_4_.rest_0_, ...), custom_call_target="tpu_custom_call" | custom-call | flops 134217728 | bytes 1179648 | tf_op jit(solution)/shard_map/pallas_call | solution.py:226
  62.6 3.3 %collective-permute-start.15 = (bf16[2,64,128]{2,1,0:T(8,128)(2,1)S(1)}, bf16[2,64,128]{2,1,0:T(8,128)(2,1)S(1)}, u32[]{:S(2)}, u32[]{:S(2)}) collective-permute-start(bf16[2,64,128]{2,1,0:T(8,128)(2,1)S(1)} %get-tuple-element.51), channel_id=1, source_target_pairs={{0,1},{1,2},{2,3},{3,0},{4,5},{5,6},{6,7},{7,4},{8,9},{9,10},{10,1... | collective-permute-start | bytes 98312 | tf_op jit(solution)/shard_map/ppermute | solution.py:317
  65.9 1.6 %collective-permute-start.14 = (bf16[2,64,128]{2,1,0:T(8,128)(2,1)S(1)}, bf16[2,64,128]{2,1,0:T(8,128)(2,1)S(1)}, u32[]{:S(2)}, u32[]{:S(2)}) collective-permute-start(bf16[2,64,128]{2,1,0:T(8,128)(2,1)S(1)} %get-tuple-element.50), channel_id=1, source_target_pairs={{0,2},{1,3},{2,0},{3,1},{4,6},{5,7},{6,4},{7,5},{8,10},{9,11},{10,... | collective-permute-start | bytes 98312 | tf_op jit(solution)/shard_map/ppermute | solution.py:317
  67.6 0.8 collective-permute-start.13
  68.4 1.0 %shard_map.89 = (bf16[8,64,128]{2,1,0:T(8,128)(2,1)S(1)}, bf16[8,64,128]{2,1,0:T(8,128)(2,1)S(1)}, bf16[8,64,128]{2,1,0:T(8,128)(2,1)S(1)}, bf16[8,64,128]{2,1,0:T(8,128)(2,1)S(1)}) custom-call(s32[2]{0:T(128)S(1)} %pad_add_fusion.where, bf16[8,64,128]{2,1,0:T(8,128)(2,1)S(1)} %get-tuple-element.32.rest_0_, ...), custom_call_target="tpu_custom_call" | custom-call | flops 134217728 | bytes 1048576 | tf_op jit(solution)/shard_map/pallas_call | solution.py:190
  69.4 1.3 %collective-permute-start.10 = (bf16[8,64,128]{2,1,0:T(8,128)(2,1)S(1)}, bf16[8,64,128]{2,1,0:T(8,128)(2,1)S(1)}, u32[]{:S(2)}, u32[]{:S(2)}) collective-permute-start(bf16[8,64,128]{2,1,0:T(8,128)(2,1)S(1)} %get-tuple-element.41), channel_id=1, source_target_pairs={{0,1},{1,2},{2,3},{3,0},{4,5},{5,6},{6,7},{7,4},{8,9},{9,10},{10,1... | collective-permute-start | bytes 393224 | tf_op jit(solution)/shard_map/ppermute | solution.py:317
  70.7 1.3 %collective-permute-start.11 = (bf16[8,64,128]{2,1,0:T(8,128)(2,1)S(1)}, bf16[8,64,128]{2,1,0:T(8,128)(2,1)S(1)}, u32[]{:S(2)}, u32[]{:S(2)}) collective-permute-start(bf16[8,64,128]{2,1,0:T(8,128)(2,1)S(1)} %get-tuple-element.42), channel_id=1, source_target_pairs={{0,2},{1,3},{2,0},{3,1},{4,6},{5,7},{6,4},{7,5},{8,10},{9,11},{10,... | collective-permute-start | bytes 393224 | tf_op jit(solution)/shard_map/ppermute | solution.py:317
  72.0 1.3 %collective-permute-start.12 = (bf16[8,64,128]{2,1,0:T(8,128)(2,1)S(1)}, bf16[8,64,128]{2,1,0:T(8,128)(2,1)S(1)}, u32[]{:S(2)}, u32[]{:S(2)}) collective-permute-start(bf16[8,64,128]{2,1,0:T(8,128)(2,1)S(1)} %get-tuple-element.43), channel_id=1, source_target_pairs={{0,3},{1,0},{2,1},{3,2},{4,7},{5,4},{6,5},{7,6},{8,11},{9,8},{10,9... | collective-permute-start | bytes 393224 | tf_op jit(solution)/shard_map/ppermute | solution.py:317
  73.4 1.2 %collective-permute-done.16 = f32[2,64,128]{2,1,0:T(8,128)S(1)} collective-permute-done((f32[2,64,128]{2,1,0:T(8,128)S(1)}, f32[2,64,128]{2,1,0:T(8,128)S(1)}, u32[]{:S(2)}, u32[]{:S(2)}) %collective-permute-start.16) | collective-permute-done | bytes 65568 | tf_op jit(solution)/shard_map/ppermute | solution.py:366
  74.6 1.4 %collective-permute-start.19 = (f32[2,64,128]{2,1,0:T(8,128)S(1)}, f32[2,64,128]{2,1,0:T(8,128)S(1)}, u32[]{:S(2)}, u32[]{:S(2)}) collective-permute-start(f32[2,64,128]{2,1,0:T(8,128)S(1)} %add.59), channel_id=1, source_target_pairs={{0,24},{4,28},{8,16},{12,20},{16,8},{20,12},{24,0},{28,4},{1,25},{... | collective-permute-start | bytes 196616 | tf_op jit(solution)/shard_map/ppermute | solution.py:368
  76.1 1.2 %collective-permute-start.17 = (f32[2,64,128]{2,1,0:T(8,128)S(1)}, f32[2,64,128]{2,1,0:T(8,128)S(1)}, u32[]{:S(2)}, u32[]{:S(2)}) collective-permute-start(f32[2,64,128]{2,1,0:T(8,128)S(1)} %add.59), channel_id=1, source_target_pairs={{0,8},{4,12},{8,0},{12,4},{16,24},{20,28},{24,16},{28,20},{1,9},{5... | collective-permute-start | bytes 196616 | tf_op jit(solution)/shard_map/ppermute | solution.py:368
  77.7 1.2 %collective-permute-start.18 = (f32[2,64,128]{2,1,0:T(8,128)S(1)}, f32[2,64,128]{2,1,0:T(8,128)S(1)}, u32[]{:S(2)}, u32[]{:S(2)}) collective-permute-start(f32[2,64,128]{2,1,0:T(8,128)S(1)} %add.59), channel_id=1, source_target_pairs={{0,16},{4,20},{8,24},{12,28},{16,0},{20,4},{24,8},{28,12},{1,17},{... | collective-permute-start | bytes 196616 | tf_op jit(solution)/shard_map/ppermute | solution.py:368
  78.9 3.0 %collective-permute-done.11.rest_2_ = bf16[8,64,128]{2,1,0:T(8,128)(2,1)S(1)} collective-permute-done((bf16[8,64,128]{2,1,0:T(8,128)(2,1)S(1)}, bf16[8,64,128]{2,1,0:T(8,128)(2,1)S(1)}, u32[]{:S(2)}, u32[]{:S(2)}) %collective-permute-start.11) | collective-permute-done | bytes 131104 | tf_op jit(solution)/shard_map/ppermute | solution.py:317
  81.9 1.4 %shard_map.90 = bf16[32,64,128]{2,1,0:T(8,128)(2,1)} custom-call(s32[2]{0:T(128)S(1)} %pad_add_fusion.where, bf16[8,64,128]{2,1,0:T(8,128)(2,1)S(1)} %get-tuple-element.40.rest_0_, bf16[8,64,128]{2,1,0:T(8,128)(2,1)S(1)} %collective-permute-done.10.rest_1_, bf16[8,64,128]{2,1,0:T(8,128)(2,1)S(1)} %collective-permute-done.11.rest_2_, ...), custom_call_target="tpu_custom_call" | custom-call | bytes 33554432 | tf_op jit(solution)/shard_map/pallas_call | solution.py:302
  (27 shorter events, 2.2 us)
Async XLA Ops:
  0.6 21.4 %copy-start = (bf16[64,256]{1,0:T(8,128)(2,1)S(1)}, bf16[64,256]{1,0:T(8,128)(2,1)}, u32[]{:S(2)}) copy-start(bf16[64,256]{1,0:T(8,128)(2,1)} %param.10) | copy-start | bytes 98308
  1.5 0.7 copy-start.1
  13.3 5.7 %collective-permute-start.1 = (bf16[32,64,128]{2,1,0:T(8,128)(2,1)}, bf16[32,64,128]{2,1,0:T(8,128)(2,1)S(1)}, u32[]{:S(2)}, u32[]{:S(2)}) collective-permute-start(bf16[32,64,128]{2,1,0:T(8,128)(2,1)} %get-tuple-element.30), channel_id=1, source_target_pairs={{0,4},{4,0},{8,12},{12,8},{16,20},{20,16},{24,28},{28,24},{1,5},{5... | collective-permute-start | bytes 1572872 | tf_op jit(solution)/shard_map/ppermute | solution.py:340
  13.3 14.3 %collective-permute-start = (bf16[32,64,128]{2,1,0:T(8,128)(2,1)}, bf16[32,64,128]{2,1,0:T(8,128)(2,1)S(1)}, u32[]{:S(2)}, u32[]{:S(2)}) collective-permute-start(bf16[32,64,128]{2,1,0:T(8,128)(2,1)} %get-tuple-element.28), channel_id=1, source_target_pairs={{0,4},{4,0},{8,12},{12,8},{16,20},{20,16},{24,28},{28,24},{1,5},{5... | collective-permute-start | bytes 1572872 | tf_op jit(solution)/shard_map/ppermute | solution.py:344
  13.8 17.4 %collective-permute-start.3 = (bf16[32,64,128]{2,1,0:T(8,128)(2,1)S(1)}, bf16[32,64,128]{2,1,0:T(8,128)(2,1)S(1)}, u32[]{:S(2)}, u32[]{:S(2)}) collective-permute-start(bf16[32,64,128]{2,1,0:T(8,128)(2,1)S(1)} %get-tuple-element.31), channel_id=1, source_target_pairs={{0,24},{4,12},{8,0},{12,20},{16,8},{20,28},{24,16},{28,4},{1,25},{... | collective-permute-start | bytes 1572872 | tf_op jit(solution)/shard_map/ppermute | solution.py:341
  19.2 22.3 %collective-permute-start.2 = (bf16[32,64,128]{2,1,0:T(8,128)(2,1)S(1)}, bf16[32,64,128]{2,1,0:T(8,128)(2,1)S(1)}, u32[]{:S(2)}, u32[]{:S(2)}) collective-permute-start(bf16[32,64,128]{2,1,0:T(8,128)(2,1)S(1)} %shard_map.87), channel_id=1, source_target_pairs={{0,28},{4,8},{8,4},{12,16},{16,12},{20,24},{24,20},{28,0},{1,29},{... | collective-permute-start | bytes 1572872 | tf_op jit(solution)/shard_map/ppermute | solution.py:343
  23.5 23.0 %collective-permute-start.7 = (bf16[18,64,128]{2,1,0:T(8,128)(2,1)S(1)}, bf16[18,64,128]{2,1,0:T(8,128)(2,1)S(1)}, u32[]{:S(2)}, u32[]{:S(2)}) collective-permute-start(bf16[18,64,128]{2,1,0:T(8,128)(2,1)S(1)} %get-tuple-element.61), channel_id=1, source_target_pairs={{0,1},{1,2},{2,3},{3,0},{4,5},{5,6},{6,7},{7,4},{8,9},{9,10},{10,1... | collective-permute-start | bytes 884744 | tf_op jit(solution)/shard_map/ppermute | solution.py:317
  25.1 22.8 %collective-permute-start.8 = (bf16[18,64,128]{2,1,0:T(8,128)(2,1)S(1)}, bf16[18,64,128]{2,1,0:T(8,128)(2,1)S(1)}, u32[]{:S(2)}, u32[]{:S(2)}) collective-permute-start(bf16[18,64,128]{2,1,0:T(8,128)(2,1)S(1)} %get-tuple-element.62), channel_id=1, source_target_pairs={{0,2},{1,3},{2,0},{3,1},{4,6},{5,7},{6,4},{7,5},{8,10},{9,11},{10,... | collective-permute-start | bytes 884744 | tf_op jit(solution)/shard_map/ppermute | solution.py:317
  27.7 20.2 %collective-permute-start.9 = (bf16[18,64,128]{2,1,0:T(8,128)(2,1)S(1)}, bf16[18,64,128]{2,1,0:T(8,128)(2,1)S(1)}, u32[]{:S(2)}, u32[]{:S(2)}) collective-permute-start(bf16[18,64,128]{2,1,0:T(8,128)(2,1)S(1)} %get-tuple-element.60), channel_id=1, source_target_pairs={{0,3},{1,0},{2,1},{3,2},{4,7},{5,4},{6,5},{7,6},{8,11},{9,8},{10,9... | collective-permute-start | bytes 884744 | tf_op jit(solution)/shard_map/ppermute | solution.py:317
  42.3 8.4 %collective-permute-start.4 = (bf16[8,64,128]{2,1,0:T(8,128)(2,1)S(1)}, bf16[8,64,128]{2,1,0:T(8,128)(2,1)S(1)}, u32[]{:S(2)}, u32[]{:S(2)}) collective-permute-start(bf16[8,64,128]{2,1,0:T(8,128)(2,1)S(1)} %get-tuple-element.33), channel_id=1, source_target_pairs={{0,1},{1,2},{2,3},{3,0},{4,5},{5,6},{6,7},{7,4},{8,9},{9,10},{10,1... | collective-permute-start | bytes 393224 | tf_op jit(solution)/shard_map/ppermute | solution.py:317
  43.9 17.7 %collective-permute-start.5 = (bf16[8,64,128]{2,1,0:T(8,128)(2,1)S(1)}, bf16[8,64,128]{2,1,0:T(8,128)(2,1)S(1)}, u32[]{:S(2)}, u32[]{:S(2)}) collective-permute-start(bf16[8,64,128]{2,1,0:T(8,128)(2,1)S(1)} %get-tuple-element.34), channel_id=1, source_target_pairs={{0,2},{1,3},{2,0},{3,1},{4,6},{5,7},{6,4},{7,5},{8,10},{9,11},{10,... | collective-permute-start | bytes 393224 | tf_op jit(solution)/shard_map/ppermute | solution.py:317
  46.5 15.1 %collective-permute-start.6 = (bf16[8,64,128]{2,1,0:T(8,128)(2,1)S(1)}, bf16[8,64,128]{2,1,0:T(8,128)(2,1)S(1)}, u32[]{:S(2)}, u32[]{:S(2)}) collective-permute-start(bf16[8,64,128]{2,1,0:T(8,128)(2,1)S(1)} %get-tuple-element.35), channel_id=1, source_target_pairs={{0,3},{1,0},{2,1},{3,2},{4,7},{5,4},{6,5},{7,6},{8,11},{9,8},{10,9... | collective-permute-start | bytes 393224 | tf_op jit(solution)/shard_map/ppermute | solution.py:317
  62.6 9.4 %collective-permute-start.15 = (bf16[2,64,128]{2,1,0:T(8,128)(2,1)S(1)}, bf16[2,64,128]{2,1,0:T(8,128)(2,1)S(1)}, u32[]{:S(2)}, u32[]{:S(2)}) collective-permute-start(bf16[2,64,128]{2,1,0:T(8,128)(2,1)S(1)} %get-tuple-element.51), channel_id=1, source_target_pairs={{0,1},{1,2},{2,3},{3,0},{4,5},{5,6},{6,7},{7,4},{8,9},{9,10},{10,1... | collective-permute-start | bytes 98312 | tf_op jit(solution)/shard_map/ppermute | solution.py:317
  65.9 7.3 %collective-permute-start.14 = (bf16[2,64,128]{2,1,0:T(8,128)(2,1)S(1)}, bf16[2,64,128]{2,1,0:T(8,128)(2,1)S(1)}, u32[]{:S(2)}, u32[]{:S(2)}) collective-permute-start(bf16[2,64,128]{2,1,0:T(8,128)(2,1)S(1)} %get-tuple-element.50), channel_id=1, source_target_pairs={{0,2},{1,3},{2,0},{3,1},{4,6},{5,7},{6,4},{7,5},{8,10},{9,11},{10,... | collective-permute-start | bytes 98312 | tf_op jit(solution)/shard_map/ppermute | solution.py:317
  67.6 5.7 %collective-permute-start.13 = (bf16[2,64,128]{2,1,0:T(8,128)(2,1)S(1)}, bf16[2,64,128]{2,1,0:T(8,128)(2,1)S(1)}, u32[]{:S(2)}, u32[]{:S(2)}) collective-permute-start(bf16[2,64,128]{2,1,0:T(8,128)(2,1)S(1)} %get-tuple-element.49), channel_id=1, source_target_pairs={{0,3},{1,0},{2,1},{3,2},{4,7},{5,4},{6,5},{7,6},{8,11},{9,8},{10,9... | collective-permute-start | bytes 98312 | tf_op jit(solution)/shard_map/ppermute | solution.py:317
  69.4 8.3 %collective-permute-start.10 = (bf16[8,64,128]{2,1,0:T(8,128)(2,1)S(1)}, bf16[8,64,128]{2,1,0:T(8,128)(2,1)S(1)}, u32[]{:S(2)}, u32[]{:S(2)}) collective-permute-start(bf16[8,64,128]{2,1,0:T(8,128)(2,1)S(1)} %get-tuple-element.41), channel_id=1, source_target_pairs={{0,1},{1,2},{2,3},{3,0},{4,5},{5,6},{6,7},{7,4},{8,9},{9,10},{10,1... | collective-permute-start | bytes 393224 | tf_op jit(solution)/shard_map/ppermute | solution.py:317
  70.7 11.2 %collective-permute-start.11 = (bf16[8,64,128]{2,1,0:T(8,128)(2,1)S(1)}, bf16[8,64,128]{2,1,0:T(8,128)(2,1)S(1)}, u32[]{:S(2)}, u32[]{:S(2)}) collective-permute-start(bf16[8,64,128]{2,1,0:T(8,128)(2,1)S(1)} %get-tuple-element.42), channel_id=1, source_target_pairs={{0,2},{1,3},{2,0},{3,1},{4,6},{5,7},{6,4},{7,5},{8,10},{9,11},{10,... | collective-permute-start | bytes 393224 | tf_op jit(solution)/shard_map/ppermute | solution.py:317
  72.0 9.9 %collective-permute-start.12 = (bf16[8,64,128]{2,1,0:T(8,128)(2,1)S(1)}, bf16[8,64,128]{2,1,0:T(8,128)(2,1)S(1)}, u32[]{:S(2)}, u32[]{:S(2)}) collective-permute-start(bf16[8,64,128]{2,1,0:T(8,128)(2,1)S(1)} %get-tuple-element.43), channel_id=1, source_target_pairs={{0,3},{1,0},{2,1},{3,2},{4,7},{5,4},{6,5},{7,6},{8,11},{9,8},{10,9... | collective-permute-start | bytes 393224 | tf_op jit(solution)/shard_map/ppermute | solution.py:317
  73.3 1.3 %collective-permute-start.16 = (f32[2,64,128]{2,1,0:T(8,128)S(1)}, f32[2,64,128]{2,1,0:T(8,128)S(1)}, u32[]{:S(2)}, u32[]{:S(2)}) collective-permute-start(f32[2,64,128]{2,1,0:T(8,128)S(1)} %convert_add_fusion), channel_id=1, source_target_pairs={{0,4},{4,0},{8,12},{12,8},{16,20},{20,16},{24,28},{28,24},{1,5},{5... | collective-permute-start | bytes 196616 | tf_op jit(solution)/shard_map/ppermute | solution.py:366
  74.6 8.6 %collective-permute-start.19 = (f32[2,64,128]{2,1,0:T(8,128)S(1)}, f32[2,64,128]{2,1,0:T(8,128)S(1)}, u32[]{:S(2)}, u32[]{:S(2)}) collective-permute-start(f32[2,64,128]{2,1,0:T(8,128)S(1)} %add.59), channel_id=1, source_target_pairs={{0,24},{4,28},{8,16},{12,20},{16,8},{20,12},{24,0},{28,4},{1,25},{... | collective-permute-start | bytes 196616 | tf_op jit(solution)/shard_map/ppermute | solution.py:368
  76.1 7.2 %collective-permute-start.17 = (f32[2,64,128]{2,1,0:T(8,128)S(1)}, f32[2,64,128]{2,1,0:T(8,128)S(1)}, u32[]{:S(2)}, u32[]{:S(2)}) collective-permute-start(f32[2,64,128]{2,1,0:T(8,128)S(1)} %add.59), channel_id=1, source_target_pairs={{0,8},{4,12},{8,0},{12,4},{16,24},{20,28},{24,16},{28,20},{1,9},{5... | collective-permute-start | bytes 196616 | tf_op jit(solution)/shard_map/ppermute | solution.py:368
  77.7 5.6 %collective-permute-start.18 = (f32[2,64,128]{2,1,0:T(8,128)S(1)}, f32[2,64,128]{2,1,0:T(8,128)S(1)}, u32[]{:S(2)}, u32[]{:S(2)}) collective-permute-start(f32[2,64,128]{2,1,0:T(8,128)S(1)} %add.59), channel_id=1, source_target_pairs={{0,16},{4,20},{8,24},{12,28},{16,0},{20,4},{24,8},{28,12},{1,17},{... | collective-permute-start | bytes 196616 | tf_op jit(solution)/shard_map/ppermute | solution.py:368

commit v8 on v7

--- a/solution.py
+++ b/solution.py
@@ -39,8 +39,9 @@
     return value & (size - 1)
 
 
-def tiles_kernel(slabs, where, cols, live, cot, mask, tiles, *rest):
-    outs, (cot_in, mask_in, z, ring, first, second, rows, left, sems, z_sems) = rest[:5], rest[5:]
+def tiles_kernel(slabs, reps, where, cols, live, weight, cot, mask, tiles, *rest):
+    outs, packed, rest = rest[:5], rest[5 : 5 + reps], rest[5 + reps :]
+    cot_in, mask_in, z, ring, first, second, rows, left, sems, z_sems = rest
     totals = (first, second)
     blocks, slots = cols.shape
     per_row = slots // GROUP
@@ -77,10 +78,10 @@
 
     def clear(i, carry):
         for total in totals:
-            total[i] = jnp.zeros(total.shape[1:], F32)
+            total[pl.ds(i * GROUP, GROUP)] = jnp.zeros((GROUP,) + total.shape[1:], F32)
         return carry
 
-    lax.fori_loop(0, window, clear, 0)
+    lax.fori_loop(0, window // GROUP, clear, 0)
     for copy in copies:
         copy.wait()
 
@@ -89,6 +90,12 @@
         return carry
 
     lax.fori_loop(0, blocks, mask_row, 0)
+    nodes = z.shape[2]
+    share = blocks // reps
+    for s in range(reps):
+        packed[s][:share] = z[pl.ds(wrap(where[1] + s, reps) * share, share)]
+        for h in range(weight.shape[1] // nodes):
+            packed[s][share + h] = weight[:, h * nodes : (h + 1) * nodes]
     shift = REACH * blocks - where[0] * blocks
 
     def step(i, carry):
@@ -115,23 +122,27 @@
         base = ((order - REACH) * sign + REACH) * blocks
 
         def store(i, carry, out=out, base=base):
-            out[i] = (first[base + i] + second[base + i]).astype(BF16)
+            for k in range(GROUP):
+                at = i * GROUP + k
+                out[at] = (first[base + at] + second[base + at]).astype(BF16)
             return carry
 
-        lax.fori_loop(0, blocks, store, 0)
-
-
-def contributions(where, cols, live, cot, mask, tiles, slabs):
+        lax.fori_loop(0, blocks // GROUP, store, 0)
+
+
+def contributions(where, cols, live, weight, cot, mask, tiles, slabs, reps):
     blocks, slots, nodes = tiles.shape[:3]
     features = cot.shape[1]
     window = (2 * REACH + 1) * blocks
     lists = blocks * (slots // GROUP) + slots // GROUP + STEP
     total = pltpu.VMEM((window + 1, features, nodes), F32)
-    return pl.pallas_call(
-        functools.partial(tiles_kernel, slabs),
-        out_shape=[jax.ShapeDtypeStruct(cot.shape, BF16)] * 5,
-        in_specs=[smem(), smem(), smem(), hbm(), hbm(), hbm()],
-        out_specs=[vmem()] * 5,
+    packs = blocks // reps + weight.shape[1] // nodes
+    return pl.pallas_call(
+        functools.partial(tiles_kernel, slabs, reps),
+        out_shape=[jax.ShapeDtypeStruct(cot.shape, BF16)] * 5
+        + [jax.ShapeDtypeStruct((packs, features, nodes), BF16)] * reps,
+        in_specs=[smem(), smem(), smem(), vmem(), hbm(), hbm(), hbm()],
+        out_specs=[vmem()] * (5 + reps),
         scratch_shapes=[
             pltpu.VMEM(cot.shape, BF16),
             pltpu.VMEM(mask.shape, jnp.int32),
@@ -152,8 +163,9 @@
         ),
     )(
         where,
-        cols,
-        live,
+        in_hbm(cols),
+        in_hbm(live),
+        weight,
         in_hbm(cot),
         in_hbm(mask),
         in_hbm(tiles.reshape(blocks * slots, nodes, nodes)),
@@ -202,12 +214,13 @@
     )(where, *shares, *packed)
 
 
-def weight_kernel(reps, blocks, where, *rest):
-    packed, outs, (whole_z, whole_a) = rest[:reps], rest[reps : 2 * reps], rest[2 * reps :]
-    features, nodes = outs[0].shape[1:]
+def weight_kernel(reps, where, *rest):
+    packed, aggs, outs = rest[:reps], rest[reps : 2 * reps], rest[2 * reps : 3 * reps]
+    whole_z, whole_a = rest[3 * reps :]
+    blocks, features, nodes = aggs[0].shape
     lay_features(where, packed, whole_z)
     for s in range(reps):
-        whole_a[:, pl.ds(s * features, features), :] = packed[s][blocks : 2 * blocks]
+        whole_a[:, pl.ds(s * features, features), :] = aggs[s][...]
     total = jnp.zeros((whole_a.shape[1], whole_z.shape[1]), F32)
     for b in range(blocks):
         total += lax.dot_general(
@@ -219,14 +232,14 @@
             outs[s][h] = part.astype(BF16)
 
 
-def weight_partial(where, packed, blocks):
+def weight_partial(where, packed, aggs):
     reps = len(packed)
-    _, features, nodes = packed[0].shape
+    blocks, features, nodes = aggs[0].shape
     width = reps * features
     return pl.pallas_call(
-        functools.partial(weight_kernel, reps, blocks),
+        functools.partial(weight_kernel, reps),
         out_shape=[jax.ShapeDtypeStruct((width // nodes, features, nodes), BF16)] * reps,
-        in_specs=[smem()] + [vmem()] * reps,
+        in_specs=[smem()] + [vmem()] * (2 * reps),
         out_specs=[vmem()] * reps,
         scratch_shapes=[pltpu.VMEM((blocks, width, nodes), BF16)] * 2,
         compiler_params=pltpu.CompilerParams(vmem_limit_bytes=4 * MIB),
@@ -235,7 +248,7 @@
             bytes_accessed=4 * blocks * nodes * width + 2 * width * width,
             transcendentals=0,
         ),
-    )(where, *packed)
+    )(where, *packed, *aggs)
 
 
 def add_kernel(one, other, out):
@@ -334,35 +347,28 @@
     pair = [(i, i ^ 1) for i in range(slabs)]
     to_one = [(i, (i + (1 if i % 2 else -1)) % slabs) for i in range(slabs)]
     to_two = [(i, (i + (2 if i % 2 else -2)) % slabs) for i in range(slabs)]
-    near, beside, own, one, two = contributions(
-        where, col_block, live_count, cotangent, relu_mask, tiles, slabs
-    )
+    aggs = [shift(node_share(aggregated, s), s) for s in range(reps)]
+    near, beside, own, one, two, *packed = contributions(
+        where, col_block, live_count, weight, cotangent, relu_mask, tiles, slabs, reps
+    )
+    near, aggs = lax.optimization_barrier((near, aggs))
     near_in = lax.ppermute(near, "blk", pair)
     two_in = lax.ppermute(two, "blk", to_two)
     one = add(one, near_in)
     one_in = lax.ppermute(one, "blk", to_one)
     beside_in = lax.ppermute(beside, "blk", pair)
 
-    cotangent, relu_mask, aggregated, weight, _ = lax.optimization_barrier(
-        (cotangent, relu_mask, aggregated, weight, one)
-    )
-    grad_z = cotangent * relu_mask.astype(BF16)
-    weight_pieces = weight.reshape(features, width // nodes, nodes).transpose(1, 0, 2)
-    packed = [
-        shift(
-            jnp.concatenate([node_share(grad_z, s), node_share(aggregated, s), weight_pieces]), s
-        )
-        for s in range(reps)
-    ]
-
+    packed, _ = lax.optimization_barrier((packed, one))
+    packed = [shift(value, s) for s, value in enumerate(packed)]
+    grad_w = weight_partial(where, packed, aggs)
+    grad_w = sum(shift(part, -s).astype(F32) for s, part in enumerate(grad_w))
+
+    own, grad_w = lax.optimization_barrier((own, grad_w))
     shares = total_shares(where, [own, beside_in, one_in, two_in], reps)
     shares = [shift(value, s) for s, value in enumerate(shares)]
-    held, _ = lax.optimization_barrier((packed, shares))
-    outs = [shift(value, s) for s, value in enumerate(mix(where, shares, packed, 2 * share))]
+    outs = [shift(value, s) for s, value in enumerate(mix(where, shares, packed, share))]
     input_grad = lay_blocks(where, outs, cotangent.shape)
 
-    grad_w = weight_partial(where, held, share)
-    grad_w = sum(shift(part, -s).astype(F32) for s, part in enumerate(grad_w))
     grad_w = grad_w + lax.ppermute(grad_w, "blk", pair)
     grad_w = grad_w + sum(
         lax.ppermute(grad_w, "blk", [(i, i ^ step) for i in range(slabs)])

time: 84.2 us -> 81.1 us (0.963)
  waiting for transfers between devices: 30.8 us -> 26.2 us
  starting transfers between devices: 31.8 us -> 35.2 us
  other arithmetic: 2.36 us -> 0.75 us
  Pallas kernels: 15.5 us -> 14.6 us
    ppermute x1, waiting for transfers between devices: 10.2 us -> 0.01 us  [on_device(): one_in = lax.ppermute(one, 'blk', to_one)]
    ppermute x12 -> x15, starting transfers between devices: 20.8 us -> 27.1 us  [shift(): lax.ppermute(value, 'rep', [(i, (i + steps) % reps) for i in range(reps)])]
    ppermute x12 -> x15, waiting for transfers between devices: 17.1 us -> 23 us  [shift(): lax.ppermute(value, 'rep', [(i, (i + steps) % reps) for i in range(reps)])]
    ppermute x1, starting transfers between devices: 5.07 us -> 1.57 us  [on_device(): two_in = lax.ppermute(two, 'blk', to_two)]
    ppermute x1, waiting for transfers between devices: 2.22 us -> 0.01 us  [on_device(): two_in = lax.ppermute(two, 'blk', to_two)]
    ppermute x1, waiting for transfers between devices: 0.01 us -> 1.9 us  [on_device(): near_in = lax.ppermute(near, 'blk', pair)]
    mul x1 -> x0, other arithmetic: 1.46 us -> none  [on_device(): grad_z = cotangent * relu_mask.astype(BF16)]
    ppermute x3, starting transfers between devices: 3.85 us -> 5.3 us  [on_device(): lax.ppermute(grad_w, 'blk', [(i, i ^ step) for i in range(slabs)])]
  transfers between devices with their start and end apart: 20 -> 23, of which waited for: 7 -> 11; matrix products, arithmetic and copies ran while one was open for 3% -> 3% of each run, Pallas kernels for 4% -> 15%
where the time goes in v8:
time: 81.1 us; the launch traced here: 80.8 us
  starting transfers between devices  35.2 us (43%)
  waiting for transfers between devices  26.2 us (32%)
  Pallas kernels  14.6 us (18%)
  local copies, waits for them, and re-layouts  3.27 us (4%)
    ppermute x15, starting transfers between devices, shift(): lax.ppermute(value, 'rep', [(i, (i + steps) % reps) for i in range(reps)])  27.1 us
    ppermute x15, waiting for transfers between devices, shift(): lax.ppermute(value, 'rep', [(i, (i + steps) % reps) for i in range(reps)])  23 us
    pallas_call x1, Pallas kernels, contributions(): pl.pallas_call(functools.partial(tiles_kernel, slabs, reps), out_shape=[j...  10.2 us
    ppermute x3, starting transfers between devices, on_device(): lax.ppermute(grad_w, 'blk', [(i, i ^ step) for i in range(slabs)])  5.3 us
    unnamed x3, local copies, waits for them, and re-layouts  2.13 us
    ppermute x1, waiting for transfers between devices, on_device(): near_in = lax.ppermute(near, 'blk', pair)  1.9 us
  transfers between devices with their start and end apart: 23, of which 11 were waited for; matrix products, arithmetic and copies ran while one was open for 3% of the time, Pallas kernels for 15%

profile of v8, /device:TPU:0, one launch (start us, length us, event | category | flops | bytes accessed | tf_op | source)
XLA Modules:
  0.0 80.8 jit_solution(8947995447223867834)
XLA Ops:
  0.7 1.1 %constant_dynamic-slice_fusion = (bf16[8,64,128]{2,1,0:T(8,128)(2,1)S(1)}, bf16[8,64,128]{2,1,0:T(8,128)(2,1)S(1)}, bf16[8,64,128]{2,1,0:T(8,128)(2,1)S(1)}, bf16[8,64,128]{2,1,0:T(8,128)(2,1)S(1)}) fusion(bf16[32,64,128]{2,1,0:T(8,128)(2,1)} %param.9, s32[]{:T(128)S(6)} %select_n.15, s32[]{:T(128)S(6)} %select_n.13, s32[]{:T(128)S(6)} %select_n.12, ...), kind=kLoop, calls=%fused_computation.3 | loop fusion | bytes 1048592 | tf_op jit(solution)/shard_map/dynamic_slice | solution.py:337
  1.8 5.1 %collective-permute-start.2 = (bf16[8,64,128]{2,1,0:T(8,128)(2,1)S(1)}, bf16[8,64,128]{2,1,0:T(8,128)(2,1)S(1)}, u32[]{:S(2)}, u32[]{:S(2)}) collective-permute-start(bf16[8,64,128]{2,1,0:T(8,128)(2,1)S(1)} %get-tuple-element.66), channel_id=1, source_target_pairs={{0,3},{1,0},{2,1},{3,2},{4,7},{5,4},{6,5},{7,6},{8,11},{9,8},{10,9... | collective-permute-start | bytes 393224 | tf_op jit(solution)/shard_map/ppermute | solution.py:330
  6.9 1.0 %collective-permute-start.1 = (bf16[8,64,128]{2,1,0:T(8,128)(2,1)S(1)}, bf16[8,64,128]{2,1,0:T(8,128)(2,1)S(1)}, u32[]{:S(2)}, u32[]{:S(2)}) collective-permute-start(bf16[8,64,128]{2,1,0:T(8,128)(2,1)S(1)} %get-tuple-element.69), channel_id=1, source_target_pairs={{0,2},{1,3},{2,0},{3,1},{4,6},{5,7},{6,4},{7,5},{8,10},{9,11},{10,... | collective-permute-start | bytes 393224 | tf_op jit(solution)/shard_map/ppermute | solution.py:330
  8.0 1.4 %copy.10.cols = s32[32,16]{1,0:T(8,128)} copy(s32[32,16]{0,1:T(8,128)} %param.12) | data formatting | bytes 4096 | tf_op args[5]
  9.4 0.8 copy-done
  10.1 10.2 %shard_map.86 = (bf16[32,64,128]{2,1,0:T(8,128)(2,1)S(1)}, bf16[32,64,128]{2,1,0:T(8,128)(2,1)S(1)}, bf16[32,64,128]{2,1,0:T(8,128)(2,1)S(1)}, bf16[32,64,128]{2...) custom-call(s32[2]{0:T(128)S(1)} %pad_add_fusion.where, ...), custom_call_target="tpu_custom_call" | custom-call | flops 1073741824 | bytes 16777216 | tf_op jit(solution)/shard_map/pallas_call | solution.py:140
  20.4 1.9 %collective-permute-done.3.other = bf16[32,64,128]{2,1,0:T(8,128)(2,1)S(1)} collective-permute-done((bf16[32,64,128]{2,1,0:T(8,128)(2,1)S(1)}, bf16[32,64,128]{2,1,0:T(8,128)(2,1)S(1)}, u32[]{:S(2)}, u32[]{:S(2)}) %collective-permute-start.3) | collective-permute-done | bytes 524320 | tf_op jit(solution)/shard_map/ppermute | solution.py:355
  22.6 3.4 %collective-permute-start.4 = (bf16[10,64,128]{2,1,0:T(8,128)(2,1)S(1)}, bf16[10,64,128]{2,1,0:T(8,128)(2,1)S(1)}, u32[]{:S(2)}, u32[]{:S(2)}) collective-permute-start(bf16[10,64,128]{2,1,0:T(8,128)(2,1)S(1)} %get-tuple-element.43), channel_id=1, source_target_pairs={{0,1},{1,2},{2,3},{3,0},{4,5},{5,6},{6,7},{7,4},{8,9},{9,10},{10,1... | collective-permute-start | bytes 491528 | tf_op jit(solution)/shard_map/ppermute | solution.py:330
  26.0 1.6 %collective-permute-start.12 = (bf16[32,64,128]{2,1,0:T(8,128)(2,1)S(1)}, bf16[32,64,128]{2,1,0:T(8,128)(2,1)S(1)}, u32[]{:S(2)}, u32[]{:S(2)}) collective-permute-start(bf16[32,64,128]{2,1,0:T(8,128)(2,1)S(1)} %get-tuple-element.56), channel_id=1, source_target_pairs={{0,24},{4,12},{8,0},{12,20},{16,8},{20,28},{24,16},{28,4},{1,25},{... | collective-permute-start | bytes 1572872 | tf_op jit(solution)/shard_map/ppermute | solution.py:356
  27.6 1.2 %collective-permute-start.11 = (bf16[32,64,128]{2,1,0:T(8,128)(2,1)S(1)}, bf16[32,64,128]{2,1,0:T(8,128)(2,1)S(1)}, u32[]{:S(2)}, u32[]{:S(2)}) collective-permute-start(bf16[32,64,128]{2,1,0:T(8,128)(2,1)S(1)} %shard_map.87), channel_id=1, source_target_pairs={{0,28},{4,8},{8,4},{12,16},{16,12},{20,24},{24,20},{28,0},{1,29},{... | collective-permute-start | bytes 1572872 | tf_op jit(solution)/shard_map/ppermute | solution.py:358
  28.8 1.9 %collective-permute-done.4.rest_1_.rest_5_ = bf16[10,64,128]{2,1,0:T(8,128)(2,1)S(1)} collective-permute-done((bf16[10,64,128]{2,1,0:T(8,128)(2,1)S(1)}, bf16[10,64,128]{2,1,0:T(8,128)(2,1)S(1)}, u32[]{:S(2)}, u32[]{:S(2)}) %collective-permute-start.4) | collective-permute-done | bytes 163872 | tf_op jit(solution)/shard_map/ppermute | solution.py:330
  30.7 1.0 %collective-permute-start.6 = (bf16[10,64,128]{2,1,0:T(8,128)(2,1)S(1)}, bf16[10,64,128]{2,1,0:T(8,128)(2,1)S(1)}, u32[]{:S(2)}, u32[]{:S(2)}) collective-permute-start(bf16[10,64,128]{2,1,0:T(8,128)(2,1)S(1)} %get-tuple-element.45), channel_id=1, source_target_pairs={{0,3},{1,0},{2,1},{3,2},{4,7},{5,4},{6,5},{7,6},{8,11},{9,8},{10,9... | collective-permute-start | bytes 491528 | tf_op jit(solution)/shard_map/ppermute | solution.py:330
  31.7 7.7 %collective-permute-done.5.rest_2_.rest_6_ = bf16[10,64,128]{2,1,0:T(8,128)(2,1)S(1)} collective-permute-done((bf16[10,64,128]{2,1,0:T(8,128)(2,1)S(1)}, bf16[10,64,128]{2,1,0:T(8,128)(2,1)S(1)}, u32[]{:S(2)}, u32[]{:S(2)}) %collective-permute-start.5) | collective-permute-done | bytes 163872 | tf_op jit(solution)/shard_map/ppermute | solution.py:330
  39.6 1.0 %shard_map.88 = (bf16[2,64,128]{2,1,0:T(8,128)(2,1)S(1)}, bf16[2,64,128]{2,1,0:T(8,128)(2,1)S(1)}, bf16[2,64,128]{2,1,0:T(8,128)(2,1)S(1)}, bf16[2,64,128]{2,1,0:T(8,128)(2,1)S(1)}) custom-call(s32[2]{0:T(128)S(1)} %pad_add_fusion.where, bf16[10,64,128]{2,1,0:T(8,128)(2,1)S(1)} %get-tuple-element.42.rest_0_.rest_4_, ...), custom_call_target="tpu_custom_call" | custom-call | flops 134217728 | bytes 1179648 | tf_op jit(solution)/shard_map/pallas_call | solution.py:239
  40.6 4.1 %collective-permute-start.7 = (bf16[2,64,128]{2,1,0:T(8,128)(2,1)S(1)}, bf16[2,64,128]{2,1,0:T(8,128)(2,1)S(1)}, u32[]{:S(2)}, u32[]{:S(2)}) collective-permute-start(bf16[2,64,128]{2,1,0:T(8,128)(2,1)S(1)} %get-tuple-element.51), channel_id=1, source_target_pairs={{0,3},{1,0},{2,1},{3,2},{4,7},{5,4},{6,5},{7,6},{8,11},{9,8},{10,9... | collective-permute-start | bytes 98312 | tf_op jit(solution)/shard_map/ppermute | solution.py:330
  44.7 1.2 %collective-permute-start.8 = (bf16[2,64,128]{2,1,0:T(8,128)(2,1)S(1)}, bf16[2,64,128]{2,1,0:T(8,128)(2,1)S(1)}, u32[]{:S(2)}, u32[]{:S(2)}) collective-permute-start(bf16[2,64,128]{2,1,0:T(8,128)(2,1)S(1)} %get-tuple-element.52), channel_id=1, source_target_pairs={{0,2},{1,3},{2,0},{3,1},{4,6},{5,7},{6,4},{7,5},{8,10},{9,11},{10,... | collective-permute-start | bytes 98312 | tf_op jit(solution)/shard_map/ppermute | solution.py:330
  46.5 2.4 %collective-permute-start.9 = (bf16[2,64,128]{2,1,0:T(8,128)(2,1)S(1)}, bf16[2,64,128]{2,1,0:T(8,128)(2,1)S(1)}, u32[]{:S(2)}, u32[]{:S(2)}) collective-permute-start(bf16[2,64,128]{2,1,0:T(8,128)(2,1)S(1)} %get-tuple-element.53), channel_id=1, source_target_pairs={{0,1},{1,2},{2,3},{3,0},{4,5},{5,6},{6,7},{7,4},{8,9},{9,10},{10,1... | collective-permute-start | bytes 98312 | tf_op jit(solution)/shard_map/ppermute | solution.py:330
  49.6 3.1 %collective-permute-done.9 = bf16[2,64,128]{2,1,0:T(8,128)(2,1)S(1)} collective-permute-done((bf16[2,64,128]{2,1,0:T(8,128)(2,1)S(1)}, bf16[2,64,128]{2,1,0:T(8,128)(2,1)S(1)}, u32[]{:S(2)}, u32[]{:S(2)}) %collective-permute-start.9) | collective-permute-done | bytes 32800 | tf_op jit(solution)/shard_map/ppermute | solution.py:330
  52.7 0.8 shard_map.89
  53.7 2.4 %collective-permute-start.14 = (bf16[8,64,128]{2,1,0:T(8,128)(2,1)S(1)}, bf16[8,64,128]{2,1,0:T(8,128)(2,1)S(1)}, u32[]{:S(2)}, u32[]{:S(2)}) collective-permute-start(bf16[8,64,128]{2,1,0:T(8,128)(2,1)S(1)} %get-tuple-element.59), channel_id=1, source_target_pairs={{0,2},{1,3},{2,0},{3,1},{4,6},{5,7},{6,4},{7,5},{8,10},{9,11},{10,... | collective-permute-start | bytes 393224 | tf_op jit(solution)/shard_map/ppermute | solution.py:330
  56.2 1.2 %collective-permute-start.15 = (bf16[8,64,128]{2,1,0:T(8,128)(2,1)S(1)}, bf16[8,64,128]{2,1,0:T(8,128)(2,1)S(1)}, u32[]{:S(2)}, u32[]{:S(2)}) collective-permute-start(bf16[8,64,128]{2,1,0:T(8,128)(2,1)S(1)} %get-tuple-element.60), channel_id=1, source_target_pairs={{0,3},{1,0},{2,1},{3,2},{4,7},{5,4},{6,5},{7,6},{8,11},{9,8},{10,9... | collective-permute-start | bytes 393224 | tf_op jit(solution)/shard_map/ppermute | solution.py:330
  57.4 1.3 %collective-permute-done.19 = f32[2,64,128]{2,1,0:T(8,128)S(1)} collective-permute-done((f32[2,64,128]{2,1,0:T(8,128)S(1)}, f32[2,64,128]{2,1,0:T(8,128)S(1)}, u32[]{:S(2)}, u32[]{:S(2)}) %collective-permute-start.19) | collective-permute-done | bytes 65568 | tf_op jit(solution)/shard_map/ppermute | solution.py:372
  58.7 1.1 %collective-permute-start.22 = (f32[2,64,128]{2,1,0:T(8,128)S(1)}, f32[2,64,128]{2,1,0:T(8,128)S(1)}, u32[]{:S(2)}, u32[]{:S(2)}) collective-permute-start(f32[2,64,128]{2,1,0:T(8,128)S(1)} %add.52), channel_id=1, source_target_pairs={{0,24},{4,28},{8,16},{12,20},{16,8},{20,12},{24,0},{28,4},{1,25},{... | collective-permute-start | bytes 196616 | tf_op jit(solution)/shard_map/ppermute | solution.py:374
  59.8 2.8 %collective-permute-start.21 = (f32[2,64,128]{2,1,0:T(8,128)S(1)}, f32[2,64,128]{2,1,0:T(8,128)S(1)}, u32[]{:S(2)}, u32[]{:S(2)}) collective-permute-start(f32[2,64,128]{2,1,0:T(8,128)S(1)} %add.52), channel_id=1, source_target_pairs={{0,16},{4,20},{8,24},{12,28},{16,0},{20,4},{24,8},{28,12},{1,17},{... | collective-permute-start | bytes 196616 | tf_op jit(solution)/shard_map/ppermute | solution.py:374
  62.6 1.4 %collective-permute-start.20 = (f32[2,64,128]{2,1,0:T(8,128)S(1)}, f32[2,64,128]{2,1,0:T(8,128)S(1)}, u32[]{:S(2)}, u32[]{:S(2)}) collective-permute-start(f32[2,64,128]{2,1,0:T(8,128)S(1)} %add.52), channel_id=1, source_target_pairs={{0,8},{4,12},{8,0},{12,4},{16,24},{20,28},{24,16},{28,20},{1,9},{5... | collective-permute-start | bytes 196616 | tf_op jit(solution)/shard_map/ppermute | solution.py:374
  64.0 2.6 %collective-permute-done.14.rest_2_ = bf16[8,64,128]{2,1,0:T(8,128)(2,1)S(1)} collective-permute-done((bf16[8,64,128]{2,1,0:T(8,128)(2,1)S(1)}, bf16[8,64,128]{2,1,0:T(8,128)(2,1)S(1)}, u32[]{:S(2)}, u32[]{:S(2)}) %collective-permute-start.14) | collective-permute-done | bytes 131104 | tf_op jit(solution)/shard_map/ppermute | solution.py:330
  66.6 1.0 %shard_map.90 = (bf16[8,64,128]{2,1,0:T(8,128)(2,1)S(1)}, bf16[8,64,128]{2,1,0:T(8,128)(2,1)S(1)}, bf16[8,64,128]{2,1,0:T(8,128)(2,1)S(1)}, bf16[8,64,128]{2,1,0:T(8,128)(2,1)S(1)}) custom-call(s32[2]{0:T(128)S(1)} %pad_add_fusion.where, bf16[8,64,128]{2,1,0:T(8,128)(2,1)S(1)} %get-tuple-element.57.rest_0_, ...), custom_call_target="tpu_custom_call" | custom-call | flops 134217728 | bytes 1048576 | tf_op jit(solution)/shard_map/pallas_call | solution.py:202
  67.6 2.5 %collective-permute-start.16 = (bf16[8,64,128]{2,1,0:T(8,128)(2,1)S(1)}, bf16[8,64,128]{2,1,0:T(8,128)(2,1)S(1)}, u32[]{:S(2)}, u32[]{:S(2)}) collective-permute-start(bf16[8,64,128]{2,1,0:T(8,128)(2,1)S(1)} %get-tuple-element.62), channel_id=1, source_target_pairs={{0,1},{1,2},{2,3},{3,0},{4,5},{5,6},{6,7},{7,4},{8,9},{9,10},{10,1... | collective-permute-start | bytes 393224 | tf_op jit(solution)/shard_map/ppermute | solution.py:330
  70.6 2.0 %collective-permute-start.18 = (bf16[8,64,128]{2,1,0:T(8,128)(2,1)S(1)}, bf16[8,64,128]{2,1,0:T(8,128)(2,1)S(1)}, u32[]{:S(2)}, u32[]{:S(2)}) collective-permute-start(bf16[8,64,128]{2,1,0:T(8,128)(2,1)S(1)} %get-tuple-element.64), channel_id=1, source_target_pairs={{0,3},{1,0},{2,1},{3,2},{4,7},{5,4},{6,5},{7,6},{8,11},{9,8},{10,9... | collective-permute-start | bytes 393224 | tf_op jit(solution)/shard_map/ppermute | solution.py:330
  73.2 2.6 %collective-permute-done.16.rest_1_ = bf16[8,64,128]{2,1,0:T(8,128)(2,1)S(1)} collective-permute-done((bf16[8,64,128]{2,1,0:T(8,128)(2,1)S(1)}, bf16[8,64,128]{2,1,0:T(8,128)(2,1)S(1)}, u32[]{:S(2)}, u32[]{:S(2)}) %collective-permute-start.16) | collective-permute-done | bytes 131104 | tf_op jit(solution)/shard_map/ppermute | solution.py:330
  75.9 3.6 %collective-permute-done.17.rest_2_ = bf16[8,64,128]{2,1,0:T(8,128)(2,1)S(1)} collective-permute-done((bf16[8,64,128]{2,1,0:T(8,128)(2,1)S(1)}, bf16[8,64,128]{2,1,0:T(8,128)(2,1)S(1)}, u32[]{:S(2)}, u32[]{:S(2)}) %collective-permute-start.17) | collective-permute-done | bytes 131104 | tf_op jit(solution)/shard_map/ppermute | solution.py:330
  79.5 1.4 %shard_map.91 = bf16[32,64,128]{2,1,0:T(8,128)(2,1)} custom-call(s32[2]{0:T(128)S(1)} %pad_add_fusion.where, bf16[8,64,128]{2,1,0:T(8,128)(2,1)S(1)} %get-tuple-element.61.rest_0_, bf16[8,64,128]{2,1,0:T(8,128)(2,1)S(1)} %collective-permute-done.16.rest_1_, bf16[8,64,128]{2,1,0:T(8,128)(2,1)S(1)} %collective-permute-done.17.rest_2_, ...), custom_call_target="tpu_custom_call" | custom-call | bytes 33554432 | tf_op jit(solution)/shard_map/pallas_call | solution.py:315
  (28 shorter events, 3.3 us)
Async XLA Ops:
  1.8 18.5 %collective-permute-start.2 = (bf16[8,64,128]{2,1,0:T(8,128)(2,1)S(1)}, bf16[8,64,128]{2,1,0:T(8,128)(2,1)S(1)}, u32[]{:S(2)}, u32[]{:S(2)}) collective-permute-start(bf16[8,64,128]{2,1,0:T(8,128)(2,1)S(1)} %get-tuple-element.66), channel_id=1, source_target_pairs={{0,3},{1,0},{2,1},{3,2},{4,7},{5,4},{6,5},{7,6},{8,11},{9,8},{10,9... | collective-permute-start | bytes 393224 | tf_op jit(solution)/shard_map/ppermute | solution.py:330
  6.9 13.4 %collective-permute-start = (bf16[8,64,128]{2,1,0:T(8,128)(2,1)S(1)}, bf16[8,64,128]{2,1,0:T(8,128)(2,1)S(1)}, u32[]{:S(2)}, u32[]{:S(2)}) collective-permute-start(bf16[8,64,128]{2,1,0:T(8,128)(2,1)S(1)} %get-tuple-element.67), channel_id=1, source_target_pairs={{0,1},{1,2},{2,3},{3,0},{4,5},{5,6},{6,7},{7,4},{8,9},{9,10},{10,1... | collective-permute-start | bytes 393224 | tf_op jit(solution)/shard_map/ppermute | solution.py:330
  6.9 13.4 %collective-permute-start.1 = (bf16[8,64,128]{2,1,0:T(8,128)(2,1)S(1)}, bf16[8,64,128]{2,1,0:T(8,128)(2,1)S(1)}, u32[]{:S(2)}, u32[]{:S(2)}) collective-permute-start(bf16[8,64,128]{2,1,0:T(8,128)(2,1)S(1)} %get-tuple-element.69), channel_id=1, source_target_pairs={{0,2},{1,3},{2,0},{3,1},{4,6},{5,7},{6,4},{7,5},{8,10},{9,11},{10,... | collective-permute-start | bytes 393224 | tf_op jit(solution)/shard_map/ppermute | solution.py:330
  9.4 0.8 copy-start
  20.3 2.0 %collective-permute-start.3 = (bf16[32,64,128]{2,1,0:T(8,128)(2,1)S(1)}, bf16[32,64,128]{2,1,0:T(8,128)(2,1)S(1)}, u32[]{:S(2)}, u32[]{:S(2)}) collective-permute-start(bf16[32,64,128]{2,1,0:T(8,128)(2,1)S(1)} %get-tuple-element.41), channel_id=1, source_target_pairs={{0,4},{4,0},{8,12},{12,8},{16,20},{20,16},{24,28},{28,24},{1,5},{5... | collective-permute-start | bytes 1572872 | tf_op jit(solution)/shard_map/ppermute | solution.py:355
  22.6 8.1 %collective-permute-start.4 = (bf16[10,64,128]{2,1,0:T(8,128)(2,1)S(1)}, bf16[10,64,128]{2,1,0:T(8,128)(2,1)S(1)}, u32[]{:S(2)}, u32[]{:S(2)}) collective-permute-start(bf16[10,64,128]{2,1,0:T(8,128)(2,1)S(1)} %get-tuple-element.43), channel_id=1, source_target_pairs={{0,1},{1,2},{2,3},{3,0},{4,5},{5,6},{6,7},{7,4},{8,9},{9,10},{10,1... | collective-permute-start | bytes 491528 | tf_op jit(solution)/shard_map/ppermute | solution.py:330
  26.0 26.7 %collective-permute-start.10 = (bf16[32,64,128]{2,1,0:T(8,128)(2,1)S(1)}, bf16[32,64,128]{2,1,0:T(8,128)(2,1)S(1)}, u32[]{:S(2)}, u32[]{:S(2)}) collective-permute-start(bf16[32,64,128]{2,1,0:T(8,128)(2,1)S(1)} %get-tuple-element.55), channel_id=1, source_target_pairs={{0,4},{4,0},{8,12},{12,8},{16,20},{20,16},{24,28},{28,24},{1,5},{5... | collective-permute-start | bytes 1572872 | tf_op jit(solution)/shard_map/ppermute | solution.py:359
  26.0 26.7 %collective-permute-start.12 = (bf16[32,64,128]{2,1,0:T(8,128)(2,1)S(1)}, bf16[32,64,128]{2,1,0:T(8,128)(2,1)S(1)}, u32[]{:S(2)}, u32[]{:S(2)}) collective-permute-start(bf16[32,64,128]{2,1,0:T(8,128)(2,1)S(1)} %get-tuple-element.56), channel_id=1, source_target_pairs={{0,24},{4,12},{8,0},{12,20},{16,8},{20,28},{24,16},{28,4},{1,25},{... | collective-permute-start | bytes 1572872 | tf_op jit(solution)/shard_map/ppermute | solution.py:356
  27.6 25.2 %collective-permute-start.11 = (bf16[32,64,128]{2,1,0:T(8,128)(2,1)S(1)}, bf16[32,64,128]{2,1,0:T(8,128)(2,1)S(1)}, u32[]{:S(2)}, u32[]{:S(2)}) collective-permute-start(bf16[32,64,128]{2,1,0:T(8,128)(2,1)S(1)} %shard_map.87), channel_id=1, source_target_pairs={{0,28},{4,8},{8,4},{12,16},{16,12},{20,24},{24,20},{28,0},{1,29},{... | collective-permute-start | bytes 1572872 | tf_op jit(solution)/shard_map/ppermute | solution.py:358
  28.8 10.6 %collective-permute-start.5 = (bf16[10,64,128]{2,1,0:T(8,128)(2,1)S(1)}, bf16[10,64,128]{2,1,0:T(8,128)(2,1)S(1)}, u32[]{:S(2)}, u32[]{:S(2)}) collective-permute-start(bf16[10,64,128]{2,1,0:T(8,128)(2,1)S(1)} %get-tuple-element.44), channel_id=1, source_target_pairs={{0,2},{1,3},{2,0},{3,1},{4,6},{5,7},{6,4},{7,5},{8,10},{9,11},{10,... | collective-permute-start | bytes 491528 | tf_op jit(solution)/shard_map/ppermute | solution.py:330
  30.7 8.9 %collective-permute-start.6 = (bf16[10,64,128]{2,1,0:T(8,128)(2,1)S(1)}, bf16[10,64,128]{2,1,0:T(8,128)(2,1)S(1)}, u32[]{:S(2)}, u32[]{:S(2)}) collective-permute-start(bf16[10,64,128]{2,1,0:T(8,128)(2,1)S(1)} %get-tuple-element.45), channel_id=1, source_target_pairs={{0,3},{1,0},{2,1},{3,2},{4,7},{5,4},{6,5},{7,6},{8,11},{9,8},{10,9... | collective-permute-start | bytes 491528 | tf_op jit(solution)/shard_map/ppermute | solution.py:330
  40.6 5.9 %collective-permute-start.7 = (bf16[2,64,128]{2,1,0:T(8,128)(2,1)S(1)}, bf16[2,64,128]{2,1,0:T(8,128)(2,1)S(1)}, u32[]{:S(2)}, u32[]{:S(2)}) collective-permute-start(bf16[2,64,128]{2,1,0:T(8,128)(2,1)S(1)} %get-tuple-element.51), channel_id=1, source_target_pairs={{0,3},{1,0},{2,1},{3,2},{4,7},{5,4},{6,5},{7,6},{8,11},{9,8},{10,9... | collective-permute-start | bytes 98312 | tf_op jit(solution)/shard_map/ppermute | solution.py:330
  44.7 4.8 %collective-permute-start.8 = (bf16[2,64,128]{2,1,0:T(8,128)(2,1)S(1)}, bf16[2,64,128]{2,1,0:T(8,128)(2,1)S(1)}, u32[]{:S(2)}, u32[]{:S(2)}) collective-permute-start(bf16[2,64,128]{2,1,0:T(8,128)(2,1)S(1)} %get-tuple-element.52), channel_id=1, source_target_pairs={{0,2},{1,3},{2,0},{3,1},{4,6},{5,7},{6,4},{7,5},{8,10},{9,11},{10,... | collective-permute-start | bytes 98312 | tf_op jit(solution)/shard_map/ppermute | solution.py:330
  46.5 6.2 %collective-permute-start.9 = (bf16[2,64,128]{2,1,0:T(8,128)(2,1)S(1)}, bf16[2,64,128]{2,1,0:T(8,128)(2,1)S(1)}, u32[]{:S(2)}, u32[]{:S(2)}) collective-permute-start(bf16[2,64,128]{2,1,0:T(8,128)(2,1)S(1)} %get-tuple-element.53), channel_id=1, source_target_pairs={{0,1},{1,2},{2,3},{3,0},{4,5},{5,6},{6,7},{7,4},{8,9},{9,10},{10,1... | collective-permute-start | bytes 98312 | tf_op jit(solution)/shard_map/ppermute | solution.py:330
  53.5 9.1 %collective-permute-start.13 = (bf16[8,64,128]{2,1,0:T(8,128)(2,1)S(1)}, bf16[8,64,128]{2,1,0:T(8,128)(2,1)S(1)}, u32[]{:S(2)}, u32[]{:S(2)}) collective-permute-start(bf16[8,64,128]{2,1,0:T(8,128)(2,1)S(1)} %get-tuple-element.58), channel_id=1, source_target_pairs={{0,1},{1,2},{2,3},{3,0},{4,5},{5,6},{6,7},{7,4},{8,9},{9,10},{10,1... | collective-permute-start | bytes 393224 | tf_op jit(solution)/shard_map/ppermute | solution.py:330
  53.7 12.9 %collective-permute-start.14 = (bf16[8,64,128]{2,1,0:T(8,128)(2,1)S(1)}, bf16[8,64,128]{2,1,0:T(8,128)(2,1)S(1)}, u32[]{:S(2)}, u32[]{:S(2)}) collective-permute-start(bf16[8,64,128]{2,1,0:T(8,128)(2,1)S(1)} %get-tuple-element.59), channel_id=1, source_target_pairs={{0,2},{1,3},{2,0},{3,1},{4,6},{5,7},{6,4},{7,5},{8,10},{9,11},{10,... | collective-permute-start | bytes 393224 | tf_op jit(solution)/shard_map/ppermute | solution.py:330
  56.2 10.4 %collective-permute-start.15 = (bf16[8,64,128]{2,1,0:T(8,128)(2,1)S(1)}, bf16[8,64,128]{2,1,0:T(8,128)(2,1)S(1)}, u32[]{:S(2)}, u32[]{:S(2)}) collective-permute-start(bf16[8,64,128]{2,1,0:T(8,128)(2,1)S(1)} %get-tuple-element.60), channel_id=1, source_target_pairs={{0,3},{1,0},{2,1},{3,2},{4,7},{5,4},{6,5},{7,6},{8,11},{9,8},{10,9... | collective-permute-start | bytes 393224 | tf_op jit(solution)/shard_map/ppermute | solution.py:330
  57.4 1.3 %collective-permute-start.19 = (f32[2,64,128]{2,1,0:T(8,128)S(1)}, f32[2,64,128]{2,1,0:T(8,128)S(1)}, u32[]{:S(2)}, u32[]{:S(2)}) collective-permute-start(f32[2,64,128]{2,1,0:T(8,128)S(1)} %convert_add_fusion), channel_id=1, source_target_pairs={{0,4},{4,0},{8,12},{12,8},{16,20},{20,16},{24,28},{28,24},{1,5},{5... | collective-permute-start | bytes 196616 | tf_op jit(solution)/shard_map/ppermute | solution.py:372
  58.7 11.9 %collective-permute-start.22 = (f32[2,64,128]{2,1,0:T(8,128)S(1)}, f32[2,64,128]{2,1,0:T(8,128)S(1)}, u32[]{:S(2)}, u32[]{:S(2)}) collective-permute-start(f32[2,64,128]{2,1,0:T(8,128)S(1)} %add.52), channel_id=1, source_target_pairs={{0,24},{4,28},{8,16},{12,20},{16,8},{20,12},{24,0},{28,4},{1,25},{... | collective-permute-start | bytes 196616 | tf_op jit(solution)/shard_map/ppermute | solution.py:374
  59.8 12.8 %collective-permute-start.21 = (f32[2,64,128]{2,1,0:T(8,128)S(1)}, f32[2,64,128]{2,1,0:T(8,128)S(1)}, u32[]{:S(2)}, u32[]{:S(2)}) collective-permute-start(f32[2,64,128]{2,1,0:T(8,128)S(1)} %add.52), channel_id=1, source_target_pairs={{0,16},{4,20},{8,24},{12,28},{16,0},{20,4},{24,8},{28,12},{1,17},{... | collective-permute-start | bytes 196616 | tf_op jit(solution)/shard_map/ppermute | solution.py:374
  62.6 10.0 %collective-permute-start.20 = (f32[2,64,128]{2,1,0:T(8,128)S(1)}, f32[2,64,128]{2,1,0:T(8,128)S(1)}, u32[]{:S(2)}, u32[]{:S(2)}) collective-permute-start(f32[2,64,128]{2,1,0:T(8,128)S(1)} %add.52), channel_id=1, source_target_pairs={{0,8},{4,12},{8,0},{12,4},{16,24},{20,28},{24,16},{28,20},{1,9},{5... | collective-permute-start | bytes 196616 | tf_op jit(solution)/shard_map/ppermute | solution.py:374
  67.6 8.3 %collective-permute-start.16 = (bf16[8,64,128]{2,1,0:T(8,128)(2,1)S(1)}, bf16[8,64,128]{2,1,0:T(8,128)(2,1)S(1)}, u32[]{:S(2)}, u32[]{:S(2)}) collective-permute-start(bf16[8,64,128]{2,1,0:T(8,128)(2,1)S(1)} %get-tuple-element.62), channel_id=1, source_target_pairs={{0,1},{1,2},{2,3},{3,0},{4,5},{5,6},{6,7},{7,4},{8,9},{9,10},{10,1... | collective-permute-start | bytes 393224 | tf_op jit(solution)/shard_map/ppermute | solution.py:330
  70.1 9.3 %collective-permute-start.17 = (bf16[8,64,128]{2,1,0:T(8,128)(2,1)S(1)}, bf16[8,64,128]{2,1,0:T(8,128)(2,1)S(1)}, u32[]{:S(2)}, u32[]{:S(2)}) collective-permute-start(bf16[8,64,128]{2,1,0:T(8,128)(2,1)S(1)} %get-tuple-element.63), channel_id=1, source_target_pairs={{0,2},{1,3},{2,0},{3,1},{4,6},{5,7},{6,4},{7,5},{8,10},{9,11},{10,... | collective-permute-start | bytes 393224 | tf_op jit(solution)/shard_map/ppermute | solution.py:330
  70.6 8.8 %collective-permute-start.18 = (bf16[8,64,128]{2,1,0:T(8,128)(2,1)S(1)}, bf16[8,64,128]{2,1,0:T(8,128)(2,1)S(1)}, u32[]{:S(2)}, u32[]{:S(2)}) collective-permute-start(bf16[8,64,128]{2,1,0:T(8,128)(2,1)S(1)} %get-tuple-element.64), channel_id=1, source_target_pairs={{0,3},{1,0},{2,1},{3,2},{4,7},{5,4},{6,5},{7,6},{8,11},{9,8},{10,9... | collective-permute-start | bytes 393224 | tf_op jit(solution)/shard_map/ppermute | solution.py:330

commit v9 on v8

--- a/solution.py
+++ b/solution.py
@@ -11,7 +11,6 @@
 REACH = 2
 GROUP = 4
 STEP = 4
-RING = 10
 BF16 = jnp.bfloat16
 F32 = jnp.float32
 MIB = 1 << 20
@@ -40,24 +39,38 @@
 
 
 def tiles_kernel(slabs, reps, where, cols, live, weight, cot, mask, tiles, *rest):
-    outs, packed, rest = rest[:5], rest[5 : 5 + reps], rest[5 + reps :]
-    cot_in, mask_in, z, ring, first, second, rows, left, sems, z_sems = rest
+    outs, packed, rest = rest[:4], rest[4 : 4 + reps], rest[4 + reps :]
+    outs = [outs[0].at[pl.ds(0, cols.shape[1])], outs[0].at[pl.ds(cols.shape[1], cols.shape[1])], *outs[1:]]
+    cot_in, mask_in, weight_in, z, held, first, second, rows, left, sems, z_sems = rest
     totals = (first, second)
-    blocks, slots = cols.shape
+    slots, blocks = cols.shape
     per_row = slots // GROUP
     window = (2 * REACH + 1) * blocks
     copies = [
         pltpu.make_async_copy(cot, cot_in, z_sems.at[0]),
         pltpu.make_async_copy(mask, mask_in, z_sems.at[1]),
+        pltpu.make_async_copy(weight, weight_in, z_sems.at[2]),
     ]
     for copy in copies:
         copy.start()
 
+    def groups_of(b):
+        return lax.shift_right_logical(live[b] + GROUP - 1, GROUP.bit_length() - 1)
+
+    def fetched(b, act):
+        groups = groups_of(b)
+        for g in range(1, per_row + 1):
+
+            @pl.when(groups == g)
+            def _(span=pl.ds(b * slots, g * GROUP)):
+                act(pltpu.make_async_copy(tiles.at[span], held.at[span], sems.at[b]))
+
     def list_row(b, count):
+        fetched(b, lambda copy: copy.start())
         for g in range(per_row):
             rows[count + g] = b * per_row + g
             left[count + g] = live[b] - g * GROUP
-        return count + lax.shift_right_logical(live[b] + GROUP - 1, GROUP.bit_length() - 1)
+        return count + groups_of(b)
 
     count = lax.fori_loop(0, blocks, list_row, jnp.int32(0))
     for u in range(STEP):
@@ -65,16 +78,9 @@
         left[count + u] = 0
     steps = lax.div(count + STEP - 1, STEP)
 
-    def fetch(i):
-        slot = lax.rem(i, RING)
-        for u in range(STEP):
-            start = rows[i * STEP + u] * GROUP
-            pltpu.make_async_copy(
-                tiles.at[pl.ds(start, GROUP)], ring.at[slot, pl.ds(u * GROUP, GROUP)], sems.at[slot]
-            ).start()
-
-    for i in range(RING - 1):
-        pl.when(i < steps)(functools.partial(fetch, jnp.int32(i)))
+    def wait_row(b, carry):
+        fetched(b, lambda copy: copy.wait())
+        return carry
 
     def clear(i, carry):
         for total in totals:
@@ -95,28 +101,27 @@
     for s in range(reps):
         packed[s][:share] = z[pl.ds(wrap(where[1] + s, reps) * share, share)]
         for h in range(weight.shape[1] // nodes):
-            packed[s][share + h] = weight[:, h * nodes : (h + 1) * nodes]
+            packed[s][share + h] = weight_in[:, h * nodes : (h + 1) * nodes]
     shift = REACH * blocks - where[0] * blocks
 
-    def step(i, carry):
-        slot = lax.rem(i, RING)
-        pltpu.make_async_copy(
-            tiles.at[pl.ds(0, STEP * GROUP)], ring.at[slot], sems.at[slot]
-        ).wait()
-        pl.when(i + RING - 1 < steps)(functools.partial(fetch, i + RING - 1))
+    def step(i, ready):
+        entries = [rows[i * STEP + u] for u in range(STEP)]
+        need = lax.div(functools.reduce(jnp.maximum, entries), per_row) + 1
+        lax.fori_loop(ready, need, wait_row, 0)
         for u in range(STEP):
-            row, remain = rows[i * STEP + u], left[i * STEP + u]
+            row, remain = entries[u], left[i * STEP + u]
             b, g = lax.div(row, per_row), lax.rem(row, per_row)
             z_row = z[b]
             for j in range(GROUP):
-                place = wrap(cols[b, g * GROUP + j] + shift, slabs * blocks)
+                place = wrap(cols[g * GROUP + j, b] + shift, slabs * blocks)
                 place = jnp.where(j < remain, place, window)
                 totals[j % 2][place] += jnp.dot(
-                    z_row, ring[slot, u * GROUP + j], preferred_element_type=F32
+                    z_row, held[row * GROUP + j], preferred_element_type=F32
                 )
-        return carry
-
-    lax.fori_loop(0, steps, step, 0)
+        return jnp.maximum(ready, need)
+
+    ready = lax.fori_loop(0, steps, step, jnp.int32(0))
+    lax.fori_loop(ready, blocks, wait_row, 0)
     sign = 2 * lax.rem(where[0], 2) - 1
     for order, out in enumerate(outs):
         base = ((order - REACH) * sign + REACH) * blocks
@@ -137,25 +142,27 @@
     lists = blocks * (slots // GROUP) + slots // GROUP + STEP
     total = pltpu.VMEM((window + 1, features, nodes), F32)
     packs = blocks // reps + weight.shape[1] // nodes
+    counts = [2 * blocks, blocks, blocks, blocks]
     return pl.pallas_call(
         functools.partial(tiles_kernel, slabs, reps),
-        out_shape=[jax.ShapeDtypeStruct(cot.shape, BF16)] * 5
+        out_shape=[jax.ShapeDtypeStruct((count, features, nodes), BF16) for count in counts]
         + [jax.ShapeDtypeStruct((packs, features, nodes), BF16)] * reps,
-        in_specs=[smem(), smem(), smem(), vmem(), hbm(), hbm(), hbm()],
-        out_specs=[vmem()] * (5 + reps),
+        in_specs=[smem()] * 3 + [hbm()] * 4,
+        out_specs=[vmem()] * (len(counts) + reps),
         scratch_shapes=[
             pltpu.VMEM(cot.shape, BF16),
             pltpu.VMEM(mask.shape, jnp.int32),
+            pltpu.VMEM(weight.shape, BF16),
             pltpu.VMEM(cot.shape, BF16),
-            pltpu.VMEM((RING, STEP * GROUP, nodes, nodes), BF16),
+            pltpu.VMEM((blocks * slots, nodes, nodes), BF16),
             total,
             total,
             pltpu.SMEM((lists,), jnp.int32),
             pltpu.SMEM((lists,), jnp.int32),
-            pltpu.SemaphoreType.DMA((RING,)),
-            pltpu.SemaphoreType.DMA((2,)),
+            pltpu.SemaphoreType.DMA((blocks,)),
+            pltpu.SemaphoreType.DMA((3,)),
         ],
-        compiler_params=pltpu.CompilerParams(vmem_limit_bytes=26 * MIB),
+        compiler_params=pltpu.CompilerParams(vmem_limit_bytes=36 * MIB),
         cost_estimate=pl.CostEstimate(
             flops=2 * blocks * slots * features * nodes * nodes,
             bytes_accessed=tiles.size * 2,
@@ -163,9 +170,9 @@
         ),
     )(
         where,
-        in_hbm(cols),
+        in_hbm(cols.T),
         in_hbm(live),
-        weight,
+        in_hbm(weight),
         in_hbm(cot),
         in_hbm(mask),
         in_hbm(tiles.reshape(blocks * slots, nodes, nodes)),
@@ -272,8 +279,9 @@
     )(one, other)
 
 
-def total_kernel(reps, where, *rest):
+def total_kernel(reps, where, aside, *rest):
     terms, outs = rest[:-reps], rest[-reps:]
+    terms = (aside.at[pl.ds(terms[0].shape[0], terms[0].shape[0])], *terms)
     share = outs[0].shape[0]
     for s, out in enumerate(outs):
         first = wrap(where[1] + s, reps) * share
@@ -284,18 +292,18 @@
             out[i] = total.astype(BF16)
 
 
-def total_shares(where, terms, reps):
+def total_shares(where, aside, terms, reps):
     blocks, features, nodes = terms[0].shape
     return pl.pallas_call(
         functools.partial(total_kernel, reps),
         out_shape=[jax.ShapeDtypeStruct((blocks // reps, features, nodes), BF16)] * reps,
-        in_specs=[smem()] + [vmem()] * len(terms),
+        in_specs=[smem()] + [vmem()] * (1 + len(terms)),
         out_specs=[vmem()] * reps,
         compiler_params=pltpu.CompilerParams(vmem_limit_bytes=2 * MIB),
         cost_estimate=pl.CostEstimate(
             flops=4 * terms[0].size, bytes_accessed=10 * terms[0].size, transcendentals=0
         ),
-    )(where, *terms)
+    )(where, aside, *terms)
 
 
 def lay_kernel(reps, where, *rest):
@@ -348,27 +356,26 @@
     to_one = [(i, (i + (1 if i % 2 else -1)) % slabs) for i in range(slabs)]
     to_two = [(i, (i + (2 if i % 2 else -2)) % slabs) for i in range(slabs)]
     aggs = [shift(node_share(aggregated, s), s) for s in range(reps)]
-    near, beside, own, one, two, *packed = contributions(
+    aside, own, one, two, *packed = contributions(
         where, col_block, live_count, weight, cotangent, relu_mask, tiles, slabs, reps
     )
-    near, aggs = lax.optimization_barrier((near, aggs))
-    near_in = lax.ppermute(near, "blk", pair)
+    aside, aggs = lax.optimization_barrier((aside, aggs))
+    aside = lax.ppermute(aside, "blk", pair)
     two_in = lax.ppermute(two, "blk", to_two)
-    one = add(one, near_in)
+    one = add(one, aside)
     one_in = lax.ppermute(one, "blk", to_one)
-    beside_in = lax.ppermute(beside, "blk", pair)
 
     packed, _ = lax.optimization_barrier((packed, one))
     packed = [shift(value, s) for s, value in enumerate(packed)]
     grad_w = weight_partial(where, packed, aggs)
-    grad_w = sum(shift(part, -s).astype(F32) for s, part in enumerate(grad_w))
 
     own, grad_w = lax.optimization_barrier((own, grad_w))
-    shares = total_shares(where, [own, beside_in, one_in, two_in], reps)
+    shares = total_shares(where, aside, [own, one_in, two_in], reps)
     shares = [shift(value, s) for s, value in enumerate(shares)]
     outs = [shift(value, s) for s, value in enumerate(mix(where, shares, packed, share))]
     input_grad = lay_blocks(where, outs, cotangent.shape)
 
+    grad_w = sum(shift(part, -s).astype(F32) for s, part in enumerate(grad_w))
     grad_w = grad_w + lax.ppermute(grad_w, "blk", pair)
     grad_w = grad_w + sum(
         lax.ppermute(grad_w, "blk", [(i, i ^ step) for i in range(slabs)])

time: 81.1 us -> 74.4 us (0.917)
  waiting for transfers between devices: 26.2 us -> 21.8 us
  local copies, waits for them, and re-layouts: 3.27 us -> 1.14 us
  Pallas kernels: 14.6 us -> 12.8 us
  starting transfers between devices: 35.2 us -> 36.3 us
    ppermute x15, waiting for transfers between devices: 23 us -> 20.3 us  [shift(): lax.ppermute(value, 'rep', [(i, (i + steps) % reps) for i in range(reps)])]
    unnamed x3 -> x0, local copies, waits for them, and re-layouts: 2.13 us -> none
    pallas_call x1, Pallas kernels: 10.2 us -> 8.39 us  [contributions(): pl.pallas_call(functools.partial(tiles_kernel, slabs, reps), out_shape=[j...]
    ppermute x3, starting transfers between devices: 5.3 us -> 3.55 us  [on_device(): lax.ppermute(grad_w, 'blk', [(i, i ^ step) for i in range(slabs)])]
    ppermute x2 -> x1, waiting for transfers between devices: 1.9 us -> 0.21 us  [on_device(): aside = lax.ppermute(aside, 'blk', pair)]
    ppermute x1, starting transfers between devices: 1.18 us -> 2.25 us  [on_device(): one_in = lax.ppermute(one, 'blk', to_one)]
    ppermute x1, starting transfers between devices: 1.57 us -> 2.45 us  [on_device(): two_in = lax.ppermute(two, 'blk', to_two)]
    ppermute x15, starting transfers between devices: 27.1 us -> 28 us  [shift(): lax.ppermute(value, 'rep', [(i, (i + steps) % reps) for i in range(reps)])]
  transfers between devices with their start and end apart: 23 -> 22, of which waited for: 11 -> 9; matrix products, arithmetic and copies ran while one was open for 3% -> 1% of each run, Pallas kernels for 15% -> 16%
where the time goes in v9:
time: 74.4 us; the launch traced here: 73.5 us
  starting transfers between devices  36.3 us (49%)
  waiting for transfers between devices  21.8 us (29%)
  Pallas kernels  12.8 us (17%)
  local copies, waits for them, and re-layouts  1.14 us (2%)
  between operations  0.76 us (1%)
  other arithmetic  0.75 us (1%)
    ppermute x15, starting transfers between devices, shift(): lax.ppermute(value, 'rep', [(i, (i + steps) % reps) for i in range(reps)])  28 us
    ppermute x15, waiting for transfers between devices, shift(): lax.ppermute(value, 'rep', [(i, (i + steps) % reps) for i in range(reps)])  20.3 us
    pallas_call x1, Pallas kernels, contributions(): pl.pallas_call(functools.partial(tiles_kernel, slabs, reps), out_shape=[j...  8.39 us
    ppermute x3, starting transfers between devices, on_device(): lax.ppermute(grad_w, 'blk', [(i, i ^ step) for i in range(slabs)])  3.55 us
    ppermute x1, starting transfers between devices, on_device(): two_in = lax.ppermute(two, 'blk', to_two)  2.45 us
    ppermute x1, starting transfers between devices, on_device(): one_in = lax.ppermute(one, 'blk', to_one)  2.25 us
  transfers between devices with their start and end apart: 22, of which 9 were waited for; matrix products, arithmetic and copies ran while one was open for 1% of the time, Pallas kernels for 16%

profile of v9, /device:TPU:0, one launch (start us, length us, event | category | flops | bytes accessed | tf_op | source)
XLA Modules:
  0.0 73.5 jit_solution(15571191898826364302)
XLA Ops:
  0.7 1.1 %constant_dynamic-slice_fusion = (bf16[8,64,128]{2,1,0:T(8,128)(2,1)S(1)}, bf16[8,64,128]{2,1,0:T(8,128)(2,1)S(1)}, bf16[8,64,128]{2,1,0:T(8,128)(2,1)S(1)}, bf16[8,64,128]{2,1,0:T(8,128)(2,1)S(1)}) fusion(bf16[32,64,128]{2,1,0:T(8,128)(2,1)} %param.9, s32[]{:T(128)S(6)} %select_n.15, s32[]{:T(128)S(6)} %select_n.13, s32[]{:T(128)S(6)} %select_n.12, ...), kind=kLoop, calls=%fused_computation.3 | loop fusion | bytes 1048592 | tf_op jit(solution)/shard_map/dynamic_slice | solution.py:345
  1.8 5.1 %collective-permute-start.2 = (bf16[8,64,128]{2,1,0:T(8,128)(2,1)S(1)}, bf16[8,64,128]{2,1,0:T(8,128)(2,1)S(1)}, u32[]{:S(2)}, u32[]{:S(2)}) collective-permute-start(bf16[8,64,128]{2,1,0:T(8,128)(2,1)S(1)} %get-tuple-element.70), channel_id=1, source_target_pairs={{0,3},{1,0},{2,1},{3,2},{4,7},{5,4},{6,5},{7,6},{8,11},{9,8},{10,9... | collective-permute-start | bytes 393224 | tf_op jit(solution)/shard_map/ppermute | solution.py:338
  6.9 1.0 %collective-permute-start.1 = (bf16[8,64,128]{2,1,0:T(8,128)(2,1)S(1)}, bf16[8,64,128]{2,1,0:T(8,128)(2,1)S(1)}, u32[]{:S(2)}, u32[]{:S(2)}) collective-permute-start(bf16[8,64,128]{2,1,0:T(8,128)(2,1)S(1)} %get-tuple-element.73), channel_id=1, source_target_pairs={{0,2},{1,3},{2,0},{3,1},{4,6},{5,7},{6,4},{7,5},{8,10},{9,11},{10,... | collective-permute-start | bytes 393224 | tf_op jit(solution)/shard_map/ppermute | solution.py:338
  8.0 8.4 %shard_map.86 = (bf16[64,64,128]{2,1,0:T(8,128)(2,1)S(1)}, bf16[32,64,128]{2,1,0:T(8,128)(2,1)S(1)}, bf16[32,64,128]{2,1,0:T(8,128)(2,1)S(1)}, bf16[32,64,128]{2...) custom-call(s32[2]{0:T(128)S(1)} %pad_add_fusion.where, ...), custom_call_target="tpu_custom_call" | custom-call | flops 1073741824 | bytes 16777216 | tf_op jit(solution)/shard_map/pallas_call | solution.py:146
  16.4 2.0 %collective-permute-done.1.rest_6_ = bf16[8,64,128]{2,1,0:T(8,128)(2,1)S(1)} collective-permute-done((bf16[8,64,128]{2,1,0:T(8,128)(2,1)S(1)}, bf16[8,64,128]{2,1,0:T(8,128)(2,1)S(1)}, u32[]{:S(2)}, u32[]{:S(2)}) %collective-permute-start.1) | collective-permute-done | bytes 131104 | tf_op jit(solution)/shard_map/ppermute | solution.py:338
  18.4 2.4 %collective-permute-start.8 = (bf16[32,64,128]{2,1,0:T(8,128)(2,1)S(1)}, bf16[32,64,128]{2,1,0:T(8,128)(2,1)S(1)}, u32[]{:S(2)}, u32[]{:S(2)}) collective-permute-start(bf16[32,64,128]{2,1,0:T(8,128)(2,1)S(1)} %get-tuple-element.57), channel_id=1, source_target_pairs={{0,24},{4,12},{8,0},{12,20},{16,8},{20,28},{24,16},{28,4},{1,25},{... | collective-permute-start | bytes 1572872 | tf_op jit(solution)/shard_map/ppermute | solution.py:364
  21.3 2.3 %collective-permute-start.7 = (bf16[32,64,128]{2,1,0:T(8,128)(2,1)S(1)}, bf16[32,64,128]{2,1,0:T(8,128)(2,1)S(1)}, u32[]{:S(2)}, u32[]{:S(2)}) collective-permute-start(bf16[32,64,128]{2,1,0:T(8,128)(2,1)S(1)} %shard_map.87), channel_id=1, source_target_pairs={{0,28},{4,8},{8,4},{12,16},{16,12},{20,24},{24,20},{28,0},{1,29},{... | collective-permute-start | bytes 1572872 | tf_op jit(solution)/shard_map/ppermute | solution.py:366
  23.5 3.1 %collective-permute-start.4 = (bf16[10,64,128]{2,1,0:T(8,128)(2,1)S(1)}, bf16[10,64,128]{2,1,0:T(8,128)(2,1)S(1)}, u32[]{:S(2)}, u32[]{:S(2)}) collective-permute-start(bf16[10,64,128]{2,1,0:T(8,128)(2,1)S(1)} %get-tuple-element.45), channel_id=1, source_target_pairs={{0,1},{1,2},{2,3},{3,0},{4,5},{5,6},{6,7},{7,4},{8,9},{9,10},{10,1... | collective-permute-start | bytes 491528 | tf_op jit(solution)/shard_map/ppermute | solution.py:338
  26.7 0.3 collective-permute-start.5
  26.9 2.1 %collective-permute-start.6 = (bf16[10,64,128]{2,1,0:T(8,128)(2,1)S(1)}, bf16[10,64,128]{2,1,0:T(8,128)(2,1)S(1)}, u32[]{:S(2)}, u32[]{:S(2)}) collective-permute-start(bf16[10,64,128]{2,1,0:T(8,128)(2,1)S(1)} %get-tuple-element.47), channel_id=1, source_target_pairs={{0,3},{1,0},{2,1},{3,2},{4,7},{5,4},{6,5},{7,6},{8,11},{9,8},{10,9... | collective-permute-start | bytes 491528 | tf_op jit(solution)/shard_map/ppermute | solution.py:338
  29.0 3.6 %collective-permute-done.4.rest_1_.rest_5_ = bf16[10,64,128]{2,1,0:T(8,128)(2,1)S(1)} collective-permute-done((bf16[10,64,128]{2,1,0:T(8,128)(2,1)S(1)}, bf16[10,64,128]{2,1,0:T(8,128)(2,1)S(1)}, u32[]{:S(2)}, u32[]{:S(2)}) %collective-permute-start.4) | collective-permute-done | bytes 163872 | tf_op jit(solution)/shard_map/ppermute | solution.py:338
  32.6 5.4 %collective-permute-done.5.rest_2_.rest_6_ = bf16[10,64,128]{2,1,0:T(8,128)(2,1)S(1)} collective-permute-done((bf16[10,64,128]{2,1,0:T(8,128)(2,1)S(1)}, bf16[10,64,128]{2,1,0:T(8,128)(2,1)S(1)}, u32[]{:S(2)}, u32[]{:S(2)}) %collective-permute-start.5) | collective-permute-done | bytes 163872 | tf_op jit(solution)/shard_map/ppermute | solution.py:338
  38.0 1.0 %shard_map.88 = (bf16[2,64,128]{2,1,0:T(8,128)(2,1)S(1)}, bf16[2,64,128]{2,1,0:T(8,128)(2,1)S(1)}, bf16[2,64,128]{2,1,0:T(8,128)(2,1)S(1)}, bf16[2,64,128]{2,1,0:T(8,128)(2,1)S(1)}) custom-call(s32[2]{0:T(128)S(1)} %pad_add_fusion.where, bf16[10,64,128]{2,1,0:T(8,128)(2,1)S(1)} %get-tuple-element.44.rest_0_.rest_4_, ...), custom_call_target="tpu_custom_call" | custom-call | flops 134217728 | bytes 1179648 | tf_op jit(solution)/shard_map/pallas_call | solution.py:246
  39.0 4.6 %collective-permute-start.15 = (bf16[2,64,128]{2,1,0:T(8,128)(2,1)S(1)}, bf16[2,64,128]{2,1,0:T(8,128)(2,1)S(1)}, u32[]{:S(2)}, u32[]{:S(2)}) collective-permute-start(bf16[2,64,128]{2,1,0:T(8,128)(2,1)S(1)} %get-tuple-element.67), channel_id=1, source_target_pairs={{0,3},{1,0},{2,1},{3,2},{4,7},{5,4},{6,5},{7,6},{8,11},{9,8},{10,9... | collective-permute-start | bytes 98312 | tf_op jit(solution)/shard_map/ppermute | solution.py:338
  43.6 0.9 %collective-permute-start.16 = (bf16[2,64,128]{2,1,0:T(8,128)(2,1)S(1)}, bf16[2,64,128]{2,1,0:T(8,128)(2,1)S(1)}, u32[]{:S(2)}, u32[]{:S(2)}) collective-permute-start(bf16[2,64,128]{2,1,0:T(8,128)(2,1)S(1)} %get-tuple-element.68), channel_id=1, source_target_pairs={{0,2},{1,3},{2,0},{3,1},{4,6},{5,7},{6,4},{7,5},{8,10},{9,11},{10,... | collective-permute-start | bytes 98312 | tf_op jit(solution)/shard_map/ppermute | solution.py:338
  44.5 0.8 %shard_map.89 = (bf16[8,64,128]{2,1,0:T(8,128)(2,1)S(1)}, bf16[8,64,128]{2,1,0:T(8,128)(2,1)S(1)}, bf16[8,64,128]{2,1,0:T(8,128)(2,1)S(1)}, bf16[8,64,128]{2,1,0:T(8,128)(2,1)S(1)}) custom-call(s32[2]{0:T(128)S(1)} %pad_add_fusion.where, bf16[64,64,128]{2,1,0:T(8,128)(2,1)S(1)} %collective-permute-done.3.other.aside, ...), custom_call_target="tpu_custom_call" | custom-call | flops 1048576 | bytes 2621440 | tf_op jit(solution)/shard_map/pallas_call | solution.py:297
  45.3 2.6 %collective-permute-start.9 = (bf16[8,64,128]{2,1,0:T(8,128)(2,1)S(1)}, bf16[8,64,128]{2,1,0:T(8,128)(2,1)S(1)}, u32[]{:S(2)}, u32[]{:S(2)}) collective-permute-start(bf16[8,64,128]{2,1,0:T(8,128)(2,1)S(1)} %get-tuple-element.59), channel_id=1, source_target_pairs={{0,1},{1,2},{2,3},{3,0},{4,5},{5,6},{6,7},{7,4},{8,9},{9,10},{10,1... | collective-permute-start | bytes 393224 | tf_op jit(solution)/shard_map/ppermute | solution.py:338
  48.0 1.8 %collective-permute-start.10 = (bf16[8,64,128]{2,1,0:T(8,128)(2,1)S(1)}, bf16[8,64,128]{2,1,0:T(8,128)(2,1)S(1)}, u32[]{:S(2)}, u32[]{:S(2)}) collective-permute-start(bf16[8,64,128]{2,1,0:T(8,128)(2,1)S(1)} %get-tuple-element.60), channel_id=1, source_target_pairs={{0,2},{1,3},{2,0},{3,1},{4,6},{5,7},{6,4},{7,5},{8,10},{9,11},{10,... | collective-permute-start | bytes 393224 | tf_op jit(solution)/shard_map/ppermute | solution.py:338
  49.8 0.7 collective-permute-start.11
  50.6 1.2 %collective-permute-done.18 = f32[2,64,128]{2,1,0:T(8,128)S(1)} collective-permute-done((f32[2,64,128]{2,1,0:T(8,128)S(1)}, f32[2,64,128]{2,1,0:T(8,128)S(1)}, u32[]{:S(2)}, u32[]{:S(2)}) %collective-permute-start.18) | collective-permute-done | bytes 65568 | tf_op jit(solution)/shard_map/ppermute | solution.py:379
  51.9 2.1 %collective-permute-start.21 = (f32[2,64,128]{2,1,0:T(8,128)S(1)}, f32[2,64,128]{2,1,0:T(8,128)S(1)}, u32[]{:S(2)}, u32[]{:S(2)}) collective-permute-start(f32[2,64,128]{2,1,0:T(8,128)S(1)} %add.52), channel_id=1, source_target_pairs={{0,24},{4,28},{8,16},{12,20},{16,8},{20,12},{24,0},{28,4},{1,25},{... | collective-permute-start | bytes 196616 | tf_op jit(solution)/shard_map/ppermute | solution.py:381
  54.0 0.4 collective-permute-start.20
  54.4 1.0 %collective-permute-start.19 = (f32[2,64,128]{2,1,0:T(8,128)S(1)}, f32[2,64,128]{2,1,0:T(8,128)S(1)}, u32[]{:S(2)}, u32[]{:S(2)}) collective-permute-start(f32[2,64,128]{2,1,0:T(8,128)S(1)} %add.52), channel_id=1, source_target_pairs={{0,8},{4,12},{8,0},{12,4},{16,24},{20,28},{24,16},{28,20},{1,9},{5... | collective-permute-start | bytes 196616 | tf_op jit(solution)/shard_map/ppermute | solution.py:381
  55.4 2.8 %collective-permute-done.10.rest_2_ = bf16[8,64,128]{2,1,0:T(8,128)(2,1)S(1)} collective-permute-done((bf16[8,64,128]{2,1,0:T(8,128)(2,1)S(1)}, bf16[8,64,128]{2,1,0:T(8,128)(2,1)S(1)}, u32[]{:S(2)}, u32[]{:S(2)}) %collective-permute-start.10) | collective-permute-done | bytes 131104 | tf_op jit(solution)/shard_map/ppermute | solution.py:338
  58.2 1.0 %shard_map.90 = (bf16[8,64,128]{2,1,0:T(8,128)(2,1)S(1)}, bf16[8,64,128]{2,1,0:T(8,128)(2,1)S(1)}, bf16[8,64,128]{2,1,0:T(8,128)(2,1)S(1)}, bf16[8,64,128]{2,1,0:T(8,128)(2,1)S(1)}) custom-call(s32[2]{0:T(128)S(1)} %pad_add_fusion.where, bf16[8,64,128]{2,1,0:T(8,128)(2,1)S(1)} %get-tuple-element.58.rest_0_, ...), custom_call_target="tpu_custom_call" | custom-call | flops 134217728 | bytes 1048576 | tf_op jit(solution)/shard_map/pallas_call | solution.py:209
  59.2 3.3 %collective-permute-start.12 = (bf16[8,64,128]{2,1,0:T(8,128)(2,1)S(1)}, bf16[8,64,128]{2,1,0:T(8,128)(2,1)S(1)}, u32[]{:S(2)}, u32[]{:S(2)}) collective-permute-start(bf16[8,64,128]{2,1,0:T(8,128)(2,1)S(1)} %get-tuple-element.63), channel_id=1, source_target_pairs={{0,1},{1,2},{2,3},{3,0},{4,5},{5,6},{6,7},{7,4},{8,9},{9,10},{10,1... | collective-permute-start | bytes 393224 | tf_op jit(solution)/shard_map/ppermute | solution.py:338
  62.6 1.0 %collective-permute-start.13 = (bf16[8,64,128]{2,1,0:T(8,128)(2,1)S(1)}, bf16[8,64,128]{2,1,0:T(8,128)(2,1)S(1)}, u32[]{:S(2)}, u32[]{:S(2)}) collective-permute-start(bf16[8,64,128]{2,1,0:T(8,128)(2,1)S(1)} %get-tuple-element.64), channel_id=1, source_target_pairs={{0,2},{1,3},{2,0},{3,1},{4,6},{5,7},{6,4},{7,5},{8,10},{9,11},{10,... | collective-permute-start | bytes 393224 | tf_op jit(solution)/shard_map/ppermute | solution.py:338
  63.6 1.5 %collective-permute-start.14 = (bf16[8,64,128]{2,1,0:T(8,128)(2,1)S(1)}, bf16[8,64,128]{2,1,0:T(8,128)(2,1)S(1)}, u32[]{:S(2)}, u32[]{:S(2)}) collective-permute-start(bf16[8,64,128]{2,1,0:T(8,128)(2,1)S(1)} %get-tuple-element.65), channel_id=1, source_target_pairs={{0,3},{1,0},{2,1},{3,2},{4,7},{5,4},{6,5},{7,6},{8,11},{9,8},{10,9... | collective-permute-start | bytes 393224 | tf_op jit(solution)/shard_map/ppermute | solution.py:338
  65.0 0.6 copy_bitcast_fusion
  65.7 1.7 %collective-permute-done.12.rest_1_ = bf16[8,64,128]{2,1,0:T(8,128)(2,1)S(1)} collective-permute-done((bf16[8,64,128]{2,1,0:T(8,128)(2,1)S(1)}, bf16[8,64,128]{2,1,0:T(8,128)(2,1)S(1)}, u32[]{:S(2)}, u32[]{:S(2)}) %collective-permute-start.12) | collective-permute-done | bytes 131104 | tf_op jit(solution)/shard_map/ppermute | solution.py:338
  67.4 4.8 %collective-permute-done.13.rest_2_ = bf16[8,64,128]{2,1,0:T(8,128)(2,1)S(1)} collective-permute-done((bf16[8,64,128]{2,1,0:T(8,128)(2,1)S(1)}, bf16[8,64,128]{2,1,0:T(8,128)(2,1)S(1)}, u32[]{:S(2)}, u32[]{:S(2)}) %collective-permute-start.13) | collective-permute-done | bytes 131104 | tf_op jit(solution)/shard_map/ppermute | solution.py:338
  72.1 1.4 %shard_map.91 = bf16[32,64,128]{2,1,0:T(8,128)(2,1)} custom-call(s32[2]{0:T(128)S(1)} %pad_add_fusion.where, bf16[8,64,128]{2,1,0:T(8,128)(2,1)S(1)} %get-tuple-element.62.rest_0_, bf16[8,64,128]{2,1,0:T(8,128)(2,1)S(1)} %collective-permute-done.12.rest_1_, bf16[8,64,128]{2,1,0:T(8,128)(2,1)S(1)} %collective-permute-done.13.rest_2_, ...), custom_call_target="tpu_custom_call" | custom-call | bytes 33554432 | tf_op jit(solution)/shard_map/pallas_call | solution.py:323
  (23 shorter events, 0.8 us)
Async XLA Ops:
  1.8 14.6 %collective-permute-start.2 = (bf16[8,64,128]{2,1,0:T(8,128)(2,1)S(1)}, bf16[8,64,128]{2,1,0:T(8,128)(2,1)S(1)}, u32[]{:S(2)}, u32[]{:S(2)}) collective-permute-start(bf16[8,64,128]{2,1,0:T(8,128)(2,1)S(1)} %get-tuple-element.70), channel_id=1, source_target_pairs={{0,3},{1,0},{2,1},{3,2},{4,7},{5,4},{6,5},{7,6},{8,11},{9,8},{10,9... | collective-permute-start | bytes 393224 | tf_op jit(solution)/shard_map/ppermute | solution.py:338
  6.9 9.5 %collective-permute-start = (bf16[8,64,128]{2,1,0:T(8,128)(2,1)S(1)}, bf16[8,64,128]{2,1,0:T(8,128)(2,1)S(1)}, u32[]{:S(2)}, u32[]{:S(2)}) collective-permute-start(bf16[8,64,128]{2,1,0:T(8,128)(2,1)S(1)} %get-tuple-element.71), channel_id=1, source_target_pairs={{0,1},{1,2},{2,3},{3,0},{4,5},{5,6},{6,7},{7,4},{8,9},{9,10},{10,1... | collective-permute-start | bytes 393224 | tf_op jit(solution)/shard_map/ppermute | solution.py:338
  6.9 11.5 %collective-permute-start.1 = (bf16[8,64,128]{2,1,0:T(8,128)(2,1)S(1)}, bf16[8,64,128]{2,1,0:T(8,128)(2,1)S(1)}, u32[]{:S(2)}, u32[]{:S(2)}) collective-permute-start(bf16[8,64,128]{2,1,0:T(8,128)(2,1)S(1)} %get-tuple-element.73), channel_id=1, source_target_pairs={{0,2},{1,3},{2,0},{3,1},{4,6},{5,7},{6,4},{7,5},{8,10},{9,11},{10,... | collective-permute-start | bytes 393224 | tf_op jit(solution)/shard_map/ppermute | solution.py:338
  18.4 2.7 %collective-permute-start.3 = (bf16[64,64,128]{2,1,0:T(8,128)(2,1)S(1)}, bf16[64,64,128]{2,1,0:T(8,128)(2,1)S(1)}, u32[]{:S(2)}, u32[]{:S(2)}) collective-permute-start(bf16[64,64,128]{2,1,0:T(8,128)(2,1)S(1)} %get-tuple-element.37), channel_id=1, source_target_pairs={{0,4},{4,0},{8,12},{12,8},{16,20},{20,16},{24,28},{28,24},{1,5},{5... | collective-permute-start | bytes 3145736 | tf_op jit(solution)/shard_map/ppermute | solution.py:363
  18.4 26.1 %collective-permute-start.8 = (bf16[32,64,128]{2,1,0:T(8,128)(2,1)S(1)}, bf16[32,64,128]{2,1,0:T(8,128)(2,1)S(1)}, u32[]{:S(2)}, u32[]{:S(2)}) collective-permute-start(bf16[32,64,128]{2,1,0:T(8,128)(2,1)S(1)} %get-tuple-element.57), channel_id=1, source_target_pairs={{0,24},{4,12},{8,0},{12,20},{16,8},{20,28},{24,16},{28,4},{1,25},{... | collective-permute-start | bytes 1572872 | tf_op jit(solution)/shard_map/ppermute | solution.py:364
  21.3 23.2 %collective-permute-start.7 = (bf16[32,64,128]{2,1,0:T(8,128)(2,1)S(1)}, bf16[32,64,128]{2,1,0:T(8,128)(2,1)S(1)}, u32[]{:S(2)}, u32[]{:S(2)}) collective-permute-start(bf16[32,64,128]{2,1,0:T(8,128)(2,1)S(1)} %shard_map.87), channel_id=1, source_target_pairs={{0,28},{4,8},{8,4},{12,16},{16,12},{20,24},{24,20},{28,0},{1,29},{... | collective-permute-start | bytes 1572872 | tf_op jit(solution)/shard_map/ppermute | solution.py:366
  23.5 9.0 %collective-permute-start.4 = (bf16[10,64,128]{2,1,0:T(8,128)(2,1)S(1)}, bf16[10,64,128]{2,1,0:T(8,128)(2,1)S(1)}, u32[]{:S(2)}, u32[]{:S(2)}) collective-permute-start(bf16[10,64,128]{2,1,0:T(8,128)(2,1)S(1)} %get-tuple-element.45), channel_id=1, source_target_pairs={{0,1},{1,2},{2,3},{3,0},{4,5},{5,6},{6,7},{7,4},{8,9},{9,10},{10,1... | collective-permute-start | bytes 491528 | tf_op jit(solution)/shard_map/ppermute | solution.py:338
  26.7 11.3 %collective-permute-start.5 = (bf16[10,64,128]{2,1,0:T(8,128)(2,1)S(1)}, bf16[10,64,128]{2,1,0:T(8,128)(2,1)S(1)}, u32[]{:S(2)}, u32[]{:S(2)}) collective-permute-start(bf16[10,64,128]{2,1,0:T(8,128)(2,1)S(1)} %get-tuple-element.46), channel_id=1, source_target_pairs={{0,2},{1,3},{2,0},{3,1},{4,6},{5,7},{6,4},{7,5},{8,10},{9,11},{10,... | collective-permute-start | bytes 491528 | tf_op jit(solution)/shard_map/ppermute | solution.py:338
  26.9 11.0 %collective-permute-start.6 = (bf16[10,64,128]{2,1,0:T(8,128)(2,1)S(1)}, bf16[10,64,128]{2,1,0:T(8,128)(2,1)S(1)}, u32[]{:S(2)}, u32[]{:S(2)}) collective-permute-start(bf16[10,64,128]{2,1,0:T(8,128)(2,1)S(1)} %get-tuple-element.47), channel_id=1, source_target_pairs={{0,3},{1,0},{2,1},{3,2},{4,7},{5,4},{6,5},{7,6},{8,11},{9,8},{10,9... | collective-permute-start | bytes 491528 | tf_op jit(solution)/shard_map/ppermute | solution.py:338
  39.0 10.8 %collective-permute-start.15 = (bf16[2,64,128]{2,1,0:T(8,128)(2,1)S(1)}, bf16[2,64,128]{2,1,0:T(8,128)(2,1)S(1)}, u32[]{:S(2)}, u32[]{:S(2)}) collective-permute-start(bf16[2,64,128]{2,1,0:T(8,128)(2,1)S(1)} %get-tuple-element.67), channel_id=1, source_target_pairs={{0,3},{1,0},{2,1},{3,2},{4,7},{5,4},{6,5},{7,6},{8,11},{9,8},{10,9... | collective-permute-start | bytes 98312 | tf_op jit(solution)/shard_map/ppermute | solution.py:338
  43.6 6.8 %collective-permute-start.16 = (bf16[2,64,128]{2,1,0:T(8,128)(2,1)S(1)}, bf16[2,64,128]{2,1,0:T(8,128)(2,1)S(1)}, u32[]{:S(2)}, u32[]{:S(2)}) collective-permute-start(bf16[2,64,128]{2,1,0:T(8,128)(2,1)S(1)} %get-tuple-element.68), channel_id=1, source_target_pairs={{0,2},{1,3},{2,0},{3,1},{4,6},{5,7},{6,4},{7,5},{8,10},{9,11},{10,... | collective-permute-start | bytes 98312 | tf_op jit(solution)/shard_map/ppermute | solution.py:338
  44.5 6.0 %collective-permute-start.17 = (bf16[2,64,128]{2,1,0:T(8,128)(2,1)S(1)}, bf16[2,64,128]{2,1,0:T(8,128)(2,1)S(1)}, u32[]{:S(2)}, u32[]{:S(2)}) collective-permute-start(bf16[2,64,128]{2,1,0:T(8,128)(2,1)S(1)} %get-tuple-element.69), channel_id=1, source_target_pairs={{0,1},{1,2},{2,3},{3,0},{4,5},{5,6},{6,7},{7,4},{8,9},{9,10},{10,1... | collective-permute-start | bytes 98312 | tf_op jit(solution)/shard_map/ppermute | solution.py:338
  45.3 9.1 %collective-permute-start.9 = (bf16[8,64,128]{2,1,0:T(8,128)(2,1)S(1)}, bf16[8,64,128]{2,1,0:T(8,128)(2,1)S(1)}, u32[]{:S(2)}, u32[]{:S(2)}) collective-permute-start(bf16[8,64,128]{2,1,0:T(8,128)(2,1)S(1)} %get-tuple-element.59), channel_id=1, source_target_pairs={{0,1},{1,2},{2,3},{3,0},{4,5},{5,6},{6,7},{7,4},{8,9},{9,10},{10,1... | collective-permute-start | bytes 393224 | tf_op jit(solution)/shard_map/ppermute | solution.py:338
  48.0 10.3 %collective-permute-start.10 = (bf16[8,64,128]{2,1,0:T(8,128)(2,1)S(1)}, bf16[8,64,128]{2,1,0:T(8,128)(2,1)S(1)}, u32[]{:S(2)}, u32[]{:S(2)}) collective-permute-start(bf16[8,64,128]{2,1,0:T(8,128)(2,1)S(1)} %get-tuple-element.60), channel_id=1, source_target_pairs={{0,2},{1,3},{2,0},{3,1},{4,6},{5,7},{6,4},{7,5},{8,10},{9,11},{10,... | collective-permute-start | bytes 393224 | tf_op jit(solution)/shard_map/ppermute | solution.py:338
  49.8 8.5 %collective-permute-start.11 = (bf16[8,64,128]{2,1,0:T(8,128)(2,1)S(1)}, bf16[8,64,128]{2,1,0:T(8,128)(2,1)S(1)}, u32[]{:S(2)}, u32[]{:S(2)}) collective-permute-start(bf16[8,64,128]{2,1,0:T(8,128)(2,1)S(1)} %get-tuple-element.61), channel_id=1, source_target_pairs={{0,3},{1,0},{2,1},{3,2},{4,7},{5,4},{6,5},{7,6},{8,11},{9,8},{10,9... | collective-permute-start | bytes 393224 | tf_op jit(solution)/shard_map/ppermute | solution.py:338
  50.5 1.3 %collective-permute-start.18 = (f32[2,64,128]{2,1,0:T(8,128)S(1)}, f32[2,64,128]{2,1,0:T(8,128)S(1)}, u32[]{:S(2)}, u32[]{:S(2)}) collective-permute-start(f32[2,64,128]{2,1,0:T(8,128)S(1)} %convert_add_fusion), channel_id=1, source_target_pairs={{0,4},{4,0},{8,12},{12,8},{16,20},{20,16},{24,28},{28,24},{1,5},{5... | collective-permute-start | bytes 196616 | tf_op jit(solution)/shard_map/ppermute | solution.py:379
  51.9 11.7 %collective-permute-start.21 = (f32[2,64,128]{2,1,0:T(8,128)S(1)}, f32[2,64,128]{2,1,0:T(8,128)S(1)}, u32[]{:S(2)}, u32[]{:S(2)}) collective-permute-start(f32[2,64,128]{2,1,0:T(8,128)S(1)} %add.52), channel_id=1, source_target_pairs={{0,24},{4,28},{8,16},{12,20},{16,8},{20,12},{24,0},{28,4},{1,25},{... | collective-permute-start | bytes 196616 | tf_op jit(solution)/shard_map/ppermute | solution.py:381
  54.0 11.0 %collective-permute-start.20 = (f32[2,64,128]{2,1,0:T(8,128)S(1)}, f32[2,64,128]{2,1,0:T(8,128)S(1)}, u32[]{:S(2)}, u32[]{:S(2)}) collective-permute-start(f32[2,64,128]{2,1,0:T(8,128)S(1)} %add.52), channel_id=1, source_target_pairs={{0,16},{4,20},{8,24},{12,28},{16,0},{20,4},{24,8},{28,12},{1,17},{... | collective-permute-start | bytes 196616 | tf_op jit(solution)/shard_map/ppermute | solution.py:381
  54.4 10.6 %collective-permute-start.19 = (f32[2,64,128]{2,1,0:T(8,128)S(1)}, f32[2,64,128]{2,1,0:T(8,128)S(1)}, u32[]{:S(2)}, u32[]{:S(2)}) collective-permute-start(f32[2,64,128]{2,1,0:T(8,128)S(1)} %add.52), channel_id=1, source_target_pairs={{0,8},{4,12},{8,0},{12,4},{16,24},{20,28},{24,16},{28,20},{1,9},{5... | collective-permute-start | bytes 196616 | tf_op jit(solution)/shard_map/ppermute | solution.py:381
  59.2 8.1 %collective-permute-start.12 = (bf16[8,64,128]{2,1,0:T(8,128)(2,1)S(1)}, bf16[8,64,128]{2,1,0:T(8,128)(2,1)S(1)}, u32[]{:S(2)}, u32[]{:S(2)}) collective-permute-start(bf16[8,64,128]{2,1,0:T(8,128)(2,1)S(1)} %get-tuple-element.63), channel_id=1, source_target_pairs={{0,1},{1,2},{2,3},{3,0},{4,5},{5,6},{6,7},{7,4},{8,9},{9,10},{10,1... | collective-permute-start | bytes 393224 | tf_op jit(solution)/shard_map/ppermute | solution.py:338
  62.6 9.5 %collective-permute-start.13 = (bf16[8,64,128]{2,1,0:T(8,128)(2,1)S(1)}, bf16[8,64,128]{2,1,0:T(8,128)(2,1)S(1)}, u32[]{:S(2)}, u32[]{:S(2)}) collective-permute-start(bf16[8,64,128]{2,1,0:T(8,128)(2,1)S(1)} %get-tuple-element.64), channel_id=1, source_target_pairs={{0,2},{1,3},{2,0},{3,1},{4,6},{5,7},{6,4},{7,5},{8,10},{9,11},{10,... | collective-permute-start | bytes 393224 | tf_op jit(solution)/shard_map/ppermute | solution.py:338
  63.6 8.6 %collective-permute-start.14 = (bf16[8,64,128]{2,1,0:T(8,128)(2,1)S(1)}, bf16[8,64,128]{2,1,0:T(8,128)(2,1)S(1)}, u32[]{:S(2)}, u32[]{:S(2)}) collective-permute-start(bf16[8,64,128]{2,1,0:T(8,128)(2,1)S(1)} %get-tuple-element.65), channel_id=1, source_target_pairs={{0,3},{1,0},{2,1},{3,2},{4,7},{5,4},{6,5},{7,6},{8,11},{9,8},{10,9... | collective-permute-start | bytes 393224 | tf_op jit(solution)/shard_map/ppermute | solution.py:338

commit v10 on v9

--- a/solution.py
+++ b/solution.py
@@ -11,6 +11,7 @@
 REACH = 2
 GROUP = 4
 STEP = 4
+CHUNKS = 2
 BF16 = jnp.bfloat16
 F32 = jnp.float32
 MIB = 1 << 20
@@ -39,8 +40,8 @@
 
 
 def tiles_kernel(slabs, reps, where, cols, live, weight, cot, mask, tiles, *rest):
-    outs, packed, rest = rest[:4], rest[4 : 4 + reps], rest[4 + reps :]
-    outs = [outs[0].at[pl.ds(0, cols.shape[1])], outs[0].at[pl.ds(cols.shape[1], cols.shape[1])], *outs[1:]]
+    count = 2 + REACH * CHUNKS
+    (aside, *outs), packed, rest = rest[:count], rest[count : count + reps], rest[count + reps :]
     cot_in, mask_in, weight_in, z, held, first, second, rows, left, sems, z_sems = rest
     totals = (first, second)
     slots, blocks = cols.shape
@@ -112,27 +113,38 @@
             row, remain = entries[u], left[i * STEP + u]
             b, g = lax.div(row, per_row), lax.rem(row, per_row)
             z_row = z[b]
-            for j in range(GROUP):
-                place = wrap(cols[g * GROUP + j, b] + shift, slabs * blocks)
-                place = jnp.where(j < remain, place, window)
-                totals[j % 2][place] += jnp.dot(
-                    z_row, held[row * GROUP + j], preferred_element_type=F32
+            for j in range(0, GROUP, 2):
+                both = [held[row * GROUP + j], held[row * GROUP + j + 1]]
+                terms = jnp.dot(
+                    z_row, jnp.concatenate(both, axis=1), preferred_element_type=F32
                 )
+                for k, total in enumerate(totals):
+                    place = wrap(cols[g * GROUP + j + k, b] + shift, slabs * blocks)
+                    place = jnp.where(j + k < remain, place, window)
+                    total[place] += terms[:, k * nodes : (k + 1) * nodes]
         return jnp.maximum(ready, need)
 
     ready = lax.fori_loop(0, steps, step, jnp.int32(0))
     lax.fori_loop(ready, blocks, wait_row, 0)
     sign = 2 * lax.rem(where[0], 2) - 1
-    for order, out in enumerate(outs):
-        base = ((order - REACH) * sign + REACH) * blocks
-
-        def store(i, carry, out=out, base=base):
+
+    def store(out, order, start=0):
+        base = ((order - REACH) * sign + REACH) * blocks + start
+
+        def some(i, carry):
             for k in range(GROUP):
                 at = i * GROUP + k
                 out[at] = (first[base + at] + second[base + at]).astype(BF16)
             return carry
 
-        lax.fori_loop(0, blocks // GROUP, store, 0)
+        lax.fori_loop(0, out.shape[0] // GROUP, some, 0)
+
+    for order in range(REACH):
+        store(aside.at[pl.ds(order * blocks, blocks)], order)
+    store(outs[0], REACH)
+    for i, out in enumerate(outs[1:]):
+        order, k = divmod(i, CHUNKS)
+        store(out, REACH + 1 + order, k * out.shape[0])
 
 
 def contributions(where, cols, live, weight, cot, mask, tiles, slabs, reps):
@@ -142,7 +154,7 @@
     lists = blocks * (slots // GROUP) + slots // GROUP + STEP
     total = pltpu.VMEM((window + 1, features, nodes), F32)
     packs = blocks // reps + weight.shape[1] // nodes
-    counts = [2 * blocks, blocks, blocks, blocks]
+    counts = [REACH * blocks, blocks] + [blocks // CHUNKS] * (REACH * CHUNKS)
     return pl.pallas_call(
         functools.partial(tiles_kernel, slabs, reps),
         out_shape=[jax.ShapeDtypeStruct((count, features, nodes), BF16) for count in counts]
@@ -258,74 +270,78 @@
     )(where, *packed, *aggs)
 
 
-def add_kernel(one, other, out):
-    def row(i, carry):
-        out[i] = (one[i].astype(F32) + other[i].astype(F32)).astype(BF16)
-        return carry
-
-    lax.fori_loop(0, out.shape[0], row, 0)
-
-
-def add(one, other):
+def add_kernel(other, *refs):
+    for part, out in enumerate(refs[CHUNKS:]):
+        one, base = refs[part], part * out.shape[0]
+
+        def row(i, carry, one=one, out=out, base=base):
+            out[i] = (one[i].astype(F32) + other[base + i].astype(F32)).astype(BF16)
+            return carry
+
+        lax.fori_loop(0, out.shape[0], row, 0)
+
+
+def add(one, aside):
     return pl.pallas_call(
         add_kernel,
-        out_shape=jax.ShapeDtypeStruct(one.shape, BF16),
-        in_specs=[vmem()] * 2,
-        out_specs=vmem(),
+        out_shape=[jax.ShapeDtypeStruct(one[0].shape, BF16)] * CHUNKS,
+        in_specs=[vmem()] * (1 + CHUNKS),
+        out_specs=[vmem()] * CHUNKS,
         compiler_params=pltpu.CompilerParams(vmem_limit_bytes=2 * MIB),
         cost_estimate=pl.CostEstimate(
-            flops=one.size, bytes_accessed=6 * one.size, transcendentals=0
+            flops=aside.size // 2, bytes_accessed=3 * aside.size, transcendentals=0
         ),
-    )(one, other)
-
-
-def total_kernel(reps, where, aside, *rest):
-    terms, outs = rest[:-reps], rest[-reps:]
-    terms = (aside.at[pl.ds(terms[0].shape[0], terms[0].shape[0])], *terms)
+    )(aside, *one)
+
+
+def total_kernel(reps, chunk, where, aside, own, one, two, *outs):
     share = outs[0].shape[0]
+    blocks = own.shape[0]
     for s, out in enumerate(outs):
         first = wrap(where[1] + s, reps) * share
         for i in range(share):
-            total = terms[0][first + i].astype(F32)
-            for term in terms[1:]:
-                total += term[first + i].astype(F32)
+            at = chunk * one.shape[0] + first + i
+            total = own[at].astype(F32) + aside[blocks + at].astype(F32)
+            total += one[first + i].astype(F32) + two[first + i].astype(F32)
             out[i] = total.astype(BF16)
 
 
-def total_shares(where, aside, terms, reps):
-    blocks, features, nodes = terms[0].shape
-    return pl.pallas_call(
-        functools.partial(total_kernel, reps),
+def total_shares(chunk, where, aside, own, one, two, reps):
+    blocks, features, nodes = one.shape
+    return pl.pallas_call(
+        functools.partial(total_kernel, reps, chunk),
         out_shape=[jax.ShapeDtypeStruct((blocks // reps, features, nodes), BF16)] * reps,
-        in_specs=[smem()] + [vmem()] * (1 + len(terms)),
+        in_specs=[smem()] + [vmem()] * 4,
         out_specs=[vmem()] * reps,
         compiler_params=pltpu.CompilerParams(vmem_limit_bytes=2 * MIB),
         cost_estimate=pl.CostEstimate(
-            flops=4 * terms[0].size, bytes_accessed=10 * terms[0].size, transcendentals=0
+            flops=4 * one.size, bytes_accessed=10 * one.size, transcendentals=0
         ),
-    )(where, aside, *terms)
+    )(where, aside, own, one, two)
 
 
 def lay_kernel(reps, where, *rest):
-    shares, out, sems = rest[:reps], rest[reps], rest[reps + 1]
+    shares, out, sems = rest[:-2], rest[-2], rest[-1]
     blocks = shares[0].shape[0]
     copies = []
-    for s in range(reps):
-        first = wrap(where[1] - s, reps) * blocks
-        copies.append(pltpu.make_async_copy(shares[s], out.at[pl.ds(first, blocks)], sems.at[s]))
-        copies[s].start()
+    for i, share in enumerate(shares):
+        chunk, s = divmod(i, reps)
+        first = (chunk * reps + wrap(where[1] - s, reps)) * blocks
+        copies.append(pltpu.make_async_copy(share, out.at[pl.ds(first, blocks)], sems.at[i]))
+        copies[i].start()
     for copy in copies:
         copy.wait()
 
 
 def lay_blocks(where, shares, shape):
-    reps = len(shares)
+    reps = len(shares[0])
+    shares = [share for chunk in shares for share in chunk]
     return pl.pallas_call(
         functools.partial(lay_kernel, reps),
         out_shape=jax.ShapeDtypeStruct(shape, BF16),
-        in_specs=[smem()] + [vmem()] * reps,
+        in_specs=[smem()] + [vmem()] * len(shares),
         out_specs=hbm(),
-        scratch_shapes=[pltpu.SemaphoreType.DMA((reps,))],
+        scratch_shapes=[pltpu.SemaphoreType.DMA((len(shares),))],
         compiler_params=pltpu.CompilerParams(vmem_limit_bytes=2 * MIB),
         cost_estimate=pl.CostEstimate(flops=0, bytes_accessed=32 * MIB, transcendentals=0),
     )(where, *shares)
@@ -356,23 +372,35 @@
     to_one = [(i, (i + (1 if i % 2 else -1)) % slabs) for i in range(slabs)]
     to_two = [(i, (i + (2 if i % 2 else -2)) % slabs) for i in range(slabs)]
     aggs = [shift(node_share(aggregated, s), s) for s in range(reps)]
-    aside, own, one, two, *packed = contributions(
+    aside, own, *rest = contributions(
         where, col_block, live_count, weight, cotangent, relu_mask, tiles, slabs, reps
     )
+    one, two, packed = rest[:CHUNKS], rest[CHUNKS : 2 * CHUNKS], rest[2 * CHUNKS :]
     aside, aggs = lax.optimization_barrier((aside, aggs))
     aside = lax.ppermute(aside, "blk", pair)
-    two_in = lax.ppermute(two, "blk", to_two)
     one = add(one, aside)
-    one_in = lax.ppermute(one, "blk", to_one)
+    one_in, two_in = [], []
+    for k in range(CHUNKS):
+        two_in.append(lax.ppermute(two[k], "blk", to_two))
+        one_in.append(lax.ppermute(one[k], "blk", to_one))
 
     packed, _ = lax.optimization_barrier((packed, one))
     packed = [shift(value, s) for s, value in enumerate(packed)]
     grad_w = weight_partial(where, packed, aggs)
 
-    own, grad_w = lax.optimization_barrier((own, grad_w))
-    shares = total_shares(where, aside, [own, one_in, two_in], reps)
-    shares = [shift(value, s) for s, value in enumerate(shares)]
-    outs = [shift(value, s) for s, value in enumerate(mix(where, shares, packed, share))]
+    def exchange(values):
+        return [shift(value, s) for s, value in enumerate(values)]
+
+    outs = []
+    for k in range(CHUNKS):
+        if k:
+            own, shares, grad_w = lax.optimization_barrier((own, shares, grad_w))
+        sums = total_shares(k, where, aside, own, one_in[k], two_in[k], reps)
+        if k:
+            outs.append(exchange(mix(where, shares, packed, share)))
+        shares = exchange(sums)
+    shares, _ = lax.optimization_barrier((shares, outs))
+    outs.append(exchange(mix(where, shares, packed, share)))
     input_grad = lay_blocks(where, outs, cotangent.shape)
 
     grad_w = sum(shift(part, -s).astype(F32) for s, part in enumerate(grad_w))

time: 74.4 us -> 78.3 us (1.052)
  starting transfers between devices: 36.3 us -> 47 us
  waiting for transfers between devices: 21.8 us -> 13.7 us
  Pallas kernels: 12.8 us -> 14.7 us
    ppermute x15 -> x21, waiting for transfers between devices: 20.3 us -> 8.8 us  [shift(): lax.ppermute(value, 'rep', [(i, (i + steps) % reps) for i in range(reps)])]
    ppermute x2 -> x4, starting transfers between devices: 4.7 us -> 11.2 us  [the longest x2 5.83 us: on_device(): two_in.append(lax.ppermute(two[k], 'blk', to_two))]
    ppermute x15 -> x21, starting transfers between devices: 28 us -> 32.1 us  [shift(): lax.ppermute(value, 'rep', [(i, (i + steps) % reps) for i in range(reps)])]
    ppermute x2 -> x4, waiting for transfers between devices: 0.01 us -> 2.44 us  [the longest x2 2.24 us: on_device(): one_in.append(lax.ppermute(one[k], 'blk', to_one))]
    ppermute x3, waiting for transfers between devices: 0.01 us -> 2.22 us  [on_device(): lax.ppermute(grad_w, 'blk', [(i, i ^ step) for i in range(slabs)])]
    ppermute x1, waiting for transfers between devices: 1.24 us -> 0.01 us  [on_device(): grad_w = grad_w + lax.ppermute(grad_w, 'blk', pair)]
    pallas_call x1 -> x2, Pallas kernels: 1 us -> 1.72 us  [mix(): pl.pallas_call(functools.partial(mix_kernel, reps, first), out_shape=[jax...]
    pallas_call x2 -> x3, Pallas kernels: 1.05 us -> 1.6 us  [the longest x2 1.35 us: total_shares(): pl.pallas_call(functools.partial(total_kernel, reps, chunk), out_shape=[j...]
  transfers between devices with their start and end apart: 22 -> 30, of which waited for: 9 -> 13; matrix products, arithmetic and copies ran while one was open for 1% -> 0% of each run, Pallas kernels for 16% -> 19%
where the time goes in v10:
time: 78.3 us; the launch traced here: 78.1 us
  starting transfers between devices  47 us (60%)
  Pallas kernels  14.7 us (19%)
  waiting for transfers between devices  13.7 us (17%)
  local copies, waits for them, and re-layouts  1.14 us (1%)
  between operations  0.81 us (1%)
    ppermute x21, starting transfers between devices, shift(): lax.ppermute(value, 'rep', [(i, (i + steps) % reps) for i in range(reps)])  32.1 us
    pallas_call x1, Pallas kernels, contributions(): pl.pallas_call(functools.partial(tiles_kernel, slabs, reps), out_shape=[j...  9.02 us
    ppermute x21, waiting for transfers between devices, shift(): lax.ppermute(value, 'rep', [(i, (i + steps) % reps) for i in range(reps)])  8.8 us
    ppermute x2, starting transfers between devices, on_device(): two_in.append(lax.ppermute(two[k], 'blk', to_two))  5.83 us
    ppermute x2, starting transfers between devices, on_device(): one_in.append(lax.ppermute(one[k], 'blk', to_one))  5.35 us
    ppermute x3, starting transfers between devices, on_device(): lax.ppermute(grad_w, 'blk', [(i, i ^ step) for i in range(slabs)])  3.7 us
    ppermute x2, waiting for transfers between devices, on_device(): one_in.append(lax.ppermute(one[k], 'blk', to_one))  2.24 us
    ppermute x3, waiting for transfers between devices, on_device(): lax.ppermute(grad_w, 'blk', [(i, i ^ step) for i in range(slabs)])  2.22 us
  transfers between devices with their start and end apart: 30, of which 13 were waited for; matrix products, arithmetic and copies ran while one was open for 0% of the time, Pallas kernels for 19%

profile of v10, /device:TPU:0, one launch (start us, length us, event | category | flops | bytes accessed | tf_op | source)
XLA Modules:
  0.0 78.1 jit_solution(17660091267463169636)
XLA Ops:
  0.7 1.1 %constant_dynamic-slice_fusion = (bf16[8,64,128]{2,1,0:T(8,128)(2,1)S(1)}, bf16[8,64,128]{2,1,0:T(8,128)(2,1)S(1)}, bf16[8,64,128]{2,1,0:T(8,128)(2,1)S(1)}, bf16[8,64,128]{2,1,0:T(8,128)(2,1)S(1)}) fusion(bf16[32,64,128]{2,1,0:T(8,128)(2,1)} %param.9, s32[]{:T(128)S(6)} %select_n.15, s32[]{:T(128)S(6)} %select_n.13, s32[]{:T(128)S(6)} %select_n.12, ...), kind=kLoop, calls=%fused_computation.3 | loop fusion | bytes 1048592 | tf_op jit(solution)/shard_map/dynamic_slice | solution.py:361
  1.8 5.1 %collective-permute-start.2 = (bf16[8,64,128]{2,1,0:T(8,128)(2,1)S(1)}, bf16[8,64,128]{2,1,0:T(8,128)(2,1)S(1)}, u32[]{:S(2)}, u32[]{:S(2)}) collective-permute-start(bf16[8,64,128]{2,1,0:T(8,128)(2,1)S(1)} %get-tuple-element.110), channel_id=1, source_target_pairs={{0,3},{1,0},{2,1},{3,2},{4,7},{5,4},{6,5},{7,6},{8,11},{9,8},{10,9... | collective-permute-start | bytes 393224 | tf_op jit(solution)/shard_map/ppermute | solution.py:354
  6.9 1.0 %collective-permute-start.1 = (bf16[8,64,128]{2,1,0:T(8,128)(2,1)S(1)}, bf16[8,64,128]{2,1,0:T(8,128)(2,1)S(1)}, u32[]{:S(2)}, u32[]{:S(2)}) collective-permute-start(bf16[8,64,128]{2,1,0:T(8,128)(2,1)S(1)} %get-tuple-element.113), channel_id=1, source_target_pairs={{0,2},{1,3},{2,0},{3,1},{4,6},{5,7},{6,4},{7,5},{8,10},{9,11},{10,... | collective-permute-start | bytes 393224 | tf_op jit(solution)/shard_map/ppermute | solution.py:354
  8.0 9.0 %shard_map.86 = (bf16[64,64,128]{2,1,0:T(8,128)(2,1)S(1)}, bf16[32,64,128]{2,1,0:T(8,128)(2,1)S(1)}, bf16[16,64,128]{2,1,0:T(8,128)(2,1)S(1)}, bf16[16,64,128]{2...) custom-call(s32[2]{0:T(128)S(1)} %pad_add_fusion.where, ...), custom_call_target="tpu_custom_call" | custom-call | flops 1073741824 | bytes 16777216 | tf_op jit(solution)/shard_map/pallas_call | solution.py:158
  17.0 1.3 %collective-permute-done.1.rest_6_ = bf16[8,64,128]{2,1,0:T(8,128)(2,1)S(1)} collective-permute-done((bf16[8,64,128]{2,1,0:T(8,128)(2,1)S(1)}, bf16[8,64,128]{2,1,0:T(8,128)(2,1)S(1)}, u32[]{:S(2)}, u32[]{:S(2)}) %collective-permute-start.1) | collective-permute-done | bytes 131104 | tf_op jit(solution)/shard_map/ppermute | solution.py:354
  18.4 2.4 %collective-permute-start.5 = (bf16[16,64,128]{2,1,0:T(8,128)(2,1)S(1)}, bf16[16,64,128]{2,1,0:T(8,128)(2,1)S(1)}, u32[]{:S(2)}, u32[]{:S(2)}) collective-permute-start(bf16[16,64,128]{2,1,0:T(8,128)(2,1)S(1)} %get-tuple-element.62), channel_id=1, source_target_pairs={{0,24},{4,12},{8,0},{12,20},{16,8},{20,28},{24,16},{28,4},{1,25},{... | collective-permute-start | bytes 786440 | tf_op jit(solution)/shard_map/ppermute | solution.py:384
  21.3 2.3 %collective-permute-start.4 = (bf16[16,64,128]{2,1,0:T(8,128)(2,1)S(1)}, bf16[16,64,128]{2,1,0:T(8,128)(2,1)S(1)}, u32[]{:S(2)}, u32[]{:S(2)}) collective-permute-start(bf16[16,64,128]{2,1,0:T(8,128)(2,1)S(1)} %get-tuple-element.61), channel_id=1, source_target_pairs={{0,28},{4,8},{8,4},{12,16},{16,12},{20,24},{24,20},{28,0},{1,29},{... | collective-permute-start | bytes 786440 | tf_op jit(solution)/shard_map/ppermute | solution.py:385
  24.3 2.1 %collective-permute-start.10 = (bf16[10,64,128]{2,1,0:T(8,128)(2,1)S(1)}, bf16[10,64,128]{2,1,0:T(8,128)(2,1)S(1)}, u32[]{:S(2)}, u32[]{:S(2)}) collective-permute-start(bf16[10,64,128]{2,1,0:T(8,128)(2,1)S(1)} %get-tuple-element.74), channel_id=1, source_target_pairs={{0,2},{1,3},{2,0},{3,1},{4,6},{5,7},{6,4},{7,5},{8,10},{9,11},{10,... | collective-permute-start | bytes 491528 | tf_op jit(solution)/shard_map/ppermute | solution.py:354
  26.4 1.0 %collective-permute-start.11 = (bf16[10,64,128]{2,1,0:T(8,128)(2,1)S(1)}, bf16[10,64,128]{2,1,0:T(8,128)(2,1)S(1)}, u32[]{:S(2)}, u32[]{:S(2)}) collective-permute-start(bf16[10,64,128]{2,1,0:T(8,128)(2,1)S(1)} %get-tuple-element.75), channel_id=1, source_target_pairs={{0,3},{1,0},{2,1},{3,2},{4,7},{5,4},{6,5},{7,6},{8,11},{9,8},{10,9... | collective-permute-start | bytes 491528 | tf_op jit(solution)/shard_map/ppermute | solution.py:354
  27.6 3.4 %collective-permute-start.16 = (bf16[16,64,128]{2,1,0:T(8,128)(2,1)S(1)}, bf16[16,64,128]{2,1,0:T(8,128)(2,1)S(1)}, u32[]{:S(2)}, u32[]{:S(2)}) collective-permute-start(bf16[16,64,128]{2,1,0:T(8,128)(2,1)S(1)} %get-tuple-element.93), channel_id=1, source_target_pairs={{0,24},{4,12},{8,0},{12,20},{16,8},{20,28},{24,16},{28,4},{1,25},{... | collective-permute-start | bytes 786440 | tf_op jit(solution)/shard_map/ppermute | solution.py:384
  31.0 2.2 %collective-permute-done.4.one = bf16[16,64,128]{2,1,0:T(8,128)(2,1)S(1)} collective-permute-done((bf16[16,64,128]{2,1,0:T(8,128)(2,1)S(1)}, bf16[16,64,128]{2,1,0:T(8,128)(2,1)S(1)}, u32[]{:S(2)}, u32[]{:S(2)}) %collective-permute-start.4) | collective-permute-done | bytes 262176 | tf_op jit(solution)/shard_map/ppermute | solution.py:385
  33.2 3.1 %collective-permute-start.15 = (bf16[16,64,128]{2,1,0:T(8,128)(2,1)S(1)}, bf16[16,64,128]{2,1,0:T(8,128)(2,1)S(1)}, u32[]{:S(2)}, u32[]{:S(2)}) collective-permute-start(bf16[16,64,128]{2,1,0:T(8,128)(2,1)S(1)} %get-tuple-element.71), channel_id=1, source_target_pairs={{0,28},{4,8},{8,4},{12,16},{16,12},{20,24},{24,20},{28,0},{1,29},{... | collective-permute-start | bytes 786440 | tf_op jit(solution)/shard_map/ppermute | solution.py:385
  38.1 1.8 %collective-permute-start.7 = (bf16[4,64,128]{2,1,0:T(8,128)(2,1)S(1)}, bf16[4,64,128]{2,1,0:T(8,128)(2,1)S(1)}, u32[]{:S(2)}, u32[]{:S(2)}) collective-permute-start(bf16[4,64,128]{2,1,0:T(8,128)(2,1)S(1)} %get-tuple-element.65), channel_id=1, source_target_pairs={{0,2},{1,3},{2,0},{3,1},{4,6},{5,7},{6,4},{7,5},{8,10},{9,11},{10,... | collective-permute-start | bytes 196616 | tf_op jit(solution)/shard_map/ppermute | solution.py:354
  39.9 1.7 %collective-permute-start.8 = (bf16[4,64,128]{2,1,0:T(8,128)(2,1)S(1)}, bf16[4,64,128]{2,1,0:T(8,128)(2,1)S(1)}, u32[]{:S(2)}, u32[]{:S(2)}) collective-permute-start(bf16[4,64,128]{2,1,0:T(8,128)(2,1)S(1)} %get-tuple-element.66), channel_id=1, source_target_pairs={{0,3},{1,0},{2,1},{3,2},{4,7},{5,4},{6,5},{7,6},{8,11},{9,8},{10,9... | collective-permute-start | bytes 196616 | tf_op jit(solution)/shard_map/ppermute | solution.py:354
  41.5 1.0 %shard_map.89 = (bf16[2,64,128]{2,1,0:T(8,128)(2,1)S(1)}, bf16[2,64,128]{2,1,0:T(8,128)(2,1)S(1)}, bf16[2,64,128]{2,1,0:T(8,128)(2,1)S(1)}, bf16[2,64,128]{2,1,0:T(8,128)(2,1)S(1)}) custom-call(s32[2]{0:T(128)S(1)} %pad_add_fusion.where, bf16[10,64,128]{2,1,0:T(8,128)(2,1)S(1)} %get-tuple-element.72.rest_0_.rest_4_, ...), custom_call_target="tpu_custom_call" | custom-call | flops 134217728 | bytes 1179648 | tf_op jit(solution)/shard_map/pallas_call | solution.py:258
  42.6 1.0 %collective-permute-done.6.rest_1_ = bf16[4,64,128]{2,1,0:T(8,128)(2,1)S(1)} collective-permute-done((bf16[4,64,128]{2,1,0:T(8,128)(2,1)S(1)}, bf16[4,64,128]{2,1,0:T(8,128)(2,1)S(1)}, u32[]{:S(2)}, u32[]{:S(2)}) %collective-permute-start.6) | collective-permute-done | bytes 65568 | tf_op jit(solution)/shard_map/ppermute | solution.py:354
  43.5 2.3 %collective-permute-done.7.rest_2_ = bf16[4,64,128]{2,1,0:T(8,128)(2,1)S(1)} collective-permute-done((bf16[4,64,128]{2,1,0:T(8,128)(2,1)S(1)}, bf16[4,64,128]{2,1,0:T(8,128)(2,1)S(1)}, u32[]{:S(2)}, u32[]{:S(2)}) %collective-permute-start.7) | collective-permute-done | bytes 65568 | tf_op jit(solution)/shard_map/ppermute | solution.py:354
  45.8 0.9 %collective-permute-done.8.rest_3_ = bf16[4,64,128]{2,1,0:T(8,128)(2,1)S(1)} collective-permute-done((bf16[4,64,128]{2,1,0:T(8,128)(2,1)S(1)}, bf16[4,64,128]{2,1,0:T(8,128)(2,1)S(1)}, u32[]{:S(2)}, u32[]{:S(2)}) %collective-permute-start.8) | collective-permute-done | bytes 65568 | tf_op jit(solution)/shard_map/ppermute | solution.py:354
  47.5 2.1 %collective-permute-start.12 = (bf16[4,64,128]{2,1,0:T(8,128)(2,1)S(1)}, bf16[4,64,128]{2,1,0:T(8,128)(2,1)S(1)}, u32[]{:S(2)}, u32[]{:S(2)}) collective-permute-start(bf16[4,64,128]{2,1,0:T(8,128)(2,1)S(1)} %get-tuple-element.89), channel_id=1, source_target_pairs={{0,1},{1,2},{2,3},{3,0},{4,5},{5,6},{6,7},{7,4},{8,9},{9,10},{10,1... | collective-permute-start | bytes 196616 | tf_op jit(solution)/shard_map/ppermute | solution.py:354
  49.6 1.8 %collective-permute-start.23 = (bf16[2,64,128]{2,1,0:T(8,128)(2,1)S(1)}, bf16[2,64,128]{2,1,0:T(8,128)(2,1)S(1)}, u32[]{:S(2)}, u32[]{:S(2)}) collective-permute-start(bf16[2,64,128]{2,1,0:T(8,128)(2,1)S(1)} %get-tuple-element.107), channel_id=1, source_target_pairs={{0,3},{1,0},{2,1},{3,2},{4,7},{5,4},{6,5},{7,6},{8,11},{9,8},{10,9... | collective-permute-start | bytes 98312 | tf_op jit(solution)/shard_map/ppermute | solution.py:354
  52.0 2.6 %collective-permute-start.13 = (bf16[4,64,128]{2,1,0:T(8,128)(2,1)S(1)}, bf16[4,64,128]{2,1,0:T(8,128)(2,1)S(1)}, u32[]{:S(2)}, u32[]{:S(2)}) collective-permute-start(bf16[4,64,128]{2,1,0:T(8,128)(2,1)S(1)} %get-tuple-element.90), channel_id=1, source_target_pairs={{0,2},{1,3},{2,0},{3,1},{4,6},{5,7},{6,4},{7,5},{8,10},{9,11},{10,... | collective-permute-start | bytes 196616 | tf_op jit(solution)/shard_map/ppermute | solution.py:354
  55.3 2.7 %collective-permute-start.14 = (bf16[4,64,128]{2,1,0:T(8,128)(2,1)S(1)}, bf16[4,64,128]{2,1,0:T(8,128)(2,1)S(1)}, u32[]{:S(2)}, u32[]{:S(2)}) collective-permute-start(bf16[4,64,128]{2,1,0:T(8,128)(2,1)S(1)} %get-tuple-element.91), channel_id=1, source_target_pairs={{0,3},{1,0},{2,1},{3,2},{4,7},{5,4},{6,5},{7,6},{8,11},{9,8},{10,9... | collective-permute-start | bytes 196616 | tf_op jit(solution)/shard_map/ppermute | solution.py:354
  58.0 0.9 %collective-permute-start.18 = (bf16[4,64,128]{2,1,0:T(8,128)(2,1)S(1)}, bf16[4,64,128]{2,1,0:T(8,128)(2,1)S(1)}, u32[]{:S(2)}, u32[]{:S(2)}) collective-permute-start(bf16[4,64,128]{2,1,0:T(8,128)(2,1)S(1)} %get-tuple-element.96), channel_id=1, source_target_pairs={{0,2},{1,3},{2,0},{3,1},{4,6},{5,7},{6,4},{7,5},{8,10},{9,11},{10,... | collective-permute-start | bytes 196616 | tf_op jit(solution)/shard_map/ppermute | solution.py:354
  58.9 3.0 %collective-permute-start.19 = (bf16[4,64,128]{2,1,0:T(8,128)(2,1)S(1)}, bf16[4,64,128]{2,1,0:T(8,128)(2,1)S(1)}, u32[]{:S(2)}, u32[]{:S(2)}) collective-permute-start(bf16[4,64,128]{2,1,0:T(8,128)(2,1)S(1)} %get-tuple-element.97), channel_id=1, source_target_pairs={{0,3},{1,0},{2,1},{3,2},{4,7},{5,4},{6,5},{7,6},{8,11},{9,8},{10,9... | collective-permute-start | bytes 196616 | tf_op jit(solution)/shard_map/ppermute | solution.py:354
  62.0 2.1 %collective-permute-done.17.rest_1_ = bf16[4,64,128]{2,1,0:T(8,128)(2,1)S(1)} collective-permute-done((bf16[4,64,128]{2,1,0:T(8,128)(2,1)S(1)}, bf16[4,64,128]{2,1,0:T(8,128)(2,1)S(1)}, u32[]{:S(2)}, u32[]{:S(2)}) %collective-permute-start.17) | collective-permute-done | bytes 65568 | tf_op jit(solution)/shard_map/ppermute | solution.py:354
  65.6 1.9 %collective-permute-start.20 = (bf16[4,64,128]{2,1,0:T(8,128)(2,1)S(1)}, bf16[4,64,128]{2,1,0:T(8,128)(2,1)S(1)}, u32[]{:S(2)}, u32[]{:S(2)}) collective-permute-start(bf16[4,64,128]{2,1,0:T(8,128)(2,1)S(1)} %get-tuple-element.103), channel_id=1, source_target_pairs={{0,1},{1,2},{2,3},{3,0},{4,5},{5,6},{6,7},{7,4},{8,9},{9,10},{10,1... | collective-permute-start | bytes 196616 | tf_op jit(solution)/shard_map/ppermute | solution.py:354
  67.6 1.9 %collective-permute-start.21 = (bf16[4,64,128]{2,1,0:T(8,128)(2,1)S(1)}, bf16[4,64,128]{2,1,0:T(8,128)(2,1)S(1)}, u32[]{:S(2)}, u32[]{:S(2)}) collective-permute-start(bf16[4,64,128]{2,1,0:T(8,128)(2,1)S(1)} %get-tuple-element.104), channel_id=1, source_target_pairs={{0,2},{1,3},{2,0},{3,1},{4,6},{5,7},{6,4},{7,5},{8,10},{9,11},{10,... | collective-permute-start | bytes 196616 | tf_op jit(solution)/shard_map/ppermute | solution.py:354
  70.0 2.1 %collective-permute-start.29 = (f32[2,64,128]{2,1,0:T(8,128)S(1)}, f32[2,64,128]{2,1,0:T(8,128)S(1)}, u32[]{:S(2)}, u32[]{:S(2)}) collective-permute-start(f32[2,64,128]{2,1,0:T(8,128)S(1)} %add.52), channel_id=1, source_target_pairs={{0,24},{4,28},{8,16},{12,20},{16,8},{20,12},{24,0},{28,4},{1,25},{... | collective-permute-start | bytes 196616 | tf_op jit(solution)/shard_map/ppermute | solution.py:409
  72.1 1.1 %collective-permute-start.28 = (f32[2,64,128]{2,1,0:T(8,128)S(1)}, f32[2,64,128]{2,1,0:T(8,128)S(1)}, u32[]{:S(2)}, u32[]{:S(2)}) collective-permute-start(f32[2,64,128]{2,1,0:T(8,128)S(1)} %add.52), channel_id=1, source_target_pairs={{0,16},{4,20},{8,24},{12,28},{16,0},{20,4},{24,8},{28,12},{1,17},{... | collective-permute-start | bytes 196616 | tf_op jit(solution)/shard_map/ppermute | solution.py:409
  73.9 1.4 %shard_map.93 = bf16[32,64,128]{2,1,0:T(8,128)(2,1)} custom-call(s32[2]{0:T(128)S(1)} %pad_add_fusion.where, bf16[4,64,128]{2,1,0:T(8,128)(2,1)S(1)} %get-tuple-element.88.rest_0_, bf16[4,64,128]{2,1,0:T(8,128)(2,1)S(1)} %collective-permute-done.12.rest_1_, bf16[4,64,128]{2,1,0:T(8,128)(2,1)S(1)} %collective-permute-done.13.rest_2_, ...), custom_call_target="tpu_custom_call" | custom-call | bytes 33554432 | tf_op jit(solution)/shard_map/pallas_call | solution.py:339
  75.3 1.1 %collective-permute-done.28 = f32[2,64,128]{2,1,0:T(8,128)S(1)} collective-permute-done((f32[2,64,128]{2,1,0:T(8,128)S(1)}, f32[2,64,128]{2,1,0:T(8,128)S(1)}, u32[]{:S(2)}, u32[]{:S(2)}) %collective-permute-start.28) | collective-permute-done | bytes 65568 | tf_op jit(solution)/shard_map/ppermute | solution.py:409
  76.4 1.1 %collective-permute-done.27 = f32[2,64,128]{2,1,0:T(8,128)S(1)} collective-permute-done((f32[2,64,128]{2,1,0:T(8,128)S(1)}, f32[2,64,128]{2,1,0:T(8,128)S(1)}, u32[]{:S(2)}, u32[]{:S(2)}) %collective-permute-start.27) | collective-permute-done | bytes 65568 | tf_op jit(solution)/shard_map/ppermute | solution.py:409
  (41 shorter events, 8.9 us)
Async XLA Ops:
  1.8 15.2 %collective-permute-start.2 = (bf16[8,64,128]{2,1,0:T(8,128)(2,1)S(1)}, bf16[8,64,128]{2,1,0:T(8,128)(2,1)S(1)}, u32[]{:S(2)}, u32[]{:S(2)}) collective-permute-start(bf16[8,64,128]{2,1,0:T(8,128)(2,1)S(1)} %get-tuple-element.110), channel_id=1, source_target_pairs={{0,3},{1,0},{2,1},{3,2},{4,7},{5,4},{6,5},{7,6},{8,11},{9,8},{10,9... | collective-permute-start | bytes 393224 | tf_op jit(solution)/shard_map/ppermute | solution.py:354
  6.9 10.1 %collective-permute-start = (bf16[8,64,128]{2,1,0:T(8,128)(2,1)S(1)}, bf16[8,64,128]{2,1,0:T(8,128)(2,1)S(1)}, u32[]{:S(2)}, u32[]{:S(2)}) collective-permute-start(bf16[8,64,128]{2,1,0:T(8,128)(2,1)S(1)} %get-tuple-element.111), channel_id=1, source_target_pairs={{0,1},{1,2},{2,3},{3,0},{4,5},{5,6},{6,7},{7,4},{8,9},{9,10},{10,1... | collective-permute-start | bytes 393224 | tf_op jit(solution)/shard_map/ppermute | solution.py:354
  6.9 11.5 %collective-permute-start.1 = (bf16[8,64,128]{2,1,0:T(8,128)(2,1)S(1)}, bf16[8,64,128]{2,1,0:T(8,128)(2,1)S(1)}, u32[]{:S(2)}, u32[]{:S(2)}) collective-permute-start(bf16[8,64,128]{2,1,0:T(8,128)(2,1)S(1)} %get-tuple-element.113), channel_id=1, source_target_pairs={{0,2},{1,3},{2,0},{3,1},{4,6},{5,7},{6,4},{7,5},{8,10},{9,11},{10,... | collective-permute-start | bytes 393224 | tf_op jit(solution)/shard_map/ppermute | solution.py:354
  18.4 2.7 %collective-permute-start.3 = (bf16[64,64,128]{2,1,0:T(8,128)(2,1)S(1)}, bf16[64,64,128]{2,1,0:T(8,128)(2,1)S(1)}, u32[]{:S(2)}, u32[]{:S(2)}) collective-permute-start(bf16[64,64,128]{2,1,0:T(8,128)(2,1)S(1)} %get-tuple-element.58), channel_id=1, source_target_pairs={{0,4},{4,0},{8,12},{12,8},{16,20},{20,16},{24,28},{28,24},{1,5},{5... | collective-permute-start | bytes 3145736 | tf_op jit(solution)/shard_map/ppermute | solution.py:380
  18.4 9.2 %collective-permute-start.5 = (bf16[16,64,128]{2,1,0:T(8,128)(2,1)S(1)}, bf16[16,64,128]{2,1,0:T(8,128)(2,1)S(1)}, u32[]{:S(2)}, u32[]{:S(2)}) collective-permute-start(bf16[16,64,128]{2,1,0:T(8,128)(2,1)S(1)} %get-tuple-element.62), channel_id=1, source_target_pairs={{0,24},{4,12},{8,0},{12,20},{16,8},{20,28},{24,16},{28,4},{1,25},{... | collective-permute-start | bytes 786440 | tf_op jit(solution)/shard_map/ppermute | solution.py:384
  21.3 11.9 %collective-permute-start.4 = (bf16[16,64,128]{2,1,0:T(8,128)(2,1)S(1)}, bf16[16,64,128]{2,1,0:T(8,128)(2,1)S(1)}, u32[]{:S(2)}, u32[]{:S(2)}) collective-permute-start(bf16[16,64,128]{2,1,0:T(8,128)(2,1)S(1)} %get-tuple-element.61), channel_id=1, source_target_pairs={{0,28},{4,8},{8,4},{12,16},{16,12},{20,24},{24,20},{28,0},{1,29},{... | collective-permute-start | bytes 786440 | tf_op jit(solution)/shard_map/ppermute | solution.py:385
  23.6 13.4 %collective-permute-start.9 = (bf16[10,64,128]{2,1,0:T(8,128)(2,1)S(1)}, bf16[10,64,128]{2,1,0:T(8,128)(2,1)S(1)}, u32[]{:S(2)}, u32[]{:S(2)}) collective-permute-start(bf16[10,64,128]{2,1,0:T(8,128)(2,1)S(1)} %get-tuple-element.73), channel_id=1, source_target_pairs={{0,1},{1,2},{2,3},{3,0},{4,5},{5,6},{6,7},{7,4},{8,9},{9,10},{10,1... | collective-permute-start | bytes 491528 | tf_op jit(solution)/shard_map/ppermute | solution.py:354
  24.3 13.8 %collective-permute-start.10 = (bf16[10,64,128]{2,1,0:T(8,128)(2,1)S(1)}, bf16[10,64,128]{2,1,0:T(8,128)(2,1)S(1)}, u32[]{:S(2)}, u32[]{:S(2)}) collective-permute-start(bf16[10,64,128]{2,1,0:T(8,128)(2,1)S(1)} %get-tuple-element.74), channel_id=1, source_target_pairs={{0,2},{1,3},{2,0},{3,1},{4,6},{5,7},{6,4},{7,5},{8,10},{9,11},{10,... | collective-permute-start | bytes 491528 | tf_op jit(solution)/shard_map/ppermute | solution.py:354
  26.4 13.5 %collective-permute-start.11 = (bf16[10,64,128]{2,1,0:T(8,128)(2,1)S(1)}, bf16[10,64,128]{2,1,0:T(8,128)(2,1)S(1)}, u32[]{:S(2)}, u32[]{:S(2)}) collective-permute-start(bf16[10,64,128]{2,1,0:T(8,128)(2,1)S(1)} %get-tuple-element.75), channel_id=1, source_target_pairs={{0,3},{1,0},{2,1},{3,2},{4,7},{5,4},{6,5},{7,6},{8,11},{9,8},{10,9... | collective-permute-start | bytes 491528 | tf_op jit(solution)/shard_map/ppermute | solution.py:354
  27.6 23.8 %collective-permute-start.16 = (bf16[16,64,128]{2,1,0:T(8,128)(2,1)S(1)}, bf16[16,64,128]{2,1,0:T(8,128)(2,1)S(1)}, u32[]{:S(2)}, u32[]{:S(2)}) collective-permute-start(bf16[16,64,128]{2,1,0:T(8,128)(2,1)S(1)} %get-tuple-element.93), channel_id=1, source_target_pairs={{0,24},{4,12},{8,0},{12,20},{16,8},{20,28},{24,16},{28,4},{1,25},{... | collective-permute-start | bytes 786440 | tf_op jit(solution)/shard_map/ppermute | solution.py:384
  33.2 18.8 %collective-permute-start.15 = (bf16[16,64,128]{2,1,0:T(8,128)(2,1)S(1)}, bf16[16,64,128]{2,1,0:T(8,128)(2,1)S(1)}, u32[]{:S(2)}, u32[]{:S(2)}) collective-permute-start(bf16[16,64,128]{2,1,0:T(8,128)(2,1)S(1)} %get-tuple-element.71), channel_id=1, source_target_pairs={{0,28},{4,8},{8,4},{12,16},{16,12},{20,24},{24,20},{28,0},{1,29},{... | collective-permute-start | bytes 786440 | tf_op jit(solution)/shard_map/ppermute | solution.py:385
  37.0 6.5 %collective-permute-start.6 = (bf16[4,64,128]{2,1,0:T(8,128)(2,1)S(1)}, bf16[4,64,128]{2,1,0:T(8,128)(2,1)S(1)}, u32[]{:S(2)}, u32[]{:S(2)}) collective-permute-start(bf16[4,64,128]{2,1,0:T(8,128)(2,1)S(1)} %get-tuple-element.64), channel_id=1, source_target_pairs={{0,1},{1,2},{2,3},{3,0},{4,5},{5,6},{6,7},{7,4},{8,9},{9,10},{10,1... | collective-permute-start | bytes 196616 | tf_op jit(solution)/shard_map/ppermute | solution.py:354
  38.1 7.7 %collective-permute-start.7 = (bf16[4,64,128]{2,1,0:T(8,128)(2,1)S(1)}, bf16[4,64,128]{2,1,0:T(8,128)(2,1)S(1)}, u32[]{:S(2)}, u32[]{:S(2)}) collective-permute-start(bf16[4,64,128]{2,1,0:T(8,128)(2,1)S(1)} %get-tuple-element.65), channel_id=1, source_target_pairs={{0,2},{1,3},{2,0},{3,1},{4,6},{5,7},{6,4},{7,5},{8,10},{9,11},{10,... | collective-permute-start | bytes 196616 | tf_op jit(solution)/shard_map/ppermute | solution.py:354
  39.9 6.8 %collective-permute-start.8 = (bf16[4,64,128]{2,1,0:T(8,128)(2,1)S(1)}, bf16[4,64,128]{2,1,0:T(8,128)(2,1)S(1)}, u32[]{:S(2)}, u32[]{:S(2)}) collective-permute-start(bf16[4,64,128]{2,1,0:T(8,128)(2,1)S(1)} %get-tuple-element.66), channel_id=1, source_target_pairs={{0,3},{1,0},{2,1},{3,2},{4,7},{5,4},{6,5},{7,6},{8,11},{9,8},{10,9... | collective-permute-start | bytes 196616 | tf_op jit(solution)/shard_map/ppermute | solution.py:354
  47.5 11.4 %collective-permute-start.12 = (bf16[4,64,128]{2,1,0:T(8,128)(2,1)S(1)}, bf16[4,64,128]{2,1,0:T(8,128)(2,1)S(1)}, u32[]{:S(2)}, u32[]{:S(2)}) collective-permute-start(bf16[4,64,128]{2,1,0:T(8,128)(2,1)S(1)} %get-tuple-element.89), channel_id=1, source_target_pairs={{0,1},{1,2},{2,3},{3,0},{4,5},{5,6},{6,7},{7,4},{8,9},{9,10},{10,1... | collective-permute-start | bytes 196616 | tf_op jit(solution)/shard_map/ppermute | solution.py:354
  49.6 5.7 %collective-permute-start.23 = (bf16[2,64,128]{2,1,0:T(8,128)(2,1)S(1)}, bf16[2,64,128]{2,1,0:T(8,128)(2,1)S(1)}, u32[]{:S(2)}, u32[]{:S(2)}) collective-permute-start(bf16[2,64,128]{2,1,0:T(8,128)(2,1)S(1)} %get-tuple-element.107), channel_id=1, source_target_pairs={{0,3},{1,0},{2,1},{3,2},{4,7},{5,4},{6,5},{7,6},{8,11},{9,8},{10,9... | collective-permute-start | bytes 98312 | tf_op jit(solution)/shard_map/ppermute | solution.py:354
  51.4 6.6 %collective-permute-start.24 = (bf16[2,64,128]{2,1,0:T(8,128)(2,1)S(1)}, bf16[2,64,128]{2,1,0:T(8,128)(2,1)S(1)}, u32[]{:S(2)}, u32[]{:S(2)}) collective-permute-start(bf16[2,64,128]{2,1,0:T(8,128)(2,1)S(1)} %get-tuple-element.108), channel_id=1, source_target_pairs={{0,2},{1,3},{2,0},{3,1},{4,6},{5,7},{6,4},{7,5},{8,10},{9,11},{10,... | collective-permute-start | bytes 98312 | tf_op jit(solution)/shard_map/ppermute | solution.py:354
  51.4 6.6 %collective-permute-start.25 = (bf16[2,64,128]{2,1,0:T(8,128)(2,1)S(1)}, bf16[2,64,128]{2,1,0:T(8,128)(2,1)S(1)}, u32[]{:S(2)}, u32[]{:S(2)}) collective-permute-start(bf16[2,64,128]{2,1,0:T(8,128)(2,1)S(1)} %get-tuple-element.109), channel_id=1, source_target_pairs={{0,1},{1,2},{2,3},{3,0},{4,5},{5,6},{6,7},{7,4},{8,9},{9,10},{10,1... | collective-permute-start | bytes 98312 | tf_op jit(solution)/shard_map/ppermute | solution.py:354
  52.0 9.9 %collective-permute-start.13 = (bf16[4,64,128]{2,1,0:T(8,128)(2,1)S(1)}, bf16[4,64,128]{2,1,0:T(8,128)(2,1)S(1)}, u32[]{:S(2)}, u32[]{:S(2)}) collective-permute-start(bf16[4,64,128]{2,1,0:T(8,128)(2,1)S(1)} %get-tuple-element.90), channel_id=1, source_target_pairs={{0,2},{1,3},{2,0},{3,1},{4,6},{5,7},{6,4},{7,5},{8,10},{9,11},{10,... | collective-permute-start | bytes 196616 | tf_op jit(solution)/shard_map/ppermute | solution.py:354
  55.3 6.7 %collective-permute-start.14 = (bf16[4,64,128]{2,1,0:T(8,128)(2,1)S(1)}, bf16[4,64,128]{2,1,0:T(8,128)(2,1)S(1)}, u32[]{:S(2)}, u32[]{:S(2)}) collective-permute-start(bf16[4,64,128]{2,1,0:T(8,128)(2,1)S(1)} %get-tuple-element.91), channel_id=1, source_target_pairs={{0,3},{1,0},{2,1},{3,2},{4,7},{5,4},{6,5},{7,6},{8,11},{9,8},{10,9... | collective-permute-start | bytes 196616 | tf_op jit(solution)/shard_map/ppermute | solution.py:354
  58.0 6.1 %collective-permute-start.17 = (bf16[4,64,128]{2,1,0:T(8,128)(2,1)S(1)}, bf16[4,64,128]{2,1,0:T(8,128)(2,1)S(1)}, u32[]{:S(2)}, u32[]{:S(2)}) collective-permute-start(bf16[4,64,128]{2,1,0:T(8,128)(2,1)S(1)} %get-tuple-element.95), channel_id=1, source_target_pairs={{0,1},{1,2},{2,3},{3,0},{4,5},{5,6},{6,7},{7,4},{8,9},{9,10},{10,1... | collective-permute-start | bytes 196616 | tf_op jit(solution)/shard_map/ppermute | solution.py:354
  58.0 6.1 %collective-permute-start.18 = (bf16[4,64,128]{2,1,0:T(8,128)(2,1)S(1)}, bf16[4,64,128]{2,1,0:T(8,128)(2,1)S(1)}, u32[]{:S(2)}, u32[]{:S(2)}) collective-permute-start(bf16[4,64,128]{2,1,0:T(8,128)(2,1)S(1)} %get-tuple-element.96), channel_id=1, source_target_pairs={{0,2},{1,3},{2,0},{3,1},{4,6},{5,7},{6,4},{7,5},{8,10},{9,11},{10,... | collective-permute-start | bytes 196616 | tf_op jit(solution)/shard_map/ppermute | solution.py:354
  58.9 5.9 %collective-permute-start.19 = (bf16[4,64,128]{2,1,0:T(8,128)(2,1)S(1)}, bf16[4,64,128]{2,1,0:T(8,128)(2,1)S(1)}, u32[]{:S(2)}, u32[]{:S(2)}) collective-permute-start(bf16[4,64,128]{2,1,0:T(8,128)(2,1)S(1)} %get-tuple-element.97), channel_id=1, source_target_pairs={{0,3},{1,0},{2,1},{3,2},{4,7},{5,4},{6,5},{7,6},{8,11},{9,8},{10,9... | collective-permute-start | bytes 196616 | tf_op jit(solution)/shard_map/ppermute | solution.py:354
  61.9 8.1 %collective-permute-start.26 = (f32[2,64,128]{2,1,0:T(8,128)S(1)}, f32[2,64,128]{2,1,0:T(8,128)S(1)}, u32[]{:S(2)}, u32[]{:S(2)}) collective-permute-start(f32[2,64,128]{2,1,0:T(8,128)S(1)} %convert_add_fusion), channel_id=1, source_target_pairs={{0,4},{4,0},{8,12},{12,8},{16,20},{20,16},{24,28},{28,24},{1,5},{5... | collective-permute-start | bytes 196616 | tf_op jit(solution)/shard_map/ppermute | solution.py:407
  65.6 7.6 %collective-permute-start.20 = (bf16[4,64,128]{2,1,0:T(8,128)(2,1)S(1)}, bf16[4,64,128]{2,1,0:T(8,128)(2,1)S(1)}, u32[]{:S(2)}, u32[]{:S(2)}) collective-permute-start(bf16[4,64,128]{2,1,0:T(8,128)(2,1)S(1)} %get-tuple-element.103), channel_id=1, source_target_pairs={{0,1},{1,2},{2,3},{3,0},{4,5},{5,6},{6,7},{7,4},{8,9},{9,10},{10,1... | collective-permute-start | bytes 196616 | tf_op jit(solution)/shard_map/ppermute | solution.py:354
  67.6 6.2 %collective-permute-start.21 = (bf16[4,64,128]{2,1,0:T(8,128)(2,1)S(1)}, bf16[4,64,128]{2,1,0:T(8,128)(2,1)S(1)}, u32[]{:S(2)}, u32[]{:S(2)}) collective-permute-start(bf16[4,64,128]{2,1,0:T(8,128)(2,1)S(1)} %get-tuple-element.104), channel_id=1, source_target_pairs={{0,2},{1,3},{2,0},{3,1},{4,6},{5,7},{6,4},{7,5},{8,10},{9,11},{10,... | collective-permute-start | bytes 196616 | tf_op jit(solution)/shard_map/ppermute | solution.py:354
  69.5 4.4 %collective-permute-start.22 = (bf16[4,64,128]{2,1,0:T(8,128)(2,1)S(1)}, bf16[4,64,128]{2,1,0:T(8,128)(2,1)S(1)}, u32[]{:S(2)}, u32[]{:S(2)}) collective-permute-start(bf16[4,64,128]{2,1,0:T(8,128)(2,1)S(1)} %get-tuple-element.105), channel_id=1, source_target_pairs={{0,3},{1,0},{2,1},{3,2},{4,7},{5,4},{6,5},{7,6},{8,11},{9,8},{10,9... | collective-permute-start | bytes 196616 | tf_op jit(solution)/shard_map/ppermute | solution.py:354
  70.0 5.2 %collective-permute-start.29 = (f32[2,64,128]{2,1,0:T(8,128)S(1)}, f32[2,64,128]{2,1,0:T(8,128)S(1)}, u32[]{:S(2)}, u32[]{:S(2)}) collective-permute-start(f32[2,64,128]{2,1,0:T(8,128)S(1)} %add.52), channel_id=1, source_target_pairs={{0,24},{4,28},{8,16},{12,20},{16,8},{20,12},{24,0},{28,4},{1,25},{... | collective-permute-start | bytes 196616 | tf_op jit(solution)/shard_map/ppermute | solution.py:409
  72.1 4.3 %collective-permute-start.28 = (f32[2,64,128]{2,1,0:T(8,128)S(1)}, f32[2,64,128]{2,1,0:T(8,128)S(1)}, u32[]{:S(2)}, u32[]{:S(2)}) collective-permute-start(f32[2,64,128]{2,1,0:T(8,128)S(1)} %add.52), channel_id=1, source_target_pairs={{0,16},{4,20},{8,24},{12,28},{16,0},{20,4},{24,8},{28,12},{1,17},{... | collective-permute-start | bytes 196616 | tf_op jit(solution)/shard_map/ppermute | solution.py:409
  73.2 4.3 %collective-permute-start.27 = (f32[2,64,128]{2,1,0:T(8,128)S(1)}, f32[2,64,128]{2,1,0:T(8,128)S(1)}, u32[]{:S(2)}, u32[]{:S(2)}) collective-permute-start(f32[2,64,128]{2,1,0:T(8,128)S(1)} %add.52), channel_id=1, source_target_pairs={{0,8},{4,12},{8,0},{12,4},{16,24},{20,28},{24,16},{28,20},{1,9},{5... | collective-permute-start | bytes 196616 | tf_op jit(solution)/shard_map/ppermute | solution.py:409

commit v11 on v9

--- a/solution.py
+++ b/solution.py
@@ -10,7 +10,7 @@
 
 REACH = 2
 GROUP = 4
-STEP = 4
+STEP = 8
 BF16 = jnp.bfloat16
 F32 = jnp.float32
 MIB = 1 << 20
@@ -38,18 +38,16 @@
     return value & (size - 1)
 
 
-def tiles_kernel(slabs, reps, where, cols, live, weight, cot, mask, tiles, *rest):
+def tiles_kernel(slabs, reps, where, cols, live, cot, mask, tiles, *rest):
     outs, packed, rest = rest[:4], rest[4 : 4 + reps], rest[4 + reps :]
     outs = [outs[0].at[pl.ds(0, cols.shape[1])], outs[0].at[pl.ds(cols.shape[1], cols.shape[1])], *outs[1:]]
-    cot_in, mask_in, weight_in, z, held, first, second, rows, left, sems, z_sems = rest
-    totals = (first, second)
+    cot_in, mask_in, z, held, total, rows, left, sems, z_sems = rest
     slots, blocks = cols.shape
     per_row = slots // GROUP
     window = (2 * REACH + 1) * blocks
     copies = [
         pltpu.make_async_copy(cot, cot_in, z_sems.at[0]),
         pltpu.make_async_copy(mask, mask_in, z_sems.at[1]),
-        pltpu.make_async_copy(weight, weight_in, z_sems.at[2]),
     ]
     for copy in copies:
         copy.start()
@@ -83,8 +81,7 @@
         return carry
 
     def clear(i, carry):
-        for total in totals:
-            total[pl.ds(i * GROUP, GROUP)] = jnp.zeros((GROUP,) + total.shape[1:], F32)
+        total[pl.ds(i * GROUP, GROUP)] = jnp.zeros((GROUP,) + total.shape[1:], F32)
         return carry
 
     lax.fori_loop(0, window // GROUP, clear, 0)
@@ -96,12 +93,9 @@
         return carry
 
     lax.fori_loop(0, blocks, mask_row, 0)
-    nodes = z.shape[2]
     share = blocks // reps
     for s in range(reps):
-        packed[s][:share] = z[pl.ds(wrap(where[1] + s, reps) * share, share)]
-        for h in range(weight.shape[1] // nodes):
-            packed[s][share + h] = weight_in[:, h * nodes : (h + 1) * nodes]
+        packed[s][...] = z[pl.ds(wrap(where[1] + s, reps) * share, share)]
     shift = REACH * blocks - where[0] * blocks
 
     def step(i, ready):
@@ -115,7 +109,7 @@
             for j in range(GROUP):
                 place = wrap(cols[g * GROUP + j, b] + shift, slabs * blocks)
                 place = jnp.where(j < remain, place, window)
-                totals[j % 2][place] += jnp.dot(
+                total[place] += jnp.dot(
                     z_row, held[row * GROUP + j], preferred_element_type=F32
                 )
         return jnp.maximum(ready, need)
@@ -129,40 +123,36 @@
         def store(i, carry, out=out, base=base):
             for k in range(GROUP):
                 at = i * GROUP + k
-                out[at] = (first[base + at] + second[base + at]).astype(BF16)
+                out[at] = total[base + at].astype(BF16)
             return carry
 
         lax.fori_loop(0, blocks // GROUP, store, 0)
 
 
-def contributions(where, cols, live, weight, cot, mask, tiles, slabs, reps):
+def contributions(where, cols, live, cot, mask, tiles, slabs, reps):
     blocks, slots, nodes = tiles.shape[:3]
     features = cot.shape[1]
     window = (2 * REACH + 1) * blocks
     lists = blocks * (slots // GROUP) + slots // GROUP + STEP
-    total = pltpu.VMEM((window + 1, features, nodes), F32)
-    packs = blocks // reps + weight.shape[1] // nodes
     counts = [2 * blocks, blocks, blocks, blocks]
     return pl.pallas_call(
         functools.partial(tiles_kernel, slabs, reps),
         out_shape=[jax.ShapeDtypeStruct((count, features, nodes), BF16) for count in counts]
-        + [jax.ShapeDtypeStruct((packs, features, nodes), BF16)] * reps,
-        in_specs=[smem()] * 3 + [hbm()] * 4,
+        + [jax.ShapeDtypeStruct((blocks // reps, features, nodes), BF16)] * reps,
+        in_specs=[smem()] * 3 + [hbm()] * 3,
         out_specs=[vmem()] * (len(counts) + reps),
         scratch_shapes=[
             pltpu.VMEM(cot.shape, BF16),
             pltpu.VMEM(mask.shape, jnp.int32),
-            pltpu.VMEM(weight.shape, BF16),
             pltpu.VMEM(cot.shape, BF16),
             pltpu.VMEM((blocks * slots, nodes, nodes), BF16),
-            total,
-            total,
+            pltpu.VMEM((window + 1, features, nodes), F32),
             pltpu.SMEM((lists,), jnp.int32),
             pltpu.SMEM((lists,), jnp.int32),
             pltpu.SemaphoreType.DMA((blocks,)),
-            pltpu.SemaphoreType.DMA((3,)),
+            pltpu.SemaphoreType.DMA((2,)),
         ],
-        compiler_params=pltpu.CompilerParams(vmem_limit_bytes=36 * MIB),
+        compiler_params=pltpu.CompilerParams(vmem_limit_bytes=30 * MIB),
         cost_estimate=pl.CostEstimate(
             flops=2 * blocks * slots * features * nodes * nodes,
             bytes_accessed=tiles.size * 2,
@@ -172,7 +162,6 @@
         where,
         in_hbm(cols.T),
         in_hbm(live),
-        in_hbm(weight),
         in_hbm(cot),
         in_hbm(mask),
         in_hbm(tiles.reshape(blocks * slots, nodes, nodes)),
@@ -188,26 +177,26 @@
 
 
 def mix_kernel(reps, first, where, *rest):
-    shares, packed, outs = rest[:reps], rest[reps : 2 * reps], rest[2 * reps : 3 * reps]
+    shares, aggs, outs = rest[:reps], rest[reps : 2 * reps], rest[2 * reps : 3 * reps]
     weights, whole = rest[3 * reps :]
     blocks, features, nodes = outs[0].shape
     lay_features(where, shares, whole)
     for s in range(reps):
         for h in range(weights.shape[1] // nodes):
             rows, columns = pl.ds(s * features, features), pl.ds(h * nodes, nodes)
-            weights[rows, columns] = packed[(reps - s) % reps][first + h]
+            weights[rows, columns] = aggs[(reps - s) % reps][first + h]
     for b in range(blocks):
         mixed = jnp.dot(weights[...], whole[b], preferred_element_type=F32)
         for s in range(reps):
             outs[s][b] = mixed[s * features : (s + 1) * features].astype(BF16)
 
 
-def mix(where, shares, packed, first):
+def mix(where, shares, aggs):
     reps = len(shares)
     blocks, features, nodes = shares[0].shape
     width = reps * features
     return pl.pallas_call(
-        functools.partial(mix_kernel, reps, first),
+        functools.partial(mix_kernel, reps, blocks),
         out_shape=[jax.ShapeDtypeStruct((blocks, features, nodes), BF16)] * reps,
         in_specs=[smem()] + [vmem()] * (2 * reps),
         out_specs=[vmem()] * reps,
@@ -218,16 +207,16 @@
             bytes_accessed=4 * blocks * nodes * width,
             transcendentals=0,
         ),
-    )(where, *shares, *packed)
+    )(where, *shares, *aggs)
 
 
 def weight_kernel(reps, where, *rest):
     packed, aggs, outs = rest[:reps], rest[reps : 2 * reps], rest[2 * reps : 3 * reps]
     whole_z, whole_a = rest[3 * reps :]
-    blocks, features, nodes = aggs[0].shape
+    blocks, features, nodes = packed[0].shape
     lay_features(where, packed, whole_z)
     for s in range(reps):
-        whole_a[:, pl.ds(s * features, features), :] = aggs[s][...]
+        whole_a[:, pl.ds(s * features, features), :] = aggs[s][:blocks]
     total = jnp.zeros((whole_a.shape[1], whole_z.shape[1]), F32)
     for b in range(blocks):
         total += lax.dot_general(
@@ -241,7 +230,7 @@
 
 def weight_partial(where, packed, aggs):
     reps = len(packed)
-    blocks, features, nodes = aggs[0].shape
+    blocks, features, nodes = packed[0].shape
     width = reps * features
     return pl.pallas_call(
         functools.partial(weight_kernel, reps),
@@ -306,6 +295,37 @@
     )(where, aside, *terms)
 
 
+def pack_kernel(reps, where, agg, weight, *rest):
+    outs, sems = rest[:reps], rest[reps]
+    features, nodes = agg.shape[1:]
+    share = agg.shape[0] // reps
+    pieces = weight.shape[1] // nodes
+    copies = []
+    for s, out in enumerate(outs):
+        first = wrap(where[1] + s, reps) * share
+        copies.append((agg.at[pl.ds(first, share)], out.at[pl.ds(0, share)]))
+        for h in range(pieces):
+            copies.append((weight.at[:, pl.ds(h * nodes, nodes)], out.at[share + h]))
+    copies = [pltpu.make_async_copy(*ends, sems.at[i]) for i, ends in enumerate(copies)]
+    for copy in copies:
+        copy.start()
+    for copy in copies:
+        copy.wait()
+
+
+def pack(where, agg, weight, reps):
+    blocks, features, nodes = agg.shape
+    share, pieces = blocks // reps, weight.shape[1] // nodes
+    return pl.pallas_call(
+        functools.partial(pack_kernel, reps),
+        out_shape=[jax.ShapeDtypeStruct((share + pieces, features, nodes), BF16)] * reps,
+        in_specs=[smem(), hbm(), hbm()],
+        out_specs=[vmem()] * reps,
+        scratch_shapes=[pltpu.SemaphoreType.DMA((reps * (1 + pieces),))],
+        compiler_params=pltpu.CompilerParams(vmem_limit_bytes=2 * MIB),
+    )(where, in_hbm(agg), in_hbm(weight))
+
+
 def lay_kernel(reps, where, *rest):
     shares, out, sems = rest[:reps], rest[reps], rest[reps + 1]
     blocks = shares[0].shape[0]
@@ -338,26 +358,18 @@
     return lax.ppermute(value, "rep", [(i, (i + steps) % reps) for i in range(reps)])
 
 
-def node_share(value, steps):
-    reps = lax.axis_size("rep")
-    blocks = value.shape[0] // reps
-    first = lax.rem(lax.axis_index("rep") + steps, reps) * blocks
-    return lax.dynamic_slice_in_dim(value, first, blocks, 0)
-
-
 def on_device(cotangent, relu_mask, aggregated, weight, tiles, col_block, live_count):
     blocks, features, nodes = cotangent.shape
     slabs, reps = lax.axis_size("blk"), lax.axis_size("rep")
     width = weight.shape[1]
-    share = blocks // reps
     where = jnp.stack([lax.axis_index("blk"), lax.axis_index("rep")]).astype(jnp.int32)
 
     pair = [(i, i ^ 1) for i in range(slabs)]
     to_one = [(i, (i + (1 if i % 2 else -1)) % slabs) for i in range(slabs)]
     to_two = [(i, (i + (2 if i % 2 else -2)) % slabs) for i in range(slabs)]
-    aggs = [shift(node_share(aggregated, s), s) for s in range(reps)]
+    aggs = [shift(value, s) for s, value in enumerate(pack(where, aggregated, weight, reps))]
     aside, own, one, two, *packed = contributions(
-        where, col_block, live_count, weight, cotangent, relu_mask, tiles, slabs, reps
+        where, col_block, live_count, cotangent, relu_mask, tiles, slabs, reps
     )
     aside, aggs = lax.optimization_barrier((aside, aggs))
     aside = lax.ppermute(aside, "blk", pair)
@@ -372,7 +384,7 @@
     own, grad_w = lax.optimization_barrier((own, grad_w))
     shares = total_shares(where, aside, [own, one_in, two_in], reps)
     shares = [shift(value, s) for s, value in enumerate(shares)]
-    outs = [shift(value, s) for s, value in enumerate(mix(where, shares, packed, share))]
+    outs = [shift(value, s) for s, value in enumerate(mix(where, shares, aggs))]
     input_grad = lay_blocks(where, outs, cotangent.shape)
 
     grad_w = sum(shift(part, -s).astype(F32) for s, part in enumerate(grad_w))

time: 74.4 us -> 75.9 us (1.020)
  Pallas kernels: 12.8 us -> 15.1 us
  starting transfers between devices: 36.3 us -> 38.4 us
  waiting for transfers between devices: 21.8 us -> 20.2 us
  local copies, waits for them, and re-layouts: 1.14 us -> 0 us
    ppermute x15, waiting for transfers between devices: 20.3 us -> 17.3 us  [shift(): lax.ppermute(value, 'rep', [(i, (i + steps) % reps) for i in range(reps)])]
    pallas_call x1 -> x2, Pallas kernels: 1 us -> 2.84 us  [the longest x1 1.83 us: pack(): pl.pallas_call(functools.partial(pack_kernel, reps), out_shape=[jax.Shape...]
    ppermute x1, waiting for transfers between devices: 0.01 us -> 1.66 us  [on_device(): one_in = lax.ppermute(one, 'blk', to_one)]
    ppermute x15, starting transfers between devices: 28 us -> 29.4 us  [shift(): lax.ppermute(value, 'rep', [(i, (i + steps) % reps) for i in range(reps)])]
    dynamic_slice x1 -> x0, local copies, waits for them, and re-layouts: 1.14 us -> none  [node_share(): return lax.dynamic_slice_in_dim(value, first, blocks, 0)]
  transfers between devices with their start and end apart: 22 -> 22, of which waited for: 9 -> 8; matrix products, arithmetic and copies ran while one was open for 1% -> 1% of each run, Pallas kernels for 16% -> 16%
where the time goes in v11:
time: 75.9 us; the launch traced here: 75.2 us
  starting transfers between devices  38.4 us (51%)
  waiting for transfers between devices  20.2 us (27%)
  Pallas kernels  15.1 us (20%)
    ppermute x15, starting transfers between devices, shift(): lax.ppermute(value, 'rep', [(i, (i + steps) % reps) for i in range(reps)])  29.4 us
    ppermute x15, waiting for transfers between devices, shift(): lax.ppermute(value, 'rep', [(i, (i + steps) % reps) for i in range(reps)])  17.3 us
    pallas_call x1, Pallas kernels, contributions(): pl.pallas_call(functools.partial(tiles_kernel, slabs, reps), out_shape=[j...  8.88 us
    ppermute x3, starting transfers between devices, on_device(): lax.ppermute(grad_w, 'blk', [(i, i ^ step) for i in range(slabs)])  3.55 us
    ppermute x1, starting transfers between devices, on_device(): two_in = lax.ppermute(two, 'blk', to_two)  2.97 us
    ppermute x1, starting transfers between devices, on_device(): one_in = lax.ppermute(one, 'blk', to_one)  2.4 us
    pallas_call x1, Pallas kernels, pack(): pl.pallas_call(functools.partial(pack_kernel, reps), out_shape=[jax.Shape...  1.83 us
    ppermute x1, waiting for transfers between devices, on_device(): one_in = lax.ppermute(one, 'blk', to_one)  1.66 us
  transfers between devices with their start and end apart: 22, of which 8 were waited for; matrix products, arithmetic and copies ran while one was open for 1% of the time, Pallas kernels for 16%

profile of v11, /device:TPU:0, one launch (start us, length us, event | category | flops | bytes accessed | tf_op | source)
XLA Modules:
  0.0 75.2 jit_solution(16376962460247346742)
XLA Ops:
  0.7 1.8 %shard_map.87 = (bf16[10,64,128]{2,1,0:T(8,128)(2,1)S(1)}, bf16[10,64,128]{2,1,0:T(8,128)(2,1)S(1)}, bf16[10,64,128]{2,1,0:T(8,128)(2,1)S(1)}, bf16[10,64,128]{2,1,0:T(8,128)(2,1)S(1)}) custom-call(s32[2]{0:T(128)S(1)} %pad_add_fusion.where, bf16[32,64,128]{2,1,0:T(8,128)(2,1)} %agg.1, bf16[64,256]{1,0:T(8,128)(2,1)} %weight.1), custom_call_target="tpu_custom_call" | custom-call | tf_op jit(solution)/shard_map/pallas_call | solution.py:319
  2.6 3.1 %collective-permute-start = (bf16[10,64,128]{2,1,0:T(8,128)(2,1)S(1)}, bf16[10,64,128]{2,1,0:T(8,128)(2,1)S(1)}, u32[]{:S(2)}, u32[]{:S(2)}) collective-permute-start(bf16[10,64,128]{2,1,0:T(8,128)(2,1)S(1)} %get-tuple-element.42), channel_id=1, source_target_pairs={{0,1},{1,2},{2,3},{3,0},{4,5},{5,6},{6,7},{7,4},{8,9},{9,10},{10,1... | collective-permute-start | bytes 491528 | tf_op jit(solution)/shard_map/ppermute | solution.py:358
  5.6 2.6 %collective-permute-start.1 = (bf16[10,64,128]{2,1,0:T(8,128)(2,1)S(1)}, bf16[10,64,128]{2,1,0:T(8,128)(2,1)S(1)}, u32[]{:S(2)}, u32[]{:S(2)}) collective-permute-start(bf16[10,64,128]{2,1,0:T(8,128)(2,1)S(1)} %get-tuple-element.43), channel_id=1, source_target_pairs={{0,2},{1,3},{2,0},{3,1},{4,6},{5,7},{6,4},{7,5},{8,10},{9,11},{10,... | collective-permute-start | bytes 491528 | tf_op jit(solution)/shard_map/ppermute | solution.py:358
  8.2 1.3 %collective-permute-start.2 = (bf16[10,64,128]{2,1,0:T(8,128)(2,1)S(1)}, bf16[10,64,128]{2,1,0:T(8,128)(2,1)S(1)}, u32[]{:S(2)}, u32[]{:S(2)}) collective-permute-start(bf16[10,64,128]{2,1,0:T(8,128)(2,1)S(1)} %get-tuple-element.44), channel_id=1, source_target_pairs={{0,3},{1,0},{2,1},{3,2},{4,7},{5,4},{6,5},{7,6},{8,11},{9,8},{10,9... | collective-permute-start | bytes 491528 | tf_op jit(solution)/shard_map/ppermute | solution.py:358
  9.6 8.9 %shard_map.86 = (bf16[64,64,128]{2,1,0:T(8,128)(2,1)S(1)}, bf16[32,64,128]{2,1,0:T(8,128)(2,1)S(1)}, bf16[32,64,128]{2,1,0:T(8,128)(2,1)S(1)}, bf16[32,64,128]{2...) custom-call(s32[2]{0:T(128)S(1)} %pad_add_fusion.where, ...), custom_call_target="tpu_custom_call" | custom-call | flops 1073741824 | bytes 16777216 | tf_op jit(solution)/shard_map/pallas_call | solution.py:138
  19.0 3.0 %collective-permute-start.8 = (bf16[32,64,128]{2,1,0:T(8,128)(2,1)S(1)}, bf16[32,64,128]{2,1,0:T(8,128)(2,1)S(1)}, u32[]{:S(2)}, u32[]{:S(2)}) collective-permute-start(bf16[32,64,128]{2,1,0:T(8,128)(2,1)S(1)} %get-tuple-element.65), channel_id=1, source_target_pairs={{0,24},{4,12},{8,0},{12,20},{16,8},{20,28},{24,16},{28,4},{1,25},{... | collective-permute-start | bytes 1572872 | tf_op jit(solution)/shard_map/ppermute | solution.py:376
  22.2 2.4 %collective-permute-start.7 = (bf16[32,64,128]{2,1,0:T(8,128)(2,1)S(1)}, bf16[32,64,128]{2,1,0:T(8,128)(2,1)S(1)}, u32[]{:S(2)}, u32[]{:S(2)}) collective-permute-start(bf16[32,64,128]{2,1,0:T(8,128)(2,1)S(1)} %shard_map.88), channel_id=1, source_target_pairs={{0,28},{4,8},{8,4},{12,16},{16,12},{20,24},{24,20},{28,0},{1,29},{... | collective-permute-start | bytes 1572872 | tf_op jit(solution)/shard_map/ppermute | solution.py:378
  24.6 3.5 %collective-permute-start.4 = (bf16[8,64,128]{2,1,0:T(8,128)(2,1)S(1)}, bf16[8,64,128]{2,1,0:T(8,128)(2,1)S(1)}, u32[]{:S(2)}, u32[]{:S(2)}) collective-permute-start(bf16[8,64,128]{2,1,0:T(8,128)(2,1)S(1)} %get-tuple-element.53), channel_id=1, source_target_pairs={{0,1},{1,2},{2,3},{3,0},{4,5},{5,6},{6,7},{7,4},{8,9},{9,10},{10,1... | collective-permute-start | bytes 393224 | tf_op jit(solution)/shard_map/ppermute | solution.py:358
  28.1 1.6 %collective-permute-start.5 = (bf16[8,64,128]{2,1,0:T(8,128)(2,1)S(1)}, bf16[8,64,128]{2,1,0:T(8,128)(2,1)S(1)}, u32[]{:S(2)}, u32[]{:S(2)}) collective-permute-start(bf16[8,64,128]{2,1,0:T(8,128)(2,1)S(1)} %get-tuple-element.54), channel_id=1, source_target_pairs={{0,2},{1,3},{2,0},{3,1},{4,6},{5,7},{6,4},{7,5},{8,10},{9,11},{10,... | collective-permute-start | bytes 393224 | tf_op jit(solution)/shard_map/ppermute | solution.py:358
  29.8 0.7 collective-permute-start.6
  30.5 3.2 %collective-permute-done.4.rest_1_ = bf16[8,64,128]{2,1,0:T(8,128)(2,1)S(1)} collective-permute-done((bf16[8,64,128]{2,1,0:T(8,128)(2,1)S(1)}, bf16[8,64,128]{2,1,0:T(8,128)(2,1)S(1)}, u32[]{:S(2)}, u32[]{:S(2)}) %collective-permute-start.4) | collective-permute-done | bytes 131104 | tf_op jit(solution)/shard_map/ppermute | solution.py:358
  33.7 4.3 %collective-permute-done.5.rest_2_ = bf16[8,64,128]{2,1,0:T(8,128)(2,1)S(1)} collective-permute-done((bf16[8,64,128]{2,1,0:T(8,128)(2,1)S(1)}, bf16[8,64,128]{2,1,0:T(8,128)(2,1)S(1)}, u32[]{:S(2)}, u32[]{:S(2)}) %collective-permute-start.5) | collective-permute-done | bytes 131104 | tf_op jit(solution)/shard_map/ppermute | solution.py:358
  38.0 1.0 %shard_map.89 = (bf16[2,64,128]{2,1,0:T(8,128)(2,1)S(1)}, bf16[2,64,128]{2,1,0:T(8,128)(2,1)S(1)}, bf16[2,64,128]{2,1,0:T(8,128)(2,1)S(1)}, bf16[2,64,128]{2,1,0:T(8,128)(2,1)S(1)}) custom-call(s32[2]{0:T(128)S(1)} %pad_add_fusion.where, bf16[8,64,128]{2,1,0:T(8,128)(2,1)S(1)} %get-tuple-element.52.rest_0_, ...), custom_call_target="tpu_custom_call" | custom-call | flops 134217728 | bytes 1179648 | tf_op jit(solution)/shard_map/pallas_call | solution.py:235
  39.0 4.1 %collective-permute-start.15 = (bf16[2,64,128]{2,1,0:T(8,128)(2,1)S(1)}, bf16[2,64,128]{2,1,0:T(8,128)(2,1)S(1)}, u32[]{:S(2)}, u32[]{:S(2)}) collective-permute-start(bf16[2,64,128]{2,1,0:T(8,128)(2,1)S(1)} %get-tuple-element.75), channel_id=1, source_target_pairs={{0,3},{1,0},{2,1},{3,2},{4,7},{5,4},{6,5},{7,6},{8,11},{9,8},{10,9... | collective-permute-start | bytes 98312 | tf_op jit(solution)/shard_map/ppermute | solution.py:358
  43.1 0.7 collective-permute-start.16
  43.8 1.7 %collective-permute-done.7.rest_1_ = bf16[32,64,128]{2,1,0:T(8,128)(2,1)S(1)} collective-permute-done((bf16[32,64,128]{2,1,0:T(8,128)(2,1)S(1)}, bf16[32,64,128]{2,1,0:T(8,128)(2,1)S(1)}, u32[]{:S(2)}, u32[]{:S(2)}) %collective-permute-start.7) | collective-permute-done | bytes 524320 | tf_op jit(solution)/shard_map/ppermute | solution.py:378
  45.5 0.8 %shard_map.90 = (bf16[8,64,128]{2,1,0:T(8,128)(2,1)S(1)}, bf16[8,64,128]{2,1,0:T(8,128)(2,1)S(1)}, bf16[8,64,128]{2,1,0:T(8,128)(2,1)S(1)}, bf16[8,64,128]{2,1,0:T(8,128)(2,1)S(1)}) custom-call(s32[2]{0:T(128)S(1)} %pad_add_fusion.where, bf16[64,64,128]{2,1,0:T(8,128)(2,1)S(1)} %collective-permute-done.3.other.aside, ...), custom_call_target="tpu_custom_call" | custom-call | flops 1048576 | bytes 2621440 | tf_op jit(solution)/shard_map/pallas_call | solution.py:286
  46.3 3.5 %collective-permute-start.9 = (bf16[8,64,128]{2,1,0:T(8,128)(2,1)S(1)}, bf16[8,64,128]{2,1,0:T(8,128)(2,1)S(1)}, u32[]{:S(2)}, u32[]{:S(2)}) collective-permute-start(bf16[8,64,128]{2,1,0:T(8,128)(2,1)S(1)} %get-tuple-element.67), channel_id=1, source_target_pairs={{0,1},{1,2},{2,3},{3,0},{4,5},{5,6},{6,7},{7,4},{8,9},{9,10},{10,1... | collective-permute-start | bytes 393224 | tf_op jit(solution)/shard_map/ppermute | solution.py:358
  49.8 1.7 %collective-permute-start.10 = (bf16[8,64,128]{2,1,0:T(8,128)(2,1)S(1)}, bf16[8,64,128]{2,1,0:T(8,128)(2,1)S(1)}, u32[]{:S(2)}, u32[]{:S(2)}) collective-permute-start(bf16[8,64,128]{2,1,0:T(8,128)(2,1)S(1)} %get-tuple-element.68), channel_id=1, source_target_pairs={{0,2},{1,3},{2,0},{3,1},{4,6},{5,7},{6,4},{7,5},{8,10},{9,11},{10,... | collective-permute-start | bytes 393224 | tf_op jit(solution)/shard_map/ppermute | solution.py:358
  51.5 0.8 %collective-permute-start.11 = (bf16[8,64,128]{2,1,0:T(8,128)(2,1)S(1)}, bf16[8,64,128]{2,1,0:T(8,128)(2,1)S(1)}, u32[]{:S(2)}, u32[]{:S(2)}) collective-permute-start(bf16[8,64,128]{2,1,0:T(8,128)(2,1)S(1)} %get-tuple-element.69), channel_id=1, source_target_pairs={{0,3},{1,0},{2,1},{3,2},{4,7},{5,4},{6,5},{7,6},{8,11},{9,8},{10,9... | collective-permute-start | bytes 393224 | tf_op jit(solution)/shard_map/ppermute | solution.py:358
  52.4 1.2 %collective-permute-done.18 = f32[2,64,128]{2,1,0:T(8,128)S(1)} collective-permute-done((f32[2,64,128]{2,1,0:T(8,128)S(1)}, f32[2,64,128]{2,1,0:T(8,128)S(1)}, u32[]{:S(2)}, u32[]{:S(2)}) %collective-permute-start.18) | collective-permute-done | bytes 65568 | tf_op jit(solution)/shard_map/ppermute | solution.py:391
  53.6 1.7 %collective-permute-start.21 = (f32[2,64,128]{2,1,0:T(8,128)S(1)}, f32[2,64,128]{2,1,0:T(8,128)S(1)}, u32[]{:S(2)}, u32[]{:S(2)}) collective-permute-start(f32[2,64,128]{2,1,0:T(8,128)S(1)} %add.24), channel_id=1, source_target_pairs={{0,24},{4,28},{8,16},{12,20},{16,8},{20,12},{24,0},{28,4},{1,25},{... | collective-permute-start | bytes 196616 | tf_op jit(solution)/shard_map/ppermute | solution.py:393
  55.4 0.7 collective-permute-start.20
  56.1 1.1 %collective-permute-start.19 = (f32[2,64,128]{2,1,0:T(8,128)S(1)}, f32[2,64,128]{2,1,0:T(8,128)S(1)}, u32[]{:S(2)}, u32[]{:S(2)}) collective-permute-start(f32[2,64,128]{2,1,0:T(8,128)S(1)} %add.24), channel_id=1, source_target_pairs={{0,8},{4,12},{8,0},{12,4},{16,24},{20,28},{24,16},{28,20},{1,9},{5... | collective-permute-start | bytes 196616 | tf_op jit(solution)/shard_map/ppermute | solution.py:393
  57.2 2.8 %collective-permute-done.10.rest_2_ = bf16[8,64,128]{2,1,0:T(8,128)(2,1)S(1)} collective-permute-done((bf16[8,64,128]{2,1,0:T(8,128)(2,1)S(1)}, bf16[8,64,128]{2,1,0:T(8,128)(2,1)S(1)}, u32[]{:S(2)}, u32[]{:S(2)}) %collective-permute-start.10) | collective-permute-done | bytes 131104 | tf_op jit(solution)/shard_map/ppermute | solution.py:358
  60.0 1.0 %shard_map.91 = (bf16[8,64,128]{2,1,0:T(8,128)(2,1)S(1)}, bf16[8,64,128]{2,1,0:T(8,128)(2,1)S(1)}, bf16[8,64,128]{2,1,0:T(8,128)(2,1)S(1)}, bf16[8,64,128]{2,1,0:T(8,128)(2,1)S(1)}) custom-call(s32[2]{0:T(128)S(1)} %pad_add_fusion.where, bf16[8,64,128]{2,1,0:T(8,128)(2,1)S(1)} %get-tuple-element.66.rest_0_, ...), custom_call_target="tpu_custom_call" | custom-call | flops 134217728 | bytes 1048576 | tf_op jit(solution)/shard_map/pallas_call | solution.py:198
  61.0 3.3 %collective-permute-start.12 = (bf16[8,64,128]{2,1,0:T(8,128)(2,1)S(1)}, bf16[8,64,128]{2,1,0:T(8,128)(2,1)S(1)}, u32[]{:S(2)}, u32[]{:S(2)}) collective-permute-start(bf16[8,64,128]{2,1,0:T(8,128)(2,1)S(1)} %get-tuple-element.71), channel_id=1, source_target_pairs={{0,1},{1,2},{2,3},{3,0},{4,5},{5,6},{6,7},{7,4},{8,9},{9,10},{10,1... | collective-permute-start | bytes 393224 | tf_op jit(solution)/shard_map/ppermute | solution.py:358
  64.3 1.3 %collective-permute-start.13 = (bf16[8,64,128]{2,1,0:T(8,128)(2,1)S(1)}, bf16[8,64,128]{2,1,0:T(8,128)(2,1)S(1)}, u32[]{:S(2)}, u32[]{:S(2)}) collective-permute-start(bf16[8,64,128]{2,1,0:T(8,128)(2,1)S(1)} %get-tuple-element.72), channel_id=1, source_target_pairs={{0,2},{1,3},{2,0},{3,1},{4,6},{5,7},{6,4},{7,5},{8,10},{9,11},{10,... | collective-permute-start | bytes 393224 | tf_op jit(solution)/shard_map/ppermute | solution.py:358
  65.7 1.1 %collective-permute-start.14 = (bf16[8,64,128]{2,1,0:T(8,128)(2,1)S(1)}, bf16[8,64,128]{2,1,0:T(8,128)(2,1)S(1)}, u32[]{:S(2)}, u32[]{:S(2)}) collective-permute-start(bf16[8,64,128]{2,1,0:T(8,128)(2,1)S(1)} %get-tuple-element.73), channel_id=1, source_target_pairs={{0,3},{1,0},{2,1},{3,2},{4,7},{5,4},{6,5},{7,6},{8,11},{9,8},{10,9... | collective-permute-start | bytes 393224 | tf_op jit(solution)/shard_map/ppermute | solution.py:358
  67.4 1.7 %collective-permute-done.12.rest_1_ = bf16[8,64,128]{2,1,0:T(8,128)(2,1)S(1)} collective-permute-done((bf16[8,64,128]{2,1,0:T(8,128)(2,1)S(1)}, bf16[8,64,128]{2,1,0:T(8,128)(2,1)S(1)}, u32[]{:S(2)}, u32[]{:S(2)}) %collective-permute-start.12) | collective-permute-done | bytes 131104 | tf_op jit(solution)/shard_map/ppermute | solution.py:358
  69.1 4.8 %collective-permute-done.13.rest_2_ = bf16[8,64,128]{2,1,0:T(8,128)(2,1)S(1)} collective-permute-done((bf16[8,64,128]{2,1,0:T(8,128)(2,1)S(1)}, bf16[8,64,128]{2,1,0:T(8,128)(2,1)S(1)}, u32[]{:S(2)}, u32[]{:S(2)}) %collective-permute-start.13) | collective-permute-done | bytes 131104 | tf_op jit(solution)/shard_map/ppermute | solution.py:358
  73.9 1.4 %shard_map.92 = bf16[32,64,128]{2,1,0:T(8,128)(2,1)} custom-call(s32[2]{0:T(128)S(1)} %pad_add_fusion.where, bf16[8,64,128]{2,1,0:T(8,128)(2,1)S(1)} %get-tuple-element.70.rest_0_, bf16[8,64,128]{2,1,0:T(8,128)(2,1)S(1)} %collective-permute-done.12.rest_1_, bf16[8,64,128]{2,1,0:T(8,128)(2,1)S(1)} %collective-permute-done.13.rest_2_, ...), custom_call_target="tpu_custom_call" | custom-call | bytes 33554432 | tf_op jit(solution)/shard_map/pallas_call | solution.py:343
  (23 shorter events, 1.6 us)
Async XLA Ops:
  2.6 15.9 %collective-permute-start = (bf16[10,64,128]{2,1,0:T(8,128)(2,1)S(1)}, bf16[10,64,128]{2,1,0:T(8,128)(2,1)S(1)}, u32[]{:S(2)}, u32[]{:S(2)}) collective-permute-start(bf16[10,64,128]{2,1,0:T(8,128)(2,1)S(1)} %get-tuple-element.42), channel_id=1, source_target_pairs={{0,1},{1,2},{2,3},{3,0},{4,5},{5,6},{6,7},{7,4},{8,9},{9,10},{10,1... | collective-permute-start | bytes 491528 | tf_op jit(solution)/shard_map/ppermute | solution.py:358
  5.6 13.3 %collective-permute-start.1 = (bf16[10,64,128]{2,1,0:T(8,128)(2,1)S(1)}, bf16[10,64,128]{2,1,0:T(8,128)(2,1)S(1)}, u32[]{:S(2)}, u32[]{:S(2)}) collective-permute-start(bf16[10,64,128]{2,1,0:T(8,128)(2,1)S(1)} %get-tuple-element.43), channel_id=1, source_target_pairs={{0,2},{1,3},{2,0},{3,1},{4,6},{5,7},{6,4},{7,5},{8,10},{9,11},{10,... | collective-permute-start | bytes 491528 | tf_op jit(solution)/shard_map/ppermute | solution.py:358
  8.2 10.8 %collective-permute-start.2 = (bf16[10,64,128]{2,1,0:T(8,128)(2,1)S(1)}, bf16[10,64,128]{2,1,0:T(8,128)(2,1)S(1)}, u32[]{:S(2)}, u32[]{:S(2)}) collective-permute-start(bf16[10,64,128]{2,1,0:T(8,128)(2,1)S(1)} %get-tuple-element.44), channel_id=1, source_target_pairs={{0,3},{1,0},{2,1},{3,2},{4,7},{5,4},{6,5},{7,6},{8,11},{9,8},{10,9... | collective-permute-start | bytes 491528 | tf_op jit(solution)/shard_map/ppermute | solution.py:358
  19.0 3.0 %collective-permute-start.3 = (bf16[64,64,128]{2,1,0:T(8,128)(2,1)S(1)}, bf16[64,64,128]{2,1,0:T(8,128)(2,1)S(1)}, u32[]{:S(2)}, u32[]{:S(2)}) collective-permute-start(bf16[64,64,128]{2,1,0:T(8,128)(2,1)S(1)} %get-tuple-element.45), channel_id=1, source_target_pairs={{0,4},{4,0},{8,12},{12,8},{16,20},{20,16},{24,28},{28,24},{1,5},{5... | collective-permute-start | bytes 3145736 | tf_op jit(solution)/shard_map/ppermute | solution.py:375
  19.0 24.8 %collective-permute-start.8 = (bf16[32,64,128]{2,1,0:T(8,128)(2,1)S(1)}, bf16[32,64,128]{2,1,0:T(8,128)(2,1)S(1)}, u32[]{:S(2)}, u32[]{:S(2)}) collective-permute-start(bf16[32,64,128]{2,1,0:T(8,128)(2,1)S(1)} %get-tuple-element.65), channel_id=1, source_target_pairs={{0,24},{4,12},{8,0},{12,20},{16,8},{20,28},{24,16},{28,4},{1,25},{... | collective-permute-start | bytes 1572872 | tf_op jit(solution)/shard_map/ppermute | solution.py:376
  22.2 23.2 %collective-permute-start.7 = (bf16[32,64,128]{2,1,0:T(8,128)(2,1)S(1)}, bf16[32,64,128]{2,1,0:T(8,128)(2,1)S(1)}, u32[]{:S(2)}, u32[]{:S(2)}) collective-permute-start(bf16[32,64,128]{2,1,0:T(8,128)(2,1)S(1)} %shard_map.88), channel_id=1, source_target_pairs={{0,28},{4,8},{8,4},{12,16},{16,12},{20,24},{24,20},{28,0},{1,29},{... | collective-permute-start | bytes 1572872 | tf_op jit(solution)/shard_map/ppermute | solution.py:378
  24.6 9.1 %collective-permute-start.4 = (bf16[8,64,128]{2,1,0:T(8,128)(2,1)S(1)}, bf16[8,64,128]{2,1,0:T(8,128)(2,1)S(1)}, u32[]{:S(2)}, u32[]{:S(2)}) collective-permute-start(bf16[8,64,128]{2,1,0:T(8,128)(2,1)S(1)} %get-tuple-element.53), channel_id=1, source_target_pairs={{0,1},{1,2},{2,3},{3,0},{4,5},{5,6},{6,7},{7,4},{8,9},{9,10},{10,1... | collective-permute-start | bytes 393224 | tf_op jit(solution)/shard_map/ppermute | solution.py:358
  28.1 9.9 %collective-permute-start.5 = (bf16[8,64,128]{2,1,0:T(8,128)(2,1)S(1)}, bf16[8,64,128]{2,1,0:T(8,128)(2,1)S(1)}, u32[]{:S(2)}, u32[]{:S(2)}) collective-permute-start(bf16[8,64,128]{2,1,0:T(8,128)(2,1)S(1)} %get-tuple-element.54), channel_id=1, source_target_pairs={{0,2},{1,3},{2,0},{3,1},{4,6},{5,7},{6,4},{7,5},{8,10},{9,11},{10,... | collective-permute-start | bytes 393224 | tf_op jit(solution)/shard_map/ppermute | solution.py:358
  29.8 8.2 %collective-permute-start.6 = (bf16[8,64,128]{2,1,0:T(8,128)(2,1)S(1)}, bf16[8,64,128]{2,1,0:T(8,128)(2,1)S(1)}, u32[]{:S(2)}, u32[]{:S(2)}) collective-permute-start(bf16[8,64,128]{2,1,0:T(8,128)(2,1)S(1)} %get-tuple-element.55), channel_id=1, source_target_pairs={{0,3},{1,0},{2,1},{3,2},{4,7},{5,4},{6,5},{7,6},{8,11},{9,8},{10,9... | collective-permute-start | bytes 393224 | tf_op jit(solution)/shard_map/ppermute | solution.py:358
  39.0 12.5 %collective-permute-start.15 = (bf16[2,64,128]{2,1,0:T(8,128)(2,1)S(1)}, bf16[2,64,128]{2,1,0:T(8,128)(2,1)S(1)}, u32[]{:S(2)}, u32[]{:S(2)}) collective-permute-start(bf16[2,64,128]{2,1,0:T(8,128)(2,1)S(1)} %get-tuple-element.75), channel_id=1, source_target_pairs={{0,3},{1,0},{2,1},{3,2},{4,7},{5,4},{6,5},{7,6},{8,11},{9,8},{10,9... | collective-permute-start | bytes 98312 | tf_op jit(solution)/shard_map/ppermute | solution.py:358
  43.1 9.2 %collective-permute-start.16 = (bf16[2,64,128]{2,1,0:T(8,128)(2,1)S(1)}, bf16[2,64,128]{2,1,0:T(8,128)(2,1)S(1)}, u32[]{:S(2)}, u32[]{:S(2)}) collective-permute-start(bf16[2,64,128]{2,1,0:T(8,128)(2,1)S(1)} %get-tuple-element.76), channel_id=1, source_target_pairs={{0,2},{1,3},{2,0},{3,1},{4,6},{5,7},{6,4},{7,5},{8,10},{9,11},{10,... | collective-permute-start | bytes 98312 | tf_op jit(solution)/shard_map/ppermute | solution.py:358
  43.8 8.5 %collective-permute-start.17 = (bf16[2,64,128]{2,1,0:T(8,128)(2,1)S(1)}, bf16[2,64,128]{2,1,0:T(8,128)(2,1)S(1)}, u32[]{:S(2)}, u32[]{:S(2)}) collective-permute-start(bf16[2,64,128]{2,1,0:T(8,128)(2,1)S(1)} %get-tuple-element.77), channel_id=1, source_target_pairs={{0,1},{1,2},{2,3},{3,0},{4,5},{5,6},{6,7},{7,4},{8,9},{9,10},{10,1... | collective-permute-start | bytes 98312 | tf_op jit(solution)/shard_map/ppermute | solution.py:358
  46.3 9.8 %collective-permute-start.9 = (bf16[8,64,128]{2,1,0:T(8,128)(2,1)S(1)}, bf16[8,64,128]{2,1,0:T(8,128)(2,1)S(1)}, u32[]{:S(2)}, u32[]{:S(2)}) collective-permute-start(bf16[8,64,128]{2,1,0:T(8,128)(2,1)S(1)} %get-tuple-element.67), channel_id=1, source_target_pairs={{0,1},{1,2},{2,3},{3,0},{4,5},{5,6},{6,7},{7,4},{8,9},{9,10},{10,1... | collective-permute-start | bytes 393224 | tf_op jit(solution)/shard_map/ppermute | solution.py:358
  49.8 10.2 %collective-permute-start.10 = (bf16[8,64,128]{2,1,0:T(8,128)(2,1)S(1)}, bf16[8,64,128]{2,1,0:T(8,128)(2,1)S(1)}, u32[]{:S(2)}, u32[]{:S(2)}) collective-permute-start(bf16[8,64,128]{2,1,0:T(8,128)(2,1)S(1)} %get-tuple-element.68), channel_id=1, source_target_pairs={{0,2},{1,3},{2,0},{3,1},{4,6},{5,7},{6,4},{7,5},{8,10},{9,11},{10,... | collective-permute-start | bytes 393224 | tf_op jit(solution)/shard_map/ppermute | solution.py:358
  51.5 8.5 %collective-permute-start.11 = (bf16[8,64,128]{2,1,0:T(8,128)(2,1)S(1)}, bf16[8,64,128]{2,1,0:T(8,128)(2,1)S(1)}, u32[]{:S(2)}, u32[]{:S(2)}) collective-permute-start(bf16[8,64,128]{2,1,0:T(8,128)(2,1)S(1)} %get-tuple-element.69), channel_id=1, source_target_pairs={{0,3},{1,0},{2,1},{3,2},{4,7},{5,4},{6,5},{7,6},{8,11},{9,8},{10,9... | collective-permute-start | bytes 393224 | tf_op jit(solution)/shard_map/ppermute | solution.py:358
  52.3 1.3 %collective-permute-start.18 = (f32[2,64,128]{2,1,0:T(8,128)S(1)}, f32[2,64,128]{2,1,0:T(8,128)S(1)}, u32[]{:S(2)}, u32[]{:S(2)}) collective-permute-start(f32[2,64,128]{2,1,0:T(8,128)S(1)} %convert_add_fusion), channel_id=1, source_target_pairs={{0,4},{4,0},{8,12},{12,8},{16,20},{20,16},{24,28},{28,24},{1,5},{5... | collective-permute-start | bytes 196616 | tf_op jit(solution)/shard_map/ppermute | solution.py:391
  53.6 12.0 %collective-permute-start.21 = (f32[2,64,128]{2,1,0:T(8,128)S(1)}, f32[2,64,128]{2,1,0:T(8,128)S(1)}, u32[]{:S(2)}, u32[]{:S(2)}) collective-permute-start(f32[2,64,128]{2,1,0:T(8,128)S(1)} %add.24), channel_id=1, source_target_pairs={{0,24},{4,28},{8,16},{12,20},{16,8},{20,12},{24,0},{28,4},{1,25},{... | collective-permute-start | bytes 196616 | tf_op jit(solution)/shard_map/ppermute | solution.py:393
  55.4 11.4 %collective-permute-start.20 = (f32[2,64,128]{2,1,0:T(8,128)S(1)}, f32[2,64,128]{2,1,0:T(8,128)S(1)}, u32[]{:S(2)}, u32[]{:S(2)}) collective-permute-start(f32[2,64,128]{2,1,0:T(8,128)S(1)} %add.24), channel_id=1, source_target_pairs={{0,16},{4,20},{8,24},{12,28},{16,0},{20,4},{24,8},{28,12},{1,17},{... | collective-permute-start | bytes 196616 | tf_op jit(solution)/shard_map/ppermute | solution.py:393
  56.1 10.7 %collective-permute-start.19 = (f32[2,64,128]{2,1,0:T(8,128)S(1)}, f32[2,64,128]{2,1,0:T(8,128)S(1)}, u32[]{:S(2)}, u32[]{:S(2)}) collective-permute-start(f32[2,64,128]{2,1,0:T(8,128)S(1)} %add.24), channel_id=1, source_target_pairs={{0,8},{4,12},{8,0},{12,4},{16,24},{20,28},{24,16},{28,20},{1,9},{5... | collective-permute-start | bytes 196616 | tf_op jit(solution)/shard_map/ppermute | solution.py:393
  61.0 8.1 %collective-permute-start.12 = (bf16[8,64,128]{2,1,0:T(8,128)(2,1)S(1)}, bf16[8,64,128]{2,1,0:T(8,128)(2,1)S(1)}, u32[]{:S(2)}, u32[]{:S(2)}) collective-permute-start(bf16[8,64,128]{2,1,0:T(8,128)(2,1)S(1)} %get-tuple-element.71), channel_id=1, source_target_pairs={{0,1},{1,2},{2,3},{3,0},{4,5},{5,6},{6,7},{7,4},{8,9},{9,10},{10,1... | collective-permute-start | bytes 393224 | tf_op jit(solution)/shard_map/ppermute | solution.py:358
  64.3 9.6 %collective-permute-start.13 = (bf16[8,64,128]{2,1,0:T(8,128)(2,1)S(1)}, bf16[8,64,128]{2,1,0:T(8,128)(2,1)S(1)}, u32[]{:S(2)}, u32[]{:S(2)}) collective-permute-start(bf16[8,64,128]{2,1,0:T(8,128)(2,1)S(1)} %get-tuple-element.72), channel_id=1, source_target_pairs={{0,2},{1,3},{2,0},{3,1},{4,6},{5,7},{6,4},{7,5},{8,10},{9,11},{10,... | collective-permute-start | bytes 393224 | tf_op jit(solution)/shard_map/ppermute | solution.py:358
  65.7 8.2 %collective-permute-start.14 = (bf16[8,64,128]{2,1,0:T(8,128)(2,1)S(1)}, bf16[8,64,128]{2,1,0:T(8,128)(2,1)S(1)}, u32[]{:S(2)}, u32[]{:S(2)}) collective-permute-start(bf16[8,64,128]{2,1,0:T(8,128)(2,1)S(1)} %get-tuple-element.73), channel_id=1, source_target_pairs={{0,3},{1,0},{2,1},{3,2},{4,7},{5,4},{6,5},{7,6},{8,11},{9,8},{10,9... | collective-permute-start | bytes 393224 | tf_op jit(solution)/shard_map/ppermute | solution.py:358

commit v12 on v8

--- a/solution.py
+++ b/solution.py
@@ -10,8 +10,8 @@
 
 REACH = 2
 GROUP = 4
-STEP = 4
-RING = 10
+STEP = 16
+AHEAD = 6
 BF16 = jnp.bfloat16
 F32 = jnp.float32
 MIB = 1 << 20
@@ -39,49 +39,85 @@
     return value & (size - 1)
 
 
-def tiles_kernel(slabs, reps, where, cols, live, weight, cot, mask, tiles, *rest):
-    outs, packed, rest = rest[:5], rest[5 : 5 + reps], rest[5 + reps :]
-    cot_in, mask_in, z, ring, first, second, rows, left, sems, z_sems = rest
-    totals = (first, second)
-    blocks, slots = cols.shape
-    per_row = slots // GROUP
+def low_bits(blocks):
+    return ((2 * REACH - 1) * blocks).bit_length()
+
+
+def add_tiles(listed, count, blocks, slots, tiles, z, total, held, sems):
+    bits = low_bits(blocks)
+    steps = lax.div(count + STEP - 1, STEP)
+
+    def fetch(i):
+        for u in range(STEP):
+            tile = lax.shift_right_logical(listed[i * STEP + u], bits)
+            pltpu.make_async_copy(tiles.at[tile], held.at[i, u], sems.at[i]).start()
+
+    for i in range(AHEAD):
+        pl.when(i < steps)(functools.partial(fetch, i))
+
+    def clear(i, carry):
+        total[pl.ds(i * GROUP, GROUP)] = jnp.zeros((GROUP,) + total.shape[1:], F32)
+        return carry
+
+    lax.fori_loop(0, total.shape[0] // GROUP, clear, 0)
+
+    def step(i, carry):
+        pl.when(i + AHEAD < steps)(functools.partial(fetch, i + AHEAD))
+        pltpu.make_async_copy(tiles.at[pl.ds(0, STEP)], held.at[i], sems.at[i]).wait()
+        for u in range(STEP):
+            entry = listed[i * STEP + u]
+            row = lax.div(lax.shift_right_logical(entry, bits), slots)
+            place = entry & ((1 << bits) - 1)
+            total[place] += jnp.dot(z[row], held[i, u], preferred_element_type=F32)
+        return carry
+
+    lax.fori_loop(0, steps, step, 0)
+
+
+def store_sums(out, total, base):
+    def some(i, carry):
+        for k in range(GROUP):
+            at = i * GROUP + k
+            out[at] = total[base + at].astype(BF16)
+        return carry
+
+    lax.fori_loop(0, out.shape[0] // GROUP, some, 0)
+
+
+def ends_kernel(slabs, reps, where, cols, live, cot, mask, tiles, weight, *rest):
+    (near, two, listed, z), packed, rest = rest[:4], rest[4 : 4 + reps], rest[4 + reps :]
+    cot_in, mask_in, weight_in, total, held, mine, sems, z_sems = rest
+    slots, blocks = cols.shape
     window = (2 * REACH + 1) * blocks
+    bits = low_bits(blocks)
     copies = [
         pltpu.make_async_copy(cot, cot_in, z_sems.at[0]),
         pltpu.make_async_copy(mask, mask_in, z_sems.at[1]),
+        pltpu.make_async_copy(weight, weight_in, z_sems.at[2]),
     ]
     for copy in copies:
         copy.start()
-
-    def list_row(b, count):
-        for g in range(per_row):
-            rows[count + g] = b * per_row + g
-            left[count + g] = live[b] - g * GROUP
-        return count + lax.shift_right_logical(live[b] + GROUP - 1, GROUP.bit_length() - 1)
-
-    count = lax.fori_loop(0, blocks, list_row, jnp.int32(0))
+    shift = REACH * blocks - where[0] * blocks
+
+    def list_row(b, counts):
+        ends, middle = counts
+        for s in range(slots):
+            place = wrap(cols[s, b] + shift, slabs * blocks)
+            first, last = place < blocks, place >= window - blocks
+            alive = s < live[b]
+            entry = (b * slots + s) << bits
+            mine[ends] = entry + jnp.where(last, place - (window - 2 * blocks), place)
+            listed[middle] = entry + place - blocks
+            is_end = first | last
+            ends += jnp.where(alive & is_end, 1, 0)
+            middle += jnp.where(alive & jnp.logical_not(is_end), 1, 0)
+        return ends, middle
+
+    ends, middle = lax.fori_loop(0, blocks, list_row, (jnp.int32(0), jnp.int32(0)))
     for u in range(STEP):
-        rows[count + u] = 0
-        left[count + u] = 0
-    steps = lax.div(count + STEP - 1, STEP)
-
-    def fetch(i):
-        slot = lax.rem(i, RING)
-        for u in range(STEP):
-            start = rows[i * STEP + u] * GROUP
-            pltpu.make_async_copy(
-                tiles.at[pl.ds(start, GROUP)], ring.at[slot, pl.ds(u * GROUP, GROUP)], sems.at[slot]
-            ).start()
-
-    for i in range(RING - 1):
-        pl.when(i < steps)(functools.partial(fetch, jnp.int32(i)))
-
-    def clear(i, carry):
-        for total in totals:
-            total[pl.ds(i * GROUP, GROUP)] = jnp.zeros((GROUP,) + total.shape[1:], F32)
-        return carry
-
-    lax.fori_loop(0, window // GROUP, clear, 0)
+        mine[ends + u] = 2 * blocks
+        listed[middle + u] = window - 2 * blocks
+    listed[blocks * slots + STEP] = middle
     for copy in copies:
         copy.wait()
 
@@ -90,86 +126,86 @@
         return carry
 
     lax.fori_loop(0, blocks, mask_row, 0)
+    add_tiles(mine, ends, blocks, slots, tiles, z, total, held, sems)
+    odd = lax.rem(where[0], 2)
+    store_sums(near, total, (1 - odd) * blocks)
+    store_sums(two, total, odd * blocks)
     nodes = z.shape[2]
     share = blocks // reps
     for s in range(reps):
         packed[s][:share] = z[pl.ds(wrap(where[1] + s, reps) * share, share)]
-        for h in range(weight.shape[1] // nodes):
-            packed[s][share + h] = weight[:, h * nodes : (h + 1) * nodes]
-    shift = REACH * blocks - where[0] * blocks
-
-    def step(i, carry):
-        slot = lax.rem(i, RING)
-        pltpu.make_async_copy(
-            tiles.at[pl.ds(0, STEP * GROUP)], ring.at[slot], sems.at[slot]
-        ).wait()
-        pl.when(i + RING - 1 < steps)(functools.partial(fetch, i + RING - 1))
-        for u in range(STEP):
-            row, remain = rows[i * STEP + u], left[i * STEP + u]
-            b, g = lax.div(row, per_row), lax.rem(row, per_row)
-            z_row = z[b]
-            for j in range(GROUP):
-                place = wrap(cols[b, g * GROUP + j] + shift, slabs * blocks)
-                place = jnp.where(j < remain, place, window)
-                totals[j % 2][place] += jnp.dot(
-                    z_row, ring[slot, u * GROUP + j], preferred_element_type=F32
-                )
-        return carry
-
-    lax.fori_loop(0, steps, step, 0)
-    sign = 2 * lax.rem(where[0], 2) - 1
-    for order, out in enumerate(outs):
-        base = ((order - REACH) * sign + REACH) * blocks
-
-        def store(i, carry, out=out, base=base):
-            for k in range(GROUP):
-                at = i * GROUP + k
-                out[at] = (first[base + at] + second[base + at]).astype(BF16)
-            return carry
-
-        lax.fori_loop(0, blocks // GROUP, store, 0)
-
-
-def contributions(where, cols, live, weight, cot, mask, tiles, slabs, reps):
-    blocks, slots, nodes = tiles.shape[:3]
-    features = cot.shape[1]
-    window = (2 * REACH + 1) * blocks
-    lists = blocks * (slots // GROUP) + slots // GROUP + STEP
-    total = pltpu.VMEM((window + 1, features, nodes), F32)
+        for h in range(weight_in.shape[1] // nodes):
+            packed[s][share + h] = weight_in[:, h * nodes : (h + 1) * nodes]
+
+
+def held_tiles(count, nodes):
+    steps = count // STEP + 1
+    return pltpu.VMEM((steps, STEP, nodes, nodes), BF16), pltpu.SemaphoreType.DMA((steps,))
+
+
+def end_sums(where, cols, live, cot, mask, tiles, weight, slabs, reps):
+    slots, blocks = cols.shape
+    _, features, nodes = cot.shape
+    count = blocks * slots
+    lists = count + STEP + 8
     packs = blocks // reps + weight.shape[1] // nodes
-    return pl.pallas_call(
-        functools.partial(tiles_kernel, slabs, reps),
-        out_shape=[jax.ShapeDtypeStruct(cot.shape, BF16)] * 5
-        + [jax.ShapeDtypeStruct((packs, features, nodes), BF16)] * reps,
-        in_specs=[smem(), smem(), smem(), vmem(), hbm(), hbm(), hbm()],
-        out_specs=[vmem()] * (5 + reps),
+    held, sems = held_tiles(count, nodes)
+    whole = jax.ShapeDtypeStruct(cot.shape, BF16)
+    share = jax.ShapeDtypeStruct((packs, features, nodes), BF16)
+    return pl.pallas_call(
+        functools.partial(ends_kernel, slabs, reps),
+        out_shape=[whole, whole, jax.ShapeDtypeStruct((lists,), jnp.int32), whole] + [share] * reps,
+        in_specs=[smem()] * 3 + [hbm()] * 4,
+        out_specs=[vmem(), vmem(), smem(), vmem()] + [vmem()] * reps,
         scratch_shapes=[
             pltpu.VMEM(cot.shape, BF16),
             pltpu.VMEM(mask.shape, jnp.int32),
-            pltpu.VMEM(cot.shape, BF16),
-            pltpu.VMEM((RING, STEP * GROUP, nodes, nodes), BF16),
-            total,
-            total,
+            pltpu.VMEM(weight.shape, BF16),
+            pltpu.VMEM((2 * blocks + GROUP, features, nodes), F32),
+            held,
             pltpu.SMEM((lists,), jnp.int32),
-            pltpu.SMEM((lists,), jnp.int32),
-            pltpu.SemaphoreType.DMA((RING,)),
-            pltpu.SemaphoreType.DMA((2,)),
+            sems,
+            pltpu.SemaphoreType.DMA((3,)),
         ],
-        compiler_params=pltpu.CompilerParams(vmem_limit_bytes=26 * MIB),
-        cost_estimate=pl.CostEstimate(
-            flops=2 * blocks * slots * features * nodes * nodes,
-            bytes_accessed=tiles.size * 2,
+        compiler_params=pltpu.CompilerParams(vmem_limit_bytes=28 * MIB),
+        cost_estimate=pl.CostEstimate(
+            flops=blocks * slots * features * nodes * nodes,
+            bytes_accessed=tiles.size,
             transcendentals=0,
         ),
-    )(
-        where,
-        in_hbm(cols),
-        in_hbm(live),
-        weight,
-        in_hbm(cot),
-        in_hbm(mask),
-        in_hbm(tiles.reshape(blocks * slots, nodes, nodes)),
-    )
+    )(where, in_hbm(cols), in_hbm(live), in_hbm(cot), in_hbm(mask), in_hbm(tiles), in_hbm(weight))
+
+
+def middle_kernel(slots, where, listed, z, tiles, beside, own, one, total, held, sems):
+    blocks = z.shape[0]
+    count = listed[blocks * slots + STEP]
+    add_tiles(listed, count, blocks, slots, tiles, z, total, held, sems)
+    odd = lax.rem(where[0], 2)
+    store_sums(one, total, 2 * odd * blocks)
+    store_sums(beside, total, (2 - 2 * odd) * blocks)
+    store_sums(own, total, blocks)
+
+
+def middle_sums(where, listed, z, tiles, slots):
+    blocks, features, nodes = z.shape
+    held, sems = held_tiles(blocks * slots, nodes)
+    return pl.pallas_call(
+        functools.partial(middle_kernel, slots),
+        out_shape=[jax.ShapeDtypeStruct(z.shape, BF16)] * 3,
+        in_specs=[smem(), smem(), vmem(), hbm()],
+        out_specs=[vmem()] * 3,
+        scratch_shapes=[
+            pltpu.VMEM(((2 * REACH - 1) * blocks + GROUP, features, nodes), F32),
+            held,
+            sems,
+        ],
+        compiler_params=pltpu.CompilerParams(vmem_limit_bytes=28 * MIB),
+        cost_estimate=pl.CostEstimate(
+            flops=blocks * slots * features * nodes * nodes,
+            bytes_accessed=tiles.size,
+            transcendentals=0,
+        ),
+    )(where, listed, z, in_hbm(tiles))
 
 
 def lay_features(where, shares, whole):
@@ -347,33 +383,38 @@
     pair = [(i, i ^ 1) for i in range(slabs)]
     to_one = [(i, (i + (1 if i % 2 else -1)) % slabs) for i in range(slabs)]
     to_two = [(i, (i + (2 if i % 2 else -2)) % slabs) for i in range(slabs)]
-    aggs = [shift(node_share(aggregated, s), s) for s in range(reps)]
-    near, beside, own, one, two, *packed = contributions(
-        where, col_block, live_count, weight, cotangent, relu_mask, tiles, slabs, reps
+    slots = tiles.shape[1]
+    tiles = tiles.reshape(blocks * slots, nodes, nodes)
+    near, two, listed, grad_z, *packed = end_sums(
+        where, col_block.T, live_count, cotangent, relu_mask, tiles, weight, slabs, reps
     )
-    near, aggs = lax.optimization_barrier((near, aggs))
     near_in = lax.ppermute(near, "blk", pair)
     two_in = lax.ppermute(two, "blk", to_two)
+    aggregated, _ = lax.optimization_barrier((aggregated, near))
+    aggs = [shift(node_share(aggregated, s), s) for s in range(reps)]
+
+    beside, own, one = middle_sums(where, listed, grad_z, tiles, slots)
+    one, aggs = lax.optimization_barrier((one, aggs))
     one = add(one, near_in)
     one_in = lax.ppermute(one, "blk", to_one)
     beside_in = lax.ppermute(beside, "blk", pair)
-
-    packed, _ = lax.optimization_barrier((packed, one))
+    packed, _ = lax.optimization_barrier((packed, (one, two_in)))
     packed = [shift(value, s) for s, value in enumerate(packed)]
-    grad_w = weight_partial(where, packed, aggs)
-    grad_w = sum(shift(part, -s).astype(F32) for s, part in enumerate(grad_w))
-
-    own, grad_w = lax.optimization_barrier((own, grad_w))
+
     shares = total_shares(where, [own, beside_in, one_in, two_in], reps)
     shares = [shift(value, s) for s, value in enumerate(shares)]
     outs = [shift(value, s) for s, value in enumerate(mix(where, shares, packed, share))]
     input_grad = lay_blocks(where, outs, cotangent.shape)
 
+    grad_w = weight_partial(where, packed, aggs)
+    grad_w = sum(shift(part, -s).astype(F32) for s, part in enumerate(grad_w))
     grad_w = grad_w + lax.ppermute(grad_w, "blk", pair)
-    grad_w = grad_w + sum(
+    parts = [
         lax.ppermute(grad_w, "blk", [(i, i ^ step) for i in range(slabs)])
         for step in range(2, slabs, 2)
-    )
+    ]
+    parts, _ = lax.optimization_barrier((parts, input_grad))
+    grad_w = grad_w + sum(parts)
     grad_w = grad_w.transpose(1, 0, 2).reshape(features, width)
     return input_grad, grad_w * (1.0 / math.sqrt(slabs * blocks * nodes))
 

time: 81.1 us -> 77.5 us (0.956)
  waiting for transfers between devices: 26.2 us -> 19.3 us
  starting transfers between devices: 35.2 us -> 38.8 us
  local copies, waits for them, and re-layouts: 3.27 us -> 1.13 us
  Pallas kernels: 14.6 us -> 16.7 us
    ppermute x15, waiting for transfers between devices: 23 us -> 10.9 us  [shift(): lax.ppermute(value, 'rep', [(i, (i + steps) % reps) for i in range(reps)])]
    ppermute x1, waiting for transfers between devices: 0.01 us -> 8.34 us  [on_device(): one_in = lax.ppermute(one, 'blk', to_one)]
    ppermute x1, starting transfers between devices: 0.07 us -> 2.32 us  [on_device(): near_in = lax.ppermute(near, 'blk', pair)]
    ppermute x3, starting transfers between devices: 5.3 us -> 3.06 us  [on_device(): lax.ppermute(grad_w, 'blk', [(i, i ^ step) for i in range(slabs)])]
    unnamed x3 -> x0, local copies, waits for them, and re-layouts: 2.13 us -> none
    pallas_call x1 -> x2, Pallas kernels: 10.2 us -> 12.2 us  [the longest x1 8.42 us: end_sums(): pl.pallas_call(functools.partial(ends_kernel, slabs, reps), out_shape=[wh...]
    ppermute x15, starting transfers between devices: 27.1 us -> 29.1 us  [shift(): lax.ppermute(value, 'rep', [(i, (i + steps) % reps) for i in range(reps)])]
    ppermute x1, waiting for transfers between devices: 1.9 us -> 0.01 us  [on_device(): near_in = lax.ppermute(near, 'blk', pair)]
  transfers between devices with their start and end apart: 23 -> 23, of which waited for: 11 -> 6; matrix products, arithmetic and copies ran while one was open for 3% -> 1% of each run, Pallas kernels for 15% -> 11%
where the time goes in v12:
time: 77.5 us; the launch traced here: 77.4 us
  starting transfers between devices  38.8 us (50%)
  waiting for transfers between devices  19.3 us (25%)
  Pallas kernels  16.7 us (22%)
  local copies, waits for them, and re-layouts  1.13 us (1%)
    ppermute x15, starting transfers between devices, shift(): lax.ppermute(value, 'rep', [(i, (i + steps) % reps) for i in range(reps)])  29.1 us
    ppermute x15, waiting for transfers between devices, shift(): lax.ppermute(value, 'rep', [(i, (i + steps) % reps) for i in range(reps)])  10.9 us
    pallas_call x1, Pallas kernels, end_sums(): pl.pallas_call(functools.partial(ends_kernel, slabs, reps), out_shape=[wh...  8.42 us
    ppermute x1, waiting for transfers between devices, on_device(): one_in = lax.ppermute(one, 'blk', to_one)  8.34 us
    pallas_call x1, Pallas kernels, middle_sums(): pl.pallas_call(functools.partial(middle_kernel, slots), out_shape=[jax.Sh...  3.81 us
    ppermute x3, starting transfers between devices, on_device(): lax.ppermute(grad_w, 'blk', [(i, i ^ step) for i in range(slabs)])  3.06 us
    ppermute x1, starting transfers between devices, on_device(): near_in = lax.ppermute(near, 'blk', pair)  2.32 us
    ppermute x1, starting transfers between devices, on_device(): two_in = lax.ppermute(two, 'blk', to_two)  2.32 us
  transfers between devices with their start and end apart: 23, of which 6 were waited for; matrix products, arithmetic and copies ran while one was open for 1% of the time, Pallas kernels for 11%

profile of v12, /device:TPU:0, one launch (start us, length us, event | category | flops | bytes accessed | tf_op | source)
XLA Modules:
  0.0 77.4 jit_solution(9629677606193863296)
XLA Ops:
  0.7 8.4 %shard_map.86 = (bf16[32,64,128]{2,1,0:T(8,128)(2,1)S(1)}, bf16[32,64,128]{2,1,0:T(8,128)(2,1)S(1)}, s32[536]{0:T(1024)S(1)}, bf16[32,64,128]{2,1,0:T(8,128)(2,1...) custom-call(s32[2]{0:T(128)S(1)} %pad_add_fusion.where, ...), custom_call_target="tpu_custom_call" | custom-call | flops 536870912 | bytes 8388608 | tf_op jit(solution)/shard_map/pallas_call | solution.py:155
  9.1 2.3 %collective-permute-start.4 = (bf16[32,64,128]{2,1,0:T(8,128)(2,1)S(1)}, bf16[32,64,128]{2,1,0:T(8,128)(2,1)S(1)}, u32[]{:S(2)}, u32[]{:S(2)}) collective-permute-start(bf16[32,64,128]{2,1,0:T(8,128)(2,1)S(1)} %get-tuple-element.43), channel_id=1, source_target_pairs={{0,4},{4,0},{8,12},{12,8},{16,20},{20,16},{24,28},{28,24},{1,5},{5... | collective-permute-start | bytes 1572872 | tf_op jit(solution)/shard_map/ppermute | solution.py:391
  11.5 2.3 %collective-permute-start.6 = (bf16[32,64,128]{2,1,0:T(8,128)(2,1)S(1)}, bf16[32,64,128]{2,1,0:T(8,128)(2,1)S(1)}, u32[]{:S(2)}, u32[]{:S(2)}) collective-permute-start(bf16[32,64,128]{2,1,0:T(8,128)(2,1)S(1)} %get-tuple-element.46), channel_id=1, source_target_pairs={{0,24},{4,12},{8,0},{12,20},{16,8},{20,28},{24,16},{28,4},{1,25},{... | collective-permute-start | bytes 1572872 | tf_op jit(solution)/shard_map/ppermute | solution.py:392
  13.8 1.1 %constant_dynamic-slice_fusion = (bf16[8,64,128]{2,1,0:T(8,128)(2,1)S(1)}, bf16[8,64,128]{2,1,0:T(8,128)(2,1)S(1)}, bf16[8,64,128]{2,1,0:T(8,128)(2,1)S(1)}, bf16[8,64,128]{2,1,0:T(8,128)(2,1)S(1)}) fusion(bf16[32,64,128]{2,1,0:T(8,128)(2,1)} %param.9, s32[]{:T(128)S(6)} %select_n.15, s32[]{:T(128)S(6)} %select_n.14, s32[]{:T(128)S(6)} %select_n.13, ...), kind=kLoop, calls=%fused_computation.3 | loop fusion | bytes 1048592 | tf_op jit(solution)/shard_map/dynamic_slice | solution.py:373
  14.9 3.7 %collective-permute-start.3 = (bf16[8,64,128]{2,1,0:T(8,128)(2,1)S(1)}, bf16[8,64,128]{2,1,0:T(8,128)(2,1)S(1)}, u32[]{:S(2)}, u32[]{:S(2)}) collective-permute-start(bf16[8,64,128]{2,1,0:T(8,128)(2,1)S(1)} %get-tuple-element.74), channel_id=1, source_target_pairs={{0,3},{1,0},{2,1},{3,2},{4,7},{5,4},{6,5},{7,6},{8,11},{9,8},{10,9... | collective-permute-start | bytes 393224 | tf_op jit(solution)/shard_map/ppermute | solution.py:366
  18.6 1.0 %collective-permute-start.1 = (bf16[8,64,128]{2,1,0:T(8,128)(2,1)S(1)}, bf16[8,64,128]{2,1,0:T(8,128)(2,1)S(1)}, u32[]{:S(2)}, u32[]{:S(2)}) collective-permute-start(bf16[8,64,128]{2,1,0:T(8,128)(2,1)S(1)} %get-tuple-element.76), channel_id=1, source_target_pairs={{0,1},{1,2},{2,3},{3,0},{4,5},{5,6},{6,7},{7,4},{8,9},{9,10},{10,1... | collective-permute-start | bytes 393224 | tf_op jit(solution)/shard_map/ppermute | solution.py:366
  19.6 3.8 %shard_map.87 = (bf16[32,64,128]{2,1,0:T(8,128)(2,1)S(1)}, bf16[32,64,128]{2,1,0:T(8,128)(2,1)S(1)}, bf16[32,64,128]{2,1,0:T(8,128)(2,1)S(1)}) custom-call(s32[2]{0:T(128)S(1)} %pad_add_fusion.where, s32[536]{0:T(1024)S(1)} %get-tuple-element.38.listed, bf16[32,64,128]{2,1,0:T(8,128)(2,1)S(1)} %get-tuple-element.39.z, bf16[512,128,128]{2,1,0:T(8,128)(2,1)} %bitcast.11), custom_call_target="tpu_custom_call" | custom-call | flops 536870912 | bytes 8388608 | tf_op jit(solution)/shard_map/pallas_call | solution.py:192
  23.4 1.5 %collective-permute-start = (bf16[32,64,128]{2,1,0:T(8,128)(2,1)S(1)}, bf16[32,64,128]{2,1,0:T(8,128)(2,1)S(1)}, u32[]{:S(2)}, u32[]{:S(2)}) collective-permute-start(bf16[32,64,128]{2,1,0:T(8,128)(2,1)S(1)} %get-tuple-element.41), channel_id=1, source_target_pairs={{0,4},{4,0},{8,12},{12,8},{16,20},{20,16},{24,28},{28,24},{1,5},{5... | collective-permute-start | bytes 1572872 | tf_op jit(solution)/shard_map/ppermute | solution.py:400
  24.9 4.7 %collective-permute-done.2.rest_6_ = bf16[8,64,128]{2,1,0:T(8,128)(2,1)S(1)} collective-permute-done((bf16[8,64,128]{2,1,0:T(8,128)(2,1)S(1)}, bf16[8,64,128]{2,1,0:T(8,128)(2,1)S(1)}, u32[]{:S(2)}, u32[]{:S(2)}) %collective-permute-start.2) | collective-permute-done | bytes 131104 | tf_op jit(solution)/shard_map/ppermute | solution.py:366
  30.3 0.7 collective-permute-start.10
  31.0 1.9 %collective-permute-start.11 = (bf16[10,64,128]{2,1,0:T(8,128)(2,1)S(1)}, bf16[10,64,128]{2,1,0:T(8,128)(2,1)S(1)}, u32[]{:S(2)}, u32[]{:S(2)}) collective-permute-start(bf16[10,64,128]{2,1,0:T(8,128)(2,1)S(1)} %get-tuple-element.57), channel_id=1, source_target_pairs={{0,2},{1,3},{2,0},{3,1},{4,6},{5,7},{6,4},{7,5},{8,10},{9,11},{10,... | collective-permute-start | bytes 491528 | tf_op jit(solution)/shard_map/ppermute | solution.py:366
  32.9 2.9 %collective-permute-start.12 = (bf16[10,64,128]{2,1,0:T(8,128)(2,1)S(1)}, bf16[10,64,128]{2,1,0:T(8,128)(2,1)S(1)}, u32[]{:S(2)}, u32[]{:S(2)}) collective-permute-start(bf16[10,64,128]{2,1,0:T(8,128)(2,1)S(1)} %get-tuple-element.58), channel_id=1, source_target_pairs={{0,3},{1,0},{2,1},{3,2},{4,7},{5,4},{6,5},{7,6},{8,11},{9,8},{10,9... | collective-permute-start | bytes 491528 | tf_op jit(solution)/shard_map/ppermute | solution.py:366
  35.9 8.3 %collective-permute-done.5.rest_2_ = bf16[32,64,128]{2,1,0:T(8,128)(2,1)S(1)} collective-permute-done((bf16[32,64,128]{2,1,0:T(8,128)(2,1)S(1)}, bf16[32,64,128]{2,1,0:T(8,128)(2,1)S(1)}, u32[]{:S(2)}, u32[]{:S(2)}) %collective-permute-start.5) | collective-permute-done | bytes 524320 | tf_op jit(solution)/shard_map/ppermute | solution.py:399
  44.2 0.8 %shard_map.89 = (bf16[8,64,128]{2,1,0:T(8,128)(2,1)S(1)}, bf16[8,64,128]{2,1,0:T(8,128)(2,1)S(1)}, bf16[8,64,128]{2,1,0:T(8,128)(2,1)S(1)}, bf16[8,64,128]{2,1,0:T(8,128)(2,1)S(1)}) custom-call(s32[2]{0:T(128)S(1)} %pad_add_fusion.where, bf16[32,64,128]{2,1,0:T(8,128)(2,1)S(1)} %get-tuple-element.40.rest_0_, ...), custom_call_target="tpu_custom_call" | custom-call | flops 1048576 | bytes 2621440 | tf_op jit(solution)/shard_map/pallas_call | solution.py:325
  45.0 0.8 %collective-permute-start.7 = (bf16[8,64,128]{2,1,0:T(8,128)(2,1)S(1)}, bf16[8,64,128]{2,1,0:T(8,128)(2,1)S(1)}, u32[]{:S(2)}, u32[]{:S(2)}) collective-permute-start(bf16[8,64,128]{2,1,0:T(8,128)(2,1)S(1)} %get-tuple-element.48), channel_id=1, source_target_pairs={{0,1},{1,2},{2,3},{3,0},{4,5},{5,6},{6,7},{7,4},{8,9},{9,10},{10,1... | collective-permute-start | bytes 393224 | tf_op jit(solution)/shard_map/ppermute | solution.py:366
  45.8 2.0 %collective-permute-start.8 = (bf16[8,64,128]{2,1,0:T(8,128)(2,1)S(1)}, bf16[8,64,128]{2,1,0:T(8,128)(2,1)S(1)}, u32[]{:S(2)}, u32[]{:S(2)}) collective-permute-start(bf16[8,64,128]{2,1,0:T(8,128)(2,1)S(1)} %get-tuple-element.49), channel_id=1, source_target_pairs={{0,2},{1,3},{2,0},{3,1},{4,6},{5,7},{6,4},{7,5},{8,10},{9,11},{10,... | collective-permute-start | bytes 393224 | tf_op jit(solution)/shard_map/ppermute | solution.py:366
  47.8 2.8 %collective-permute-start.9 = (bf16[8,64,128]{2,1,0:T(8,128)(2,1)S(1)}, bf16[8,64,128]{2,1,0:T(8,128)(2,1)S(1)}, u32[]{:S(2)}, u32[]{:S(2)}) collective-permute-start(bf16[8,64,128]{2,1,0:T(8,128)(2,1)S(1)} %get-tuple-element.50), channel_id=1, source_target_pairs={{0,3},{1,0},{2,1},{3,2},{4,7},{5,4},{6,5},{7,6},{8,11},{9,8},{10,9... | collective-permute-start | bytes 393224 | tf_op jit(solution)/shard_map/ppermute | solution.py:366
  50.7 1.0 %shard_map.92 = (bf16[2,64,128]{2,1,0:T(8,128)(2,1)S(1)}, bf16[2,64,128]{2,1,0:T(8,128)(2,1)S(1)}, bf16[2,64,128]{2,1,0:T(8,128)(2,1)S(1)}, bf16[2,64,128]{2,1,0:T(8,128)(2,1)S(1)}) custom-call(s32[2]{0:T(128)S(1)} %pad_add_fusion.where, bf16[10,64,128]{2,1,0:T(8,128)(2,1)S(1)} %get-tuple-element.55.rest_4_.rest_0_, ...), custom_call_target="tpu_custom_call" | custom-call | flops 134217728 | bytes 1179648 | tf_op jit(solution)/shard_map/pallas_call | solution.py:275
  51.7 0.6 collective-permute-start.16
  52.5 0.8 %collective-permute-done.7.rest_1_ = bf16[8,64,128]{2,1,0:T(8,128)(2,1)S(1)} collective-permute-done((bf16[8,64,128]{2,1,0:T(8,128)(2,1)S(1)}, bf16[8,64,128]{2,1,0:T(8,128)(2,1)S(1)}, u32[]{:S(2)}, u32[]{:S(2)}) %collective-permute-start.7) | collective-permute-done | bytes 131104 | tf_op jit(solution)/shard_map/ppermute | solution.py:366
  53.3 6.0 %collective-permute-start.18 = (bf16[2,64,128]{2,1,0:T(8,128)(2,1)S(1)}, bf16[2,64,128]{2,1,0:T(8,128)(2,1)S(1)}, u32[]{:S(2)}, u32[]{:S(2)}) collective-permute-start(bf16[2,64,128]{2,1,0:T(8,128)(2,1)S(1)} %get-tuple-element.70), channel_id=1, source_target_pairs={{0,1},{1,2},{2,3},{3,0},{4,5},{5,6},{6,7},{7,4},{8,9},{9,10},{10,1... | collective-permute-start | bytes 98312 | tf_op jit(solution)/shard_map/ppermute | solution.py:366
  59.3 1.0 %shard_map.90 = (bf16[8,64,128]{2,1,0:T(8,128)(2,1)S(1)}, bf16[8,64,128]{2,1,0:T(8,128)(2,1)S(1)}, bf16[8,64,128]{2,1,0:T(8,128)(2,1)S(1)}, bf16[8,64,128]{2,1,0:T(8,128)(2,1)S(1)}) custom-call(s32[2]{0:T(128)S(1)} %pad_add_fusion.where, bf16[8,64,128]{2,1,0:T(8,128)(2,1)S(1)} %get-tuple-element.47.rest_0_, ...), custom_call_target="tpu_custom_call" | custom-call | flops 134217728 | bytes 1048576 | tf_op jit(solution)/shard_map/pallas_call | solution.py:238
  60.3 4.0 %collective-permute-start.13 = (bf16[8,64,128]{2,1,0:T(8,128)(2,1)S(1)}, bf16[8,64,128]{2,1,0:T(8,128)(2,1)S(1)}, u32[]{:S(2)}, u32[]{:S(2)}) collective-permute-start(bf16[8,64,128]{2,1,0:T(8,128)(2,1)S(1)} %get-tuple-element.60), channel_id=1, source_target_pairs={{0,1},{1,2},{2,3},{3,0},{4,5},{5,6},{6,7},{7,4},{8,9},{9,10},{10,1... | collective-permute-start | bytes 393224 | tf_op jit(solution)/shard_map/ppermute | solution.py:366
  64.4 2.3 %collective-permute-start.14 = (bf16[8,64,128]{2,1,0:T(8,128)(2,1)S(1)}, bf16[8,64,128]{2,1,0:T(8,128)(2,1)S(1)}, u32[]{:S(2)}, u32[]{:S(2)}) collective-permute-start(bf16[8,64,128]{2,1,0:T(8,128)(2,1)S(1)} %get-tuple-element.61), channel_id=1, source_target_pairs={{0,2},{1,3},{2,0},{3,1},{4,6},{5,7},{6,4},{7,5},{8,10},{9,11},{10,... | collective-permute-start | bytes 393224 | tf_op jit(solution)/shard_map/ppermute | solution.py:366
  66.9 0.8 %collective-permute-start.22 = (f32[2,64,128]{2,1,0:T(8,128)S(1)}, f32[2,64,128]{2,1,0:T(8,128)S(1)}, u32[]{:S(2)}, u32[]{:S(2)}) collective-permute-start(f32[2,64,128]{2,1,0:T(8,128)S(1)} %add.52), channel_id=1, source_target_pairs={{0,24},{4,28},{8,16},{12,20},{16,8},{20,12},{24,0},{28,4},{1,25},{... | collective-permute-start | bytes 196616 | tf_op jit(solution)/shard_map/ppermute | solution.py:413
  67.7 1.8 %collective-permute-start.21 = (f32[2,64,128]{2,1,0:T(8,128)S(1)}, f32[2,64,128]{2,1,0:T(8,128)S(1)}, u32[]{:S(2)}, u32[]{:S(2)}) collective-permute-start(f32[2,64,128]{2,1,0:T(8,128)S(1)} %add.52), channel_id=1, source_target_pairs={{0,16},{4,20},{8,24},{12,28},{16,0},{20,4},{24,8},{28,12},{1,17},{... | collective-permute-start | bytes 196616 | tf_op jit(solution)/shard_map/ppermute | solution.py:413
  69.5 0.6 collective-permute-done.13.rest_1_
  70.1 0.4 collective-permute-start.20
  70.5 4.1 %collective-permute-done.14.rest_2_ = bf16[8,64,128]{2,1,0:T(8,128)(2,1)S(1)} collective-permute-done((bf16[8,64,128]{2,1,0:T(8,128)(2,1)S(1)}, bf16[8,64,128]{2,1,0:T(8,128)(2,1)S(1)}, u32[]{:S(2)}, u32[]{:S(2)}) %collective-permute-start.14) | collective-permute-done | bytes 131104 | tf_op jit(solution)/shard_map/ppermute | solution.py:366
  74.6 0.7 collective-permute-done.15.rest_3_
  75.3 1.4 %shard_map.91 = bf16[32,64,128]{2,1,0:T(8,128)(2,1)} custom-call(s32[2]{0:T(128)S(1)} %pad_add_fusion.where, bf16[8,64,128]{2,1,0:T(8,128)(2,1)S(1)} %get-tuple-element.59.rest_0_, bf16[8,64,128]{2,1,0:T(8,128)(2,1)S(1)} %collective-permute-done.13.rest_1_, bf16[8,64,128]{2,1,0:T(8,128)(2,1)S(1)} %collective-permute-done.14.rest_2_, ...), custom_call_target="tpu_custom_call" | custom-call | bytes 33554432 | tf_op jit(solution)/shard_map/pallas_call | solution.py:351
  76.7 0.6 copy_bitcast_fusion
  (26 shorter events, 1.3 us)
Async XLA Ops:
  9.1 20.5 %collective-permute-start.4 = (bf16[32,64,128]{2,1,0:T(8,128)(2,1)S(1)}, bf16[32,64,128]{2,1,0:T(8,128)(2,1)S(1)}, u32[]{:S(2)}, u32[]{:S(2)}) collective-permute-start(bf16[32,64,128]{2,1,0:T(8,128)(2,1)S(1)} %get-tuple-element.43), channel_id=1, source_target_pairs={{0,4},{4,0},{8,12},{12,8},{16,20},{20,16},{24,28},{28,24},{1,5},{5... | collective-permute-start | bytes 1572872 | tf_op jit(solution)/shard_map/ppermute | solution.py:391
  11.5 18.9 %collective-permute-start.6 = (bf16[32,64,128]{2,1,0:T(8,128)(2,1)S(1)}, bf16[32,64,128]{2,1,0:T(8,128)(2,1)S(1)}, u32[]{:S(2)}, u32[]{:S(2)}) collective-permute-start(bf16[32,64,128]{2,1,0:T(8,128)(2,1)S(1)} %get-tuple-element.46), channel_id=1, source_target_pairs={{0,24},{4,12},{8,0},{12,20},{16,8},{20,28},{24,16},{28,4},{1,25},{... | collective-permute-start | bytes 1572872 | tf_op jit(solution)/shard_map/ppermute | solution.py:392
  14.9 8.5 %collective-permute-start.3 = (bf16[8,64,128]{2,1,0:T(8,128)(2,1)S(1)}, bf16[8,64,128]{2,1,0:T(8,128)(2,1)S(1)}, u32[]{:S(2)}, u32[]{:S(2)}) collective-permute-start(bf16[8,64,128]{2,1,0:T(8,128)(2,1)S(1)} %get-tuple-element.74), channel_id=1, source_target_pairs={{0,3},{1,0},{2,1},{3,2},{4,7},{5,4},{6,5},{7,6},{8,11},{9,8},{10,9... | collective-permute-start | bytes 393224 | tf_op jit(solution)/shard_map/ppermute | solution.py:366
  18.6 11.1 %collective-permute-start.2 = (bf16[8,64,128]{2,1,0:T(8,128)(2,1)S(1)}, bf16[8,64,128]{2,1,0:T(8,128)(2,1)S(1)}, u32[]{:S(2)}, u32[]{:S(2)}) collective-permute-start(bf16[8,64,128]{2,1,0:T(8,128)(2,1)S(1)} %get-tuple-element.75), channel_id=1, source_target_pairs={{0,2},{1,3},{2,0},{3,1},{4,6},{5,7},{6,4},{7,5},{8,10},{9,11},{10,... | collective-permute-start | bytes 393224 | tf_op jit(solution)/shard_map/ppermute | solution.py:366
  18.6 11.1 %collective-permute-start.1 = (bf16[8,64,128]{2,1,0:T(8,128)(2,1)S(1)}, bf16[8,64,128]{2,1,0:T(8,128)(2,1)S(1)}, u32[]{:S(2)}, u32[]{:S(2)}) collective-permute-start(bf16[8,64,128]{2,1,0:T(8,128)(2,1)S(1)} %get-tuple-element.76), channel_id=1, source_target_pairs={{0,1},{1,2},{2,3},{3,0},{4,5},{5,6},{6,7},{7,4},{8,9},{9,10},{10,1... | collective-permute-start | bytes 393224 | tf_op jit(solution)/shard_map/ppermute | solution.py:366
  23.4 12.5 %collective-permute-start = (bf16[32,64,128]{2,1,0:T(8,128)(2,1)S(1)}, bf16[32,64,128]{2,1,0:T(8,128)(2,1)S(1)}, u32[]{:S(2)}, u32[]{:S(2)}) collective-permute-start(bf16[32,64,128]{2,1,0:T(8,128)(2,1)S(1)} %get-tuple-element.41), channel_id=1, source_target_pairs={{0,4},{4,0},{8,12},{12,8},{16,20},{20,16},{24,28},{28,24},{1,5},{5... | collective-permute-start | bytes 1572872 | tf_op jit(solution)/shard_map/ppermute | solution.py:400
  29.9 14.3 %collective-permute-start.5 = (bf16[32,64,128]{2,1,0:T(8,128)(2,1)S(1)}, bf16[32,64,128]{2,1,0:T(8,128)(2,1)S(1)}, u32[]{:S(2)}, u32[]{:S(2)}) collective-permute-start(bf16[32,64,128]{2,1,0:T(8,128)(2,1)S(1)} %shard_map.88), channel_id=1, source_target_pairs={{0,28},{4,8},{8,4},{12,16},{16,12},{20,24},{24,20},{28,0},{1,29},{... | collective-permute-start | bytes 1572872 | tf_op jit(solution)/shard_map/ppermute | solution.py:399
  30.3 17.5 %collective-permute-start.10 = (bf16[10,64,128]{2,1,0:T(8,128)(2,1)S(1)}, bf16[10,64,128]{2,1,0:T(8,128)(2,1)S(1)}, u32[]{:S(2)}, u32[]{:S(2)}) collective-permute-start(bf16[10,64,128]{2,1,0:T(8,128)(2,1)S(1)} %get-tuple-element.56), channel_id=1, source_target_pairs={{0,1},{1,2},{2,3},{3,0},{4,5},{5,6},{6,7},{7,4},{8,9},{9,10},{10,1... | collective-permute-start | bytes 491528 | tf_op jit(solution)/shard_map/ppermute | solution.py:366
  31.0 19.7 %collective-permute-start.11 = (bf16[10,64,128]{2,1,0:T(8,128)(2,1)S(1)}, bf16[10,64,128]{2,1,0:T(8,128)(2,1)S(1)}, u32[]{:S(2)}, u32[]{:S(2)}) collective-permute-start(bf16[10,64,128]{2,1,0:T(8,128)(2,1)S(1)} %get-tuple-element.57), channel_id=1, source_target_pairs={{0,2},{1,3},{2,0},{3,1},{4,6},{5,7},{6,4},{7,5},{8,10},{9,11},{10,... | collective-permute-start | bytes 491528 | tf_op jit(solution)/shard_map/ppermute | solution.py:366
  32.9 17.7 %collective-permute-start.12 = (bf16[10,64,128]{2,1,0:T(8,128)(2,1)S(1)}, bf16[10,64,128]{2,1,0:T(8,128)(2,1)S(1)}, u32[]{:S(2)}, u32[]{:S(2)}) collective-permute-start(bf16[10,64,128]{2,1,0:T(8,128)(2,1)S(1)} %get-tuple-element.58), channel_id=1, source_target_pairs={{0,3},{1,0},{2,1},{3,2},{4,7},{5,4},{6,5},{7,6},{8,11},{9,8},{10,9... | collective-permute-start | bytes 491528 | tf_op jit(solution)/shard_map/ppermute | solution.py:366
  45.0 8.3 %collective-permute-start.7 = (bf16[8,64,128]{2,1,0:T(8,128)(2,1)S(1)}, bf16[8,64,128]{2,1,0:T(8,128)(2,1)S(1)}, u32[]{:S(2)}, u32[]{:S(2)}) collective-permute-start(bf16[8,64,128]{2,1,0:T(8,128)(2,1)S(1)} %get-tuple-element.48), channel_id=1, source_target_pairs={{0,1},{1,2},{2,3},{3,0},{4,5},{5,6},{6,7},{7,4},{8,9},{9,10},{10,1... | collective-permute-start | bytes 393224 | tf_op jit(solution)/shard_map/ppermute | solution.py:366
  45.8 13.5 %collective-permute-start.8 = (bf16[8,64,128]{2,1,0:T(8,128)(2,1)S(1)}, bf16[8,64,128]{2,1,0:T(8,128)(2,1)S(1)}, u32[]{:S(2)}, u32[]{:S(2)}) collective-permute-start(bf16[8,64,128]{2,1,0:T(8,128)(2,1)S(1)} %get-tuple-element.49), channel_id=1, source_target_pairs={{0,2},{1,3},{2,0},{3,1},{4,6},{5,7},{6,4},{7,5},{8,10},{9,11},{10,... | collective-permute-start | bytes 393224 | tf_op jit(solution)/shard_map/ppermute | solution.py:366
  47.8 11.5 %collective-permute-start.9 = (bf16[8,64,128]{2,1,0:T(8,128)(2,1)S(1)}, bf16[8,64,128]{2,1,0:T(8,128)(2,1)S(1)}, u32[]{:S(2)}, u32[]{:S(2)}) collective-permute-start(bf16[8,64,128]{2,1,0:T(8,128)(2,1)S(1)} %get-tuple-element.50), channel_id=1, source_target_pairs={{0,3},{1,0},{2,1},{3,2},{4,7},{5,4},{6,5},{7,6},{8,11},{9,8},{10,9... | collective-permute-start | bytes 393224 | tf_op jit(solution)/shard_map/ppermute | solution.py:366
  51.7 12.6 %collective-permute-start.16 = (bf16[2,64,128]{2,1,0:T(8,128)(2,1)S(1)}, bf16[2,64,128]{2,1,0:T(8,128)(2,1)S(1)}, u32[]{:S(2)}, u32[]{:S(2)}) collective-permute-start(bf16[2,64,128]{2,1,0:T(8,128)(2,1)S(1)} %get-tuple-element.68), channel_id=1, source_target_pairs={{0,3},{1,0},{2,1},{3,2},{4,7},{5,4},{6,5},{7,6},{8,11},{9,8},{10,9... | collective-permute-start | bytes 98312 | tf_op jit(solution)/shard_map/ppermute | solution.py:366
  52.3 12.0 %collective-permute-start.17 = (bf16[2,64,128]{2,1,0:T(8,128)(2,1)S(1)}, bf16[2,64,128]{2,1,0:T(8,128)(2,1)S(1)}, u32[]{:S(2)}, u32[]{:S(2)}) collective-permute-start(bf16[2,64,128]{2,1,0:T(8,128)(2,1)S(1)} %get-tuple-element.69), channel_id=1, source_target_pairs={{0,2},{1,3},{2,0},{3,1},{4,6},{5,7},{6,4},{7,5},{8,10},{9,11},{10,... | collective-permute-start | bytes 98312 | tf_op jit(solution)/shard_map/ppermute | solution.py:366
  53.3 11.0 %collective-permute-start.18 = (bf16[2,64,128]{2,1,0:T(8,128)(2,1)S(1)}, bf16[2,64,128]{2,1,0:T(8,128)(2,1)S(1)}, u32[]{:S(2)}, u32[]{:S(2)}) collective-permute-start(bf16[2,64,128]{2,1,0:T(8,128)(2,1)S(1)} %get-tuple-element.70), channel_id=1, source_target_pairs={{0,1},{1,2},{2,3},{3,0},{4,5},{5,6},{6,7},{7,4},{8,9},{9,10},{10,1... | collective-permute-start | bytes 98312 | tf_op jit(solution)/shard_map/ppermute | solution.py:366
  60.3 9.8 %collective-permute-start.13 = (bf16[8,64,128]{2,1,0:T(8,128)(2,1)S(1)}, bf16[8,64,128]{2,1,0:T(8,128)(2,1)S(1)}, u32[]{:S(2)}, u32[]{:S(2)}) collective-permute-start(bf16[8,64,128]{2,1,0:T(8,128)(2,1)S(1)} %get-tuple-element.60), channel_id=1, source_target_pairs={{0,1},{1,2},{2,3},{3,0},{4,5},{5,6},{6,7},{7,4},{8,9},{9,10},{10,1... | collective-permute-start | bytes 393224 | tf_op jit(solution)/shard_map/ppermute | solution.py:366
  64.3 2.5 %collective-permute-start.19 = (f32[2,64,128]{2,1,0:T(8,128)S(1)}, f32[2,64,128]{2,1,0:T(8,128)S(1)}, u32[]{:S(2)}, u32[]{:S(2)}) collective-permute-start(f32[2,64,128]{2,1,0:T(8,128)S(1)} %convert_add_fusion), channel_id=1, source_target_pairs={{0,4},{4,0},{8,12},{12,8},{16,20},{20,16},{24,28},{28,24},{1,5},{5... | collective-permute-start | bytes 196616 | tf_op jit(solution)/shard_map/ppermute | solution.py:411
  64.4 10.2 %collective-permute-start.14 = (bf16[8,64,128]{2,1,0:T(8,128)(2,1)S(1)}, bf16[8,64,128]{2,1,0:T(8,128)(2,1)S(1)}, u32[]{:S(2)}, u32[]{:S(2)}) collective-permute-start(bf16[8,64,128]{2,1,0:T(8,128)(2,1)S(1)} %get-tuple-element.61), channel_id=1, source_target_pairs={{0,2},{1,3},{2,0},{3,1},{4,6},{5,7},{6,4},{7,5},{8,10},{9,11},{10,... | collective-permute-start | bytes 393224 | tf_op jit(solution)/shard_map/ppermute | solution.py:366
  66.7 8.6 %collective-permute-start.15 = (bf16[8,64,128]{2,1,0:T(8,128)(2,1)S(1)}, bf16[8,64,128]{2,1,0:T(8,128)(2,1)S(1)}, u32[]{:S(2)}, u32[]{:S(2)}) collective-permute-start(bf16[8,64,128]{2,1,0:T(8,128)(2,1)S(1)} %get-tuple-element.62), channel_id=1, source_target_pairs={{0,3},{1,0},{2,1},{3,2},{4,7},{5,4},{6,5},{7,6},{8,11},{9,8},{10,9... | collective-permute-start | bytes 393224 | tf_op jit(solution)/shard_map/ppermute | solution.py:366
  66.9 9.8 %collective-permute-start.22 = (f32[2,64,128]{2,1,0:T(8,128)S(1)}, f32[2,64,128]{2,1,0:T(8,128)S(1)}, u32[]{:S(2)}, u32[]{:S(2)}) collective-permute-start(f32[2,64,128]{2,1,0:T(8,128)S(1)} %add.52), channel_id=1, source_target_pairs={{0,24},{4,28},{8,16},{12,20},{16,8},{20,12},{24,0},{28,4},{1,25},{... | collective-permute-start | bytes 196616 | tf_op jit(solution)/shard_map/ppermute | solution.py:413
  67.7 9.0 %collective-permute-start.21 = (f32[2,64,128]{2,1,0:T(8,128)S(1)}, f32[2,64,128]{2,1,0:T(8,128)S(1)}, u32[]{:S(2)}, u32[]{:S(2)}) collective-permute-start(f32[2,64,128]{2,1,0:T(8,128)S(1)} %add.52), channel_id=1, source_target_pairs={{0,16},{4,20},{8,24},{12,28},{16,0},{20,4},{24,8},{28,12},{1,17},{... | collective-permute-start | bytes 196616 | tf_op jit(solution)/shard_map/ppermute | solution.py:413
  70.1 6.6 %collective-permute-start.20 = (f32[2,64,128]{2,1,0:T(8,128)S(1)}, f32[2,64,128]{2,1,0:T(8,128)S(1)}, u32[]{:S(2)}, u32[]{:S(2)}) collective-permute-start(f32[2,64,128]{2,1,0:T(8,128)S(1)} %add.52), channel_id=1, source_target_pairs={{0,8},{4,12},{8,0},{12,4},{16,24},{20,28},{24,16},{28,20},{1,9},{5... | collective-permute-start | bytes 196616 | tf_op jit(solution)/shard_map/ppermute | solution.py:413

commit v13 on v11

--- a/solution.py
+++ b/solution.py
@@ -176,27 +176,28 @@
         whole[:, pl.ds(first, features), :] = shares[s][:blocks]
 
 
-def mix_kernel(reps, first, where, *rest):
-    shares, aggs, outs = rest[:reps], rest[reps : 2 * reps], rest[2 * reps : 3 * reps]
+def mix_kernel(reps, where, *rest):
+    shares, pieces, outs = rest[:reps], rest[reps : 2 * reps], rest[2 * reps : 3 * reps]
     weights, whole = rest[3 * reps :]
     blocks, features, nodes = outs[0].shape
+    halves = weights.shape[1] // nodes
     lay_features(where, shares, whole)
     for s in range(reps):
-        for h in range(weights.shape[1] // nodes):
+        for h in range(halves):
             rows, columns = pl.ds(s * features, features), pl.ds(h * nodes, nodes)
-            weights[rows, columns] = aggs[(reps - s) % reps][first + h]
+            weights[rows, columns] = pieces[s][halves + h]
     for b in range(blocks):
         mixed = jnp.dot(weights[...], whole[b], preferred_element_type=F32)
         for s in range(reps):
             outs[s][b] = mixed[s * features : (s + 1) * features].astype(BF16)
 
 
-def mix(where, shares, aggs):
+def mix(where, shares, pieces):
     reps = len(shares)
     blocks, features, nodes = shares[0].shape
     width = reps * features
     return pl.pallas_call(
-        functools.partial(mix_kernel, reps, blocks),
+        functools.partial(mix_kernel, reps),
         out_shape=[jax.ShapeDtypeStruct((blocks, features, nodes), BF16)] * reps,
         in_specs=[smem()] + [vmem()] * (2 * reps),
         out_specs=[vmem()] * reps,
@@ -207,35 +208,37 @@
             bytes_accessed=4 * blocks * nodes * width,
             transcendentals=0,
         ),
-    )(where, *shares, *aggs)
-
-
-def weight_kernel(reps, where, *rest):
-    packed, aggs, outs = rest[:reps], rest[reps : 2 * reps], rest[2 * reps : 3 * reps]
-    whole_z, whole_a = rest[3 * reps :]
-    blocks, features, nodes = packed[0].shape
-    lay_features(where, packed, whole_z)
-    for s in range(reps):
-        whole_a[:, pl.ds(s * features, features), :] = aggs[s][:blocks]
+    )(where, *shares, *pieces)
+
+
+def weight_kernel(reps, where, aggs, weight, *rest):
+    shares, outs, (whole_z, whole_a) = rest[:reps], rest[reps : 2 * reps], rest[2 * reps :]
+    blocks, features, nodes = shares[0].shape
+    halves = weight.shape[1] // nodes
+    lay_features(where, shares, whole_z)
+    for s in range(reps):
+        whole_a[:, pl.ds(s * features, features), :] = aggs[wrap(where[1] - s, reps)]
     total = jnp.zeros((whole_a.shape[1], whole_z.shape[1]), F32)
     for b in range(blocks):
         total += lax.dot_general(
             whole_a[b], whole_z[b], (((1,), (1,)), ((), ())), preferred_element_type=F32
         )
     for s in range(reps):
-        for h in range(outs[s].shape[0]):
-            part = total[s * features : (s + 1) * features, h * nodes : (h + 1) * nodes]
-            outs[s][h] = part.astype(BF16)
-
-
-def weight_partial(where, packed, aggs):
-    reps = len(packed)
-    blocks, features, nodes = packed[0].shape
+        for h in range(halves):
+            columns = slice(h * nodes, (h + 1) * nodes)
+            outs[s][h] = total[s * features : (s + 1) * features, columns].astype(BF16)
+            outs[s][halves + h] = weight[:, columns]
+
+
+def weight_partial(where, aggs, weight, shares):
+    reps = len(shares)
+    blocks, features, nodes = shares[0].shape
     width = reps * features
+    pieces = jax.ShapeDtypeStruct((2 * (width // nodes), features, nodes), BF16)
     return pl.pallas_call(
         functools.partial(weight_kernel, reps),
-        out_shape=[jax.ShapeDtypeStruct((width // nodes, features, nodes), BF16)] * reps,
-        in_specs=[smem()] + [vmem()] * (2 * reps),
+        out_shape=[pieces] * reps,
+        in_specs=[smem()] + [vmem()] * (2 + reps),
         out_specs=[vmem()] * reps,
         scratch_shapes=[pltpu.VMEM((blocks, width, nodes), BF16)] * 2,
         compiler_params=pltpu.CompilerParams(vmem_limit_bytes=4 * MIB),
@@ -244,7 +247,7 @@
             bytes_accessed=4 * blocks * nodes * width + 2 * width * width,
             transcendentals=0,
         ),
-    )(where, *packed, *aggs)
+    )(where, aggs, weight, *shares)
 
 
 def add_kernel(one, other, out):
@@ -295,37 +298,6 @@
     )(where, aside, *terms)
 
 
-def pack_kernel(reps, where, agg, weight, *rest):
-    outs, sems = rest[:reps], rest[reps]
-    features, nodes = agg.shape[1:]
-    share = agg.shape[0] // reps
-    pieces = weight.shape[1] // nodes
-    copies = []
-    for s, out in enumerate(outs):
-        first = wrap(where[1] + s, reps) * share
-        copies.append((agg.at[pl.ds(first, share)], out.at[pl.ds(0, share)]))
-        for h in range(pieces):
-            copies.append((weight.at[:, pl.ds(h * nodes, nodes)], out.at[share + h]))
-    copies = [pltpu.make_async_copy(*ends, sems.at[i]) for i, ends in enumerate(copies)]
-    for copy in copies:
-        copy.start()
-    for copy in copies:
-        copy.wait()
-
-
-def pack(where, agg, weight, reps):
-    blocks, features, nodes = agg.shape
-    share, pieces = blocks // reps, weight.shape[1] // nodes
-    return pl.pallas_call(
-        functools.partial(pack_kernel, reps),
-        out_shape=[jax.ShapeDtypeStruct((share + pieces, features, nodes), BF16)] * reps,
-        in_specs=[smem(), hbm(), hbm()],
-        out_specs=[vmem()] * reps,
-        scratch_shapes=[pltpu.SemaphoreType.DMA((reps * (1 + pieces),))],
-        compiler_params=pltpu.CompilerParams(vmem_limit_bytes=2 * MIB),
-    )(where, in_hbm(agg), in_hbm(weight))
-
-
 def lay_kernel(reps, where, *rest):
     shares, out, sems = rest[:reps], rest[reps], rest[reps + 1]
     blocks = shares[0].shape[0]
@@ -367,7 +339,9 @@
     pair = [(i, i ^ 1) for i in range(slabs)]
     to_one = [(i, (i + (1 if i % 2 else -1)) % slabs) for i in range(slabs)]
     to_two = [(i, (i + (2 if i % 2 else -2)) % slabs) for i in range(slabs)]
-    aggs = [shift(value, s) for s, value in enumerate(pack(where, aggregated, weight, reps))]
+    aggs = lax.all_to_all(
+        aggregated.reshape(reps, blocks // reps, features, nodes), "rep", 0, 0, tiled=True
+    )
     aside, own, one, two, *packed = contributions(
         where, col_block, live_count, cotangent, relu_mask, tiles, slabs, reps
     )
@@ -379,15 +353,16 @@
 
     packed, _ = lax.optimization_barrier((packed, one))
     packed = [shift(value, s) for s, value in enumerate(packed)]
-    grad_w = weight_partial(where, packed, aggs)
-
-    own, grad_w = lax.optimization_barrier((own, grad_w))
+    pieces = weight_partial(where, aggs, weight, packed)
+
+    own, pieces = lax.optimization_barrier((own, pieces))
+    pieces = [shift(value, -s) for s, value in enumerate(pieces)]
     shares = total_shares(where, aside, [own, one_in, two_in], reps)
     shares = [shift(value, s) for s, value in enumerate(shares)]
-    outs = [shift(value, s) for s, value in enumerate(mix(where, shares, aggs))]
+    outs = [shift(value, s) for s, value in enumerate(mix(where, shares, pieces))]
     input_grad = lay_blocks(where, outs, cotangent.shape)
 
-    grad_w = sum(shift(part, -s).astype(F32) for s, part in enumerate(grad_w))
+    grad_w = sum(value[: width // nodes].astype(F32) for value in pieces)
     grad_w = grad_w + lax.ppermute(grad_w, "blk", pair)
     grad_w = grad_w + sum(
         lax.ppermute(grad_w, "blk", [(i, i ^ step) for i in range(slabs)])

time: 75.9 us -> 75.8 us (level)
  waiting for transfers between devices: 20.2 us -> 28.7 us
  starting transfers between devices: 38.4 us -> 30.8 us
  Pallas kernels: 15.1 us -> 12.9 us
  local copies, waits for them, and re-layouts: 0 us -> 1.3 us
    ppermute x15 -> x12, starting transfers between devices: 29.4 us -> 16.5 us  [shift(): lax.ppermute(value, 'rep', [(i, (i + steps) % reps) for i in range(reps)])]
    all_to_all x0 -> x1, starting transfers between devices: none -> 6.33 us  [on_device(): lax.all_to_all(aggregated.reshape(reps, blocks // reps, features, nodes),...]
    all_to_all x0 -> x1, waiting for transfers between devices: none -> 4.65 us  [on_device(): lax.all_to_all(aggregated.reshape(reps, blocks // reps, features, nodes),...]
    ppermute x15 -> x12, waiting for transfers between devices: 17.3 us -> 19.2 us  [shift(): lax.ppermute(value, 'rep', [(i, (i + steps) % reps) for i in range(reps)])]
    pallas_call x3 -> x2, Pallas kernels: 3.85 us -> 2.03 us  [the longest x1 1.03 us: weight_partial(): pl.pallas_call(functools.partial(weight_kernel, reps), out_shape=[pieces]...]
    ppermute x1, waiting for transfers between devices: 1.66 us -> 3.37 us  [on_device(): one_in = lax.ppermute(one, 'blk', to_one)]
    unnamed x0 -> x6, local copies, waits for them, and re-layouts: none -> 1.3 us
  transfers between devices with their start and end apart: 22 -> 20, of which waited for: 8 -> 10; matrix products, arithmetic and copies ran while one was open for 1% -> 1% of each run, Pallas kernels for 16% -> 15%
where the time goes in v13:
time: 75.8 us; the launch traced here: 75.2 us
  starting transfers between devices  30.8 us (41%)
  waiting for transfers between devices  28.7 us (38%)
  Pallas kernels  12.9 us (17%)
  local copies, waits for them, and re-layouts  1.3 us (2%)
    ppermute x12, waiting for transfers between devices, shift(): lax.ppermute(value, 'rep', [(i, (i + steps) % reps) for i in range(reps)])  19.2 us
    ppermute x12, starting transfers between devices, shift(): lax.ppermute(value, 'rep', [(i, (i + steps) % reps) for i in range(reps)])  16.5 us
    pallas_call x1, Pallas kernels, contributions(): pl.pallas_call(functools.partial(tiles_kernel, slabs, reps), out_shape=[j...  8.45 us
    all_to_all x1, starting transfers between devices, on_device(): lax.all_to_all(aggregated.reshape(reps, blocks // reps, features, nodes),...  6.33 us
    all_to_all x1, waiting for transfers between devices, on_device(): lax.all_to_all(aggregated.reshape(reps, blocks // reps, features, nodes),...  4.65 us
    ppermute x1, waiting for transfers between devices, on_device(): one_in = lax.ppermute(one, 'blk', to_one)  3.37 us
    ppermute x3, starting transfers between devices, on_device(): lax.ppermute(grad_w, 'blk', [(i, i ^ step) for i in range(slabs)])  3.23 us
    ppermute x1, starting transfers between devices, on_device(): two_in = lax.ppermute(two, 'blk', to_two)  2.45 us
  transfers between devices with their start and end apart: 20, of which 10 were waited for; matrix products, arithmetic and copies ran while one was open for 1% of the time, Pallas kernels for 15%

profile of v13, /device:TPU:0, one launch (start us, length us, event | category | flops | bytes accessed | tf_op | source)
XLA Modules:
  0.0 75.2 jit_solution(10886991147431307634)
XLA Ops:
  0.6 6.3 %all-to-all-start = ((bf16[4,8,64,128]{3,2,1,0:T(8,128)(2,1)}), bf16[4,8,64,128]{3,2,1,0:T(8,128)(2,1)S(1)}, u32[]{:S(2)}, u32[]{:S(2)}) async-start(bf16[4,8,64,128]{3,2,1,0:T(8,128)(2,1)} %bitcast.12), calls=%async_computation | async-start | bytes 1048576 | tf_op jit(solution)/shard_map/all_to_all | solution.py:342
  7.0 8.5 %shard_map.86 = (bf16[64,64,128]{2,1,0:T(8,128)(2,1)S(1)}, bf16[32,64,128]{2,1,0:T(8,128)(2,1)S(1)}, bf16[32,64,128]{2,1,0:T(8,128)(2,1)S(1)}, bf16[32,64,128]{2...) custom-call(s32[2]{0:T(128)S(1)} %pad_add_fusion.where, ...), custom_call_target="tpu_custom_call" | custom-call | flops 1073741824 | bytes 16777216 | tf_op jit(solution)/shard_map/pallas_call | solution.py:138
  15.5 0.6 copy-done.1
  16.2 0.7 copy-done.2
  16.8 4.6 %all-to-all-done.aggs = bf16[4,8,64,128]{3,2,1,0:T(8,128)(2,1)S(1)} async-done(((bf16[4,8,64,128]{3,2,1,0:T(8,128)(2,1)}), bf16[4,8,64,128]{3,2,1,0:T(8,128)(2,1)S(1)}, u32[]{:S(2)}, u32[]{:S(2)}) %all-to-all-start) | async-done | bytes 524320 | tf_op jit(solution)/shard_map/all_to_all | solution.py:342
  21.5 2.4 %collective-permute-start.5 = (bf16[32,64,128]{2,1,0:T(8,128)(2,1)S(1)}, bf16[32,64,128]{2,1,0:T(8,128)(2,1)S(1)}, u32[]{:S(2)}, u32[]{:S(2)}) collective-permute-start(bf16[32,64,128]{2,1,0:T(8,128)(2,1)S(1)} %get-tuple-element.51), channel_id=1, source_target_pairs={{0,24},{4,12},{8,0},{12,20},{16,8},{20,28},{24,16},{28,4},{1,25},{... | collective-permute-start | bytes 1572872 | tf_op jit(solution)/shard_map/ppermute | solution.py:350
  24.4 2.3 %collective-permute-start.4 = (bf16[32,64,128]{2,1,0:T(8,128)(2,1)S(1)}, bf16[32,64,128]{2,1,0:T(8,128)(2,1)S(1)}, u32[]{:S(2)}, u32[]{:S(2)}) collective-permute-start(bf16[32,64,128]{2,1,0:T(8,128)(2,1)S(1)} %shard_map.87), channel_id=1, source_target_pairs={{0,28},{4,8},{8,4},{12,16},{16,12},{20,24},{24,20},{28,0},{1,29},{... | collective-permute-start | bytes 1572872 | tf_op jit(solution)/shard_map/ppermute | solution.py:352
  26.6 2.0 %collective-permute-start.2 = (bf16[8,64,128]{2,1,0:T(8,128)(2,1)}, bf16[8,64,128]{2,1,0:T(8,128)(2,1)S(1)}, u32[]{:S(2)}, u32[]{:S(2)}) collective-permute-start(bf16[8,64,128]{2,1,0:T(8,128)(2,1)} %copy-done.1), channel_id=1, source_target_pairs={{0,2},{1,3},{2,0},{3,1},{4,6},{5,7},{6,4},{7,5},{8,10},{9,11},{10,... | collective-permute-start | bytes 393224 | tf_op jit(solution)/shard_map/ppermute | solution.py:330
  28.7 1.8 %collective-permute-start.3 = (bf16[8,64,128]{2,1,0:T(8,128)(2,1)S(1)}, bf16[8,64,128]{2,1,0:T(8,128)(2,1)S(1)}, u32[]{:S(2)}, u32[]{:S(2)}) collective-permute-start(bf16[8,64,128]{2,1,0:T(8,128)(2,1)S(1)} %get-tuple-element.45), channel_id=1, source_target_pairs={{0,3},{1,0},{2,1},{3,2},{4,7},{5,4},{6,5},{7,6},{8,11},{9,8},{10,9... | collective-permute-start | bytes 393224 | tf_op jit(solution)/shard_map/ppermute | solution.py:330
  30.5 4.6 %collective-permute-done.1.rest_1_ = bf16[8,64,128]{2,1,0:T(8,128)(2,1)S(1)} collective-permute-done((bf16[8,64,128]{2,1,0:T(8,128)(2,1)}, bf16[8,64,128]{2,1,0:T(8,128)(2,1)S(1)}, u32[]{:S(2)}, u32[]{:S(2)}) %collective-permute-start.1) | collective-permute-done | bytes 131104 | tf_op jit(solution)/shard_map/ppermute | solution.py:330
  35.1 4.1 %collective-permute-done.2.rest_2_ = bf16[8,64,128]{2,1,0:T(8,128)(2,1)S(1)} collective-permute-done((bf16[8,64,128]{2,1,0:T(8,128)(2,1)}, bf16[8,64,128]{2,1,0:T(8,128)(2,1)S(1)}, u32[]{:S(2)}, u32[]{:S(2)}) %collective-permute-start.2) | collective-permute-done | bytes 131104 | tf_op jit(solution)/shard_map/ppermute | solution.py:330
  39.2 1.0 %shard_map.88 = (bf16[4,64,128]{2,1,0:T(8,128)(2,1)S(1)}, bf16[4,64,128]{2,1,0:T(8,128)(2,1)S(1)}, bf16[4,64,128]{2,1,0:T(8,128)(2,1)S(1)}, bf16[4,64,128]{2,1,0:T(8,128)(2,1)S(1)}) custom-call(s32[2]{0:T(128)S(1)} %pad_add_fusion.where, bf16[4,8,64,128]{3,2,1,0:T(8,128)(2,1)S(1)} %all-to-all-done.aggs, bf16[64,256]{1,0:T(8,128)(2,1)S(1)} %copy-done, ...), custom_call_target="tpu_custom_call" | custom-call | flops 134217728 | bytes 1179648 | tf_op jit(solution)/shard_map/pallas_call | solution.py:238
  40.3 2.1 %collective-permute-start.9 = (bf16[4,64,128]{2,1,0:T(8,128)(2,1)S(1)}, bf16[4,64,128]{2,1,0:T(8,128)(2,1)S(1)}, u32[]{:S(2)}, u32[]{:S(2)}) collective-permute-start(bf16[4,64,128]{2,1,0:T(8,128)(2,1)S(1)} %get-tuple-element.57), channel_id=1, source_target_pairs={{0,3},{1,0},{2,1},{3,2},{4,7},{5,4},{6,5},{7,6},{8,11},{9,8},{10,9... | collective-permute-start | bytes 196616 | tf_op jit(solution)/shard_map/ppermute | solution.py:330
  42.4 1.7 %collective-permute-start.10 = (bf16[4,64,128]{2,1,0:T(8,128)(2,1)S(1)}, bf16[4,64,128]{2,1,0:T(8,128)(2,1)S(1)}, u32[]{:S(2)}, u32[]{:S(2)}) collective-permute-start(bf16[4,64,128]{2,1,0:T(8,128)(2,1)S(1)} %get-tuple-element.58), channel_id=1, source_target_pairs={{0,2},{1,3},{2,0},{3,1},{4,6},{5,7},{6,4},{7,5},{8,10},{9,11},{10,... | collective-permute-start | bytes 196616 | tf_op jit(solution)/shard_map/ppermute | solution.py:330
  44.1 3.4 %collective-permute-done.4.rest_1_ = bf16[32,64,128]{2,1,0:T(8,128)(2,1)S(1)} collective-permute-done((bf16[32,64,128]{2,1,0:T(8,128)(2,1)S(1)}, bf16[32,64,128]{2,1,0:T(8,128)(2,1)S(1)}, u32[]{:S(2)}, u32[]{:S(2)}) %collective-permute-start.4) | collective-permute-done | bytes 524320 | tf_op jit(solution)/shard_map/ppermute | solution.py:352
  47.5 0.8 %shard_map.89 = (bf16[8,64,128]{2,1,0:T(8,128)(2,1)S(1)}, bf16[8,64,128]{2,1,0:T(8,128)(2,1)S(1)}, bf16[8,64,128]{2,1,0:T(8,128)(2,1)S(1)}, bf16[8,64,128]{2,1,0:T(8,128)(2,1)S(1)}) custom-call(s32[2]{0:T(128)S(1)} %pad_add_fusion.where, bf16[64,64,128]{2,1,0:T(8,128)(2,1)S(1)} %collective-permute-done.other.aside, ...), custom_call_target="tpu_custom_call" | custom-call | flops 1048576 | bytes 2621440 | tf_op jit(solution)/shard_map/pallas_call | solution.py:289
  48.4 2.0 %collective-permute-start.7 = (bf16[8,64,128]{2,1,0:T(8,128)(2,1)S(1)}, bf16[8,64,128]{2,1,0:T(8,128)(2,1)S(1)}, u32[]{:S(2)}, u32[]{:S(2)}) collective-permute-start(bf16[8,64,128]{2,1,0:T(8,128)(2,1)S(1)} %get-tuple-element.54), channel_id=1, source_target_pairs={{0,2},{1,3},{2,0},{3,1},{4,6},{5,7},{6,4},{7,5},{8,10},{9,11},{10,... | collective-permute-start | bytes 393224 | tf_op jit(solution)/shard_map/ppermute | solution.py:330
  50.4 1.8 %collective-permute-start.8 = (bf16[8,64,128]{2,1,0:T(8,128)(2,1)S(1)}, bf16[8,64,128]{2,1,0:T(8,128)(2,1)S(1)}, u32[]{:S(2)}, u32[]{:S(2)}) collective-permute-start(bf16[8,64,128]{2,1,0:T(8,128)(2,1)S(1)} %get-tuple-element.55), channel_id=1, source_target_pairs={{0,3},{1,0},{2,1},{3,2},{4,7},{5,4},{6,5},{7,6},{8,11},{9,8},{10,9... | collective-permute-start | bytes 393224 | tf_op jit(solution)/shard_map/ppermute | solution.py:330
  52.3 1.2 %collective-permute-done.15 = f32[2,64,128]{2,1,0:T(8,128)S(1)} collective-permute-done((f32[2,64,128]{2,1,0:T(8,128)S(1)}, f32[2,64,128]{2,1,0:T(8,128)S(1)}, u32[]{:S(2)}, u32[]{:S(2)}) %collective-permute-start.15) | collective-permute-done | bytes 65568 | tf_op jit(solution)/shard_map/ppermute | solution.py:366
  53.5 1.7 %collective-permute-start.18 = (f32[2,64,128]{2,1,0:T(8,128)S(1)}, f32[2,64,128]{2,1,0:T(8,128)S(1)}, u32[]{:S(2)}, u32[]{:S(2)}) collective-permute-start(f32[2,64,128]{2,1,0:T(8,128)S(1)} %add.24), channel_id=1, source_target_pairs={{0,24},{4,28},{8,16},{12,20},{16,8},{20,12},{24,0},{28,4},{1,25},{... | collective-permute-start | bytes 196616 | tf_op jit(solution)/shard_map/ppermute | solution.py:368
  55.3 1.0 %collective-permute-start.17 = (f32[2,64,128]{2,1,0:T(8,128)S(1)}, f32[2,64,128]{2,1,0:T(8,128)S(1)}, u32[]{:S(2)}, u32[]{:S(2)}) collective-permute-start(f32[2,64,128]{2,1,0:T(8,128)S(1)} %add.24), channel_id=1, source_target_pairs={{0,16},{4,20},{8,24},{12,28},{16,0},{20,4},{24,8},{28,12},{1,17},{... | collective-permute-start | bytes 196616 | tf_op jit(solution)/shard_map/ppermute | solution.py:368
  56.3 0.3 collective-permute-done.6.rest_1_
  56.6 0.5 collective-permute-start.16
  57.1 3.9 %collective-permute-done.7.rest_2_ = bf16[8,64,128]{2,1,0:T(8,128)(2,1)S(1)} collective-permute-done((bf16[8,64,128]{2,1,0:T(8,128)(2,1)S(1)}, bf16[8,64,128]{2,1,0:T(8,128)(2,1)S(1)}, u32[]{:S(2)}, u32[]{:S(2)}) %collective-permute-start.7) | collective-permute-done | bytes 131104 | tf_op jit(solution)/shard_map/ppermute | solution.py:330
  61.0 1.0 %shard_map.90 = (bf16[8,64,128]{2,1,0:T(8,128)(2,1)S(1)}, bf16[8,64,128]{2,1,0:T(8,128)(2,1)S(1)}, bf16[8,64,128]{2,1,0:T(8,128)(2,1)S(1)}, bf16[8,64,128]{2,1,0:T(8,128)(2,1)S(1)}) custom-call(s32[2]{0:T(128)S(1)} %pad_add_fusion.where, bf16[8,64,128]{2,1,0:T(8,128)(2,1)S(1)} %get-tuple-element.52.rest_0_, ...), custom_call_target="tpu_custom_call" | custom-call | flops 134217728 | bytes 1048576 | tf_op jit(solution)/shard_map/pallas_call | solution.py:199
  62.0 2.5 %collective-permute-start.12 = (bf16[8,64,128]{2,1,0:T(8,128)(2,1)S(1)}, bf16[8,64,128]{2,1,0:T(8,128)(2,1)S(1)}, u32[]{:S(2)}, u32[]{:S(2)}) collective-permute-start(bf16[8,64,128]{2,1,0:T(8,128)(2,1)S(1)} %get-tuple-element.61), channel_id=1, source_target_pairs={{0,1},{1,2},{2,3},{3,0},{4,5},{5,6},{6,7},{7,4},{8,9},{9,10},{10,1... | collective-permute-start | bytes 393224 | tf_op jit(solution)/shard_map/ppermute | solution.py:330
  64.5 0.4 collective-permute-start.13
  64.9 2.1 %collective-permute-start.14 = (bf16[8,64,128]{2,1,0:T(8,128)(2,1)S(1)}, bf16[8,64,128]{2,1,0:T(8,128)(2,1)S(1)}, u32[]{:S(2)}, u32[]{:S(2)}) collective-permute-start(bf16[8,64,128]{2,1,0:T(8,128)(2,1)S(1)} %get-tuple-element.63), channel_id=1, source_target_pairs={{0,3},{1,0},{2,1},{3,2},{4,7},{5,4},{6,5},{7,6},{8,11},{9,8},{10,9... | collective-permute-start | bytes 393224 | tf_op jit(solution)/shard_map/ppermute | solution.py:330
  66.9 0.6 copy_bitcast_fusion
  67.6 2.7 %collective-permute-done.12.rest_1_ = bf16[8,64,128]{2,1,0:T(8,128)(2,1)S(1)} collective-permute-done((bf16[8,64,128]{2,1,0:T(8,128)(2,1)S(1)}, bf16[8,64,128]{2,1,0:T(8,128)(2,1)S(1)}, u32[]{:S(2)}, u32[]{:S(2)}) %collective-permute-start.12) | collective-permute-done | bytes 131104 | tf_op jit(solution)/shard_map/ppermute | solution.py:330
  70.3 3.5 %collective-permute-done.13.rest_2_ = bf16[8,64,128]{2,1,0:T(8,128)(2,1)S(1)} collective-permute-done((bf16[8,64,128]{2,1,0:T(8,128)(2,1)S(1)}, bf16[8,64,128]{2,1,0:T(8,128)(2,1)S(1)}, u32[]{:S(2)}, u32[]{:S(2)}) %collective-permute-start.13) | collective-permute-done | bytes 131104 | tf_op jit(solution)/shard_map/ppermute | solution.py:330
  73.8 1.4 %shard_map.91 = bf16[32,64,128]{2,1,0:T(8,128)(2,1)} custom-call(s32[2]{0:T(128)S(1)} %pad_add_fusion.where, bf16[8,64,128]{2,1,0:T(8,128)(2,1)S(1)} %get-tuple-element.60.rest_0_, bf16[8,64,128]{2,1,0:T(8,128)(2,1)S(1)} %collective-permute-done.12.rest_1_, bf16[8,64,128]{2,1,0:T(8,128)(2,1)S(1)} %collective-permute-done.13.rest_2_, ...), custom_call_target="tpu_custom_call" | custom-call | bytes 33554432 | tf_op jit(solution)/shard_map/pallas_call | solution.py:315
  (24 shorter events, 0.7 us)
Async XLA Ops:
  0.6 38.6 %copy-start = (bf16[64,256]{1,0:T(8,128)(2,1)S(1)}, bf16[64,256]{1,0:T(8,128)(2,1)}, u32[]{:S(2)}) copy-start(bf16[64,256]{1,0:T(8,128)(2,1)} %weight.1) | copy-start | bytes 98308
  0.6 20.8 %all-to-all-start = ((bf16[4,8,64,128]{3,2,1,0:T(8,128)(2,1)}), bf16[4,8,64,128]{3,2,1,0:T(8,128)(2,1)S(1)}, u32[]{:S(2)}, u32[]{:S(2)}) async-start(bf16[4,8,64,128]{3,2,1,0:T(8,128)(2,1)} %bitcast.12), calls=%async_computation | async-start | bytes 1048576 | tf_op jit(solution)/shard_map/all_to_all | solution.py:342
  15.5 0.6 copy-start.1
  16.2 0.7 copy-start.2
  21.5 2.7 %collective-permute-start = (bf16[64,64,128]{2,1,0:T(8,128)(2,1)S(1)}, bf16[64,64,128]{2,1,0:T(8,128)(2,1)S(1)}, u32[]{:S(2)}, u32[]{:S(2)}) collective-permute-start(bf16[64,64,128]{2,1,0:T(8,128)(2,1)S(1)} %get-tuple-element.34), channel_id=1, source_target_pairs={{0,4},{4,0},{8,12},{12,8},{16,20},{20,16},{24,28},{28,24},{1,5},{5... | collective-permute-start | bytes 3145736 | tf_op jit(solution)/shard_map/ppermute | solution.py:349
  21.5 22.7 %collective-permute-start.5 = (bf16[32,64,128]{2,1,0:T(8,128)(2,1)S(1)}, bf16[32,64,128]{2,1,0:T(8,128)(2,1)S(1)}, u32[]{:S(2)}, u32[]{:S(2)}) collective-permute-start(bf16[32,64,128]{2,1,0:T(8,128)(2,1)S(1)} %get-tuple-element.51), channel_id=1, source_target_pairs={{0,24},{4,12},{8,0},{12,20},{16,8},{20,28},{24,16},{28,4},{1,25},{... | collective-permute-start | bytes 1572872 | tf_op jit(solution)/shard_map/ppermute | solution.py:350
  24.4 23.1 %collective-permute-start.4 = (bf16[32,64,128]{2,1,0:T(8,128)(2,1)S(1)}, bf16[32,64,128]{2,1,0:T(8,128)(2,1)S(1)}, u32[]{:S(2)}, u32[]{:S(2)}) collective-permute-start(bf16[32,64,128]{2,1,0:T(8,128)(2,1)S(1)} %shard_map.87), channel_id=1, source_target_pairs={{0,28},{4,8},{8,4},{12,16},{16,12},{20,24},{24,20},{28,0},{1,29},{... | collective-permute-start | bytes 1572872 | tf_op jit(solution)/shard_map/ppermute | solution.py:352
  26.6 8.5 %collective-permute-start.1 = (bf16[8,64,128]{2,1,0:T(8,128)(2,1)}, bf16[8,64,128]{2,1,0:T(8,128)(2,1)S(1)}, u32[]{:S(2)}, u32[]{:S(2)}) collective-permute-start(bf16[8,64,128]{2,1,0:T(8,128)(2,1)} %copy-done.2), channel_id=1, source_target_pairs={{0,1},{1,2},{2,3},{3,0},{4,5},{5,6},{6,7},{7,4},{8,9},{9,10},{10,1... | collective-permute-start | bytes 393224 | tf_op jit(solution)/shard_map/ppermute | solution.py:330
  26.6 12.6 %collective-permute-start.2 = (bf16[8,64,128]{2,1,0:T(8,128)(2,1)}, bf16[8,64,128]{2,1,0:T(8,128)(2,1)S(1)}, u32[]{:S(2)}, u32[]{:S(2)}) collective-permute-start(bf16[8,64,128]{2,1,0:T(8,128)(2,1)} %copy-done.1), channel_id=1, source_target_pairs={{0,2},{1,3},{2,0},{3,1},{4,6},{5,7},{6,4},{7,5},{8,10},{9,11},{10,... | collective-permute-start | bytes 393224 | tf_op jit(solution)/shard_map/ppermute | solution.py:330
  28.7 10.6 %collective-permute-start.3 = (bf16[8,64,128]{2,1,0:T(8,128)(2,1)S(1)}, bf16[8,64,128]{2,1,0:T(8,128)(2,1)S(1)}, u32[]{:S(2)}, u32[]{:S(2)}) collective-permute-start(bf16[8,64,128]{2,1,0:T(8,128)(2,1)S(1)} %get-tuple-element.45), channel_id=1, source_target_pairs={{0,3},{1,0},{2,1},{3,2},{4,7},{5,4},{6,5},{7,6},{8,11},{9,8},{10,9... | collective-permute-start | bytes 393224 | tf_op jit(solution)/shard_map/ppermute | solution.py:330
  40.3 10.1 %collective-permute-start.9 = (bf16[4,64,128]{2,1,0:T(8,128)(2,1)S(1)}, bf16[4,64,128]{2,1,0:T(8,128)(2,1)S(1)}, u32[]{:S(2)}, u32[]{:S(2)}) collective-permute-start(bf16[4,64,128]{2,1,0:T(8,128)(2,1)S(1)} %get-tuple-element.57), channel_id=1, source_target_pairs={{0,3},{1,0},{2,1},{3,2},{4,7},{5,4},{6,5},{7,6},{8,11},{9,8},{10,9... | collective-permute-start | bytes 196616 | tf_op jit(solution)/shard_map/ppermute | solution.py:330
  42.4 9.8 %collective-permute-start.10 = (bf16[4,64,128]{2,1,0:T(8,128)(2,1)S(1)}, bf16[4,64,128]{2,1,0:T(8,128)(2,1)S(1)}, u32[]{:S(2)}, u32[]{:S(2)}) collective-permute-start(bf16[4,64,128]{2,1,0:T(8,128)(2,1)S(1)} %get-tuple-element.58), channel_id=1, source_target_pairs={{0,2},{1,3},{2,0},{3,1},{4,6},{5,7},{6,4},{7,5},{8,10},{9,11},{10,... | collective-permute-start | bytes 196616 | tf_op jit(solution)/shard_map/ppermute | solution.py:330
  44.1 8.1 %collective-permute-start.11 = (bf16[4,64,128]{2,1,0:T(8,128)(2,1)S(1)}, bf16[4,64,128]{2,1,0:T(8,128)(2,1)S(1)}, u32[]{:S(2)}, u32[]{:S(2)}) collective-permute-start(bf16[4,64,128]{2,1,0:T(8,128)(2,1)S(1)} %get-tuple-element.59), channel_id=1, source_target_pairs={{0,1},{1,2},{2,3},{3,0},{4,5},{5,6},{6,7},{7,4},{8,9},{9,10},{10,1... | collective-permute-start | bytes 196616 | tf_op jit(solution)/shard_map/ppermute | solution.py:330
  48.3 8.3 %collective-permute-start.6 = (bf16[8,64,128]{2,1,0:T(8,128)(2,1)S(1)}, bf16[8,64,128]{2,1,0:T(8,128)(2,1)S(1)}, u32[]{:S(2)}, u32[]{:S(2)}) collective-permute-start(bf16[8,64,128]{2,1,0:T(8,128)(2,1)S(1)} %get-tuple-element.53), channel_id=1, source_target_pairs={{0,1},{1,2},{2,3},{3,0},{4,5},{5,6},{6,7},{7,4},{8,9},{9,10},{10,1... | collective-permute-start | bytes 393224 | tf_op jit(solution)/shard_map/ppermute | solution.py:330
  48.4 12.6 %collective-permute-start.7 = (bf16[8,64,128]{2,1,0:T(8,128)(2,1)S(1)}, bf16[8,64,128]{2,1,0:T(8,128)(2,1)S(1)}, u32[]{:S(2)}, u32[]{:S(2)}) collective-permute-start(bf16[8,64,128]{2,1,0:T(8,128)(2,1)S(1)} %get-tuple-element.54), channel_id=1, source_target_pairs={{0,2},{1,3},{2,0},{3,1},{4,6},{5,7},{6,4},{7,5},{8,10},{9,11},{10,... | collective-permute-start | bytes 393224 | tf_op jit(solution)/shard_map/ppermute | solution.py:330
  50.4 10.6 %collective-permute-start.8 = (bf16[8,64,128]{2,1,0:T(8,128)(2,1)S(1)}, bf16[8,64,128]{2,1,0:T(8,128)(2,1)S(1)}, u32[]{:S(2)}, u32[]{:S(2)}) collective-permute-start(bf16[8,64,128]{2,1,0:T(8,128)(2,1)S(1)} %get-tuple-element.55), channel_id=1, source_target_pairs={{0,3},{1,0},{2,1},{3,2},{4,7},{5,4},{6,5},{7,6},{8,11},{9,8},{10,9... | collective-permute-start | bytes 393224 | tf_op jit(solution)/shard_map/ppermute | solution.py:330
  52.2 1.3 %collective-permute-start.15 = (f32[2,64,128]{2,1,0:T(8,128)S(1)}, f32[2,64,128]{2,1,0:T(8,128)S(1)}, u32[]{:S(2)}, u32[]{:S(2)}) collective-permute-start(f32[2,64,128]{2,1,0:T(8,128)S(1)} %convert_add_fusion), channel_id=1, source_target_pairs={{0,4},{4,0},{8,12},{12,8},{16,20},{20,16},{24,28},{28,24},{1,5},{5... | collective-permute-start | bytes 196616 | tf_op jit(solution)/shard_map/ppermute | solution.py:366
  53.5 11.4 %collective-permute-start.18 = (f32[2,64,128]{2,1,0:T(8,128)S(1)}, f32[2,64,128]{2,1,0:T(8,128)S(1)}, u32[]{:S(2)}, u32[]{:S(2)}) collective-permute-start(f32[2,64,128]{2,1,0:T(8,128)S(1)} %add.24), channel_id=1, source_target_pairs={{0,24},{4,28},{8,16},{12,20},{16,8},{20,12},{24,0},{28,4},{1,25},{... | collective-permute-start | bytes 196616 | tf_op jit(solution)/shard_map/ppermute | solution.py:368
  55.3 11.7 %collective-permute-start.17 = (f32[2,64,128]{2,1,0:T(8,128)S(1)}, f32[2,64,128]{2,1,0:T(8,128)S(1)}, u32[]{:S(2)}, u32[]{:S(2)}) collective-permute-start(f32[2,64,128]{2,1,0:T(8,128)S(1)} %add.24), channel_id=1, source_target_pairs={{0,16},{4,20},{8,24},{12,28},{16,0},{20,4},{24,8},{28,12},{1,17},{... | collective-permute-start | bytes 196616 | tf_op jit(solution)/shard_map/ppermute | solution.py:368
  56.6 10.3 %collective-permute-start.16 = (f32[2,64,128]{2,1,0:T(8,128)S(1)}, f32[2,64,128]{2,1,0:T(8,128)S(1)}, u32[]{:S(2)}, u32[]{:S(2)}) collective-permute-start(f32[2,64,128]{2,1,0:T(8,128)S(1)} %add.24), channel_id=1, source_target_pairs={{0,8},{4,12},{8,0},{12,4},{16,24},{20,28},{24,16},{28,20},{1,9},{5... | collective-permute-start | bytes 196616 | tf_op jit(solution)/shard_map/ppermute | solution.py:368
  62.0 8.3 %collective-permute-start.12 = (bf16[8,64,128]{2,1,0:T(8,128)(2,1)S(1)}, bf16[8,64,128]{2,1,0:T(8,128)(2,1)S(1)}, u32[]{:S(2)}, u32[]{:S(2)}) collective-permute-start(bf16[8,64,128]{2,1,0:T(8,128)(2,1)S(1)} %get-tuple-element.61), channel_id=1, source_target_pairs={{0,1},{1,2},{2,3},{3,0},{4,5},{5,6},{6,7},{7,4},{8,9},{9,10},{10,1... | collective-permute-start | bytes 393224 | tf_op jit(solution)/shard_map/ppermute | solution.py:330
  64.5 9.3 %collective-permute-start.13 = (bf16[8,64,128]{2,1,0:T(8,128)(2,1)S(1)}, bf16[8,64,128]{2,1,0:T(8,128)(2,1)S(1)}, u32[]{:S(2)}, u32[]{:S(2)}) collective-permute-start(bf16[8,64,128]{2,1,0:T(8,128)(2,1)S(1)} %get-tuple-element.62), channel_id=1, source_target_pairs={{0,2},{1,3},{2,0},{3,1},{4,6},{5,7},{6,4},{7,5},{8,10},{9,11},{10,... | collective-permute-start | bytes 393224 | tf_op jit(solution)/shard_map/ppermute | solution.py:330
  64.9 8.9 %collective-permute-start.14 = (bf16[8,64,128]{2,1,0:T(8,128)(2,1)S(1)}, bf16[8,64,128]{2,1,0:T(8,128)(2,1)S(1)}, u32[]{:S(2)}, u32[]{:S(2)}) collective-permute-start(bf16[8,64,128]{2,1,0:T(8,128)(2,1)S(1)} %get-tuple-element.63), channel_id=1, source_target_pairs={{0,3},{1,0},{2,1},{3,2},{4,7},{5,4},{6,5},{7,6},{8,11},{9,8},{10,9... | collective-permute-start | bytes 393224 | tf_op jit(solution)/shard_map/ppermute | solution.py:330

commit v14 on v13

--- a/solution.py
+++ b/solution.py
@@ -38,10 +38,11 @@
     return value & (size - 1)
 
 
-def tiles_kernel(slabs, reps, where, cols, live, cot, mask, tiles, *rest):
+def tiles_kernel(slabs, reps, where, cols, live, cot, mask, agg, weight, tiles, *rest):
     outs, packed, rest = rest[:4], rest[4 : 4 + reps], rest[4 + reps :]
     outs = [outs[0].at[pl.ds(0, cols.shape[1])], outs[0].at[pl.ds(cols.shape[1], cols.shape[1])], *outs[1:]]
-    cot_in, mask_in, z, held, total, rows, left, sems, z_sems = rest
+    cot_in, mask_in, z, held, total, rows, left, sems, z_sems, agg_sems = rest
+    share = cols.shape[1] // reps
     slots, blocks = cols.shape
     per_row = slots // GROUP
     window = (2 * REACH + 1) * blocks
@@ -93,9 +94,19 @@
         return carry
 
     lax.fori_loop(0, blocks, mask_row, 0)
-    share = blocks // reps
-    for s in range(reps):
-        packed[s][...] = z[pl.ds(wrap(where[1] + s, reps) * share, share)]
+    agg_copies = []
+    for s in range(reps):
+        span = pl.ds(wrap(where[1] + s, reps) * share, share)
+        packed[s][:share] = z[span]
+        end = packed[s].at[pl.ds(share, share)]
+        ends = [(agg.at[span], end)]
+        for h in range(weight.shape[1] // z.shape[2]):
+            columns = pl.ds(h * z.shape[2], z.shape[2])
+            ends.append((weight.at[:, columns], packed[s].at[2 * share + h]))
+        for source, target in ends:
+            copy = pltpu.make_async_copy(source, target, agg_sems.at[len(agg_copies)])
+            copy.start()
+            agg_copies.append(copy)
     shift = REACH * blocks - where[0] * blocks
 
     def step(i, ready):
@@ -116,6 +127,8 @@
 
     ready = lax.fori_loop(0, steps, step, jnp.int32(0))
     lax.fori_loop(ready, blocks, wait_row, 0)
+    for copy in agg_copies:
+        copy.wait()
     sign = 2 * lax.rem(where[0], 2) - 1
     for order, out in enumerate(outs):
         base = ((order - REACH) * sign + REACH) * blocks
@@ -129,17 +142,19 @@
         lax.fori_loop(0, blocks // GROUP, store, 0)
 
 
-def contributions(where, cols, live, cot, mask, tiles, slabs, reps):
+def contributions(where, cols, live, cot, mask, agg, weight, tiles, slabs, reps):
     blocks, slots, nodes = tiles.shape[:3]
     features = cot.shape[1]
     window = (2 * REACH + 1) * blocks
     lists = blocks * (slots // GROUP) + slots // GROUP + STEP
     counts = [2 * blocks, blocks, blocks, blocks]
+    halves = weight.shape[1] // nodes
+    packs = 2 * blocks // reps + halves
     return pl.pallas_call(
         functools.partial(tiles_kernel, slabs, reps),
         out_shape=[jax.ShapeDtypeStruct((count, features, nodes), BF16) for count in counts]
-        + [jax.ShapeDtypeStruct((blocks // reps, features, nodes), BF16)] * reps,
-        in_specs=[smem()] * 3 + [hbm()] * 3,
+        + [jax.ShapeDtypeStruct((packs, features, nodes), BF16)] * reps,
+        in_specs=[smem()] * 3 + [hbm()] * 5,
         out_specs=[vmem()] * (len(counts) + reps),
         scratch_shapes=[
             pltpu.VMEM(cot.shape, BF16),
@@ -151,6 +166,7 @@
             pltpu.SMEM((lists,), jnp.int32),
             pltpu.SemaphoreType.DMA((blocks,)),
             pltpu.SemaphoreType.DMA((2,)),
+            pltpu.SemaphoreType.DMA((reps * (1 + halves),)),
         ],
         compiler_params=pltpu.CompilerParams(vmem_limit_bytes=30 * MIB),
         cost_estimate=pl.CostEstimate(
@@ -164,6 +180,8 @@
         in_hbm(live),
         in_hbm(cot),
         in_hbm(mask),
+        in_hbm(agg),
+        in_hbm(weight),
         in_hbm(tiles.reshape(blocks * slots, nodes, nodes)),
     )
 
@@ -177,22 +195,21 @@
 
 
 def mix_kernel(reps, where, *rest):
-    shares, pieces, outs = rest[:reps], rest[reps : 2 * reps], rest[2 * reps : 3 * reps]
+    shares, packed, outs = rest[:reps], rest[reps : 2 * reps], rest[2 * reps : 3 * reps]
     weights, whole = rest[3 * reps :]
     blocks, features, nodes = outs[0].shape
-    halves = weights.shape[1] // nodes
     lay_features(where, shares, whole)
     for s in range(reps):
-        for h in range(halves):
+        for h in range(weights.shape[1] // nodes):
             rows, columns = pl.ds(s * features, features), pl.ds(h * nodes, nodes)
-            weights[rows, columns] = pieces[s][halves + h]
+            weights[rows, columns] = packed[(reps - s) % reps][2 * blocks + h]
     for b in range(blocks):
         mixed = jnp.dot(weights[...], whole[b], preferred_element_type=F32)
         for s in range(reps):
             outs[s][b] = mixed[s * features : (s + 1) * features].astype(BF16)
 
 
-def mix(where, shares, pieces):
+def mix(where, shares, packed):
     reps = len(shares)
     blocks, features, nodes = shares[0].shape
     width = reps * features
@@ -208,37 +225,35 @@
             bytes_accessed=4 * blocks * nodes * width,
             transcendentals=0,
         ),
-    )(where, *shares, *pieces)
-
-
-def weight_kernel(reps, where, aggs, weight, *rest):
-    shares, outs, (whole_z, whole_a) = rest[:reps], rest[reps : 2 * reps], rest[2 * reps :]
-    blocks, features, nodes = shares[0].shape
-    halves = weight.shape[1] // nodes
-    lay_features(where, shares, whole_z)
-    for s in range(reps):
-        whole_a[:, pl.ds(s * features, features), :] = aggs[wrap(where[1] - s, reps)]
+    )(where, *shares, *packed)
+
+
+def weight_kernel(reps, where, *rest):
+    packed, outs, (whole_z, whole_a) = rest[:reps], rest[reps : 2 * reps], rest[2 * reps :]
+    blocks, _, nodes = whole_z.shape
+    features = packed[0].shape[1]
+    lay_features(where, packed, whole_z)
+    for s in range(reps):
+        whole_a[:, pl.ds(s * features, features), :] = packed[s][blocks : 2 * blocks]
     total = jnp.zeros((whole_a.shape[1], whole_z.shape[1]), F32)
     for b in range(blocks):
         total += lax.dot_general(
             whole_a[b], whole_z[b], (((1,), (1,)), ((), ())), preferred_element_type=F32
         )
     for s in range(reps):
-        for h in range(halves):
-            columns = slice(h * nodes, (h + 1) * nodes)
-            outs[s][h] = total[s * features : (s + 1) * features, columns].astype(BF16)
-            outs[s][halves + h] = weight[:, columns]
-
-
-def weight_partial(where, aggs, weight, shares):
-    reps = len(shares)
-    blocks, features, nodes = shares[0].shape
+        for h in range(outs[s].shape[0]):
+            part = total[s * features : (s + 1) * features, h * nodes : (h + 1) * nodes]
+            outs[s][h] = part.astype(BF16)
+
+
+def weight_partial(where, packed, blocks):
+    reps = len(packed)
+    _, features, nodes = packed[0].shape
     width = reps * features
-    pieces = jax.ShapeDtypeStruct((2 * (width // nodes), features, nodes), BF16)
     return pl.pallas_call(
         functools.partial(weight_kernel, reps),
-        out_shape=[pieces] * reps,
-        in_specs=[smem()] + [vmem()] * (2 + reps),
+        out_shape=[jax.ShapeDtypeStruct((width // nodes, features, nodes), BF16)] * reps,
+        in_specs=[smem()] + [vmem()] * reps,
         out_specs=[vmem()] * reps,
         scratch_shapes=[pltpu.VMEM((blocks, width, nodes), BF16)] * 2,
         compiler_params=pltpu.CompilerParams(vmem_limit_bytes=4 * MIB),
@@ -247,7 +262,7 @@
             bytes_accessed=4 * blocks * nodes * width + 2 * width * width,
             transcendentals=0,
         ),
-    )(where, aggs, weight, *shares)
+    )(where, *packed)
 
 
 def add_kernel(one, other, out):
@@ -339,13 +354,9 @@
     pair = [(i, i ^ 1) for i in range(slabs)]
     to_one = [(i, (i + (1 if i % 2 else -1)) % slabs) for i in range(slabs)]
     to_two = [(i, (i + (2 if i % 2 else -2)) % slabs) for i in range(slabs)]
-    aggs = lax.all_to_all(
-        aggregated.reshape(reps, blocks // reps, features, nodes), "rep", 0, 0, tiled=True
+    aside, own, one, two, *packed = contributions(
+        where, col_block, live_count, cotangent, relu_mask, aggregated, weight, tiles, slabs, reps
     )
-    aside, own, one, two, *packed = contributions(
-        where, col_block, live_count, cotangent, relu_mask, tiles, slabs, reps
-    )
-    aside, aggs = lax.optimization_barrier((aside, aggs))
     aside = lax.ppermute(aside, "blk", pair)
     two_in = lax.ppermute(two, "blk", to_two)
     one = add(one, aside)
@@ -353,21 +364,22 @@
 
     packed, _ = lax.optimization_barrier((packed, one))
     packed = [shift(value, s) for s, value in enumerate(packed)]
-    pieces = weight_partial(where, aggs, weight, packed)
-
-    own, pieces = lax.optimization_barrier((own, pieces))
+    shares = total_shares(where, aside, [own, one_in, two_in], reps)
+    held, _ = lax.optimization_barrier((packed, shares))
+    pieces = weight_partial(where, held, blocks // reps)
     pieces = [shift(value, -s) for s, value in enumerate(pieces)]
-    shares = total_shares(where, aside, [own, one_in, two_in], reps)
     shares = [shift(value, s) for s, value in enumerate(shares)]
-    outs = [shift(value, s) for s, value in enumerate(mix(where, shares, pieces))]
+    outs = [shift(value, s) for s, value in enumerate(mix(where, shares, packed))]
     input_grad = lay_blocks(where, outs, cotangent.shape)
 
-    grad_w = sum(value[: width // nodes].astype(F32) for value in pieces)
+    grad_w = sum(value.astype(F32) for value in pieces)
     grad_w = grad_w + lax.ppermute(grad_w, "blk", pair)
-    grad_w = grad_w + sum(
+    parts = [
         lax.ppermute(grad_w, "blk", [(i, i ^ step) for i in range(slabs)])
         for step in range(2, slabs, 2)
-    )
+    ]
+    parts, _ = lax.optimization_barrier((parts, input_grad))
+    grad_w = grad_w + sum(parts)
     grad_w = grad_w.transpose(1, 0, 2).reshape(features, width)
     return input_grad, grad_w * (1.0 / math.sqrt(slabs * blocks * nodes))
 

time: 75.8 us -> 72.9 us (0.962)
  starting transfers between devices: 30.8 us -> 38.7 us
  waiting for transfers between devices: 28.7 us -> 20.9 us
  Pallas kernels: 12.9 us -> 11.3 us
  local copies, waits for them, and re-layouts: 1.3 us -> 0 us
    ppermute x12, waiting for transfers between devices: 19.2 us -> 5.57 us  [shift(): lax.ppermute(value, 'rep', [(i, (i + steps) % reps) for i in range(reps)])]
    ppermute x12, starting transfers between devices: 16.5 us -> 27 us  [shift(): lax.ppermute(value, 'rep', [(i, (i + steps) % reps) for i in range(reps)])]
    ppermute x1, waiting for transfers between devices: 3.37 us -> 10.8 us  [on_device(): one_in = lax.ppermute(one, 'blk', to_one)]
    all_to_all x1 -> x0, starting transfers between devices: 6.33 us -> none  [on_device(): lax.all_to_all(aggregated.reshape(reps, blocks // reps, features, nodes),...]
    all_to_all x1 -> x0, waiting for transfers between devices: 4.65 us -> none  [on_device(): lax.all_to_all(aggregated.reshape(reps, blocks // reps, features, nodes),...]
    ppermute x1, waiting for transfers between devices: 0.01 us -> 4.52 us  [on_device(): two_in = lax.ppermute(two, 'blk', to_two)]
    ppermute x1, starting transfers between devices: 2.45 us -> 5.23 us  [on_device(): two_in = lax.ppermute(two, 'blk', to_two)]
    pallas_call x1, Pallas kernels: 8.45 us -> 6.85 us  [contributions(): pl.pallas_call(functools.partial(tiles_kernel, slabs, reps), out_shape=[j...]
  transfers between devices with their start and end apart: 20 -> 19, of which waited for: 10 -> 6; matrix products, arithmetic and copies ran while one was open for 1% -> 0% of each run, Pallas kernels for 15% -> 6%
where the time goes in v14:
time: 72.9 us; the launch traced here: 72.4 us
  starting transfers between devices  38.7 us (53%)
  waiting for transfers between devices  20.9 us (29%)
  Pallas kernels  11.3 us (16%)
  other arithmetic  0.75 us (1%)
  between operations  0.74 us (1%)
    ppermute x12, starting transfers between devices, shift(): lax.ppermute(value, 'rep', [(i, (i + steps) % reps) for i in range(reps)])  27 us
    ppermute x1, waiting for transfers between devices, on_device(): one_in = lax.ppermute(one, 'blk', to_one)  10.8 us
    pallas_call x1, Pallas kernels, contributions(): pl.pallas_call(functools.partial(tiles_kernel, slabs, reps), out_shape=[j...  6.85 us
    ppermute x12, waiting for transfers between devices, shift(): lax.ppermute(value, 'rep', [(i, (i + steps) % reps) for i in range(reps)])  5.57 us
    ppermute x1, starting transfers between devices, on_device(): two_in = lax.ppermute(two, 'blk', to_two)  5.23 us
    ppermute x1, waiting for transfers between devices, on_device(): two_in = lax.ppermute(two, 'blk', to_two)  4.52 us
    ppermute x3, starting transfers between devices, on_device(): lax.ppermute(grad_w, 'blk', [(i, i ^ step) for i in range(slabs)])  3.55 us
    ppermute x1, starting transfers between devices, on_device(): one_in = lax.ppermute(one, 'blk', to_one)  2.4 us
  transfers between devices with their start and end apart: 19, of which 6 were waited for; matrix products, arithmetic and copies ran while one was open for 0% of the time, Pallas kernels for 6%

profile of v14, /device:TPU:0, one launch (start us, length us, event | category | flops | bytes accessed | tf_op | source)
XLA Modules:
  0.0 72.4 jit_solution(15520825597510076805)
XLA Ops:
  0.6 0.1 pad_add_fusion.where
  0.7 6.8 %shard_map.86 = (bf16[64,64,128]{2,1,0:T(8,128)(2,1)S(1)}, bf16[32,64,128]{2,1,0:T(8,128)(2,1)S(1)}, bf16[32,64,128]{2,1,0:T(8,128)(2,1)S(1)}, bf16[32,64,128]{2...) custom-call(s32[2]{0:T(128)S(1)} %pad_add_fusion.where, ...), custom_call_target="tpu_custom_call" | custom-call | flops 1073741824 | bytes 16777216 | tf_op jit(solution)/shard_map/pallas_call | solution.py:153
  7.6 0.5 collective-permute-start
  8.1 5.2 %collective-permute-start.2 = (bf16[32,64,128]{2,1,0:T(8,128)(2,1)S(1)}, bf16[32,64,128]{2,1,0:T(8,128)(2,1)S(1)}, u32[]{:S(2)}, u32[]{:S(2)}) collective-permute-start(bf16[32,64,128]{2,1,0:T(8,128)(2,1)S(1)} %get-tuple-element.36), channel_id=1, source_target_pairs={{0,24},{4,12},{8,0},{12,20},{16,8},{20,28},{24,16},{28,4},{1,25},{... | collective-permute-start | bytes 1572872 | tf_op jit(solution)/shard_map/ppermute | solution.py:361
  13.3 0.2 shard_map.87
  13.6 2.4 %collective-permute-start.1 = (bf16[32,64,128]{2,1,0:T(8,128)(2,1)S(1)}, bf16[32,64,128]{2,1,0:T(8,128)(2,1)S(1)}, u32[]{:S(2)}, u32[]{:S(2)}) collective-permute-start(bf16[32,64,128]{2,1,0:T(8,128)(2,1)S(1)} %shard_map.87), channel_id=1, source_target_pairs={{0,28},{4,8},{8,4},{12,16},{16,12},{20,24},{24,20},{28,0},{1,29},{... | collective-permute-start | bytes 1572872 | tf_op jit(solution)/shard_map/ppermute | solution.py:363
  16.0 1.6 %collective-permute-start.6 = (bf16[18,64,128]{2,1,0:T(8,128)(2,1)S(1)}, bf16[18,64,128]{2,1,0:T(8,128)(2,1)S(1)}, u32[]{:S(2)}, u32[]{:S(2)}) collective-permute-start(bf16[18,64,128]{2,1,0:T(8,128)(2,1)S(1)} %get-tuple-element.46), channel_id=1, source_target_pairs={{0,1},{1,2},{2,3},{3,0},{4,5},{5,6},{6,7},{7,4},{8,9},{9,10},{10,1... | collective-permute-start | bytes 884744 | tf_op jit(solution)/shard_map/ppermute | solution.py:345
  17.5 2.6 %collective-permute-start.7 = (bf16[18,64,128]{2,1,0:T(8,128)(2,1)S(1)}, bf16[18,64,128]{2,1,0:T(8,128)(2,1)S(1)}, u32[]{:S(2)}, u32[]{:S(2)}) collective-permute-start(bf16[18,64,128]{2,1,0:T(8,128)(2,1)S(1)} %get-tuple-element.47), channel_id=1, source_target_pairs={{0,2},{1,3},{2,0},{3,1},{4,6},{5,7},{6,4},{7,5},{8,10},{9,11},{10,... | collective-permute-start | bytes 884744 | tf_op jit(solution)/shard_map/ppermute | solution.py:345
  20.1 1.3 %collective-permute-start.8 = (bf16[18,64,128]{2,1,0:T(8,128)(2,1)S(1)}, bf16[18,64,128]{2,1,0:T(8,128)(2,1)S(1)}, u32[]{:S(2)}, u32[]{:S(2)}) collective-permute-start(bf16[18,64,128]{2,1,0:T(8,128)(2,1)S(1)} %get-tuple-element.48), channel_id=1, source_target_pairs={{0,3},{1,0},{2,1},{3,2},{4,7},{5,4},{6,5},{7,6},{8,11},{9,8},{10,9... | collective-permute-start | bytes 884744 | tf_op jit(solution)/shard_map/ppermute | solution.py:345
  21.5 4.5 %collective-permute-done.2.rest_2_ = bf16[32,64,128]{2,1,0:T(8,128)(2,1)S(1)} collective-permute-done((bf16[32,64,128]{2,1,0:T(8,128)(2,1)S(1)}, bf16[32,64,128]{2,1,0:T(8,128)(2,1)S(1)}, u32[]{:S(2)}, u32[]{:S(2)}) %collective-permute-start.2) | collective-permute-done | bytes 524320 | tf_op jit(solution)/shard_map/ppermute | solution.py:361
  26.0 10.8 %collective-permute-done.1.rest_1_ = bf16[32,64,128]{2,1,0:T(8,128)(2,1)S(1)} collective-permute-done((bf16[32,64,128]{2,1,0:T(8,128)(2,1)S(1)}, bf16[32,64,128]{2,1,0:T(8,128)(2,1)S(1)}, u32[]{:S(2)}, u32[]{:S(2)}) %collective-permute-start.1) | collective-permute-done | bytes 524320 | tf_op jit(solution)/shard_map/ppermute | solution.py:363
  36.8 0.8 %shard_map.88 = (bf16[8,64,128]{2,1,0:T(8,128)(2,1)S(1)}, bf16[8,64,128]{2,1,0:T(8,128)(2,1)S(1)}, bf16[8,64,128]{2,1,0:T(8,128)(2,1)S(1)}, bf16[8,64,128]{2,1,0:T(8,128)(2,1)S(1)}) custom-call(s32[2]{0:T(128)S(1)} %pad_add_fusion.where, bf16[64,64,128]{2,1,0:T(8,128)(2,1)S(1)} %collective-permute-done.other.aside, ...), custom_call_target="tpu_custom_call" | custom-call | flops 1048576 | bytes 2621440 | tf_op jit(solution)/shard_map/pallas_call | solution.py:304
  37.6 1.6 %collective-permute-start.3 = (bf16[8,64,128]{2,1,0:T(8,128)(2,1)S(1)}, bf16[8,64,128]{2,1,0:T(8,128)(2,1)S(1)}, u32[]{:S(2)}, u32[]{:S(2)}) collective-permute-start(bf16[8,64,128]{2,1,0:T(8,128)(2,1)S(1)} %get-tuple-element.38), channel_id=1, source_target_pairs={{0,1},{1,2},{2,3},{3,0},{4,5},{5,6},{6,7},{7,4},{8,9},{9,10},{10,1... | collective-permute-start | bytes 393224 | tf_op jit(solution)/shard_map/ppermute | solution.py:345
  39.3 2.6 %collective-permute-start.4 = (bf16[8,64,128]{2,1,0:T(8,128)(2,1)S(1)}, bf16[8,64,128]{2,1,0:T(8,128)(2,1)S(1)}, u32[]{:S(2)}, u32[]{:S(2)}) collective-permute-start(bf16[8,64,128]{2,1,0:T(8,128)(2,1)S(1)} %get-tuple-element.39), channel_id=1, source_target_pairs={{0,2},{1,3},{2,0},{3,1},{4,6},{5,7},{6,4},{7,5},{8,10},{9,11},{10,... | collective-permute-start | bytes 393224 | tf_op jit(solution)/shard_map/ppermute | solution.py:345
  41.8 1.3 %collective-permute-start.5 = (bf16[8,64,128]{2,1,0:T(8,128)(2,1)S(1)}, bf16[8,64,128]{2,1,0:T(8,128)(2,1)S(1)}, u32[]{:S(2)}, u32[]{:S(2)}) collective-permute-start(bf16[8,64,128]{2,1,0:T(8,128)(2,1)S(1)} %get-tuple-element.40), channel_id=1, source_target_pairs={{0,3},{1,0},{2,1},{3,2},{4,7},{5,4},{6,5},{7,6},{8,11},{9,8},{10,9... | collective-permute-start | bytes 393224 | tf_op jit(solution)/shard_map/ppermute | solution.py:345
  43.2 1.0 %shard_map.91 = (bf16[2,64,128]{2,1,0:T(8,128)(2,1)S(1)}, bf16[2,64,128]{2,1,0:T(8,128)(2,1)S(1)}, bf16[2,64,128]{2,1,0:T(8,128)(2,1)S(1)}, bf16[2,64,128]{2,1,0:T(8,128)(2,1)S(1)}) custom-call(s32[2]{0:T(128)S(1)} %pad_add_fusion.where, bf16[18,64,128]{2,1,0:T(8,128)(2,1)S(1)} %get-tuple-element.53.rest_4_.rest_0_, ...), custom_call_target="tpu_custom_call" | custom-call | flops 134217728 | bytes 1179648 | tf_op jit(solution)/shard_map/pallas_call | solution.py:253
  44.2 10.8 %collective-permute-start.12 = (bf16[2,64,128]{2,1,0:T(8,128)(2,1)S(1)}, bf16[2,64,128]{2,1,0:T(8,128)(2,1)S(1)}, u32[]{:S(2)}, u32[]{:S(2)}) collective-permute-start(bf16[2,64,128]{2,1,0:T(8,128)(2,1)S(1)} %get-tuple-element.58), channel_id=1, source_target_pairs={{0,3},{1,0},{2,1},{3,2},{4,7},{5,4},{6,5},{7,6},{8,11},{9,8},{10,9... | collective-permute-start | bytes 98312 | tf_op jit(solution)/shard_map/ppermute | solution.py:345
  55.0 0.6 collective-permute-start.14
  55.6 1.0 %shard_map.89 = (bf16[8,64,128]{2,1,0:T(8,128)(2,1)S(1)}, bf16[8,64,128]{2,1,0:T(8,128)(2,1)S(1)}, bf16[8,64,128]{2,1,0:T(8,128)(2,1)S(1)}, bf16[8,64,128]{2,1,0:T(8,128)(2,1)S(1)}) custom-call(s32[2]{0:T(128)S(1)} %pad_add_fusion.where, bf16[8,64,128]{2,1,0:T(8,128)(2,1)S(1)} %get-tuple-element.37.rest_0_, ...), custom_call_target="tpu_custom_call" | custom-call | flops 134217728 | bytes 1048576 | tf_op jit(solution)/shard_map/pallas_call | solution.py:216
  56.6 3.0 %collective-permute-start.9 = (bf16[8,64,128]{2,1,0:T(8,128)(2,1)S(1)}, bf16[8,64,128]{2,1,0:T(8,128)(2,1)S(1)}, u32[]{:S(2)}, u32[]{:S(2)}) collective-permute-start(bf16[8,64,128]{2,1,0:T(8,128)(2,1)S(1)} %get-tuple-element.50), channel_id=1, source_target_pairs={{0,1},{1,2},{2,3},{3,0},{4,5},{5,6},{6,7},{7,4},{8,9},{9,10},{10,1... | collective-permute-start | bytes 393224 | tf_op jit(solution)/shard_map/ppermute | solution.py:345
  59.7 0.1 collective-permute-done.13
  59.8 1.3 %collective-permute-done.14 = bf16[2,64,128]{2,1,0:T(8,128)(2,1)S(1)} collective-permute-done((bf16[2,64,128]{2,1,0:T(8,128)(2,1)S(1)}, bf16[2,64,128]{2,1,0:T(8,128)(2,1)S(1)}, u32[]{:S(2)}, u32[]{:S(2)}) %collective-permute-start.14) | collective-permute-done | bytes 32800 | tf_op jit(solution)/shard_map/ppermute | solution.py:345
  61.1 0.1 collective-permute-start.15
  61.2 0.8 %collective-permute-start.10 = (bf16[8,64,128]{2,1,0:T(8,128)(2,1)S(1)}, bf16[8,64,128]{2,1,0:T(8,128)(2,1)S(1)}, u32[]{:S(2)}, u32[]{:S(2)}) collective-permute-start(bf16[8,64,128]{2,1,0:T(8,128)(2,1)S(1)} %get-tuple-element.51), channel_id=1, source_target_pairs={{0,2},{1,3},{2,0},{3,1},{4,6},{5,7},{6,4},{7,5},{8,10},{9,11},{10,... | collective-permute-start | bytes 393224 | tf_op jit(solution)/shard_map/ppermute | solution.py:345
  62.0 0.6 collective-permute-start.11
  62.6 0.8 %collective-permute-start.18 = (f32[2,64,128]{2,1,0:T(8,128)S(1)}, f32[2,64,128]{2,1,0:T(8,128)S(1)}, u32[]{:S(2)}, u32[]{:S(2)}) collective-permute-start(f32[2,64,128]{2,1,0:T(8,128)S(1)} %add.24), channel_id=1, source_target_pairs={{0,24},{4,28},{8,16},{12,20},{16,8},{20,12},{24,0},{28,4},{1,25},{... | collective-permute-start | bytes 196616 | tf_op jit(solution)/shard_map/ppermute | solution.py:378
  63.4 1.4 %collective-permute-start.17 = (f32[2,64,128]{2,1,0:T(8,128)S(1)}, f32[2,64,128]{2,1,0:T(8,128)S(1)}, u32[]{:S(2)}, u32[]{:S(2)}) collective-permute-start(f32[2,64,128]{2,1,0:T(8,128)S(1)} %add.24), channel_id=1, source_target_pairs={{0,16},{4,20},{8,24},{12,28},{16,0},{20,4},{24,8},{28,12},{1,17},{... | collective-permute-start | bytes 196616 | tf_op jit(solution)/shard_map/ppermute | solution.py:378
  64.8 1.4 %collective-permute-start.16 = (f32[2,64,128]{2,1,0:T(8,128)S(1)}, f32[2,64,128]{2,1,0:T(8,128)S(1)}, u32[]{:S(2)}, u32[]{:S(2)}) collective-permute-start(f32[2,64,128]{2,1,0:T(8,128)S(1)} %add.24), channel_id=1, source_target_pairs={{0,8},{4,12},{8,0},{12,4},{16,24},{20,28},{24,16},{28,20},{1,9},{5... | collective-permute-start | bytes 196616 | tf_op jit(solution)/shard_map/ppermute | solution.py:378
  66.2 3.7 %collective-permute-done.10.rest_2_ = bf16[8,64,128]{2,1,0:T(8,128)(2,1)S(1)} collective-permute-done((bf16[8,64,128]{2,1,0:T(8,128)(2,1)S(1)}, bf16[8,64,128]{2,1,0:T(8,128)(2,1)S(1)}, u32[]{:S(2)}, u32[]{:S(2)}) %collective-permute-start.10) | collective-permute-done | bytes 131104 | tf_op jit(solution)/shard_map/ppermute | solution.py:345
  69.9 0.5 collective-permute-done.11.rest_3_
  70.4 1.4 %shard_map.90 = bf16[32,64,128]{2,1,0:T(8,128)(2,1)} custom-call(s32[2]{0:T(128)S(1)} %pad_add_fusion.where, bf16[8,64,128]{2,1,0:T(8,128)(2,1)S(1)} %get-tuple-element.49.rest_0_, bf16[8,64,128]{2,1,0:T(8,128)(2,1)S(1)} %collective-permute-done.9.rest_1_, bf16[8,64,128]{2,1,0:T(8,128)(2,1)S(1)} %collective-permute-done.10.rest_2_, ...), custom_call_target="tpu_custom_call" | custom-call | bytes 33554432 | tf_op jit(solution)/shard_map/pallas_call | solution.py:330
  71.8 0.6 copy_bitcast_fusion
  (16 shorter events, 0.1 us)
Async XLA Ops:
  7.6 5.7 %collective-permute-start = (bf16[64,64,128]{2,1,0:T(8,128)(2,1)S(1)}, bf16[64,64,128]{2,1,0:T(8,128)(2,1)S(1)}, u32[]{:S(2)}, u32[]{:S(2)}) collective-permute-start(bf16[64,64,128]{2,1,0:T(8,128)(2,1)S(1)} %get-tuple-element.33), channel_id=1, source_target_pairs={{0,4},{4,0},{8,12},{12,8},{16,20},{20,16},{24,28},{28,24},{1,5},{5... | collective-permute-start | bytes 3145736 | tf_op jit(solution)/shard_map/ppermute | solution.py:360
  8.1 17.9 %collective-permute-start.2 = (bf16[32,64,128]{2,1,0:T(8,128)(2,1)S(1)}, bf16[32,64,128]{2,1,0:T(8,128)(2,1)S(1)}, u32[]{:S(2)}, u32[]{:S(2)}) collective-permute-start(bf16[32,64,128]{2,1,0:T(8,128)(2,1)S(1)} %get-tuple-element.36), channel_id=1, source_target_pairs={{0,24},{4,12},{8,0},{12,20},{16,8},{20,28},{24,16},{28,4},{1,25},{... | collective-permute-start | bytes 1572872 | tf_op jit(solution)/shard_map/ppermute | solution.py:361
  13.6 23.2 %collective-permute-start.1 = (bf16[32,64,128]{2,1,0:T(8,128)(2,1)S(1)}, bf16[32,64,128]{2,1,0:T(8,128)(2,1)S(1)}, u32[]{:S(2)}, u32[]{:S(2)}) collective-permute-start(bf16[32,64,128]{2,1,0:T(8,128)(2,1)S(1)} %shard_map.87), channel_id=1, source_target_pairs={{0,28},{4,8},{8,4},{12,16},{16,12},{20,24},{24,20},{28,0},{1,29},{... | collective-permute-start | bytes 1572872 | tf_op jit(solution)/shard_map/ppermute | solution.py:363
  16.0 25.9 %collective-permute-start.6 = (bf16[18,64,128]{2,1,0:T(8,128)(2,1)S(1)}, bf16[18,64,128]{2,1,0:T(8,128)(2,1)S(1)}, u32[]{:S(2)}, u32[]{:S(2)}) collective-permute-start(bf16[18,64,128]{2,1,0:T(8,128)(2,1)S(1)} %get-tuple-element.46), channel_id=1, source_target_pairs={{0,1},{1,2},{2,3},{3,0},{4,5},{5,6},{6,7},{7,4},{8,9},{9,10},{10,1... | collective-permute-start | bytes 884744 | tf_op jit(solution)/shard_map/ppermute | solution.py:345
  17.5 25.6 %collective-permute-start.7 = (bf16[18,64,128]{2,1,0:T(8,128)(2,1)S(1)}, bf16[18,64,128]{2,1,0:T(8,128)(2,1)S(1)}, u32[]{:S(2)}, u32[]{:S(2)}) collective-permute-start(bf16[18,64,128]{2,1,0:T(8,128)(2,1)S(1)} %get-tuple-element.47), channel_id=1, source_target_pairs={{0,2},{1,3},{2,0},{3,1},{4,6},{5,7},{6,4},{7,5},{8,10},{9,11},{10,... | collective-permute-start | bytes 884744 | tf_op jit(solution)/shard_map/ppermute | solution.py:345
  20.1 23.1 %collective-permute-start.8 = (bf16[18,64,128]{2,1,0:T(8,128)(2,1)S(1)}, bf16[18,64,128]{2,1,0:T(8,128)(2,1)S(1)}, u32[]{:S(2)}, u32[]{:S(2)}) collective-permute-start(bf16[18,64,128]{2,1,0:T(8,128)(2,1)S(1)} %get-tuple-element.48), channel_id=1, source_target_pairs={{0,3},{1,0},{2,1},{3,2},{4,7},{5,4},{6,5},{7,6},{8,11},{9,8},{10,9... | collective-permute-start | bytes 884744 | tf_op jit(solution)/shard_map/ppermute | solution.py:345
  37.6 17.4 %collective-permute-start.3 = (bf16[8,64,128]{2,1,0:T(8,128)(2,1)S(1)}, bf16[8,64,128]{2,1,0:T(8,128)(2,1)S(1)}, u32[]{:S(2)}, u32[]{:S(2)}) collective-permute-start(bf16[8,64,128]{2,1,0:T(8,128)(2,1)S(1)} %get-tuple-element.38), channel_id=1, source_target_pairs={{0,1},{1,2},{2,3},{3,0},{4,5},{5,6},{6,7},{7,4},{8,9},{9,10},{10,1... | collective-permute-start | bytes 393224 | tf_op jit(solution)/shard_map/ppermute | solution.py:345
  39.3 16.4 %collective-permute-start.4 = (bf16[8,64,128]{2,1,0:T(8,128)(2,1)S(1)}, bf16[8,64,128]{2,1,0:T(8,128)(2,1)S(1)}, u32[]{:S(2)}, u32[]{:S(2)}) collective-permute-start(bf16[8,64,128]{2,1,0:T(8,128)(2,1)S(1)} %get-tuple-element.39), channel_id=1, source_target_pairs={{0,2},{1,3},{2,0},{3,1},{4,6},{5,7},{6,4},{7,5},{8,10},{9,11},{10,... | collective-permute-start | bytes 393224 | tf_op jit(solution)/shard_map/ppermute | solution.py:345
  41.8 13.8 %collective-permute-start.5 = (bf16[8,64,128]{2,1,0:T(8,128)(2,1)S(1)}, bf16[8,64,128]{2,1,0:T(8,128)(2,1)S(1)}, u32[]{:S(2)}, u32[]{:S(2)}) collective-permute-start(bf16[8,64,128]{2,1,0:T(8,128)(2,1)S(1)} %get-tuple-element.40), channel_id=1, source_target_pairs={{0,3},{1,0},{2,1},{3,2},{4,7},{5,4},{6,5},{7,6},{8,11},{9,8},{10,9... | collective-permute-start | bytes 393224 | tf_op jit(solution)/shard_map/ppermute | solution.py:345
  44.2 15.5 %collective-permute-start.12 = (bf16[2,64,128]{2,1,0:T(8,128)(2,1)S(1)}, bf16[2,64,128]{2,1,0:T(8,128)(2,1)S(1)}, u32[]{:S(2)}, u32[]{:S(2)}) collective-permute-start(bf16[2,64,128]{2,1,0:T(8,128)(2,1)S(1)} %get-tuple-element.58), channel_id=1, source_target_pairs={{0,3},{1,0},{2,1},{3,2},{4,7},{5,4},{6,5},{7,6},{8,11},{9,8},{10,9... | collective-permute-start | bytes 98312 | tf_op jit(solution)/shard_map/ppermute | solution.py:345
  55.0 4.8 %collective-permute-start.13 = (bf16[2,64,128]{2,1,0:T(8,128)(2,1)S(1)}, bf16[2,64,128]{2,1,0:T(8,128)(2,1)S(1)}, u32[]{:S(2)}, u32[]{:S(2)}) collective-permute-start(bf16[2,64,128]{2,1,0:T(8,128)(2,1)S(1)} %get-tuple-element.59), channel_id=1, source_target_pairs={{0,2},{1,3},{2,0},{3,1},{4,6},{5,7},{6,4},{7,5},{8,10},{9,11},{10,... | collective-permute-start | bytes 98312 | tf_op jit(solution)/shard_map/ppermute | solution.py:345
  55.0 6.1 %collective-permute-start.14 = (bf16[2,64,128]{2,1,0:T(8,128)(2,1)S(1)}, bf16[2,64,128]{2,1,0:T(8,128)(2,1)S(1)}, u32[]{:S(2)}, u32[]{:S(2)}) collective-permute-start(bf16[2,64,128]{2,1,0:T(8,128)(2,1)S(1)} %get-tuple-element.60), channel_id=1, source_target_pairs={{0,1},{1,2},{2,3},{3,0},{4,5},{5,6},{6,7},{7,4},{8,9},{9,10},{10,1... | collective-permute-start | bytes 98312 | tf_op jit(solution)/shard_map/ppermute | solution.py:345
  56.6 8.1 %collective-permute-start.9 = (bf16[8,64,128]{2,1,0:T(8,128)(2,1)S(1)}, bf16[8,64,128]{2,1,0:T(8,128)(2,1)S(1)}, u32[]{:S(2)}, u32[]{:S(2)}) collective-permute-start(bf16[8,64,128]{2,1,0:T(8,128)(2,1)S(1)} %get-tuple-element.50), channel_id=1, source_target_pairs={{0,1},{1,2},{2,3},{3,0},{4,5},{5,6},{6,7},{7,4},{8,9},{9,10},{10,1... | collective-permute-start | bytes 393224 | tf_op jit(solution)/shard_map/ppermute | solution.py:345
  61.1 1.5 %collective-permute-start.15 = (f32[2,64,128]{2,1,0:T(8,128)S(1)}, f32[2,64,128]{2,1,0:T(8,128)S(1)}, u32[]{:S(2)}, u32[]{:S(2)}) collective-permute-start(f32[2,64,128]{2,1,0:T(8,128)S(1)} %convert_add_fusion), channel_id=1, source_target_pairs={{0,4},{4,0},{8,12},{12,8},{16,20},{20,16},{24,28},{28,24},{1,5},{5... | collective-permute-start | bytes 196616 | tf_op jit(solution)/shard_map/ppermute | solution.py:376
  61.2 8.7 %collective-permute-start.10 = (bf16[8,64,128]{2,1,0:T(8,128)(2,1)S(1)}, bf16[8,64,128]{2,1,0:T(8,128)(2,1)S(1)}, u32[]{:S(2)}, u32[]{:S(2)}) collective-permute-start(bf16[8,64,128]{2,1,0:T(8,128)(2,1)S(1)} %get-tuple-element.51), channel_id=1, source_target_pairs={{0,2},{1,3},{2,0},{3,1},{4,6},{5,7},{6,4},{7,5},{8,10},{9,11},{10,... | collective-permute-start | bytes 393224 | tf_op jit(solution)/shard_map/ppermute | solution.py:345
  62.0 8.4 %collective-permute-start.11 = (bf16[8,64,128]{2,1,0:T(8,128)(2,1)S(1)}, bf16[8,64,128]{2,1,0:T(8,128)(2,1)S(1)}, u32[]{:S(2)}, u32[]{:S(2)}) collective-permute-start(bf16[8,64,128]{2,1,0:T(8,128)(2,1)S(1)} %get-tuple-element.52), channel_id=1, source_target_pairs={{0,3},{1,0},{2,1},{3,2},{4,7},{5,4},{6,5},{7,6},{8,11},{9,8},{10,9... | collective-permute-start | bytes 393224 | tf_op jit(solution)/shard_map/ppermute | solution.py:345
  62.6 9.1 %collective-permute-start.18 = (f32[2,64,128]{2,1,0:T(8,128)S(1)}, f32[2,64,128]{2,1,0:T(8,128)S(1)}, u32[]{:S(2)}, u32[]{:S(2)}) collective-permute-start(f32[2,64,128]{2,1,0:T(8,128)S(1)} %add.24), channel_id=1, source_target_pairs={{0,24},{4,28},{8,16},{12,20},{16,8},{20,12},{24,0},{28,4},{1,25},{... | collective-permute-start | bytes 196616 | tf_op jit(solution)/shard_map/ppermute | solution.py:378
  63.4 8.4 %collective-permute-start.17 = (f32[2,64,128]{2,1,0:T(8,128)S(1)}, f32[2,64,128]{2,1,0:T(8,128)S(1)}, u32[]{:S(2)}, u32[]{:S(2)}) collective-permute-start(f32[2,64,128]{2,1,0:T(8,128)S(1)} %add.24), channel_id=1, source_target_pairs={{0,16},{4,20},{8,24},{12,28},{16,0},{20,4},{24,8},{28,12},{1,17},{... | collective-permute-start | bytes 196616 | tf_op jit(solution)/shard_map/ppermute | solution.py:378
  64.8 7.0 %collective-permute-start.16 = (f32[2,64,128]{2,1,0:T(8,128)S(1)}, f32[2,64,128]{2,1,0:T(8,128)S(1)}, u32[]{:S(2)}, u32[]{:S(2)}) collective-permute-start(f32[2,64,128]{2,1,0:T(8,128)S(1)} %add.24), channel_id=1, source_target_pairs={{0,8},{4,12},{8,0},{12,4},{16,24},{20,28},{24,16},{28,20},{1,9},{5... | collective-permute-start | bytes 196616 | tf_op jit(solution)/shard_map/ppermute | solution.py:378

commit v15 on v14

--- a/solution.py
+++ b/solution.py
@@ -362,11 +362,11 @@
     one = add(one, aside)
     one_in = lax.ppermute(one, "blk", to_one)
 
-    packed, _ = lax.optimization_barrier((packed, one))
     packed = [shift(value, s) for s, value in enumerate(packed)]
+    pieces = weight_partial(where, packed, blocks // reps)
+    own, pieces = lax.optimization_barrier((own, pieces))
     shares = total_shares(where, aside, [own, one_in, two_in], reps)
-    held, _ = lax.optimization_barrier((packed, shares))
-    pieces = weight_partial(where, held, blocks // reps)
+    pieces, _ = lax.optimization_barrier((pieces, shares))
     pieces = [shift(value, -s) for s, value in enumerate(pieces)]
     shares = [shift(value, s) for s, value in enumerate(shares)]
     outs = [shift(value, s) for s, value in enumerate(mix(where, shares, packed))]

time: 72.9 us -> 76.8 us (1.053)
  waiting for transfers between devices: 20.9 us -> 24.6 us
  starting transfers between devices: 38.7 us -> 37 us
  Pallas kernels: 11.3 us -> 12.6 us
    ppermute x12, waiting for transfers between devices: 5.57 us -> 24.6 us  [shift(): lax.ppermute(value, 'rep', [(i, (i + steps) % reps) for i in range(reps)])]
    ppermute x1, waiting for transfers between devices: 10.8 us -> 0.01 us  [on_device(): one_in = lax.ppermute(one, 'blk', to_one)]
    ppermute x1, waiting for transfers between devices: 4.52 us -> 0.01 us  [on_device(): two_in = lax.ppermute(two, 'blk', to_two)]
    ppermute x1, starting transfers between devices: 5.23 us -> 3.28 us  [on_device(): two_in = lax.ppermute(two, 'blk', to_two)]
    ppermute x12, starting transfers between devices: 27 us -> 25.6 us  [shift(): lax.ppermute(value, 'rep', [(i, (i + steps) % reps) for i in range(reps)])]
    pallas_call x1, Pallas kernels: 6.85 us -> 8.15 us  [contributions(): pl.pallas_call(functools.partial(tiles_kernel, slabs, reps), out_shape=[j...]
    ppermute x3, starting transfers between devices: 3.55 us -> 4.72 us  [on_device(): lax.ppermute(grad_w, 'blk', [(i, i ^ step) for i in range(slabs)])]
  transfers between devices with their start and end apart: 19 -> 19, of which waited for: 6 -> 7; matrix products, arithmetic and copies ran while one was open for 0% -> 0% of each run, Pallas kernels for 6% -> 5%
where the time goes in v15:
time: 76.8 us; the launch traced here: 75.6 us
  starting transfers between devices  37 us (48%)
  waiting for transfers between devices  24.6 us (32%)
  Pallas kernels  12.6 us (16%)
    ppermute x12, starting transfers between devices, shift(): lax.ppermute(value, 'rep', [(i, (i + steps) % reps) for i in range(reps)])  25.6 us
    ppermute x12, waiting for transfers between devices, shift(): lax.ppermute(value, 'rep', [(i, (i + steps) % reps) for i in range(reps)])  24.6 us
    pallas_call x1, Pallas kernels, contributions(): pl.pallas_call(functools.partial(tiles_kernel, slabs, reps), out_shape=[j...  8.15 us
    ppermute x3, starting transfers between devices, on_device(): lax.ppermute(grad_w, 'blk', [(i, i ^ step) for i in range(slabs)])  4.72 us
    ppermute x1, starting transfers between devices, on_device(): two_in = lax.ppermute(two, 'blk', to_two)  3.28 us
    ppermute x1, starting transfers between devices, on_device(): one_in = lax.ppermute(one, 'blk', to_one)  2.33 us
  transfers between devices with their start and end apart: 19, of which 7 were waited for; matrix products, arithmetic and copies ran while one was open for 0% of the time, Pallas kernels for 5%

profile of v15, /device:TPU:0, one launch (start us, length us, event | category | flops | bytes accessed | tf_op | source)
XLA Modules:
  0.0 75.6 jit_solution(11227939522089342515)
XLA Ops:
  0.6 0.1 pad_add_fusion.where
  0.7 8.1 %shard_map.86 = (bf16[64,64,128]{2,1,0:T(8,128)(2,1)S(1)}, bf16[32,64,128]{2,1,0:T(8,128)(2,1)S(1)}, bf16[32,64,128]{2,1,0:T(8,128)(2,1)S(1)}, bf16[32,64,128]{2...) custom-call(s32[2]{0:T(128)S(1)} %pad_add_fusion.where, ...), custom_call_target="tpu_custom_call" | custom-call | flops 1073741824 | bytes 16777216 | tf_op jit(solution)/shard_map/pallas_call | solution.py:153
  8.9 0.9 %collective-permute-start = (bf16[64,64,128]{2,1,0:T(8,128)(2,1)S(1)}, bf16[64,64,128]{2,1,0:T(8,128)(2,1)S(1)}, u32[]{:S(2)}, u32[]{:S(2)}) collective-permute-start(bf16[64,64,128]{2,1,0:T(8,128)(2,1)S(1)} %get-tuple-element.34), channel_id=1, source_target_pairs={{0,4},{4,0},{8,12},{12,8},{16,20},{20,16},{24,28},{28,24},{1,5},{5... | collective-permute-start | bytes 3145736 | tf_op jit(solution)/shard_map/ppermute | solution.py:360
  9.8 3.3 %collective-permute-start.5 = (bf16[32,64,128]{2,1,0:T(8,128)(2,1)S(1)}, bf16[32,64,128]{2,1,0:T(8,128)(2,1)S(1)}, u32[]{:S(2)}, u32[]{:S(2)}) collective-permute-start(bf16[32,64,128]{2,1,0:T(8,128)(2,1)S(1)} %get-tuple-element.46), channel_id=1, source_target_pairs={{0,24},{4,12},{8,0},{12,20},{16,8},{20,28},{24,16},{28,4},{1,25},{... | collective-permute-start | bytes 1572872 | tf_op jit(solution)/shard_map/ppermute | solution.py:361
  13.1 0.2 shard_map.88
  13.4 2.3 %collective-permute-start.4 = (bf16[32,64,128]{2,1,0:T(8,128)(2,1)S(1)}, bf16[32,64,128]{2,1,0:T(8,128)(2,1)S(1)}, u32[]{:S(2)}, u32[]{:S(2)}) collective-permute-start(bf16[32,64,128]{2,1,0:T(8,128)(2,1)S(1)} %shard_map.88), channel_id=1, source_target_pairs={{0,28},{4,8},{8,4},{12,16},{16,12},{20,24},{24,20},{28,0},{1,29},{... | collective-permute-start | bytes 1572872 | tf_op jit(solution)/shard_map/ppermute | solution.py:363
  15.7 1.6 %collective-permute-start.1 = (bf16[18,64,128]{2,1,0:T(8,128)(2,1)S(1)}, bf16[18,64,128]{2,1,0:T(8,128)(2,1)S(1)}, u32[]{:S(2)}, u32[]{:S(2)}) collective-permute-start(bf16[18,64,128]{2,1,0:T(8,128)(2,1)S(1)} %get-tuple-element.37), channel_id=1, source_target_pairs={{0,1},{1,2},{2,3},{3,0},{4,5},{5,6},{6,7},{7,4},{8,9},{9,10},{10,1... | collective-permute-start | bytes 884744 | tf_op jit(solution)/shard_map/ppermute | solution.py:345
  17.3 2.6 %collective-permute-start.2 = (bf16[18,64,128]{2,1,0:T(8,128)(2,1)S(1)}, bf16[18,64,128]{2,1,0:T(8,128)(2,1)S(1)}, u32[]{:S(2)}, u32[]{:S(2)}) collective-permute-start(bf16[18,64,128]{2,1,0:T(8,128)(2,1)S(1)} %get-tuple-element.38), channel_id=1, source_target_pairs={{0,2},{1,3},{2,0},{3,1},{4,6},{5,7},{6,4},{7,5},{8,10},{9,11},{10,... | collective-permute-start | bytes 884744 | tf_op jit(solution)/shard_map/ppermute | solution.py:345
  19.8 1.3 %collective-permute-start.3 = (bf16[18,64,128]{2,1,0:T(8,128)(2,1)S(1)}, bf16[18,64,128]{2,1,0:T(8,128)(2,1)S(1)}, u32[]{:S(2)}, u32[]{:S(2)}) collective-permute-start(bf16[18,64,128]{2,1,0:T(8,128)(2,1)S(1)} %get-tuple-element.39), channel_id=1, source_target_pairs={{0,3},{1,0},{2,1},{3,2},{4,7},{5,4},{6,5},{7,6},{8,11},{9,8},{10,9... | collective-permute-start | bytes 884744 | tf_op jit(solution)/shard_map/ppermute | solution.py:345
  21.2 6.3 %collective-permute-done.1.rest_1_.rest_5_ = bf16[18,64,128]{2,1,0:T(8,128)(2,1)S(1)} collective-permute-done((bf16[18,64,128]{2,1,0:T(8,128)(2,1)S(1)}, bf16[18,64,128]{2,1,0:T(8,128)(2,1)S(1)}, u32[]{:S(2)}, u32[]{:S(2)}) %collective-permute-start.1) | collective-permute-done | bytes 294944 | tf_op jit(solution)/shard_map/ppermute | solution.py:345
  27.5 10.4 %collective-permute-done.2.rest_2_.rest_6_ = bf16[18,64,128]{2,1,0:T(8,128)(2,1)S(1)} collective-permute-done((bf16[18,64,128]{2,1,0:T(8,128)(2,1)S(1)}, bf16[18,64,128]{2,1,0:T(8,128)(2,1)S(1)}, u32[]{:S(2)}, u32[]{:S(2)}) %collective-permute-start.2) | collective-permute-done | bytes 294944 | tf_op jit(solution)/shard_map/ppermute | solution.py:345
  38.0 1.0 %shard_map.87 = (bf16[2,64,128]{2,1,0:T(8,128)(2,1)S(1)}, bf16[2,64,128]{2,1,0:T(8,128)(2,1)S(1)}, bf16[2,64,128]{2,1,0:T(8,128)(2,1)S(1)}, bf16[2,64,128]{2,1,0:T(8,128)(2,1)S(1)}) custom-call(s32[2]{0:T(128)S(1)} %pad_add_fusion.where, bf16[18,64,128]{2,1,0:T(8,128)(2,1)S(1)} %get-tuple-element.36.rest_0_.rest_4_, ...), custom_call_target="tpu_custom_call" | custom-call | flops 134217728 | bytes 1179648 | tf_op jit(solution)/shard_map/pallas_call | solution.py:253
  39.0 0.8 %shard_map.89 = (bf16[8,64,128]{2,1,0:T(8,128)(2,1)S(1)}, bf16[8,64,128]{2,1,0:T(8,128)(2,1)S(1)}, bf16[8,64,128]{2,1,0:T(8,128)(2,1)S(1)}, bf16[8,64,128]{2,1,0:T(8,128)(2,1)S(1)}) custom-call(s32[2]{0:T(128)S(1)} %pad_add_fusion.where, bf16[64,64,128]{2,1,0:T(8,128)(2,1)S(1)} %collective-permute-done.other.aside, ...), custom_call_target="tpu_custom_call" | custom-call | flops 1048576 | bytes 2621440 | tf_op jit(solution)/shard_map/pallas_call | solution.py:304
  39.8 6.8 %collective-permute-start.6 = (bf16[8,64,128]{2,1,0:T(8,128)(2,1)S(1)}, bf16[8,64,128]{2,1,0:T(8,128)(2,1)S(1)}, u32[]{:S(2)}, u32[]{:S(2)}) collective-permute-start(bf16[8,64,128]{2,1,0:T(8,128)(2,1)S(1)} %get-tuple-element.48), channel_id=1, source_target_pairs={{0,1},{1,2},{2,3},{3,0},{4,5},{5,6},{6,7},{7,4},{8,9},{9,10},{10,1... | collective-permute-start | bytes 393224 | tf_op jit(solution)/shard_map/ppermute | solution.py:345
  46.7 1.6 %collective-permute-start.7 = (bf16[8,64,128]{2,1,0:T(8,128)(2,1)S(1)}, bf16[8,64,128]{2,1,0:T(8,128)(2,1)S(1)}, u32[]{:S(2)}, u32[]{:S(2)}) collective-permute-start(bf16[8,64,128]{2,1,0:T(8,128)(2,1)S(1)} %get-tuple-element.49), channel_id=1, source_target_pairs={{0,2},{1,3},{2,0},{3,1},{4,6},{5,7},{6,4},{7,5},{8,10},{9,11},{10,... | collective-permute-start | bytes 393224 | tf_op jit(solution)/shard_map/ppermute | solution.py:345
  48.3 0.8 %collective-permute-start.8 = (bf16[8,64,128]{2,1,0:T(8,128)(2,1)S(1)}, bf16[8,64,128]{2,1,0:T(8,128)(2,1)S(1)}, u32[]{:S(2)}, u32[]{:S(2)}) collective-permute-start(bf16[8,64,128]{2,1,0:T(8,128)(2,1)S(1)} %get-tuple-element.50), channel_id=1, source_target_pairs={{0,3},{1,0},{2,1},{3,2},{4,7},{5,4},{6,5},{7,6},{8,11},{9,8},{10,9... | collective-permute-start | bytes 393224 | tf_op jit(solution)/shard_map/ppermute | solution.py:345
  49.1 1.2 %collective-permute-start.14 = (bf16[2,64,128]{2,1,0:T(8,128)(2,1)S(1)}, bf16[2,64,128]{2,1,0:T(8,128)(2,1)S(1)}, u32[]{:S(2)}, u32[]{:S(2)}) collective-permute-start(bf16[2,64,128]{2,1,0:T(8,128)(2,1)S(1)} %get-tuple-element.62), channel_id=1, source_target_pairs={{0,1},{1,2},{2,3},{3,0},{4,5},{5,6},{6,7},{7,4},{8,9},{9,10},{10,1... | collective-permute-start | bytes 98312 | tf_op jit(solution)/shard_map/ppermute | solution.py:345
  50.3 1.3 %collective-permute-start.13 = (bf16[2,64,128]{2,1,0:T(8,128)(2,1)S(1)}, bf16[2,64,128]{2,1,0:T(8,128)(2,1)S(1)}, u32[]{:S(2)}, u32[]{:S(2)}) collective-permute-start(bf16[2,64,128]{2,1,0:T(8,128)(2,1)S(1)} %get-tuple-element.61), channel_id=1, source_target_pairs={{0,2},{1,3},{2,0},{3,1},{4,6},{5,7},{6,4},{7,5},{8,10},{9,11},{10,... | collective-permute-start | bytes 98312 | tf_op jit(solution)/shard_map/ppermute | solution.py:345
  51.6 0.2 collective-permute-done.6.rest_1_
  51.8 1.6 %collective-permute-start.12 = (bf16[2,64,128]{2,1,0:T(8,128)(2,1)S(1)}, bf16[2,64,128]{2,1,0:T(8,128)(2,1)S(1)}, u32[]{:S(2)}, u32[]{:S(2)}) collective-permute-start(bf16[2,64,128]{2,1,0:T(8,128)(2,1)S(1)} %get-tuple-element.60), channel_id=1, source_target_pairs={{0,3},{1,0},{2,1},{3,2},{4,7},{5,4},{6,5},{7,6},{8,11},{9,8},{10,9... | collective-permute-start | bytes 98312 | tf_op jit(solution)/shard_map/ppermute | solution.py:345
  53.3 3.8 %collective-permute-done.7.rest_2_ = bf16[8,64,128]{2,1,0:T(8,128)(2,1)S(1)} collective-permute-done((bf16[8,64,128]{2,1,0:T(8,128)(2,1)S(1)}, bf16[8,64,128]{2,1,0:T(8,128)(2,1)S(1)}, u32[]{:S(2)}, u32[]{:S(2)}) %collective-permute-start.7) | collective-permute-done | bytes 131104 | tf_op jit(solution)/shard_map/ppermute | solution.py:345
  57.1 1.0 %shard_map.90 = (bf16[8,64,128]{2,1,0:T(8,128)(2,1)S(1)}, bf16[8,64,128]{2,1,0:T(8,128)(2,1)S(1)}, bf16[8,64,128]{2,1,0:T(8,128)(2,1)S(1)}, bf16[8,64,128]{2,1,0:T(8,128)(2,1)S(1)}) custom-call(s32[2]{0:T(128)S(1)} %pad_add_fusion.where, bf16[8,64,128]{2,1,0:T(8,128)(2,1)S(1)} %get-tuple-element.47.rest_0_, ...), custom_call_target="tpu_custom_call" | custom-call | flops 134217728 | bytes 1048576 | tf_op jit(solution)/shard_map/pallas_call | solution.py:216
  58.1 4.1 %collective-permute-start.9 = (bf16[8,64,128]{2,1,0:T(8,128)(2,1)S(1)}, bf16[8,64,128]{2,1,0:T(8,128)(2,1)S(1)}, u32[]{:S(2)}, u32[]{:S(2)}) collective-permute-start(bf16[8,64,128]{2,1,0:T(8,128)(2,1)S(1)} %get-tuple-element.52), channel_id=1, source_target_pairs={{0,1},{1,2},{2,3},{3,0},{4,5},{5,6},{6,7},{7,4},{8,9},{9,10},{10,1... | collective-permute-start | bytes 393224 | tf_op jit(solution)/shard_map/ppermute | solution.py:345
  62.4 2.6 %collective-permute-start.10 = (bf16[8,64,128]{2,1,0:T(8,128)(2,1)S(1)}, bf16[8,64,128]{2,1,0:T(8,128)(2,1)S(1)}, u32[]{:S(2)}, u32[]{:S(2)}) collective-permute-start(bf16[8,64,128]{2,1,0:T(8,128)(2,1)S(1)} %get-tuple-element.53), channel_id=1, source_target_pairs={{0,2},{1,3},{2,0},{3,1},{4,6},{5,7},{6,4},{7,5},{8,10},{9,11},{10,... | collective-permute-start | bytes 393224 | tf_op jit(solution)/shard_map/ppermute | solution.py:345
  65.0 2.2 %collective-permute-start.16 = (f32[2,64,128]{2,1,0:T(8,128)S(1)}, f32[2,64,128]{2,1,0:T(8,128)S(1)}, u32[]{:S(2)}, u32[]{:S(2)}) collective-permute-start(f32[2,64,128]{2,1,0:T(8,128)S(1)} %add.24), channel_id=1, source_target_pairs={{0,8},{4,12},{8,0},{12,4},{16,24},{20,28},{24,16},{28,20},{1,9},{5... | collective-permute-start | bytes 196616 | tf_op jit(solution)/shard_map/ppermute | solution.py:378
  67.2 0.5 collective-permute-start.17
  67.7 0.7 collective-permute-done.9.rest_1_
  68.4 2.1 %collective-permute-start.18 = (f32[2,64,128]{2,1,0:T(8,128)S(1)}, f32[2,64,128]{2,1,0:T(8,128)S(1)}, u32[]{:S(2)}, u32[]{:S(2)}) collective-permute-start(f32[2,64,128]{2,1,0:T(8,128)S(1)} %add.24), channel_id=1, source_target_pairs={{0,24},{4,28},{8,16},{12,20},{16,8},{20,12},{24,0},{28,4},{1,25},{... | collective-permute-start | bytes 196616 | tf_op jit(solution)/shard_map/ppermute | solution.py:378
  70.5 2.4 %collective-permute-done.10.rest_2_ = bf16[8,64,128]{2,1,0:T(8,128)(2,1)S(1)} collective-permute-done((bf16[8,64,128]{2,1,0:T(8,128)(2,1)S(1)}, bf16[8,64,128]{2,1,0:T(8,128)(2,1)S(1)}, u32[]{:S(2)}, u32[]{:S(2)}) %collective-permute-start.10) | collective-permute-done | bytes 131104 | tf_op jit(solution)/shard_map/ppermute | solution.py:345
  72.9 0.7 collective-permute-done.11.rest_3_
  73.6 1.4 %shard_map.91 = bf16[32,64,128]{2,1,0:T(8,128)(2,1)} custom-call(s32[2]{0:T(128)S(1)} %pad_add_fusion.where, bf16[8,64,128]{2,1,0:T(8,128)(2,1)S(1)} %get-tuple-element.51.rest_0_, bf16[8,64,128]{2,1,0:T(8,128)(2,1)S(1)} %collective-permute-done.9.rest_1_, bf16[8,64,128]{2,1,0:T(8,128)(2,1)S(1)} %collective-permute-done.10.rest_2_, ...), custom_call_target="tpu_custom_call" | custom-call | bytes 33554432 | tf_op jit(solution)/shard_map/pallas_call | solution.py:330
  75.0 0.6 copy_bitcast_fusion
  (16 shorter events, 0.2 us)
Async XLA Ops:
  8.9 4.2 %collective-permute-start = (bf16[64,64,128]{2,1,0:T(8,128)(2,1)S(1)}, bf16[64,64,128]{2,1,0:T(8,128)(2,1)S(1)}, u32[]{:S(2)}, u32[]{:S(2)}) collective-permute-start(bf16[64,64,128]{2,1,0:T(8,128)(2,1)S(1)} %get-tuple-element.34), channel_id=1, source_target_pairs={{0,4},{4,0},{8,12},{12,8},{16,20},{20,16},{24,28},{28,24},{1,5},{5... | collective-permute-start | bytes 3145736 | tf_op jit(solution)/shard_map/ppermute | solution.py:360
  9.8 29.2 %collective-permute-start.5 = (bf16[32,64,128]{2,1,0:T(8,128)(2,1)S(1)}, bf16[32,64,128]{2,1,0:T(8,128)(2,1)S(1)}, u32[]{:S(2)}, u32[]{:S(2)}) collective-permute-start(bf16[32,64,128]{2,1,0:T(8,128)(2,1)S(1)} %get-tuple-element.46), channel_id=1, source_target_pairs={{0,24},{4,12},{8,0},{12,20},{16,8},{20,28},{24,16},{28,4},{1,25},{... | collective-permute-start | bytes 1572872 | tf_op jit(solution)/shard_map/ppermute | solution.py:361
  13.4 25.7 %collective-permute-start.4 = (bf16[32,64,128]{2,1,0:T(8,128)(2,1)S(1)}, bf16[32,64,128]{2,1,0:T(8,128)(2,1)S(1)}, u32[]{:S(2)}, u32[]{:S(2)}) collective-permute-start(bf16[32,64,128]{2,1,0:T(8,128)(2,1)S(1)} %shard_map.88), channel_id=1, source_target_pairs={{0,28},{4,8},{8,4},{12,16},{16,12},{20,24},{24,20},{28,0},{1,29},{... | collective-permute-start | bytes 1572872 | tf_op jit(solution)/shard_map/ppermute | solution.py:363
  15.7 11.9 %collective-permute-start.1 = (bf16[18,64,128]{2,1,0:T(8,128)(2,1)S(1)}, bf16[18,64,128]{2,1,0:T(8,128)(2,1)S(1)}, u32[]{:S(2)}, u32[]{:S(2)}) collective-permute-start(bf16[18,64,128]{2,1,0:T(8,128)(2,1)S(1)} %get-tuple-element.37), channel_id=1, source_target_pairs={{0,1},{1,2},{2,3},{3,0},{4,5},{5,6},{6,7},{7,4},{8,9},{9,10},{10,1... | collective-permute-start | bytes 884744 | tf_op jit(solution)/shard_map/ppermute | solution.py:345
  17.3 20.7 %collective-permute-start.2 = (bf16[18,64,128]{2,1,0:T(8,128)(2,1)S(1)}, bf16[18,64,128]{2,1,0:T(8,128)(2,1)S(1)}, u32[]{:S(2)}, u32[]{:S(2)}) collective-permute-start(bf16[18,64,128]{2,1,0:T(8,128)(2,1)S(1)} %get-tuple-element.38), channel_id=1, source_target_pairs={{0,2},{1,3},{2,0},{3,1},{4,6},{5,7},{6,4},{7,5},{8,10},{9,11},{10,... | collective-permute-start | bytes 884744 | tf_op jit(solution)/shard_map/ppermute | solution.py:345
  19.8 18.1 %collective-permute-start.3 = (bf16[18,64,128]{2,1,0:T(8,128)(2,1)S(1)}, bf16[18,64,128]{2,1,0:T(8,128)(2,1)S(1)}, u32[]{:S(2)}, u32[]{:S(2)}) collective-permute-start(bf16[18,64,128]{2,1,0:T(8,128)(2,1)S(1)} %get-tuple-element.39), channel_id=1, source_target_pairs={{0,3},{1,0},{2,1},{3,2},{4,7},{5,4},{6,5},{7,6},{8,11},{9,8},{10,9... | collective-permute-start | bytes 884744 | tf_op jit(solution)/shard_map/ppermute | solution.py:345
  39.8 12.0 %collective-permute-start.6 = (bf16[8,64,128]{2,1,0:T(8,128)(2,1)S(1)}, bf16[8,64,128]{2,1,0:T(8,128)(2,1)S(1)}, u32[]{:S(2)}, u32[]{:S(2)}) collective-permute-start(bf16[8,64,128]{2,1,0:T(8,128)(2,1)S(1)} %get-tuple-element.48), channel_id=1, source_target_pairs={{0,1},{1,2},{2,3},{3,0},{4,5},{5,6},{6,7},{7,4},{8,9},{9,10},{10,1... | collective-permute-start | bytes 393224 | tf_op jit(solution)/shard_map/ppermute | solution.py:345
  46.7 10.4 %collective-permute-start.7 = (bf16[8,64,128]{2,1,0:T(8,128)(2,1)S(1)}, bf16[8,64,128]{2,1,0:T(8,128)(2,1)S(1)}, u32[]{:S(2)}, u32[]{:S(2)}) collective-permute-start(bf16[8,64,128]{2,1,0:T(8,128)(2,1)S(1)} %get-tuple-element.49), channel_id=1, source_target_pairs={{0,2},{1,3},{2,0},{3,1},{4,6},{5,7},{6,4},{7,5},{8,10},{9,11},{10,... | collective-permute-start | bytes 393224 | tf_op jit(solution)/shard_map/ppermute | solution.py:345
  48.3 8.8 %collective-permute-start.8 = (bf16[8,64,128]{2,1,0:T(8,128)(2,1)S(1)}, bf16[8,64,128]{2,1,0:T(8,128)(2,1)S(1)}, u32[]{:S(2)}, u32[]{:S(2)}) collective-permute-start(bf16[8,64,128]{2,1,0:T(8,128)(2,1)S(1)} %get-tuple-element.50), channel_id=1, source_target_pairs={{0,3},{1,0},{2,1},{3,2},{4,7},{5,4},{6,5},{7,6},{8,11},{9,8},{10,9... | collective-permute-start | bytes 393224 | tf_op jit(solution)/shard_map/ppermute | solution.py:345
  49.1 13.1 %collective-permute-start.14 = (bf16[2,64,128]{2,1,0:T(8,128)(2,1)S(1)}, bf16[2,64,128]{2,1,0:T(8,128)(2,1)S(1)}, u32[]{:S(2)}, u32[]{:S(2)}) collective-permute-start(bf16[2,64,128]{2,1,0:T(8,128)(2,1)S(1)} %get-tuple-element.62), channel_id=1, source_target_pairs={{0,1},{1,2},{2,3},{3,0},{4,5},{5,6},{6,7},{7,4},{8,9},{9,10},{10,1... | collective-permute-start | bytes 98312 | tf_op jit(solution)/shard_map/ppermute | solution.py:345
  50.3 12.0 %collective-permute-start.13 = (bf16[2,64,128]{2,1,0:T(8,128)(2,1)S(1)}, bf16[2,64,128]{2,1,0:T(8,128)(2,1)S(1)}, u32[]{:S(2)}, u32[]{:S(2)}) collective-permute-start(bf16[2,64,128]{2,1,0:T(8,128)(2,1)S(1)} %get-tuple-element.61), channel_id=1, source_target_pairs={{0,2},{1,3},{2,0},{3,1},{4,6},{5,7},{6,4},{7,5},{8,10},{9,11},{10,... | collective-permute-start | bytes 98312 | tf_op jit(solution)/shard_map/ppermute | solution.py:345
  51.8 10.5 %collective-permute-start.12 = (bf16[2,64,128]{2,1,0:T(8,128)(2,1)S(1)}, bf16[2,64,128]{2,1,0:T(8,128)(2,1)S(1)}, u32[]{:S(2)}, u32[]{:S(2)}) collective-permute-start(bf16[2,64,128]{2,1,0:T(8,128)(2,1)S(1)} %get-tuple-element.60), channel_id=1, source_target_pairs={{0,3},{1,0},{2,1},{3,2},{4,7},{5,4},{6,5},{7,6},{8,11},{9,8},{10,9... | collective-permute-start | bytes 98312 | tf_op jit(solution)/shard_map/ppermute | solution.py:345
  58.1 10.3 %collective-permute-start.9 = (bf16[8,64,128]{2,1,0:T(8,128)(2,1)S(1)}, bf16[8,64,128]{2,1,0:T(8,128)(2,1)S(1)}, u32[]{:S(2)}, u32[]{:S(2)}) collective-permute-start(bf16[8,64,128]{2,1,0:T(8,128)(2,1)S(1)} %get-tuple-element.52), channel_id=1, source_target_pairs={{0,1},{1,2},{2,3},{3,0},{4,5},{5,6},{6,7},{7,4},{8,9},{9,10},{10,1... | collective-permute-start | bytes 393224 | tf_op jit(solution)/shard_map/ppermute | solution.py:345
  62.3 2.7 %collective-permute-start.15 = (f32[2,64,128]{2,1,0:T(8,128)S(1)}, f32[2,64,128]{2,1,0:T(8,128)S(1)}, u32[]{:S(2)}, u32[]{:S(2)}) collective-permute-start(f32[2,64,128]{2,1,0:T(8,128)S(1)} %convert_add_fusion), channel_id=1, source_target_pairs={{0,4},{4,0},{8,12},{12,8},{16,20},{20,16},{24,28},{28,24},{1,5},{5... | collective-permute-start | bytes 196616 | tf_op jit(solution)/shard_map/ppermute | solution.py:376
  62.4 10.5 %collective-permute-start.10 = (bf16[8,64,128]{2,1,0:T(8,128)(2,1)S(1)}, bf16[8,64,128]{2,1,0:T(8,128)(2,1)S(1)}, u32[]{:S(2)}, u32[]{:S(2)}) collective-permute-start(bf16[8,64,128]{2,1,0:T(8,128)(2,1)S(1)} %get-tuple-element.53), channel_id=1, source_target_pairs={{0,2},{1,3},{2,0},{3,1},{4,6},{5,7},{6,4},{7,5},{8,10},{9,11},{10,... | collective-permute-start | bytes 393224 | tf_op jit(solution)/shard_map/ppermute | solution.py:345
  65.0 8.6 %collective-permute-start.11 = (bf16[8,64,128]{2,1,0:T(8,128)(2,1)S(1)}, bf16[8,64,128]{2,1,0:T(8,128)(2,1)S(1)}, u32[]{:S(2)}, u32[]{:S(2)}) collective-permute-start(bf16[8,64,128]{2,1,0:T(8,128)(2,1)S(1)} %get-tuple-element.54), channel_id=1, source_target_pairs={{0,3},{1,0},{2,1},{3,2},{4,7},{5,4},{6,5},{7,6},{8,11},{9,8},{10,9... | collective-permute-start | bytes 393224 | tf_op jit(solution)/shard_map/ppermute | solution.py:345
  65.0 9.9 %collective-permute-start.16 = (f32[2,64,128]{2,1,0:T(8,128)S(1)}, f32[2,64,128]{2,1,0:T(8,128)S(1)}, u32[]{:S(2)}, u32[]{:S(2)}) collective-permute-start(f32[2,64,128]{2,1,0:T(8,128)S(1)} %add.24), channel_id=1, source_target_pairs={{0,8},{4,12},{8,0},{12,4},{16,24},{20,28},{24,16},{28,20},{1,9},{5... | collective-permute-start | bytes 196616 | tf_op jit(solution)/shard_map/ppermute | solution.py:378
  67.2 7.8 %collective-permute-start.17 = (f32[2,64,128]{2,1,0:T(8,128)S(1)}, f32[2,64,128]{2,1,0:T(8,128)S(1)}, u32[]{:S(2)}, u32[]{:S(2)}) collective-permute-start(f32[2,64,128]{2,1,0:T(8,128)S(1)} %add.24), channel_id=1, source_target_pairs={{0,16},{4,20},{8,24},{12,28},{16,0},{20,4},{24,8},{28,12},{1,17},{... | collective-permute-start | bytes 196616 | tf_op jit(solution)/shard_map/ppermute | solution.py:378
  68.4 6.6 %collective-permute-start.18 = (f32[2,64,128]{2,1,0:T(8,128)S(1)}, f32[2,64,128]{2,1,0:T(8,128)S(1)}, u32[]{:S(2)}, u32[]{:S(2)}) collective-permute-start(f32[2,64,128]{2,1,0:T(8,128)S(1)} %add.24), channel_id=1, source_target_pairs={{0,24},{4,28},{8,16},{12,20},{16,8},{20,12},{24,0},{28,4},{1,25},{... | collective-permute-start | bytes 196616 | tf_op jit(solution)/shard_map/ppermute | solution.py:378

commit v16 on v14

--- a/solution.py
+++ b/solution.py
@@ -95,14 +95,16 @@
 
     lax.fori_loop(0, blocks, mask_row, 0)
     agg_copies = []
+    halves = weight.shape[1] // z.shape[2]
     for s in range(reps):
         span = pl.ds(wrap(where[1] + s, reps) * share, share)
         packed[s][:share] = z[span]
-        end = packed[s].at[pl.ds(share, share)]
-        ends = [(agg.at[span], end)]
-        for h in range(weight.shape[1] // z.shape[2]):
+        ends = []
+        for h in range(halves):
             columns = pl.ds(h * z.shape[2], z.shape[2])
-            ends.append((weight.at[:, columns], packed[s].at[2 * share + h]))
+            ends.append((weight.at[:, columns], packed[s].at[share + h]))
+        if s != reps // 2:
+            ends.append((agg.at[span], packed[s].at[pl.ds(share + halves, share)]))
         for source, target in ends:
             copy = pltpu.make_async_copy(source, target, agg_sems.at[len(agg_copies)])
             copy.start()
@@ -149,11 +151,11 @@
     lists = blocks * (slots // GROUP) + slots // GROUP + STEP
     counts = [2 * blocks, blocks, blocks, blocks]
     halves = weight.shape[1] // nodes
-    packs = 2 * blocks // reps + halves
+    packs = [(2 - (s == reps // 2)) * blocks // reps + halves for s in range(reps)]
     return pl.pallas_call(
         functools.partial(tiles_kernel, slabs, reps),
         out_shape=[jax.ShapeDtypeStruct((count, features, nodes), BF16) for count in counts]
-        + [jax.ShapeDtypeStruct((packs, features, nodes), BF16)] * reps,
+        + [jax.ShapeDtypeStruct((count, features, nodes), BF16) for count in packs],
         in_specs=[smem()] * 3 + [hbm()] * 5,
         out_specs=[vmem()] * (len(counts) + reps),
         scratch_shapes=[
@@ -202,7 +204,7 @@
     for s in range(reps):
         for h in range(weights.shape[1] // nodes):
             rows, columns = pl.ds(s * features, features), pl.ds(h * nodes, nodes)
-            weights[rows, columns] = packed[(reps - s) % reps][2 * blocks + h]
+            weights[rows, columns] = packed[(reps - s) % reps][blocks + h]
     for b in range(blocks):
         mixed = jnp.dot(weights[...], whole[b], preferred_element_type=F32)
         for s in range(reps):
@@ -229,12 +231,14 @@
 
 
 def weight_kernel(reps, where, *rest):
-    packed, outs, (whole_z, whole_a) = rest[:reps], rest[reps : 2 * reps], rest[2 * reps :]
+    agg, packed, outs = rest[0], rest[1 : 1 + reps], rest[1 + reps : 1 + 2 * reps]
+    whole_z, whole_a = rest[1 + 2 * reps :]
     blocks, _, nodes = whole_z.shape
     features = packed[0].shape[1]
     lay_features(where, packed, whole_z)
     for s in range(reps):
-        whole_a[:, pl.ds(s * features, features), :] = packed[s][blocks : 2 * blocks]
+        part = agg[...] if s == reps // 2 else packed[s][packed[s].shape[0] - blocks :]
+        whole_a[:, pl.ds(s * features, features), :] = part
     total = jnp.zeros((whole_a.shape[1], whole_z.shape[1]), F32)
     for b in range(blocks):
         total += lax.dot_general(
@@ -246,14 +250,14 @@
             outs[s][h] = part.astype(BF16)
 
 
-def weight_partial(where, packed, blocks):
+def weight_partial(where, agg, packed):
     reps = len(packed)
-    _, features, nodes = packed[0].shape
+    blocks, features, nodes = agg.shape
     width = reps * features
     return pl.pallas_call(
         functools.partial(weight_kernel, reps),
         out_shape=[jax.ShapeDtypeStruct((width // nodes, features, nodes), BF16)] * reps,
-        in_specs=[smem()] + [vmem()] * reps,
+        in_specs=[smem()] + [vmem()] * (1 + reps),
         out_specs=[vmem()] * reps,
         scratch_shapes=[pltpu.VMEM((blocks, width, nodes), BF16)] * 2,
         compiler_params=pltpu.CompilerParams(vmem_limit_bytes=4 * MIB),
@@ -262,7 +266,7 @@
             bytes_accessed=4 * blocks * nodes * width + 2 * width * width,
             transcendentals=0,
         ),
-    )(where, *packed)
+    )(where, agg, *packed)
 
 
 def add_kernel(one, other, out):
@@ -354,9 +358,13 @@
     pair = [(i, i ^ 1) for i in range(slabs)]
     to_one = [(i, (i + (1 if i % 2 else -1)) % slabs) for i in range(slabs)]
     to_two = [(i, (i + (2 if i % 2 else -2)) % slabs) for i in range(slabs)]
+    share = blocks // reps
+    first = lax.rem(lax.axis_index("rep") + reps // 2, reps) * share
+    middle = shift(lax.dynamic_slice_in_dim(aggregated, first, share, 0), reps // 2)
     aside, own, one, two, *packed = contributions(
         where, col_block, live_count, cotangent, relu_mask, aggregated, weight, tiles, slabs, reps
     )
+    aside, middle = lax.optimization_barrier((aside, middle))
     aside = lax.ppermute(aside, "blk", pair)
     two_in = lax.ppermute(two, "blk", to_two)
     one = add(one, aside)
@@ -366,7 +374,7 @@
     packed = [shift(value, s) for s, value in enumerate(packed)]
     shares = total_shares(where, aside, [own, one_in, two_in], reps)
     held, _ = lax.optimization_barrier((packed, shares))
-    pieces = weight_partial(where, held, blocks // reps)
+    pieces = weight_partial(where, middle, held)
     pieces = [shift(value, -s) for s, value in enumerate(pieces)]
     shares = [shift(value, s) for s, value in enumerate(shares)]
     outs = [shift(value, s) for s, value in enumerate(mix(where, shares, packed))]

time: 72.9 us -> 72.2 us (level)
  the two profiles are of different devices: /device:TPU:0 before, /device:TPU:13 now
where the time goes in v16:
time: 72.2 us; the launch traced here: 71.1 us
  waiting for transfers between devices  36.8 us (51%)
  starting transfers between devices  17.5 us (24%)
  Pallas kernels  14.3 us (20%)
  local copies, waits for them, and re-layouts  0.92 us (1%)
  between operations  0.8 us (1%)
  other arithmetic  0.75 us (1%)
    ppermute x13, waiting for transfers between devices, shift(): lax.ppermute(value, 'rep', [(i, (i + steps) % reps) for i in range(reps)])  15.8 us
    ppermute x13, starting transfers between devices, shift(): lax.ppermute(value, 'rep', [(i, (i + steps) % reps) for i in range(reps)])  13.3 us
    pallas_call x1, Pallas kernels, contributions(): pl.pallas_call(functools.partial(tiles_kernel, slabs, reps), out_shape=[j...  9.86 us
    ppermute x1, waiting for transfers between devices, on_device(): two_in = lax.ppermute(two, 'blk', to_two)  9.54 us
    ppermute x1, waiting for transfers between devices, on_device(): one_in = lax.ppermute(one, 'blk', to_one)  9.21 us
    ppermute x3, starting transfers between devices, on_device(): lax.ppermute(grad_w, 'blk', [(i, i ^ step) for i in range(slabs)])  2.71 us
    ppermute x1, waiting for transfers between devices, on_device(): aside = lax.ppermute(aside, 'blk', pair)  2.28 us
  transfers between devices with their start and end apart: 20, of which 7 were waited for; matrix products, arithmetic and copies ran while one was open for 0% of the time, Pallas kernels for 20%

profile of v16, /device:TPU:13, one launch (start us, length us, event | category | flops | bytes accessed | tf_op | source)
XLA Modules:
  0.0 71.1 jit_solution(15779417495248261608)
XLA Ops:
  0.6 0.9 %constant_dynamic-slice_fusion = bf16[8,64,128]{2,1,0:T(8,128)(2,1)S(1)} fusion(bf16[32,64,128]{2,1,0:T(8,128)(2,1)} %agg.1, s32[]{:T(128)S(6)} %select_n.3), kind=kLoop, calls=%fused_computation.4 | loop fusion | bytes 262148 | tf_op jit(solution)/shard_map/dynamic_slice | solution.py:363
  1.6 2.4 %collective-permute-start = (bf16[8,64,128]{2,1,0:T(8,128)(2,1)S(1)}, bf16[8,64,128]{2,1,0:T(8,128)(2,1)S(1)}, u32[]{:S(2)}, u32[]{:S(2)}) collective-permute-start(bf16[8,64,128]{2,1,0:T(8,128)(2,1)S(1)} %constant_dynamic-slice_fusion), channel_id=1, source_target_pairs={{0,2},{1,3},{2,0},{3,1},{4,6},{5,7},{6,4},{7,5},{8,10},{9,11},{10,... | collective-permute-start | bytes 393224 | tf_op jit(solution)/shard_map/ppermute | solution.py:349
  3.9 0.1 pad_add_fusion.where
  4.0 9.9 %shard_map.86 = (bf16[64,64,128]{2,1,0:T(8,128)(2,1)S(1)}, bf16[32,64,128]{2,1,0:T(8,128)(2,1)S(1)}, bf16[32,64,128]{2,1,0:T(8,128)(2,1)S(1)}, bf16[32,64,128]{2...) custom-call(s32[2]{0:T(128)S(1)} %pad_add_fusion.where, ...), custom_call_target="tpu_custom_call" | custom-call | flops 1073741824 | bytes 16777216 | tf_op jit(solution)/shard_map/pallas_call | solution.py:155
  13.9 0.6 collective-permute-start.1
  14.5 2.3 %collective-permute-done.1.other.aside = bf16[64,64,128]{2,1,0:T(8,128)(2,1)S(1)} collective-permute-done((bf16[64,64,128]{2,1,0:T(8,128)(2,1)S(1)}, bf16[64,64,128]{2,1,0:T(8,128)(2,1)S(1)}, u32[]{:S(2)}, u32[]{:S(2)}) %collective-permute-start.1) | collective-permute-done | bytes 1048608 | tf_op jit(solution)/shard_map/ppermute | solution.py:368
  16.8 0.2 shard_map.87
  17.0 0.3 collective-permute-start.2
  17.3 1.5 %collective-permute-start.9 = (bf16[18,64,128]{2,1,0:T(8,128)(2,1)S(1)}, bf16[18,64,128]{2,1,0:T(8,128)(2,1)S(1)}, u32[]{:S(2)}, u32[]{:S(2)}) collective-permute-start(bf16[18,64,128]{2,1,0:T(8,128)(2,1)S(1)} %get-tuple-element.51), channel_id=1, source_target_pairs={{0,3},{1,0},{2,1},{3,2},{4,7},{5,4},{6,5},{7,6},{8,11},{9,8},{10,9... | collective-permute-start | bytes 884744 | tf_op jit(solution)/shard_map/ppermute | solution.py:349
  18.8 0.8 %collective-permute-start.8 = (bf16[10,64,128]{2,1,0:T(8,128)(2,1)S(1)}, bf16[10,64,128]{2,1,0:T(8,128)(2,1)S(1)}, u32[]{:S(2)}, u32[]{:S(2)}) collective-permute-start(bf16[10,64,128]{2,1,0:T(8,128)(2,1)S(1)} %get-tuple-element.50), channel_id=1, source_target_pairs={{0,2},{1,3},{2,0},{3,1},{4,6},{5,7},{6,4},{7,5},{8,10},{9,11},{10,... | collective-permute-start | bytes 491528 | tf_op jit(solution)/shard_map/ppermute | solution.py:349
  19.6 9.5 %collective-permute-done.3.rest_2_ = bf16[32,64,128]{2,1,0:T(8,128)(2,1)S(1)} collective-permute-done((bf16[32,64,128]{2,1,0:T(8,128)(2,1)S(1)}, bf16[32,64,128]{2,1,0:T(8,128)(2,1)S(1)}, u32[]{:S(2)}, u32[]{:S(2)}) %collective-permute-start.3) | collective-permute-done | bytes 524320 | tf_op jit(solution)/shard_map/ppermute | solution.py:369
  29.1 9.2 %collective-permute-done.2.rest_1_ = bf16[32,64,128]{2,1,0:T(8,128)(2,1)S(1)} collective-permute-done((bf16[32,64,128]{2,1,0:T(8,128)(2,1)S(1)}, bf16[32,64,128]{2,1,0:T(8,128)(2,1)S(1)}, u32[]{:S(2)}, u32[]{:S(2)}) %collective-permute-start.2) | collective-permute-done | bytes 524320 | tf_op jit(solution)/shard_map/ppermute | solution.py:371
  38.3 0.8 %shard_map.88 = (bf16[8,64,128]{2,1,0:T(8,128)(2,1)S(1)}, bf16[8,64,128]{2,1,0:T(8,128)(2,1)S(1)}, bf16[8,64,128]{2,1,0:T(8,128)(2,1)S(1)}, bf16[8,64,128]{2,1,0:T(8,128)(2,1)S(1)}) custom-call(s32[2]{0:T(128)S(1)} %pad_add_fusion.where, bf16[64,64,128]{2,1,0:T(8,128)(2,1)S(1)} %collective-permute-done.1.other.aside, ...), custom_call_target="tpu_custom_call" | custom-call | flops 1048576 | bytes 2621440 | tf_op jit(solution)/shard_map/pallas_call | solution.py:308
  39.1 0.1 collective-permute-start.4
  39.2 2.2 %collective-permute-start.5 = (bf16[8,64,128]{2,1,0:T(8,128)(2,1)S(1)}, bf16[8,64,128]{2,1,0:T(8,128)(2,1)S(1)}, u32[]{:S(2)}, u32[]{:S(2)}) collective-permute-start(bf16[8,64,128]{2,1,0:T(8,128)(2,1)S(1)} %get-tuple-element.42), channel_id=1, source_target_pairs={{0,2},{1,3},{2,0},{3,1},{4,6},{5,7},{6,4},{7,5},{8,10},{9,11},{10,... | collective-permute-start | bytes 393224 | tf_op jit(solution)/shard_map/ppermute | solution.py:349
  41.4 1.0 %shard_map.91 = (bf16[2,64,128]{2,1,0:T(8,128)(2,1)S(1)}, bf16[2,64,128]{2,1,0:T(8,128)(2,1)S(1)}, bf16[2,64,128]{2,1,0:T(8,128)(2,1)S(1)}, bf16[2,64,128]{2,1,0:T(8,128)(2,1)S(1)}) custom-call(s32[2]{0:T(128)S(1)} %pad_add_fusion.where, bf16[8,64,128]{2,1,0:T(8,128)(2,1)S(1)} %collective-permute-done.rest_0_, ...), custom_call_target="tpu_custom_call" | custom-call | flops 134217728 | bytes 1179648 | tf_op jit(solution)/shard_map/pallas_call | solution.py:257
  42.5 1.4 %collective-permute-start.13 = (bf16[2,64,128]{2,1,0:T(8,128)(2,1)S(1)}, bf16[2,64,128]{2,1,0:T(8,128)(2,1)S(1)}, u32[]{:S(2)}, u32[]{:S(2)}) collective-permute-start(bf16[2,64,128]{2,1,0:T(8,128)(2,1)S(1)} %get-tuple-element.62), channel_id=1, source_target_pairs={{0,3},{1,0},{2,1},{3,2},{4,7},{5,4},{6,5},{7,6},{8,11},{9,8},{10,9... | collective-permute-start | bytes 98312 | tf_op jit(solution)/shard_map/ppermute | solution.py:349
  43.9 1.3 %collective-permute-start.14 = (bf16[2,64,128]{2,1,0:T(8,128)(2,1)S(1)}, bf16[2,64,128]{2,1,0:T(8,128)(2,1)S(1)}, u32[]{:S(2)}, u32[]{:S(2)}) collective-permute-start(bf16[2,64,128]{2,1,0:T(8,128)(2,1)S(1)} %get-tuple-element.63), channel_id=1, source_target_pairs={{0,2},{1,3},{2,0},{3,1},{4,6},{5,7},{6,4},{7,5},{8,10},{9,11},{10,... | collective-permute-start | bytes 98312 | tf_op jit(solution)/shard_map/ppermute | solution.py:349
  45.2 1.3 %collective-permute-start.15 = (bf16[2,64,128]{2,1,0:T(8,128)(2,1)S(1)}, bf16[2,64,128]{2,1,0:T(8,128)(2,1)S(1)}, u32[]{:S(2)}, u32[]{:S(2)}) collective-permute-start(bf16[2,64,128]{2,1,0:T(8,128)(2,1)S(1)} %get-tuple-element.64), channel_id=1, source_target_pairs={{0,1},{1,2},{2,3},{3,0},{4,5},{5,6},{6,7},{7,4},{8,9},{9,10},{10,1... | collective-permute-start | bytes 98312 | tf_op jit(solution)/shard_map/ppermute | solution.py:349
  46.5 5.2 %collective-permute-done.5.rest_2_ = bf16[8,64,128]{2,1,0:T(8,128)(2,1)S(1)} collective-permute-done((bf16[8,64,128]{2,1,0:T(8,128)(2,1)S(1)}, bf16[8,64,128]{2,1,0:T(8,128)(2,1)S(1)}, u32[]{:S(2)}, u32[]{:S(2)}) %collective-permute-start.5) | collective-permute-done | bytes 131104 | tf_op jit(solution)/shard_map/ppermute | solution.py:349
  51.6 3.6 %collective-permute-done.6.rest_3_ = bf16[8,64,128]{2,1,0:T(8,128)(2,1)S(1)} collective-permute-done((bf16[8,64,128]{2,1,0:T(8,128)(2,1)S(1)}, bf16[8,64,128]{2,1,0:T(8,128)(2,1)S(1)}, u32[]{:S(2)}, u32[]{:S(2)}) %collective-permute-start.6) | collective-permute-done | bytes 131104 | tf_op jit(solution)/shard_map/ppermute | solution.py:349
  55.2 1.0 %shard_map.89 = (bf16[8,64,128]{2,1,0:T(8,128)(2,1)S(1)}, bf16[8,64,128]{2,1,0:T(8,128)(2,1)S(1)}, bf16[8,64,128]{2,1,0:T(8,128)(2,1)S(1)}, bf16[8,64,128]{2,1,0:T(8,128)(2,1)S(1)}) custom-call(s32[2]{0:T(128)S(1)} %pad_add_fusion.where, bf16[8,64,128]{2,1,0:T(8,128)(2,1)S(1)} %get-tuple-element.40.rest_0_, ...), custom_call_target="tpu_custom_call" | custom-call | flops 134217728 | bytes 1048576 | tf_op jit(solution)/shard_map/pallas_call | solution.py:218
  56.3 0.7 collective-permute-start.16
  57.0 0.6 collective-permute-start.11
  57.6 1.7 %collective-permute-start.12 = (bf16[8,64,128]{2,1,0:T(8,128)(2,1)S(1)}, bf16[8,64,128]{2,1,0:T(8,128)(2,1)S(1)}, u32[]{:S(2)}, u32[]{:S(2)}) collective-permute-start(bf16[8,64,128]{2,1,0:T(8,128)(2,1)S(1)} %get-tuple-element.55), channel_id=1, source_target_pairs={{0,3},{1,0},{2,1},{3,2},{4,7},{5,4},{6,5},{7,6},{8,11},{9,8},{10,9... | collective-permute-start | bytes 393224 | tf_op jit(solution)/shard_map/ppermute | solution.py:349
  59.3 0.1 collective-permute-start.19
  59.4 1.5 %collective-permute-start.18 = (f32[2,64,128]{2,1,0:T(8,128)S(1)}, f32[2,64,128]{2,1,0:T(8,128)S(1)}, u32[]{:S(2)}, u32[]{:S(2)}) collective-permute-start(f32[2,64,128]{2,1,0:T(8,128)S(1)} %add.32), channel_id=1, source_target_pairs={{0,16},{4,20},{8,24},{12,28},{16,0},{20,4},{24,8},{28,12},{1,17},{... | collective-permute-start | bytes 196616 | tf_op jit(solution)/shard_map/ppermute | solution.py:386
  60.9 1.2 %collective-permute-start.17 = (f32[2,64,128]{2,1,0:T(8,128)S(1)}, f32[2,64,128]{2,1,0:T(8,128)S(1)}, u32[]{:S(2)}, u32[]{:S(2)}) collective-permute-start(f32[2,64,128]{2,1,0:T(8,128)S(1)} %add.32), channel_id=1, source_target_pairs={{0,8},{4,12},{8,0},{12,4},{16,24},{20,28},{24,16},{28,20},{1,9},{5... | collective-permute-start | bytes 196616 | tf_op jit(solution)/shard_map/ppermute | solution.py:386
  62.0 5.1 %collective-permute-done.11.rest_2_ = bf16[8,64,128]{2,1,0:T(8,128)(2,1)S(1)} collective-permute-done((bf16[8,64,128]{2,1,0:T(8,128)(2,1)S(1)}, bf16[8,64,128]{2,1,0:T(8,128)(2,1)S(1)}, u32[]{:S(2)}, u32[]{:S(2)}) %collective-permute-start.11) | collective-permute-done | bytes 131104 | tf_op jit(solution)/shard_map/ppermute | solution.py:349
  67.1 1.9 %collective-permute-done.12.rest_3_ = bf16[8,64,128]{2,1,0:T(8,128)(2,1)S(1)} collective-permute-done((bf16[8,64,128]{2,1,0:T(8,128)(2,1)S(1)}, bf16[8,64,128]{2,1,0:T(8,128)(2,1)S(1)}, u32[]{:S(2)}, u32[]{:S(2)}) %collective-permute-start.12) | collective-permute-done | bytes 131104 | tf_op jit(solution)/shard_map/ppermute | solution.py:349
  69.1 1.4 %shard_map.90 = bf16[32,64,128]{2,1,0:T(8,128)(2,1)} custom-call(s32[2]{0:T(128)S(1)} %pad_add_fusion.where, bf16[8,64,128]{2,1,0:T(8,128)(2,1)S(1)} %get-tuple-element.52.rest_0_, bf16[8,64,128]{2,1,0:T(8,128)(2,1)S(1)} %collective-permute-done.10.rest_1_, bf16[8,64,128]{2,1,0:T(8,128)(2,1)S(1)} %collective-permute-done.11.rest_2_, ...), custom_call_target="tpu_custom_call" | custom-call | bytes 33554432 | tf_op jit(solution)/shard_map/pallas_call | solution.py:334
  70.5 0.6 copy_bitcast_fusion
  (19 shorter events, 0.1 us)
Async XLA Ops:
  1.6 12.3 %collective-permute-start = (bf16[8,64,128]{2,1,0:T(8,128)(2,1)S(1)}, bf16[8,64,128]{2,1,0:T(8,128)(2,1)S(1)}, u32[]{:S(2)}, u32[]{:S(2)}) collective-permute-start(bf16[8,64,128]{2,1,0:T(8,128)(2,1)S(1)} %constant_dynamic-slice_fusion), channel_id=1, source_target_pairs={{0,2},{1,3},{2,0},{3,1},{4,6},{5,7},{6,4},{7,5},{8,10},{9,11},{10,... | collective-permute-start | bytes 393224 | tf_op jit(solution)/shard_map/ppermute | solution.py:349
  13.9 2.9 %collective-permute-start.1 = (bf16[64,64,128]{2,1,0:T(8,128)(2,1)S(1)}, bf16[64,64,128]{2,1,0:T(8,128)(2,1)S(1)}, u32[]{:S(2)}, u32[]{:S(2)}) collective-permute-start(bf16[64,64,128]{2,1,0:T(8,128)(2,1)S(1)} %get-tuple-element.36), channel_id=1, source_target_pairs={{0,4},{4,0},{8,12},{12,8},{16,20},{20,16},{24,28},{28,24},{1,5},{5... | collective-permute-start | bytes 3145736 | tf_op jit(solution)/shard_map/ppermute | solution.py:368
  14.5 14.6 %collective-permute-start.3 = (bf16[32,64,128]{2,1,0:T(8,128)(2,1)S(1)}, bf16[32,64,128]{2,1,0:T(8,128)(2,1)S(1)}, u32[]{:S(2)}, u32[]{:S(2)}) collective-permute-start(bf16[32,64,128]{2,1,0:T(8,128)(2,1)S(1)} %get-tuple-element.39), channel_id=1, source_target_pairs={{0,24},{4,12},{8,0},{12,20},{16,8},{20,28},{24,16},{28,4},{1,25},{... | collective-permute-start | bytes 1572872 | tf_op jit(solution)/shard_map/ppermute | solution.py:369
  17.0 21.3 %collective-permute-start.2 = (bf16[32,64,128]{2,1,0:T(8,128)(2,1)S(1)}, bf16[32,64,128]{2,1,0:T(8,128)(2,1)S(1)}, u32[]{:S(2)}, u32[]{:S(2)}) collective-permute-start(bf16[32,64,128]{2,1,0:T(8,128)(2,1)S(1)} %shard_map.87), channel_id=1, source_target_pairs={{0,28},{4,8},{8,4},{12,16},{16,12},{20,24},{24,20},{28,0},{1,29},{... | collective-permute-start | bytes 1572872 | tf_op jit(solution)/shard_map/ppermute | solution.py:371
  17.3 24.1 %collective-permute-start.7 = (bf16[18,64,128]{2,1,0:T(8,128)(2,1)S(1)}, bf16[18,64,128]{2,1,0:T(8,128)(2,1)S(1)}, u32[]{:S(2)}, u32[]{:S(2)}) collective-permute-start(bf16[18,64,128]{2,1,0:T(8,128)(2,1)S(1)} %get-tuple-element.49), channel_id=1, source_target_pairs={{0,1},{1,2},{2,3},{3,0},{4,5},{5,6},{6,7},{7,4},{8,9},{9,10},{10,1... | collective-permute-start | bytes 884744 | tf_op jit(solution)/shard_map/ppermute | solution.py:349
  17.3 24.1 %collective-permute-start.9 = (bf16[18,64,128]{2,1,0:T(8,128)(2,1)S(1)}, bf16[18,64,128]{2,1,0:T(8,128)(2,1)S(1)}, u32[]{:S(2)}, u32[]{:S(2)}) collective-permute-start(bf16[18,64,128]{2,1,0:T(8,128)(2,1)S(1)} %get-tuple-element.51), channel_id=1, source_target_pairs={{0,3},{1,0},{2,1},{3,2},{4,7},{5,4},{6,5},{7,6},{8,11},{9,8},{10,9... | collective-permute-start | bytes 884744 | tf_op jit(solution)/shard_map/ppermute | solution.py:349
  18.8 22.7 %collective-permute-start.8 = (bf16[10,64,128]{2,1,0:T(8,128)(2,1)S(1)}, bf16[10,64,128]{2,1,0:T(8,128)(2,1)S(1)}, u32[]{:S(2)}, u32[]{:S(2)}) collective-permute-start(bf16[10,64,128]{2,1,0:T(8,128)(2,1)S(1)} %get-tuple-element.50), channel_id=1, source_target_pairs={{0,2},{1,3},{2,0},{3,1},{4,6},{5,7},{6,4},{7,5},{8,10},{9,11},{10,... | collective-permute-start | bytes 491528 | tf_op jit(solution)/shard_map/ppermute | solution.py:349
  39.1 6.1 %collective-permute-start.4 = (bf16[8,64,128]{2,1,0:T(8,128)(2,1)S(1)}, bf16[8,64,128]{2,1,0:T(8,128)(2,1)S(1)}, u32[]{:S(2)}, u32[]{:S(2)}) collective-permute-start(bf16[8,64,128]{2,1,0:T(8,128)(2,1)S(1)} %get-tuple-element.41), channel_id=1, source_target_pairs={{0,1},{1,2},{2,3},{3,0},{4,5},{5,6},{6,7},{7,4},{8,9},{9,10},{10,1... | collective-permute-start | bytes 393224 | tf_op jit(solution)/shard_map/ppermute | solution.py:349
  39.2 12.4 %collective-permute-start.5 = (bf16[8,64,128]{2,1,0:T(8,128)(2,1)S(1)}, bf16[8,64,128]{2,1,0:T(8,128)(2,1)S(1)}, u32[]{:S(2)}, u32[]{:S(2)}) collective-permute-start(bf16[8,64,128]{2,1,0:T(8,128)(2,1)S(1)} %get-tuple-element.42), channel_id=1, source_target_pairs={{0,2},{1,3},{2,0},{3,1},{4,6},{5,7},{6,4},{7,5},{8,10},{9,11},{10,... | collective-permute-start | bytes 393224 | tf_op jit(solution)/shard_map/ppermute | solution.py:349
  41.4 13.8 %collective-permute-start.6 = (bf16[8,64,128]{2,1,0:T(8,128)(2,1)S(1)}, bf16[8,64,128]{2,1,0:T(8,128)(2,1)S(1)}, u32[]{:S(2)}, u32[]{:S(2)}) collective-permute-start(bf16[8,64,128]{2,1,0:T(8,128)(2,1)S(1)} %get-tuple-element.43), channel_id=1, source_target_pairs={{0,3},{1,0},{2,1},{3,2},{4,7},{5,4},{6,5},{7,6},{8,11},{9,8},{10,9... | collective-permute-start | bytes 393224 | tf_op jit(solution)/shard_map/ppermute | solution.py:349
  42.5 13.8 %collective-permute-start.13 = (bf16[2,64,128]{2,1,0:T(8,128)(2,1)S(1)}, bf16[2,64,128]{2,1,0:T(8,128)(2,1)S(1)}, u32[]{:S(2)}, u32[]{:S(2)}) collective-permute-start(bf16[2,64,128]{2,1,0:T(8,128)(2,1)S(1)} %get-tuple-element.62), channel_id=1, source_target_pairs={{0,3},{1,0},{2,1},{3,2},{4,7},{5,4},{6,5},{7,6},{8,11},{9,8},{10,9... | collective-permute-start | bytes 98312 | tf_op jit(solution)/shard_map/ppermute | solution.py:349
  43.9 12.4 %collective-permute-start.14 = (bf16[2,64,128]{2,1,0:T(8,128)(2,1)S(1)}, bf16[2,64,128]{2,1,0:T(8,128)(2,1)S(1)}, u32[]{:S(2)}, u32[]{:S(2)}) collective-permute-start(bf16[2,64,128]{2,1,0:T(8,128)(2,1)S(1)} %get-tuple-element.63), channel_id=1, source_target_pairs={{0,2},{1,3},{2,0},{3,1},{4,6},{5,7},{6,4},{7,5},{8,10},{9,11},{10,... | collective-permute-start | bytes 98312 | tf_op jit(solution)/shard_map/ppermute | solution.py:349
  45.2 11.1 %collective-permute-start.15 = (bf16[2,64,128]{2,1,0:T(8,128)(2,1)S(1)}, bf16[2,64,128]{2,1,0:T(8,128)(2,1)S(1)}, u32[]{:S(2)}, u32[]{:S(2)}) collective-permute-start(bf16[2,64,128]{2,1,0:T(8,128)(2,1)S(1)} %get-tuple-element.64), channel_id=1, source_target_pairs={{0,1},{1,2},{2,3},{3,0},{4,5},{5,6},{6,7},{7,4},{8,9},{9,10},{10,1... | collective-permute-start | bytes 98312 | tf_op jit(solution)/shard_map/ppermute | solution.py:349
  56.2 4.7 %collective-permute-start.10 = (bf16[8,64,128]{2,1,0:T(8,128)(2,1)S(1)}, bf16[8,64,128]{2,1,0:T(8,128)(2,1)S(1)}, u32[]{:S(2)}, u32[]{:S(2)}) collective-permute-start(bf16[8,64,128]{2,1,0:T(8,128)(2,1)S(1)} %get-tuple-element.53), channel_id=1, source_target_pairs={{0,1},{1,2},{2,3},{3,0},{4,5},{5,6},{6,7},{7,4},{8,9},{9,10},{10,1... | collective-permute-start | bytes 393224 | tf_op jit(solution)/shard_map/ppermute | solution.py:349
  56.3 3.0 %collective-permute-start.16 = (f32[2,64,128]{2,1,0:T(8,128)S(1)}, f32[2,64,128]{2,1,0:T(8,128)S(1)}, u32[]{:S(2)}, u32[]{:S(2)}) collective-permute-start(f32[2,64,128]{2,1,0:T(8,128)S(1)} %convert_add_fusion), channel_id=1, source_target_pairs={{0,4},{4,0},{8,12},{12,8},{16,20},{20,16},{24,28},{28,24},{1,5},{5... | collective-permute-start | bytes 196616 | tf_op jit(solution)/shard_map/ppermute | solution.py:384
  57.0 10.1 %collective-permute-start.11 = (bf16[8,64,128]{2,1,0:T(8,128)(2,1)S(1)}, bf16[8,64,128]{2,1,0:T(8,128)(2,1)S(1)}, u32[]{:S(2)}, u32[]{:S(2)}) collective-permute-start(bf16[8,64,128]{2,1,0:T(8,128)(2,1)S(1)} %get-tuple-element.54), channel_id=1, source_target_pairs={{0,2},{1,3},{2,0},{3,1},{4,6},{5,7},{6,4},{7,5},{8,10},{9,11},{10,... | collective-permute-start | bytes 393224 | tf_op jit(solution)/shard_map/ppermute | solution.py:349
  57.6 11.5 %collective-permute-start.12 = (bf16[8,64,128]{2,1,0:T(8,128)(2,1)S(1)}, bf16[8,64,128]{2,1,0:T(8,128)(2,1)S(1)}, u32[]{:S(2)}, u32[]{:S(2)}) collective-permute-start(bf16[8,64,128]{2,1,0:T(8,128)(2,1)S(1)} %get-tuple-element.55), channel_id=1, source_target_pairs={{0,3},{1,0},{2,1},{3,2},{4,7},{5,4},{6,5},{7,6},{8,11},{9,8},{10,9... | collective-permute-start | bytes 393224 | tf_op jit(solution)/shard_map/ppermute | solution.py:349
  59.3 11.1 %collective-permute-start.19 = (f32[2,64,128]{2,1,0:T(8,128)S(1)}, f32[2,64,128]{2,1,0:T(8,128)S(1)}, u32[]{:S(2)}, u32[]{:S(2)}) collective-permute-start(f32[2,64,128]{2,1,0:T(8,128)S(1)} %add.32), channel_id=1, source_target_pairs={{0,24},{4,28},{8,16},{12,20},{16,8},{20,12},{24,0},{28,4},{1,25},{... | collective-permute-start | bytes 196616 | tf_op jit(solution)/shard_map/ppermute | solution.py:386
  59.4 11.0 %collective-permute-start.18 = (f32[2,64,128]{2,1,0:T(8,128)S(1)}, f32[2,64,128]{2,1,0:T(8,128)S(1)}, u32[]{:S(2)}, u32[]{:S(2)}) collective-permute-start(f32[2,64,128]{2,1,0:T(8,128)S(1)} %add.32), channel_id=1, source_target_pairs={{0,16},{4,20},{8,24},{12,28},{16,0},{20,4},{24,8},{28,12},{1,17},{... | collective-permute-start | bytes 196616 | tf_op jit(solution)/shard_map/ppermute | solution.py:386
  60.9 9.6 %collective-permute-start.17 = (f32[2,64,128]{2,1,0:T(8,128)S(1)}, f32[2,64,128]{2,1,0:T(8,128)S(1)}, u32[]{:S(2)}, u32[]{:S(2)}) collective-permute-start(f32[2,64,128]{2,1,0:T(8,128)S(1)} %add.32), channel_id=1, source_target_pairs={{0,8},{4,12},{8,0},{12,4},{16,24},{20,28},{24,16},{28,20},{1,9},{5... | collective-permute-start | bytes 196616 | tf_op jit(solution)/shard_map/ppermute | solution.py:386

commit v17 on v14

--- a/solution.py
+++ b/solution.py
@@ -10,7 +10,7 @@
 
 REACH = 2
 GROUP = 4
-STEP = 8
+STEP = 16
 BF16 = jnp.bfloat16
 F32 = jnp.float32
 MIB = 1 << 20
@@ -186,6 +186,18 @@
     )
 
 
+def order_of(reps):
+    return sorted(range(reps), key=lambda s: (s == 0, abs(2 * s - reps), s))
+
+
+def in_order(shares):
+    return [shares[s] for s in order_of(len(shares))]
+
+
+def by_distance(refs):
+    return [refs[order_of(len(refs)).index(s)] for s in range(len(refs))]
+
+
 def lay_features(where, shares, whole):
     reps, blocks = len(shares), whole.shape[0]
     features = shares[0].shape[1]
@@ -195,8 +207,8 @@
 
 
 def mix_kernel(reps, where, *rest):
-    shares, packed, outs = rest[:reps], rest[reps : 2 * reps], rest[2 * reps : 3 * reps]
-    weights, whole = rest[3 * reps :]
+    shares, packed = by_distance(rest[:reps]), by_distance(rest[reps : 2 * reps])
+    outs, (weights, whole) = rest[2 * reps : 3 * reps], rest[3 * reps :]
     blocks, features, nodes = outs[0].shape
     lay_features(where, shares, whole)
     for s in range(reps):
@@ -225,11 +237,12 @@
             bytes_accessed=4 * blocks * nodes * width,
             transcendentals=0,
         ),
-    )(where, *shares, *packed)
+    )(where, *in_order(shares), *in_order(packed))
 
 
 def weight_kernel(reps, where, *rest):
-    packed, outs, (whole_z, whole_a) = rest[:reps], rest[reps : 2 * reps], rest[2 * reps :]
+    packed, outs = by_distance(rest[:reps]), rest[reps : 2 * reps]
+    whole_z, whole_a = rest[2 * reps :]
     blocks, _, nodes = whole_z.shape
     features = packed[0].shape[1]
     lay_features(where, packed, whole_z)
@@ -262,7 +275,7 @@
             bytes_accessed=4 * blocks * nodes * width + 2 * width * width,
             transcendentals=0,
         ),
-    )(where, *packed)
+    )(where, *in_order(packed))
 
 
 def add_kernel(one, other, out):
@@ -314,7 +327,7 @@
 
 
 def lay_kernel(reps, where, *rest):
-    shares, out, sems = rest[:reps], rest[reps], rest[reps + 1]
+    shares, out, sems = by_distance(rest[:reps]), rest[reps], rest[reps + 1]
     blocks = shares[0].shape[0]
     copies = []
     for s in range(reps):
@@ -335,7 +348,7 @@
         scratch_shapes=[pltpu.SemaphoreType.DMA((reps,))],
         compiler_params=pltpu.CompilerParams(vmem_limit_bytes=2 * MIB),
         cost_estimate=pl.CostEstimate(flops=0, bytes_accessed=32 * MIB, transcendentals=0),
-    )(where, *shares)
+    )(where, *in_order(shares))
 
 
 def shift(value, steps):
@@ -343,6 +356,10 @@
     if steps % reps == 0:
         return value
     return lax.ppermute(value, "rep", [(i, (i + steps) % reps) for i in range(reps)])
+
+
+def exchange(shares, sign=1):
+    return [shift(value, sign * s) for s, value in enumerate(shares)]
 
 
 def on_device(cotangent, relu_mask, aggregated, weight, tiles, col_block, live_count):
@@ -363,13 +380,13 @@
     one_in = lax.ppermute(one, "blk", to_one)
 
     packed, _ = lax.optimization_barrier((packed, one))
-    packed = [shift(value, s) for s, value in enumerate(packed)]
+    packed = exchange(packed)
     shares = total_shares(where, aside, [own, one_in, two_in], reps)
     held, _ = lax.optimization_barrier((packed, shares))
     pieces = weight_partial(where, held, blocks // reps)
-    pieces = [shift(value, -s) for s, value in enumerate(pieces)]
-    shares = [shift(value, s) for s, value in enumerate(shares)]
-    outs = [shift(value, s) for s, value in enumerate(mix(where, shares, packed))]
+    pieces = exchange(pieces, -1)
+    shares = exchange(shares)
+    outs = exchange(mix(where, shares, packed))
     input_grad = lay_blocks(where, outs, cotangent.shape)
 
     grad_w = sum(value.astype(F32) for value in pieces)

time: 72.9 us -> 75.1 us (1.030)
  starting transfers between devices: 38.7 us -> 41.8 us
  waiting for transfers between devices: 20.9 us -> 18.3 us
  Pallas kernels: 11.3 us -> 12.7 us
    ppermute x12, starting transfers between devices: 27 us -> 32.4 us  [shift(): lax.ppermute(value, 'rep', [(i, (i + steps) % reps) for i in range(reps)])]
    ppermute x1, starting transfers between devices: 5.23 us -> 2.01 us  [on_device(): two_in = lax.ppermute(two, 'blk', to_two)]
    ppermute x12, waiting for transfers between devices: 5.57 us -> 3.64 us  [shift(): lax.ppermute(value, 'rep', [(i, (i + steps) % reps) for i in range(reps)])]
    pallas_call x1, Pallas kernels: 6.85 us -> 8.32 us  [contributions(): pl.pallas_call(functools.partial(tiles_kernel, slabs, reps), out_shape=[j...]
    ppermute x1, waiting for transfers between devices: 4.52 us -> 3.55 us  [on_device(): two_in = lax.ppermute(two, 'blk', to_two)]
    ppermute x1, starting transfers between devices: 0.51 us -> 1.27 us  [on_device(): aside = lax.ppermute(aside, 'blk', pair)]
where the time goes in v17:
time: 75.1 us; the launch traced here: 74.4 us
  starting transfers between devices  41.8 us (56%)
  waiting for transfers between devices  18.3 us (24%)
  Pallas kernels  12.7 us (17%)
    ppermute x12, starting transfers between devices, shift(): lax.ppermute(value, 'rep', [(i, (i + steps) % reps) for i in range(reps)])  32.4 us
    ppermute x1, waiting for transfers between devices, on_device(): one_in = lax.ppermute(one, 'blk', to_one)  10.3 us
    pallas_call x1, Pallas kernels, contributions(): pl.pallas_call(functools.partial(tiles_kernel, slabs, reps), out_shape=[j...  8.32 us
    ppermute x3, starting transfers between devices, on_device(): lax.ppermute(grad_w, 'blk', [(i, i ^ step) for i in range(slabs)])  3.91 us
    ppermute x12, waiting for transfers between devices, shift(): lax.ppermute(value, 'rep', [(i, (i + steps) % reps) for i in range(reps)])  3.64 us
    ppermute x1, waiting for transfers between devices, on_device(): two_in = lax.ppermute(two, 'blk', to_two)  3.55 us
    ppermute x1, starting transfers between devices, on_device(): one_in = lax.ppermute(one, 'blk', to_one)  2.12 us
    ppermute x1, starting transfers between devices, on_device(): two_in = lax.ppermute(two, 'blk', to_two)  2.01 us
  transfers between devices with their start and end apart: 19, of which 6 were waited for; matrix products, arithmetic and copies ran while one was open for 0% of the time, Pallas kernels for 6%

profile of v17, /device:TPU:0, one launch (start us, length us, event | category | flops | bytes accessed | tf_op | source)
XLA Modules:
  0.0 74.4 jit_solution(10805769197085770778)
XLA Ops:
  0.6 0.1 pad_add_fusion.where
  0.7 8.3 %shard_map.86 = (bf16[64,64,128]{2,1,0:T(8,128)(2,1)S(1)}, bf16[32,64,128]{2,1,0:T(8,128)(2,1)S(1)}, bf16[32,64,128]{2,1,0:T(8,128)(2,1)S(1)}, bf16[32,64,128]{2...) custom-call(s32[2]{0:T(128)S(1)} %pad_add_fusion.where, ...), custom_call_target="tpu_custom_call" | custom-call | flops 1073741824 | bytes 16777216 | tf_op jit(solution)/shard_map/pallas_call | solution.py:153
  9.0 1.3 %collective-permute-start = (bf16[64,64,128]{2,1,0:T(8,128)(2,1)S(1)}, bf16[64,64,128]{2,1,0:T(8,128)(2,1)S(1)}, u32[]{:S(2)}, u32[]{:S(2)}) collective-permute-start(bf16[64,64,128]{2,1,0:T(8,128)(2,1)S(1)} %get-tuple-element.33), channel_id=1, source_target_pairs={{0,4},{4,0},{8,12},{12,8},{16,20},{20,16},{24,28},{28,24},{1,5},{5... | collective-permute-start | bytes 3145736 | tf_op jit(solution)/shard_map/ppermute | solution.py:377
  10.3 2.0 %collective-permute-start.2 = (bf16[32,64,128]{2,1,0:T(8,128)(2,1)S(1)}, bf16[32,64,128]{2,1,0:T(8,128)(2,1)S(1)}, u32[]{:S(2)}, u32[]{:S(2)}) collective-permute-start(bf16[32,64,128]{2,1,0:T(8,128)(2,1)S(1)} %get-tuple-element.36), channel_id=1, source_target_pairs={{0,24},{4,12},{8,0},{12,20},{16,8},{20,28},{24,16},{28,4},{1,25},{... | collective-permute-start | bytes 1572872 | tf_op jit(solution)/shard_map/ppermute | solution.py:378
  12.3 0.3 collective-permute-done.other.aside
  12.6 0.2 shard_map.87
  12.8 2.1 %collective-permute-start.1 = (bf16[32,64,128]{2,1,0:T(8,128)(2,1)S(1)}, bf16[32,64,128]{2,1,0:T(8,128)(2,1)S(1)}, u32[]{:S(2)}, u32[]{:S(2)}) collective-permute-start(bf16[32,64,128]{2,1,0:T(8,128)(2,1)S(1)} %shard_map.87), channel_id=1, source_target_pairs={{0,28},{4,8},{8,4},{12,16},{16,12},{20,24},{24,20},{28,0},{1,29},{... | collective-permute-start | bytes 1572872 | tf_op jit(solution)/shard_map/ppermute | solution.py:380
  15.0 2.6 %collective-permute-start.6 = (bf16[18,64,128]{2,1,0:T(8,128)(2,1)S(1)}, bf16[18,64,128]{2,1,0:T(8,128)(2,1)S(1)}, u32[]{:S(2)}, u32[]{:S(2)}) collective-permute-start(bf16[18,64,128]{2,1,0:T(8,128)(2,1)S(1)} %get-tuple-element.45), channel_id=1, source_target_pairs={{0,2},{1,3},{2,0},{3,1},{4,6},{5,7},{6,4},{7,5},{8,10},{9,11},{10,... | collective-permute-start | bytes 884744 | tf_op jit(solution)/shard_map/ppermute | solution.py:358
  17.6 1.6 %collective-permute-start.7 = (bf16[18,64,128]{2,1,0:T(8,128)(2,1)S(1)}, bf16[18,64,128]{2,1,0:T(8,128)(2,1)S(1)}, u32[]{:S(2)}, u32[]{:S(2)}) collective-permute-start(bf16[18,64,128]{2,1,0:T(8,128)(2,1)S(1)} %get-tuple-element.46), channel_id=1, source_target_pairs={{0,1},{1,2},{2,3},{3,0},{4,5},{5,6},{6,7},{7,4},{8,9},{9,10},{10,1... | collective-permute-start | bytes 884744 | tf_op jit(solution)/shard_map/ppermute | solution.py:358
  19.1 2.3 %collective-permute-start.8 = (bf16[18,64,128]{2,1,0:T(8,128)(2,1)S(1)}, bf16[18,64,128]{2,1,0:T(8,128)(2,1)S(1)}, u32[]{:S(2)}, u32[]{:S(2)}) collective-permute-start(bf16[18,64,128]{2,1,0:T(8,128)(2,1)S(1)} %get-tuple-element.47), channel_id=1, source_target_pairs={{0,3},{1,0},{2,1},{3,2},{4,7},{5,4},{6,5},{7,6},{8,11},{9,8},{10,9... | collective-permute-start | bytes 884744 | tf_op jit(solution)/shard_map/ppermute | solution.py:358
  21.4 3.5 %collective-permute-done.2.rest_2_ = bf16[32,64,128]{2,1,0:T(8,128)(2,1)S(1)} collective-permute-done((bf16[32,64,128]{2,1,0:T(8,128)(2,1)S(1)}, bf16[32,64,128]{2,1,0:T(8,128)(2,1)S(1)}, u32[]{:S(2)}, u32[]{:S(2)}) %collective-permute-start.2) | collective-permute-done | bytes 524320 | tf_op jit(solution)/shard_map/ppermute | solution.py:378
  24.9 10.3 %collective-permute-done.1.rest_1_ = bf16[32,64,128]{2,1,0:T(8,128)(2,1)S(1)} collective-permute-done((bf16[32,64,128]{2,1,0:T(8,128)(2,1)S(1)}, bf16[32,64,128]{2,1,0:T(8,128)(2,1)S(1)}, u32[]{:S(2)}, u32[]{:S(2)}) %collective-permute-start.1) | collective-permute-done | bytes 524320 | tf_op jit(solution)/shard_map/ppermute | solution.py:380
  35.2 0.8 %shard_map.88 = (bf16[8,64,128]{2,1,0:T(8,128)(2,1)S(1)}, bf16[8,64,128]{2,1,0:T(8,128)(2,1)S(1)}, bf16[8,64,128]{2,1,0:T(8,128)(2,1)S(1)}, bf16[8,64,128]{2,1,0:T(8,128)(2,1)S(1)}) custom-call(s32[2]{0:T(128)S(1)} %pad_add_fusion.where, bf16[64,64,128]{2,1,0:T(8,128)(2,1)S(1)} %collective-permute-done.other.aside, ...), custom_call_target="tpu_custom_call" | custom-call | flops 1048576 | bytes 2621440 | tf_op jit(solution)/shard_map/pallas_call | solution.py:317
  36.1 4.3 %collective-permute-start.3 = (bf16[8,64,128]{2,1,0:T(8,128)(2,1)S(1)}, bf16[8,64,128]{2,1,0:T(8,128)(2,1)S(1)}, u32[]{:S(2)}, u32[]{:S(2)}) collective-permute-start(bf16[8,64,128]{2,1,0:T(8,128)(2,1)S(1)} %get-tuple-element.37), channel_id=1, source_target_pairs={{0,2},{1,3},{2,0},{3,1},{4,6},{5,7},{6,4},{7,5},{8,10},{9,11},{10,... | collective-permute-start | bytes 393224 | tf_op jit(solution)/shard_map/ppermute | solution.py:358
  40.4 1.6 %collective-permute-start.4 = (bf16[8,64,128]{2,1,0:T(8,128)(2,1)S(1)}, bf16[8,64,128]{2,1,0:T(8,128)(2,1)S(1)}, u32[]{:S(2)}, u32[]{:S(2)}) collective-permute-start(bf16[8,64,128]{2,1,0:T(8,128)(2,1)S(1)} %get-tuple-element.38), channel_id=1, source_target_pairs={{0,1},{1,2},{2,3},{3,0},{4,5},{5,6},{6,7},{7,4},{8,9},{9,10},{10,1... | collective-permute-start | bytes 393224 | tf_op jit(solution)/shard_map/ppermute | solution.py:358
  42.0 2.2 %collective-permute-start.5 = (bf16[8,64,128]{2,1,0:T(8,128)(2,1)S(1)}, bf16[8,64,128]{2,1,0:T(8,128)(2,1)S(1)}, u32[]{:S(2)}, u32[]{:S(2)}) collective-permute-start(bf16[8,64,128]{2,1,0:T(8,128)(2,1)S(1)} %get-tuple-element.39), channel_id=1, source_target_pairs={{0,3},{1,0},{2,1},{3,2},{4,7},{5,4},{6,5},{7,6},{8,11},{9,8},{10,9... | collective-permute-start | bytes 393224 | tf_op jit(solution)/shard_map/ppermute | solution.py:358
  44.2 1.0 %shard_map.91 = (bf16[2,64,128]{2,1,0:T(8,128)(2,1)S(1)}, bf16[2,64,128]{2,1,0:T(8,128)(2,1)S(1)}, bf16[2,64,128]{2,1,0:T(8,128)(2,1)S(1)}, bf16[2,64,128]{2,1,0:T(8,128)(2,1)S(1)}) custom-call(s32[2]{0:T(128)S(1)} %pad_add_fusion.where, bf16[18,64,128]{2,1,0:T(8,128)(2,1)S(1)} %collective-permute-done.6.rest_4_.rest_0_, ...), custom_call_target="tpu_custom_call" | custom-call | flops 134217728 | bytes 1179648 | tf_op jit(solution)/shard_map/pallas_call | solution.py:266
  45.2 0.1 collective-permute-start.12
  45.3 8.7 %collective-permute-start.13 = (bf16[2,64,128]{2,1,0:T(8,128)(2,1)S(1)}, bf16[2,64,128]{2,1,0:T(8,128)(2,1)S(1)}, u32[]{:S(2)}, u32[]{:S(2)}) collective-permute-start(bf16[2,64,128]{2,1,0:T(8,128)(2,1)S(1)} %get-tuple-element.59), channel_id=1, source_target_pairs={{0,2},{1,3},{2,0},{3,1},{4,6},{5,7},{6,4},{7,5},{8,10},{9,11},{10,... | collective-permute-start | bytes 98312 | tf_op jit(solution)/shard_map/ppermute | solution.py:358
  54.0 1.9 %collective-permute-start.14 = (bf16[2,64,128]{2,1,0:T(8,128)(2,1)S(1)}, bf16[2,64,128]{2,1,0:T(8,128)(2,1)S(1)}, u32[]{:S(2)}, u32[]{:S(2)}) collective-permute-start(bf16[2,64,128]{2,1,0:T(8,128)(2,1)S(1)} %get-tuple-element.60), channel_id=1, source_target_pairs={{0,1},{1,2},{2,3},{3,0},{4,5},{5,6},{6,7},{7,4},{8,9},{9,10},{10,1... | collective-permute-start | bytes 98312 | tf_op jit(solution)/shard_map/ppermute | solution.py:358
  56.0 1.0 %shard_map.89 = (bf16[8,64,128]{2,1,0:T(8,128)(2,1)S(1)}, bf16[8,64,128]{2,1,0:T(8,128)(2,1)S(1)}, bf16[8,64,128]{2,1,0:T(8,128)(2,1)S(1)}, bf16[8,64,128]{2,1,0:T(8,128)(2,1)S(1)}) custom-call(s32[2]{0:T(128)S(1)} %pad_add_fusion.where, bf16[8,64,128]{2,1,0:T(8,128)(2,1)S(1)} %collective-permute-done.3.rest_0_, ...), custom_call_target="tpu_custom_call" | custom-call | flops 134217728 | bytes 1048576 | tf_op jit(solution)/shard_map/pallas_call | solution.py:228
  57.0 3.3 %collective-permute-start.9 = (bf16[8,64,128]{2,1,0:T(8,128)(2,1)S(1)}, bf16[8,64,128]{2,1,0:T(8,128)(2,1)S(1)}, u32[]{:S(2)}, u32[]{:S(2)}) collective-permute-start(bf16[8,64,128]{2,1,0:T(8,128)(2,1)S(1)} %get-tuple-element.49), channel_id=1, source_target_pairs={{0,2},{1,3},{2,0},{3,1},{4,6},{5,7},{6,4},{7,5},{8,10},{9,11},{10,... | collective-permute-start | bytes 393224 | tf_op jit(solution)/shard_map/ppermute | solution.py:358
  60.3 0.1 collective-permute-start.15
  60.5 3.8 %collective-permute-start.11 = (bf16[8,64,128]{2,1,0:T(8,128)(2,1)S(1)}, bf16[8,64,128]{2,1,0:T(8,128)(2,1)S(1)}, u32[]{:S(2)}, u32[]{:S(2)}) collective-permute-start(bf16[8,64,128]{2,1,0:T(8,128)(2,1)S(1)} %get-tuple-element.51), channel_id=1, source_target_pairs={{0,3},{1,0},{2,1},{3,2},{4,7},{5,4},{6,5},{7,6},{8,11},{9,8},{10,9... | collective-permute-start | bytes 393224 | tf_op jit(solution)/shard_map/ppermute | solution.py:358
  64.3 1.7 %collective-permute-start.18 = (f32[2,64,128]{2,1,0:T(8,128)S(1)}, f32[2,64,128]{2,1,0:T(8,128)S(1)}, u32[]{:S(2)}, u32[]{:S(2)}) collective-permute-start(f32[2,64,128]{2,1,0:T(8,128)S(1)} %add.24), channel_id=1, source_target_pairs={{0,24},{4,28},{8,16},{12,20},{16,8},{20,12},{24,0},{28,4},{1,25},{... | collective-permute-start | bytes 196616 | tf_op jit(solution)/shard_map/ppermute | solution.py:395
  66.0 0.8 %collective-permute-start.17 = (f32[2,64,128]{2,1,0:T(8,128)S(1)}, f32[2,64,128]{2,1,0:T(8,128)S(1)}, u32[]{:S(2)}, u32[]{:S(2)}) collective-permute-start(f32[2,64,128]{2,1,0:T(8,128)S(1)} %add.24), channel_id=1, source_target_pairs={{0,16},{4,20},{8,24},{12,28},{16,0},{20,4},{24,8},{28,12},{1,17},{... | collective-permute-start | bytes 196616 | tf_op jit(solution)/shard_map/ppermute | solution.py:395
  66.8 2.7 %collective-permute-done.9.rest_0_ = bf16[8,64,128]{2,1,0:T(8,128)(2,1)S(1)} collective-permute-done((bf16[8,64,128]{2,1,0:T(8,128)(2,1)S(1)}, bf16[8,64,128]{2,1,0:T(8,128)(2,1)S(1)}, u32[]{:S(2)}, u32[]{:S(2)}) %collective-permute-start.9) | collective-permute-done | bytes 131104 | tf_op jit(solution)/shard_map/ppermute | solution.py:358
  69.5 1.4 %collective-permute-start.16 = (f32[2,64,128]{2,1,0:T(8,128)S(1)}, f32[2,64,128]{2,1,0:T(8,128)S(1)}, u32[]{:S(2)}, u32[]{:S(2)}) collective-permute-start(f32[2,64,128]{2,1,0:T(8,128)S(1)} %add.24), channel_id=1, source_target_pairs={{0,8},{4,12},{8,0},{12,4},{16,24},{20,28},{24,16},{28,20},{1,9},{5... | collective-permute-start | bytes 196616 | tf_op jit(solution)/shard_map/ppermute | solution.py:395
  70.9 1.0 %collective-permute-done.11.rest_2_ = bf16[8,64,128]{2,1,0:T(8,128)(2,1)S(1)} collective-permute-done((bf16[8,64,128]{2,1,0:T(8,128)(2,1)S(1)}, bf16[8,64,128]{2,1,0:T(8,128)(2,1)S(1)}, u32[]{:S(2)}, u32[]{:S(2)}) %collective-permute-start.11) | collective-permute-done | bytes 131104 | tf_op jit(solution)/shard_map/ppermute | solution.py:358
  71.8 1.4 %shard_map.90 = bf16[32,64,128]{2,1,0:T(8,128)(2,1)} custom-call(s32[2]{0:T(128)S(1)} %pad_add_fusion.where, bf16[8,64,128]{2,1,0:T(8,128)(2,1)S(1)} %collective-permute-done.9.rest_0_, bf16[8,64,128]{2,1,0:T(8,128)(2,1)S(1)} %collective-permute-done.10.rest_1_, bf16[8,64,128]{2,1,0:T(8,128)(2,1)S(1)} %collective-permute-done.11.rest_2_, ...), custom_call_target="tpu_custom_call" | custom-call | bytes 33554432 | tf_op jit(solution)/shard_map/pallas_call | solution.py:343
  73.2 0.5 collective-permute-done.16
  73.7 0.6 copy_bitcast_fusion
  (16 shorter events, 0.1 us)
Async XLA Ops:
  9.0 3.6 %collective-permute-start = (bf16[64,64,128]{2,1,0:T(8,128)(2,1)S(1)}, bf16[64,64,128]{2,1,0:T(8,128)(2,1)S(1)}, u32[]{:S(2)}, u32[]{:S(2)}) collective-permute-start(bf16[64,64,128]{2,1,0:T(8,128)(2,1)S(1)} %get-tuple-element.33), channel_id=1, source_target_pairs={{0,4},{4,0},{8,12},{12,8},{16,20},{20,16},{24,28},{28,24},{1,5},{5... | collective-permute-start | bytes 3145736 | tf_op jit(solution)/shard_map/ppermute | solution.py:377
  10.3 14.6 %collective-permute-start.2 = (bf16[32,64,128]{2,1,0:T(8,128)(2,1)S(1)}, bf16[32,64,128]{2,1,0:T(8,128)(2,1)S(1)}, u32[]{:S(2)}, u32[]{:S(2)}) collective-permute-start(bf16[32,64,128]{2,1,0:T(8,128)(2,1)S(1)} %get-tuple-element.36), channel_id=1, source_target_pairs={{0,24},{4,12},{8,0},{12,20},{16,8},{20,28},{24,16},{28,4},{1,25},{... | collective-permute-start | bytes 1572872 | tf_op jit(solution)/shard_map/ppermute | solution.py:378
  12.8 22.4 %collective-permute-start.1 = (bf16[32,64,128]{2,1,0:T(8,128)(2,1)S(1)}, bf16[32,64,128]{2,1,0:T(8,128)(2,1)S(1)}, u32[]{:S(2)}, u32[]{:S(2)}) collective-permute-start(bf16[32,64,128]{2,1,0:T(8,128)(2,1)S(1)} %shard_map.87), channel_id=1, source_target_pairs={{0,28},{4,8},{8,4},{12,16},{16,12},{20,24},{24,20},{28,0},{1,29},{... | collective-permute-start | bytes 1572872 | tf_op jit(solution)/shard_map/ppermute | solution.py:380
  15.0 27.0 %collective-permute-start.6 = (bf16[18,64,128]{2,1,0:T(8,128)(2,1)S(1)}, bf16[18,64,128]{2,1,0:T(8,128)(2,1)S(1)}, u32[]{:S(2)}, u32[]{:S(2)}) collective-permute-start(bf16[18,64,128]{2,1,0:T(8,128)(2,1)S(1)} %get-tuple-element.45), channel_id=1, source_target_pairs={{0,2},{1,3},{2,0},{3,1},{4,6},{5,7},{6,4},{7,5},{8,10},{9,11},{10,... | collective-permute-start | bytes 884744 | tf_op jit(solution)/shard_map/ppermute | solution.py:358
  17.6 26.7 %collective-permute-start.7 = (bf16[18,64,128]{2,1,0:T(8,128)(2,1)S(1)}, bf16[18,64,128]{2,1,0:T(8,128)(2,1)S(1)}, u32[]{:S(2)}, u32[]{:S(2)}) collective-permute-start(bf16[18,64,128]{2,1,0:T(8,128)(2,1)S(1)} %get-tuple-element.46), channel_id=1, source_target_pairs={{0,1},{1,2},{2,3},{3,0},{4,5},{5,6},{6,7},{7,4},{8,9},{9,10},{10,1... | collective-permute-start | bytes 884744 | tf_op jit(solution)/shard_map/ppermute | solution.py:358
  19.1 25.1 %collective-permute-start.8 = (bf16[18,64,128]{2,1,0:T(8,128)(2,1)S(1)}, bf16[18,64,128]{2,1,0:T(8,128)(2,1)S(1)}, u32[]{:S(2)}, u32[]{:S(2)}) collective-permute-start(bf16[18,64,128]{2,1,0:T(8,128)(2,1)S(1)} %get-tuple-element.47), channel_id=1, source_target_pairs={{0,3},{1,0},{2,1},{3,2},{4,7},{5,4},{6,5},{7,6},{8,11},{9,8},{10,9... | collective-permute-start | bytes 884744 | tf_op jit(solution)/shard_map/ppermute | solution.py:358
  36.1 18.0 %collective-permute-start.3 = (bf16[8,64,128]{2,1,0:T(8,128)(2,1)S(1)}, bf16[8,64,128]{2,1,0:T(8,128)(2,1)S(1)}, u32[]{:S(2)}, u32[]{:S(2)}) collective-permute-start(bf16[8,64,128]{2,1,0:T(8,128)(2,1)S(1)} %get-tuple-element.37), channel_id=1, source_target_pairs={{0,2},{1,3},{2,0},{3,1},{4,6},{5,7},{6,4},{7,5},{8,10},{9,11},{10,... | collective-permute-start | bytes 393224 | tf_op jit(solution)/shard_map/ppermute | solution.py:358
  40.4 15.6 %collective-permute-start.4 = (bf16[8,64,128]{2,1,0:T(8,128)(2,1)S(1)}, bf16[8,64,128]{2,1,0:T(8,128)(2,1)S(1)}, u32[]{:S(2)}, u32[]{:S(2)}) collective-permute-start(bf16[8,64,128]{2,1,0:T(8,128)(2,1)S(1)} %get-tuple-element.38), channel_id=1, source_target_pairs={{0,1},{1,2},{2,3},{3,0},{4,5},{5,6},{6,7},{7,4},{8,9},{9,10},{10,1... | collective-permute-start | bytes 393224 | tf_op jit(solution)/shard_map/ppermute | solution.py:358
  42.0 14.0 %collective-permute-start.5 = (bf16[8,64,128]{2,1,0:T(8,128)(2,1)S(1)}, bf16[8,64,128]{2,1,0:T(8,128)(2,1)S(1)}, u32[]{:S(2)}, u32[]{:S(2)}) collective-permute-start(bf16[8,64,128]{2,1,0:T(8,128)(2,1)S(1)} %get-tuple-element.39), channel_id=1, source_target_pairs={{0,3},{1,0},{2,1},{3,2},{4,7},{5,4},{6,5},{7,6},{8,11},{9,8},{10,9... | collective-permute-start | bytes 393224 | tf_op jit(solution)/shard_map/ppermute | solution.py:358
  45.2 15.0 %collective-permute-start.12 = (bf16[2,64,128]{2,1,0:T(8,128)(2,1)S(1)}, bf16[2,64,128]{2,1,0:T(8,128)(2,1)S(1)}, u32[]{:S(2)}, u32[]{:S(2)}) collective-permute-start(bf16[2,64,128]{2,1,0:T(8,128)(2,1)S(1)} %get-tuple-element.58), channel_id=1, source_target_pairs={{0,3},{1,0},{2,1},{3,2},{4,7},{5,4},{6,5},{7,6},{8,11},{9,8},{10,9... | collective-permute-start | bytes 98312 | tf_op jit(solution)/shard_map/ppermute | solution.py:358
  45.3 15.0 %collective-permute-start.13 = (bf16[2,64,128]{2,1,0:T(8,128)(2,1)S(1)}, bf16[2,64,128]{2,1,0:T(8,128)(2,1)S(1)}, u32[]{:S(2)}, u32[]{:S(2)}) collective-permute-start(bf16[2,64,128]{2,1,0:T(8,128)(2,1)S(1)} %get-tuple-element.59), channel_id=1, source_target_pairs={{0,2},{1,3},{2,0},{3,1},{4,6},{5,7},{6,4},{7,5},{8,10},{9,11},{10,... | collective-permute-start | bytes 98312 | tf_op jit(solution)/shard_map/ppermute | solution.py:358
  54.0 6.2 %collective-permute-start.14 = (bf16[2,64,128]{2,1,0:T(8,128)(2,1)S(1)}, bf16[2,64,128]{2,1,0:T(8,128)(2,1)S(1)}, u32[]{:S(2)}, u32[]{:S(2)}) collective-permute-start(bf16[2,64,128]{2,1,0:T(8,128)(2,1)S(1)} %get-tuple-element.60), channel_id=1, source_target_pairs={{0,1},{1,2},{2,3},{3,0},{4,5},{5,6},{6,7},{7,4},{8,9},{9,10},{10,1... | collective-permute-start | bytes 98312 | tf_op jit(solution)/shard_map/ppermute | solution.py:358
  57.0 12.5 %collective-permute-start.9 = (bf16[8,64,128]{2,1,0:T(8,128)(2,1)S(1)}, bf16[8,64,128]{2,1,0:T(8,128)(2,1)S(1)}, u32[]{:S(2)}, u32[]{:S(2)}) collective-permute-start(bf16[8,64,128]{2,1,0:T(8,128)(2,1)S(1)} %get-tuple-element.49), channel_id=1, source_target_pairs={{0,2},{1,3},{2,0},{3,1},{4,6},{5,7},{6,4},{7,5},{8,10},{9,11},{10,... | collective-permute-start | bytes 393224 | tf_op jit(solution)/shard_map/ppermute | solution.py:358
  60.3 4.0 %collective-permute-start.15 = (f32[2,64,128]{2,1,0:T(8,128)S(1)}, f32[2,64,128]{2,1,0:T(8,128)S(1)}, u32[]{:S(2)}, u32[]{:S(2)}) collective-permute-start(f32[2,64,128]{2,1,0:T(8,128)S(1)} %convert_add_fusion), channel_id=1, source_target_pairs={{0,4},{4,0},{8,12},{12,8},{16,20},{20,16},{24,28},{28,24},{1,5},{5... | collective-permute-start | bytes 196616 | tf_op jit(solution)/shard_map/ppermute | solution.py:393
  60.4 10.5 %collective-permute-start.10 = (bf16[8,64,128]{2,1,0:T(8,128)(2,1)S(1)}, bf16[8,64,128]{2,1,0:T(8,128)(2,1)S(1)}, u32[]{:S(2)}, u32[]{:S(2)}) collective-permute-start(bf16[8,64,128]{2,1,0:T(8,128)(2,1)S(1)} %get-tuple-element.50), channel_id=1, source_target_pairs={{0,1},{1,2},{2,3},{3,0},{4,5},{5,6},{6,7},{7,4},{8,9},{9,10},{10,1... | collective-permute-start | bytes 393224 | tf_op jit(solution)/shard_map/ppermute | solution.py:358
  60.5 11.4 %collective-permute-start.11 = (bf16[8,64,128]{2,1,0:T(8,128)(2,1)S(1)}, bf16[8,64,128]{2,1,0:T(8,128)(2,1)S(1)}, u32[]{:S(2)}, u32[]{:S(2)}) collective-permute-start(bf16[8,64,128]{2,1,0:T(8,128)(2,1)S(1)} %get-tuple-element.51), channel_id=1, source_target_pairs={{0,3},{1,0},{2,1},{3,2},{4,7},{5,4},{6,5},{7,6},{8,11},{9,8},{10,9... | collective-permute-start | bytes 393224 | tf_op jit(solution)/shard_map/ppermute | solution.py:358
  64.3 8.9 %collective-permute-start.18 = (f32[2,64,128]{2,1,0:T(8,128)S(1)}, f32[2,64,128]{2,1,0:T(8,128)S(1)}, u32[]{:S(2)}, u32[]{:S(2)}) collective-permute-start(f32[2,64,128]{2,1,0:T(8,128)S(1)} %add.24), channel_id=1, source_target_pairs={{0,24},{4,28},{8,16},{12,20},{16,8},{20,12},{24,0},{28,4},{1,25},{... | collective-permute-start | bytes 196616 | tf_op jit(solution)/shard_map/ppermute | solution.py:395
  66.0 7.2 %collective-permute-start.17 = (f32[2,64,128]{2,1,0:T(8,128)S(1)}, f32[2,64,128]{2,1,0:T(8,128)S(1)}, u32[]{:S(2)}, u32[]{:S(2)}) collective-permute-start(f32[2,64,128]{2,1,0:T(8,128)S(1)} %add.24), channel_id=1, source_target_pairs={{0,16},{4,20},{8,24},{12,28},{16,0},{20,4},{24,8},{28,12},{1,17},{... | collective-permute-start | bytes 196616 | tf_op jit(solution)/shard_map/ppermute | solution.py:395
  69.5 4.3 %collective-permute-start.16 = (f32[2,64,128]{2,1,0:T(8,128)S(1)}, f32[2,64,128]{2,1,0:T(8,128)S(1)}, u32[]{:S(2)}, u32[]{:S(2)}) collective-permute-start(f32[2,64,128]{2,1,0:T(8,128)S(1)} %add.24), channel_id=1, source_target_pairs={{0,8},{4,12},{8,0},{12,4},{16,24},{20,28},{24,16},{28,20},{1,9},{5... | collective-permute-start | bytes 196616 | tf_op jit(solution)/shard_map/ppermute | solution.py:395

commit v18 on v14

--- a/solution.py
+++ b/solution.py
@@ -56,13 +56,16 @@
     def groups_of(b):
         return lax.shift_right_logical(live[b] + GROUP - 1, GROUP.bit_length() - 1)
 
+    half = slots // 2
+
     def fetched(b, act):
-        groups = groups_of(b)
-        for g in range(1, per_row + 1):
-
-            @pl.when(groups == g)
-            def _(span=pl.ds(b * slots, g * GROUP)):
-                act(pltpu.make_async_copy(tiles.at[span], held.at[span], sems.at[b]))
+        span = pl.ds(b * slots, half)
+        act(pltpu.make_async_copy(tiles.at[span], held.at[span], sems.at[b, 0]))
+
+        @pl.when(live[b] > half)
+        def _():
+            span = pl.ds(b * slots + half, half)
+            act(pltpu.make_async_copy(tiles.at[span], held.at[span], sems.at[b, 1]))
 
     def list_row(b, count):
         fetched(b, lambda copy: copy.start())
@@ -164,7 +167,7 @@
             pltpu.VMEM((window + 1, features, nodes), F32),
             pltpu.SMEM((lists,), jnp.int32),
             pltpu.SMEM((lists,), jnp.int32),
-            pltpu.SemaphoreType.DMA((blocks,)),
+            pltpu.SemaphoreType.DMA((blocks, 2)),
             pltpu.SemaphoreType.DMA((2,)),
             pltpu.SemaphoreType.DMA((reps * (1 + halves),)),
         ],

time: 72.9 us -> 73 us (level)
  Pallas kernels: 11.3 us -> 13.7 us
  starting transfers between devices: 38.7 us -> 36.5 us
    pallas_call x1, Pallas kernels: 6.85 us -> 9.24 us  [contributions(): pl.pallas_call(functools.partial(tiles_kernel, slabs, reps), out_shape=[j...]
    ppermute x12, starting transfers between devices: 27 us -> 26 us  [shift(): lax.ppermute(value, 'rep', [(i, (i + steps) % reps) for i in range(reps)])]
    ppermute x1, starting transfers between devices: 5.23 us -> 4.34 us  [on_device(): two_in = lax.ppermute(two, 'blk', to_two)]
  transfers between devices with their start and end apart: 19 -> 19, of which waited for: 6 -> 5; matrix products, arithmetic and copies ran while one was open for 0% -> 0% of each run, Pallas kernels for 6% -> 6%
where the time goes in v18:
time: 73 us; the launch traced here: 72.3 us
  starting transfers between devices  36.5 us (50%)
  waiting for transfers between devices  20.7 us (28%)
  Pallas kernels  13.7 us (19%)
  other arithmetic  0.75 us (1%)
  between operations  0.75 us (1%)
    ppermute x12, starting transfers between devices, shift(): lax.ppermute(value, 'rep', [(i, (i + steps) % reps) for i in range(reps)])  26 us
    ppermute x1, waiting for transfers between devices, on_device(): one_in = lax.ppermute(one, 'blk', to_one)  10.9 us
    pallas_call x1, Pallas kernels, contributions(): pl.pallas_call(functools.partial(tiles_kernel, slabs, reps), out_shape=[j...  9.24 us
    ppermute x12, waiting for transfers between devices, shift(): lax.ppermute(value, 'rep', [(i, (i + steps) % reps) for i in range(reps)])  5.57 us
    ppermute x1, starting transfers between devices, on_device(): two_in = lax.ppermute(two, 'blk', to_two)  4.34 us
    ppermute x1, waiting for transfers between devices, on_device(): two_in = lax.ppermute(two, 'blk', to_two)  4.21 us
    ppermute x3, starting transfers between devices, on_device(): lax.ppermute(grad_w, 'blk', [(i, i ^ step) for i in range(slabs)])  3.55 us
    ppermute x1, starting transfers between devices, on_device(): one_in = lax.ppermute(one, 'blk', to_one)  2.4 us
  transfers between devices with their start and end apart: 19, of which 5 were waited for; matrix products, arithmetic and copies ran while one was open for 0% of the time, Pallas kernels for 6%

profile of v18, /device:TPU:0, one launch (start us, length us, event | category | flops | bytes accessed | tf_op | source)
XLA Modules:
  0.0 72.3 jit_solution(8011097542327309296)
XLA Ops:
  0.6 0.1 pad_add_fusion.where
  0.7 9.2 %shard_map.86 = (bf16[64,64,128]{2,1,0:T(8,128)(2,1)S(1)}, bf16[32,64,128]{2,1,0:T(8,128)(2,1)S(1)}, bf16[32,64,128]{2,1,0:T(8,128)(2,1)S(1)}, bf16[32,64,128]{2...) custom-call(s32[2]{0:T(128)S(1)} %pad_add_fusion.where, ...), custom_call_target="tpu_custom_call" | custom-call | flops 1073741824 | bytes 16777216 | tf_op jit(solution)/shard_map/pallas_call | solution.py:156
  10.0 0.1 collective-permute-start
  10.0 4.3 %collective-permute-start.2 = (bf16[32,64,128]{2,1,0:T(8,128)(2,1)S(1)}, bf16[32,64,128]{2,1,0:T(8,128)(2,1)S(1)}, u32[]{:S(2)}, u32[]{:S(2)}) collective-permute-start(bf16[32,64,128]{2,1,0:T(8,128)(2,1)S(1)} %get-tuple-element.36), channel_id=1, source_target_pairs={{0,24},{4,12},{8,0},{12,20},{16,8},{20,28},{24,16},{28,4},{1,25},{... | collective-permute-start | bytes 1572872 | tf_op jit(solution)/shard_map/ppermute | solution.py:364
  14.4 0.0 collective-permute-done.other.aside
  14.4 0.2 shard_map.87
  14.6 2.4 %collective-permute-start.1 = (bf16[32,64,128]{2,1,0:T(8,128)(2,1)S(1)}, bf16[32,64,128]{2,1,0:T(8,128)(2,1)S(1)}, u32[]{:S(2)}, u32[]{:S(2)}) collective-permute-start(bf16[32,64,128]{2,1,0:T(8,128)(2,1)S(1)} %shard_map.87), channel_id=1, source_target_pairs={{0,28},{4,8},{8,4},{12,16},{16,12},{20,24},{24,20},{28,0},{1,29},{... | collective-permute-start | bytes 1572872 | tf_op jit(solution)/shard_map/ppermute | solution.py:366
  17.0 1.6 %collective-permute-start.6 = (bf16[18,64,128]{2,1,0:T(8,128)(2,1)S(1)}, bf16[18,64,128]{2,1,0:T(8,128)(2,1)S(1)}, u32[]{:S(2)}, u32[]{:S(2)}) collective-permute-start(bf16[18,64,128]{2,1,0:T(8,128)(2,1)S(1)} %get-tuple-element.46), channel_id=1, source_target_pairs={{0,1},{1,2},{2,3},{3,0},{4,5},{5,6},{6,7},{7,4},{8,9},{9,10},{10,1... | collective-permute-start | bytes 884744 | tf_op jit(solution)/shard_map/ppermute | solution.py:348
  18.6 2.6 %collective-permute-start.7 = (bf16[18,64,128]{2,1,0:T(8,128)(2,1)S(1)}, bf16[18,64,128]{2,1,0:T(8,128)(2,1)S(1)}, u32[]{:S(2)}, u32[]{:S(2)}) collective-permute-start(bf16[18,64,128]{2,1,0:T(8,128)(2,1)S(1)} %get-tuple-element.47), channel_id=1, source_target_pairs={{0,2},{1,3},{2,0},{3,1},{4,6},{5,7},{6,4},{7,5},{8,10},{9,11},{10,... | collective-permute-start | bytes 884744 | tf_op jit(solution)/shard_map/ppermute | solution.py:348
  21.2 1.4 %collective-permute-start.8 = (bf16[18,64,128]{2,1,0:T(8,128)(2,1)S(1)}, bf16[18,64,128]{2,1,0:T(8,128)(2,1)S(1)}, u32[]{:S(2)}, u32[]{:S(2)}) collective-permute-start(bf16[18,64,128]{2,1,0:T(8,128)(2,1)S(1)} %get-tuple-element.48), channel_id=1, source_target_pairs={{0,3},{1,0},{2,1},{3,2},{4,7},{5,4},{6,5},{7,6},{8,11},{9,8},{10,9... | collective-permute-start | bytes 884744 | tf_op jit(solution)/shard_map/ppermute | solution.py:348
  22.6 4.2 %collective-permute-done.2.rest_2_ = bf16[32,64,128]{2,1,0:T(8,128)(2,1)S(1)} collective-permute-done((bf16[32,64,128]{2,1,0:T(8,128)(2,1)S(1)}, bf16[32,64,128]{2,1,0:T(8,128)(2,1)S(1)}, u32[]{:S(2)}, u32[]{:S(2)}) %collective-permute-start.2) | collective-permute-done | bytes 524320 | tf_op jit(solution)/shard_map/ppermute | solution.py:364
  26.8 10.9 %collective-permute-done.1.rest_1_ = bf16[32,64,128]{2,1,0:T(8,128)(2,1)S(1)} collective-permute-done((bf16[32,64,128]{2,1,0:T(8,128)(2,1)S(1)}, bf16[32,64,128]{2,1,0:T(8,128)(2,1)S(1)}, u32[]{:S(2)}, u32[]{:S(2)}) %collective-permute-start.1) | collective-permute-done | bytes 524320 | tf_op jit(solution)/shard_map/ppermute | solution.py:366
  37.6 0.8 %shard_map.88 = (bf16[8,64,128]{2,1,0:T(8,128)(2,1)S(1)}, bf16[8,64,128]{2,1,0:T(8,128)(2,1)S(1)}, bf16[8,64,128]{2,1,0:T(8,128)(2,1)S(1)}, bf16[8,64,128]{2,1,0:T(8,128)(2,1)S(1)}) custom-call(s32[2]{0:T(128)S(1)} %pad_add_fusion.where, bf16[64,64,128]{2,1,0:T(8,128)(2,1)S(1)} %collective-permute-done.other.aside, ...), custom_call_target="tpu_custom_call" | custom-call | flops 1048576 | bytes 2621440 | tf_op jit(solution)/shard_map/pallas_call | solution.py:307
  38.4 1.6 %collective-permute-start.3 = (bf16[8,64,128]{2,1,0:T(8,128)(2,1)S(1)}, bf16[8,64,128]{2,1,0:T(8,128)(2,1)S(1)}, u32[]{:S(2)}, u32[]{:S(2)}) collective-permute-start(bf16[8,64,128]{2,1,0:T(8,128)(2,1)S(1)} %get-tuple-element.38), channel_id=1, source_target_pairs={{0,1},{1,2},{2,3},{3,0},{4,5},{5,6},{6,7},{7,4},{8,9},{9,10},{10,1... | collective-permute-start | bytes 393224 | tf_op jit(solution)/shard_map/ppermute | solution.py:348
  40.1 2.6 %collective-permute-start.4 = (bf16[8,64,128]{2,1,0:T(8,128)(2,1)S(1)}, bf16[8,64,128]{2,1,0:T(8,128)(2,1)S(1)}, u32[]{:S(2)}, u32[]{:S(2)}) collective-permute-start(bf16[8,64,128]{2,1,0:T(8,128)(2,1)S(1)} %get-tuple-element.39), channel_id=1, source_target_pairs={{0,2},{1,3},{2,0},{3,1},{4,6},{5,7},{6,4},{7,5},{8,10},{9,11},{10,... | collective-permute-start | bytes 393224 | tf_op jit(solution)/shard_map/ppermute | solution.py:348
  42.6 1.4 %collective-permute-start.5 = (bf16[8,64,128]{2,1,0:T(8,128)(2,1)S(1)}, bf16[8,64,128]{2,1,0:T(8,128)(2,1)S(1)}, u32[]{:S(2)}, u32[]{:S(2)}) collective-permute-start(bf16[8,64,128]{2,1,0:T(8,128)(2,1)S(1)} %get-tuple-element.40), channel_id=1, source_target_pairs={{0,3},{1,0},{2,1},{3,2},{4,7},{5,4},{6,5},{7,6},{8,11},{9,8},{10,9... | collective-permute-start | bytes 393224 | tf_op jit(solution)/shard_map/ppermute | solution.py:348
  44.0 1.0 %shard_map.91 = (bf16[2,64,128]{2,1,0:T(8,128)(2,1)S(1)}, bf16[2,64,128]{2,1,0:T(8,128)(2,1)S(1)}, bf16[2,64,128]{2,1,0:T(8,128)(2,1)S(1)}, bf16[2,64,128]{2,1,0:T(8,128)(2,1)S(1)}) custom-call(s32[2]{0:T(128)S(1)} %pad_add_fusion.where, bf16[18,64,128]{2,1,0:T(8,128)(2,1)S(1)} %get-tuple-element.53.rest_4_.rest_0_, ...), custom_call_target="tpu_custom_call" | custom-call | flops 134217728 | bytes 1179648 | tf_op jit(solution)/shard_map/pallas_call | solution.py:256
  45.0 9.6 %collective-permute-start.12 = (bf16[2,64,128]{2,1,0:T(8,128)(2,1)S(1)}, bf16[2,64,128]{2,1,0:T(8,128)(2,1)S(1)}, u32[]{:S(2)}, u32[]{:S(2)}) collective-permute-start(bf16[2,64,128]{2,1,0:T(8,128)(2,1)S(1)} %get-tuple-element.58), channel_id=1, source_target_pairs={{0,3},{1,0},{2,1},{3,2},{4,7},{5,4},{6,5},{7,6},{8,11},{9,8},{10,9... | collective-permute-start | bytes 98312 | tf_op jit(solution)/shard_map/ppermute | solution.py:348
  54.6 0.6 collective-permute-start.14
  55.3 1.0 %shard_map.89 = (bf16[8,64,128]{2,1,0:T(8,128)(2,1)S(1)}, bf16[8,64,128]{2,1,0:T(8,128)(2,1)S(1)}, bf16[8,64,128]{2,1,0:T(8,128)(2,1)S(1)}, bf16[8,64,128]{2,1,0:T(8,128)(2,1)S(1)}) custom-call(s32[2]{0:T(128)S(1)} %pad_add_fusion.where, bf16[8,64,128]{2,1,0:T(8,128)(2,1)S(1)} %get-tuple-element.37.rest_0_, ...), custom_call_target="tpu_custom_call" | custom-call | flops 134217728 | bytes 1048576 | tf_op jit(solution)/shard_map/pallas_call | solution.py:219
  56.3 2.9 %collective-permute-start.9 = (bf16[8,64,128]{2,1,0:T(8,128)(2,1)S(1)}, bf16[8,64,128]{2,1,0:T(8,128)(2,1)S(1)}, u32[]{:S(2)}, u32[]{:S(2)}) collective-permute-start(bf16[8,64,128]{2,1,0:T(8,128)(2,1)S(1)} %get-tuple-element.50), channel_id=1, source_target_pairs={{0,1},{1,2},{2,3},{3,0},{4,5},{5,6},{6,7},{7,4},{8,9},{9,10},{10,1... | collective-permute-start | bytes 393224 | tf_op jit(solution)/shard_map/ppermute | solution.py:348
  59.2 1.2 %collective-permute-done.13 = bf16[2,64,128]{2,1,0:T(8,128)(2,1)S(1)} collective-permute-done((bf16[2,64,128]{2,1,0:T(8,128)(2,1)S(1)}, bf16[2,64,128]{2,1,0:T(8,128)(2,1)S(1)}, u32[]{:S(2)}, u32[]{:S(2)}) %collective-permute-start.13) | collective-permute-done | bytes 32800 | tf_op jit(solution)/shard_map/ppermute | solution.py:348
  60.4 0.1 collective-permute-start.15
  60.5 1.4 %collective-permute-start.10 = (bf16[8,64,128]{2,1,0:T(8,128)(2,1)S(1)}, bf16[8,64,128]{2,1,0:T(8,128)(2,1)S(1)}, u32[]{:S(2)}, u32[]{:S(2)}) collective-permute-start(bf16[8,64,128]{2,1,0:T(8,128)(2,1)S(1)} %get-tuple-element.51), channel_id=1, source_target_pairs={{0,2},{1,3},{2,0},{3,1},{4,6},{5,7},{6,4},{7,5},{8,10},{9,11},{10,... | collective-permute-start | bytes 393224 | tf_op jit(solution)/shard_map/ppermute | solution.py:348
  61.9 0.4 collective-permute-start.11
  62.3 1.8 %collective-permute-start.18 = (f32[2,64,128]{2,1,0:T(8,128)S(1)}, f32[2,64,128]{2,1,0:T(8,128)S(1)}, u32[]{:S(2)}, u32[]{:S(2)}) collective-permute-start(f32[2,64,128]{2,1,0:T(8,128)S(1)} %add.24), channel_id=1, source_target_pairs={{0,24},{4,28},{8,16},{12,20},{16,8},{20,12},{24,0},{28,4},{1,25},{... | collective-permute-start | bytes 196616 | tf_op jit(solution)/shard_map/ppermute | solution.py:381
  64.1 0.4 collective-permute-start.17
  64.5 1.4 %collective-permute-start.16 = (f32[2,64,128]{2,1,0:T(8,128)S(1)}, f32[2,64,128]{2,1,0:T(8,128)S(1)}, u32[]{:S(2)}, u32[]{:S(2)}) collective-permute-start(f32[2,64,128]{2,1,0:T(8,128)S(1)} %add.24), channel_id=1, source_target_pairs={{0,8},{4,12},{8,0},{12,4},{16,24},{20,28},{24,16},{28,20},{1,9},{5... | collective-permute-start | bytes 196616 | tf_op jit(solution)/shard_map/ppermute | solution.py:381
  65.9 3.2 %collective-permute-done.10.rest_2_ = bf16[8,64,128]{2,1,0:T(8,128)(2,1)S(1)} collective-permute-done((bf16[8,64,128]{2,1,0:T(8,128)(2,1)S(1)}, bf16[8,64,128]{2,1,0:T(8,128)(2,1)S(1)}, u32[]{:S(2)}, u32[]{:S(2)}) %collective-permute-start.10) | collective-permute-done | bytes 131104 | tf_op jit(solution)/shard_map/ppermute | solution.py:348
  69.1 1.2 %collective-permute-done.11.rest_3_ = bf16[8,64,128]{2,1,0:T(8,128)(2,1)S(1)} collective-permute-done((bf16[8,64,128]{2,1,0:T(8,128)(2,1)S(1)}, bf16[8,64,128]{2,1,0:T(8,128)(2,1)S(1)}, u32[]{:S(2)}, u32[]{:S(2)}) %collective-permute-start.11) | collective-permute-done | bytes 131104 | tf_op jit(solution)/shard_map/ppermute | solution.py:348
  70.2 1.4 %shard_map.90 = bf16[32,64,128]{2,1,0:T(8,128)(2,1)} custom-call(s32[2]{0:T(128)S(1)} %pad_add_fusion.where, bf16[8,64,128]{2,1,0:T(8,128)(2,1)S(1)} %get-tuple-element.49.rest_0_, bf16[8,64,128]{2,1,0:T(8,128)(2,1)S(1)} %collective-permute-done.9.rest_1_, bf16[8,64,128]{2,1,0:T(8,128)(2,1)S(1)} %collective-permute-done.10.rest_2_, ...), custom_call_target="tpu_custom_call" | custom-call | bytes 33554432 | tf_op jit(solution)/shard_map/pallas_call | solution.py:333
  71.6 0.6 copy_bitcast_fusion
  (16 shorter events, 0.1 us)
Async XLA Ops:
  10.0 4.4 %collective-permute-start = (bf16[64,64,128]{2,1,0:T(8,128)(2,1)S(1)}, bf16[64,64,128]{2,1,0:T(8,128)(2,1)S(1)}, u32[]{:S(2)}, u32[]{:S(2)}) collective-permute-start(bf16[64,64,128]{2,1,0:T(8,128)(2,1)S(1)} %get-tuple-element.33), channel_id=1, source_target_pairs={{0,4},{4,0},{8,12},{12,8},{16,20},{20,16},{24,28},{28,24},{1,5},{5... | collective-permute-start | bytes 3145736 | tf_op jit(solution)/shard_map/ppermute | solution.py:363
  10.0 16.7 %collective-permute-start.2 = (bf16[32,64,128]{2,1,0:T(8,128)(2,1)S(1)}, bf16[32,64,128]{2,1,0:T(8,128)(2,1)S(1)}, u32[]{:S(2)}, u32[]{:S(2)}) collective-permute-start(bf16[32,64,128]{2,1,0:T(8,128)(2,1)S(1)} %get-tuple-element.36), channel_id=1, source_target_pairs={{0,24},{4,12},{8,0},{12,20},{16,8},{20,28},{24,16},{28,4},{1,25},{... | collective-permute-start | bytes 1572872 | tf_op jit(solution)/shard_map/ppermute | solution.py:364
  14.6 23.0 %collective-permute-start.1 = (bf16[32,64,128]{2,1,0:T(8,128)(2,1)S(1)}, bf16[32,64,128]{2,1,0:T(8,128)(2,1)S(1)}, u32[]{:S(2)}, u32[]{:S(2)}) collective-permute-start(bf16[32,64,128]{2,1,0:T(8,128)(2,1)S(1)} %shard_map.87), channel_id=1, source_target_pairs={{0,28},{4,8},{8,4},{12,16},{16,12},{20,24},{24,20},{28,0},{1,29},{... | collective-permute-start | bytes 1572872 | tf_op jit(solution)/shard_map/ppermute | solution.py:366
  17.0 25.6 %collective-permute-start.6 = (bf16[18,64,128]{2,1,0:T(8,128)(2,1)S(1)}, bf16[18,64,128]{2,1,0:T(8,128)(2,1)S(1)}, u32[]{:S(2)}, u32[]{:S(2)}) collective-permute-start(bf16[18,64,128]{2,1,0:T(8,128)(2,1)S(1)} %get-tuple-element.46), channel_id=1, source_target_pairs={{0,1},{1,2},{2,3},{3,0},{4,5},{5,6},{6,7},{7,4},{8,9},{9,10},{10,1... | collective-permute-start | bytes 884744 | tf_op jit(solution)/shard_map/ppermute | solution.py:348
  18.6 25.4 %collective-permute-start.7 = (bf16[18,64,128]{2,1,0:T(8,128)(2,1)S(1)}, bf16[18,64,128]{2,1,0:T(8,128)(2,1)S(1)}, u32[]{:S(2)}, u32[]{:S(2)}) collective-permute-start(bf16[18,64,128]{2,1,0:T(8,128)(2,1)S(1)} %get-tuple-element.47), channel_id=1, source_target_pairs={{0,2},{1,3},{2,0},{3,1},{4,6},{5,7},{6,4},{7,5},{8,10},{9,11},{10,... | collective-permute-start | bytes 884744 | tf_op jit(solution)/shard_map/ppermute | solution.py:348
  21.2 22.8 %collective-permute-start.8 = (bf16[18,64,128]{2,1,0:T(8,128)(2,1)S(1)}, bf16[18,64,128]{2,1,0:T(8,128)(2,1)S(1)}, u32[]{:S(2)}, u32[]{:S(2)}) collective-permute-start(bf16[18,64,128]{2,1,0:T(8,128)(2,1)S(1)} %get-tuple-element.48), channel_id=1, source_target_pairs={{0,3},{1,0},{2,1},{3,2},{4,7},{5,4},{6,5},{7,6},{8,11},{9,8},{10,9... | collective-permute-start | bytes 884744 | tf_op jit(solution)/shard_map/ppermute | solution.py:348
  38.4 16.2 %collective-permute-start.3 = (bf16[8,64,128]{2,1,0:T(8,128)(2,1)S(1)}, bf16[8,64,128]{2,1,0:T(8,128)(2,1)S(1)}, u32[]{:S(2)}, u32[]{:S(2)}) collective-permute-start(bf16[8,64,128]{2,1,0:T(8,128)(2,1)S(1)} %get-tuple-element.38), channel_id=1, source_target_pairs={{0,1},{1,2},{2,3},{3,0},{4,5},{5,6},{6,7},{7,4},{8,9},{9,10},{10,1... | collective-permute-start | bytes 393224 | tf_op jit(solution)/shard_map/ppermute | solution.py:348
  40.1 15.2 %collective-permute-start.4 = (bf16[8,64,128]{2,1,0:T(8,128)(2,1)S(1)}, bf16[8,64,128]{2,1,0:T(8,128)(2,1)S(1)}, u32[]{:S(2)}, u32[]{:S(2)}) collective-permute-start(bf16[8,64,128]{2,1,0:T(8,128)(2,1)S(1)} %get-tuple-element.39), channel_id=1, source_target_pairs={{0,2},{1,3},{2,0},{3,1},{4,6},{5,7},{6,4},{7,5},{8,10},{9,11},{10,... | collective-permute-start | bytes 393224 | tf_op jit(solution)/shard_map/ppermute | solution.py:348
  42.6 12.6 %collective-permute-start.5 = (bf16[8,64,128]{2,1,0:T(8,128)(2,1)S(1)}, bf16[8,64,128]{2,1,0:T(8,128)(2,1)S(1)}, u32[]{:S(2)}, u32[]{:S(2)}) collective-permute-start(bf16[8,64,128]{2,1,0:T(8,128)(2,1)S(1)} %get-tuple-element.40), channel_id=1, source_target_pairs={{0,3},{1,0},{2,1},{3,2},{4,7},{5,4},{6,5},{7,6},{8,11},{9,8},{10,9... | collective-permute-start | bytes 393224 | tf_op jit(solution)/shard_map/ppermute | solution.py:348
  45.0 14.2 %collective-permute-start.12 = (bf16[2,64,128]{2,1,0:T(8,128)(2,1)S(1)}, bf16[2,64,128]{2,1,0:T(8,128)(2,1)S(1)}, u32[]{:S(2)}, u32[]{:S(2)}) collective-permute-start(bf16[2,64,128]{2,1,0:T(8,128)(2,1)S(1)} %get-tuple-element.58), channel_id=1, source_target_pairs={{0,3},{1,0},{2,1},{3,2},{4,7},{5,4},{6,5},{7,6},{8,11},{9,8},{10,9... | collective-permute-start | bytes 98312 | tf_op jit(solution)/shard_map/ppermute | solution.py:348
  54.6 5.8 %collective-permute-start.13 = (bf16[2,64,128]{2,1,0:T(8,128)(2,1)S(1)}, bf16[2,64,128]{2,1,0:T(8,128)(2,1)S(1)}, u32[]{:S(2)}, u32[]{:S(2)}) collective-permute-start(bf16[2,64,128]{2,1,0:T(8,128)(2,1)S(1)} %get-tuple-element.59), channel_id=1, source_target_pairs={{0,2},{1,3},{2,0},{3,1},{4,6},{5,7},{6,4},{7,5},{8,10},{9,11},{10,... | collective-permute-start | bytes 98312 | tf_op jit(solution)/shard_map/ppermute | solution.py:348
  54.6 5.8 %collective-permute-start.14 = (bf16[2,64,128]{2,1,0:T(8,128)(2,1)S(1)}, bf16[2,64,128]{2,1,0:T(8,128)(2,1)S(1)}, u32[]{:S(2)}, u32[]{:S(2)}) collective-permute-start(bf16[2,64,128]{2,1,0:T(8,128)(2,1)S(1)} %get-tuple-element.60), channel_id=1, source_target_pairs={{0,1},{1,2},{2,3},{3,0},{4,5},{5,6},{6,7},{7,4},{8,9},{9,10},{10,1... | collective-permute-start | bytes 98312 | tf_op jit(solution)/shard_map/ppermute | solution.py:348
  56.3 8.2 %collective-permute-start.9 = (bf16[8,64,128]{2,1,0:T(8,128)(2,1)S(1)}, bf16[8,64,128]{2,1,0:T(8,128)(2,1)S(1)}, u32[]{:S(2)}, u32[]{:S(2)}) collective-permute-start(bf16[8,64,128]{2,1,0:T(8,128)(2,1)S(1)} %get-tuple-element.50), channel_id=1, source_target_pairs={{0,1},{1,2},{2,3},{3,0},{4,5},{5,6},{6,7},{7,4},{8,9},{9,10},{10,1... | collective-permute-start | bytes 393224 | tf_op jit(solution)/shard_map/ppermute | solution.py:348
  60.4 1.9 %collective-permute-start.15 = (f32[2,64,128]{2,1,0:T(8,128)S(1)}, f32[2,64,128]{2,1,0:T(8,128)S(1)}, u32[]{:S(2)}, u32[]{:S(2)}) collective-permute-start(f32[2,64,128]{2,1,0:T(8,128)S(1)} %convert_add_fusion), channel_id=1, source_target_pairs={{0,4},{4,0},{8,12},{12,8},{16,20},{20,16},{24,28},{28,24},{1,5},{5... | collective-permute-start | bytes 196616 | tf_op jit(solution)/shard_map/ppermute | solution.py:379
  60.5 8.5 %collective-permute-start.10 = (bf16[8,64,128]{2,1,0:T(8,128)(2,1)S(1)}, bf16[8,64,128]{2,1,0:T(8,128)(2,1)S(1)}, u32[]{:S(2)}, u32[]{:S(2)}) collective-permute-start(bf16[8,64,128]{2,1,0:T(8,128)(2,1)S(1)} %get-tuple-element.51), channel_id=1, source_target_pairs={{0,2},{1,3},{2,0},{3,1},{4,6},{5,7},{6,4},{7,5},{8,10},{9,11},{10,... | collective-permute-start | bytes 393224 | tf_op jit(solution)/shard_map/ppermute | solution.py:348
  61.9 8.4 %collective-permute-start.11 = (bf16[8,64,128]{2,1,0:T(8,128)(2,1)S(1)}, bf16[8,64,128]{2,1,0:T(8,128)(2,1)S(1)}, u32[]{:S(2)}, u32[]{:S(2)}) collective-permute-start(bf16[8,64,128]{2,1,0:T(8,128)(2,1)S(1)} %get-tuple-element.52), channel_id=1, source_target_pairs={{0,3},{1,0},{2,1},{3,2},{4,7},{5,4},{6,5},{7,6},{8,11},{9,8},{10,9... | collective-permute-start | bytes 393224 | tf_op jit(solution)/shard_map/ppermute | solution.py:348
  62.3 9.3 %collective-permute-start.18 = (f32[2,64,128]{2,1,0:T(8,128)S(1)}, f32[2,64,128]{2,1,0:T(8,128)S(1)}, u32[]{:S(2)}, u32[]{:S(2)}) collective-permute-start(f32[2,64,128]{2,1,0:T(8,128)S(1)} %add.24), channel_id=1, source_target_pairs={{0,24},{4,28},{8,16},{12,20},{16,8},{20,12},{24,0},{28,4},{1,25},{... | collective-permute-start | bytes 196616 | tf_op jit(solution)/shard_map/ppermute | solution.py:381
  64.1 7.5 %collective-permute-start.17 = (f32[2,64,128]{2,1,0:T(8,128)S(1)}, f32[2,64,128]{2,1,0:T(8,128)S(1)}, u32[]{:S(2)}, u32[]{:S(2)}) collective-permute-start(f32[2,64,128]{2,1,0:T(8,128)S(1)} %add.24), channel_id=1, source_target_pairs={{0,16},{4,20},{8,24},{12,28},{16,0},{20,4},{24,8},{28,12},{1,17},{... | collective-permute-start | bytes 196616 | tf_op jit(solution)/shard_map/ppermute | solution.py:381
  64.5 7.2 %collective-permute-start.16 = (f32[2,64,128]{2,1,0:T(8,128)S(1)}, f32[2,64,128]{2,1,0:T(8,128)S(1)}, u32[]{:S(2)}, u32[]{:S(2)}) collective-permute-start(f32[2,64,128]{2,1,0:T(8,128)S(1)} %add.24), channel_id=1, source_target_pairs={{0,8},{4,12},{8,0},{12,4},{16,24},{20,28},{24,16},{28,20},{1,9},{5... | collective-permute-start | bytes 196616 | tf_op jit(solution)/shard_map/ppermute | solution.py:381

commit v19 on v18

--- a/solution.py
+++ b/solution.py
@@ -11,6 +11,7 @@
 REACH = 2
 GROUP = 4
 STEP = 8
+PARTS = 2
 BF16 = jnp.bfloat16
 F32 = jnp.float32
 MIB = 1 << 20
@@ -268,20 +269,25 @@
     )(where, *packed)
 
 
-def add_kernel(one, other, out):
-    def row(i, carry):
-        out[i] = (one[i].astype(F32) + other[i].astype(F32)).astype(BF16)
-        return carry
-
-    lax.fori_loop(0, out.shape[0], row, 0)
+def add_kernel(one, other, *outs):
+    for part, out in enumerate(outs):
+        base = part * out.shape[0]
+
+        def row(i, carry, out=out, base=base):
+            out[i] = (one[base + i].astype(F32) + other[base + i].astype(F32)).astype(BF16)
+            return carry
+
+        lax.fori_loop(0, out.shape[0], row, 0)
 
 
 def add(one, other):
+    blocks, features, nodes = one.shape
+    part = jax.ShapeDtypeStruct((blocks // PARTS, features, nodes), BF16)
     return pl.pallas_call(
         add_kernel,
-        out_shape=jax.ShapeDtypeStruct(one.shape, BF16),
+        out_shape=[part] * PARTS,
         in_specs=[vmem()] * 2,
-        out_specs=vmem(),
+        out_specs=[vmem()] * PARTS,
         compiler_params=pltpu.CompilerParams(vmem_limit_bytes=2 * MIB),
         cost_estimate=pl.CostEstimate(
             flops=one.size, bytes_accessed=6 * one.size, transcendentals=0
@@ -289,31 +295,38 @@
     )(one, other)
 
 
-def total_kernel(reps, where, aside, *rest):
-    terms, outs = rest[:-reps], rest[-reps:]
-    terms = (aside.at[pl.ds(terms[0].shape[0], terms[0].shape[0])], *terms)
+def total_kernel(reps, where, aside, own, two, *rest):
+    one, outs = rest[:-reps], rest[-reps:]
     share = outs[0].shape[0]
-    for s, out in enumerate(outs):
+    blocks, span = own.shape[0], one[0].shape[0]
+
+    def add_up(s, part):
         first = wrap(where[1] + s, reps) * share
         for i in range(share):
-            total = terms[0][first + i].astype(F32)
-            for term in terms[1:]:
-                total += term[first + i].astype(F32)
-            out[i] = total.astype(BF16)
-
-
-def total_shares(where, aside, terms, reps):
-    blocks, features, nodes = terms[0].shape
+            at = first + i
+            total = own[at].astype(F32) + aside[blocks + at].astype(F32)
+            total += two[at].astype(F32) + one[part][at - part * span].astype(F32)
+            outs[s][i] = total.astype(BF16)
+
+    for s in range(reps):
+        for part in range(PARTS):
+            pl.when(lax.div(wrap(where[1] + s, reps) * share, span) == part)(
+                functools.partial(add_up, s, part)
+            )
+
+
+def total_shares(where, aside, own, two, one, reps):
+    blocks, features, nodes = own.shape
     return pl.pallas_call(
         functools.partial(total_kernel, reps),
         out_shape=[jax.ShapeDtypeStruct((blocks // reps, features, nodes), BF16)] * reps,
-        in_specs=[smem()] + [vmem()] * (1 + len(terms)),
+        in_specs=[smem()] + [vmem()] * (3 + PARTS),
         out_specs=[vmem()] * reps,
         compiler_params=pltpu.CompilerParams(vmem_limit_bytes=2 * MIB),
         cost_estimate=pl.CostEstimate(
-            flops=4 * terms[0].size, bytes_accessed=10 * terms[0].size, transcendentals=0
+            flops=4 * own.size, bytes_accessed=10 * own.size, transcendentals=0
         ),
-    )(where, aside, *terms)
+    )(where, aside, own, two, *one)
 
 
 def lay_kernel(reps, where, *rest):
@@ -363,11 +376,10 @@
     aside = lax.ppermute(aside, "blk", pair)
     two_in = lax.ppermute(two, "blk", to_two)
     one = add(one, aside)
-    one_in = lax.ppermute(one, "blk", to_one)
-
-    packed, _ = lax.optimization_barrier((packed, one))
+    one_in = [lax.ppermute(part, "blk", to_one) for part in one]
+
     packed = [shift(value, s) for s, value in enumerate(packed)]
-    shares = total_shares(where, aside, [own, one_in, two_in], reps)
+    shares = total_shares(where, aside, own, two_in, one_in, reps)
     held, _ = lax.optimization_barrier((packed, shares))
     pieces = weight_partial(where, held, blocks // reps)
     pieces = [shift(value, -s) for s, value in enumerate(pieces)]

time: 73 us -> 70.4 us (0.964)
  waiting for transfers between devices: 20.7 us -> 16.4 us
  starting transfers between devices: 36.5 us -> 37.7 us
    ppermute x1 -> x2, waiting for transfers between devices: 10.9 us -> 6.82 us  [on_device(): one_in = [lax.ppermute(part, 'blk', to_one) for part in one]]
    ppermute x1, starting transfers between devices: 4.34 us -> 2.61 us  [on_device(): two_in = lax.ppermute(two, 'blk', to_two)]
    ppermute x1, starting transfers between devices: 0.07 us -> 1.38 us  [on_device(): aside = lax.ppermute(aside, 'blk', pair)]
    ppermute x12, starting transfers between devices: 26 us -> 27.3 us  [shift(): lax.ppermute(value, 'rep', [(i, (i + steps) % reps) for i in range(reps)])]
    ppermute x12, waiting for transfers between devices: 5.57 us -> 4.3 us  [shift(): lax.ppermute(value, 'rep', [(i, (i + steps) % reps) for i in range(reps)])]
    ppermute x1, waiting for transfers between devices: 4.21 us -> 5.24 us  [on_device(): two_in = lax.ppermute(two, 'blk', to_two)]
    ppermute x1 -> x2, starting transfers between devices: 2.4 us -> 2.71 us  [on_device(): one_in = [lax.ppermute(part, 'blk', to_one) for part in one]]
  transfers between devices with their start and end apart: 19 -> 20, of which waited for: 5 -> 5; matrix products, arithmetic and copies ran while one was open for 0% -> 0% of each run, Pallas kernels for 6% -> 7%
where the time goes in v19:
time: 70.4 us; the launch traced here: 69.3 us
  starting transfers between devices  37.7 us (54%)
  waiting for transfers between devices  16.4 us (23%)
  Pallas kernels  13.8 us (20%)
  other arithmetic  0.75 us (1%)
  between operations  0.74 us (1%)
    ppermute x12, starting transfers between devices, shift(): lax.ppermute(value, 'rep', [(i, (i + steps) % reps) for i in range(reps)])  27.3 us
    pallas_call x1, Pallas kernels, contributions(): pl.pallas_call(functools.partial(tiles_kernel, slabs, reps), out_shape=[j...  9.24 us
    ppermute x2, waiting for transfers between devices, on_device(): one_in = [lax.ppermute(part, 'blk', to_one) for part in one]  6.82 us
    ppermute x1, waiting for transfers between devices, on_device(): two_in = lax.ppermute(two, 'blk', to_two)  5.24 us
    ppermute x12, waiting for transfers between devices, shift(): lax.ppermute(value, 'rep', [(i, (i + steps) % reps) for i in range(reps)])  4.3 us
    ppermute x3, starting transfers between devices, on_device(): lax.ppermute(grad_w, 'blk', [(i, i ^ step) for i in range(slabs)])  3.55 us
    ppermute x2, starting transfers between devices, on_device(): one_in = [lax.ppermute(part, 'blk', to_one) for part in one]  2.71 us
    ppermute x1, starting transfers between devices, on_device(): two_in = lax.ppermute(two, 'blk', to_two)  2.61 us
  transfers between devices with their start and end apart: 20, of which 5 were waited for; matrix products, arithmetic and copies ran while one was open for 0% of the time, Pallas kernels for 7%

profile of v19, /device:TPU:0, one launch (start us, length us, event | category | flops | bytes accessed | tf_op | source)
XLA Modules:
  0.0 69.3 jit_solution(5557666295733198286)
XLA Ops:
  0.6 0.1 pad_add_fusion.where
  0.7 9.2 %shard_map.86 = (bf16[64,64,128]{2,1,0:T(8,128)(2,1)S(1)}, bf16[32,64,128]{2,1,0:T(8,128)(2,1)S(1)}, bf16[32,64,128]{2,1,0:T(8,128)(2,1)S(1)}, bf16[32,64,128]{2...) custom-call(s32[2]{0:T(128)S(1)} %pad_add_fusion.where, ...), custom_call_target="tpu_custom_call" | custom-call | flops 1073741824 | bytes 16777216 | tf_op jit(solution)/shard_map/pallas_call | solution.py:157
  10.0 1.4 %collective-permute-start = (bf16[64,64,128]{2,1,0:T(8,128)(2,1)S(1)}, bf16[64,64,128]{2,1,0:T(8,128)(2,1)S(1)}, u32[]{:S(2)}, u32[]{:S(2)}) collective-permute-start(bf16[64,64,128]{2,1,0:T(8,128)(2,1)S(1)} %get-tuple-element.31), channel_id=1, source_target_pairs={{0,4},{4,0},{8,12},{12,8},{16,20},{20,16},{24,28},{28,24},{1,5},{5... | collective-permute-start | bytes 3145736 | tf_op jit(solution)/shard_map/ppermute | solution.py:376
  11.3 2.6 %collective-permute-start.1 = (bf16[32,64,128]{2,1,0:T(8,128)(2,1)S(1)}, bf16[32,64,128]{2,1,0:T(8,128)(2,1)S(1)}, u32[]{:S(2)}, u32[]{:S(2)}) collective-permute-start(bf16[32,64,128]{2,1,0:T(8,128)(2,1)S(1)} %get-tuple-element.33), channel_id=1, source_target_pairs={{0,24},{4,12},{8,0},{12,20},{16,8},{20,28},{24,16},{28,4},{1,25},{... | collective-permute-start | bytes 1572872 | tf_op jit(solution)/shard_map/ppermute | solution.py:377
  14.0 1.6 %collective-permute-start.7 = (bf16[18,64,128]{2,1,0:T(8,128)(2,1)S(1)}, bf16[18,64,128]{2,1,0:T(8,128)(2,1)S(1)}, u32[]{:S(2)}, u32[]{:S(2)}) collective-permute-start(bf16[18,64,128]{2,1,0:T(8,128)(2,1)S(1)} %get-tuple-element.42), channel_id=1, source_target_pairs={{0,1},{1,2},{2,3},{3,0},{4,5},{5,6},{6,7},{7,4},{8,9},{9,10},{10,1... | collective-permute-start | bytes 884744 | tf_op jit(solution)/shard_map/ppermute | solution.py:361
  15.5 0.3 shard_map.87
  15.8 0.8 %collective-permute-start.2 = (bf16[16,64,128]{2,1,0:T(8,128)(2,1)S(1)}, bf16[16,64,128]{2,1,0:T(8,128)(2,1)S(1)}, u32[]{:S(2)}, u32[]{:S(2)}) collective-permute-start(bf16[16,64,128]{2,1,0:T(8,128)(2,1)S(1)} %get-tuple-element.35), channel_id=1, source_target_pairs={{0,28},{4,8},{8,4},{12,16},{16,12},{20,24},{24,20},{28,0},{1,29},{... | collective-permute-start | bytes 786440 | tf_op jit(solution)/shard_map/ppermute | solution.py:379
  16.6 1.9 %collective-permute-start.3 = (bf16[16,64,128]{2,1,0:T(8,128)(2,1)S(1)}, bf16[16,64,128]{2,1,0:T(8,128)(2,1)S(1)}, u32[]{:S(2)}, u32[]{:S(2)}) collective-permute-start(bf16[16,64,128]{2,1,0:T(8,128)(2,1)S(1)} %get-tuple-element.36), channel_id=1, source_target_pairs={{0,28},{4,8},{8,4},{12,16},{16,12},{20,24},{24,20},{28,0},{1,29},{... | collective-permute-start | bytes 786440 | tf_op jit(solution)/shard_map/ppermute | solution.py:379
  18.5 2.6 %collective-permute-start.8 = (bf16[18,64,128]{2,1,0:T(8,128)(2,1)S(1)}, bf16[18,64,128]{2,1,0:T(8,128)(2,1)S(1)}, u32[]{:S(2)}, u32[]{:S(2)}) collective-permute-start(bf16[18,64,128]{2,1,0:T(8,128)(2,1)S(1)} %get-tuple-element.43), channel_id=1, source_target_pairs={{0,2},{1,3},{2,0},{3,1},{4,6},{5,7},{6,4},{7,5},{8,10},{9,11},{10,... | collective-permute-start | bytes 884744 | tf_op jit(solution)/shard_map/ppermute | solution.py:361
  21.1 5.2 %collective-permute-done.1.two = bf16[32,64,128]{2,1,0:T(8,128)(2,1)S(1)} collective-permute-done((bf16[32,64,128]{2,1,0:T(8,128)(2,1)S(1)}, bf16[32,64,128]{2,1,0:T(8,128)(2,1)S(1)}, u32[]{:S(2)}, u32[]{:S(2)}) %collective-permute-start.1) | collective-permute-done | bytes 524320 | tf_op jit(solution)/shard_map/ppermute | solution.py:377
  26.3 4.3 %collective-permute-start.9 = (bf16[18,64,128]{2,1,0:T(8,128)(2,1)S(1)}, bf16[18,64,128]{2,1,0:T(8,128)(2,1)S(1)}, u32[]{:S(2)}, u32[]{:S(2)}) collective-permute-start(bf16[18,64,128]{2,1,0:T(8,128)(2,1)S(1)} %get-tuple-element.44), channel_id=1, source_target_pairs={{0,3},{1,0},{2,1},{3,2},{4,7},{5,4},{6,5},{7,6},{8,11},{9,8},{10,9... | collective-permute-start | bytes 884744 | tf_op jit(solution)/shard_map/ppermute | solution.py:361
  30.6 1.2 %collective-permute-done.2.rest_0_ = bf16[16,64,128]{2,1,0:T(8,128)(2,1)S(1)} collective-permute-done((bf16[16,64,128]{2,1,0:T(8,128)(2,1)S(1)}, bf16[16,64,128]{2,1,0:T(8,128)(2,1)S(1)}, u32[]{:S(2)}, u32[]{:S(2)}) %collective-permute-start.2) | collective-permute-done | bytes 262176 | tf_op jit(solution)/shard_map/ppermute | solution.py:379
  31.8 5.6 %collective-permute-done.3.rest_1_ = bf16[16,64,128]{2,1,0:T(8,128)(2,1)S(1)} collective-permute-done((bf16[16,64,128]{2,1,0:T(8,128)(2,1)S(1)}, bf16[16,64,128]{2,1,0:T(8,128)(2,1)S(1)}, u32[]{:S(2)}, u32[]{:S(2)}) %collective-permute-start.3) | collective-permute-done | bytes 262176 | tf_op jit(solution)/shard_map/ppermute | solution.py:379
  37.5 0.9 %shard_map.88 = (bf16[8,64,128]{2,1,0:T(8,128)(2,1)S(1)}, bf16[8,64,128]{2,1,0:T(8,128)(2,1)S(1)}, bf16[8,64,128]{2,1,0:T(8,128)(2,1)S(1)}, bf16[8,64,128]{2,1,0:T(8,128)(2,1)S(1)}) custom-call(s32[2]{0:T(128)S(1)} %pad_add_fusion.where, bf16[64,64,128]{2,1,0:T(8,128)(2,1)S(1)} %collective-permute-done.other.aside, ...), custom_call_target="tpu_custom_call" | custom-call | flops 1048576 | bytes 2621440 | tf_op jit(solution)/shard_map/pallas_call | solution.py:320
  38.4 2.1 %collective-permute-start.4 = (bf16[8,64,128]{2,1,0:T(8,128)(2,1)S(1)}, bf16[8,64,128]{2,1,0:T(8,128)(2,1)S(1)}, u32[]{:S(2)}, u32[]{:S(2)}) collective-permute-start(bf16[8,64,128]{2,1,0:T(8,128)(2,1)S(1)} %get-tuple-element.38), channel_id=1, source_target_pairs={{0,1},{1,2},{2,3},{3,0},{4,5},{5,6},{6,7},{7,4},{8,9},{9,10},{10,1... | collective-permute-start | bytes 393224 | tf_op jit(solution)/shard_map/ppermute | solution.py:361
  40.5 2.6 %collective-permute-start.5 = (bf16[8,64,128]{2,1,0:T(8,128)(2,1)S(1)}, bf16[8,64,128]{2,1,0:T(8,128)(2,1)S(1)}, u32[]{:S(2)}, u32[]{:S(2)}) collective-permute-start(bf16[8,64,128]{2,1,0:T(8,128)(2,1)S(1)} %get-tuple-element.39), channel_id=1, source_target_pairs={{0,2},{1,3},{2,0},{3,1},{4,6},{5,7},{6,4},{7,5},{8,10},{9,11},{10,... | collective-permute-start | bytes 393224 | tf_op jit(solution)/shard_map/ppermute | solution.py:361
  43.1 1.4 %collective-permute-start.6 = (bf16[8,64,128]{2,1,0:T(8,128)(2,1)S(1)}, bf16[8,64,128]{2,1,0:T(8,128)(2,1)S(1)}, u32[]{:S(2)}, u32[]{:S(2)}) collective-permute-start(bf16[8,64,128]{2,1,0:T(8,128)(2,1)S(1)} %get-tuple-element.40), channel_id=1, source_target_pairs={{0,3},{1,0},{2,1},{3,2},{4,7},{5,4},{6,5},{7,6},{8,11},{9,8},{10,9... | collective-permute-start | bytes 393224 | tf_op jit(solution)/shard_map/ppermute | solution.py:361
  44.5 1.0 %shard_map.91 = (bf16[2,64,128]{2,1,0:T(8,128)(2,1)S(1)}, bf16[2,64,128]{2,1,0:T(8,128)(2,1)S(1)}, bf16[2,64,128]{2,1,0:T(8,128)(2,1)S(1)}, bf16[2,64,128]{2,1,0:T(8,128)(2,1)S(1)}) custom-call(s32[2]{0:T(128)S(1)} %pad_add_fusion.where, bf16[18,64,128]{2,1,0:T(8,128)(2,1)S(1)} %get-tuple-element.49.rest_4_.rest_0_, ...), custom_call_target="tpu_custom_call" | custom-call | flops 134217728 | bytes 1179648 | tf_op jit(solution)/shard_map/pallas_call | solution.py:257
  45.5 0.5 collective-permute-start.13
  46.0 3.0 %collective-permute-start.14 = (bf16[2,64,128]{2,1,0:T(8,128)(2,1)S(1)}, bf16[2,64,128]{2,1,0:T(8,128)(2,1)S(1)}, u32[]{:S(2)}, u32[]{:S(2)}) collective-permute-start(bf16[2,64,128]{2,1,0:T(8,128)(2,1)S(1)} %get-tuple-element.55), channel_id=1, source_target_pairs={{0,2},{1,3},{2,0},{3,1},{4,6},{5,7},{6,4},{7,5},{8,10},{9,11},{10,... | collective-permute-start | bytes 98312 | tf_op jit(solution)/shard_map/ppermute | solution.py:361
  48.9 3.8 %collective-permute-start.15 = (bf16[2,64,128]{2,1,0:T(8,128)(2,1)S(1)}, bf16[2,64,128]{2,1,0:T(8,128)(2,1)S(1)}, u32[]{:S(2)}, u32[]{:S(2)}) collective-permute-start(bf16[2,64,128]{2,1,0:T(8,128)(2,1)S(1)} %get-tuple-element.56), channel_id=1, source_target_pairs={{0,1},{1,2},{2,3},{3,0},{4,5},{5,6},{6,7},{7,4},{8,9},{9,10},{10,1... | collective-permute-start | bytes 98312 | tf_op jit(solution)/shard_map/ppermute | solution.py:361
  52.8 1.0 %shard_map.89 = (bf16[8,64,128]{2,1,0:T(8,128)(2,1)S(1)}, bf16[8,64,128]{2,1,0:T(8,128)(2,1)S(1)}, bf16[8,64,128]{2,1,0:T(8,128)(2,1)S(1)}, bf16[8,64,128]{2,1,0:T(8,128)(2,1)S(1)}) custom-call(s32[2]{0:T(128)S(1)} %pad_add_fusion.where, bf16[8,64,128]{2,1,0:T(8,128)(2,1)S(1)} %get-tuple-element.37.rest_0_, ...), custom_call_target="tpu_custom_call" | custom-call | flops 134217728 | bytes 1048576 | tf_op jit(solution)/shard_map/pallas_call | solution.py:220
  53.8 2.7 %collective-permute-start.10 = (bf16[8,64,128]{2,1,0:T(8,128)(2,1)S(1)}, bf16[8,64,128]{2,1,0:T(8,128)(2,1)S(1)}, u32[]{:S(2)}, u32[]{:S(2)}) collective-permute-start(bf16[8,64,128]{2,1,0:T(8,128)(2,1)S(1)} %get-tuple-element.46), channel_id=1, source_target_pairs={{0,1},{1,2},{2,3},{3,0},{4,5},{5,6},{6,7},{7,4},{8,9},{9,10},{10,1... | collective-permute-start | bytes 393224 | tf_op jit(solution)/shard_map/ppermute | solution.py:361
  56.6 2.4 %collective-permute-start.11 = (bf16[8,64,128]{2,1,0:T(8,128)(2,1)S(1)}, bf16[8,64,128]{2,1,0:T(8,128)(2,1)S(1)}, u32[]{:S(2)}, u32[]{:S(2)}) collective-permute-start(bf16[8,64,128]{2,1,0:T(8,128)(2,1)S(1)} %get-tuple-element.47), channel_id=1, source_target_pairs={{0,2},{1,3},{2,0},{3,1},{4,6},{5,7},{6,4},{7,5},{8,10},{9,11},{10,... | collective-permute-start | bytes 393224 | tf_op jit(solution)/shard_map/ppermute | solution.py:361
  59.0 0.4 collective-permute-start.12
  59.4 1.5 %collective-permute-start.19 = (f32[2,64,128]{2,1,0:T(8,128)S(1)}, f32[2,64,128]{2,1,0:T(8,128)S(1)}, u32[]{:S(2)}, u32[]{:S(2)}) collective-permute-start(f32[2,64,128]{2,1,0:T(8,128)S(1)} %add.24), channel_id=1, source_target_pairs={{0,24},{4,28},{8,16},{12,20},{16,8},{20,12},{24,0},{28,4},{1,25},{... | collective-permute-start | bytes 196616 | tf_op jit(solution)/shard_map/ppermute | solution.py:393
  60.9 1.4 %collective-permute-start.18 = (f32[2,64,128]{2,1,0:T(8,128)S(1)}, f32[2,64,128]{2,1,0:T(8,128)S(1)}, u32[]{:S(2)}, u32[]{:S(2)}) collective-permute-start(f32[2,64,128]{2,1,0:T(8,128)S(1)} %add.24), channel_id=1, source_target_pairs={{0,16},{4,20},{8,24},{12,28},{16,0},{20,4},{24,8},{28,12},{1,17},{... | collective-permute-start | bytes 196616 | tf_op jit(solution)/shard_map/ppermute | solution.py:393
  62.3 0.7 collective-permute-start.17
  63.0 3.8 %collective-permute-done.11.rest_2_ = bf16[8,64,128]{2,1,0:T(8,128)(2,1)S(1)} collective-permute-done((bf16[8,64,128]{2,1,0:T(8,128)(2,1)S(1)}, bf16[8,64,128]{2,1,0:T(8,128)(2,1)S(1)}, u32[]{:S(2)}, u32[]{:S(2)}) %collective-permute-start.11) | collective-permute-done | bytes 131104 | tf_op jit(solution)/shard_map/ppermute | solution.py:361
  66.8 0.5 collective-permute-done.12.rest_3_
  67.3 1.4 %shard_map.90 = bf16[32,64,128]{2,1,0:T(8,128)(2,1)} custom-call(s32[2]{0:T(128)S(1)} %pad_add_fusion.where, bf16[8,64,128]{2,1,0:T(8,128)(2,1)S(1)} %get-tuple-element.45.rest_0_, bf16[8,64,128]{2,1,0:T(8,128)(2,1)S(1)} %collective-permute-done.10.rest_1_, bf16[8,64,128]{2,1,0:T(8,128)(2,1)S(1)} %collective-permute-done.11.rest_2_, ...), custom_call_target="tpu_custom_call" | custom-call | bytes 33554432 | tf_op jit(solution)/shard_map/pallas_call | solution.py:346
  68.7 0.6 copy_bitcast_fusion
  (18 shorter events, 0.1 us)
Async XLA Ops:
  10.0 5.6 %collective-permute-start = (bf16[64,64,128]{2,1,0:T(8,128)(2,1)S(1)}, bf16[64,64,128]{2,1,0:T(8,128)(2,1)S(1)}, u32[]{:S(2)}, u32[]{:S(2)}) collective-permute-start(bf16[64,64,128]{2,1,0:T(8,128)(2,1)S(1)} %get-tuple-element.31), channel_id=1, source_target_pairs={{0,4},{4,0},{8,12},{12,8},{16,20},{20,16},{24,28},{28,24},{1,5},{5... | collective-permute-start | bytes 3145736 | tf_op jit(solution)/shard_map/ppermute | solution.py:376
  11.3 15.0 %collective-permute-start.1 = (bf16[32,64,128]{2,1,0:T(8,128)(2,1)S(1)}, bf16[32,64,128]{2,1,0:T(8,128)(2,1)S(1)}, u32[]{:S(2)}, u32[]{:S(2)}) collective-permute-start(bf16[32,64,128]{2,1,0:T(8,128)(2,1)S(1)} %get-tuple-element.33), channel_id=1, source_target_pairs={{0,24},{4,12},{8,0},{12,20},{16,8},{20,28},{24,16},{28,4},{1,25},{... | collective-permute-start | bytes 1572872 | tf_op jit(solution)/shard_map/ppermute | solution.py:377
  14.0 29.1 %collective-permute-start.7 = (bf16[18,64,128]{2,1,0:T(8,128)(2,1)S(1)}, bf16[18,64,128]{2,1,0:T(8,128)(2,1)S(1)}, u32[]{:S(2)}, u32[]{:S(2)}) collective-permute-start(bf16[18,64,128]{2,1,0:T(8,128)(2,1)S(1)} %get-tuple-element.42), channel_id=1, source_target_pairs={{0,1},{1,2},{2,3},{3,0},{4,5},{5,6},{6,7},{7,4},{8,9},{9,10},{10,1... | collective-permute-start | bytes 884744 | tf_op jit(solution)/shard_map/ppermute | solution.py:361
  15.8 16.1 %collective-permute-start.2 = (bf16[16,64,128]{2,1,0:T(8,128)(2,1)S(1)}, bf16[16,64,128]{2,1,0:T(8,128)(2,1)S(1)}, u32[]{:S(2)}, u32[]{:S(2)}) collective-permute-start(bf16[16,64,128]{2,1,0:T(8,128)(2,1)S(1)} %get-tuple-element.35), channel_id=1, source_target_pairs={{0,28},{4,8},{8,4},{12,16},{16,12},{20,24},{24,20},{28,0},{1,29},{... | collective-permute-start | bytes 786440 | tf_op jit(solution)/shard_map/ppermute | solution.py:379
  16.6 20.8 %collective-permute-start.3 = (bf16[16,64,128]{2,1,0:T(8,128)(2,1)S(1)}, bf16[16,64,128]{2,1,0:T(8,128)(2,1)S(1)}, u32[]{:S(2)}, u32[]{:S(2)}) collective-permute-start(bf16[16,64,128]{2,1,0:T(8,128)(2,1)S(1)} %get-tuple-element.36), channel_id=1, source_target_pairs={{0,28},{4,8},{8,4},{12,16},{16,12},{20,24},{24,20},{28,0},{1,29},{... | collective-permute-start | bytes 786440 | tf_op jit(solution)/shard_map/ppermute | solution.py:379
  18.5 25.9 %collective-permute-start.8 = (bf16[18,64,128]{2,1,0:T(8,128)(2,1)S(1)}, bf16[18,64,128]{2,1,0:T(8,128)(2,1)S(1)}, u32[]{:S(2)}, u32[]{:S(2)}) collective-permute-start(bf16[18,64,128]{2,1,0:T(8,128)(2,1)S(1)} %get-tuple-element.43), channel_id=1, source_target_pairs={{0,2},{1,3},{2,0},{3,1},{4,6},{5,7},{6,4},{7,5},{8,10},{9,11},{10,... | collective-permute-start | bytes 884744 | tf_op jit(solution)/shard_map/ppermute | solution.py:361
  26.3 18.1 %collective-permute-start.9 = (bf16[18,64,128]{2,1,0:T(8,128)(2,1)S(1)}, bf16[18,64,128]{2,1,0:T(8,128)(2,1)S(1)}, u32[]{:S(2)}, u32[]{:S(2)}) collective-permute-start(bf16[18,64,128]{2,1,0:T(8,128)(2,1)S(1)} %get-tuple-element.44), channel_id=1, source_target_pairs={{0,3},{1,0},{2,1},{3,2},{4,7},{5,4},{6,5},{7,6},{8,11},{9,8},{10,9... | collective-permute-start | bytes 884744 | tf_op jit(solution)/shard_map/ppermute | solution.py:361
  38.4 10.6 %collective-permute-start.4 = (bf16[8,64,128]{2,1,0:T(8,128)(2,1)S(1)}, bf16[8,64,128]{2,1,0:T(8,128)(2,1)S(1)}, u32[]{:S(2)}, u32[]{:S(2)}) collective-permute-start(bf16[8,64,128]{2,1,0:T(8,128)(2,1)S(1)} %get-tuple-element.38), channel_id=1, source_target_pairs={{0,1},{1,2},{2,3},{3,0},{4,5},{5,6},{6,7},{7,4},{8,9},{9,10},{10,1... | collective-permute-start | bytes 393224 | tf_op jit(solution)/shard_map/ppermute | solution.py:361
  40.5 12.3 %collective-permute-start.5 = (bf16[8,64,128]{2,1,0:T(8,128)(2,1)S(1)}, bf16[8,64,128]{2,1,0:T(8,128)(2,1)S(1)}, u32[]{:S(2)}, u32[]{:S(2)}) collective-permute-start(bf16[8,64,128]{2,1,0:T(8,128)(2,1)S(1)} %get-tuple-element.39), channel_id=1, source_target_pairs={{0,2},{1,3},{2,0},{3,1},{4,6},{5,7},{6,4},{7,5},{8,10},{9,11},{10,... | collective-permute-start | bytes 393224 | tf_op jit(solution)/shard_map/ppermute | solution.py:361
  43.1 9.7 %collective-permute-start.6 = (bf16[8,64,128]{2,1,0:T(8,128)(2,1)S(1)}, bf16[8,64,128]{2,1,0:T(8,128)(2,1)S(1)}, u32[]{:S(2)}, u32[]{:S(2)}) collective-permute-start(bf16[8,64,128]{2,1,0:T(8,128)(2,1)S(1)} %get-tuple-element.40), channel_id=1, source_target_pairs={{0,3},{1,0},{2,1},{3,2},{4,7},{5,4},{6,5},{7,6},{8,11},{9,8},{10,9... | collective-permute-start | bytes 393224 | tf_op jit(solution)/shard_map/ppermute | solution.py:361
  45.5 11.0 %collective-permute-start.13 = (bf16[2,64,128]{2,1,0:T(8,128)(2,1)S(1)}, bf16[2,64,128]{2,1,0:T(8,128)(2,1)S(1)}, u32[]{:S(2)}, u32[]{:S(2)}) collective-permute-start(bf16[2,64,128]{2,1,0:T(8,128)(2,1)S(1)} %get-tuple-element.54), channel_id=1, source_target_pairs={{0,3},{1,0},{2,1},{3,2},{4,7},{5,4},{6,5},{7,6},{8,11},{9,8},{10,9... | collective-permute-start | bytes 98312 | tf_op jit(solution)/shard_map/ppermute | solution.py:361
  46.0 10.5 %collective-permute-start.14 = (bf16[2,64,128]{2,1,0:T(8,128)(2,1)S(1)}, bf16[2,64,128]{2,1,0:T(8,128)(2,1)S(1)}, u32[]{:S(2)}, u32[]{:S(2)}) collective-permute-start(bf16[2,64,128]{2,1,0:T(8,128)(2,1)S(1)} %get-tuple-element.55), channel_id=1, source_target_pairs={{0,2},{1,3},{2,0},{3,1},{4,6},{5,7},{6,4},{7,5},{8,10},{9,11},{10,... | collective-permute-start | bytes 98312 | tf_op jit(solution)/shard_map/ppermute | solution.py:361
  48.9 7.6 %collective-permute-start.15 = (bf16[2,64,128]{2,1,0:T(8,128)(2,1)S(1)}, bf16[2,64,128]{2,1,0:T(8,128)(2,1)S(1)}, u32[]{:S(2)}, u32[]{:S(2)}) collective-permute-start(bf16[2,64,128]{2,1,0:T(8,128)(2,1)S(1)} %get-tuple-element.56), channel_id=1, source_target_pairs={{0,1},{1,2},{2,3},{3,0},{4,5},{5,6},{6,7},{7,4},{8,9},{9,10},{10,1... | collective-permute-start | bytes 98312 | tf_op jit(solution)/shard_map/ppermute | solution.py:361
  53.8 8.5 %collective-permute-start.10 = (bf16[8,64,128]{2,1,0:T(8,128)(2,1)S(1)}, bf16[8,64,128]{2,1,0:T(8,128)(2,1)S(1)}, u32[]{:S(2)}, u32[]{:S(2)}) collective-permute-start(bf16[8,64,128]{2,1,0:T(8,128)(2,1)S(1)} %get-tuple-element.46), channel_id=1, source_target_pairs={{0,1},{1,2},{2,3},{3,0},{4,5},{5,6},{6,7},{7,4},{8,9},{9,10},{10,1... | collective-permute-start | bytes 393224 | tf_op jit(solution)/shard_map/ppermute | solution.py:361
  56.5 2.9 %collective-permute-start.16 = (f32[2,64,128]{2,1,0:T(8,128)S(1)}, f32[2,64,128]{2,1,0:T(8,128)S(1)}, u32[]{:S(2)}, u32[]{:S(2)}) collective-permute-start(f32[2,64,128]{2,1,0:T(8,128)S(1)} %convert_add_fusion), channel_id=1, source_target_pairs={{0,4},{4,0},{8,12},{12,8},{16,20},{20,16},{24,28},{28,24},{1,5},{5... | collective-permute-start | bytes 196616 | tf_op jit(solution)/shard_map/ppermute | solution.py:391
  56.6 10.1 %collective-permute-start.11 = (bf16[8,64,128]{2,1,0:T(8,128)(2,1)S(1)}, bf16[8,64,128]{2,1,0:T(8,128)(2,1)S(1)}, u32[]{:S(2)}, u32[]{:S(2)}) collective-permute-start(bf16[8,64,128]{2,1,0:T(8,128)(2,1)S(1)} %get-tuple-element.47), channel_id=1, source_target_pairs={{0,2},{1,3},{2,0},{3,1},{4,6},{5,7},{6,4},{7,5},{8,10},{9,11},{10,... | collective-permute-start | bytes 393224 | tf_op jit(solution)/shard_map/ppermute | solution.py:361
  59.0 8.3 %collective-permute-start.12 = (bf16[8,64,128]{2,1,0:T(8,128)(2,1)S(1)}, bf16[8,64,128]{2,1,0:T(8,128)(2,1)S(1)}, u32[]{:S(2)}, u32[]{:S(2)}) collective-permute-start(bf16[8,64,128]{2,1,0:T(8,128)(2,1)S(1)} %get-tuple-element.48), channel_id=1, source_target_pairs={{0,3},{1,0},{2,1},{3,2},{4,7},{5,4},{6,5},{7,6},{8,11},{9,8},{10,9... | collective-permute-start | bytes 393224 | tf_op jit(solution)/shard_map/ppermute | solution.py:361
  59.4 9.2 %collective-permute-start.19 = (f32[2,64,128]{2,1,0:T(8,128)S(1)}, f32[2,64,128]{2,1,0:T(8,128)S(1)}, u32[]{:S(2)}, u32[]{:S(2)}) collective-permute-start(f32[2,64,128]{2,1,0:T(8,128)S(1)} %add.24), channel_id=1, source_target_pairs={{0,24},{4,28},{8,16},{12,20},{16,8},{20,12},{24,0},{28,4},{1,25},{... | collective-permute-start | bytes 196616 | tf_op jit(solution)/shard_map/ppermute | solution.py:393
  60.9 7.7 %collective-permute-start.18 = (f32[2,64,128]{2,1,0:T(8,128)S(1)}, f32[2,64,128]{2,1,0:T(8,128)S(1)}, u32[]{:S(2)}, u32[]{:S(2)}) collective-permute-start(f32[2,64,128]{2,1,0:T(8,128)S(1)} %add.24), channel_id=1, source_target_pairs={{0,16},{4,20},{8,24},{12,28},{16,0},{20,4},{24,8},{28,12},{1,17},{... | collective-permute-start | bytes 196616 | tf_op jit(solution)/shard_map/ppermute | solution.py:393
  62.3 6.4 %collective-permute-start.17 = (f32[2,64,128]{2,1,0:T(8,128)S(1)}, f32[2,64,128]{2,1,0:T(8,128)S(1)}, u32[]{:S(2)}, u32[]{:S(2)}) collective-permute-start(f32[2,64,128]{2,1,0:T(8,128)S(1)} %add.24), channel_id=1, source_target_pairs={{0,8},{4,12},{8,0},{12,4},{16,24},{20,28},{24,16},{28,20},{1,9},{5... | collective-permute-start | bytes 196616 | tf_op jit(solution)/shard_map/ppermute | solution.py:393

commit v20 on v19

--- a/solution.py
+++ b/solution.py
@@ -62,11 +62,11 @@
     def fetched(b, act):
         span = pl.ds(b * slots, half)
         act(pltpu.make_async_copy(tiles.at[span], held.at[span], sems.at[b, 0]))
-
-        @pl.when(live[b] > half)
-        def _():
-            span = pl.ds(b * slots + half, half)
-            act(pltpu.make_async_copy(tiles.at[span], held.at[span], sems.at[b, 1]))
+        for i, start in enumerate(range(half, slots, GROUP)):
+
+            @pl.when(live[b] > start)
+            def _(i=i, span=pl.ds(b * slots + start, GROUP)):
+                act(pltpu.make_async_copy(tiles.at[span], held.at[span], sems.at[b, 1 + i]))
 
     def list_row(b, count):
         fetched(b, lambda copy: copy.start())
@@ -168,7 +168,7 @@
             pltpu.VMEM((window + 1, features, nodes), F32),
             pltpu.SMEM((lists,), jnp.int32),
             pltpu.SMEM((lists,), jnp.int32),
-            pltpu.SemaphoreType.DMA((blocks, 2)),
+            pltpu.SemaphoreType.DMA((blocks, 1 + slots // 2 // GROUP)),
             pltpu.SemaphoreType.DMA((2,)),
             pltpu.SemaphoreType.DMA((reps * (1 + halves),)),
         ],
@@ -384,6 +384,7 @@
     pieces = weight_partial(where, held, blocks // reps)
     pieces = [shift(value, -s) for s, value in enumerate(pieces)]
     shares = [shift(value, s) for s, value in enumerate(shares)]
+    shares, _ = lax.optimization_barrier((shares, pieces[1:]))
     outs = [shift(value, s) for s, value in enumerate(mix(where, shares, packed))]
     input_grad = lay_blocks(where, outs, cotangent.shape)
 

time: 70.4 us -> 74.7 us (1.061)
  waiting for transfers between devices: 16.4 us -> 23.3 us
  starting transfers between devices: 37.7 us -> 34.6 us
  Pallas kernels: 13.8 us -> 14.6 us
    ppermute x12, waiting for transfers between devices: 4.3 us -> 10.9 us  [shift(): lax.ppermute(value, 'rep', [(i, (i + steps) % reps) for i in range(reps)])]
    ppermute x1, starting transfers between devices: 1.38 us -> 0.07 us  [on_device(): aside = lax.ppermute(aside, 'blk', pair)]
    ppermute x1, waiting for transfers between devices: 5.24 us -> 6.55 us  [on_device(): two_in = lax.ppermute(two, 'blk', to_two)]
    ppermute x1, starting transfers between devices: 2.61 us -> 1.37 us  [on_device(): two_in = lax.ppermute(two, 'blk', to_two)]
    ppermute x2, waiting for transfers between devices: 6.82 us -> 5.86 us  [on_device(): one_in = [lax.ppermute(part, 'blk', to_one) for part in one]]
    pallas_call x1, Pallas kernels: 9.24 us -> 10.1 us  [contributions(): pl.pallas_call(functools.partial(tiles_kernel, slabs, reps), out_shape=[j...]
  transfers between devices with their start and end apart: 20 -> 20, of which waited for: 5 -> 8; matrix products, arithmetic and copies ran while one was open for 0% -> 0% of each run, Pallas kernels for 7% -> 5%
where the time goes in v20:
time: 74.7 us; the launch traced here: 74.1 us
  starting transfers between devices  34.6 us (46%)
  waiting for transfers between devices  23.3 us (31%)
  Pallas kernels  14.6 us (20%)
  other arithmetic  0.75 us (1%)
  between operations  0.75 us (1%)
    ppermute x12, starting transfers between devices, shift(): lax.ppermute(value, 'rep', [(i, (i + steps) % reps) for i in range(reps)])  27.2 us
    ppermute x12, waiting for transfers between devices, shift(): lax.ppermute(value, 'rep', [(i, (i + steps) % reps) for i in range(reps)])  10.9 us
    pallas_call x1, Pallas kernels, contributions(): pl.pallas_call(functools.partial(tiles_kernel, slabs, reps), out_shape=[j...  10.1 us
    ppermute x1, waiting for transfers between devices, on_device(): two_in = lax.ppermute(two, 'blk', to_two)  6.55 us
    ppermute x2, waiting for transfers between devices, on_device(): one_in = [lax.ppermute(part, 'blk', to_one) for part in one]  5.86 us
    ppermute x3, starting transfers between devices, on_device(): lax.ppermute(grad_w, 'blk', [(i, i ^ step) for i in range(slabs)])  3.2 us
    ppermute x2, starting transfers between devices, on_device(): one_in = [lax.ppermute(part, 'blk', to_one) for part in one]  2.71 us
  transfers between devices with their start and end apart: 20, of which 8 were waited for; matrix products, arithmetic and copies ran while one was open for 0% of the time, Pallas kernels for 5%

profile of v20, /device:TPU:0, one launch (start us, length us, event | category | flops | bytes accessed | tf_op | source)
XLA Modules:
  0.0 74.1 jit_solution(9922010625176580866)
XLA Ops:
  0.7 10.1 %shard_map.86 = (bf16[64,64,128]{2,1,0:T(8,128)(2,1)S(1)}, bf16[32,64,128]{2,1,0:T(8,128)(2,1)S(1)}, bf16[32,64,128]{2,1,0:T(8,128)(2,1)S(1)}, bf16[32,64,128]{2...) custom-call(s32[2]{0:T(128)S(1)} %pad_add_fusion.where, ...), custom_call_target="tpu_custom_call" | custom-call | flops 1073741824 | bytes 16777216 | tf_op jit(solution)/shard_map/pallas_call | solution.py:157
  10.9 1.4 %collective-permute-start.1 = (bf16[32,64,128]{2,1,0:T(8,128)(2,1)S(1)}, bf16[32,64,128]{2,1,0:T(8,128)(2,1)S(1)}, u32[]{:S(2)}, u32[]{:S(2)}) collective-permute-start(bf16[32,64,128]{2,1,0:T(8,128)(2,1)S(1)} %get-tuple-element.37), channel_id=1, source_target_pairs={{0,24},{4,12},{8,0},{12,20},{16,8},{20,28},{24,16},{28,4},{1,25},{... | collective-permute-start | bytes 1572872 | tf_op jit(solution)/shard_map/ppermute | solution.py:377
  12.2 1.8 %collective-permute-start.7 = (bf16[18,64,128]{2,1,0:T(8,128)(2,1)S(1)}, bf16[18,64,128]{2,1,0:T(8,128)(2,1)S(1)}, u32[]{:S(2)}, u32[]{:S(2)}) collective-permute-start(bf16[18,64,128]{2,1,0:T(8,128)(2,1)S(1)} %get-tuple-element.46), channel_id=1, source_target_pairs={{0,1},{1,2},{2,3},{3,0},{4,5},{5,6},{6,7},{7,4},{8,9},{9,10},{10,1... | collective-permute-start | bytes 884744 | tf_op jit(solution)/shard_map/ppermute | solution.py:361
  14.0 0.3 shard_map.87
  14.3 2.4 %collective-permute-start.2 = (bf16[16,64,128]{2,1,0:T(8,128)(2,1)S(1)}, bf16[16,64,128]{2,1,0:T(8,128)(2,1)S(1)}, u32[]{:S(2)}, u32[]{:S(2)}) collective-permute-start(bf16[16,64,128]{2,1,0:T(8,128)(2,1)S(1)} %get-tuple-element.39), channel_id=1, source_target_pairs={{0,28},{4,8},{8,4},{12,16},{16,12},{20,24},{24,20},{28,0},{1,29},{... | collective-permute-start | bytes 786440 | tf_op jit(solution)/shard_map/ppermute | solution.py:379
  16.7 0.3 collective-permute-start.3
  17.0 3.5 %collective-permute-start.8 = (bf16[18,64,128]{2,1,0:T(8,128)(2,1)S(1)}, bf16[18,64,128]{2,1,0:T(8,128)(2,1)S(1)}, u32[]{:S(2)}, u32[]{:S(2)}) collective-permute-start(bf16[18,64,128]{2,1,0:T(8,128)(2,1)S(1)} %get-tuple-element.47), channel_id=1, source_target_pairs={{0,2},{1,3},{2,0},{3,1},{4,6},{5,7},{6,4},{7,5},{8,10},{9,11},{10,... | collective-permute-start | bytes 884744 | tf_op jit(solution)/shard_map/ppermute | solution.py:361
  20.5 6.5 %collective-permute-done.1.two = bf16[32,64,128]{2,1,0:T(8,128)(2,1)S(1)} collective-permute-done((bf16[32,64,128]{2,1,0:T(8,128)(2,1)S(1)}, bf16[32,64,128]{2,1,0:T(8,128)(2,1)S(1)}, u32[]{:S(2)}, u32[]{:S(2)}) %collective-permute-start.1) | collective-permute-done | bytes 524320 | tf_op jit(solution)/shard_map/ppermute | solution.py:377
  27.1 3.7 %collective-permute-start.9 = (bf16[18,64,128]{2,1,0:T(8,128)(2,1)S(1)}, bf16[18,64,128]{2,1,0:T(8,128)(2,1)S(1)}, u32[]{:S(2)}, u32[]{:S(2)}) collective-permute-start(bf16[18,64,128]{2,1,0:T(8,128)(2,1)S(1)} %get-tuple-element.48), channel_id=1, source_target_pairs={{0,3},{1,0},{2,1},{3,2},{4,7},{5,4},{6,5},{7,6},{8,11},{9,8},{10,9... | collective-permute-start | bytes 884744 | tf_op jit(solution)/shard_map/ppermute | solution.py:361
  30.8 0.2 collective-permute-done.2.rest_0_
  31.0 5.6 %collective-permute-done.3.rest_1_ = bf16[16,64,128]{2,1,0:T(8,128)(2,1)S(1)} collective-permute-done((bf16[16,64,128]{2,1,0:T(8,128)(2,1)S(1)}, bf16[16,64,128]{2,1,0:T(8,128)(2,1)S(1)}, u32[]{:S(2)}, u32[]{:S(2)}) %collective-permute-start.3) | collective-permute-done | bytes 262176 | tf_op jit(solution)/shard_map/ppermute | solution.py:379
  36.6 0.9 %shard_map.88 = (bf16[8,64,128]{2,1,0:T(8,128)(2,1)S(1)}, bf16[8,64,128]{2,1,0:T(8,128)(2,1)S(1)}, bf16[8,64,128]{2,1,0:T(8,128)(2,1)S(1)}, bf16[8,64,128]{2,1,0:T(8,128)(2,1)S(1)}) custom-call(s32[2]{0:T(128)S(1)} %pad_add_fusion.where, bf16[64,64,128]{2,1,0:T(8,128)(2,1)S(1)} %collective-permute-done.other.aside, ...), custom_call_target="tpu_custom_call" | custom-call | flops 1048576 | bytes 2621440 | tf_op jit(solution)/shard_map/pallas_call | solution.py:320
  37.5 3.1 %collective-permute-start.4 = (bf16[8,64,128]{2,1,0:T(8,128)(2,1)S(1)}, bf16[8,64,128]{2,1,0:T(8,128)(2,1)S(1)}, u32[]{:S(2)}, u32[]{:S(2)}) collective-permute-start(bf16[8,64,128]{2,1,0:T(8,128)(2,1)S(1)} %get-tuple-element.42), channel_id=1, source_target_pairs={{0,1},{1,2},{2,3},{3,0},{4,5},{5,6},{6,7},{7,4},{8,9},{9,10},{10,1... | collective-permute-start | bytes 393224 | tf_op jit(solution)/shard_map/ppermute | solution.py:361
  40.6 2.6 %collective-permute-start.5 = (bf16[8,64,128]{2,1,0:T(8,128)(2,1)S(1)}, bf16[8,64,128]{2,1,0:T(8,128)(2,1)S(1)}, u32[]{:S(2)}, u32[]{:S(2)}) collective-permute-start(bf16[8,64,128]{2,1,0:T(8,128)(2,1)S(1)} %get-tuple-element.43), channel_id=1, source_target_pairs={{0,2},{1,3},{2,0},{3,1},{4,6},{5,7},{6,4},{7,5},{8,10},{9,11},{10,... | collective-permute-start | bytes 393224 | tf_op jit(solution)/shard_map/ppermute | solution.py:361
  43.2 1.3 %collective-permute-start.6 = (bf16[8,64,128]{2,1,0:T(8,128)(2,1)S(1)}, bf16[8,64,128]{2,1,0:T(8,128)(2,1)S(1)}, u32[]{:S(2)}, u32[]{:S(2)}) collective-permute-start(bf16[8,64,128]{2,1,0:T(8,128)(2,1)S(1)} %get-tuple-element.44), channel_id=1, source_target_pairs={{0,3},{1,0},{2,1},{3,2},{4,7},{5,4},{6,5},{7,6},{8,11},{9,8},{10,9... | collective-permute-start | bytes 393224 | tf_op jit(solution)/shard_map/ppermute | solution.py:361
  44.6 1.0 %shard_map.89 = (bf16[2,64,128]{2,1,0:T(8,128)(2,1)S(1)}, bf16[2,64,128]{2,1,0:T(8,128)(2,1)S(1)}, bf16[2,64,128]{2,1,0:T(8,128)(2,1)S(1)}, bf16[2,64,128]{2,1,0:T(8,128)(2,1)S(1)}) custom-call(s32[2]{0:T(128)S(1)} %pad_add_fusion.where, bf16[18,64,128]{2,1,0:T(8,128)(2,1)S(1)} %get-tuple-element.49.rest_0_.rest_4_, ...), custom_call_target="tpu_custom_call" | custom-call | flops 134217728 | bytes 1179648 | tf_op jit(solution)/shard_map/pallas_call | solution.py:257
  45.6 0.5 collective-permute-start.10
  46.1 1.7 %collective-permute-start.11 = (bf16[2,64,128]{2,1,0:T(8,128)(2,1)S(1)}, bf16[2,64,128]{2,1,0:T(8,128)(2,1)S(1)}, u32[]{:S(2)}, u32[]{:S(2)}) collective-permute-start(bf16[2,64,128]{2,1,0:T(8,128)(2,1)S(1)} %get-tuple-element.54), channel_id=1, source_target_pairs={{0,2},{1,3},{2,0},{3,1},{4,6},{5,7},{6,4},{7,5},{8,10},{9,11},{10,... | collective-permute-start | bytes 98312 | tf_op jit(solution)/shard_map/ppermute | solution.py:361
  47.8 5.0 %collective-permute-done.10 = bf16[2,64,128]{2,1,0:T(8,128)(2,1)S(1)} collective-permute-done((bf16[2,64,128]{2,1,0:T(8,128)(2,1)S(1)}, bf16[2,64,128]{2,1,0:T(8,128)(2,1)S(1)}, u32[]{:S(2)}, u32[]{:S(2)}) %collective-permute-start.10) | collective-permute-done | bytes 32800 | tf_op jit(solution)/shard_map/ppermute | solution.py:361
  52.7 4.2 %collective-permute-start.12 = (bf16[2,64,128]{2,1,0:T(8,128)(2,1)S(1)}, bf16[2,64,128]{2,1,0:T(8,128)(2,1)S(1)}, u32[]{:S(2)}, u32[]{:S(2)}) collective-permute-start(bf16[2,64,128]{2,1,0:T(8,128)(2,1)S(1)} %get-tuple-element.55), channel_id=1, source_target_pairs={{0,1},{1,2},{2,3},{3,0},{4,5},{5,6},{6,7},{7,4},{8,9},{9,10},{10,1... | collective-permute-start | bytes 98312 | tf_op jit(solution)/shard_map/ppermute | solution.py:361
  56.9 0.4 collective-permute-done.11
  57.3 1.2 %collective-permute-done.12 = bf16[2,64,128]{2,1,0:T(8,128)(2,1)S(1)} collective-permute-done((bf16[2,64,128]{2,1,0:T(8,128)(2,1)S(1)}, bf16[2,64,128]{2,1,0:T(8,128)(2,1)S(1)}, u32[]{:S(2)}, u32[]{:S(2)}) %collective-permute-start.12) | collective-permute-done | bytes 32800 | tf_op jit(solution)/shard_map/ppermute | solution.py:361
  58.5 1.0 %shard_map.90 = (bf16[8,64,128]{2,1,0:T(8,128)(2,1)S(1)}, bf16[8,64,128]{2,1,0:T(8,128)(2,1)S(1)}, bf16[8,64,128]{2,1,0:T(8,128)(2,1)S(1)}, bf16[8,64,128]{2,1,0:T(8,128)(2,1)S(1)}) custom-call(s32[2]{0:T(128)S(1)} %pad_add_fusion.where, bf16[8,64,128]{2,1,0:T(8,128)(2,1)S(1)} %get-tuple-element.56.rest_0_, ...), custom_call_target="tpu_custom_call" | custom-call | flops 134217728 | bytes 1048576 | tf_op jit(solution)/shard_map/pallas_call | solution.py:220
  59.6 2.4 %collective-permute-start.13 = (bf16[8,64,128]{2,1,0:T(8,128)(2,1)S(1)}, bf16[8,64,128]{2,1,0:T(8,128)(2,1)S(1)}, u32[]{:S(2)}, u32[]{:S(2)}) collective-permute-start(bf16[8,64,128]{2,1,0:T(8,128)(2,1)S(1)} %get-tuple-element.61), channel_id=1, source_target_pairs={{0,1},{1,2},{2,3},{3,0},{4,5},{5,6},{6,7},{7,4},{8,9},{9,10},{10,1... | collective-permute-start | bytes 393224 | tf_op jit(solution)/shard_map/ppermute | solution.py:361
  62.1 2.4 %collective-permute-start.15 = (bf16[8,64,128]{2,1,0:T(8,128)(2,1)S(1)}, bf16[8,64,128]{2,1,0:T(8,128)(2,1)S(1)}, u32[]{:S(2)}, u32[]{:S(2)}) collective-permute-start(bf16[8,64,128]{2,1,0:T(8,128)(2,1)S(1)} %get-tuple-element.63), channel_id=1, source_target_pairs={{0,3},{1,0},{2,1},{3,2},{4,7},{5,4},{6,5},{7,6},{8,11},{9,8},{10,9... | collective-permute-start | bytes 393224 | tf_op jit(solution)/shard_map/ppermute | solution.py:361
  64.5 1.0 %collective-permute-start.19 = (f32[2,64,128]{2,1,0:T(8,128)S(1)}, f32[2,64,128]{2,1,0:T(8,128)S(1)}, u32[]{:S(2)}, u32[]{:S(2)}) collective-permute-start(f32[2,64,128]{2,1,0:T(8,128)S(1)} %add.24), channel_id=1, source_target_pairs={{0,24},{4,28},{8,16},{12,20},{16,8},{20,12},{24,0},{28,4},{1,25},{... | collective-permute-start | bytes 196616 | tf_op jit(solution)/shard_map/ppermute | solution.py:394
  65.5 1.3 %collective-permute-start.18 = (f32[2,64,128]{2,1,0:T(8,128)S(1)}, f32[2,64,128]{2,1,0:T(8,128)S(1)}, u32[]{:S(2)}, u32[]{:S(2)}) collective-permute-start(f32[2,64,128]{2,1,0:T(8,128)S(1)} %add.24), channel_id=1, source_target_pairs={{0,16},{4,20},{8,24},{12,28},{16,0},{20,4},{24,8},{28,12},{1,17},{... | collective-permute-start | bytes 196616 | tf_op jit(solution)/shard_map/ppermute | solution.py:394
  66.8 0.6 collective-permute-done.13.rest_1_
  67.4 0.9 %collective-permute-start.17 = (f32[2,64,128]{2,1,0:T(8,128)S(1)}, f32[2,64,128]{2,1,0:T(8,128)S(1)}, u32[]{:S(2)}, u32[]{:S(2)}) collective-permute-start(f32[2,64,128]{2,1,0:T(8,128)S(1)} %add.24), channel_id=1, source_target_pairs={{0,8},{4,12},{8,0},{12,4},{16,24},{20,28},{24,16},{28,20},{1,9},{5... | collective-permute-start | bytes 196616 | tf_op jit(solution)/shard_map/ppermute | solution.py:394
  68.3 3.7 %collective-permute-done.14.rest_2_ = bf16[8,64,128]{2,1,0:T(8,128)(2,1)S(1)} collective-permute-done((bf16[8,64,128]{2,1,0:T(8,128)(2,1)S(1)}, bf16[8,64,128]{2,1,0:T(8,128)(2,1)S(1)}, u32[]{:S(2)}, u32[]{:S(2)}) %collective-permute-start.14) | collective-permute-done | bytes 131104 | tf_op jit(solution)/shard_map/ppermute | solution.py:361
  72.0 1.4 %shard_map.91 = bf16[32,64,128]{2,1,0:T(8,128)(2,1)} custom-call(s32[2]{0:T(128)S(1)} %pad_add_fusion.where, bf16[8,64,128]{2,1,0:T(8,128)(2,1)S(1)} %get-tuple-element.60.rest_0_, bf16[8,64,128]{2,1,0:T(8,128)(2,1)S(1)} %collective-permute-done.13.rest_1_, bf16[8,64,128]{2,1,0:T(8,128)(2,1)S(1)} %collective-permute-done.14.rest_2_, ...), custom_call_target="tpu_custom_call" | custom-call | bytes 33554432 | tf_op jit(solution)/shard_map/pallas_call | solution.py:346
  73.4 0.6 copy_bitcast_fusion
  (18 shorter events, 0.3 us)
Async XLA Ops:
  10.8 3.2 %collective-permute-start = (bf16[64,64,128]{2,1,0:T(8,128)(2,1)S(1)}, bf16[64,64,128]{2,1,0:T(8,128)(2,1)S(1)}, u32[]{:S(2)}, u32[]{:S(2)}) collective-permute-start(bf16[64,64,128]{2,1,0:T(8,128)(2,1)S(1)} %get-tuple-element.35), channel_id=1, source_target_pairs={{0,4},{4,0},{8,12},{12,8},{16,20},{20,16},{24,28},{28,24},{1,5},{5... | collective-permute-start | bytes 3145736 | tf_op jit(solution)/shard_map/ppermute | solution.py:376
  10.9 16.2 %collective-permute-start.1 = (bf16[32,64,128]{2,1,0:T(8,128)(2,1)S(1)}, bf16[32,64,128]{2,1,0:T(8,128)(2,1)S(1)}, u32[]{:S(2)}, u32[]{:S(2)}) collective-permute-start(bf16[32,64,128]{2,1,0:T(8,128)(2,1)S(1)} %get-tuple-element.37), channel_id=1, source_target_pairs={{0,24},{4,12},{8,0},{12,20},{16,8},{20,28},{24,16},{28,4},{1,25},{... | collective-permute-start | bytes 1572872 | tf_op jit(solution)/shard_map/ppermute | solution.py:377
  12.2 31.0 %collective-permute-start.7 = (bf16[18,64,128]{2,1,0:T(8,128)(2,1)S(1)}, bf16[18,64,128]{2,1,0:T(8,128)(2,1)S(1)}, u32[]{:S(2)}, u32[]{:S(2)}) collective-permute-start(bf16[18,64,128]{2,1,0:T(8,128)(2,1)S(1)} %get-tuple-element.46), channel_id=1, source_target_pairs={{0,1},{1,2},{2,3},{3,0},{4,5},{5,6},{6,7},{7,4},{8,9},{9,10},{10,1... | collective-permute-start | bytes 884744 | tf_op jit(solution)/shard_map/ppermute | solution.py:361
  14.3 16.7 %collective-permute-start.2 = (bf16[16,64,128]{2,1,0:T(8,128)(2,1)S(1)}, bf16[16,64,128]{2,1,0:T(8,128)(2,1)S(1)}, u32[]{:S(2)}, u32[]{:S(2)}) collective-permute-start(bf16[16,64,128]{2,1,0:T(8,128)(2,1)S(1)} %get-tuple-element.39), channel_id=1, source_target_pairs={{0,28},{4,8},{8,4},{12,16},{16,12},{20,24},{24,20},{28,0},{1,29},{... | collective-permute-start | bytes 786440 | tf_op jit(solution)/shard_map/ppermute | solution.py:379
  16.7 19.9 %collective-permute-start.3 = (bf16[16,64,128]{2,1,0:T(8,128)(2,1)S(1)}, bf16[16,64,128]{2,1,0:T(8,128)(2,1)S(1)}, u32[]{:S(2)}, u32[]{:S(2)}) collective-permute-start(bf16[16,64,128]{2,1,0:T(8,128)(2,1)S(1)} %get-tuple-element.40), channel_id=1, source_target_pairs={{0,28},{4,8},{8,4},{12,16},{16,12},{20,24},{24,20},{28,0},{1,29},{... | collective-permute-start | bytes 786440 | tf_op jit(solution)/shard_map/ppermute | solution.py:379
  17.0 27.6 %collective-permute-start.8 = (bf16[18,64,128]{2,1,0:T(8,128)(2,1)S(1)}, bf16[18,64,128]{2,1,0:T(8,128)(2,1)S(1)}, u32[]{:S(2)}, u32[]{:S(2)}) collective-permute-start(bf16[18,64,128]{2,1,0:T(8,128)(2,1)S(1)} %get-tuple-element.47), channel_id=1, source_target_pairs={{0,2},{1,3},{2,0},{3,1},{4,6},{5,7},{6,4},{7,5},{8,10},{9,11},{10,... | collective-permute-start | bytes 884744 | tf_op jit(solution)/shard_map/ppermute | solution.py:361
  27.1 17.5 %collective-permute-start.9 = (bf16[18,64,128]{2,1,0:T(8,128)(2,1)S(1)}, bf16[18,64,128]{2,1,0:T(8,128)(2,1)S(1)}, u32[]{:S(2)}, u32[]{:S(2)}) collective-permute-start(bf16[18,64,128]{2,1,0:T(8,128)(2,1)S(1)} %get-tuple-element.48), channel_id=1, source_target_pairs={{0,3},{1,0},{2,1},{3,2},{4,7},{5,4},{6,5},{7,6},{8,11},{9,8},{10,9... | collective-permute-start | bytes 884744 | tf_op jit(solution)/shard_map/ppermute | solution.py:361
  37.5 21.0 %collective-permute-start.4 = (bf16[8,64,128]{2,1,0:T(8,128)(2,1)S(1)}, bf16[8,64,128]{2,1,0:T(8,128)(2,1)S(1)}, u32[]{:S(2)}, u32[]{:S(2)}) collective-permute-start(bf16[8,64,128]{2,1,0:T(8,128)(2,1)S(1)} %get-tuple-element.42), channel_id=1, source_target_pairs={{0,1},{1,2},{2,3},{3,0},{4,5},{5,6},{6,7},{7,4},{8,9},{9,10},{10,1... | collective-permute-start | bytes 393224 | tf_op jit(solution)/shard_map/ppermute | solution.py:361
  40.6 17.9 %collective-permute-start.5 = (bf16[8,64,128]{2,1,0:T(8,128)(2,1)S(1)}, bf16[8,64,128]{2,1,0:T(8,128)(2,1)S(1)}, u32[]{:S(2)}, u32[]{:S(2)}) collective-permute-start(bf16[8,64,128]{2,1,0:T(8,128)(2,1)S(1)} %get-tuple-element.43), channel_id=1, source_target_pairs={{0,2},{1,3},{2,0},{3,1},{4,6},{5,7},{6,4},{7,5},{8,10},{9,11},{10,... | collective-permute-start | bytes 393224 | tf_op jit(solution)/shard_map/ppermute | solution.py:361
  43.2 15.3 %collective-permute-start.6 = (bf16[8,64,128]{2,1,0:T(8,128)(2,1)S(1)}, bf16[8,64,128]{2,1,0:T(8,128)(2,1)S(1)}, u32[]{:S(2)}, u32[]{:S(2)}) collective-permute-start(bf16[8,64,128]{2,1,0:T(8,128)(2,1)S(1)} %get-tuple-element.44), channel_id=1, source_target_pairs={{0,3},{1,0},{2,1},{3,2},{4,7},{5,4},{6,5},{7,6},{8,11},{9,8},{10,9... | collective-permute-start | bytes 393224 | tf_op jit(solution)/shard_map/ppermute | solution.py:361
  45.6 7.1 %collective-permute-start.10 = (bf16[2,64,128]{2,1,0:T(8,128)(2,1)S(1)}, bf16[2,64,128]{2,1,0:T(8,128)(2,1)S(1)}, u32[]{:S(2)}, u32[]{:S(2)}) collective-permute-start(bf16[2,64,128]{2,1,0:T(8,128)(2,1)S(1)} %get-tuple-element.53), channel_id=1, source_target_pairs={{0,3},{1,0},{2,1},{3,2},{4,7},{5,4},{6,5},{7,6},{8,11},{9,8},{10,9... | collective-permute-start | bytes 98312 | tf_op jit(solution)/shard_map/ppermute | solution.py:361
  46.1 11.3 %collective-permute-start.11 = (bf16[2,64,128]{2,1,0:T(8,128)(2,1)S(1)}, bf16[2,64,128]{2,1,0:T(8,128)(2,1)S(1)}, u32[]{:S(2)}, u32[]{:S(2)}) collective-permute-start(bf16[2,64,128]{2,1,0:T(8,128)(2,1)S(1)} %get-tuple-element.54), channel_id=1, source_target_pairs={{0,2},{1,3},{2,0},{3,1},{4,6},{5,7},{6,4},{7,5},{8,10},{9,11},{10,... | collective-permute-start | bytes 98312 | tf_op jit(solution)/shard_map/ppermute | solution.py:361
  52.7 5.8 %collective-permute-start.12 = (bf16[2,64,128]{2,1,0:T(8,128)(2,1)S(1)}, bf16[2,64,128]{2,1,0:T(8,128)(2,1)S(1)}, u32[]{:S(2)}, u32[]{:S(2)}) collective-permute-start(bf16[2,64,128]{2,1,0:T(8,128)(2,1)S(1)} %get-tuple-element.55), channel_id=1, source_target_pairs={{0,1},{1,2},{2,3},{3,0},{4,5},{5,6},{6,7},{7,4},{8,9},{9,10},{10,1... | collective-permute-start | bytes 98312 | tf_op jit(solution)/shard_map/ppermute | solution.py:361
  59.6 7.9 %collective-permute-start.13 = (bf16[8,64,128]{2,1,0:T(8,128)(2,1)S(1)}, bf16[8,64,128]{2,1,0:T(8,128)(2,1)S(1)}, u32[]{:S(2)}, u32[]{:S(2)}) collective-permute-start(bf16[8,64,128]{2,1,0:T(8,128)(2,1)S(1)} %get-tuple-element.61), channel_id=1, source_target_pairs={{0,1},{1,2},{2,3},{3,0},{4,5},{5,6},{6,7},{7,4},{8,9},{9,10},{10,1... | collective-permute-start | bytes 393224 | tf_op jit(solution)/shard_map/ppermute | solution.py:361
  62.0 2.5 %collective-permute-start.16 = (f32[2,64,128]{2,1,0:T(8,128)S(1)}, f32[2,64,128]{2,1,0:T(8,128)S(1)}, u32[]{:S(2)}, u32[]{:S(2)}) collective-permute-start(f32[2,64,128]{2,1,0:T(8,128)S(1)} %convert_add_fusion), channel_id=1, source_target_pairs={{0,4},{4,0},{8,12},{12,8},{16,20},{20,16},{24,28},{28,24},{1,5},{5... | collective-permute-start | bytes 196616 | tf_op jit(solution)/shard_map/ppermute | solution.py:392
  62.0 10.0 %collective-permute-start.14 = (bf16[8,64,128]{2,1,0:T(8,128)(2,1)S(1)}, bf16[8,64,128]{2,1,0:T(8,128)(2,1)S(1)}, u32[]{:S(2)}, u32[]{:S(2)}) collective-permute-start(bf16[8,64,128]{2,1,0:T(8,128)(2,1)S(1)} %get-tuple-element.62), channel_id=1, source_target_pairs={{0,2},{1,3},{2,0},{3,1},{4,6},{5,7},{6,4},{7,5},{8,10},{9,11},{10,... | collective-permute-start | bytes 393224 | tf_op jit(solution)/shard_map/ppermute | solution.py:361
  62.1 9.9 %collective-permute-start.15 = (bf16[8,64,128]{2,1,0:T(8,128)(2,1)S(1)}, bf16[8,64,128]{2,1,0:T(8,128)(2,1)S(1)}, u32[]{:S(2)}, u32[]{:S(2)}) collective-permute-start(bf16[8,64,128]{2,1,0:T(8,128)(2,1)S(1)} %get-tuple-element.63), channel_id=1, source_target_pairs={{0,3},{1,0},{2,1},{3,2},{4,7},{5,4},{6,5},{7,6},{8,11},{9,8},{10,9... | collective-permute-start | bytes 393224 | tf_op jit(solution)/shard_map/ppermute | solution.py:361
  64.5 8.9 %collective-permute-start.19 = (f32[2,64,128]{2,1,0:T(8,128)S(1)}, f32[2,64,128]{2,1,0:T(8,128)S(1)}, u32[]{:S(2)}, u32[]{:S(2)}) collective-permute-start(f32[2,64,128]{2,1,0:T(8,128)S(1)} %add.24), channel_id=1, source_target_pairs={{0,24},{4,28},{8,16},{12,20},{16,8},{20,12},{24,0},{28,4},{1,25},{... | collective-permute-start | bytes 196616 | tf_op jit(solution)/shard_map/ppermute | solution.py:394
  65.5 7.9 %collective-permute-start.18 = (f32[2,64,128]{2,1,0:T(8,128)S(1)}, f32[2,64,128]{2,1,0:T(8,128)S(1)}, u32[]{:S(2)}, u32[]{:S(2)}) collective-permute-start(f32[2,64,128]{2,1,0:T(8,128)S(1)} %add.24), channel_id=1, source_target_pairs={{0,16},{4,20},{8,24},{12,28},{16,0},{20,4},{24,8},{28,12},{1,17},{... | collective-permute-start | bytes 196616 | tf_op jit(solution)/shard_map/ppermute | solution.py:394
  67.4 6.0 %collective-permute-start.17 = (f32[2,64,128]{2,1,0:T(8,128)S(1)}, f32[2,64,128]{2,1,0:T(8,128)S(1)}, u32[]{:S(2)}, u32[]{:S(2)}) collective-permute-start(f32[2,64,128]{2,1,0:T(8,128)S(1)} %add.24), channel_id=1, source_target_pairs={{0,8},{4,12},{8,0},{12,4},{16,24},{20,28},{24,16},{28,20},{1,9},{5... | collective-permute-start | bytes 196616 | tf_op jit(solution)/shard_map/ppermute | solution.py:394

commit v21 on v19

--- a/solution.py
+++ b/solution.py
@@ -233,7 +233,7 @@
 
 
 def weight_kernel(reps, where, *rest):
-    packed, outs, (whole_z, whole_a) = rest[:reps], rest[reps : 2 * reps], rest[2 * reps :]
+    packed, (out, whole_z, whole_a) = rest[:reps], rest[reps:]
     blocks, _, nodes = whole_z.shape
     features = packed[0].shape[1]
     lay_features(where, packed, whole_z)
@@ -245,9 +245,9 @@
             whole_a[b], whole_z[b], (((1,), (1,)), ((), ())), preferred_element_type=F32
         )
     for s in range(reps):
-        for h in range(outs[s].shape[0]):
+        for h in range(out.shape[1]):
             part = total[s * features : (s + 1) * features, h * nodes : (h + 1) * nodes]
-            outs[s][h] = part.astype(BF16)
+            out[wrap(where[1] - s, reps), h] = part.astype(BF16)
 
 
 def weight_partial(where, packed, blocks):
@@ -256,9 +256,9 @@
     width = reps * features
     return pl.pallas_call(
         functools.partial(weight_kernel, reps),
-        out_shape=[jax.ShapeDtypeStruct((width // nodes, features, nodes), BF16)] * reps,
+        out_shape=jax.ShapeDtypeStruct((reps, width // nodes, features, nodes), BF16),
         in_specs=[smem()] + [vmem()] * reps,
-        out_specs=[vmem()] * reps,
+        out_specs=vmem(),
         scratch_shapes=[pltpu.VMEM((blocks, width, nodes), BF16)] * 2,
         compiler_params=pltpu.CompilerParams(vmem_limit_bytes=4 * MIB),
         cost_estimate=pl.CostEstimate(
@@ -382,12 +382,12 @@
     shares = total_shares(where, aside, own, two_in, one_in, reps)
     held, _ = lax.optimization_barrier((packed, shares))
     pieces = weight_partial(where, held, blocks // reps)
-    pieces = [shift(value, -s) for s, value in enumerate(pieces)]
+    pieces = lax.all_to_all(pieces, "rep", 0, 0, tiled=True)
     shares = [shift(value, s) for s, value in enumerate(shares)]
     outs = [shift(value, s) for s, value in enumerate(mix(where, shares, packed))]
     input_grad = lay_blocks(where, outs, cotangent.shape)
 
-    grad_w = sum(value.astype(F32) for value in pieces)
+    grad_w = pieces.astype(F32).sum(0)
     grad_w = grad_w + lax.ppermute(grad_w, "blk", pair)
     parts = [
         lax.ppermute(grad_w, "blk", [(i, i ^ step) for i in range(slabs)])

time: 70.4 us -> 78.6 us (1.12)
  the two profiles are of different devices: /device:TPU:0 before, /device:TPU:16 now
where the time goes in v21:
time: 78.6 us; the launch traced here: 77.8 us
  waiting for transfers between devices  39.4 us (50%)
  starting transfers between devices  23.4 us (30%)
  Pallas kernels  13.5 us (17%)
    ppermute x9, waiting for transfers between devices, shift(): lax.ppermute(value, 'rep', [(i, (i + steps) % reps) for i in range(reps)])  16.2 us
    ppermute x2, waiting for transfers between devices, on_device(): one_in = [lax.ppermute(part, 'blk', to_one) for part in one]  11.2 us
    ppermute x9, starting transfers between devices, shift(): lax.ppermute(value, 'rep', [(i, (i + steps) % reps) for i in range(reps)])  10.5 us
    ppermute x1, waiting for transfers between devices, on_device(): two_in = lax.ppermute(two, 'blk', to_two)  9.06 us
    pallas_call x1, Pallas kernels, contributions(): pl.pallas_call(functools.partial(tiles_kernel, slabs, reps), out_shape=[j...  8.34 us
    all_to_all x1, starting transfers between devices, on_device(): pieces = lax.all_to_all(pieces, 'rep', 0, 0, tiled=True)  6.24 us
    ppermute x3, starting transfers between devices, on_device(): lax.ppermute(grad_w, 'blk', [(i, i ^ step) for i in range(slabs)])  4.21 us
    ppermute x1, starting transfers between devices, on_device(): two_in = lax.ppermute(two, 'blk', to_two)  2.28 us
  transfers between devices with their start and end apart: 18, of which 9 were waited for; matrix products, arithmetic and copies ran while one was open for 0% of the time, Pallas kernels for 5%

profile of v21, /device:TPU:16, one launch (start us, length us, event | category | flops | bytes accessed | tf_op | source)
XLA Modules:
  0.0 77.8 jit_solution(4759519950514433474)
XLA Ops:
  0.6 0.1 pad_add_fusion.where
  0.7 8.3 %shard_map.86 = (bf16[64,64,128]{2,1,0:T(8,128)(2,1)S(1)}, bf16[32,64,128]{2,1,0:T(8,128)(2,1)S(1)}, bf16[32,64,128]{2,1,0:T(8,128)(2,1)S(1)}, bf16[32,64,128]{2...) custom-call(s32[2]{0:T(128)S(1)} %pad_add_fusion.where, ...), custom_call_target="tpu_custom_call" | custom-call | flops 1073741824 | bytes 16777216 | tf_op jit(solution)/shard_map/pallas_call | solution.py:157
  9.1 0.1 collective-permute-start
  9.1 2.3 %collective-permute-start.1 = (bf16[32,64,128]{2,1,0:T(8,128)(2,1)S(1)}, bf16[32,64,128]{2,1,0:T(8,128)(2,1)S(1)}, u32[]{:S(2)}, u32[]{:S(2)}) collective-permute-start(bf16[32,64,128]{2,1,0:T(8,128)(2,1)S(1)} %get-tuple-element.29), channel_id=1, source_target_pairs={{0,24},{4,12},{8,0},{12,20},{16,8},{20,28},{24,16},{28,4},{1,25},{... | collective-permute-start | bytes 1572872 | tf_op jit(solution)/shard_map/ppermute | solution.py:377
  11.4 1.6 %collective-permute-start.7 = (bf16[18,64,128]{2,1,0:T(8,128)(2,1)S(1)}, bf16[18,64,128]{2,1,0:T(8,128)(2,1)S(1)}, u32[]{:S(2)}, u32[]{:S(2)}) collective-permute-start(bf16[18,64,128]{2,1,0:T(8,128)(2,1)S(1)} %get-tuple-element.38), channel_id=1, source_target_pairs={{0,1},{1,2},{2,3},{3,0},{4,5},{5,6},{6,7},{7,4},{8,9},{9,10},{10,1... | collective-permute-start | bytes 884744 | tf_op jit(solution)/shard_map/ppermute | solution.py:361
  13.0 0.3 collective-permute-start.8
  13.3 1.3 %collective-permute-start.9 = (bf16[18,64,128]{2,1,0:T(8,128)(2,1)S(1)}, bf16[18,64,128]{2,1,0:T(8,128)(2,1)S(1)}, u32[]{:S(2)}, u32[]{:S(2)}) collective-permute-start(bf16[18,64,128]{2,1,0:T(8,128)(2,1)S(1)} %get-tuple-element.40), channel_id=1, source_target_pairs={{0,3},{1,0},{2,1},{3,2},{4,7},{5,4},{6,5},{7,6},{8,11},{9,8},{10,9... | collective-permute-start | bytes 884744 | tf_op jit(solution)/shard_map/ppermute | solution.py:361
  14.7 0.3 shard_map.87
  15.0 9.1 %collective-permute-done.1.two = bf16[32,64,128]{2,1,0:T(8,128)(2,1)S(1)} collective-permute-done((bf16[32,64,128]{2,1,0:T(8,128)(2,1)S(1)}, bf16[32,64,128]{2,1,0:T(8,128)(2,1)S(1)}, u32[]{:S(2)}, u32[]{:S(2)}) %collective-permute-start.1) | collective-permute-done | bytes 524320 | tf_op jit(solution)/shard_map/ppermute | solution.py:377
  24.1 5.6 %collective-permute-done.2.rest_0_ = bf16[16,64,128]{2,1,0:T(8,128)(2,1)S(1)} collective-permute-done((bf16[16,64,128]{2,1,0:T(8,128)(2,1)S(1)}, bf16[16,64,128]{2,1,0:T(8,128)(2,1)S(1)}, u32[]{:S(2)}, u32[]{:S(2)}) %collective-permute-start.2) | collective-permute-done | bytes 262176 | tf_op jit(solution)/shard_map/ppermute | solution.py:379
  29.7 5.6 %collective-permute-done.3.rest_1_ = bf16[16,64,128]{2,1,0:T(8,128)(2,1)S(1)} collective-permute-done((bf16[16,64,128]{2,1,0:T(8,128)(2,1)S(1)}, bf16[16,64,128]{2,1,0:T(8,128)(2,1)S(1)}, u32[]{:S(2)}, u32[]{:S(2)}) %collective-permute-start.3) | collective-permute-done | bytes 262176 | tf_op jit(solution)/shard_map/ppermute | solution.py:379
  35.3 0.9 %shard_map.88 = (bf16[8,64,128]{2,1,0:T(8,128)(2,1)S(1)}, bf16[8,64,128]{2,1,0:T(8,128)(2,1)S(1)}, bf16[8,64,128]{2,1,0:T(8,128)(2,1)S(1)}, bf16[8,64,128]{2,1,0:T(8,128)(2,1)S(1)}) custom-call(s32[2]{0:T(128)S(1)} %pad_add_fusion.where, bf16[64,64,128]{2,1,0:T(8,128)(2,1)S(1)} %collective-permute-done.other.aside, ...), custom_call_target="tpu_custom_call" | custom-call | flops 1048576 | bytes 2621440 | tf_op jit(solution)/shard_map/pallas_call | solution.py:320
  36.2 1.6 %collective-permute-done.9.rest_7_.rest_3_ = bf16[18,64,128]{2,1,0:T(8,128)(2,1)S(1)} collective-permute-done((bf16[18,64,128]{2,1,0:T(8,128)(2,1)S(1)}, bf16[18,64,128]{2,1,0:T(8,128)(2,1)S(1)}, u32[]{:S(2)}, u32[]{:S(2)}) %collective-permute-start.9) | collective-permute-done | bytes 294944 | tf_op jit(solution)/shard_map/ppermute | solution.py:361
  37.8 1.7 %shard_map.91 = bf16[4,2,64,128]{3,2,1,0:T(8,128)(2,1)} custom-call(s32[2]{0:T(128)S(1)} %pad_add_fusion.where, bf16[18,64,128]{2,1,0:T(8,128)(2,1)S(1)} %get-tuple-element.45.rest_4_.rest_0_, bf16[18,64,128]{2,1,0:T(8,128)(2,1)S(1)} %collective-permute-done.7.rest_5_.rest_1_, bf16[18,64,128]{2,1,0:T(8,128)(2,1)S(1)} %collective-permute-done.8.rest_6_.rest_2_, ...), custom_call_target="tpu_custom_call" | custom-call | flops 134217728 | bytes 1179648 | tf_op jit(solution)/shard_map/pallas_call | solution.py:257
  39.5 6.2 %all-to-all-start = ((bf16[4,2,64,128]{3,2,1,0:T(8,128)(2,1)}), bf16[4,2,64,128]{3,2,1,0:T(8,128)(2,1)S(1)}, u32[]{:S(2)}, u32[]{:S(2)}) async-start(bf16[4,2,64,128]{3,2,1,0:T(8,128)(2,1)} %shard_map.91), calls=%async_computation | async-start | bytes 262144 | tf_op jit(solution)/shard_map/all_to_all | solution.py:385
  45.7 1.5 %collective-permute-start.4 = (bf16[8,64,128]{2,1,0:T(8,128)(2,1)S(1)}, bf16[8,64,128]{2,1,0:T(8,128)(2,1)S(1)}, u32[]{:S(2)}, u32[]{:S(2)}) collective-permute-start(bf16[8,64,128]{2,1,0:T(8,128)(2,1)S(1)} %get-tuple-element.34), channel_id=1, source_target_pairs={{0,1},{1,2},{2,3},{3,0},{4,5},{5,6},{6,7},{7,4},{8,9},{9,10},{10,1... | collective-permute-start | bytes 393224 | tf_op jit(solution)/shard_map/ppermute | solution.py:361
  47.2 0.6 collective-permute-start.5
  47.8 0.9 %collective-permute-start.6 = (bf16[8,64,128]{2,1,0:T(8,128)(2,1)S(1)}, bf16[8,64,128]{2,1,0:T(8,128)(2,1)S(1)}, u32[]{:S(2)}, u32[]{:S(2)}) collective-permute-start(bf16[8,64,128]{2,1,0:T(8,128)(2,1)S(1)} %get-tuple-element.36), channel_id=1, source_target_pairs={{0,3},{1,0},{2,1},{3,2},{4,7},{5,4},{6,5},{7,6},{8,11},{9,8},{10,9... | collective-permute-start | bytes 393224 | tf_op jit(solution)/shard_map/ppermute | solution.py:361
  48.7 9.8 %collective-permute-done.4.rest_1_ = bf16[8,64,128]{2,1,0:T(8,128)(2,1)S(1)} collective-permute-done((bf16[8,64,128]{2,1,0:T(8,128)(2,1)S(1)}, bf16[8,64,128]{2,1,0:T(8,128)(2,1)S(1)}, u32[]{:S(2)}, u32[]{:S(2)}) %collective-permute-start.4) | collective-permute-done | bytes 131104 | tf_op jit(solution)/shard_map/ppermute | solution.py:361
  58.5 0.9 %collective-permute-done.6.rest_3_ = bf16[8,64,128]{2,1,0:T(8,128)(2,1)S(1)} collective-permute-done((bf16[8,64,128]{2,1,0:T(8,128)(2,1)S(1)}, bf16[8,64,128]{2,1,0:T(8,128)(2,1)S(1)}, u32[]{:S(2)}, u32[]{:S(2)}) %collective-permute-start.6) | collective-permute-done | bytes 131104 | tf_op jit(solution)/shard_map/ppermute | solution.py:361
  59.4 1.0 %shard_map.89 = (bf16[8,64,128]{2,1,0:T(8,128)(2,1)S(1)}, bf16[8,64,128]{2,1,0:T(8,128)(2,1)S(1)}, bf16[8,64,128]{2,1,0:T(8,128)(2,1)S(1)}, bf16[8,64,128]{2,1,0:T(8,128)(2,1)S(1)}) custom-call(s32[2]{0:T(128)S(1)} %pad_add_fusion.where, bf16[8,64,128]{2,1,0:T(8,128)(2,1)S(1)} %get-tuple-element.33.rest_0_, ...), custom_call_target="tpu_custom_call" | custom-call | flops 134217728 | bytes 1048576 | tf_op jit(solution)/shard_map/pallas_call | solution.py:220
  60.4 2.1 %collective-permute-start.10 = (bf16[8,64,128]{2,1,0:T(8,128)(2,1)S(1)}, bf16[8,64,128]{2,1,0:T(8,128)(2,1)S(1)}, u32[]{:S(2)}, u32[]{:S(2)}) collective-permute-start(bf16[8,64,128]{2,1,0:T(8,128)(2,1)S(1)} %get-tuple-element.42), channel_id=1, source_target_pairs={{0,1},{1,2},{2,3},{3,0},{4,5},{5,6},{6,7},{7,4},{8,9},{9,10},{10,1... | collective-permute-start | bytes 393224 | tf_op jit(solution)/shard_map/ppermute | solution.py:361
  62.4 1.9 %collective-permute-start.11 = (bf16[8,64,128]{2,1,0:T(8,128)(2,1)S(1)}, bf16[8,64,128]{2,1,0:T(8,128)(2,1)S(1)}, u32[]{:S(2)}, u32[]{:S(2)}) collective-permute-start(bf16[8,64,128]{2,1,0:T(8,128)(2,1)S(1)} %get-tuple-element.43), channel_id=1, source_target_pairs={{0,2},{1,3},{2,0},{3,1},{4,6},{5,7},{6,4},{7,5},{8,10},{9,11},{10,... | collective-permute-start | bytes 393224 | tf_op jit(solution)/shard_map/ppermute | solution.py:361
  64.4 0.3 collective-permute-start.12
  64.8 1.2 %collective-permute-done.13 = f32[2,64,128]{2,1,0:T(8,128)S(1)} collective-permute-done((f32[2,64,128]{2,1,0:T(8,128)S(1)}, f32[2,64,128]{2,1,0:T(8,128)S(1)}, u32[]{:S(2)}, u32[]{:S(2)}) %collective-permute-start.13) | collective-permute-done | bytes 65568 | tf_op jit(solution)/shard_map/ppermute | solution.py:391
  66.0 1.8 %collective-permute-start.16 = (f32[2,64,128]{2,1,0:T(8,128)S(1)}, f32[2,64,128]{2,1,0:T(8,128)S(1)}, u32[]{:S(2)}, u32[]{:S(2)}) collective-permute-start(f32[2,64,128]{2,1,0:T(8,128)S(1)} %add.12), channel_id=1, source_target_pairs={{0,24},{4,28},{8,16},{12,20},{16,8},{20,12},{24,0},{28,4},{1,25},{... | collective-permute-start | bytes 196616 | tf_op jit(solution)/shard_map/ppermute | solution.py:393
  67.8 1.2 %collective-permute-start.15 = (f32[2,64,128]{2,1,0:T(8,128)S(1)}, f32[2,64,128]{2,1,0:T(8,128)S(1)}, u32[]{:S(2)}, u32[]{:S(2)}) collective-permute-start(f32[2,64,128]{2,1,0:T(8,128)S(1)} %add.12), channel_id=1, source_target_pairs={{0,16},{4,20},{8,24},{12,28},{16,0},{20,4},{24,8},{28,12},{1,17},{... | collective-permute-start | bytes 196616 | tf_op jit(solution)/shard_map/ppermute | solution.py:393
  69.0 3.9 %collective-permute-done.10.rest_1_ = bf16[8,64,128]{2,1,0:T(8,128)(2,1)S(1)} collective-permute-done((bf16[8,64,128]{2,1,0:T(8,128)(2,1)S(1)}, bf16[8,64,128]{2,1,0:T(8,128)(2,1)S(1)}, u32[]{:S(2)}, u32[]{:S(2)}) %collective-permute-start.10) | collective-permute-done | bytes 131104 | tf_op jit(solution)/shard_map/ppermute | solution.py:361
  72.9 1.2 %collective-permute-start.14 = (f32[2,64,128]{2,1,0:T(8,128)S(1)}, f32[2,64,128]{2,1,0:T(8,128)S(1)}, u32[]{:S(2)}, u32[]{:S(2)}) collective-permute-start(f32[2,64,128]{2,1,0:T(8,128)S(1)} %add.12), channel_id=1, source_target_pairs={{0,8},{4,12},{8,0},{12,4},{16,24},{20,28},{24,16},{28,20},{1,9},{5... | collective-permute-start | bytes 196616 | tf_op jit(solution)/shard_map/ppermute | solution.py:393
  74.2 1.4 %shard_map.90 = bf16[32,64,128]{2,1,0:T(8,128)(2,1)} custom-call(s32[2]{0:T(128)S(1)} %pad_add_fusion.where, bf16[8,64,128]{2,1,0:T(8,128)(2,1)S(1)} %get-tuple-element.41.rest_0_, bf16[8,64,128]{2,1,0:T(8,128)(2,1)S(1)} %collective-permute-done.10.rest_1_, bf16[8,64,128]{2,1,0:T(8,128)(2,1)S(1)} %collective-permute-done.11.rest_2_, ...), custom_call_target="tpu_custom_call" | custom-call | bytes 33554432 | tf_op jit(solution)/shard_map/pallas_call | solution.py:346
  75.6 1.6 %collective-permute-done.14 = f32[2,64,128]{2,1,0:T(8,128)S(1)} collective-permute-done((f32[2,64,128]{2,1,0:T(8,128)S(1)}, f32[2,64,128]{2,1,0:T(8,128)S(1)}, u32[]{:S(2)}, u32[]{:S(2)}) %collective-permute-start.14) | collective-permute-done | bytes 65568 | tf_op jit(solution)/shard_map/ppermute | solution.py:393
  77.2 0.6 copy_bitcast_fusion
  (14 shorter events, 0.2 us)
Async XLA Ops:
  9.1 5.6 %collective-permute-start = (bf16[64,64,128]{2,1,0:T(8,128)(2,1)S(1)}, bf16[64,64,128]{2,1,0:T(8,128)(2,1)S(1)}, u32[]{:S(2)}, u32[]{:S(2)}) collective-permute-start(bf16[64,64,128]{2,1,0:T(8,128)(2,1)S(1)} %get-tuple-element.27), channel_id=1, source_target_pairs={{0,4},{4,0},{8,12},{12,8},{16,20},{20,16},{24,28},{28,24},{1,5},{5... | collective-permute-start | bytes 3145736 | tf_op jit(solution)/shard_map/ppermute | solution.py:376
  9.1 15.0 %collective-permute-start.1 = (bf16[32,64,128]{2,1,0:T(8,128)(2,1)S(1)}, bf16[32,64,128]{2,1,0:T(8,128)(2,1)S(1)}, u32[]{:S(2)}, u32[]{:S(2)}) collective-permute-start(bf16[32,64,128]{2,1,0:T(8,128)(2,1)S(1)} %get-tuple-element.29), channel_id=1, source_target_pairs={{0,24},{4,12},{8,0},{12,20},{16,8},{20,28},{24,16},{28,4},{1,25},{... | collective-permute-start | bytes 1572872 | tf_op jit(solution)/shard_map/ppermute | solution.py:377
  11.4 24.8 %collective-permute-start.7 = (bf16[18,64,128]{2,1,0:T(8,128)(2,1)S(1)}, bf16[18,64,128]{2,1,0:T(8,128)(2,1)S(1)}, u32[]{:S(2)}, u32[]{:S(2)}) collective-permute-start(bf16[18,64,128]{2,1,0:T(8,128)(2,1)S(1)} %get-tuple-element.38), channel_id=1, source_target_pairs={{0,1},{1,2},{2,3},{3,0},{4,5},{5,6},{6,7},{7,4},{8,9},{9,10},{10,1... | collective-permute-start | bytes 884744 | tf_op jit(solution)/shard_map/ppermute | solution.py:361
  13.0 23.2 %collective-permute-start.8 = (bf16[18,64,128]{2,1,0:T(8,128)(2,1)S(1)}, bf16[18,64,128]{2,1,0:T(8,128)(2,1)S(1)}, u32[]{:S(2)}, u32[]{:S(2)}) collective-permute-start(bf16[18,64,128]{2,1,0:T(8,128)(2,1)S(1)} %get-tuple-element.39), channel_id=1, source_target_pairs={{0,2},{1,3},{2,0},{3,1},{4,6},{5,7},{6,4},{7,5},{8,10},{9,11},{10,... | collective-permute-start | bytes 884744 | tf_op jit(solution)/shard_map/ppermute | solution.py:361
  13.3 24.5 %collective-permute-start.9 = (bf16[18,64,128]{2,1,0:T(8,128)(2,1)S(1)}, bf16[18,64,128]{2,1,0:T(8,128)(2,1)S(1)}, u32[]{:S(2)}, u32[]{:S(2)}) collective-permute-start(bf16[18,64,128]{2,1,0:T(8,128)(2,1)S(1)} %get-tuple-element.40), channel_id=1, source_target_pairs={{0,3},{1,0},{2,1},{3,2},{4,7},{5,4},{6,5},{7,6},{8,11},{9,8},{10,9... | collective-permute-start | bytes 884744 | tf_op jit(solution)/shard_map/ppermute | solution.py:361
  14.9 14.7 %collective-permute-start.2 = (bf16[16,64,128]{2,1,0:T(8,128)(2,1)S(1)}, bf16[16,64,128]{2,1,0:T(8,128)(2,1)S(1)}, u32[]{:S(2)}, u32[]{:S(2)}) collective-permute-start(bf16[16,64,128]{2,1,0:T(8,128)(2,1)S(1)} %get-tuple-element.31), channel_id=1, source_target_pairs={{0,28},{4,8},{8,4},{12,16},{16,12},{20,24},{24,20},{28,0},{1,29},{... | collective-permute-start | bytes 786440 | tf_op jit(solution)/shard_map/ppermute | solution.py:379
  24.1 11.2 %collective-permute-start.3 = (bf16[16,64,128]{2,1,0:T(8,128)(2,1)S(1)}, bf16[16,64,128]{2,1,0:T(8,128)(2,1)S(1)}, u32[]{:S(2)}, u32[]{:S(2)}) collective-permute-start(bf16[16,64,128]{2,1,0:T(8,128)(2,1)S(1)} %get-tuple-element.32), channel_id=1, source_target_pairs={{0,28},{4,8},{8,4},{12,16},{16,12},{20,24},{24,20},{28,0},{1,29},{... | collective-permute-start | bytes 786440 | tf_op jit(solution)/shard_map/ppermute | solution.py:379
  39.5 25.2 %all-to-all-start = ((bf16[4,2,64,128]{3,2,1,0:T(8,128)(2,1)}), bf16[4,2,64,128]{3,2,1,0:T(8,128)(2,1)S(1)}, u32[]{:S(2)}, u32[]{:S(2)}) async-start(bf16[4,2,64,128]{3,2,1,0:T(8,128)(2,1)} %shard_map.91), calls=%async_computation | async-start | bytes 262144 | tf_op jit(solution)/shard_map/all_to_all | solution.py:385
  45.7 12.8 %collective-permute-start.4 = (bf16[8,64,128]{2,1,0:T(8,128)(2,1)S(1)}, bf16[8,64,128]{2,1,0:T(8,128)(2,1)S(1)}, u32[]{:S(2)}, u32[]{:S(2)}) collective-permute-start(bf16[8,64,128]{2,1,0:T(8,128)(2,1)S(1)} %get-tuple-element.34), channel_id=1, source_target_pairs={{0,1},{1,2},{2,3},{3,0},{4,5},{5,6},{6,7},{7,4},{8,9},{9,10},{10,1... | collective-permute-start | bytes 393224 | tf_op jit(solution)/shard_map/ppermute | solution.py:361
  47.2 11.3 %collective-permute-start.5 = (bf16[8,64,128]{2,1,0:T(8,128)(2,1)S(1)}, bf16[8,64,128]{2,1,0:T(8,128)(2,1)S(1)}, u32[]{:S(2)}, u32[]{:S(2)}) collective-permute-start(bf16[8,64,128]{2,1,0:T(8,128)(2,1)S(1)} %get-tuple-element.35), channel_id=1, source_target_pairs={{0,2},{1,3},{2,0},{3,1},{4,6},{5,7},{6,4},{7,5},{8,10},{9,11},{10,... | collective-permute-start | bytes 393224 | tf_op jit(solution)/shard_map/ppermute | solution.py:361
  47.8 11.6 %collective-permute-start.6 = (bf16[8,64,128]{2,1,0:T(8,128)(2,1)S(1)}, bf16[8,64,128]{2,1,0:T(8,128)(2,1)S(1)}, u32[]{:S(2)}, u32[]{:S(2)}) collective-permute-start(bf16[8,64,128]{2,1,0:T(8,128)(2,1)S(1)} %get-tuple-element.36), channel_id=1, source_target_pairs={{0,3},{1,0},{2,1},{3,2},{4,7},{5,4},{6,5},{7,6},{8,11},{9,8},{10,9... | collective-permute-start | bytes 393224 | tf_op jit(solution)/shard_map/ppermute | solution.py:361
  60.4 12.5 %collective-permute-start.10 = (bf16[8,64,128]{2,1,0:T(8,128)(2,1)S(1)}, bf16[8,64,128]{2,1,0:T(8,128)(2,1)S(1)}, u32[]{:S(2)}, u32[]{:S(2)}) collective-permute-start(bf16[8,64,128]{2,1,0:T(8,128)(2,1)S(1)} %get-tuple-element.42), channel_id=1, source_target_pairs={{0,1},{1,2},{2,3},{3,0},{4,5},{5,6},{6,7},{7,4},{8,9},{9,10},{10,1... | collective-permute-start | bytes 393224 | tf_op jit(solution)/shard_map/ppermute | solution.py:361
  62.4 11.7 %collective-permute-start.11 = (bf16[8,64,128]{2,1,0:T(8,128)(2,1)S(1)}, bf16[8,64,128]{2,1,0:T(8,128)(2,1)S(1)}, u32[]{:S(2)}, u32[]{:S(2)}) collective-permute-start(bf16[8,64,128]{2,1,0:T(8,128)(2,1)S(1)} %get-tuple-element.43), channel_id=1, source_target_pairs={{0,2},{1,3},{2,0},{3,1},{4,6},{5,7},{6,4},{7,5},{8,10},{9,11},{10,... | collective-permute-start | bytes 393224 | tf_op jit(solution)/shard_map/ppermute | solution.py:361
  64.4 9.8 %collective-permute-start.12 = (bf16[8,64,128]{2,1,0:T(8,128)(2,1)S(1)}, bf16[8,64,128]{2,1,0:T(8,128)(2,1)S(1)}, u32[]{:S(2)}, u32[]{:S(2)}) collective-permute-start(bf16[8,64,128]{2,1,0:T(8,128)(2,1)S(1)} %get-tuple-element.44), channel_id=1, source_target_pairs={{0,3},{1,0},{2,1},{3,2},{4,7},{5,4},{6,5},{7,6},{8,11},{9,8},{10,9... | collective-permute-start | bytes 393224 | tf_op jit(solution)/shard_map/ppermute | solution.py:361
  64.7 1.3 %collective-permute-start.13 = (f32[2,64,128]{2,1,0:T(8,128)S(1)}, f32[2,64,128]{2,1,0:T(8,128)S(1)}, u32[]{:S(2)}, u32[]{:S(2)}) collective-permute-start(f32[2,64,128]{2,1,0:T(8,128)S(1)} %convert_reduce_fusion), channel_id=1, source_target_pairs={{0,4},{4,0},{8,12},{12,8},{16,20},{20,16},{24,28},{28,24},{1,5},{5... | collective-permute-start | bytes 196616 | tf_op jit(solution)/shard_map/ppermute | solution.py:391
  66.0 9.5 %collective-permute-start.16 = (f32[2,64,128]{2,1,0:T(8,128)S(1)}, f32[2,64,128]{2,1,0:T(8,128)S(1)}, u32[]{:S(2)}, u32[]{:S(2)}) collective-permute-start(f32[2,64,128]{2,1,0:T(8,128)S(1)} %add.12), channel_id=1, source_target_pairs={{0,24},{4,28},{8,16},{12,20},{16,8},{20,12},{24,0},{28,4},{1,25},{... | collective-permute-start | bytes 196616 | tf_op jit(solution)/shard_map/ppermute | solution.py:393
  67.8 7.7 %collective-permute-start.15 = (f32[2,64,128]{2,1,0:T(8,128)S(1)}, f32[2,64,128]{2,1,0:T(8,128)S(1)}, u32[]{:S(2)}, u32[]{:S(2)}) collective-permute-start(f32[2,64,128]{2,1,0:T(8,128)S(1)} %add.12), channel_id=1, source_target_pairs={{0,16},{4,20},{8,24},{12,28},{16,0},{20,4},{24,8},{28,12},{1,17},{... | collective-permute-start | bytes 196616 | tf_op jit(solution)/shard_map/ppermute | solution.py:393
  72.9 4.3 %collective-permute-start.14 = (f32[2,64,128]{2,1,0:T(8,128)S(1)}, f32[2,64,128]{2,1,0:T(8,128)S(1)}, u32[]{:S(2)}, u32[]{:S(2)}) collective-permute-start(f32[2,64,128]{2,1,0:T(8,128)S(1)} %add.12), channel_id=1, source_target_pairs={{0,8},{4,12},{8,0},{12,4},{16,24},{20,28},{24,16},{28,20},{1,9},{5... | collective-permute-start | bytes 196616 | tf_op jit(solution)/shard_map/ppermute | solution.py:393

commit v22 on v19

--- a/solution.py
+++ b/solution.py
@@ -10,7 +10,7 @@
 
 REACH = 2
 GROUP = 4
-STEP = 8
+STEP = 4
 PARTS = 2
 BF16 = jnp.bfloat16
 F32 = jnp.float32

time: 70.4 us -> 71.3 us (1.013); the launches traced: 69.3 us -> 71.2 us
  Pallas kernels: 13.8 us -> 11.1 us
  waiting for transfers between devices: 16.4 us -> 18.6 us
  starting transfers between devices: 37.7 us -> 39.9 us
    ppermute x1, starting transfers between devices: 1.38 us -> 5.06 us  [on_device(): aside = lax.ppermute(aside, 'blk', pair)]
    pallas_call x1, Pallas kernels: 9.24 us -> 6.6 us  [contributions(): pl.pallas_call(functools.partial(tiles_kernel, slabs, reps), out_shape=[j...]
    ppermute x12, waiting for transfers between devices: 4.3 us -> 6.35 us  [shift(): lax.ppermute(value, 'rep', [(i, (i + steps) % reps) for i in range(reps)])]
    ppermute x3, starting transfers between devices: 3.55 us -> 2.06 us  [on_device(): lax.ppermute(grad_w, 'blk', [(i, i ^ step) for i in range(slabs)])]
    ppermute x12, starting transfers between devices: 27.3 us -> 28.2 us  [shift(): lax.ppermute(value, 'rep', [(i, (i + steps) % reps) for i in range(reps)])]
    ppermute x1, starting transfers between devices: 2.61 us -> 1.85 us  [on_device(): two_in = lax.ppermute(two, 'blk', to_two)]
  transfers between devices with their start and end apart: 20 -> 20, of which waited for: 5 -> 6; matrix products, arithmetic and copies ran while one was open for 0% -> 0% of each run, Pallas kernels for 7% -> 6%
where the time goes in v22:
time: 71.3 us; the launch traced here: 71.2 us
  starting transfers between devices  39.9 us (56%)
  waiting for transfers between devices  18.6 us (26%)
  Pallas kernels  11.1 us (16%)
  other arithmetic  0.75 us (1%)
  between operations  0.74 us (1%)
    ppermute x12, starting transfers between devices, shift(): lax.ppermute(value, 'rep', [(i, (i + steps) % reps) for i in range(reps)])  28.2 us
    pallas_call x1, Pallas kernels, contributions(): pl.pallas_call(functools.partial(tiles_kernel, slabs, reps), out_shape=[j...  6.6 us
    ppermute x2, waiting for transfers between devices, on_device(): one_in = [lax.ppermute(part, 'blk', to_one) for part in one]  6.47 us
    ppermute x12, waiting for transfers between devices, shift(): lax.ppermute(value, 'rep', [(i, (i + steps) % reps) for i in range(reps)])  6.35 us
    ppermute x1, waiting for transfers between devices, on_device(): two_in = lax.ppermute(two, 'blk', to_two)  5.8 us
    ppermute x1, starting transfers between devices, on_device(): aside = lax.ppermute(aside, 'blk', pair)  5.06 us
    ppermute x2, starting transfers between devices, on_device(): one_in = [lax.ppermute(part, 'blk', to_one) for part in one]  2.71 us
    ppermute x3, starting transfers between devices, on_device(): lax.ppermute(grad_w, 'blk', [(i, i ^ step) for i in range(slabs)])  2.06 us
  transfers between devices with their start and end apart: 20, of which 6 were waited for; matrix products, arithmetic and copies ran while one was open for 0% of the time, Pallas kernels for 6%

profile of v22, /device:TPU:0, one launch (start us, length us, event | category | flops | bytes accessed | tf_op | source)
XLA Modules:
  0.0 71.2 jit_solution(6319029150322539034)
XLA Ops:
  0.7 6.6 %shard_map.86 = (bf16[64,64,128]{2,1,0:T(8,128)(2,1)S(1)}, bf16[32,64,128]{2,1,0:T(8,128)(2,1)S(1)}, bf16[32,64,128]{2,1,0:T(8,128)(2,1)S(1)}, bf16[32,64,128]{2...) custom-call(s32[2]{0:T(128)S(1)} %pad_add_fusion.where, ...), custom_call_target="tpu_custom_call" | custom-call | flops 1073741824 | bytes 16777216 | tf_op jit(solution)/shard_map/pallas_call | solution.py:157
  7.3 5.1 %collective-permute-start = (bf16[64,64,128]{2,1,0:T(8,128)(2,1)S(1)}, bf16[64,64,128]{2,1,0:T(8,128)(2,1)S(1)}, u32[]{:S(2)}, u32[]{:S(2)}) collective-permute-start(bf16[64,64,128]{2,1,0:T(8,128)(2,1)S(1)} %get-tuple-element.31), channel_id=1, source_target_pairs={{0,4},{4,0},{8,12},{12,8},{16,20},{20,16},{24,28},{28,24},{1,5},{5... | collective-permute-start | bytes 3145736 | tf_op jit(solution)/shard_map/ppermute | solution.py:376
  12.4 1.9 %collective-permute-start.1 = (bf16[32,64,128]{2,1,0:T(8,128)(2,1)S(1)}, bf16[32,64,128]{2,1,0:T(8,128)(2,1)S(1)}, u32[]{:S(2)}, u32[]{:S(2)}) collective-permute-start(bf16[32,64,128]{2,1,0:T(8,128)(2,1)S(1)} %get-tuple-element.33), channel_id=1, source_target_pairs={{0,24},{4,12},{8,0},{12,20},{16,8},{20,28},{24,16},{28,4},{1,25},{... | collective-permute-start | bytes 1572872 | tf_op jit(solution)/shard_map/ppermute | solution.py:377
  14.2 1.6 %collective-permute-start.7 = (bf16[18,64,128]{2,1,0:T(8,128)(2,1)S(1)}, bf16[18,64,128]{2,1,0:T(8,128)(2,1)S(1)}, u32[]{:S(2)}, u32[]{:S(2)}) collective-permute-start(bf16[18,64,128]{2,1,0:T(8,128)(2,1)S(1)} %get-tuple-element.42), channel_id=1, source_target_pairs={{0,1},{1,2},{2,3},{3,0},{4,5},{5,6},{6,7},{7,4},{8,9},{9,10},{10,1... | collective-permute-start | bytes 884744 | tf_op jit(solution)/shard_map/ppermute | solution.py:361
  15.8 0.3 shard_map.87
  16.1 1.1 %collective-permute-start.2 = (bf16[16,64,128]{2,1,0:T(8,128)(2,1)S(1)}, bf16[16,64,128]{2,1,0:T(8,128)(2,1)S(1)}, u32[]{:S(2)}, u32[]{:S(2)}) collective-permute-start(bf16[16,64,128]{2,1,0:T(8,128)(2,1)S(1)} %get-tuple-element.35), channel_id=1, source_target_pairs={{0,28},{4,8},{8,4},{12,16},{16,12},{20,24},{24,20},{28,0},{1,29},{... | collective-permute-start | bytes 786440 | tf_op jit(solution)/shard_map/ppermute | solution.py:379
  17.1 1.6 %collective-permute-start.3 = (bf16[16,64,128]{2,1,0:T(8,128)(2,1)S(1)}, bf16[16,64,128]{2,1,0:T(8,128)(2,1)S(1)}, u32[]{:S(2)}, u32[]{:S(2)}) collective-permute-start(bf16[16,64,128]{2,1,0:T(8,128)(2,1)S(1)} %get-tuple-element.36), channel_id=1, source_target_pairs={{0,28},{4,8},{8,4},{12,16},{16,12},{20,24},{24,20},{28,0},{1,29},{... | collective-permute-start | bytes 786440 | tf_op jit(solution)/shard_map/ppermute | solution.py:379
  18.8 2.6 %collective-permute-start.8 = (bf16[18,64,128]{2,1,0:T(8,128)(2,1)S(1)}, bf16[18,64,128]{2,1,0:T(8,128)(2,1)S(1)}, u32[]{:S(2)}, u32[]{:S(2)}) collective-permute-start(bf16[18,64,128]{2,1,0:T(8,128)(2,1)S(1)} %get-tuple-element.43), channel_id=1, source_target_pairs={{0,2},{1,3},{2,0},{3,1},{4,6},{5,7},{6,4},{7,5},{8,10},{9,11},{10,... | collective-permute-start | bytes 884744 | tf_op jit(solution)/shard_map/ppermute | solution.py:361
  21.4 5.8 %collective-permute-done.1.two = bf16[32,64,128]{2,1,0:T(8,128)(2,1)S(1)} collective-permute-done((bf16[32,64,128]{2,1,0:T(8,128)(2,1)S(1)}, bf16[32,64,128]{2,1,0:T(8,128)(2,1)S(1)}, u32[]{:S(2)}, u32[]{:S(2)}) %collective-permute-start.1) | collective-permute-done | bytes 524320 | tf_op jit(solution)/shard_map/ppermute | solution.py:377
  27.2 4.4 %collective-permute-start.9 = (bf16[18,64,128]{2,1,0:T(8,128)(2,1)S(1)}, bf16[18,64,128]{2,1,0:T(8,128)(2,1)S(1)}, u32[]{:S(2)}, u32[]{:S(2)}) collective-permute-start(bf16[18,64,128]{2,1,0:T(8,128)(2,1)S(1)} %get-tuple-element.44), channel_id=1, source_target_pairs={{0,3},{1,0},{2,1},{3,2},{4,7},{5,4},{6,5},{7,6},{8,11},{9,8},{10,9... | collective-permute-start | bytes 884744 | tf_op jit(solution)/shard_map/ppermute | solution.py:361
  31.6 0.9 %collective-permute-done.2.rest_0_ = bf16[16,64,128]{2,1,0:T(8,128)(2,1)S(1)} collective-permute-done((bf16[16,64,128]{2,1,0:T(8,128)(2,1)S(1)}, bf16[16,64,128]{2,1,0:T(8,128)(2,1)S(1)}, u32[]{:S(2)}, u32[]{:S(2)}) %collective-permute-start.2) | collective-permute-done | bytes 262176 | tf_op jit(solution)/shard_map/ppermute | solution.py:379
  32.5 5.6 %collective-permute-done.3.rest_1_ = bf16[16,64,128]{2,1,0:T(8,128)(2,1)S(1)} collective-permute-done((bf16[16,64,128]{2,1,0:T(8,128)(2,1)S(1)}, bf16[16,64,128]{2,1,0:T(8,128)(2,1)S(1)}, u32[]{:S(2)}, u32[]{:S(2)}) %collective-permute-start.3) | collective-permute-done | bytes 262176 | tf_op jit(solution)/shard_map/ppermute | solution.py:379
  38.1 0.9 %shard_map.88 = (bf16[8,64,128]{2,1,0:T(8,128)(2,1)S(1)}, bf16[8,64,128]{2,1,0:T(8,128)(2,1)S(1)}, bf16[8,64,128]{2,1,0:T(8,128)(2,1)S(1)}, bf16[8,64,128]{2,1,0:T(8,128)(2,1)S(1)}) custom-call(s32[2]{0:T(128)S(1)} %pad_add_fusion.where, bf16[64,64,128]{2,1,0:T(8,128)(2,1)S(1)} %collective-permute-done.other.aside, ...), custom_call_target="tpu_custom_call" | custom-call | flops 1048576 | bytes 2621440 | tf_op jit(solution)/shard_map/pallas_call | solution.py:320
  39.0 2.3 %collective-permute-start.4 = (bf16[8,64,128]{2,1,0:T(8,128)(2,1)S(1)}, bf16[8,64,128]{2,1,0:T(8,128)(2,1)S(1)}, u32[]{:S(2)}, u32[]{:S(2)}) collective-permute-start(bf16[8,64,128]{2,1,0:T(8,128)(2,1)S(1)} %get-tuple-element.38), channel_id=1, source_target_pairs={{0,1},{1,2},{2,3},{3,0},{4,5},{5,6},{6,7},{7,4},{8,9},{9,10},{10,1... | collective-permute-start | bytes 393224 | tf_op jit(solution)/shard_map/ppermute | solution.py:361
  41.3 2.6 %collective-permute-start.5 = (bf16[8,64,128]{2,1,0:T(8,128)(2,1)S(1)}, bf16[8,64,128]{2,1,0:T(8,128)(2,1)S(1)}, u32[]{:S(2)}, u32[]{:S(2)}) collective-permute-start(bf16[8,64,128]{2,1,0:T(8,128)(2,1)S(1)} %get-tuple-element.39), channel_id=1, source_target_pairs={{0,2},{1,3},{2,0},{3,1},{4,6},{5,7},{6,4},{7,5},{8,10},{9,11},{10,... | collective-permute-start | bytes 393224 | tf_op jit(solution)/shard_map/ppermute | solution.py:361
  43.9 1.4 %collective-permute-start.6 = (bf16[8,64,128]{2,1,0:T(8,128)(2,1)S(1)}, bf16[8,64,128]{2,1,0:T(8,128)(2,1)S(1)}, u32[]{:S(2)}, u32[]{:S(2)}) collective-permute-start(bf16[8,64,128]{2,1,0:T(8,128)(2,1)S(1)} %get-tuple-element.40), channel_id=1, source_target_pairs={{0,3},{1,0},{2,1},{3,2},{4,7},{5,4},{6,5},{7,6},{8,11},{9,8},{10,9... | collective-permute-start | bytes 393224 | tf_op jit(solution)/shard_map/ppermute | solution.py:361
  45.2 1.0 %shard_map.91 = (bf16[2,64,128]{2,1,0:T(8,128)(2,1)S(1)}, bf16[2,64,128]{2,1,0:T(8,128)(2,1)S(1)}, bf16[2,64,128]{2,1,0:T(8,128)(2,1)S(1)}, bf16[2,64,128]{2,1,0:T(8,128)(2,1)S(1)}) custom-call(s32[2]{0:T(128)S(1)} %pad_add_fusion.where, bf16[18,64,128]{2,1,0:T(8,128)(2,1)S(1)} %get-tuple-element.49.rest_4_.rest_0_, ...), custom_call_target="tpu_custom_call" | custom-call | flops 134217728 | bytes 1179648 | tf_op jit(solution)/shard_map/pallas_call | solution.py:257
  46.2 0.5 collective-permute-start.13
  46.7 1.7 %collective-permute-start.14 = (bf16[2,64,128]{2,1,0:T(8,128)(2,1)S(1)}, bf16[2,64,128]{2,1,0:T(8,128)(2,1)S(1)}, u32[]{:S(2)}, u32[]{:S(2)}) collective-permute-start(bf16[2,64,128]{2,1,0:T(8,128)(2,1)S(1)} %get-tuple-element.55), channel_id=1, source_target_pairs={{0,2},{1,3},{2,0},{3,1},{4,6},{5,7},{6,4},{7,5},{8,10},{9,11},{10,... | collective-permute-start | bytes 98312 | tf_op jit(solution)/shard_map/ppermute | solution.py:361
  48.4 5.4 %collective-permute-start.15 = (bf16[2,64,128]{2,1,0:T(8,128)(2,1)S(1)}, bf16[2,64,128]{2,1,0:T(8,128)(2,1)S(1)}, u32[]{:S(2)}, u32[]{:S(2)}) collective-permute-start(bf16[2,64,128]{2,1,0:T(8,128)(2,1)S(1)} %get-tuple-element.56), channel_id=1, source_target_pairs={{0,1},{1,2},{2,3},{3,0},{4,5},{5,6},{6,7},{7,4},{8,9},{9,10},{10,1... | collective-permute-start | bytes 98312 | tf_op jit(solution)/shard_map/ppermute | solution.py:361
  53.8 1.0 %shard_map.89 = (bf16[8,64,128]{2,1,0:T(8,128)(2,1)S(1)}, bf16[8,64,128]{2,1,0:T(8,128)(2,1)S(1)}, bf16[8,64,128]{2,1,0:T(8,128)(2,1)S(1)}, bf16[8,64,128]{2,1,0:T(8,128)(2,1)S(1)}) custom-call(s32[2]{0:T(128)S(1)} %pad_add_fusion.where, bf16[8,64,128]{2,1,0:T(8,128)(2,1)S(1)} %get-tuple-element.37.rest_0_, ...), custom_call_target="tpu_custom_call" | custom-call | flops 134217728 | bytes 1048576 | tf_op jit(solution)/shard_map/pallas_call | solution.py:220
  54.8 3.3 %collective-permute-start.10 = (bf16[8,64,128]{2,1,0:T(8,128)(2,1)S(1)}, bf16[8,64,128]{2,1,0:T(8,128)(2,1)S(1)}, u32[]{:S(2)}, u32[]{:S(2)}) collective-permute-start(bf16[8,64,128]{2,1,0:T(8,128)(2,1)S(1)} %get-tuple-element.46), channel_id=1, source_target_pairs={{0,1},{1,2},{2,3},{3,0},{4,5},{5,6},{6,7},{7,4},{8,9},{9,10},{10,1... | collective-permute-start | bytes 393224 | tf_op jit(solution)/shard_map/ppermute | solution.py:361
  58.3 2.3 %collective-permute-start.11 = (bf16[8,64,128]{2,1,0:T(8,128)(2,1)S(1)}, bf16[8,64,128]{2,1,0:T(8,128)(2,1)S(1)}, u32[]{:S(2)}, u32[]{:S(2)}) collective-permute-start(bf16[8,64,128]{2,1,0:T(8,128)(2,1)S(1)} %get-tuple-element.47), channel_id=1, source_target_pairs={{0,2},{1,3},{2,0},{3,1},{4,6},{5,7},{6,4},{7,5},{8,10},{9,11},{10,... | collective-permute-start | bytes 393224 | tf_op jit(solution)/shard_map/ppermute | solution.py:361
  60.5 0.2 collective-permute-start.12
  60.7 1.0 %collective-permute-start.19 = (f32[2,64,128]{2,1,0:T(8,128)S(1)}, f32[2,64,128]{2,1,0:T(8,128)S(1)}, u32[]{:S(2)}, u32[]{:S(2)}) collective-permute-start(f32[2,64,128]{2,1,0:T(8,128)S(1)} %add.24), channel_id=1, source_target_pairs={{0,24},{4,28},{8,16},{12,20},{16,8},{20,12},{24,0},{28,4},{1,25},{... | collective-permute-start | bytes 196616 | tf_op jit(solution)/shard_map/ppermute | solution.py:393
  61.7 0.7 collective-permute-start.18
  62.4 1.5 %collective-permute-done.10.rest_1_ = bf16[8,64,128]{2,1,0:T(8,128)(2,1)S(1)} collective-permute-done((bf16[8,64,128]{2,1,0:T(8,128)(2,1)S(1)}, bf16[8,64,128]{2,1,0:T(8,128)(2,1)S(1)}, u32[]{:S(2)}, u32[]{:S(2)}) %collective-permute-start.10) | collective-permute-done | bytes 131104 | tf_op jit(solution)/shard_map/ppermute | solution.py:361
  63.9 0.4 collective-permute-start.17
  64.3 4.2 %collective-permute-done.11.rest_2_ = bf16[8,64,128]{2,1,0:T(8,128)(2,1)S(1)} collective-permute-done((bf16[8,64,128]{2,1,0:T(8,128)(2,1)S(1)}, bf16[8,64,128]{2,1,0:T(8,128)(2,1)S(1)}, u32[]{:S(2)}, u32[]{:S(2)}) %collective-permute-start.11) | collective-permute-done | bytes 131104 | tf_op jit(solution)/shard_map/ppermute | solution.py:361
  68.5 0.7 collective-permute-done.12.rest_3_
  69.1 1.4 %shard_map.90 = bf16[32,64,128]{2,1,0:T(8,128)(2,1)} custom-call(s32[2]{0:T(128)S(1)} %pad_add_fusion.where, bf16[8,64,128]{2,1,0:T(8,128)(2,1)S(1)} %get-tuple-element.45.rest_0_, bf16[8,64,128]{2,1,0:T(8,128)(2,1)S(1)} %collective-permute-done.10.rest_1_, bf16[8,64,128]{2,1,0:T(8,128)(2,1)S(1)} %collective-permute-done.11.rest_2_, ...), custom_call_target="tpu_custom_call" | custom-call | bytes 33554432 | tf_op jit(solution)/shard_map/pallas_call | solution.py:346
  70.5 0.6 copy_bitcast_fusion
  (18 shorter events, 0.2 us)
Async XLA Ops:
  7.3 8.5 %collective-permute-start = (bf16[64,64,128]{2,1,0:T(8,128)(2,1)S(1)}, bf16[64,64,128]{2,1,0:T(8,128)(2,1)S(1)}, u32[]{:S(2)}, u32[]{:S(2)}) collective-permute-start(bf16[64,64,128]{2,1,0:T(8,128)(2,1)S(1)} %get-tuple-element.31), channel_id=1, source_target_pairs={{0,4},{4,0},{8,12},{12,8},{16,20},{20,16},{24,28},{28,24},{1,5},{5... | collective-permute-start | bytes 3145736 | tf_op jit(solution)/shard_map/ppermute | solution.py:376
  12.4 14.8 %collective-permute-start.1 = (bf16[32,64,128]{2,1,0:T(8,128)(2,1)S(1)}, bf16[32,64,128]{2,1,0:T(8,128)(2,1)S(1)}, u32[]{:S(2)}, u32[]{:S(2)}) collective-permute-start(bf16[32,64,128]{2,1,0:T(8,128)(2,1)S(1)} %get-tuple-element.33), channel_id=1, source_target_pairs={{0,24},{4,12},{8,0},{12,20},{16,8},{20,28},{24,16},{28,4},{1,25},{... | collective-permute-start | bytes 1572872 | tf_op jit(solution)/shard_map/ppermute | solution.py:377
  14.2 29.6 %collective-permute-start.7 = (bf16[18,64,128]{2,1,0:T(8,128)(2,1)S(1)}, bf16[18,64,128]{2,1,0:T(8,128)(2,1)S(1)}, u32[]{:S(2)}, u32[]{:S(2)}) collective-permute-start(bf16[18,64,128]{2,1,0:T(8,128)(2,1)S(1)} %get-tuple-element.42), channel_id=1, source_target_pairs={{0,1},{1,2},{2,3},{3,0},{4,5},{5,6},{6,7},{7,4},{8,9},{9,10},{10,1... | collective-permute-start | bytes 884744 | tf_op jit(solution)/shard_map/ppermute | solution.py:361
  16.1 16.4 %collective-permute-start.2 = (bf16[16,64,128]{2,1,0:T(8,128)(2,1)S(1)}, bf16[16,64,128]{2,1,0:T(8,128)(2,1)S(1)}, u32[]{:S(2)}, u32[]{:S(2)}) collective-permute-start(bf16[16,64,128]{2,1,0:T(8,128)(2,1)S(1)} %get-tuple-element.35), channel_id=1, source_target_pairs={{0,28},{4,8},{8,4},{12,16},{16,12},{20,24},{24,20},{28,0},{1,29},{... | collective-permute-start | bytes 786440 | tf_op jit(solution)/shard_map/ppermute | solution.py:379
  17.1 20.9 %collective-permute-start.3 = (bf16[16,64,128]{2,1,0:T(8,128)(2,1)S(1)}, bf16[16,64,128]{2,1,0:T(8,128)(2,1)S(1)}, u32[]{:S(2)}, u32[]{:S(2)}) collective-permute-start(bf16[16,64,128]{2,1,0:T(8,128)(2,1)S(1)} %get-tuple-element.36), channel_id=1, source_target_pairs={{0,28},{4,8},{8,4},{12,16},{16,12},{20,24},{24,20},{28,0},{1,29},{... | collective-permute-start | bytes 786440 | tf_op jit(solution)/shard_map/ppermute | solution.py:379
  18.8 26.4 %collective-permute-start.8 = (bf16[18,64,128]{2,1,0:T(8,128)(2,1)S(1)}, bf16[18,64,128]{2,1,0:T(8,128)(2,1)S(1)}, u32[]{:S(2)}, u32[]{:S(2)}) collective-permute-start(bf16[18,64,128]{2,1,0:T(8,128)(2,1)S(1)} %get-tuple-element.43), channel_id=1, source_target_pairs={{0,2},{1,3},{2,0},{3,1},{4,6},{5,7},{6,4},{7,5},{8,10},{9,11},{10,... | collective-permute-start | bytes 884744 | tf_op jit(solution)/shard_map/ppermute | solution.py:361
  27.2 18.0 %collective-permute-start.9 = (bf16[18,64,128]{2,1,0:T(8,128)(2,1)S(1)}, bf16[18,64,128]{2,1,0:T(8,128)(2,1)S(1)}, u32[]{:S(2)}, u32[]{:S(2)}) collective-permute-start(bf16[18,64,128]{2,1,0:T(8,128)(2,1)S(1)} %get-tuple-element.44), channel_id=1, source_target_pairs={{0,3},{1,0},{2,1},{3,2},{4,7},{5,4},{6,5},{7,6},{8,11},{9,8},{10,9... | collective-permute-start | bytes 884744 | tf_op jit(solution)/shard_map/ppermute | solution.py:361
  39.0 9.4 %collective-permute-start.4 = (bf16[8,64,128]{2,1,0:T(8,128)(2,1)S(1)}, bf16[8,64,128]{2,1,0:T(8,128)(2,1)S(1)}, u32[]{:S(2)}, u32[]{:S(2)}) collective-permute-start(bf16[8,64,128]{2,1,0:T(8,128)(2,1)S(1)} %get-tuple-element.38), channel_id=1, source_target_pairs={{0,1},{1,2},{2,3},{3,0},{4,5},{5,6},{6,7},{7,4},{8,9},{9,10},{10,1... | collective-permute-start | bytes 393224 | tf_op jit(solution)/shard_map/ppermute | solution.py:361
  41.3 12.5 %collective-permute-start.5 = (bf16[8,64,128]{2,1,0:T(8,128)(2,1)S(1)}, bf16[8,64,128]{2,1,0:T(8,128)(2,1)S(1)}, u32[]{:S(2)}, u32[]{:S(2)}) collective-permute-start(bf16[8,64,128]{2,1,0:T(8,128)(2,1)S(1)} %get-tuple-element.39), channel_id=1, source_target_pairs={{0,2},{1,3},{2,0},{3,1},{4,6},{5,7},{6,4},{7,5},{8,10},{9,11},{10,... | collective-permute-start | bytes 393224 | tf_op jit(solution)/shard_map/ppermute | solution.py:361
  43.9 10.0 %collective-permute-start.6 = (bf16[8,64,128]{2,1,0:T(8,128)(2,1)S(1)}, bf16[8,64,128]{2,1,0:T(8,128)(2,1)S(1)}, u32[]{:S(2)}, u32[]{:S(2)}) collective-permute-start(bf16[8,64,128]{2,1,0:T(8,128)(2,1)S(1)} %get-tuple-element.40), channel_id=1, source_target_pairs={{0,3},{1,0},{2,1},{3,2},{4,7},{5,4},{6,5},{7,6},{8,11},{9,8},{10,9... | collective-permute-start | bytes 393224 | tf_op jit(solution)/shard_map/ppermute | solution.py:361
  46.2 11.9 %collective-permute-start.13 = (bf16[2,64,128]{2,1,0:T(8,128)(2,1)S(1)}, bf16[2,64,128]{2,1,0:T(8,128)(2,1)S(1)}, u32[]{:S(2)}, u32[]{:S(2)}) collective-permute-start(bf16[2,64,128]{2,1,0:T(8,128)(2,1)S(1)} %get-tuple-element.54), channel_id=1, source_target_pairs={{0,3},{1,0},{2,1},{3,2},{4,7},{5,4},{6,5},{7,6},{8,11},{9,8},{10,9... | collective-permute-start | bytes 98312 | tf_op jit(solution)/shard_map/ppermute | solution.py:361
  46.7 11.4 %collective-permute-start.14 = (bf16[2,64,128]{2,1,0:T(8,128)(2,1)S(1)}, bf16[2,64,128]{2,1,0:T(8,128)(2,1)S(1)}, u32[]{:S(2)}, u32[]{:S(2)}) collective-permute-start(bf16[2,64,128]{2,1,0:T(8,128)(2,1)S(1)} %get-tuple-element.55), channel_id=1, source_target_pairs={{0,2},{1,3},{2,0},{3,1},{4,6},{5,7},{6,4},{7,5},{8,10},{9,11},{10,... | collective-permute-start | bytes 98312 | tf_op jit(solution)/shard_map/ppermute | solution.py:361
  48.4 9.7 %collective-permute-start.15 = (bf16[2,64,128]{2,1,0:T(8,128)(2,1)S(1)}, bf16[2,64,128]{2,1,0:T(8,128)(2,1)S(1)}, u32[]{:S(2)}, u32[]{:S(2)}) collective-permute-start(bf16[2,64,128]{2,1,0:T(8,128)(2,1)S(1)} %get-tuple-element.56), channel_id=1, source_target_pairs={{0,1},{1,2},{2,3},{3,0},{4,5},{5,6},{6,7},{7,4},{8,9},{9,10},{10,1... | collective-permute-start | bytes 98312 | tf_op jit(solution)/shard_map/ppermute | solution.py:361
  54.8 9.1 %collective-permute-start.10 = (bf16[8,64,128]{2,1,0:T(8,128)(2,1)S(1)}, bf16[8,64,128]{2,1,0:T(8,128)(2,1)S(1)}, u32[]{:S(2)}, u32[]{:S(2)}) collective-permute-start(bf16[8,64,128]{2,1,0:T(8,128)(2,1)S(1)} %get-tuple-element.46), channel_id=1, source_target_pairs={{0,1},{1,2},{2,3},{3,0},{4,5},{5,6},{6,7},{7,4},{8,9},{9,10},{10,1... | collective-permute-start | bytes 393224 | tf_op jit(solution)/shard_map/ppermute | solution.py:361
  58.2 2.5 %collective-permute-start.16 = (f32[2,64,128]{2,1,0:T(8,128)S(1)}, f32[2,64,128]{2,1,0:T(8,128)S(1)}, u32[]{:S(2)}, u32[]{:S(2)}) collective-permute-start(f32[2,64,128]{2,1,0:T(8,128)S(1)} %convert_add_fusion), channel_id=1, source_target_pairs={{0,4},{4,0},{8,12},{12,8},{16,20},{20,16},{24,28},{28,24},{1,5},{5... | collective-permute-start | bytes 196616 | tf_op jit(solution)/shard_map/ppermute | solution.py:391
  58.3 10.2 %collective-permute-start.11 = (bf16[8,64,128]{2,1,0:T(8,128)(2,1)S(1)}, bf16[8,64,128]{2,1,0:T(8,128)(2,1)S(1)}, u32[]{:S(2)}, u32[]{:S(2)}) collective-permute-start(bf16[8,64,128]{2,1,0:T(8,128)(2,1)S(1)} %get-tuple-element.47), channel_id=1, source_target_pairs={{0,2},{1,3},{2,0},{3,1},{4,6},{5,7},{6,4},{7,5},{8,10},{9,11},{10,... | collective-permute-start | bytes 393224 | tf_op jit(solution)/shard_map/ppermute | solution.py:361
  60.5 8.6 %collective-permute-start.12 = (bf16[8,64,128]{2,1,0:T(8,128)(2,1)S(1)}, bf16[8,64,128]{2,1,0:T(8,128)(2,1)S(1)}, u32[]{:S(2)}, u32[]{:S(2)}) collective-permute-start(bf16[8,64,128]{2,1,0:T(8,128)(2,1)S(1)} %get-tuple-element.48), channel_id=1, source_target_pairs={{0,3},{1,0},{2,1},{3,2},{4,7},{5,4},{6,5},{7,6},{8,11},{9,8},{10,9... | collective-permute-start | bytes 393224 | tf_op jit(solution)/shard_map/ppermute | solution.py:361
  60.7 9.8 %collective-permute-start.19 = (f32[2,64,128]{2,1,0:T(8,128)S(1)}, f32[2,64,128]{2,1,0:T(8,128)S(1)}, u32[]{:S(2)}, u32[]{:S(2)}) collective-permute-start(f32[2,64,128]{2,1,0:T(8,128)S(1)} %add.24), channel_id=1, source_target_pairs={{0,24},{4,28},{8,16},{12,20},{16,8},{20,12},{24,0},{28,4},{1,25},{... | collective-permute-start | bytes 196616 | tf_op jit(solution)/shard_map/ppermute | solution.py:393
  61.7 8.8 %collective-permute-start.18 = (f32[2,64,128]{2,1,0:T(8,128)S(1)}, f32[2,64,128]{2,1,0:T(8,128)S(1)}, u32[]{:S(2)}, u32[]{:S(2)}) collective-permute-start(f32[2,64,128]{2,1,0:T(8,128)S(1)} %add.24), channel_id=1, source_target_pairs={{0,16},{4,20},{8,24},{12,28},{16,0},{20,4},{24,8},{28,12},{1,17},{... | collective-permute-start | bytes 196616 | tf_op jit(solution)/shard_map/ppermute | solution.py:393
  63.9 6.6 %collective-permute-start.17 = (f32[2,64,128]{2,1,0:T(8,128)S(1)}, f32[2,64,128]{2,1,0:T(8,128)S(1)}, u32[]{:S(2)}, u32[]{:S(2)}) collective-permute-start(f32[2,64,128]{2,1,0:T(8,128)S(1)} %add.24), channel_id=1, source_target_pairs={{0,8},{4,12},{8,0},{12,4},{16,24},{20,28},{24,16},{28,20},{1,9},{5... | collective-permute-start | bytes 196616 | tf_op jit(solution)/shard_map/ppermute | solution.py:393
